TPU v7x, 32 devices: a whole 2x2x4 slice. The times are simulated.
32 devices in a mesh: groups: 2 (over x), tp: 16 (over z, y, core).
Axes of the slice: x: 2, y: 2, z: 4, core: 2. Of those that a mesh axis runs over, the one named last changes fastest.
Arguments:
- normed_layer_input: bfloat16 [64, 8192], P(('groups', 'tp')), parts along dimension 0, may hold values from -6 to 6
- hidden_unit_gradient: bfloat16 [64, 28672], P('groups', 'tp'), parts along dimension 0, may hold values from -6 to 6
- gate_weight: bfloat16 [8192, 28672], P(None, 'tp'), may hold values from -0.0625 to 0.0625
- up_weight: bfloat16 [8192, 28672], P(None, 'tp'), may hold values from -0.0625 to 0.0625
- adapter_down_maps: bfloat16 [8192, 2048], P('tp'), may hold values from -0.125 to 0.125
- adapter_up_maps: bfloat16 [2048, 28672], P(None, 'tp'), may hold values from -0.03125 to 0.03125
- token_tenant_index: int32 [64], P('groups'), parts along dimension 0, may hold values from 0 to 31
Outputs:
- grad_input: bfloat16 [64, 8192], P(('groups', 'tp')), parts along dimension 0
- down_map_gradient: bfloat16 [8192, 4096], P('tp', 'groups'), parts along dimension 1
- up_map_gradient: bfloat16 [4096, 28672], P('groups', 'tp'), parts along dimension 0
There are 2 independent parts, one for each index of `groups`. A program takes and returns all parts, laid end to end along the dimension named above; an argument that names none is the same for every part. Nothing has to cross between parts.
All inputs are finite; a program needn't handle non-finite values.
Results may differ from a plain program's by a relative error of at most 0.006.
Values may be sent and summed in bfloat16 or wider, within the bound.
No kernel may reach another device: no remote copies, remote signals or barrier semaphores. Data moves between devices by JAX's collectives and lax.ppermute only.
A program may use at most 192 MiB of HBM per device.

v0:
```python
import jax
import jax.numpy as jnp
from jax import lax
from jax.sharding import PartitionSpec as P

ADAPTER_RANK = 64
TENANT_COUNT = 32


adapter_scale = 2.0


def select_block(wide_rows, tenant_match_mask):
    return (
        (wide_rows * tenant_match_mask)
        .reshape(wide_rows.shape[0], TENANT_COUNT, ADAPTER_RANK)
        .sum(axis=1)
    )


def contracted_rows(left, right):
    return lax.dot_general(
        left, right, (((0,), (0,)), ((), ())), preferred_element_type=jnp.float32
    )


def contracted_columns(left, right):
    return lax.dot_general(
        left, right, (((1,), (1,)), ((), ())), preferred_element_type=jnp.float32
    )


def spread_rows(low_rows, tenant_match_mask):
    return (jnp.tile(low_rows, (1, TENANT_COUNT)) * tenant_match_mask).astype(jnp.bfloat16)


def local(
    normed_layer_input,
    hidden_unit_gradient,
    gate_weight,
    up_weight,
    adapter_down_maps,
    adapter_up_maps,
    token_tenant_index,
):
    columns = lax.broadcasted_iota(jnp.int32, (1, TENANT_COUNT * ADAPTER_RANK), 1) // ADAPTER_RANK
    tenant_match_mask = (token_tenant_index[:, None] == columns).astype(jnp.float32)
    feature_column_span = adapter_down_maps.shape[0]
    col_start = lax.axis_index("tp") * feature_column_span
    whole = lax.all_gather(normed_layer_input, "tp", axis=0, tiled=True)
    input_column_span = lax.dynamic_slice_in_dim(whole, col_start, feature_column_span, 1)
    input_part = select_block(
        jnp.dot(input_column_span, adapter_down_maps, preferred_element_type=jnp.float32),
        tenant_match_mask,
    )
    reduced_input = lax.psum(input_part, "tp")
    input_spread_rows = spread_rows(reduced_input, tenant_match_mask)
    gate_activation = jnp.dot(whole, gate_weight, preferred_element_type=jnp.float32)
    gate_activation = gate_activation + adapter_scale * jnp.dot(
        input_spread_rows, adapter_up_maps, preferred_element_type=jnp.float32
    )
    up_val = jnp.dot(whole, up_weight, preferred_element_type=jnp.float32)
    sigmoid_gate = jax.nn.sigmoid(gate_activation)
    hidden_grad = hidden_unit_gradient.astype(jnp.float32)
    gate_gradient = (
        hidden_grad * up_val * sigmoid_gate * (1.0 + gate_activation * (1.0 - sigmoid_gate))
    ).astype(jnp.bfloat16)
    d_up = (hidden_grad * gate_activation * sigmoid_gate).astype(jnp.bfloat16)
    gradient_portion = select_block(
        contracted_columns(gate_gradient, adapter_up_maps), tenant_match_mask
    )
    reduced_gradient = lax.psum(gradient_portion, "tp")
    gradient_spread_rows = spread_rows(reduced_gradient, tenant_match_mask)
    down_map_gradient = (
        adapter_scale * contracted_rows(input_column_span, gradient_spread_rows)
    ).astype(jnp.bfloat16)
    up_map_gradient = (adapter_scale * contracted_rows(input_spread_rows, gate_gradient)).astype(
        jnp.bfloat16
    )
    adapter_column_span = adapter_scale * contracted_columns(
        gradient_spread_rows, adapter_down_maps
    )
    running_sum = lax.psum_scatter(
        contracted_columns(gate_gradient, gate_weight) + contracted_columns(d_up, up_weight),
        "tp",
        scatter_dimension=0,
        tiled=True,
    )
    running_sum = running_sum + lax.all_to_all(
        adapter_column_span, "tp", split_axis=0, concat_axis=1, tiled=True
    )
    return (running_sum.astype(jnp.bfloat16), down_map_gradient, up_map_gradient)


def solution(mesh):
    placed = (
        P(("groups", "tp"), None),
        P("groups", "tp"),
        P(None, "tp"),
        P(None, "tp"),
        P("tp", None),
        P(None, "tp"),
        P("groups"),
    )
    return jax.shard_map(
        local,
        mesh=mesh,
        in_specs=placed,
        out_specs=(P(("groups", "tp"), None), P("tp", "groups"), P("groups", "tp")),
        check_vma=False,
    )
```

profile of v0, /device:TPU:0, one launch (start us, length us, event | category | flops | bytes accessed | tf_op | source)
XLA Modules:
  0.0 322.2 jit_solution(13651130206422711699)
XLA Ops:
  7.2 0.0 copy-start
  7.2 24.9 %all-gather = bf16[16,2,8192]{2,1,0:T(2,128)(2,1)S(1)} all-gather(bf16[1,2,8192]{2,1,0:T(2,128)(2,1)} %bitcast.21), channel_id=1, replica_groups=mesh['groups'=2,'tp'=16] {'tp'}, dimensions={0}, use_global_device_ids=true | all-gather | bytes 557056 | tf_op jit(solution)/shard_map/all_gather | solution.py:50
  32.1 0.2 reshape.64
  32.3 0.0 copy-start.4
  32.3 12.6 %fusion.23 = f32[32,1792]{1,0:T(8,128)} fusion(bf16[32,8192]{1,0:T(8,128)(2,1)S(1)} %reshape.64, bf16[8192,1792]{1,0:T(8,128)(2,1)} %param.9), kind=kOutput, calls=%fused_computation.35 | convolution fusion | flops 939524096 | bytes 30113792 | tf_op jit(solution)/shard_map/dot_general | solution.py:58
  44.9 0.0 copy-done
  44.9 0.0 copy-done.4
  44.9 0.5 convolution_select_fusion.1
  45.4 0.2 reshape.61
  45.6 0.1 reduce_sum.18
  45.7 57.8 %psum.14 = bf16[32,64]{1,0:T(8,128)(2,1)S(1)} all-reduce(f32[32,64]{1,0:T(8,128)S(1)} %reduce_sum.18), channel_id=1, replica_groups=mesh['groups'=2,'tp'=16] {'tp'}, use_global_device_ids=true, to_apply=%region_1.2 | all-reduce | flops 2048 | bytes 12288 | tf_op jit(solution)/shard_map/psum | solution.py:56
  103.6 0.3 tile.9
  103.9 0.0 copy-start.1
  103.9 0.0 slice-start
  103.9 4.6 %fusion = f32[32,1792]{1,0:T(8,128)S(1)} fusion(f32[32,1792]{1,0:T(8,128)} %fusion.23, bf16[2048,1792]{1,0:T(8,128)(2,1)} %param.12, bf16[32,2048]{1,0:T(8,128)(2,1)S(1)} %tile.9, s32[2048]{0:T(1024)S(1)} %add_select_fusion, s32[32]{0:T(128)S(1)} %copy-done.4), kind=kOutput, calls=%fused_computation.4 | convolution fusion | flops 235126784 | bytes 7938176 | tf_op jit(solution)/shard_map/dot_general | solution.py:59
  108.5 0.0 slice-start.1
  108.6 12.2 %fusion.3 = bf16[32,1792]{1,0:T(8,128)(2,1)S(1)} fusion(bf16[32,8192]{1,0:T(8,128)(2,1)S(1)} %reshape.64, bf16[8192,1792]{1,0:T(8,128)(2,1)} %param.10, bf16[32,1792]{1,0:T(8,128)(2,1)} %param.8, f32[32,1792]{1,0:T(8,128)S(1)} %fusion), kind=kOutput, calls=%fused_computation.10 | convolution fusion | flops 940154880 | bytes 30343168 | tf_op jit(solution)/shard_map/dot_general | solution.py:62
  120.8 0.0 copy-done.1
  120.8 0.0 slice-done
  120.8 0.0 slice-done.1
  120.8 2.9 convolution_select_fusion
  123.7 1.1 reshape.62
  124.9 0.1 reduce_sum.19
  125.0 57.6 %psum.15 = bf16[32,64]{1,0:T(8,128)(2,1)S(1)} all-reduce(f32[32,64]{1,0:T(8,128)S(1)} %reduce_sum.19), channel_id=1, replica_groups=mesh['groups'=2,'tp'=16] {'tp'}, use_global_device_ids=true, to_apply=%region_4.5 | all-reduce | flops 2048 | bytes 12288 | tf_op jit(solution)/shard_map/psum | solution.py:72
  182.6 0.3 tile.21
  182.9 0.7 convolution_multiply_fusion.2
  183.6 0.7 all_to_all.14
  184.3 3.5 %all-to-all-start = ((f32[16,2,512]{2,1,0:T(2,128)}), f32[16,2,512]{2,1,0:T(2,128)S(1)}, u32[]{:S(2)}, u32[]{:S(2)}) async-start(f32[16,2,512]{2,1,0:T(2,128)} %all_to_all.14), calls=%async_computation | async-start | bytes 131072 | tf_op jit(solution)/shard_map/all_to_all | solution.py:89
  187.8 0.0 copy-start.3
  187.8 0.2 all-reduce.3.cloned.1.call-start
  188.1 15.0 %fusion.24 = f32[32,8192]{1,0:T(8,128)} fusion(bf16[32,1792]{1,0:T(8,128)(2,1)S(1)} %fusion.3, bf16[8192,1792]{1,0:T(8,128)(2,1)} %param.9), kind=kOutput, calls=%fused_computation.36 | convolution fusion | flops 939524096 | bytes 30523392 | tf_op jit(solution)/shard_map/dot_general | solution.py:28
  203.1 0.0 copy-done.3
  203.1 0.0 copy-start.2
  203.1 15.8 %convolution_add_fusion = f32[32,8192]{1,0:T(8,128)} fusion(f32[32,8192]{1,0:T(8,128)} %fusion.24, bf16[8192,1792]{1,0:T(8,128)(2,1)} %param.10, f32[32,1792]{1,0:T(8,128)S(1)} %fusion, bf16[32,1792]{1,0:T(8,128)(2,1)S(1)} %copy-done.3), kind=kOutput, calls=%fused_computation.1 | convolution fusion | flops 940187648 | bytes 31801344 | tf_op jit(solution)/shard_map/dot_general | solution.py:28
  218.9 0.0 all-reduce.3.cloned.1.call-update
  219.0 0.0 copy-done.2
  219.0 0.0 copy-start.5
  219.0 5.2 %multiply_convert_fusion = bf16[2048,1792]{1,0:T(8,128)(2,1)} fusion(bf16[32,1792]{1,0:T(8,128)(2,1)S(1)} %fusion.3, bf16[32,2048]{1,0:T(8,128)(2,1)S(1)} %copy-done.2, s32[2048]{0:T(1024)S(1)} %add_select_fusion, s32[32]{0:T(128)S(1)} %copy-done.4), kind=kOutput, calls=%fused_computation | convolution fusion | flops 242352128 | bytes 7594112 | tf_op jit(solution)/shard_map/dot_general | solution.py:22
  224.2 2.1 multiply_convert_fusion.1
  226.3 0.0 copy-done.5
  226.3 0.6 dynamic-slice
  227.5 0.0 all-to-all-done
  227.5 86.2 %all-reduce.3.cloned.1.call-done = f32[32,8192]{1,0:T(8,128)} async-done(((f32[32,8192]{1,0:T(8,128)}), f32[32,8192]{1,0:T(8,128)}) %all-reduce.3.cloned.1.call-update) | async-done | bytes 1048592
  313.8 1.6 fusion.10
  (4 shorter events, 0.1 us)
Async XLA Ops:
  7.2 37.8 %copy-start = (bf16[512,2048]{1,0:T(8,128)(2,1)S(1)}, bf16[512,2048]{1,0:T(8,128)(2,1)}, u32[]{:S(2)}) copy-start(bf16[512,2048]{1,0:T(8,128)(2,1)} %param.11) | copy-start | bytes 6291460
  32.3 12.6 %copy-start.4 = (s32[32]{0:T(128)S(1)}, s32[32]{0:T(128)}, u32[]{:S(2)}) copy-start(s32[32]{0:T(128)} %param.13) | copy-start | bytes 388
  103.9 16.9 %copy-start.1 = (bf16[32,2048]{1,0:T(8,128)(2,1)}, bf16[32,2048]{1,0:T(8,128)(2,1)S(1)}, u32[]{:S(2)}) copy-start(bf16[32,2048]{1,0:T(8,128)(2,1)S(1)} %tile.9) | copy-start | bytes 393220
  103.9 16.9 %slice-start = ((s8[7340032]{0:T(1024)(128)(4,1)}), s8[4194304]{0:T(1024)(128)(4,1)S(1)}, s32[]{:S(2)}) async-start(s8[7340032]{0:T(1024)(128)(4,1)} %bitcast.18), calls=%async_computation.2 | async-start | bytes 8388608
  108.5 12.2 %slice-start.1 = ((s8[7340032]{0:T(1024)(128)(4,1)}), s8[3145728]{0:T(1024)(128)(4,1)S(1)}, s32[]{:S(2)}) async-start(s8[7340032]{0:T(1024)(128)(4,1)} %bitcast.18), calls=%async_computation.3 | async-start | bytes 6291456
  184.3 43.2 %all-to-all-start = ((f32[16,2,512]{2,1,0:T(2,128)}), f32[16,2,512]{2,1,0:T(2,128)S(1)}, u32[]{:S(2)}, u32[]{:S(2)}) async-start(f32[16,2,512]{2,1,0:T(2,128)} %all_to_all.14), calls=%async_computation | async-start | bytes 131072 | tf_op jit(solution)/shard_map/all_to_all | solution.py:89
  187.8 15.3 %copy-start.3 = (bf16[32,1792]{1,0:T(8,128)(2,1)S(1)}, bf16[32,1792]{1,0:T(8,128)(2,1)}, u32[]{:S(2)}) copy-start(bf16[32,1792]{1,0:T(8,128)(2,1)} %param.8) | copy-start | bytes 344068
  187.8 125.9 %all-reduce.3.cloned.1.call-start = ((), (), s32[]{:S(2)}) async-start(), calls=%async_computation.1 | async-start | bytes 2097152
  203.1 15.9 %copy-start.2 = (bf16[32,2048]{1,0:T(8,128)(2,1)S(1)}, bf16[32,2048]{1,0:T(8,128)(2,1)}, u32[]{:S(2)}) copy-start(bf16[32,2048]{1,0:T(8,128)(2,1)} %copy-done.1) | copy-start | bytes 393220
  219.0 7.3 %copy-start.5 = (u32[32]{0:T(128)S(1)}, u32[32]{0:T(128)}, u32[]{:S(2)}) copy-start(u32[32]{0:T(128)} %constant.43) | copy-start | bytes 388
Sparse Core Ops, SparseCore 0:
  219.1 94.6 all-reduce.2
where the time goes:
time: 323 us; the launch traced here: 322 us
  blocking collectives  140 us (43%)
  waiting for transfers between devices  86.2 us (27%)
  matrix products  71.8 us (22%)
  between operations  14.9 us (5%)
  starting transfers between devices  3.71 us (1%)
  local copies, waits for them, and re-layouts  3.5 us (1%)
    unnamed x2, waiting for transfers between devices  86.2 us
    psum x1, blocking collectives, local(): reduced_input = lax.psum(input_part, 'tp')  57.8 us
    psum x1, blocking collectives, local(): reduced_gradient = lax.psum(gradient_portion, 'tp')  57.6 us
    dot_general x4, matrix products, contracted_columns(): lax.dot_general(left, right, (((1,), (1,)), ((), ())), preferred_element_...  34.5 us
    all_gather x1, blocking collectives, local(): whole = lax.all_gather(normed_layer_input, 'tp', axis=0, tiled=True)  24.9 us
    dot_general x1, matrix products, local(): jnp.dot(whole, gate_weight, preferred_element_type=jnp.float32)  12.6 us
    dot_general x1, matrix products, local(): up_val = jnp.dot(whole, up_weight, preferred_element_type=jnp.float32)  12.2 us
    dot_general x2, matrix products, contracted_rows(): lax.dot_general(left, right, (((0,), (0,)), ((), ())), preferred_element_...  7.31 us
  transfers between devices with their start and end apart: 2, of which 1 were waited for; matrix products, arithmetic and copies ran while one was open for 12% of the time, Pallas kernels for 0%

commit v1 on v0

--- a/solution.py
+++ b/solution.py
@@ -34,6 +34,12 @@
     return (jnp.tile(low_rows, (1, TENANT_COUNT)) * tenant_match_mask).astype(jnp.bfloat16)
 
 
+def from_everyone(block):
+    count = lax.axis_size("tp")
+    copies = jnp.broadcast_to(block[None], (count,) + block.shape)
+    return lax.all_to_all(copies, "tp", split_axis=0, concat_axis=0, tiled=True)
+
+
 def local(
     normed_layer_input,
     hidden_unit_gradient,
@@ -43,23 +49,26 @@
     adapter_up_maps,
     token_tenant_index,
 ):
+    count = lax.axis_size("tp")
+    own_rows, width = normed_layer_input.shape
+    rows = own_rows * count
     columns = lax.broadcasted_iota(jnp.int32, (1, TENANT_COUNT * ADAPTER_RANK), 1) // ADAPTER_RANK
     tenant_match_mask = (token_tenant_index[:, None] == columns).astype(jnp.float32)
     feature_column_span = adapter_down_maps.shape[0]
     col_start = lax.axis_index("tp") * feature_column_span
-    whole = lax.all_gather(normed_layer_input, "tp", axis=0, tiled=True)
+    whole = from_everyone(normed_layer_input).reshape(rows, width)
     input_column_span = lax.dynamic_slice_in_dim(whole, col_start, feature_column_span, 1)
     input_part = select_block(
         jnp.dot(input_column_span, adapter_down_maps, preferred_element_type=jnp.float32),
         tenant_match_mask,
     )
-    reduced_input = lax.psum(input_part, "tp")
+    reduced_input = from_everyone(input_part).sum(axis=0)
     input_spread_rows = spread_rows(reduced_input, tenant_match_mask)
     gate_activation = jnp.dot(whole, gate_weight, preferred_element_type=jnp.float32)
+    up_val = jnp.dot(whole, up_weight, preferred_element_type=jnp.float32)
     gate_activation = gate_activation + adapter_scale * jnp.dot(
         input_spread_rows, adapter_up_maps, preferred_element_type=jnp.float32
     )
-    up_val = jnp.dot(whole, up_weight, preferred_element_type=jnp.float32)
     sigmoid_gate = jax.nn.sigmoid(gate_activation)
     hidden_grad = hidden_unit_gradient.astype(jnp.float32)
     gate_gradient = (
@@ -69,7 +78,7 @@
     gradient_portion = select_block(
         contracted_columns(gate_gradient, adapter_up_maps), tenant_match_mask
     )
-    reduced_gradient = lax.psum(gradient_portion, "tp")
+    reduced_gradient = from_everyone(gradient_portion).sum(axis=0)
     gradient_spread_rows = spread_rows(reduced_gradient, tenant_match_mask)
     down_map_gradient = (
         adapter_scale * contracted_rows(input_column_span, gradient_spread_rows)
@@ -80,15 +89,24 @@
     adapter_column_span = adapter_scale * contracted_columns(
         gradient_spread_rows, adapter_down_maps
     )
-    running_sum = lax.psum_scatter(
-        contracted_columns(gate_gradient, gate_weight) + contracted_columns(d_up, up_weight),
-        "tp",
-        scatter_dimension=0,
-        tiled=True,
+    half = width // 2
+    arrived = []
+    for start in (0, half):
+        part = contracted_columns(
+            gate_gradient, gate_weight[start : start + half]
+        ) + contracted_columns(d_up, up_weight[start : start + half])
+        part = part.astype(jnp.bfloat16)
+        if start > 0:
+            part = jnp.concatenate([part, adapter_column_span.astype(jnp.bfloat16)], axis=1)
+        part = part.reshape(count, own_rows, part.shape[1])
+        arrived.append(
+            lax.all_to_all(part, "tp", split_axis=0, concat_axis=0, tiled=True).astype(jnp.float32)
+        )
+    adapter_part = arrived[1][:, :, half:].transpose(1, 0, 2).reshape(own_rows, width)
+    running_sum = jnp.concatenate(
+        [arrived[0].sum(axis=0), arrived[1][:, :, :half].sum(axis=0)], axis=1
     )
-    running_sum = running_sum + lax.all_to_all(
-        adapter_column_span, "tp", split_axis=0, concat_axis=1, tiled=True
-    )
+    running_sum = running_sum + adapter_part
     return (running_sum.astype(jnp.bfloat16), down_map_gradient, up_map_gradient)
 
 

time: 323 us -> 139 us (0.43)
  blocking collectives: 140 us -> 0 us
  waiting for transfers between devices: 86.2 us -> 22.2 us
  starting transfers between devices: 3.71 us -> 27 us
  between operations: 14.9 us -> 0.99 us
  matrix products: 71.8 us -> 76.6 us
  local copies, waits for them, and re-layouts: 3.5 us -> 7.64 us
    psum x2 -> x0, blocking collectives: 115 us -> none  [the longest x1 57.8 us: local(): reduced_input = lax.psum(input_part, 'tp')]
    unnamed x2 -> x0, waiting for transfers between devices: 86.2 us -> none
    all_gather x1 -> x0, blocking collectives: 24.9 us -> none  [local(): whole = lax.all_gather(normed_layer_input, 'tp', axis=0, tiled=True)]
    all_to_all x1 -> x5, starting transfers between devices: 3.49 us -> 27 us  [the longest x3 17.5 us: from_everyone(): return lax.all_to_all(copies, 'tp', split_axis=0, concat_axis=0, tiled=True)]
    all_to_all x1 -> x5, waiting for transfers between devices: 0.01 us -> 22.2 us  [the longest x3 14.4 us: from_everyone(): return lax.all_to_all(copies, 'tp', split_axis=0, concat_axis=0, tiled=True)]
    dot_general x4 -> x6, matrix products: 34.5 us -> 38.3 us  [contracted_columns(): lax.dot_general(left, right, (((1,), (1,)), ((), ())), preferred_element_...]
  transfers between devices with their start and end apart: 2 -> 5, of which waited for: 1 -> 3; matrix products, arithmetic and copies ran while one was open for 12% -> 32% of each run, Pallas kernels for 0% -> 0%
where the time goes in v1:
time: 139 us
  matrix products  76.6 us (55%)
  starting transfers between devices  27 us (19%)
  waiting for transfers between devices  22.2 us (16%)
  local copies, waits for them, and re-layouts  7.64 us (5%)
  other arithmetic  4.22 us (3%)
    dot_general x6, matrix products, contracted_columns(): lax.dot_general(left, right, (((1,), (1,)), ((), ())), preferred_element_...  38.3 us
    all_to_all x3, starting transfers between devices, from_everyone(): return lax.all_to_all(copies, 'tp', split_axis=0, concat_axis=0, tiled=True)  17.5 us
    all_to_all x3, waiting for transfers between devices, from_everyone(): return lax.all_to_all(copies, 'tp', split_axis=0, concat_axis=0, tiled=True)  14.4 us
    dot_general x1, matrix products, local(): up_val = jnp.dot(whole, up_weight, preferred_element_type=jnp.float32)  12 us
    dot_general x1, matrix products, local(): jnp.dot(whole, gate_weight, preferred_element_type=jnp.float32)  11.9 us
    all_to_all x2, starting transfers between devices, local(): lax.all_to_all(part, 'tp', split_axis=0, concat_axis=0, tiled=True)  9.53 us
    dot_general x2, matrix products, contracted_rows(): lax.dot_general(left, right, (((0,), (0,)), ((), ())), preferred_element_...  8.71 us
    all_to_all x2, waiting for transfers between devices, local(): lax.all_to_all(part, 'tp', split_axis=0, concat_axis=0, tiled=True)  7.72 us
  transfers between devices with their start and end apart: 5, of which 3 were waited for; matrix products, arithmetic and copies ran while one was open for 32% of the time, Pallas kernels for 0%

profile of v1, /device:TPU:0, one launch (start us, length us, event | category | flops | bytes accessed | tf_op | source)
XLA Modules:
  0.0 138.6 jit_solution(18171383047407999276)
XLA Ops:
  0.6 0.0 copy-start
  0.6 2.1 %broadcast_in_dim.6 = bf16[16,2,8192]{2,1,0:T(2,128)(2,1)} broadcast(bf16[2,8192]{1,0:T(2,128)(2,1)} %param.7), dimensions={1,2} | broadcast | bytes 557056 | tf_op jit(solution)/shard_map/broadcast_in_dim | solution.py:39
  2.8 7.4 %all-to-all-start = ((bf16[16,2,8192]{2,1,0:T(2,128)(2,1)}), bf16[16,2,8192]{2,1,0:T(2,128)(2,1)S(1)}, u32[]{:S(2)}, u32[]{:S(2)}) async-start(bf16[16,2,8192]{2,1,0:T(2,128)(2,1)} %broadcast_in_dim.6), calls=%async_computation | async-start | bytes 1048576 | tf_op jit(solution)/shard_map/all_to_all | solution.py:40
  10.2 0.0 copy-start.3
  10.2 14.4 %all-to-all-done = bf16[16,2,8192]{2,1,0:T(2,128)(2,1)S(1)} async-done(((bf16[16,2,8192]{2,1,0:T(2,128)(2,1)}), bf16[16,2,8192]{2,1,0:T(2,128)(2,1)S(1)}, u32[]{:S(2)}, u32[]{:S(2)}) %all-to-all-start) | async-done | bytes 524320 | tf_op jit(solution)/shard_map/all_to_all | solution.py:40
  24.6 0.2 reshape.73
  24.8 0.0 copy-done
  24.8 1.1 convolution_select_fusion.1
  25.9 0.2 reshape.74
  26.2 0.1 reduce_sum.54
  26.3 0.8 reshape.79
  27.1 4.1 %all-to-all-start.1 = ((f32[16,1,2048]{2,1,0:T(1,128)}), f32[16,1,2048]{2,1,0:T(1,128)S(1)}, u32[]{:S(2)}, u32[]{:S(2)}) async-start(f32[16,1,2048]{2,1,0:T(1,128)} %reshape.79), calls=%async_computation.1 | async-start | bytes 262144 | tf_op jit(solution)/shard_map/all_to_all | solution.py:40
  31.2 0.0 copy-start.6
  31.2 0.0 copy-start.5
  31.3 11.9 %fusion.43 = f32[32,1792]{1,0:T(8,128)S(1)} fusion(bf16[32,8192]{1,0:T(8,128)(2,1)S(1)} %reshape.73, bf16[8192,1792]{1,0:T(8,128)(2,1)} %param.9), kind=kOutput, calls=%fused_computation.48 | convolution fusion | flops 939524096 | bytes 30113792 | tf_op jit(solution)/shard_map/dot_general | solution.py:67
  43.2 0.0 all-to-all-done.1
  43.2 0.5 broadcast.69
  43.8 0.9 reduce
  44.7 0.1 reshape.80
  44.9 0.3 tile.9
  45.1 0.0 copy-done.6
  45.1 4.5 %fusion.20 = f32[32,1792]{1,0:T(8,128)S(1)} fusion(f32[32,1792]{1,0:T(8,128)S(1)} %fusion.43, bf16[2048,1792]{1,0:T(8,128)(2,1)} %param.12, bf16[32,2048]{1,0:T(8,128)(2,1)S(1)} %tile.9, s32[2048]{0:T(1024)S(1)} %add_select_fusion, s32[32]{0:T(128)S(1)} %copy-done.6), kind=kOutput, calls=%fused_computation.15 | convolution fusion | flops 235126784 | bytes 7938176 | tf_op jit(solution)/shard_map/dot_general | solution.py:69
  49.6 0.0 copy-done.5
  49.7 12.0 %fusion.23 = bf16[32,1792]{1,0:T(8,128)(2,1)S(1)} fusion(bf16[32,8192]{1,0:T(8,128)(2,1)S(1)} %reshape.73, bf16[8192,1792]{1,0:T(8,128)(2,1)} %param.10, bf16[32,1792]{1,0:T(8,128)(2,1)S(1)} %copy-done.5, f32[32,1792]{1,0:T(8,128)S(1)} %fusion.20), kind=kOutput, calls=%fused_computation.21 | convolution fusion | flops 940154880 | bytes 30343168 | tf_op jit(solution)/shard_map/dot_general | solution.py:68
  61.7 0.0 copy-start.1
  61.7 0.0 slice-start
  61.7 8.6 %fusion = f32[32,4096]{1,0:T(8,128)} fusion(bf16[8192,1792]{1,0:T(8,128)(2,1)} %param.10, f32[32,1792]{1,0:T(8,128)S(1)} %fusion.20, bf16[32,1792]{1,0:T(8,128)(2,1)S(1)} %copy-done.5), kind=kOutput, calls=%fused_computation.1 | convolution fusion | flops 470163456 | bytes 15548416 | tf_op jit(solution)/shard_map/dot_general | solution.py:28
  70.3 8.6 %fusion.4 = f32[32,4096]{1,0:T(8,128)} fusion(bf16[8192,1792]{1,0:T(8,128)(2,1)} %param.10, f32[32,1792]{1,0:T(8,128)S(1)} %fusion.20, bf16[32,1792]{1,0:T(8,128)(2,1)S(1)} %copy-done.5), kind=kOutput, calls=%fused_computation.5 | convolution fusion | flops 470163456 | bytes 15548416 | tf_op jit(solution)/shard_map/dot_general | solution.py:28
  78.9 0.0 copy-done.3
  78.9 0.0 copy-done.1
  78.9 0.0 slice-done
  78.9 0.0 slice-done.1
  78.9 2.2 %convolution_select_fusion = f32[32,2048]{1,0:T(8,128)S(1)} fusion(bf16[32,1792]{1,0:T(8,128)(2,1)S(1)} %fusion.23, bf16[2048,1792]{1,0:T(8,128)(2,1)S(1)} %bitcast.16, s32[2048]{0:T(1024)S(1)} %add_select_fusion, s32[32]{0:T(128)S(1)} %copy-done.6), kind=kOutput, calls=%fused_computation.19 | convolution fusion | flops 235012096 | bytes 7725184 | tf_op jit(solution)/shard_map/dot_general | solution.py:28
  81.1 0.2 reshape.76
  81.3 0.0 copy-start.2
  81.4 0.1 reduce_sum.57
  81.5 0.8 reshape.81
  82.3 6.0 %all-to-all-start.3 = ((f32[16,1,2048]{2,1,0:T(1,128)}), f32[16,1,2048]{2,1,0:T(1,128)S(1)}, u32[]{:S(2)}, u32[]{:S(2)}) async-start(f32[16,1,2048]{2,1,0:T(1,128)} %reshape.81), calls=%async_computation.3 | async-start | bytes 262144 | tf_op jit(solution)/shard_map/all_to_all | solution.py:40
  88.3 0.0 copy-start.8
  88.3 0.0 copy-start.4
  88.3 0.0 copy-start.7
  88.4 10.4 %fusion.14 = bf16[32,4096]{1,0:T(8,128)(2,1)} fusion(f32[32,4096]{1,0:T(8,128)} %fusion, bf16[32,1792]{1,0:T(8,128)(2,1)} %copy-done.1, bf16[8192,1792]{1,0:T(8,128)(2,1)} %param.9), kind=kOutput, calls=%fused_computation.11 | convolution fusion | flops 470024192 | bytes 15581184 | tf_op jit(solution)/shard_map/dot_general | solution.py:28
  98.7 0.0 copy-done.2
  98.7 0.0 copy-done.8
  98.7 7.8 %fusion.17 = bf16[32,4096]{1,0:T(8,128)(2,1)S(1)} fusion(f32[32,4096]{1,0:T(8,128)S(1)} %copy-done.8, bf16[32,1792]{1,0:T(8,128)(2,1)S(1)} %copy-done.2, bf16[8192,1792]{1,0:T(8,128)(2,1)} %param.9), kind=kOutput, calls=%fused_computation.12 | convolution fusion | flops 470024192 | bytes 15581184 | tf_op jit(solution)/shard_map/dot_general | solution.py:28
  106.6 0.9 reshape.75
  107.5 0.0 all-to-all-done.3
  107.5 6.0 %all-to-all-start.2 = ((bf16[16,2,4096]{2,1,0:T(2,128)(2,1)}), bf16[16,2,4096]{2,1,0:T(2,128)(2,1)S(1)}, u32[]{:S(2)}, u32[]{:S(2)}) async-start(bf16[16,2,4096]{2,1,0:T(2,128)(2,1)} %reshape.75), calls=%async_computation.2 | async-start | bytes 524288 | tf_op jit(solution)/shard_map/all_to_all | solution.py:103
  113.5 0.9 reduce.1
  114.4 0.1 reshape.82
  114.6 0.3 tile.21
  114.8 0.0 copy-done.7
  114.9 0.7 fusion.24
  115.6 1.0 pad_maximum_fusion
  116.6 0.8 reshape.77
  117.4 6.1 %all-to-all-done.2 = bf16[16,2,4096]{2,1,0:T(2,128)(2,1)S(1)} async-done(((bf16[16,2,4096]{2,1,0:T(2,128)(2,1)}), bf16[16,2,4096]{2,1,0:T(2,128)(2,1)S(1)}, u32[]{:S(2)}, u32[]{:S(2)}) %all-to-all-start.2) | async-done | bytes 262176 | tf_op jit(solution)/shard_map/all_to_all | solution.py:103
  123.5 3.5 %all-to-all-start.4 = ((bf16[16,2,4608]{2,1,0:T(2,128)(2,1)}), bf16[16,2,4608]{2,1,0:T(2,128)(2,1)S(1)}, u32[]{:S(2)}, u32[]{:S(2)}) async-start(bf16[16,2,4608]{2,1,0:T(2,128)(2,1)} %reshape.77), calls=%async_computation.4 | async-start | bytes 589824 | tf_op jit(solution)/shard_map/all_to_all | solution.py:103
  127.0 5.9 %multiply_convert_fusion = bf16[2048,1792]{1,0:T(8,128)(2,1)} fusion(bf16[32,1792]{1,0:T(8,128)(2,1)S(1)} %copy-done.2, bf16[32,2048]{1,0:T(8,128)(2,1)S(1)} %tile.9, s32[2048]{0:T(1024)} %copy-done.3, s32[32]{0:T(128)} %param.13), kind=kOutput, calls=%fused_computation | convolution fusion | flops 242352128 | bytes 7594112 | tf_op jit(solution)/shard_map/dot_general | solution.py:22
  133.0 2.8 %multiply_convert_fusion.1 = bf16[512,2048]{1,0:T(8,128)(2,1)} fusion(bf16[32,8192]{1,0:T(8,128)(2,1)S(1)} %reshape.73, s32[]{:T(128)S(6)} %select_n.14, bf16[32,2048]{1,0:T(8,128)(2,1)S(1)} %tile.21, s32[2048]{0:T(1024)} %copy-done.3, s32[32]{0:T(128)} %param.13), kind=kOutput, calls=%fused_computation.13 | convolution fusion | flops 69337088 | bytes 2269316 | tf_op jit(solution)/shard_map/dot_general | solution.py:22
  135.8 0.2 convert_reduce_fusion
  136.0 1.6 %all-to-all-done.4 = bf16[16,2,4608]{2,1,0:T(2,128)(2,1)S(1)} async-done(((bf16[16,2,4608]{2,1,0:T(2,128)(2,1)}), bf16[16,2,4608]{2,1,0:T(2,128)(2,1)S(1)}, u32[]{:S(2)}, u32[]{:S(2)}) %all-to-all-start.4) | async-done | bytes 294944 | tf_op jit(solution)/shard_map/all_to_all | solution.py:103
  137.6 0.2 convert_element_type.49
  137.8 0.1 slice_reduce_fusion
  137.9 0.7 fusion.29
  (11 shorter events, 0.2 us)
Async XLA Ops:
  0.6 24.2 %copy-start = (bf16[512,2048]{1,0:T(8,128)(2,1)S(1)}, bf16[512,2048]{1,0:T(8,128)(2,1)}, u32[]{:S(2)}) copy-start(bf16[512,2048]{1,0:T(8,128)(2,1)} %param.11) | copy-start | bytes 6291460
  2.8 21.9 %all-to-all-start = ((bf16[16,2,8192]{2,1,0:T(2,128)(2,1)}), bf16[16,2,8192]{2,1,0:T(2,128)(2,1)S(1)}, u32[]{:S(2)}, u32[]{:S(2)}) async-start(bf16[16,2,8192]{2,1,0:T(2,128)(2,1)} %broadcast_in_dim.6), calls=%async_computation | async-start | bytes 1048576 | tf_op jit(solution)/shard_map/all_to_all | solution.py:40
  10.2 68.7 %copy-start.3 = (s32[2048]{0:T(1024)}, s32[2048]{0:T(1024)S(1)}, u32[]{:S(2)}) copy-start(s32[2048]{0:T(1024)S(1)} %add_select_fusion) | copy-start | bytes 24580
  27.1 16.1 %all-to-all-start.1 = ((f32[16,1,2048]{2,1,0:T(1,128)}), f32[16,1,2048]{2,1,0:T(1,128)S(1)}, u32[]{:S(2)}, u32[]{:S(2)}) async-start(f32[16,1,2048]{2,1,0:T(1,128)} %reshape.79), calls=%async_computation.1 | async-start | bytes 262144 | tf_op jit(solution)/shard_map/all_to_all | solution.py:40
  31.2 13.9 %copy-start.6 = (s32[32]{0:T(128)S(1)}, s32[32]{0:T(128)}, u32[]{:S(2)}) copy-start(s32[32]{0:T(128)} %param.13) | copy-start | bytes 388
  31.2 18.4 %copy-start.5 = (bf16[32,1792]{1,0:T(8,128)(2,1)S(1)}, bf16[32,1792]{1,0:T(8,128)(2,1)}, u32[]{:S(2)}) copy-start(bf16[32,1792]{1,0:T(8,128)(2,1)} %param.8) | copy-start | bytes 344068
  61.7 17.2 %copy-start.1 = (bf16[32,1792]{1,0:T(8,128)(2,1)}, bf16[32,1792]{1,0:T(8,128)(2,1)S(1)}, u32[]{:S(2)}) copy-start(bf16[32,1792]{1,0:T(8,128)(2,1)S(1)} %fusion.23) | copy-start | bytes 344068
  61.7 17.2 %slice-start = ((s8[7340032]{0:T(1024)(128)(4,1)}), s8[4194304]{0:T(1024)(128)(4,1)S(1)}, s32[]{:S(2)}) async-start(s8[7340032]{0:T(1024)(128)(4,1)} %bitcast.15), calls=%async_computation.5 | async-start | bytes 8388608
  70.3 8.6 %slice-start.1 = ((s8[7340032]{0:T(1024)(128)(4,1)}), s8[3145728]{0:T(1024)(128)(4,1)S(1)}, s32[]{:S(2)}) async-start(s8[7340032]{0:T(1024)(128)(4,1)} %bitcast.15), calls=%async_computation.6 | async-start | bytes 6291456
  81.3 17.4 %copy-start.2 = (bf16[32,1792]{1,0:T(8,128)(2,1)S(1)}, bf16[32,1792]{1,0:T(8,128)(2,1)}, u32[]{:S(2)}) copy-start(bf16[32,1792]{1,0:T(8,128)(2,1)} %copy-done.1) | copy-start | bytes 344068
  82.3 25.2 %all-to-all-start.3 = ((f32[16,1,2048]{2,1,0:T(1,128)}), f32[16,1,2048]{2,1,0:T(1,128)S(1)}, u32[]{:S(2)}, u32[]{:S(2)}) async-start(f32[16,1,2048]{2,1,0:T(1,128)} %reshape.81), calls=%async_computation.3 | async-start | bytes 262144 | tf_op jit(solution)/shard_map/all_to_all | solution.py:40
  88.3 10.4 %copy-start.8 = (f32[32,4096]{1,0:T(8,128)S(1)}, f32[32,4096]{1,0:T(8,128)}, u32[]{:S(2)}) copy-start(f32[32,4096]{1,0:T(8,128)} %fusion.4) | copy-start | bytes 1572868
  88.3 26.5 %copy-start.4 = (s32[2048]{0:T(1024)S(1)}, s32[2048]{0:T(1024)}, u32[]{:S(2)}) copy-start(s32[2048]{0:T(1024)} %copy-done.3) | copy-start | bytes 24580
  88.3 26.5 %copy-start.7 = (s32[32]{0:T(128)S(1)}, s32[32]{0:T(128)}, u32[]{:S(2)}) copy-start(s32[32]{0:T(128)} %param.13) | copy-start | bytes 388
  107.5 16.0 %all-to-all-start.2 = ((bf16[16,2,4096]{2,1,0:T(2,128)(2,1)}), bf16[16,2,4096]{2,1,0:T(2,128)(2,1)S(1)}, u32[]{:S(2)}, u32[]{:S(2)}) async-start(bf16[16,2,4096]{2,1,0:T(2,128)(2,1)} %reshape.75), calls=%async_computation.2 | async-start | bytes 524288 | tf_op jit(solution)/shard_map/all_to_all | solution.py:103
  123.5 14.1 %all-to-all-start.4 = ((bf16[16,2,4608]{2,1,0:T(2,128)(2,1)}), bf16[16,2,4608]{2,1,0:T(2,128)(2,1)S(1)}, u32[]{:S(2)}, u32[]{:S(2)}) async-start(bf16[16,2,4608]{2,1,0:T(2,128)(2,1)} %reshape.77), calls=%async_computation.4 | async-start | bytes 589824 | tf_op jit(solution)/shard_map/all_to_all | solution.py:103

commit v2 on v1

--- a/solution.py
+++ b/solution.py
@@ -34,10 +34,48 @@
     return (jnp.tile(low_rows, (1, TENANT_COUNT)) * tenant_match_mask).astype(jnp.bfloat16)
 
 
-def from_everyone(block):
+def swap(block, hop):
     count = lax.axis_size("tp")
-    copies = jnp.broadcast_to(block[None], (count,) + block.shape)
-    return lax.all_to_all(copies, "tp", split_axis=0, concat_axis=0, tiled=True)
+    return lax.ppermute(block, "tp", [(i, i ^ hop) for i in range(count)])
+
+
+def hops():
+    count = lax.axis_size("tp")
+    return [1 << bit for bit in range(count.bit_length() - 1)]
+
+
+def gathered(block):
+    count = lax.axis_size("tp")
+    held = {0: block}
+    for hop in reversed(hops()):
+        order = sorted(held)
+        stacked = jnp.concatenate([held[p] for p in order], axis=0) if len(order) > 1 else block
+        came = swap(stacked, hop)
+        size = block.shape[0]
+        for k, p in enumerate(order):
+            held[p ^ hop] = came[k * size : (k + 1) * size]
+    return jnp.concatenate([held[p] for p in range(count)], axis=0)
+
+
+def summed_directly(block):
+    total = block
+    for hop in range(1, lax.axis_size("tp")):
+        total = total + swap(block, hop)
+    return total
+
+
+def summed_by_doubling(block):
+    for hop in hops():
+        block = block + swap(block, hop)
+    return block
+
+
+def scattered_sum(part):
+    for hop in reversed(hops()):
+        rows = part.shape[0] // 2
+        came = swap(part[rows:].astype(jnp.bfloat16), hop)
+        part = part[:rows] + came.astype(jnp.float32)
+    return part
 
 
 def local(
@@ -50,19 +88,31 @@
     token_tenant_index,
 ):
     count = lax.axis_size("tp")
+    own = lax.axis_index("tp")
     own_rows, width = normed_layer_input.shape
     rows = own_rows * count
+    row = jnp.arange(rows, dtype=jnp.int32)
+    source = ((row // own_rows) ^ own) * own_rows + row % own_rows
+    turn = (source[:, None] == row[None, :]).astype(jnp.float32)
+
+    def turned(block):
+        return jnp.dot(turn, block, precision=lax.Precision.HIGHEST)
+
+    tenants = jnp.where(source[:, None] == row[None, :], token_tenant_index[None, :], 0).sum(axis=1)
     columns = lax.broadcasted_iota(jnp.int32, (1, TENANT_COUNT * ADAPTER_RANK), 1) // ADAPTER_RANK
-    tenant_match_mask = (token_tenant_index[:, None] == columns).astype(jnp.float32)
+    tenant_match_mask = (tenants[:, None] == columns).astype(jnp.float32)
+    hidden_grad = jnp.dot(
+        turn.astype(jnp.bfloat16), hidden_unit_gradient, preferred_element_type=jnp.float32
+    )
     feature_column_span = adapter_down_maps.shape[0]
-    col_start = lax.axis_index("tp") * feature_column_span
-    whole = from_everyone(normed_layer_input).reshape(rows, width)
+    col_start = own * feature_column_span
+    whole = gathered(normed_layer_input)
     input_column_span = lax.dynamic_slice_in_dim(whole, col_start, feature_column_span, 1)
     input_part = select_block(
         jnp.dot(input_column_span, adapter_down_maps, preferred_element_type=jnp.float32),
         tenant_match_mask,
     )
-    reduced_input = from_everyone(input_part).sum(axis=0)
+    reduced_input = turned(summed_directly(turned(input_part)))
     input_spread_rows = spread_rows(reduced_input, tenant_match_mask)
     gate_activation = jnp.dot(whole, gate_weight, preferred_element_type=jnp.float32)
     up_val = jnp.dot(whole, up_weight, preferred_element_type=jnp.float32)
@@ -70,7 +120,6 @@
         input_spread_rows, adapter_up_maps, preferred_element_type=jnp.float32
     )
     sigmoid_gate = jax.nn.sigmoid(gate_activation)
-    hidden_grad = hidden_unit_gradient.astype(jnp.float32)
     gate_gradient = (
         hidden_grad * up_val * sigmoid_gate * (1.0 + gate_activation * (1.0 - sigmoid_gate))
     ).astype(jnp.bfloat16)
@@ -78,7 +127,7 @@
     gradient_portion = select_block(
         contracted_columns(gate_gradient, adapter_up_maps), tenant_match_mask
     )
-    reduced_gradient = from_everyone(gradient_portion).sum(axis=0)
+    reduced_gradient = turned(summed_by_doubling(turned(gradient_portion)))
     gradient_spread_rows = spread_rows(reduced_gradient, tenant_match_mask)
     down_map_gradient = (
         adapter_scale * contracted_rows(input_column_span, gradient_spread_rows)
@@ -90,23 +139,18 @@
         gradient_spread_rows, adapter_down_maps
     )
     half = width // 2
-    arrived = []
+    sums = []
     for start in (0, half):
         part = contracted_columns(
             gate_gradient, gate_weight[start : start + half]
         ) + contracted_columns(d_up, up_weight[start : start + half])
-        part = part.astype(jnp.bfloat16)
-        if start > 0:
-            part = jnp.concatenate([part, adapter_column_span.astype(jnp.bfloat16)], axis=1)
-        part = part.reshape(count, own_rows, part.shape[1])
-        arrived.append(
-            lax.all_to_all(part, "tp", split_axis=0, concat_axis=0, tiled=True).astype(jnp.float32)
-        )
-    adapter_part = arrived[1][:, :, half:].transpose(1, 0, 2).reshape(own_rows, width)
-    running_sum = jnp.concatenate(
-        [arrived[0].sum(axis=0), arrived[1][:, :, :half].sum(axis=0)], axis=1
-    )
-    running_sum = running_sum + adapter_part
+        sums.append(scattered_sum(part))
+    adapter_part = lax.all_to_all(
+        turned(adapter_column_span).astype(jnp.bfloat16).reshape(count, own_rows, -1),
+        "tp", split_axis=0, concat_axis=0, tiled=True,
+    ).astype(jnp.float32)
+    adapter_part = adapter_part.transpose(1, 0, 2).reshape(own_rows, width)
+    running_sum = jnp.concatenate(sums, axis=1) + adapter_part
     return (running_sum.astype(jnp.bfloat16), down_map_gradient, up_map_gradient)
 
 

time: 139 us -> 156 us (1.12)
  starting transfers between devices: 27 us -> 43.2 us
  matrix products: 76.6 us -> 74.4 us
    ppermute x0 -> x31, starting transfers between devices: none -> 39.7 us  [swap(): return lax.ppermute(block, 'tp', [(i, i ^ hop) for i in range(count)])]
    all_to_all x5 -> x1, starting transfers between devices: 27 us -> 3.5 us  [local(): lax.all_to_all(turned(adapter_column_span).astype(jnp.bfloat16).reshape(c...]
    ppermute x0 -> x31, waiting for transfers between devices: none -> 18.5 us  [swap(): return lax.ppermute(block, 'tp', [(i, i ^ hop) for i in range(count)])]
    all_to_all x5 -> x1, waiting for transfers between devices: 22.2 us -> 4.51 us  [local(): lax.all_to_all(turned(adapter_column_span).astype(jnp.bfloat16).reshape(c...]
    concatenate x0 -> x2, local copies, waits for them, and re-layouts: none -> 2.65 us  [the longest x1 1.52 us: gathered(): return jnp.concatenate([held[p] for p in range(count)], axis=0)]
    dot_general x6, matrix products: 38.3 us -> 35.7 us  [contracted_columns(): lax.dot_general(left, right, (((1,), (1,)), ((), ())), preferred_element_...]
    broadcast_in_dim x3 -> x0, local copies, waits for them, and re-layouts: 2.14 us -> none  [from_everyone(): copies = jnp.broadcast_to(block[None], (count,) + block.shape)]
    add x0 -> x12, other arithmetic: none -> 2.06 us  [the longest x8 2.04 us: scattered_sum(): part = part[:rows] + came.astype(jnp.float32)]
  transfers between devices with their start and end apart: 5 -> 32, of which waited for: 3 -> 14; matrix products, arithmetic and copies ran while one was open for 32% -> 30% of each run, Pallas kernels for 0% -> 0%
where the time goes in v2:
time: 156 us; the launch traced here: 155 us
  matrix products  74.4 us (48%)
  starting transfers between devices  43.2 us (28%)
  waiting for transfers between devices  23 us (15%)
  local copies, waits for them, and re-layouts  7.88 us (5%)
  other arithmetic  5.47 us (4%)
    ppermute x31, starting transfers between devices, swap(): return lax.ppermute(block, 'tp', [(i, i ^ hop) for i in range(count)])  39.7 us
    dot_general x6, matrix products, contracted_columns(): lax.dot_general(left, right, (((1,), (1,)), ((), ())), preferred_element_...  35.7 us
    ppermute x31, waiting for transfers between devices, swap(): return lax.ppermute(block, 'tp', [(i, i ^ hop) for i in range(count)])  18.5 us
    dot_general x1, matrix products, local(): up_val = jnp.dot(whole, up_weight, preferred_element_type=jnp.float32)  12.4 us
    dot_general x1, matrix products, local(): jnp.dot(whole, gate_weight, preferred_element_type=jnp.float32)  12.1 us
    dot_general x2, matrix products, contracted_rows(): lax.dot_general(left, right, (((0,), (0,)), ((), ())), preferred_element_...  7.32 us
    all_to_all x1, waiting for transfers between devices, local(): lax.all_to_all(turned(adapter_column_span).astype(jnp.bfloat16).reshape(c...  4.51 us
    dot_general x1, matrix products, local(): jnp.dot(input_spread_rows, adapter_up_maps, preferred_element_type=jnp.fl...  4.5 us
  transfers between devices with their start and end apart: 32, of which 14 were waited for; matrix products, arithmetic and copies ran while one was open for 30% of the time, Pallas kernels for 0%

profile of v2, /device:TPU:0, one launch (start us, length us, event | category | flops | bytes accessed | tf_op | source)
XLA Modules:
  0.0 155.0 jit_solution(3984324539439892391)
XLA Ops:
  0.6 4.1 %collective-permute-start = (bf16[2,8192]{1,0:T(2,128)(2,1)}, bf16[2,8192]{1,0:T(2,128)(2,1)S(1)}, u32[]{:S(2)}, u32[]{:S(2)}) collective-permute-start(bf16[2,8192]{1,0:T(2,128)(2,1)} %param.7), channel_id=1, source_target_pairs={{0,8},{1,9},{2,10},{3,11},{4,12},{5,13},{6,14},{7,15},{8,0},{9,1},... | collective-permute-start | bytes 98312 | tf_op jit(solution)/shard_map/ppermute | solution.py:39
  4.7 2.5 %collective-permute-done = bf16[2,8192]{1,0:T(2,128)(2,1)S(1)} collective-permute-done((bf16[2,8192]{1,0:T(2,128)(2,1)}, bf16[2,8192]{1,0:T(2,128)(2,1)S(1)}, u32[]{:S(2)}, u32[]{:S(2)}) %collective-permute-start) | collective-permute-done | bytes 32800 | tf_op jit(solution)/shard_map/ppermute | solution.py:39
  7.2 0.8 pad_maximum_fusion.1
  8.0 1.6 %collective-permute-start.1 = (bf16[4,8192]{1,0:T(4,128)(2,1)S(1)}, bf16[4,8192]{1,0:T(4,128)(2,1)S(1)}, u32[]{:S(2)}, u32[]{:S(2)}) collective-permute-start(bf16[4,8192]{1,0:T(4,128)(2,1)S(1)} %pad_maximum_fusion.1), channel_id=1, source_target_pairs={{0,4},{1,5},{2,6},{3,7},{4,0},{5,1},{6,2},{7,3},{8,12},{9,13},{10,... | collective-permute-start | bytes 196616 | tf_op jit(solution)/shard_map/ppermute | solution.py:39
  9.7 2.7 %collective-permute-done.1 = bf16[4,8192]{1,0:T(4,128)(2,1)S(1)} collective-permute-done((bf16[4,8192]{1,0:T(4,128)(2,1)S(1)}, bf16[4,8192]{1,0:T(4,128)(2,1)S(1)}, u32[]{:S(2)}, u32[]{:S(2)}) %collective-permute-start.1) | collective-permute-done | bytes 65568 | tf_op jit(solution)/shard_map/ppermute | solution.py:39
  12.4 0.9 pad_maximum_fusion
  13.3 1.8 %collective-permute-start.2 = (bf16[8,8192]{1,0:T(8,128)(2,1)S(1)}, bf16[8,8192]{1,0:T(8,128)(2,1)S(1)}, u32[]{:S(2)}, u32[]{:S(2)}) collective-permute-start(bf16[8,8192]{1,0:T(8,128)(2,1)S(1)} %pad_maximum_fusion), channel_id=1, source_target_pairs={{0,2},{1,3},{2,0},{3,1},{4,6},{5,7},{6,4},{7,5},{8,10},{9,11},{10,... | collective-permute-start | bytes 393224 | tf_op jit(solution)/shard_map/ppermute | solution.py:39
  15.1 3.2 %collective-permute-done.2 = bf16[8,8192]{1,0:T(8,128)(2,1)S(1)} collective-permute-done((bf16[8,8192]{1,0:T(8,128)(2,1)S(1)}, bf16[8,8192]{1,0:T(8,128)(2,1)S(1)}, u32[]{:S(2)}, u32[]{:S(2)}) %collective-permute-start.2) | collective-permute-done | bytes 131104 | tf_op jit(solution)/shard_map/ppermute | solution.py:39
  18.5 1.1 concatenate.17
  19.7 0.8 select_reduce_fusion
  20.6 0.7 collective-permute-done.3
  21.4 1.5 concatenate.18
  22.9 0.5 convolution_select_fusion.1
  23.9 4.5 %collective-permute-start.18 = (f32[32,64]{1,0:T(8,128)S(1)}, f32[32,64]{1,0:T(8,128)S(1)}, u32[]{:S(2)}, u32[]{:S(2)}) collective-permute-start(f32[32,64]{1,0:T(8,128)S(1)} %fusion.41), channel_id=1, source_target_pairs={{0,15},{1,14},{2,13},{3,12},{4,11},{5,10},{6,9},{7,8},{8,7},{9,6},... | collective-permute-start | bytes 24584 | tf_op jit(solution)/shard_map/ppermute | solution.py:39
  28.4 0.3 collective-permute-start.17
  28.8 3.1 %collective-permute-start.16 = (f32[32,64]{1,0:T(8,128)S(1)}, f32[32,64]{1,0:T(8,128)S(1)}, u32[]{:S(2)}, u32[]{:S(2)}) collective-permute-start(f32[32,64]{1,0:T(8,128)S(1)} %fusion.41), channel_id=1, source_target_pairs={{0,13},{1,12},{2,15},{3,14},{4,9},{5,8},{6,11},{7,10},{8,5},{9,4},... | collective-permute-start | bytes 24584 | tf_op jit(solution)/shard_map/ppermute | solution.py:39
  31.9 0.4 collective-permute-start.15
  32.3 3.6 %collective-permute-start.13 = (f32[32,64]{1,0:T(8,128)S(1)}, f32[32,64]{1,0:T(8,128)S(1)}, u32[]{:S(2)}, u32[]{:S(2)}) collective-permute-start(f32[32,64]{1,0:T(8,128)S(1)} %fusion.41), channel_id=1, source_target_pairs={{0,10},{1,11},{2,8},{3,9},{4,14},{5,15},{6,12},{7,13},{8,2},{9,3},... | collective-permute-start | bytes 24584 | tf_op jit(solution)/shard_map/ppermute | solution.py:39
  35.9 2.5 %collective-permute-start.11 = (f32[32,64]{1,0:T(8,128)S(1)}, f32[32,64]{1,0:T(8,128)S(1)}, u32[]{:S(2)}, u32[]{:S(2)}) collective-permute-start(f32[32,64]{1,0:T(8,128)S(1)} %fusion.41), channel_id=1, source_target_pairs={{0,8},{1,9},{2,10},{3,11},{4,12},{5,13},{6,14},{7,15},{8,0},{9,1},... | collective-permute-start | bytes 24584 | tf_op jit(solution)/shard_map/ppermute | solution.py:39
  38.5 2.2 %collective-permute-start.10 = (f32[32,64]{1,0:T(8,128)S(1)}, f32[32,64]{1,0:T(8,128)S(1)}, u32[]{:S(2)}, u32[]{:S(2)}) collective-permute-start(f32[32,64]{1,0:T(8,128)S(1)} %fusion.41), channel_id=1, source_target_pairs={{0,7},{1,6},{2,5},{3,4},{4,3},{5,2},{6,1},{7,0},{8,15},{9,14},{10,... | collective-permute-start | bytes 24584 | tf_op jit(solution)/shard_map/ppermute | solution.py:39
  40.6 0.5 collective-permute-start.9
  41.2 1.2 collective-permute-start.8
  42.4 0.5 collective-permute-start.7
  42.9 1.2 collective-permute-start.6
  44.1 0.6 collective-permute-start.5
  44.7 0.7 collective-permute-done.9
  45.4 0.8 collective-permute-done.7
  46.1 1.7 %collective-permute-done.5 = f32[32,64]{1,0:T(8,128)S(1)} collective-permute-done((f32[32,64]{1,0:T(8,128)S(1)}, f32[32,64]{1,0:T(8,128)S(1)}, u32[]{:S(2)}, u32[]{:S(2)}) %collective-permute-start.5) | collective-permute-done | bytes 8224 | tf_op jit(solution)/shard_map/ppermute | solution.py:39
  48.1 0.3 tile.9
  48.3 4.5 %convolution_multiply_fusion = f32[32,1792]{1,0:T(8,128)S(1)} fusion(bf16[2048,1792]{1,0:T(8,128)(2,1)} %param.12, bf16[32,2048]{1,0:T(8,128)(2,1)S(1)} %tile.9, s32[2048]{0:T(1024)S(1)} %add_select_fusion, s32[32]{0:T(128)S(1)} %select_reduce_fusion), kind=kOutput, calls=%fused_computation.12 | convolution fusion | flops 235069440 | bytes 7708800 | tf_op jit(solution)/shard_map/dot_general | solution.py:119
  52.8 12.1 %convolution_add_fusion = f32[32,1792]{1,0:T(8,128)S(1)} fusion(f32[32,1792]{1,0:T(8,128)S(1)} %convolution_multiply_fusion, bf16[32,8192]{1,0:T(8,128)(2,1)S(1)} %concatenate.18, bf16[8192,1792]{1,0:T(8,128)(2,1)} %param.9), kind=kOutput, calls=%fused_computation.13 | convolution fusion | flops 939581440 | bytes 30343168 | tf_op jit(solution)/shard_map/dot_general | solution.py:117
  65.0 0.9 multiply_convert_fusion.2
  65.9 12.4 %fusion.16 = bf16[32,1792]{1,0:T(8,128)(2,1)S(1)} fusion(f32[32,1792]{1,0:T(8,128)S(1)} %get-tuple-element.18, bf16[32,8192]{1,0:T(8,128)(2,1)S(1)} %concatenate.18, bf16[8192,1792]{1,0:T(8,128)(2,1)} %param.10, f32[32,1792]{1,0:T(8,128)S(1)} %convolution_add_fusion), kind=kOutput, calls=%fused_computation.19 | convolution fusion | flops 940097536 | bytes 30457856 | tf_op jit(solution)/shard_map/dot_general | solution.py:118
  78.3 2.9 %convolution_select_fusion = f32[32,2048]{1,0:T(8,128)} fusion(bf16[32,1792]{1,0:T(8,128)(2,1)S(1)} %fusion.16, bf16[2048,1792]{1,0:T(8,128)(2,1)S(1)} %bitcast.22, s32[2048]{0:T(1024)S(1)} %add_select_fusion, s32[32]{0:T(128)S(1)} %select_reduce_fusion), kind=kOutput, calls=%fused_computation.17 | convolution fusion | flops 235012096 | bytes 7725184 | tf_op jit(solution)/shard_map/dot_general | solution.py:28
  81.3 1.1 reshape.92
  82.7 9.4 %fusion = f32[32,4096]{1,0:T(8,128)S(1)} fusion(bf16[32,1792]{1,0:T(8,128)(2,1)} %get-tuple-element.17, bf16[8192,1792]{1,0:T(8,128)(2,1)} %param.10), kind=kOutput, calls=%fused_computation.1 | convolution fusion | flops 469762048 | bytes 15319040 | tf_op jit(solution)/shard_map/dot_general | solution.py:28
  92.2 7.5 %fusion.11 = f32[32,4096]{1,0:T(8,128)S(1)} fusion(f32[32,4096]{1,0:T(8,128)S(1)} %fusion, bf16[32,1792]{1,0:T(8,128)(2,1)S(1)} %fusion.16, bf16[8192,1792]{1,0:T(8,128)(2,1)} %param.9), kind=kOutput, calls=%fused_computation.10 | convolution fusion | flops 469893120 | bytes 15843328 | tf_op jit(solution)/shard_map/dot_general | solution.py:28
  99.8 0.7 collective-permute-start.28
  100.4 7.5 %fusion.4 = f32[32,4096]{1,0:T(8,128)S(1)} fusion(bf16[32,1792]{1,0:T(8,128)(2,1)S(1)} %copy-done.3, bf16[8192,1792]{1,0:T(8,128)(2,1)} %param.10), kind=kOutput, calls=%fused_computation.5 | convolution fusion | flops 469762048 | bytes 15319040 | tf_op jit(solution)/shard_map/dot_general | solution.py:28
  108.0 1.5 collective-permute-start.29
  109.5 5.2 %multiply_convert_fusion = bf16[2048,1792]{1,0:T(8,128)(2,1)} fusion(bf16[32,1792]{1,0:T(8,128)(2,1)S(1)} %fusion.16, bf16[32,2048]{1,0:T(8,128)(2,1)S(1)} %tile.9, s32[2048]{0:T(1024)S(1)} %add_select_fusion, s32[32]{0:T(128)S(1)} %select_reduce_fusion), kind=kOutput, calls=%fused_computation | convolution fusion | flops 242352128 | bytes 7594112 | tf_op jit(solution)/shard_map/dot_general | solution.py:22
  114.7 0.7 slice.202
  115.4 2.6 %collective-permute-start.23 = (bf16[16,4096]{1,0:T(8,128)(2,1)}, bf16[16,4096]{1,0:T(8,128)(2,1)}, u32[]{:S(2)}, u32[]{:S(2)}) collective-permute-start(bf16[16,4096]{1,0:T(8,128)(2,1)} %slice.202), channel_id=1, source_target_pairs={{0,8},{1,9},{2,10},{3,11},{4,12},{5,13},{6,14},{7,15},{8,0},{9,1},... | collective-permute-start | bytes 393224 | tf_op jit(solution)/shard_map/ppermute | solution.py:39
  118.0 0.4 collective-permute-start.30
  118.4 7.5 %fusion.8 = f32[32,4096]{1,0:T(8,128)S(1)} fusion(f32[32,4096]{1,0:T(8,128)S(1)} %fusion.4, bf16[32,1792]{1,0:T(8,128)(2,1)S(1)} %fusion.16, bf16[8192,1792]{1,0:T(8,128)(2,1)} %param.9), kind=kOutput, calls=%fused_computation.9 | convolution fusion | flops 469893120 | bytes 15843328 | tf_op jit(solution)/shard_map/dot_general | solution.py:28
  125.9 0.8 copy-done.1
  126.7 0.7 slice.203
  127.4 2.6 %collective-permute-start.19 = (bf16[16,4096]{1,0:T(8,128)(2,1)}, bf16[16,4096]{1,0:T(8,128)(2,1)}, u32[]{:S(2)}, u32[]{:S(2)}) collective-permute-start(bf16[16,4096]{1,0:T(8,128)(2,1)} %slice.203), channel_id=1, source_target_pairs={{0,8},{1,9},{2,10},{3,11},{4,12},{5,13},{6,14},{7,15},{8,0},{9,1},... | collective-permute-start | bytes 393224 | tf_op jit(solution)/shard_map/ppermute | solution.py:39
  130.5 0.7 convolution_multiply_fusion.2
  131.5 0.6 reshape.93
  132.1 3.5 %all-to-all-start = ((bf16[16,2,512]{2,1,0:T(2,128)(2,1)}), bf16[16,2,512]{2,1,0:T(2,128)(2,1)S(1)}, u32[]{:S(2)}, u32[]{:S(2)}) async-start(bf16[16,2,512]{2,1,0:T(2,128)(2,1)} %reshape.93), calls=%async_computation | async-start | bytes 65536 | tf_op jit(solution)/shard_map/all_to_all | solution.py:148
  135.6 2.1 %multiply_convert_fusion.1 = bf16[512,2048]{1,0:T(8,128)(2,1)} fusion(bf16[32,8192]{1,0:T(8,128)(2,1)S(1)} %concatenate.18, s32[]{:T(128)S(6)} %select_n.41, bf16[32,2048]{1,0:T(8,128)(2,1)S(1)} %tile.21, s32[2048]{0:T(1024)S(1)} %add_select_fusion, s32[32]{0:T(128)S(1)} %select_reduce_fusion), kind=kOutput, calls=%fused_computation.11 | convolution fusion | flops 69337088 | bytes 2269700 | tf_op jit(solution)/shard_map/dot_general | solution.py:22
  137.7 4.5 %all-to-all-done = bf16[16,2,512]{2,1,0:T(2,128)(2,1)S(1)} async-done(((bf16[16,2,512]{2,1,0:T(2,128)(2,1)}), bf16[16,2,512]{2,1,0:T(2,128)(2,1)S(1)}, u32[]{:S(2)}, u32[]{:S(2)}) %all-to-all-start) | async-done | bytes 32800 | tf_op jit(solution)/shard_map/all_to_all | solution.py:148
  142.2 0.9 slice_add_fusion
  143.2 0.4 collective-permute-start.24
  143.6 1.0 slice_add_fusion.1
  144.6 1.7 %collective-permute-start.20 = (bf16[8,4096]{1,0:T(8,128)(2,1)S(1)}, bf16[8,4096]{1,0:T(8,128)(2,1)S(1)}, u32[]{:S(2)}, u32[]{:S(2)}) collective-permute-start(bf16[8,4096]{1,0:T(8,128)(2,1)S(1)} %slice.205), channel_id=1, source_target_pairs={{0,4},{1,5},{2,6},{3,7},{4,0},{5,1},{6,2},{7,3},{8,12},{9,13},{10,... | collective-permute-start | bytes 196616 | tf_op jit(solution)/shard_map/ppermute | solution.py:39
  146.4 1.5 collective-permute-done.24
  148.1 0.8 collective-permute-done.20
  149.0 1.2 collective-permute-start.21
  150.2 1.8 %collective-permute-done.25 = bf16[4,4096]{1,0:T(4,128)(2,1)S(1)} collective-permute-done((bf16[4,4096]{1,0:T(4,128)(2,1)S(1)}, bf16[4,4096]{1,0:T(4,128)(2,1)S(1)}, u32[]{:S(2)}, u32[]{:S(2)}) %collective-permute-start.25) | collective-permute-done | bytes 32800 | tf_op jit(solution)/shard_map/ppermute | solution.py:39
  152.1 0.9 collective-permute-done.21
  153.3 1.0 collective-permute-done.22
  154.3 0.7 fusion.19
  (71 shorter events, 3.0 us)
Async XLA Ops:
  0.6 22.3 %copy-start = (bf16[512,2048]{1,0:T(8,128)(2,1)S(1)}, bf16[512,2048]{1,0:T(8,128)(2,1)}, u32[]{:S(2)}) copy-start(bf16[512,2048]{1,0:T(8,128)(2,1)} %param.11) | copy-start | bytes 6291460
  0.6 6.6 %collective-permute-start = (bf16[2,8192]{1,0:T(2,128)(2,1)}, bf16[2,8192]{1,0:T(2,128)(2,1)S(1)}, u32[]{:S(2)}, u32[]{:S(2)}) collective-permute-start(bf16[2,8192]{1,0:T(2,128)(2,1)} %param.7), channel_id=1, source_target_pairs={{0,8},{1,9},{2,10},{3,11},{4,12},{5,13},{6,14},{7,15},{8,0},{9,1},... | collective-permute-start | bytes 98312 | tf_op jit(solution)/shard_map/ppermute | solution.py:39
  8.0 4.3 %collective-permute-start.1 = (bf16[4,8192]{1,0:T(4,128)(2,1)S(1)}, bf16[4,8192]{1,0:T(4,128)(2,1)S(1)}, u32[]{:S(2)}, u32[]{:S(2)}) collective-permute-start(bf16[4,8192]{1,0:T(4,128)(2,1)S(1)} %pad_maximum_fusion.1), channel_id=1, source_target_pairs={{0,4},{1,5},{2,6},{3,7},{4,0},{5,1},{6,2},{7,3},{8,12},{9,13},{10,... | collective-permute-start | bytes 196616 | tf_op jit(solution)/shard_map/ppermute | solution.py:39
  13.3 5.0 %collective-permute-start.2 = (bf16[8,8192]{1,0:T(8,128)(2,1)S(1)}, bf16[8,8192]{1,0:T(8,128)(2,1)S(1)}, u32[]{:S(2)}, u32[]{:S(2)}) collective-permute-start(bf16[8,8192]{1,0:T(8,128)(2,1)S(1)} %pad_maximum_fusion), channel_id=1, source_target_pairs={{0,2},{1,3},{2,0},{3,1},{4,6},{5,7},{6,4},{7,5},{8,10},{9,11},{10,... | collective-permute-start | bytes 393224 | tf_op jit(solution)/shard_map/ppermute | solution.py:39
  19.6 1.6 %collective-permute-start.3 = (bf16[16,8192]{1,0:T(8,128)(2,1)S(1)}, bf16[16,8192]{1,0:T(8,128)(2,1)S(1)}, u32[]{:S(2)}, u32[]{:S(2)}) collective-permute-start(bf16[16,8192]{1,0:T(8,128)(2,1)S(1)} %concatenate.17), channel_id=1, source_target_pairs={{0,1},{1,0},{2,3},{3,2},{4,5},{5,4},{6,7},{7,6},{8,9},{9,8},{10,11... | collective-permute-start | bytes 786440 | tf_op jit(solution)/shard_map/ppermute | solution.py:39
  23.9 8.4 %collective-permute-start.18 = (f32[32,64]{1,0:T(8,128)S(1)}, f32[32,64]{1,0:T(8,128)S(1)}, u32[]{:S(2)}, u32[]{:S(2)}) collective-permute-start(f32[32,64]{1,0:T(8,128)S(1)} %fusion.41), channel_id=1, source_target_pairs={{0,15},{1,14},{2,13},{3,12},{4,11},{5,10},{6,9},{7,8},{8,7},{9,6},... | collective-permute-start | bytes 24584 | tf_op jit(solution)/shard_map/ppermute | solution.py:39
  28.4 7.4 %collective-permute-start.17 = (f32[32,64]{1,0:T(8,128)S(1)}, f32[32,64]{1,0:T(8,128)S(1)}, u32[]{:S(2)}, u32[]{:S(2)}) collective-permute-start(f32[32,64]{1,0:T(8,128)S(1)} %fusion.41), channel_id=1, source_target_pairs={{0,14},{1,15},{2,12},{3,13},{4,10},{5,11},{6,8},{7,9},{8,6},{9,7},... | collective-permute-start | bytes 24584 | tf_op jit(solution)/shard_map/ppermute | solution.py:39
  28.8 7.2 %collective-permute-start.16 = (f32[32,64]{1,0:T(8,128)S(1)}, f32[32,64]{1,0:T(8,128)S(1)}, u32[]{:S(2)}, u32[]{:S(2)}) collective-permute-start(f32[32,64]{1,0:T(8,128)S(1)} %fusion.41), channel_id=1, source_target_pairs={{0,13},{1,12},{2,15},{3,14},{4,9},{5,8},{6,11},{7,10},{8,5},{9,4},... | collective-permute-start | bytes 24584 | tf_op jit(solution)/shard_map/ppermute | solution.py:39
  31.9 6.6 %collective-permute-start.15 = (f32[32,64]{1,0:T(8,128)S(1)}, f32[32,64]{1,0:T(8,128)S(1)}, u32[]{:S(2)}, u32[]{:S(2)}) collective-permute-start(f32[32,64]{1,0:T(8,128)S(1)} %fusion.41), channel_id=1, source_target_pairs={{0,12},{1,13},{2,14},{3,15},{4,8},{5,9},{6,10},{7,11},{8,4},{9,5},... | collective-permute-start | bytes 24584 | tf_op jit(solution)/shard_map/ppermute | solution.py:39
  32.3 8.4 %collective-permute-start.14 = (f32[32,64]{1,0:T(8,128)S(1)}, f32[32,64]{1,0:T(8,128)S(1)}, u32[]{:S(2)}, u32[]{:S(2)}) collective-permute-start(f32[32,64]{1,0:T(8,128)S(1)} %fusion.41), channel_id=1, source_target_pairs={{0,11},{1,10},{2,9},{3,8},{4,15},{5,14},{6,13},{7,12},{8,3},{9,2},... | collective-permute-start | bytes 24584 | tf_op jit(solution)/shard_map/ppermute | solution.py:39
  32.3 8.9 %collective-permute-start.13 = (f32[32,64]{1,0:T(8,128)S(1)}, f32[32,64]{1,0:T(8,128)S(1)}, u32[]{:S(2)}, u32[]{:S(2)}) collective-permute-start(f32[32,64]{1,0:T(8,128)S(1)} %fusion.41), channel_id=1, source_target_pairs={{0,10},{1,11},{2,8},{3,9},{4,14},{5,15},{6,12},{7,13},{8,2},{9,3},... | collective-permute-start | bytes 24584 | tf_op jit(solution)/shard_map/ppermute | solution.py:39
  35.9 6.5 %collective-permute-start.12 = (f32[32,64]{1,0:T(8,128)S(1)}, f32[32,64]{1,0:T(8,128)S(1)}, u32[]{:S(2)}, u32[]{:S(2)}) collective-permute-start(f32[32,64]{1,0:T(8,128)S(1)} %fusion.41), channel_id=1, source_target_pairs={{0,9},{1,8},{2,11},{3,10},{4,13},{5,12},{6,15},{7,14},{8,1},{9,0},... | collective-permute-start | bytes 24584 | tf_op jit(solution)/shard_map/ppermute | solution.py:39
  35.9 6.9 %collective-permute-start.11 = (f32[32,64]{1,0:T(8,128)S(1)}, f32[32,64]{1,0:T(8,128)S(1)}, u32[]{:S(2)}, u32[]{:S(2)}) collective-permute-start(f32[32,64]{1,0:T(8,128)S(1)} %fusion.41), channel_id=1, source_target_pairs={{0,8},{1,9},{2,10},{3,11},{4,12},{5,13},{6,14},{7,15},{8,0},{9,1},... | collective-permute-start | bytes 24584 | tf_op jit(solution)/shard_map/ppermute | solution.py:39
  38.5 5.6 %collective-permute-start.10 = (f32[32,64]{1,0:T(8,128)S(1)}, f32[32,64]{1,0:T(8,128)S(1)}, u32[]{:S(2)}, u32[]{:S(2)}) collective-permute-start(f32[32,64]{1,0:T(8,128)S(1)} %fusion.41), channel_id=1, source_target_pairs={{0,7},{1,6},{2,5},{3,4},{4,3},{5,2},{6,1},{7,0},{8,15},{9,14},{10,... | collective-permute-start | bytes 24584 | tf_op jit(solution)/shard_map/ppermute | solution.py:39
  40.6 4.7 %collective-permute-start.9 = (f32[32,64]{1,0:T(8,128)S(1)}, f32[32,64]{1,0:T(8,128)S(1)}, u32[]{:S(2)}, u32[]{:S(2)}) collective-permute-start(f32[32,64]{1,0:T(8,128)S(1)} %fusion.41), channel_id=1, source_target_pairs={{0,6},{1,7},{2,4},{3,5},{4,2},{5,3},{6,0},{7,1},{8,14},{9,15},{10,... | collective-permute-start | bytes 24584 | tf_op jit(solution)/shard_map/ppermute | solution.py:39
  41.2 4.2 %collective-permute-start.8 = (f32[32,64]{1,0:T(8,128)S(1)}, f32[32,64]{1,0:T(8,128)S(1)}, u32[]{:S(2)}, u32[]{:S(2)}) collective-permute-start(f32[32,64]{1,0:T(8,128)S(1)} %fusion.41), channel_id=1, source_target_pairs={{0,5},{1,4},{2,7},{3,6},{4,1},{5,0},{6,3},{7,2},{8,13},{9,12},{10,... | collective-permute-start | bytes 24584 | tf_op jit(solution)/shard_map/ppermute | solution.py:39
  42.4 3.8 %collective-permute-start.7 = (f32[32,64]{1,0:T(8,128)S(1)}, f32[32,64]{1,0:T(8,128)S(1)}, u32[]{:S(2)}, u32[]{:S(2)}) collective-permute-start(f32[32,64]{1,0:T(8,128)S(1)} %fusion.41), channel_id=1, source_target_pairs={{0,4},{1,5},{2,6},{3,7},{4,0},{5,1},{6,2},{7,3},{8,12},{9,13},{10,... | collective-permute-start | bytes 24584 | tf_op jit(solution)/shard_map/ppermute | solution.py:39
  42.9 3.3 %collective-permute-start.6 = (f32[32,64]{1,0:T(8,128)S(1)}, f32[32,64]{1,0:T(8,128)S(1)}, u32[]{:S(2)}, u32[]{:S(2)}) collective-permute-start(f32[32,64]{1,0:T(8,128)S(1)} %fusion.41), channel_id=1, source_target_pairs={{0,3},{1,2},{2,1},{3,0},{4,7},{5,6},{6,5},{7,4},{8,11},{9,10},{10,... | collective-permute-start | bytes 24584 | tf_op jit(solution)/shard_map/ppermute | solution.py:39
  44.1 3.7 %collective-permute-start.5 = (f32[32,64]{1,0:T(8,128)S(1)}, f32[32,64]{1,0:T(8,128)S(1)}, u32[]{:S(2)}, u32[]{:S(2)}) collective-permute-start(f32[32,64]{1,0:T(8,128)S(1)} %fusion.41), channel_id=1, source_target_pairs={{0,2},{1,3},{2,0},{3,1},{4,6},{5,7},{6,4},{7,5},{8,10},{9,11},{10,... | collective-permute-start | bytes 24584 | tf_op jit(solution)/shard_map/ppermute | solution.py:39
  45.4 2.4 %collective-permute-start.4 = (f32[32,64]{1,0:T(8,128)S(1)}, f32[32,64]{1,0:T(8,128)S(1)}, u32[]{:S(2)}, u32[]{:S(2)}) collective-permute-start(f32[32,64]{1,0:T(8,128)S(1)} %fusion.41), channel_id=1, source_target_pairs={{0,1},{1,0},{2,3},{3,2},{4,5},{5,4},{6,7},{7,6},{8,9},{9,8},{10,11... | collective-permute-start | bytes 24584 | tf_op jit(solution)/shard_map/ppermute | solution.py:39
  52.8 12.2 %copy-start.2 = (bf16[32,1792]{1,0:T(8,128)(2,1)S(1)}, bf16[32,1792]{1,0:T(8,128)(2,1)}, u32[]{:S(2)}) copy-start(bf16[32,1792]{1,0:T(8,128)(2,1)} %param.8) | copy-start | bytes 344068
  65.0 13.3 %slice-start = ((s8[7340032]{0:T(1024)(128)(4,1)}), s8[4194304]{0:T(1024)(128)(4,1)S(1)}, s32[]{:S(2)}) async-start(s8[7340032]{0:T(1024)(128)(4,1)} %bitcast.21), calls=%async_computation.1 | async-start | bytes 8388608
  65.9 12.4 %slice-start.1 = ((s8[7340032]{0:T(1024)(128)(4,1)}), s8[3145728]{0:T(1024)(128)(4,1)S(1)}, s32[]{:S(2)}) async-start(s8[7340032]{0:T(1024)(128)(4,1)} %bitcast.21), calls=%async_computation.2 | async-start | bytes 6291456
  82.7 17.0 %collective-permute-start.27 = (f32[32,64]{1,0:T(8,128)S(1)}, f32[32,64]{1,0:T(8,128)S(1)}, u32[]{:S(2)}, u32[]{:S(2)}) collective-permute-start(f32[32,64]{1,0:T(8,128)S(1)} %fusion.40), channel_id=1, source_target_pairs={{0,1},{1,0},{2,3},{3,2},{4,5},{5,4},{6,7},{7,6},{8,9},{9,8},{10,11... | collective-permute-start | bytes 24584 | tf_op jit(solution)/shard_map/ppermute | solution.py:39
  82.7 17.7 %copy-start.3 = (bf16[32,1792]{1,0:T(8,128)(2,1)S(1)}, bf16[32,1792]{1,0:T(8,128)(2,1)}, u32[]{:S(2)}) copy-start(bf16[32,1792]{1,0:T(8,128)(2,1)} %get-tuple-element.17) | copy-start | bytes 344068
  99.8 8.2 %collective-permute-start.28 = (f32[32,64]{1,0:T(8,128)S(1)}, f32[32,64]{1,0:T(8,128)S(1)}, u32[]{:S(2)}, u32[]{:S(2)}) collective-permute-start(f32[32,64]{1,0:T(8,128)S(1)} %add.161), channel_id=1, source_target_pairs={{0,2},{1,3},{2,0},{3,1},{4,6},{5,7},{6,4},{7,5},{8,10},{9,11},{10,... | collective-permute-start | bytes 24584 | tf_op jit(solution)/shard_map/ppermute | solution.py:39
  108.0 10.0 %collective-permute-start.29 = (f32[32,64]{1,0:T(8,128)S(1)}, f32[32,64]{1,0:T(8,128)S(1)}, u32[]{:S(2)}, u32[]{:S(2)}) collective-permute-start(f32[32,64]{1,0:T(8,128)S(1)} %add.162), channel_id=1, source_target_pairs={{0,4},{1,5},{2,6},{3,7},{4,0},{5,1},{6,2},{7,3},{8,12},{9,13},{10,... | collective-permute-start | bytes 24584 | tf_op jit(solution)/shard_map/ppermute | solution.py:39
  115.4 26.8 %collective-permute-start.23 = (bf16[16,4096]{1,0:T(8,128)(2,1)}, bf16[16,4096]{1,0:T(8,128)(2,1)}, u32[]{:S(2)}, u32[]{:S(2)}) collective-permute-start(bf16[16,4096]{1,0:T(8,128)(2,1)} %slice.202), channel_id=1, source_target_pairs={{0,8},{1,9},{2,10},{3,11},{4,12},{5,13},{6,14},{7,15},{8,0},{9,1},... | collective-permute-start | bytes 393224 | tf_op jit(solution)/shard_map/ppermute | solution.py:39
  118.0 12.0 %collective-permute-start.30 = (f32[32,64]{1,0:T(8,128)S(1)}, f32[32,64]{1,0:T(8,128)S(1)}, u32[]{:S(2)}, u32[]{:S(2)}) collective-permute-start(f32[32,64]{1,0:T(8,128)S(1)} %add.163), channel_id=1, source_target_pairs={{0,8},{1,9},{2,10},{3,11},{4,12},{5,13},{6,14},{7,15},{8,0},{9,1},... | collective-permute-start | bytes 24584 | tf_op jit(solution)/shard_map/ppermute | solution.py:39
  125.9 0.8 copy-start.1
  127.4 16.2 %collective-permute-start.19 = (bf16[16,4096]{1,0:T(8,128)(2,1)}, bf16[16,4096]{1,0:T(8,128)(2,1)}, u32[]{:S(2)}, u32[]{:S(2)}) collective-permute-start(bf16[16,4096]{1,0:T(8,128)(2,1)} %slice.203), channel_id=1, source_target_pairs={{0,8},{1,9},{2,10},{3,11},{4,12},{5,13},{6,14},{7,15},{8,0},{9,1},... | collective-permute-start | bytes 393224 | tf_op jit(solution)/shard_map/ppermute | solution.py:39
  132.1 10.1 %all-to-all-start = ((bf16[16,2,512]{2,1,0:T(2,128)(2,1)}), bf16[16,2,512]{2,1,0:T(2,128)(2,1)S(1)}, u32[]{:S(2)}, u32[]{:S(2)}) async-start(bf16[16,2,512]{2,1,0:T(2,128)(2,1)} %reshape.93), calls=%async_computation | async-start | bytes 65536 | tf_op jit(solution)/shard_map/all_to_all | solution.py:148
  143.2 4.7 %collective-permute-start.24 = (bf16[8,4096]{1,0:T(8,128)(2,1)S(1)}, bf16[8,4096]{1,0:T(8,128)(2,1)S(1)}, u32[]{:S(2)}, u32[]{:S(2)}) collective-permute-start(bf16[8,4096]{1,0:T(8,128)(2,1)S(1)} %slice.204), channel_id=1, source_target_pairs={{0,4},{1,5},{2,6},{3,7},{4,0},{5,1},{6,2},{7,3},{8,12},{9,13},{10,... | collective-permute-start | bytes 196616 | tf_op jit(solution)/shard_map/ppermute | solution.py:39
  144.6 4.3 %collective-permute-start.20 = (bf16[8,4096]{1,0:T(8,128)(2,1)S(1)}, bf16[8,4096]{1,0:T(8,128)(2,1)S(1)}, u32[]{:S(2)}, u32[]{:S(2)}) collective-permute-start(bf16[8,4096]{1,0:T(8,128)(2,1)S(1)} %slice.205), channel_id=1, source_target_pairs={{0,4},{1,5},{2,6},{3,7},{4,0},{5,1},{6,2},{7,3},{8,12},{9,13},{10,... | collective-permute-start | bytes 196616 | tf_op jit(solution)/shard_map/ppermute | solution.py:39
  148.0 4.0 %collective-permute-start.25 = (bf16[4,4096]{1,0:T(4,128)(2,1)S(1)}, bf16[4,4096]{1,0:T(4,128)(2,1)S(1)}, u32[]{:S(2)}, u32[]{:S(2)}) collective-permute-start(bf16[4,4096]{1,0:T(4,128)(2,1)S(1)} %slice.206), channel_id=1, source_target_pairs={{0,2},{1,3},{2,0},{3,1},{4,6},{5,7},{6,4},{7,5},{8,10},{9,11},{10,... | collective-permute-start | bytes 98312 | tf_op jit(solution)/shard_map/ppermute | solution.py:39
  149.0 4.0 %collective-permute-start.21 = (bf16[4,4096]{1,0:T(4,128)(2,1)S(1)}, bf16[4,4096]{1,0:T(4,128)(2,1)S(1)}, u32[]{:S(2)}, u32[]{:S(2)}) collective-permute-start(bf16[4,4096]{1,0:T(4,128)(2,1)S(1)} %slice.207), channel_id=1, source_target_pairs={{0,2},{1,3},{2,0},{3,1},{4,6},{5,7},{6,4},{7,5},{8,10},{9,11},{10,... | collective-permute-start | bytes 98312 | tf_op jit(solution)/shard_map/ppermute | solution.py:39
  152.0 1.2 collective-permute-start.26
  153.0 1.2 collective-permute-start.22

commit v3 on v0

v3 whole, which is shorter than its diff:
```python
import jax
import jax.numpy as jnp
from jax import lax
from jax.experimental import pallas as pl
from jax.experimental.pallas import tpu as pltpu
from jax.sharding import PartitionSpec as P

ADAPTER_RANK = 64
TENANT_COUNT = 32
SPREAD = ADAPTER_RANK * TENANT_COUNT

adapter_scale = 2.0


def block_of(size, largest):
    block = largest
    while size % block:
        block //= 2
    return block


def contracted_rows(left, right):
    return lax.dot_general(
        left, right, (((0,), (0,)), ((), ())), preferred_element_type=jnp.float32
    )


def contracted_columns(left, right):
    return lax.dot_general(
        left, right, (((1,), (1,)), ((), ())), preferred_element_type=jnp.float32
    )


def tenant_mask(tenants, rows):
    columns = lax.broadcasted_iota(jnp.int32, (rows, SPREAD), 1) // ADAPTER_RANK
    return tenants == columns


def select_block(wide_rows, mask):
    kept = jnp.where(mask, wide_rows, 0.0)
    pair = 2 * ADAPTER_RANK
    total = kept[:, :pair]
    for start in range(pair, SPREAD, pair):
        total = total + kept[:, start : start + pair]
    return total[:, :ADAPTER_RANK] + total[:, ADAPTER_RANK:]


def spread_rows(low_rows, mask):
    pair = jnp.concatenate([low_rows, low_rows], axis=1)
    wide = jnp.concatenate([pair] * (TENANT_COUNT // 2), axis=1)
    return jnp.where(mask, wide, 0.0).astype(jnp.bfloat16)


def low_kernel(span_ref, down_ref, tenants_ref, low_ref):
    wide = jnp.dot(span_ref[...], down_ref[...], preferred_element_type=jnp.float32)
    low_ref[...] = select_block(wide, tenant_mask(tenants_ref[...], wide.shape[0]))


def low_part(span, down, tenants):
    rows = span.shape[0]
    return pl.pallas_call(
        low_kernel,
        out_shape=jax.ShapeDtypeStruct((rows, ADAPTER_RANK), jnp.float32),
        compiler_params=pltpu.CompilerParams(vmem_limit_bytes=16 << 20),
        cost_estimate=pl.CostEstimate(
            flops=2 * rows * down.size, bytes_accessed=2 * down.size, transcendentals=0
        ),
        name="low_part",
    )(span, down, tenants)


def forward_kernel(own_ref, other_ref, gate_ref, up_ref, gate_out, up_out):
    @pl.when(pl.program_id(0) == 0)
    def _():
        gate_out[...] = jnp.zeros_like(gate_out)
        up_out[...] = jnp.zeros_like(up_out)

    rows = jnp.concatenate([own_ref[...], other_ref[...]], axis=0)
    gate_out[...] += jnp.dot(rows, gate_ref[...], preferred_element_type=jnp.float32)
    up_out[...] += jnp.dot(rows, up_ref[...], preferred_element_type=jnp.float32)


def forward(own, other, gate_weight, up_weight):
    half, width = own.shape
    hidden = gate_weight.shape[1]
    block = block_of(width, 512)
    result = jax.ShapeDtypeStruct((2 * half, hidden), jnp.float32)
    whole = pl.BlockSpec((2 * half, hidden), lambda k: (0, 0))
    tokens = pl.BlockSpec((half, block), lambda k: (0, k))
    weight = pl.BlockSpec((block, hidden), lambda k: (k, 0))
    return pl.pallas_call(
        forward_kernel,
        grid=(width // block,),
        in_specs=[tokens, tokens, weight, weight],
        out_specs=[whole, whole],
        out_shape=[result, result],
        compiler_params=pltpu.CompilerParams(vmem_limit_bytes=24 << 20),
        cost_estimate=pl.CostEstimate(
            flops=8 * half * gate_weight.size, bytes_accessed=4 * gate_weight.size, transcendentals=0
        ),
        name="forward",
    )(own, other, gate_weight, up_weight)


def activation_kernel(
    gate_ref, up_ref, hidden_ref, low_ref, tenants_ref, maps_ref, dgate_ref, dup_ref, part_ref, spread_ref
):
    rows = gate_ref.shape[0]
    mask = tenant_mask(tenants_ref[...], rows)
    spread = spread_rows(low_ref[...], mask)
    spread_ref[...] = spread
    gate = gate_ref[...] + adapter_scale * jnp.dot(
        spread, maps_ref[...], preferred_element_type=jnp.float32
    )
    s = jax.nn.sigmoid(gate)
    hidden = hidden_ref[...].astype(jnp.float32)
    dgate = (hidden * up_ref[...] * s * (1.0 + gate * (1.0 - s))).astype(jnp.bfloat16)
    dgate_ref[...] = dgate
    dup_ref[...] = (hidden * gate * s).astype(jnp.bfloat16)
    part_ref[...] = select_block(contracted_columns(dgate, maps_ref[...]), mask)


def activation(gate, up, hidden, low, tenants, maps):
    shape = gate.shape
    return pl.pallas_call(
        activation_kernel,
        out_shape=[
            jax.ShapeDtypeStruct(shape, jnp.bfloat16),
            jax.ShapeDtypeStruct(shape, jnp.bfloat16),
            jax.ShapeDtypeStruct((shape[0], ADAPTER_RANK), jnp.float32),
            jax.ShapeDtypeStruct((shape[0], SPREAD), jnp.bfloat16),
        ],
        compiler_params=pltpu.CompilerParams(vmem_limit_bytes=32 << 20),
        cost_estimate=pl.CostEstimate(
            flops=4 * shape[0] * maps.size, bytes_accessed=2 * maps.size, transcendentals=0
        ),
        name="activation",
    )(gate, up, hidden, low, tenants, maps)


def backward_kernel(dgate_ref, dup_ref, gate_ref, up_ref, own_out, other_out):
    half = own_out.shape[0]
    part = contracted_columns(dgate_ref[...], gate_ref[...])
    part = part + contracted_columns(dup_ref[...], up_ref[...])
    own_out[...] = part[:half]
    other_out[...] = part[half:].astype(jnp.bfloat16)


def backward(dgate, dup, gate_weight, up_weight, start, width):
    rows, hidden = dgate.shape
    half = rows // 2
    block = block_of(width, 512)
    first = start // block
    gradient = pl.BlockSpec((rows, hidden), lambda k: (0, 0))
    weight = pl.BlockSpec((block, hidden), lambda k: (k + first, 0))
    out = pl.BlockSpec((half, block), lambda k: (0, k))
    return pl.pallas_call(
        backward_kernel,
        grid=(width // block,),
        in_specs=[gradient, gradient, weight, weight],
        out_specs=[out, out],
        out_shape=[
            jax.ShapeDtypeStruct((half, width), jnp.float32),
            jax.ShapeDtypeStruct((half, width), jnp.bfloat16),
        ],
        compiler_params=pltpu.CompilerParams(vmem_limit_bytes=24 << 20),
        cost_estimate=pl.CostEstimate(
            flops=4 * rows * hidden * width, bytes_accessed=4 * hidden * width, transcendentals=0
        ),
        name="backward",
    )(dgate, dup, gate_weight, up_weight)


def outer_kernel(left_ref, right_ref, out_ref):
    out_ref[...] = (adapter_scale * contracted_rows(left_ref[...], right_ref[...])).astype(
        jnp.bfloat16
    )


def outer(left, right, name):
    rows, height = left.shape
    width = right.shape[1]
    block = block_of(height, 256)
    if block % 128:
        block = height
    return pl.pallas_call(
        outer_kernel,
        grid=(height // block,),
        in_specs=[
            pl.BlockSpec((rows, block), lambda k: (0, k)),
            pl.BlockSpec((rows, width), lambda k: (0, 0)),
        ],
        out_specs=pl.BlockSpec((block, width), lambda k: (k, 0)),
        out_shape=jax.ShapeDtypeStruct((height, width), jnp.bfloat16),
        compiler_params=pltpu.CompilerParams(vmem_limit_bytes=24 << 20),
        cost_estimate=pl.CostEstimate(
            flops=2 * rows * height * width, bytes_accessed=2 * height * width, transcendentals=0
        ),
        name=name,
    )(left, right)


def same_core_groups():
    count = lax.axis_size("tp")
    return [list(range(core, count, 2)) for core in range(2)]


def between_same_cores(blocks):
    return lax.all_to_all(
        blocks, "tp", split_axis=0, concat_axis=0, tiled=True, axis_index_groups=same_core_groups()
    )


def other_core(block):
    return lax.ppermute(block, "tp", [(i, i ^ 1) for i in range(lax.axis_size("tp"))])


def summed(block):
    copies = jnp.broadcast_to(block[None], (lax.axis_size("tp"),) + block.shape)
    return lax.all_to_all(copies, "tp", split_axis=0, concat_axis=0, tiled=True).sum(axis=0)


def local(
    normed_layer_input,
    hidden_unit_gradient,
    gate_weight,
    up_weight,
    adapter_down_maps,
    adapter_up_maps,
    token_tenant_index,
):
    count = lax.axis_size("tp")
    chips = count // 2
    own = lax.axis_index("tp")
    core = own % 2
    own_rows, width = normed_layer_input.shape
    rows = own_rows * count
    half = rows // 2
    span = adapter_down_maps.shape[0]

    def turned(block):
        blocks = block.reshape((chips, 2, own_rows) + block.shape[1:])
        blocks = jnp.where(core == 0, blocks, blocks[:, ::-1])
        return blocks.swapaxes(0, 1).reshape(block.shape)

    def returned(block):
        blocks = block.reshape((2, chips, own_rows) + block.shape[1:]).swapaxes(0, 1)
        return jnp.where(core == 0, blocks, blocks[:, ::-1]).reshape(block.shape)

    hidden = turned(hidden_unit_gradient)
    tenants = turned(token_tenant_index)[:, None]

    own_tokens = between_same_cores(
        jnp.broadcast_to(normed_layer_input[None], (chips, own_rows, width))
    ).reshape(half, width)
    other_tokens = other_core(own_tokens)
    input_span = jnp.concatenate(
        [lax.dynamic_slice_in_dim(x, own * span, span, 1) for x in (own_tokens, other_tokens)], axis=0
    )
    low = turned(summed(returned(low_part(input_span, adapter_down_maps, tenants))))
    gate, up = forward(own_tokens, other_tokens, gate_weight, up_weight)
    dgate, dup, low_grad, input_spread = activation(
        gate, up, hidden, low, tenants, adapter_up_maps
    )
    low_grad = turned(summed(returned(low_grad)))
    grad_spread = spread_rows(low_grad, tenant_mask(tenants, rows))
    adapter = (adapter_scale * contracted_columns(grad_spread, adapter_down_maps)).astype(
        jnp.bfloat16
    )

    chunk = width // 2
    arrived = []
    for start in (0, chunk):
        own_part, other_part = backward(dgate, dup, gate_weight, up_weight, start, chunk)
        if start > 0:
            other_part = jnp.concatenate([other_part, adapter[half:]], axis=1)
        came = other_core(other_part)
        part = (own_part + came[:, :chunk].astype(jnp.float32)).astype(jnp.bfloat16)
        if start > 0:
            part = jnp.concatenate([part, adapter[:half], came[:, chunk:]], axis=1)
        part = between_same_cores(part.reshape(chips, own_rows, part.shape[1]))
        arrived.append(part.astype(jnp.float32))
    down_map_gradient = outer(input_span, grad_spread, "down_maps")
    up_map_gradient = outer(input_spread, dgate, "up_maps")
    pair = arrived[1][:, :, chunk:].reshape(chips, own_rows, 2, span)
    pair = jnp.where(core == 0, pair, pair[:, :, ::-1])
    total = jnp.concatenate(
        [arrived[0].sum(axis=0), arrived[1][:, :, :chunk].sum(axis=0)], axis=1
    )
    total = total + pair.transpose(1, 0, 2, 3).reshape(own_rows, width)
    return (total.astype(jnp.bfloat16), down_map_gradient, up_map_gradient)


def solution(mesh):
    placed = (
        P(("groups", "tp"), None),
        P("groups", "tp"),
        P(None, "tp"),
        P(None, "tp"),
        P("tp", None),
        P(None, "tp"),
        P("groups"),
    )
    return jax.shard_map(
        local,
        mesh=mesh,
        in_specs=placed,
        out_specs=(P(("groups", "tp"), None), P("tp", "groups"), P("groups", "tp")),
        check_vma=False,
    )
```

time: 323 us -> 138 us (0.43)
  blocking collectives: 140 us -> 0 us
  waiting for transfers between devices: 86.2 us -> 14.2 us
  matrix products: 71.8 us -> 0.73 us
  Pallas kernels: 0 us -> 55.6 us
  local copies, waits for them, and re-layouts: 3.5 us -> 31.5 us
  starting transfers between devices: 3.71 us -> 27 us
  between operations: 14.9 us -> 1.02 us
  other arithmetic: 1.75 us -> 6.97 us
    psum x2 -> x0, blocking collectives: 115 us -> none  [the longest x1 57.8 us: local(): reduced_input = lax.psum(input_part, 'tp')]
    unnamed x2 -> x0, waiting for transfers between devices: 86.2 us -> none
    pallas_call x0 -> x7, Pallas kernels: none -> 55.6 us  [the longest x2 24.1 us: backward(): pl.pallas_call(backward_kernel, grid=(width // block,), in_specs=[gradien...]
    dot_general x6 -> x0, matrix products: 37.2 us -> none  [the longest x1 12.6 us: local(): jnp.dot(whole, gate_weight, preferred_element_type=jnp.float32)]
    dot_general x4 -> x1, matrix products: 34.5 us -> 0.73 us  [contracted_columns(): lax.dot_general(left, right, (((1,), (1,)), ((), ())), preferred_element_...]
    all_gather x1 -> x0, blocking collectives: 24.9 us -> none  [local(): whole = lax.all_gather(normed_layer_input, 'tp', axis=0, tiled=True)]
    unnamed x18 -> x14, local copies, waits for them, and re-layouts: 0.83 us -> 24.3 us
    all_to_all x1 -> x5, starting transfers between devices: 3.49 us -> 26.3 us  [the longest x3 16.6 us: between_same_cores(): lax.all_to_all(blocks, 'tp', split_axis=0, concat_axis=0, tiled=True, axi...]
  transfers between devices with their start and end apart: 2 -> 8, of which waited for: 1 -> 3; matrix products, arithmetic and copies ran while one was open for 12% -> 7% of each run, Pallas kernels for 0% -> 38%
where the time goes in v3:
time: 138 us; the launch traced here: 137 us
  Pallas kernels  55.6 us (40%)
  local copies, waits for them, and re-layouts  31.5 us (23%)
  starting transfers between devices  27 us (20%)
  waiting for transfers between devices  14.2 us (10%)
  other arithmetic  6.97 us (5%)
    unnamed x14, local copies, waits for them, and re-layouts  24.3 us
    pallas_call x2, Pallas kernels, backward(): pl.pallas_call(backward_kernel, grid=(width // block,), in_specs=[gradien...  24.1 us
    pallas_call x1, Pallas kernels, forward(): pl.pallas_call(forward_kernel, grid=(width // block,), in_specs=[tokens,...  19.6 us
    all_to_all x3, starting transfers between devices, between_same_cores(): lax.all_to_all(blocks, 'tp', split_axis=0, concat_axis=0, tiled=True, axi...  16.6 us
    all_to_all x3, waiting for transfers between devices, between_same_cores(): lax.all_to_all(blocks, 'tp', split_axis=0, concat_axis=0, tiled=True, axi...  13.5 us
    all_to_all x2, starting transfers between devices, summed(): lax.all_to_all(copies, 'tp', split_axis=0, concat_axis=0, tiled=True)  9.7 us
    pallas_call x2, Pallas kernels, outer(): pl.pallas_call(outer_kernel, grid=(height // block,), in_specs=[pl.BlockS...  7.77 us
    pallas_call x1, Pallas kernels, activation(): pl.pallas_call(activation_kernel, out_shape=[jax.ShapeDtypeStruct(shape,...  3.57 us
  transfers between devices with their start and end apart: 8, of which 3 were waited for; matrix products, arithmetic and copies ran while one was open for 7% of the time, Pallas kernels for 38%

profile of v3, /device:TPU:0, one launch (start us, length us, event | category | flops | bytes accessed | tf_op | source)
XLA Modules:
  0.0 137.1 jit_solution(13841031207828805337)
XLA Ops:
  0.6 0.0 copy-start.2
  0.6 1.7 %broadcast_in_dim.24 = bf16[8,2,8192]{2,1,0:T(2,128)(2,1)} broadcast(bf16[2,8192]{1,0:T(2,128)(2,1)} %param.7), dimensions={1,2} | broadcast | bytes 294912 | tf_op jit(solution)/shard_map/broadcast_in_dim | solution.py:254
  2.4 7.3 %all-to-all-start = ((bf16[8,2,8192]{2,1,0:T(2,128)(2,1)}), bf16[8,2,8192]{2,1,0:T(2,128)(2,1)S(1)}, u32[]{:S(2)}, u32[]{:S(2)}) async-start(bf16[8,2,8192]{2,1,0:T(2,128)(2,1)} %broadcast_in_dim.24), calls=%async_computation | async-start | bytes 524288 | tf_op jit(solution)/shard_map/all_to_all | solution.py:209
  9.7 0.7 reshape.55
  10.5 0.9 reshape.53
  11.4 0.1 copy.31
  11.5 0.1 fusion.1
  11.6 7.0 %all-to-all-done = bf16[8,2,8192]{2,1,0:T(2,128)(2,1)S(1)} async-done(((bf16[8,2,8192]{2,1,0:T(2,128)(2,1)}), bf16[8,2,8192]{2,1,0:T(2,128)(2,1)S(1)}, u32[]{:S(2)}, u32[]{:S(2)}) %all-to-all-start) | async-done | bytes 262176 | tf_op jit(solution)/shard_map/all_to_all | solution.py:209
  18.6 0.1 reshape.52.own_ref
  18.7 0.1 collective-permute-start
  18.8 0.7 eq.11
  19.5 0.1 broadcast_in_dim_reshape.6.tenants_ref
  19.6 0.7 collective-permute-done.other_ref
  20.3 0.0 copy-done.2
  20.3 0.5 low_part.1
  20.9 0.8 reshape.66
  21.7 3.7 %all-to-all-start.1 = ((f32[16,1,2048]{2,1,0:T(1,128)}), f32[16,1,2048]{2,1,0:T(1,128)S(1)}, u32[]{:S(2)}, u32[]{:S(2)}) async-start(f32[16,1,2048]{2,1,0:T(1,128)} %reshape.66), calls=%async_computation.1 | async-start | bytes 262144 | tf_op jit(solution)/shard_map/all_to_all | solution.py:220
  25.4 0.6 iota_shift-right-logical_fusion
  26.0 0.0 copy-start
  26.0 9.3 %copy-done = bf16[8192,1792]{1,0:T(8,128)(2,1)S(1)} copy-done((bf16[8192,1792]{1,0:T(8,128)(2,1)S(1)}, bf16[8192,1792]{1,0:T(8,128)(2,1)}, u32[]{:S(2)}) %copy-start) | copy-done | bytes 29360152
  35.4 19.6 %forward.1 = (f32[32,1792]{1,0:T(8,128)S(1)}, f32[32,1792]{1,0:T(8,128)S(1)}) custom-call(bf16[16,8192]{1,0:T(8,128)(2,1)S(1)} %reshape.52.own_ref, bf16[16,8192]{1,0:T(8,128)(2,1)S(1)} %collective-permute-done.other_ref, bf16[8192,1792]{1,0:T(8,128)(2,1)S(1)} %copy-done, bf16[8192,1792]{1,0:T(8,128)(2,1)} %up_ref.5), custom_call_target="tpu_custom_call" | custom-call | flops 1879048192 | bytes 58720256 | tf_op jit(solution)/shard_map/forward/pallas_call | solution.py:91
  55.0 0.0 all-to-all-done.1
  55.0 0.0 copy-start.4
  55.0 0.6 copy-done.4
  55.6 0.5 broadcast.24
  56.2 1.8 %reduce = f32[16,2048]{1,0:T(8,128)S(1)} reduce(f32[16,1,2048]{2,1,0:T(1,128)} %copy-done.4, f32[]{:T(128)} %broadcast.24), dimensions={1}, to_apply=%all_to_all.16.reduce_sub_computation | reduce | bytes 262148 | tf_op jit(solution)/shard_map/all_to_all | solution.py:220
  58.0 0.1 reshape.67
  58.2 0.0 copy-start.3
  58.2 3.1 %copy-done.3 = bf16[2048,1792]{1,0:T(8,128)(2,1)S(1)} copy-done((bf16[2048,1792]{1,0:T(8,128)(2,1)S(1)}, bf16[2048,1792]{1,0:T(8,128)(2,1)}, u32[]{:S(2)}) %copy-start.3) | copy-done | bytes 7340056
  61.3 3.6 %activation.1 = (bf16[32,1792]{1,0:T(8,128)(2,1)S(1)}, bf16[32,1792]{1,0:T(8,128)(2,1)S(1)}, f32[32,64]{1,0:T(8,128)S(1)}, bf16[32,2048]{1,0:T(8,128)(2,1)S(1)}) custom-call(f32[32,1792]{1,0:T(8,128)S(1)} %get-tuple-element.13.gate_ref, f32[32,1792]{1,0:T(8,128)S(1)} %get-tuple-element.14.up_ref, bf16[32,1792]{1,0:T(8,128)(2,1)S(1)} %reshape.54.hidden_ref, ...), custom_call_target="tpu_custom_call" | custom-call | flops 469762048 | bytes 7340032 | tf_op jit(solution)/shard_map/activation/pallas_call | solution.py:125
  64.9 0.8 reshape.68
  65.8 6.0 %all-to-all-start.3 = ((f32[16,1,2048]{2,1,0:T(1,128)}), f32[16,1,2048]{2,1,0:T(1,128)S(1)}, u32[]{:S(2)}, u32[]{:S(2)}) async-start(f32[16,1,2048]{2,1,0:T(1,128)} %reshape.68), calls=%async_computation.3 | async-start | bytes 262144 | tf_op jit(solution)/shard_map/all_to_all | solution.py:220
  71.8 0.6 fusion.7
  72.4 0.0 copy-start.1
  72.4 9.3 %copy-done.1 = bf16[8192,1792]{1,0:T(8,128)(2,1)S(1)} copy-done((bf16[8192,1792]{1,0:T(8,128)(2,1)S(1)}, bf16[8192,1792]{1,0:T(8,128)(2,1)}, u32[]{:S(2)}) %copy-start.1) | copy-done | bytes 29360152
  81.7 12.1 %backward.2 = (f32[16,4096]{1,0:T(8,128)S(1)}, bf16[16,4096]{1,0:T(8,128)(2,1)S(1)}) custom-call(bf16[32,1792]{1,0:T(8,128)(2,1)S(1)} %get-tuple-element.15.dgate_ref.right_ref, bf16[32,1792]{1,0:T(8,128)(2,1)S(1)} %get-tuple-element.16.dup_ref, bf16[8192,1792]{1,0:T(8,128)(2,1)S(1)} %copy-done.1, bf16[8192,1792]{1,0:T(8,128)(2,1)} %up_ref.5), custom_call_target="tpu_custom_call" | custom-call | flops 939524096 | bytes 29360128 | tf_op jit(solution)/shard_map/backward/pallas_call | solution.py:157
  93.8 0.5 collective-permute-start.1
  94.3 12.1 %backward.3 = (f32[16,4096]{1,0:T(8,128)S(1)}, bf16[16,4096]{1,0:T(8,128)(2,1)S(1)}) custom-call(bf16[32,1792]{1,0:T(8,128)(2,1)S(1)} %get-tuple-element.15.dgate_ref.right_ref, bf16[32,1792]{1,0:T(8,128)(2,1)S(1)} %get-tuple-element.16.dup_ref, bf16[8192,1792]{1,0:T(8,128)(2,1)S(1)} %copy-done.1, bf16[8192,1792]{1,0:T(8,128)(2,1)} %up_ref.5), custom_call_target="tpu_custom_call" | custom-call | flops 939524096 | bytes 29360128 | tf_op jit(solution)/shard_map/backward/pallas_call | solution.py:157
  106.3 0.0 all-to-all-done.3
  106.4 0.9 reduce.1
  107.3 0.1 reshape.69
  107.5 0.2 concatenate.18
  107.7 0.8 select_convert_fusion.right_ref
  108.5 0.7 fusion
  109.3 0.2 collective-permute-start.2
  109.4 0.0 collective-permute-done.1
  109.4 0.9 add_convert_fusion.1
  110.4 0.8 reshape.59
  111.1 5.9 %all-to-all-start.2 = ((bf16[8,2,4096]{2,1,0:T(2,128)(2,1)}), bf16[8,2,4096]{2,1,0:T(2,128)(2,1)S(1)}, u32[]{:S(2)}, u32[]{:S(2)}) async-start(bf16[8,2,4096]{2,1,0:T(2,128)(2,1)} %reshape.59), calls=%async_computation.2 | async-start | bytes 262144 | tf_op jit(solution)/shard_map/all_to_all | solution.py:209
  117.0 0.0 collective-permute-done.2
  117.1 0.7 reshape.63
  117.8 6.5 %all-to-all-done.2 = bf16[8,2,4096]{2,1,0:T(2,128)(2,1)S(1)} async-done(((bf16[8,2,4096]{2,1,0:T(2,128)(2,1)}), bf16[8,2,4096]{2,1,0:T(2,128)(2,1)S(1)}, u32[]{:S(2)}, u32[]{:S(2)}) %all-to-all-start.2) | async-done | bytes 131104 | tf_op jit(solution)/shard_map/all_to_all | solution.py:209
  124.4 3.4 %all-to-all-start.4 = ((bf16[8,2,5120]{2,1,0:T(2,128)(2,1)}), bf16[8,2,5120]{2,1,0:T(2,128)(2,1)S(1)}, u32[]{:S(2)}, u32[]{:S(2)}) async-start(bf16[8,2,5120]{2,1,0:T(2,128)(2,1)} %reshape.63), calls=%async_computation.4 | async-start | bytes 327680 | tf_op jit(solution)/shard_map/all_to_all | solution.py:209
  127.8 5.9 %up_maps.1 = bf16[2048,1792]{1,0:T(8,128)(2,1)} custom-call(bf16[32,2048]{1,0:T(8,128)(2,1)S(1)} %get-tuple-element.22.left_ref, bf16[32,1792]{1,0:T(8,128)(2,1)S(1)} %get-tuple-element.15.dgate_ref.right_ref), custom_call_target="tpu_custom_call" | custom-call | flops 234881024 | bytes 7340032 | tf_op jit(solution)/shard_map/up_maps/pallas_call | solution.py:186
  133.6 1.9 %down_maps.1 = bf16[512,2048]{1,0:T(8,128)(2,1)} custom-call(bf16[32,512]{1,0:T(8,128)(2,1)S(1)} %pad_maximum_fusion.2.span_ref.left_ref, bf16[32,2048]{1,0:T(8,128)(2,1)S(1)} %select_convert_fusion.right_ref), custom_call_target="tpu_custom_call" | custom-call | flops 67108864 | bytes 2097152 | tf_op jit(solution)/shard_map/down_maps/pallas_call | solution.py:186
  135.5 0.1 convert_reduce_fusion
  135.7 0.0 all-to-all-done.4
  135.7 0.1 reshape.64
  135.8 0.3 rev.27
  136.1 0.1 reshape.65
  136.2 0.1 convert_element_type.34
  136.3 0.1 slice_reduce_fusion
  136.4 0.7 fusion.2
  (27 shorter events, 0.4 us)
Async XLA Ops:
  0.6 19.7 %copy-start.2 = (bf16[512,2048]{1,0:T(8,128)(2,1)S(1)}, bf16[512,2048]{1,0:T(8,128)(2,1)}, u32[]{:S(2)}) copy-start(bf16[512,2048]{1,0:T(8,128)(2,1)} %down_ref.1) | copy-start | bytes 6291460
  2.4 16.2 %all-to-all-start = ((bf16[8,2,8192]{2,1,0:T(2,128)(2,1)}), bf16[8,2,8192]{2,1,0:T(2,128)(2,1)S(1)}, u32[]{:S(2)}, u32[]{:S(2)}) async-start(bf16[8,2,8192]{2,1,0:T(2,128)(2,1)} %broadcast_in_dim.24), calls=%async_computation | async-start | bytes 524288 | tf_op jit(solution)/shard_map/all_to_all | solution.py:209
  18.7 1.6 %collective-permute-start = (bf16[16,8192]{1,0:T(8,128)(2,1)S(1)}, bf16[16,8192]{1,0:T(8,128)(2,1)S(1)}, u32[]{:S(2)}, u32[]{:S(2)}) collective-permute-start(bf16[16,8192]{1,0:T(8,128)(2,1)S(1)} %reshape.52.own_ref), channel_id=1, source_target_pairs={{0,1},{1,0},{2,3},{3,2},{4,5},{5,4},{6,7},{7,6},{8,9},{9,8},{10,11... | collective-permute-start | bytes 786440 | tf_op jit(solution)/shard_map/ppermute | solution.py:215
  21.7 33.2 %all-to-all-start.1 = ((f32[16,1,2048]{2,1,0:T(1,128)}), f32[16,1,2048]{2,1,0:T(1,128)S(1)}, u32[]{:S(2)}, u32[]{:S(2)}) async-start(f32[16,1,2048]{2,1,0:T(1,128)} %reshape.66), calls=%async_computation.1 | async-start | bytes 262144 | tf_op jit(solution)/shard_map/all_to_all | solution.py:220
  26.0 9.4 %copy-start = (bf16[8192,1792]{1,0:T(8,128)(2,1)S(1)}, bf16[8192,1792]{1,0:T(8,128)(2,1)}, u32[]{:S(2)}) copy-start(bf16[8192,1792]{1,0:T(8,128)(2,1)} %gate_ref.5) | copy-start | bytes 88080384
  55.0 0.7 copy-start.4
  58.2 3.1 %copy-start.3 = (bf16[2048,1792]{1,0:T(8,128)(2,1)S(1)}, bf16[2048,1792]{1,0:T(8,128)(2,1)}, u32[]{:S(2)}) copy-start(bf16[2048,1792]{1,0:T(8,128)(2,1)} %maps_ref.1) | copy-start | bytes 22020100
  65.8 40.6 %all-to-all-start.3 = ((f32[16,1,2048]{2,1,0:T(1,128)}), f32[16,1,2048]{2,1,0:T(1,128)S(1)}, u32[]{:S(2)}, u32[]{:S(2)}) async-start(f32[16,1,2048]{2,1,0:T(1,128)} %reshape.68), calls=%async_computation.3 | async-start | bytes 262144 | tf_op jit(solution)/shard_map/all_to_all | solution.py:220
  72.4 9.4 %copy-start.1 = (bf16[8192,1792]{1,0:T(8,128)(2,1)S(1)}, bf16[8192,1792]{1,0:T(8,128)(2,1)}, u32[]{:S(2)}) copy-start(bf16[8192,1792]{1,0:T(8,128)(2,1)} %gate_ref.5) | copy-start | bytes 88080384
  93.8 15.7 %collective-permute-start.1 = (bf16[16,4096]{1,0:T(8,128)(2,1)S(1)}, bf16[16,4096]{1,0:T(8,128)(2,1)}, u32[]{:S(2)}, u32[]{:S(2)}) collective-permute-start(bf16[16,4096]{1,0:T(8,128)(2,1)S(1)} %get-tuple-element.18), channel_id=1, source_target_pairs={{0,1},{1,0},{2,3},{3,2},{4,5},{5,4},{6,7},{7,6},{8,9},{9,8},{10,11... | collective-permute-start | bytes 393224 | tf_op jit(solution)/shard_map/ppermute | solution.py:215
  109.3 7.8 %collective-permute-start.2 = (bf16[16,4608]{1,0:T(8,128)(2,1)S(1)}, bf16[16,4608]{1,0:T(8,128)(2,1)S(1)}, u32[]{:S(2)}, u32[]{:S(2)}) collective-permute-start(bf16[16,4608]{1,0:T(8,128)(2,1)S(1)} %pad_maximum_fusion.1), channel_id=1, source_target_pairs={{0,1},{1,0},{2,3},{3,2},{4,5},{5,4},{6,7},{7,6},{8,9},{9,8},{10,11... | collective-permute-start | bytes 442376 | tf_op jit(solution)/shard_map/ppermute | solution.py:215
  111.1 13.2 %all-to-all-start.2 = ((bf16[8,2,4096]{2,1,0:T(2,128)(2,1)}), bf16[8,2,4096]{2,1,0:T(2,128)(2,1)S(1)}, u32[]{:S(2)}, u32[]{:S(2)}) async-start(bf16[8,2,4096]{2,1,0:T(2,128)(2,1)} %reshape.59), calls=%async_computation.2 | async-start | bytes 262144 | tf_op jit(solution)/shard_map/all_to_all | solution.py:209
  124.4 11.3 %all-to-all-start.4 = ((bf16[8,2,5120]{2,1,0:T(2,128)(2,1)}), bf16[8,2,5120]{2,1,0:T(2,128)(2,1)S(1)}, u32[]{:S(2)}, u32[]{:S(2)}) async-start(bf16[8,2,5120]{2,1,0:T(2,128)(2,1)} %reshape.63), calls=%async_computation.4 | async-start | bytes 327680 | tf_op jit(solution)/shard_map/all_to_all | solution.py:209

commit v4 on v3

--- a/solution.py
+++ b/solution.py
@@ -51,17 +51,42 @@
     return jnp.where(mask, wide, 0.0).astype(jnp.bfloat16)
 
 
-def low_kernel(span_ref, down_ref, tenants_ref, low_ref):
+def packed(low):
+    half = low.shape[0] // 2
+    return jnp.concatenate([low[:half], low[half:]], axis=1)
+
+
+def unpacked_sum(core, copies_ref):
+    sums = []
+    for parity in range(2):
+        total = copies_ref[parity]
+        for k in range(parity + 2, copies_ref.shape[0], 2):
+            total = total + copies_ref[k]
+        sums.append(total)
+    same = jnp.where(core == 0, sums[0], sums[1])
+    other = jnp.where(core == 0, sums[1], sums[0])
+    first = same[:, :ADAPTER_RANK] + other[:, ADAPTER_RANK:]
+    second = same[:, ADAPTER_RANK:] + other[:, :ADAPTER_RANK]
+    return jnp.concatenate([first, second], axis=0)
+
+
+def write_copies(copies_ref, low):
+    tile = packed(low)
+    for k in range(copies_ref.shape[0]):
+        copies_ref[k] = tile
+
+
+def low_kernel(span_ref, down_ref, tenants_ref, copies_ref):
     wide = jnp.dot(span_ref[...], down_ref[...], preferred_element_type=jnp.float32)
-    low_ref[...] = select_block(wide, tenant_mask(tenants_ref[...], wide.shape[0]))
-
-
-def low_part(span, down, tenants):
+    write_copies(copies_ref, select_block(wide, tenant_mask(tenants_ref[...], wide.shape[0])))
+
+
+def low_part(span, down, tenants, count):
     rows = span.shape[0]
     return pl.pallas_call(
         low_kernel,
-        out_shape=jax.ShapeDtypeStruct((rows, ADAPTER_RANK), jnp.float32),
-        compiler_params=pltpu.CompilerParams(vmem_limit_bytes=16 << 20),
+        out_shape=jax.ShapeDtypeStruct((count, rows // 2, 2 * ADAPTER_RANK), jnp.float32),
+        compiler_params=pltpu.CompilerParams(vmem_limit_bytes=40 << 20),
         cost_estimate=pl.CostEstimate(
             flops=2 * rows * down.size, bytes_accessed=2 * down.size, transcendentals=0
         ),
@@ -94,7 +119,7 @@
         in_specs=[tokens, tokens, weight, weight],
         out_specs=[whole, whole],
         out_shape=[result, result],
-        compiler_params=pltpu.CompilerParams(vmem_limit_bytes=24 << 20),
+        compiler_params=pltpu.CompilerParams(vmem_limit_bytes=52 << 20),
         cost_estimate=pl.CostEstimate(
             flops=8 * half * gate_weight.size, bytes_accessed=4 * gate_weight.size, transcendentals=0
         ),
@@ -103,11 +128,12 @@
 
 
 def activation_kernel(
-    gate_ref, up_ref, hidden_ref, low_ref, tenants_ref, maps_ref, dgate_ref, dup_ref, part_ref, spread_ref
+    core_ref, gate_ref, up_ref, hidden_ref, low_ref, tenants_ref, maps_ref,
+    dgate_ref, dgate_turned_ref, dup_turned_ref, copies_ref, spread_ref,
 ):
     rows = gate_ref.shape[0]
     mask = tenant_mask(tenants_ref[...], rows)
-    spread = spread_rows(low_ref[...], mask)
+    spread = spread_rows(unpacked_sum(core_ref[0], low_ref), mask)
     spread_ref[...] = spread
     gate = gate_ref[...] + adapter_scale * jnp.dot(
         spread, maps_ref[...], preferred_element_type=jnp.float32
@@ -115,43 +141,89 @@
     s = jax.nn.sigmoid(gate)
     hidden = hidden_ref[...].astype(jnp.float32)
     dgate = (hidden * up_ref[...] * s * (1.0 + gate * (1.0 - s))).astype(jnp.bfloat16)
+    dup = (hidden * gate * s).astype(jnp.bfloat16)
     dgate_ref[...] = dgate
-    dup_ref[...] = (hidden * gate * s).astype(jnp.bfloat16)
-    part_ref[...] = select_block(contracted_columns(dgate, maps_ref[...]), mask)
-
-
-def activation(gate, up, hidden, low, tenants, maps):
-    shape = gate.shape
+    lanes = dgate_turned_ref.shape[1]
+    for value, out_ref in ((dgate, dgate_turned_ref), (dup, dup_turned_ref)):
+        value = value.astype(jnp.float32)
+        if lanes > rows:
+            value = jnp.concatenate(
+                [value, jnp.zeros((lanes - rows, value.shape[1]), jnp.float32)], axis=0
+            )
+        out_ref[...] = value.T.astype(jnp.bfloat16)
+    write_copies(copies_ref, select_block(contracted_columns(dgate, maps_ref[...]), mask))
+
+
+VMEM = pl.BlockSpec(memory_space=pltpu.VMEM)
+SMEM = pl.BlockSpec(memory_space=pltpu.SMEM)
+
+
+def activation(core, gate, up, hidden, low, tenants, maps):
+    rows, width = gate.shape
+    lanes = max(rows, 128)
     return pl.pallas_call(
         activation_kernel,
+        in_specs=[SMEM] + [VMEM] * 6,
         out_shape=[
-            jax.ShapeDtypeStruct(shape, jnp.bfloat16),
-            jax.ShapeDtypeStruct(shape, jnp.bfloat16),
-            jax.ShapeDtypeStruct((shape[0], ADAPTER_RANK), jnp.float32),
-            jax.ShapeDtypeStruct((shape[0], SPREAD), jnp.bfloat16),
+            jax.ShapeDtypeStruct((rows, width), jnp.bfloat16),
+            jax.ShapeDtypeStruct((width, lanes), jnp.bfloat16),
+            jax.ShapeDtypeStruct((width, lanes), jnp.bfloat16),
+            jax.ShapeDtypeStruct(low.shape, jnp.float32),
+            jax.ShapeDtypeStruct((rows, SPREAD), jnp.bfloat16),
         ],
-        compiler_params=pltpu.CompilerParams(vmem_limit_bytes=32 << 20),
-        cost_estimate=pl.CostEstimate(
-            flops=4 * shape[0] * maps.size, bytes_accessed=2 * maps.size, transcendentals=0
+        compiler_params=pltpu.CompilerParams(vmem_limit_bytes=48 << 20),
+        cost_estimate=pl.CostEstimate(
+            flops=4 * rows * maps.size, bytes_accessed=2 * maps.size, transcendentals=0
         ),
         name="activation",
-    )(gate, up, hidden, low, tenants, maps)
+    )(core, gate, up, hidden, low, tenants, maps)
+
+
+def adapter_kernel(
+    core_ref, low_ref, tenants_ref, span_ref, down_ref, own_out, other_out, gradient_ref
+):
+    rows = tenants_ref.shape[0]
+    spread = spread_rows(
+        unpacked_sum(core_ref[0], low_ref), tenant_mask(tenants_ref[...], rows)
+    )
+    part = (adapter_scale * contracted_columns(spread, down_ref[...])).astype(jnp.bfloat16)
+    own_out[...] = part[: rows // 2]
+    other_out[...] = part[rows // 2 :]
+    gradient_ref[...] = (adapter_scale * contracted_rows(span_ref[...], spread)).astype(
+        jnp.bfloat16
+    )
+
+
+def adapter_part(core, low, tenants, input_span, down):
+    rows, span = input_span.shape
+    half = jax.ShapeDtypeStruct((rows // 2, span), jnp.bfloat16)
+    return pl.pallas_call(
+        adapter_kernel,
+        in_specs=[SMEM] + [VMEM] * 4,
+        out_shape=[half, half, jax.ShapeDtypeStruct(down.shape, jnp.bfloat16)],
+        compiler_params=pltpu.CompilerParams(vmem_limit_bytes=40 << 20),
+        cost_estimate=pl.CostEstimate(
+            flops=4 * rows * down.size, bytes_accessed=4 * down.size, transcendentals=0
+        ),
+        name="adapter_part",
+    )(core, low, tenants, input_span, down)
 
 
 def backward_kernel(dgate_ref, dup_ref, gate_ref, up_ref, own_out, other_out):
     half = own_out.shape[0]
-    part = contracted_columns(dgate_ref[...], gate_ref[...])
-    part = part + contracted_columns(dup_ref[...], up_ref[...])
+    part = jnp.dot(gate_ref[...], dgate_ref[...], preferred_element_type=jnp.float32)
+    part = part + jnp.dot(up_ref[...], dup_ref[...], preferred_element_type=jnp.float32)
+    part = part.T
     own_out[...] = part[:half]
-    other_out[...] = part[half:].astype(jnp.bfloat16)
-
-
-def backward(dgate, dup, gate_weight, up_weight, start, width):
-    rows, hidden = dgate.shape
+    other_out[...] = part[half : 2 * half].astype(jnp.bfloat16)
+
+
+def backward(rows, dgate, dup, gate_weight, up_weight, start, width):
+    hidden, lanes = dgate.shape
     half = rows // 2
     block = block_of(width, 512)
     first = start // block
-    gradient = pl.BlockSpec((rows, hidden), lambda k: (0, 0))
+    gradient = pl.BlockSpec((hidden, lanes), lambda k: (0, 0))
     weight = pl.BlockSpec((block, hidden), lambda k: (k + first, 0))
     out = pl.BlockSpec((half, block), lambda k: (0, k))
     return pl.pallas_call(
@@ -163,12 +235,118 @@
             jax.ShapeDtypeStruct((half, width), jnp.float32),
             jax.ShapeDtypeStruct((half, width), jnp.bfloat16),
         ],
-        compiler_params=pltpu.CompilerParams(vmem_limit_bytes=24 << 20),
+        compiler_params=pltpu.CompilerParams(vmem_limit_bytes=60 << 20),
         cost_estimate=pl.CostEstimate(
             flops=4 * rows * hidden * width, bytes_accessed=4 * hidden * width, transcendentals=0
         ),
         name="backward",
     )(dgate, dup, gate_weight, up_weight)
+
+
+PARTS = 8
+
+
+def merge_kernel(
+    core_ref, own0, own1, came0, came1, adapter_own, adapter_came, out_ref, sums, tiles
+):
+    chips, tile, lanes = out_ref.shape
+    tokens = tile // PARTS
+    chunk = own0.shape[1]
+    per_part = (lanes - 128) // 128
+    blocks = PARTS * per_part
+
+    def put(first, value):
+        for k in range(value.shape[1] // 128):
+            sums[first + k] = value[:, k * 128 : (k + 1) * 128]
+
+    put(0, own0[...] + came0[...].astype(jnp.float32))
+    put(chunk // 128, own1[...] + came1[...].astype(jnp.float32))
+    mine = adapter_own[...].astype(jnp.float32)
+    came = adapter_came[...].astype(jnp.float32)
+    put(
+        blocks,
+        jnp.where(
+            core_ref[0] == 0,
+            jnp.concatenate([mine, came], axis=1),
+            jnp.concatenate([came, mine], axis=1),
+        ),
+    )
+    if sums.shape[0] < blocks + PARTS:
+        tiles[per_part] = jnp.zeros(tiles.shape[1:], jnp.float32)
+    for token in range(tokens):
+        of_token = pl.ds(token, chips, stride=tokens)
+        for part in range(PARTS):
+            to = pl.ds(token * PARTS + part, chips, stride=tile)
+            for k in range(per_part):
+                tiles[k, to, :] = sums[part * per_part + k, of_token, :]
+            if blocks + part < sums.shape[0]:
+                tiles[per_part, to, :] = sums[blocks + part, of_token, :]
+    for k in range(lanes // 128):
+        out_ref[:, :, k * 128 : (k + 1) * 128] = (
+            tiles[k].astype(jnp.bfloat16).reshape(chips, tile, 128)
+        )
+
+
+def merge(core, own, came, adapter_own, adapter_came, own_rows):
+    half, chunk = own[0].shape
+    width = 2 * chunk
+    pair = 2 * adapter_own.shape[1]
+    lanes = width // PARTS + 128
+    chips, tile = half // own_rows, own_rows * PARTS
+    return pl.pallas_call(
+        merge_kernel,
+        in_specs=[SMEM] + [VMEM] * 6,
+        out_shape=jax.ShapeDtypeStruct((chips, tile, lanes), jnp.bfloat16),
+        scratch_shapes=[
+            pltpu.VMEM(((width + pair) // 128, half, 128), jnp.float32),
+            pltpu.VMEM((lanes // 128, chips * tile, 128), jnp.float32),
+        ],
+        compiler_params=pltpu.CompilerParams(vmem_limit_bytes=40 << 20),
+        name="merge",
+    )(core, own[0], own[1], came[0], came[1], adapter_own, adapter_came)
+
+
+def final_kernel(pair, came_ref, out_ref, total, adapter):
+    chips, tile, lanes = came_ref.shape
+    tokens = tile // PARTS
+    blocks = (lanes - 128) // 128
+    for k in range(blocks):
+        at = slice(k * 128, (k + 1) * 128)
+        value = came_ref[0, :, at].astype(jnp.float32)
+        for chip in range(1, chips):
+            value = value + came_ref[chip, :, at].astype(jnp.float32)
+        total[k] = value
+    adapter[...] = came_ref[:, :, lanes - 128 :].astype(jnp.float32).reshape(adapter.shape)
+    of_pair = pair // 128
+    for token in range(tokens):
+        rows = slice(token * PARTS, (token + 1) * PARTS)
+        for k in range(blocks):
+            chip, part = divmod(k, of_pair)
+            source = pl.ds(
+                chip * tile + token * PARTS + part, PARTS, stride=blocks // of_pair * tile
+            )
+            total[k, rows, :] += adapter[source, :]
+    for part in range(PARTS):
+        for k in range(blocks):
+            at = (part * blocks + k) * 128
+            out_ref[:, at : at + 128] = total[k, pl.ds(part, tokens, stride=PARTS), :].astype(
+                jnp.bfloat16
+            )
+
+
+def final(came, pair):
+    chips, tile, lanes = came.shape
+    piece = lanes - 128
+    return pl.pallas_call(
+        lambda *refs: final_kernel(pair, *refs),
+        out_shape=jax.ShapeDtypeStruct((tile // PARTS, piece * PARTS), jnp.bfloat16),
+        scratch_shapes=[
+            pltpu.VMEM((piece // 128, tile, 128), jnp.float32),
+            pltpu.VMEM((chips * tile, 128), jnp.float32),
+        ],
+        compiler_params=pltpu.CompilerParams(vmem_limit_bytes=40 << 20),
+        name="final",
+    )(came)
 
 
 def outer_kernel(left_ref, right_ref, out_ref):
@@ -213,11 +391,6 @@
 
 def other_core(block):
     return lax.ppermute(block, "tp", [(i, i ^ 1) for i in range(lax.axis_size("tp"))])
-
-
-def summed(block):
-    copies = jnp.broadcast_to(block[None], (lax.axis_size("tp"),) + block.shape)
-    return lax.all_to_all(copies, "tp", split_axis=0, concat_axis=0, tiled=True).sum(axis=0)
 
 
 def local(
@@ -243,12 +416,12 @@
         blocks = jnp.where(core == 0, blocks, blocks[:, ::-1])
         return blocks.swapaxes(0, 1).reshape(block.shape)
 
-    def returned(block):
-        blocks = block.reshape((2, chips, own_rows) + block.shape[1:]).swapaxes(0, 1)
-        return jnp.where(core == 0, blocks, blocks[:, ::-1]).reshape(block.shape)
+    def between_all(blocks):
+        return lax.all_to_all(blocks, "tp", split_axis=0, concat_axis=0, tiled=True)
 
     hidden = turned(hidden_unit_gradient)
     tenants = turned(token_tenant_index)[:, None]
+    core = core.reshape(1)
 
     own_tokens = between_same_cores(
         jnp.broadcast_to(normed_layer_input[None], (chips, own_rows, width))
@@ -257,38 +430,29 @@
     input_span = jnp.concatenate(
         [lax.dynamic_slice_in_dim(x, own * span, span, 1) for x in (own_tokens, other_tokens)], axis=0
     )
-    low = turned(summed(returned(low_part(input_span, adapter_down_maps, tenants))))
+    low = between_all(low_part(input_span, adapter_down_maps, tenants, count))
     gate, up = forward(own_tokens, other_tokens, gate_weight, up_weight)
-    dgate, dup, low_grad, input_spread = activation(
-        gate, up, hidden, low, tenants, adapter_up_maps
-    )
-    low_grad = turned(summed(returned(low_grad)))
-    grad_spread = spread_rows(low_grad, tenant_mask(tenants, rows))
-    adapter = (adapter_scale * contracted_columns(grad_spread, adapter_down_maps)).astype(
-        jnp.bfloat16
-    )
+    dgate, dgate_turned, dup_turned, low_grad, input_spread = activation(
+        core, gate, up, hidden, low, tenants, adapter_up_maps
+    )
+    low_grad = between_all(low_grad)
 
     chunk = width // 2
-    arrived = []
-    for start in (0, chunk):
-        own_part, other_part = backward(dgate, dup, gate_weight, up_weight, start, chunk)
-        if start > 0:
-            other_part = jnp.concatenate([other_part, adapter[half:]], axis=1)
-        came = other_core(other_part)
-        part = (own_part + came[:, :chunk].astype(jnp.float32)).astype(jnp.bfloat16)
-        if start > 0:
-            part = jnp.concatenate([part, adapter[:half], came[:, chunk:]], axis=1)
-        part = between_same_cores(part.reshape(chips, own_rows, part.shape[1]))
-        arrived.append(part.astype(jnp.float32))
-    down_map_gradient = outer(input_span, grad_spread, "down_maps")
+    own0, other0 = backward(rows, dgate_turned, dup_turned, gate_weight, up_weight, 0, chunk)
+    came0 = other_core(other0)
+    adapter_own, adapter_other, down_map_gradient = adapter_part(
+        core, low_grad, tenants, input_span, adapter_down_maps
+    )
+    dgate_turned, dup_turned, adapter_other = lax.optimization_barrier(
+        (dgate_turned, dup_turned, adapter_other)
+    )
+    adapter_came = other_core(adapter_other)
+    own1, other1 = backward(rows, dgate_turned, dup_turned, gate_weight, up_weight, chunk, chunk)
+    came1 = other_core(other1)
+    merged = merge(core, (own0, own1), (came0, came1), adapter_own, adapter_came, own_rows)
+    arrived = between_same_cores(merged)
     up_map_gradient = outer(input_spread, dgate, "up_maps")
-    pair = arrived[1][:, :, chunk:].reshape(chips, own_rows, 2, span)
-    pair = jnp.where(core == 0, pair, pair[:, :, ::-1])
-    total = jnp.concatenate(
-        [arrived[0].sum(axis=0), arrived[1][:, :, :chunk].sum(axis=0)], axis=1
-    )
-    total = total + pair.transpose(1, 0, 2, 3).reshape(own_rows, width)
-    return (total.astype(jnp.bfloat16), down_map_gradient, up_map_gradient)
+    return (final(arrived, 2 * span), down_map_gradient, up_map_gradient)
 
 
 def solution(mesh):

time: 138 us -> 122 us (0.88)
  local copies, waits for them, and re-layouts: 31.5 us -> 7.73 us
  Pallas kernels: 55.6 us -> 75 us
  other arithmetic: 6.97 us -> 0.11 us
  starting transfers between devices: 27 us -> 23.6 us
    unnamed x14 -> x12, local copies, waits for them, and re-layouts: 24.3 us -> 4.09 us
    pallas_call x2 -> x5, Pallas kernels: 4.1 us -> 13.3 us  [the longest x1 7.52 us: activation(): pl.pallas_call(activation_kernel, in_specs=[SMEM] + [VMEM] * 6, out_shape...]
    pallas_call x2, Pallas kernels: 24.1 us -> 31 us  [backward(): pl.pallas_call(backward_kernel, grid=(width // block,), in_specs=[gradien...]
    pallas_call x1, Pallas kernels: 19.6 us -> 24.8 us  [forward(): pl.pallas_call(forward_kernel, grid=(width // block,), in_specs=[tokens,...]
    all_to_all x3 -> x2, starting transfers between devices: 16.6 us -> 12.9 us  [between_same_cores(): lax.all_to_all(blocks, 'tp', split_axis=0, concat_axis=0, tiled=True, axi...]
    all_to_all x2 -> x0, other arithmetic: 2.79 us -> none  [summed(): lax.all_to_all(copies, 'tp', split_axis=0, concat_axis=0, tiled=True)]
    convert_element_type x5 -> x0, other arithmetic: 2.55 us -> none  [the longest x2 0.96 us: local(): part = (own_part + came[:, :chunk].astype(jnp.float32)).astype(jnp.bfloat16)]
    pallas_call x2 -> x1, Pallas kernels: 7.77 us -> 5.87 us  [outer(): pl.pallas_call(outer_kernel, grid=(height // block,), in_specs=[pl.BlockS...]
  transfers between devices with their start and end apart: 8 -> 8, of which waited for: 3 -> 5; matrix products, arithmetic and copies ran while one was open for 7% -> 2% of each run, Pallas kernels for 38% -> 53%
where the time goes in v4:
time: 122 us; the launch traced here: 121 us
  Pallas kernels  75 us (61%)
  starting transfers between devices  23.6 us (19%)
  waiting for transfers between devices  13.8 us (11%)
  local copies, waits for them, and re-layouts  7.73 us (6%)
    pallas_call x2, Pallas kernels, backward(): pl.pallas_call(backward_kernel, grid=(width // block,), in_specs=[gradien...  31 us
    pallas_call x1, Pallas kernels, forward(): pl.pallas_call(forward_kernel, grid=(width // block,), in_specs=[tokens,...  24.8 us
    all_to_all x2, starting transfers between devices, between_same_cores(): lax.all_to_all(blocks, 'tp', split_axis=0, concat_axis=0, tiled=True, axi...  12.9 us
    all_to_all x2, waiting for transfers between devices, between_same_cores(): lax.all_to_all(blocks, 'tp', split_axis=0, concat_axis=0, tiled=True, axi...  12.3 us
    all_to_all x2, starting transfers between devices, between_all(): return lax.all_to_all(blocks, 'tp', split_axis=0, concat_axis=0, tiled=True)  9.69 us
    pallas_call x1, Pallas kernels, activation(): pl.pallas_call(activation_kernel, in_specs=[SMEM] + [VMEM] * 6, out_shape...  7.52 us
    pallas_call x1, Pallas kernels, outer(): pl.pallas_call(outer_kernel, grid=(height // block,), in_specs=[pl.BlockS...  5.87 us
    unnamed x12, local copies, waits for them, and re-layouts  4.09 us
  transfers between devices with their start and end apart: 8, of which 5 were waited for; matrix products, arithmetic and copies ran while one was open for 2% of the time, Pallas kernels for 53%

profile of v4, /device:TPU:0, one launch (start us, length us, event | category | flops | bytes accessed | tf_op | source)
XLA Modules:
  0.0 120.9 jit_solution(2108362537686793510)
XLA Ops:
  0.6 1.6 %broadcast_in_dim.2 = bf16[8,2,8192]{2,1,0:T(2,128)(2,1)} broadcast(bf16[2,8192]{1,0:T(2,128)(2,1)} %param.7), dimensions={1,2} | broadcast | bytes 294912 | tf_op jit(solution)/shard_map/broadcast_in_dim | solution.py:427
  2.2 7.3 %all-to-all-start = ((bf16[8,2,8192]{2,1,0:T(2,128)(2,1)}), bf16[8,2,8192]{2,1,0:T(2,128)(2,1)S(1)}, u32[]{:S(2)}, u32[]{:S(2)}) async-start(bf16[8,2,8192]{2,1,0:T(2,128)(2,1)} %broadcast_in_dim.2), calls=%async_computation | async-start | bytes 524288 | tf_op jit(solution)/shard_map/all_to_all | solution.py:387
  9.5 0.7 reshape.26
  10.3 8.1 %all-to-all-done = bf16[8,2,8192]{2,1,0:T(2,128)(2,1)S(1)} async-done(((bf16[8,2,8192]{2,1,0:T(2,128)(2,1)}), bf16[8,2,8192]{2,1,0:T(2,128)(2,1)S(1)}, u32[]{:S(2)}, u32[]{:S(2)}) %all-to-all-start) | async-done | bytes 262176 | tf_op jit(solution)/shard_map/all_to_all | solution.py:387
  18.4 0.1 reshape.23.own_ref
  18.5 0.1 collective-permute-start
  18.6 0.1 broadcast_in_dim_reshape.4.tenants_ref
  18.7 0.9 reshape.24
  19.7 0.1 copy.17
  19.8 0.4 collective-permute-done.other_ref
  20.1 0.0 copy-start
  20.1 1.6 %copy-done = bf16[512,2048]{1,0:T(8,128)(2,1)S(1)} copy-done((bf16[512,2048]{1,0:T(8,128)(2,1)S(1)}, bf16[512,2048]{1,0:T(8,128)(2,1)}, u32[]{:S(2)}) %copy-start) | copy-done | bytes 2097176
  21.7 1.3 %low_part.1 = f32[16,16,128]{2,1,0:T(8,128)} custom-call(bf16[32,512]{1,0:T(8,128)(2,1)S(1)} %pad_maximum_fusion.span_ref, bf16[512,2048]{1,0:T(8,128)(2,1)S(1)} %copy-done, s32[32,1]{1,0:T(8,128)S(1)} %broadcast_in_dim_reshape.4.tenants_ref), custom_call_target="tpu_custom_call" | custom-call | flops 67108864 | bytes 2097152 | tf_op jit(solution)/shard_map/low_part/pallas_call | solution.py:86
  23.0 3.7 %all-to-all-start.1 = ((f32[16,16,128]{2,1,0:T(8,128)}), f32[16,16,128]{2,1,0:T(8,128)S(1)}, u32[]{:S(2)}, u32[]{:S(2)}) async-start(f32[16,16,128]{2,1,0:T(8,128)} %low_part.1), calls=%async_computation.1 | async-start | bytes 262144 | tf_op jit(solution)/shard_map/all_to_all | solution.py:420
  26.7 0.1 fusion
  26.9 24.8 %forward.1 = (f32[32,1792]{1,0:T(8,128)S(1)}, f32[32,1792]{1,0:T(8,128)S(1)}) custom-call(bf16[16,8192]{1,0:T(8,128)(2,1)S(1)} %reshape.23.own_ref, bf16[16,8192]{1,0:T(8,128)(2,1)S(1)} %collective-permute-done.other_ref, bf16[8192,1792]{1,0:T(8,128)(2,1)} %gate_ref.5, bf16[8192,1792]{1,0:T(8,128)(2,1)} %up_ref.5), custom_call_target="tpu_custom_call" | custom-call | flops 1879048192 | bytes 58720256 | tf_op jit(solution)/shard_map/forward/pallas_call | solution.py:116
  51.7 0.0 all-to-all-done.1.low_ref
  51.7 7.5 %activation.1 = (bf16[32,1792]{1,0:T(8,128)(2,1)S(1)}, bf16[1792,128]{1,0:T(8,128)(2,1)S(1)}, bf16[1792,128]{1,0:T(8,128)(2,1)S(1)}, f32[16,16,128]{2,1,0:T(8,128)}, bf16[32,2048]{1,0:T(8,128)(2,1)S(1)}) custom-call(s32[1]{0:T(128)} %bitcast.core_ref, f32[32,1792]{1,0:T(8,128)S(1)} %get-tuple-element.20.gate_ref, f32[32,1792]{1,0:T(8,128)S(1)} %get-tuple-element.21.up_ref, ...), custom_call_target="tpu_custom_call" | custom-call | flops 469762048 | bytes 7340032 | tf_op jit(solution)/shard_map/activation/pallas_call | solution.py:164
  59.2 0.0 copy-start.2
  59.2 0.8 copy-done.2
  60.0 0.0 copy-start.3
  60.0 0.8 copy-done.3
  60.7 6.0 %all-to-all-start.2 = ((f32[16,16,128]{2,1,0:T(8,128)}), f32[16,16,128]{2,1,0:T(8,128)S(1)}, u32[]{:S(2)}, u32[]{:S(2)}) async-start(f32[16,16,128]{2,1,0:T(8,128)} %get-tuple-element.25), calls=%async_computation.2 | async-start | bytes 262144 | tf_op jit(solution)/shard_map/all_to_all | solution.py:420
  66.7 0.0 copy-start.1
  66.8 15.6 %backward.2 = (f32[16,4096]{1,0:T(8,128)}, bf16[16,4096]{1,0:T(8,128)(2,1)}) custom-call(bf16[1792,128]{1,0:T(8,128)(2,1)} %copy-done.2, bf16[1792,128]{1,0:T(8,128)(2,1)} %copy-done.3, bf16[8192,1792]{1,0:T(8,128)(2,1)} %gate_ref.5, bf16[8192,1792]{1,0:T(8,128)(2,1)} %up_ref.5), custom_call_target="tpu_custom_call" | custom-call | flops 939524096 | bytes 29360128 | tf_op jit(solution)/shard_map/backward/pallas_call | solution.py:229
  82.3 0.4 collective-permute-start.1
  82.7 0.0 all-to-all-done.2.low_ref
  82.7 0.0 copy-done.1
  82.7 2.7 %adapter_part.1 = (bf16[16,512]{1,0:T(8,128)(2,1)S(1)}, bf16[16,512]{1,0:T(8,128)(2,1)S(1)}, bf16[512,2048]{1,0:T(8,128)(2,1)}) custom-call(s32[1]{0:T(128)} %bitcast.core_ref, f32[16,16,128]{2,1,0:T(8,128)S(1)} %all-to-all-done.2.low_ref, s32[32,1]{1,0:T(8,128)S(1)} %broadcast_in_dim_reshape.4.tenants_ref, bf16[32,512]{1,0:T(8,128)(2,1)S(1)} %pad_maximum_fusion.span_ref, ...), custom_call_target="tpu_custom_call" | custom-call | flops 134217728 | bytes 4194304 | tf_op jit(solution)/shard_map/adapter_part/pallas_call | solution.py:200
  85.4 0.0 copy-start.4
  85.4 15.5 %backward.3 = (f32[16,4096]{1,0:T(8,128)}, bf16[16,4096]{1,0:T(8,128)(2,1)}) custom-call(bf16[1792,128]{1,0:T(8,128)(2,1)} %copy-done.2, bf16[1792,128]{1,0:T(8,128)(2,1)} %copy-done.3, bf16[8192,1792]{1,0:T(8,128)(2,1)} %gate_ref.5, bf16[8192,1792]{1,0:T(8,128)(2,1)} %up_ref.5), custom_call_target="tpu_custom_call" | custom-call | flops 939524096 | bytes 29360128 | tf_op jit(solution)/shard_map/backward/pallas_call | solution.py:229
  100.9 0.1 collective-permute-start.2
  101.0 0.4 collective-permute-start.3
  101.4 0.0 collective-permute-done.1.came0
  101.4 0.9 collective-permute-done.3.adapter_came
  102.3 0.2 collective-permute-done.2.came1
  102.5 0.0 copy-done.4
  102.5 0.0 copy-start.5
  102.5 0.9 copy-done.5
  103.4 1.1 merge.1
  104.5 5.7 %all-to-all-start.3 = ((bf16[8,16,1152]{2,1,0:T(8,128)(2,1)}), bf16[8,16,1152]{2,1,0:T(8,128)(2,1)S(1)}, u32[]{:S(2)}, u32[]{:S(2)}) async-start(bf16[8,16,1152]{2,1,0:T(8,128)(2,1)} %merge.1), calls=%async_computation.3 | async-start | bytes 589824 | tf_op jit(solution)/shard_map/all_to_all | solution.py:387
  110.2 5.9 %up_maps.1 = bf16[2048,1792]{1,0:T(8,128)(2,1)} custom-call(bf16[32,2048]{1,0:T(8,128)(2,1)S(1)} %get-tuple-element.35.left_ref, bf16[32,1792]{1,0:T(8,128)(2,1)S(1)} %get-tuple-element.36.right_ref), custom_call_target="tpu_custom_call" | custom-call | flops 234881024 | bytes 7340032 | tf_op jit(solution)/shard_map/up_maps/pallas_call | solution.py:364
  116.0 4.2 %all-to-all-done.3.refs_0_ = bf16[8,16,1152]{2,1,0:T(8,128)(2,1)S(1)} async-done(((bf16[8,16,1152]{2,1,0:T(8,128)(2,1)}), bf16[8,16,1152]{2,1,0:T(8,128)(2,1)S(1)}, u32[]{:S(2)}, u32[]{:S(2)}) %all-to-all-start.3) | async-done | bytes 294944 | tf_op jit(solution)/shard_map/all_to_all | solution.py:387
  120.2 0.7 final.1
  (7 shorter events, 0.1 us)
Async XLA Ops:
  2.2 16.2 %all-to-all-start = ((bf16[8,2,8192]{2,1,0:T(2,128)(2,1)}), bf16[8,2,8192]{2,1,0:T(2,128)(2,1)S(1)}, u32[]{:S(2)}, u32[]{:S(2)}) async-start(bf16[8,2,8192]{2,1,0:T(2,128)(2,1)} %broadcast_in_dim.2), calls=%async_computation | async-start | bytes 524288 | tf_op jit(solution)/shard_map/all_to_all | solution.py:387
  18.5 1.6 %collective-permute-start = (bf16[16,8192]{1,0:T(8,128)(2,1)S(1)}, bf16[16,8192]{1,0:T(8,128)(2,1)S(1)}, u32[]{:S(2)}, u32[]{:S(2)}) collective-permute-start(bf16[16,8192]{1,0:T(8,128)(2,1)S(1)} %reshape.23.own_ref), channel_id=1, source_target_pairs={{0,1},{1,0},{2,3},{3,2},{4,5},{5,4},{6,7},{7,6},{8,9},{9,8},{10,11... | collective-permute-start | bytes 786440 | tf_op jit(solution)/shard_map/ppermute | solution.py:393
  20.1 1.6 %copy-start = (bf16[512,2048]{1,0:T(8,128)(2,1)S(1)}, bf16[512,2048]{1,0:T(8,128)(2,1)}, u32[]{:S(2)}) copy-start(bf16[512,2048]{1,0:T(8,128)(2,1)} %down_ref.3) | copy-start | bytes 6291460
  23.0 28.7 %all-to-all-start.1 = ((f32[16,16,128]{2,1,0:T(8,128)}), f32[16,16,128]{2,1,0:T(8,128)S(1)}, u32[]{:S(2)}, u32[]{:S(2)}) async-start(f32[16,16,128]{2,1,0:T(8,128)} %low_part.1), calls=%async_computation.1 | async-start | bytes 262144 | tf_op jit(solution)/shard_map/all_to_all | solution.py:420
  59.2 0.8 copy-start.2
  60.0 0.8 copy-start.3
  60.7 22.0 %all-to-all-start.2 = ((f32[16,16,128]{2,1,0:T(8,128)}), f32[16,16,128]{2,1,0:T(8,128)S(1)}, u32[]{:S(2)}, u32[]{:S(2)}) async-start(f32[16,16,128]{2,1,0:T(8,128)} %get-tuple-element.25), calls=%async_computation.2 | async-start | bytes 262144 | tf_op jit(solution)/shard_map/all_to_all | solution.py:420
  66.7 16.0 %copy-start.1 = (bf16[512,2048]{1,0:T(8,128)(2,1)S(1)}, bf16[512,2048]{1,0:T(8,128)(2,1)}, u32[]{:S(2)}) copy-start(bf16[512,2048]{1,0:T(8,128)(2,1)} %down_ref.3) | copy-start | bytes 6291460
  82.3 19.1 %collective-permute-start.1 = (bf16[16,4096]{1,0:T(8,128)(2,1)}, bf16[16,4096]{1,0:T(8,128)(2,1)S(1)}, u32[]{:S(2)}, u32[]{:S(2)}) collective-permute-start(bf16[16,4096]{1,0:T(8,128)(2,1)} %get-tuple-element.30), channel_id=1, source_target_pairs={{0,1},{1,0},{2,3},{3,2},{4,5},{5,4},{6,7},{7,6},{8,9},{9,8},{10,11... | collective-permute-start | bytes 393224 | tf_op jit(solution)/shard_map/ppermute | solution.py:393
  85.4 17.0 %copy-start.4 = (f32[16,4096]{1,0:T(8,128)S(1)}, f32[16,4096]{1,0:T(8,128)}, u32[]{:S(2)}) copy-start(f32[16,4096]{1,0:T(8,128)} %get-tuple-element.24.own0) | copy-start | bytes 786436
  100.9 1.6 %collective-permute-start.2 = (bf16[16,4096]{1,0:T(8,128)(2,1)}, bf16[16,4096]{1,0:T(8,128)(2,1)S(1)}, u32[]{:S(2)}, u32[]{:S(2)}) collective-permute-start(bf16[16,4096]{1,0:T(8,128)(2,1)} %get-tuple-element.31), channel_id=1, source_target_pairs={{0,1},{1,0},{2,3},{3,2},{4,5},{5,4},{6,7},{7,6},{8,9},{9,8},{10,11... | collective-permute-start | bytes 393224 | tf_op jit(solution)/shard_map/ppermute | solution.py:393
  101.0 1.3 %collective-permute-start.3 = (bf16[16,512]{1,0:T(8,128)(2,1)S(1)}, bf16[16,512]{1,0:T(8,128)(2,1)S(1)}, u32[]{:S(2)}, u32[]{:S(2)}) collective-permute-start(bf16[16,512]{1,0:T(8,128)(2,1)S(1)} %get-tuple-element.33), channel_id=1, source_target_pairs={{0,1},{1,0},{2,3},{3,2},{4,5},{5,4},{6,7},{7,6},{8,9},{9,8},{10,11... | collective-permute-start | bytes 49160 | tf_op jit(solution)/shard_map/ppermute | solution.py:393
  102.5 1.0 copy-start.5
  104.5 15.7 %all-to-all-start.3 = ((bf16[8,16,1152]{2,1,0:T(8,128)(2,1)}), bf16[8,16,1152]{2,1,0:T(8,128)(2,1)S(1)}, u32[]{:S(2)}, u32[]{:S(2)}) async-start(bf16[8,16,1152]{2,1,0:T(8,128)(2,1)} %merge.1), calls=%async_computation.3 | async-start | bytes 589824 | tf_op jit(solution)/shard_map/all_to_all | solution.py:387

commit v5 on v4

v5 whole, which is shorter than its diff:
```python
import jax
import jax.numpy as jnp
from jax import lax
from jax.experimental import pallas as pl
from jax.experimental.pallas import tpu as pltpu
from jax.sharding import PartitionSpec as P

ADAPTER_RANK = 64
TENANT_COUNT = 32
SPREAD = ADAPTER_RANK * TENANT_COUNT

adapter_scale = 2.0


def block_of(size, largest):
    block = largest
    while size % block:
        block //= 2
    return block


def contracted_rows(left, right):
    return lax.dot_general(
        left, right, (((0,), (0,)), ((), ())), preferred_element_type=jnp.float32
    )


def contracted_columns(left, right):
    return lax.dot_general(
        left, right, (((1,), (1,)), ((), ())), preferred_element_type=jnp.float32
    )


def tenant_mask(tenants, rows):
    columns = lax.broadcasted_iota(jnp.int32, (rows, SPREAD), 1) // ADAPTER_RANK
    return tenants == columns


def select_block(wide_rows, mask):
    kept = jnp.where(mask, wide_rows, 0.0)
    pair = 2 * ADAPTER_RANK
    total = kept[:, :pair]
    for start in range(pair, SPREAD, pair):
        total = total + kept[:, start : start + pair]
    return total[:, :ADAPTER_RANK] + total[:, ADAPTER_RANK:]


def spread_rows(low_rows, mask):
    pair = jnp.concatenate([low_rows, low_rows], axis=1)
    wide = jnp.concatenate([pair] * (TENANT_COUNT // 2), axis=1)
    return jnp.where(mask, wide, 0.0).astype(jnp.bfloat16)


VMEM = pl.BlockSpec(memory_space=pltpu.VMEM)
SMEM = pl.BlockSpec(memory_space=pltpu.SMEM)
ANY = pl.BlockSpec(memory_space=pl.ANY)
HBM = pl.BlockSpec(memory_space=pltpu.HBM)
CUTS = 4
COPIES = 4


def with_fetches(kernel, wanted, operands, out_shapes, vmem_mib, flops, name, after=()):
    sources = []
    for weight, _ in wanted:
        if not any(weight is known for known in sources):
            sources.append(weight)
    places = [
        next(i for i, known in enumerate(sources) if known is weight) for weight, _ in wanted
    ]
    n_in, n_out = len(operands), len(out_shapes)

    def body(*refs):
        ins = refs[:n_in]
        hbm = refs[n_in : n_in + len(sources)]
        rest = refs[n_in + len(sources) + len(after) :]
        outs, pieces = rest[:n_out], rest[n_out : n_out + len(wanted)]
        scratch = rest[n_out + len(wanted) :]
        copies = []
        for n, (place, (_, cut)) in enumerate(zip(places, wanted)):
            part = pieces[n].shape[0] // COPIES
            for k in range(COPIES):
                copies.append(
                    pltpu.make_async_copy(
                        hbm[place].at[pl.ds(cut * part * COPIES + k * part, part)],
                        pieces[n].at[pl.ds(k * part, part)],
                        scratch[0].at[n * COPIES + k],
                    )
                )
        for copy in copies:
            copy.start()
        kernel(*ins, *outs)
        for copy in copies:
            copy.wait()

    piece_shapes = [
        pltpu.VMEM((weight.shape[0] // (CUTS if cut is not None else 1), weight.shape[1]), weight.dtype)
        for weight, cut in wanted
    ]
    wanted = [(weight, cut or 0) for weight, cut in wanted]
    moved = sum(2 * shape.shape[0] * shape.shape[1] for shape in piece_shapes)
    return pl.pallas_call(
        body,
        in_specs=[VMEM] * n_in + [HBM] * len(sources) + [ANY] * len(after),
        out_specs=[VMEM] * n_out + [ANY] * len(wanted),
        out_shape=list(out_shapes) + piece_shapes,
        scratch_shapes=[pltpu.SemaphoreType.DMA((COPIES * len(wanted),))] if wanted else [],
        compiler_params=pltpu.CompilerParams(vmem_limit_bytes=vmem_mib << 20),
        cost_estimate=pl.CostEstimate(flops=flops, bytes_accessed=moved, transcendentals=0),
        name=name,
    )(*operands, *[pltpu.with_memory_space_constraint(w, pltpu.HBM) for w in sources], *after)


def stacked(blocks, after=()):
    rows = sum(block.shape[0] for block in blocks)

    def stack_kernel(*refs):
        refs[-1][...] = jnp.concatenate([ref[...] for ref in refs[: len(blocks)]], axis=0)

    return pl.pallas_call(
        stack_kernel,
        in_specs=[VMEM] * len(blocks) + [ANY] * len(after),
        out_shape=jax.ShapeDtypeStruct((rows, blocks[0].shape[1]), blocks[0].dtype),
        compiler_params=pltpu.CompilerParams(vmem_limit_bytes=8 << 20),
        name="stacked",
    )(*blocks, *after)


def turned_rows(source, block):
    rows = source.shape[0]
    pick = source == lax.broadcasted_iota(jnp.int32, (rows, rows), 1)
    if block.dtype == jnp.bfloat16:
        return jnp.dot(pick.astype(jnp.bfloat16), block, preferred_element_type=jnp.float32)
    return jnp.dot(pick.astype(jnp.float32), block, precision=lax.Precision.HIGHEST)


def returned_rows(source_row, block):
    rows = source_row.shape[1]
    pick = source_row == lax.broadcasted_iota(jnp.int32, (rows, rows), 0)
    return jnp.dot(pick.astype(jnp.float32), block, precision=lax.Precision.HIGHEST)


def held_mask(source, tenants_row):
    rows = source.shape[0]
    pick = source == lax.broadcasted_iota(jnp.int32, (rows, rows), 1)
    tenants = jnp.sum(jnp.where(pick, tenants_row, 0).astype(jnp.float32), axis=1, keepdims=True)
    return tenant_mask(tenants.astype(jnp.int32), rows)


def low_kernel(span_ref, down_ref, tenants_ref, source_ref, source_row_ref, low_ref):
    wide = jnp.dot(span_ref[...], down_ref[...], preferred_element_type=jnp.float32)
    low = select_block(wide, held_mask(source_ref[...], tenants_ref[...]))
    low_ref[...] = returned_rows(source_row_ref[...], low)


def low_part(span, down, tenants, source, source_row):
    rows = span.shape[0]
    return pl.pallas_call(
        low_kernel,
        out_shape=jax.ShapeDtypeStruct((rows, ADAPTER_RANK), jnp.float32),
        compiler_params=pltpu.CompilerParams(vmem_limit_bytes=10 << 20),
        cost_estimate=pl.CostEstimate(
            flops=2 * rows * down.size, bytes_accessed=2 * down.size, transcendentals=0
        ),
        name="low_part",
    )(span, down, tenants, source, source_row)


def forward_kernel(cut, blocks, first, refs):
    x = refs[:blocks]
    gate_ref, up_ref = refs[blocks : blocks + 2]
    gate_out, up_out = refs[-2:]
    depth = gate_ref.shape[0]
    at = slice(cut * depth, (cut + 1) * depth)
    rows = jnp.concatenate([ref[:, at] for ref in x], axis=0)
    gate = jnp.dot(rows, gate_ref[...], preferred_element_type=jnp.float32)
    up = jnp.dot(rows, up_ref[...], preferred_element_type=jnp.float32)
    if not first:
        gate = gate + refs[blocks + 2][...]
        up = up + refs[blocks + 3][...]
    gate_out[...] = gate
    up_out[...] = up


def forward(cut, x, pieces, sums, wanted, after):
    rows = sum(block.shape[0] for block in x)
    depth, hidden = pieces[0].shape
    result = jax.ShapeDtypeStruct((rows, hidden), jnp.float32)
    return with_fetches(
        lambda *refs: forward_kernel(cut, len(x), not sums, refs),
        wanted,
        [*x, *pieces, *sums],
        [result, result],
        8,
        4 * rows * depth * hidden,
        "forward",
        after,
    )


def activation_kernel(
    gate_ref, up_ref, hidden_ref, low_ref, tenants_ref, source_ref, source_row_ref, maps_ref,
    dgate_ref, dup_ref, part_ref, spread_ref,
):
    source = source_ref[...]
    mask = held_mask(source, tenants_ref[...])
    spread = spread_rows(turned_rows(source, low_ref[...]), mask)
    spread_ref[...] = spread
    gate = gate_ref[...] + adapter_scale * jnp.dot(
        spread, maps_ref[...], preferred_element_type=jnp.float32
    )
    s = jax.nn.sigmoid(gate)
    hidden = turned_rows(source, hidden_ref[...])
    dgate = (hidden * up_ref[...] * s * (1.0 + gate * (1.0 - s))).astype(jnp.bfloat16)
    dgate_ref[...] = dgate
    dup_ref[...] = (hidden * gate * s).astype(jnp.bfloat16)
    part = select_block(contracted_columns(dgate, maps_ref[...]), mask)
    part_ref[...] = returned_rows(source_row_ref[...], part)


def activation(gate, up, hidden, low, tenants, source, source_row, maps, wanted):
    rows, width = gate.shape
    value = jax.ShapeDtypeStruct((rows, width), jnp.bfloat16)
    return with_fetches(
        activation_kernel,
        wanted,
        [gate, up, hidden, low, tenants, source, source_row, maps],
        [
            value,
            value,
            jax.ShapeDtypeStruct((rows, ADAPTER_RANK), jnp.float32),
            jax.ShapeDtypeStruct((rows, SPREAD), jnp.bfloat16),
        ],
        10,
        4 * rows * maps.size,
        "activation",
    )


def adapter_kernel(low_ref, tenants_ref, source_ref, down_ref, own_out, other_out, spread_ref):
    source = source_ref[...]
    half = own_out.shape[0]
    spread = spread_rows(
        turned_rows(source, low_ref[...]), held_mask(source, tenants_ref[...])
    )
    spread_ref[...] = spread
    part = (adapter_scale * contracted_columns(spread, down_ref[...])).astype(jnp.bfloat16)
    own_out[...] = part[:half]
    other_out[...] = part[half:]


def adapter_part(low, tenants, source, down):
    rows, span = low.shape[0], down.shape[0]
    half = jax.ShapeDtypeStruct((rows // 2, span), jnp.bfloat16)
    return pl.pallas_call(
        adapter_kernel,
        out_shape=[half, half, jax.ShapeDtypeStruct((rows, SPREAD), jnp.bfloat16)],
        compiler_params=pltpu.CompilerParams(vmem_limit_bytes=10 << 20),
        cost_estimate=pl.CostEstimate(
            flops=2 * rows * down.size, bytes_accessed=2 * down.size, transcendentals=0
        ),
        name="adapter_part",
    )(low, tenants, source, down)


def backward_kernel(dgate_ref, dup_ref, gate_ref, up_ref, own_out, other_out):
    half = own_out.shape[0]
    part = contracted_columns(dgate_ref[...], gate_ref[...])
    part = part + contracted_columns(dup_ref[...], up_ref[...])
    own_out[...] = part[:half]
    other_out[...] = part[half:].astype(jnp.bfloat16)


def backward(dgate, dup, pieces, wanted, after):
    rows, hidden = dgate.shape
    depth = pieces[0].shape[0]
    return with_fetches(
        backward_kernel,
        wanted,
        [dgate, dup, *pieces],
        [
            jax.ShapeDtypeStruct((rows // 2, depth), jnp.float32),
            jax.ShapeDtypeStruct((rows // 2, depth), jnp.bfloat16),
        ],
        8,
        4 * rows * hidden * depth,
        "backward",
        after,
    )


PARTS = 8


def merge_kernel(chip_ref, core_ref, *refs):
    own, came = refs[:CUTS], refs[CUTS : 2 * CUTS]
    adapter_own, adapter_came, out_ref, sums, tiles = refs[2 * CUTS :]
    chips, tile, lanes = out_ref.shape
    tokens = tile // PARTS
    per_part = (lanes - 128) // 128
    blocks = PARTS * per_part

    def put(first, value):
        for k in range(value.shape[1] // 128):
            sums[first + k] = value[:, k * 128 : (k + 1) * 128]

    for cut in range(CUTS):
        put(cut * blocks // CUTS, own[cut][...] + came[cut][...].astype(jnp.float32))
    mine = adapter_own[...].astype(jnp.float32)
    other = adapter_came[...].astype(jnp.float32)
    put(
        blocks,
        jnp.where(
            core_ref[0] == 0,
            jnp.concatenate([mine, other], axis=1),
            jnp.concatenate([other, mine], axis=1),
        ),
    )
    if sums.shape[0] < blocks + PARTS:
        tiles[per_part] = jnp.zeros(tiles.shape[1:], jnp.float32)
    for token in range(tokens):
        of_token = pl.ds(token, chips, stride=tokens)
        for part in range(PARTS):
            to = pl.ds(token * PARTS + part, chips, stride=tile)
            for k in range(per_part):
                tiles[k, to, :] = sums[part * per_part + k, of_token, :]
            if blocks + part < sums.shape[0]:
                tiles[per_part, to, :] = sums[blocks + part, of_token, :]
    for position in range(chips):
        chip = chip_ref[position]
        for k in range(lanes // 128):
            out_ref[chip, :, k * 128 : (k + 1) * 128] = tiles[
                k, position * tile : (position + 1) * tile, :
            ].astype(jnp.bfloat16)


def merge(chip_table, core, own, came, adapter_own, adapter_came, own_rows):
    half, depth = own[0].shape
    width = CUTS * depth
    pair = 2 * adapter_own.shape[1]
    lanes = width // PARTS + 128
    chips, tile = half // own_rows, own_rows * PARTS
    return pl.pallas_call(
        merge_kernel,
        in_specs=[SMEM] * 2 + [VMEM] * (2 * CUTS + 2),
        out_shape=jax.ShapeDtypeStruct((chips, tile, lanes), jnp.bfloat16),
        scratch_shapes=[
            pltpu.VMEM(((width + pair) // 128, half, 128), jnp.float32),
            pltpu.VMEM((lanes // 128, chips * tile, 128), jnp.float32),
        ],
        compiler_params=pltpu.CompilerParams(vmem_limit_bytes=40 << 20),
        name="merge",
    )(chip_table, core, *own, *came, adapter_own, adapter_came)


def final_kernel(pair, came_ref, out_ref, total, adapter):
    chips, tile, lanes = came_ref.shape
    tokens = tile // PARTS
    blocks = (lanes - 128) // 128
    for k in range(blocks):
        at = slice(k * 128, (k + 1) * 128)
        value = came_ref[0, :, at].astype(jnp.float32)
        for chip in range(1, chips):
            value = value + came_ref[chip, :, at].astype(jnp.float32)
        total[k] = value
    adapter[...] = came_ref[:, :, lanes - 128 :].astype(jnp.float32).reshape(adapter.shape)
    of_pair = pair // 128
    for token in range(tokens):
        rows = slice(token * PARTS, (token + 1) * PARTS)
        for k in range(blocks):
            chip, part = divmod(k, of_pair)
            source = pl.ds(
                chip * tile + token * PARTS + part, PARTS, stride=blocks // of_pair * tile
            )
            total[k, rows, :] += adapter[source, :]
    for part in range(PARTS):
        for k in range(blocks):
            at = (part * blocks + k) * 128
            out_ref[:, at : at + 128] = total[k, pl.ds(part, tokens, stride=PARTS), :].astype(
                jnp.bfloat16
            )


def final(came, pair):
    chips, tile, lanes = came.shape
    piece = lanes - 128
    return pl.pallas_call(
        lambda *refs: final_kernel(pair, *refs),
        out_shape=jax.ShapeDtypeStruct((tile // PARTS, piece * PARTS), jnp.bfloat16),
        scratch_shapes=[
            pltpu.VMEM((piece // 128, tile, 128), jnp.float32),
            pltpu.VMEM((chips * tile, 128), jnp.float32),
        ],
        compiler_params=pltpu.CompilerParams(vmem_limit_bytes=40 << 20),
        name="final",
    )(came)


def outer_kernel(left_ref, right_ref, out_ref):
    out_ref[...] = contracted_rows(
        left_ref[...] * jnp.bfloat16(adapter_scale), right_ref[...]
    ).astype(jnp.bfloat16)


def outer(left, right, name):
    rows, height = left.shape
    width = right.shape[1]
    block = block_of(height, 256)
    if block % 128:
        block = height
    return pl.pallas_call(
        outer_kernel,
        grid=(height // block,),
        in_specs=[
            pl.BlockSpec((rows, block), lambda k: (0, k)),
            pl.BlockSpec((rows, width), lambda k: (0, 0)),
        ],
        out_specs=pl.BlockSpec((block, width), lambda k: (k, 0)),
        out_shape=jax.ShapeDtypeStruct((height, width), jnp.bfloat16),
        compiler_params=pltpu.CompilerParams(vmem_limit_bytes=24 << 20),
        cost_estimate=pl.CostEstimate(
            flops=2 * rows * height * width, bytes_accessed=2 * height * width, transcendentals=0
        ),
        name=name,
    )(left, right)


def same_core_groups():
    count = lax.axis_size("tp")
    return [list(range(core, count, 2)) for core in range(2)]


def between_same_cores(blocks):
    return lax.all_to_all(
        blocks, "tp", split_axis=0, concat_axis=0, tiled=True, axis_index_groups=same_core_groups()
    )


def swapped(block, hop):
    return lax.ppermute(block, "tp", [(i, i ^ hop) for i in range(lax.axis_size("tp"))])


def local(
    normed_layer_input,
    hidden_unit_gradient,
    gate_weight,
    up_weight,
    adapter_down_maps,
    adapter_up_maps,
    token_tenant_index,
):
    count = lax.axis_size("tp")
    own = lax.axis_index("tp")
    own_rows, width = normed_layer_input.shape
    rows = own_rows * count
    span = adapter_down_maps.shape[0]
    hops = [1 << bit for bit in range(count.bit_length() - 1)]

    far, near = hops[-1], hops[-2]
    order = [0, near, far, near | far]
    for hop in reversed(hops[:-2]):
        order = order + [p ^ hop for p in order]
    order = jnp.array(order, jnp.int32)
    held = (order ^ own)[:, None] * own_rows + jnp.arange(own_rows, dtype=jnp.int32)
    source, source_row = held.reshape(rows, 1), held.reshape(1, rows)
    chip_table = (order[: count // 2] ^ own) // 2
    core = (own % 2).reshape(1)
    start = own * span
    tenants = token_tenant_index.reshape(1, rows)
    normed_layer_input, source, source_row, chip_table, core, start, tenants = (
        lax.optimization_barrier(
            (normed_layer_input, source, source_row, chip_table, core, start, tenants)
        )
    )

    def fetched(cut, after):
        return with_fetches(
            lambda *refs: None, [(gate_weight, cut), (up_weight, cut)], [], [], 1, 0, "fetch", after
        )

    pieces = {}
    came = [swapped(normed_layer_input, hop) for hop in (near, far, near | far)]
    pieces[0] = fetched(0, [source, source_row, chip_table, core, tenants])
    block = stacked([normed_layer_input, *came], pieces[0])
    for hop in reversed(hops[2:-2]):
        block = stacked([block, swapped(block, hop)])
    other = swapped(block, hops[1])
    x = [block, other, swapped(block, 1), swapped(other, 1)]
    pieces[1] = fetched(1, [block, *pieces[0]])

    input_span = jnp.concatenate(
        [lax.dynamic_slice_in_dim(part, start, span, 1) for part in x], axis=0
    )
    low = low_part(input_span, adapter_down_maps, tenants, source, source_row)
    sums = []
    wanted = {
        0: [(gate_weight, 2), (up_weight, 2)],
        1: [(gate_weight, 3), (up_weight, 3)],
        2: [(adapter_up_maps, None)],
        3: [],
    }
    step = 0
    for cut in range(CUTS):
        after = [low]
        if step < len(hops):
            low = low + swapped(low, hops[step])
            step += 1
        *sums, = forward(cut, x, pieces[cut], sums, wanted[cut], after)
        sums, extra = sums[:2], sums[2:]
        if cut < 2:
            pieces[cut + 2] = extra
        elif cut == 2:
            maps = extra[0]
    for hop in hops[step:]:
        low = low + swapped(low, hop)
    dgate, dup, low_grad, input_spread, gate1 = activation(
        *sums, hidden_unit_gradient, low, tenants, source, source_row, maps, [(gate_weight, 1)]
    )

    low_grad = low_grad + swapped(low_grad, hops[0])
    step = 1
    parts, arrived = {}, {}
    wanted = {3: [(up_weight, 1), (gate_weight, 0)], 2: [(up_weight, 0)], 1: [], 0: []}
    after = [low_grad]
    for cut in reversed(range(CUTS)):
        if cut > 0:
            after = [low_grad]
            if step < len(hops):
                low_grad = low_grad + swapped(low_grad, hops[step])
                step += 1
        own_part, other_part, *extra = backward(dgate, dup, pieces[cut], wanted[cut], after)
        if cut == 3:
            pieces[1] = [gate1, extra[0]]
            gate0 = extra[1]
        elif cut == 2:
            pieces[0] = [gate0, extra[0]]
        elif cut == 1:
            for hop in hops[step:]:
                low_grad = low_grad + swapped(low_grad, hop)
            adapter_own, adapter_other, grad_spread = adapter_part(
                low_grad, tenants, source, adapter_down_maps
            )
            adapter_came = swapped(adapter_other, 1)
            after = [adapter_other]
        parts[cut] = own_part
        arrived[cut] = swapped(other_part, 1)
    merged = merge(
        chip_table,
        core,
        [parts[cut] for cut in range(CUTS)],
        [arrived[cut] for cut in range(CUTS)],
        adapter_own,
        adapter_came,
        own_rows,
    )
    exchanged = between_same_cores(merged)
    down_map_gradient = outer(input_span, grad_spread, "down_maps")
    up_map_gradient = outer(input_spread, dgate, "up_maps")
    return (final(exchanged, 2 * span), down_map_gradient, up_map_gradient)


def solution(mesh):
    placed = (
        P(("groups", "tp"), None),
        P("groups", "tp"),
        P(None, "tp"),
        P(None, "tp"),
        P("tp", None),
        P(None, "tp"),
        P("groups"),
    )
    return jax.shard_map(
        local,
        mesh=mesh,
        in_specs=placed,
        out_specs=(P(("groups", "tp"), None), P("tp", "groups"), P("groups", "tp")),
        check_vma=False,
    )
```

time: 122 us -> 138 us (1.13)
  local copies, waits for them, and re-layouts: 7.73 us -> 35.9 us
  waiting for transfers between devices: 13.8 us -> 5.32 us
  Pallas kernels: 75 us -> 72.6 us
  starting transfers between devices: 23.6 us -> 21.3 us
    unnamed x12 -> x52, local copies, waits for them, and re-layouts: 4.09 us -> 35.3 us
    ppermute x4 -> x19, starting transfers between devices: 0.99 us -> 17.9 us  [swapped(): lax.ppermute(block, 'tp', [(i, i ^ hop) for i in range(lax.axis_size('tp'...]
    all_to_all x2 -> x1, waiting for transfers between devices: 12.3 us -> 2.32 us  [between_same_cores(): lax.all_to_all(blocks, 'tp', split_axis=0, concat_axis=0, tiled=True, axi...]
    all_to_all x2 -> x0, starting transfers between devices: 9.69 us -> none  [between_all(): return lax.all_to_all(blocks, 'tp', split_axis=0, concat_axis=0, tiled=True)]
    all_to_all x2 -> x1, starting transfers between devices: 12.9 us -> 3.42 us  [between_same_cores(): lax.all_to_all(blocks, 'tp', split_axis=0, concat_axis=0, tiled=True, axi...]
    pallas_call x7 -> x15, Pallas kernels: 68.4 us -> 64.1 us  [the longest x11 60.8 us: with_fetches(): pl.pallas_call(body, in_specs=[VMEM] * n_in + [HBM] * len(sources) + [ANY...]
    reshape x5 -> x0, local copies, waits for them, and re-layouts: 1.92 us -> none  [the longest x3 1.77 us: turned(): blocks = block.reshape((chips, 2, own_rows) + block.shape[1:])]
    pallas_call x1 -> x2, Pallas kernels: 5.87 us -> 7.78 us  [outer(): pl.pallas_call(outer_kernel, grid=(height // block,), in_specs=[pl.BlockS...]
  transfers between devices with their start and end apart: 8 -> 20, of which waited for: 5 -> 4; matrix products, arithmetic and copies ran while one was open for 2% -> 0% of each run, Pallas kernels for 53% -> 47%
where the time goes in v5:
time: 138 us
  Pallas kernels  72.6 us (53%)
  local copies, waits for them, and re-layouts  35.9 us (26%)
  starting transfers between devices  21.3 us (15%)
  waiting for transfers between devices  5.32 us (4%)
  other arithmetic  1.45 us (1%)
    pallas_call x11, Pallas kernels, with_fetches(): pl.pallas_call(body, in_specs=[VMEM] * n_in + [HBM] * len(sources) + [ANY...  60.8 us
    unnamed x52, local copies, waits for them, and re-layouts  35.3 us
    ppermute x19, starting transfers between devices, swapped(): lax.ppermute(block, 'tp', [(i, i ^ hop) for i in range(lax.axis_size('tp'...  17.9 us
    pallas_call x2, Pallas kernels, outer(): pl.pallas_call(outer_kernel, grid=(height // block,), in_specs=[pl.BlockS...  7.78 us
    all_to_all x1, starting transfers between devices, between_same_cores(): lax.all_to_all(blocks, 'tp', split_axis=0, concat_axis=0, tiled=True, axi...  3.42 us
    ppermute x19, waiting for transfers between devices, swapped(): lax.ppermute(block, 'tp', [(i, i ^ hop) for i in range(lax.axis_size('tp'...  3 us
  transfers between devices with their start and end apart: 20, of which 4 were waited for; matrix products, arithmetic and copies ran while one was open for 0% of the time, Pallas kernels for 47%

profile of v5, /device:TPU:0, one launch (start us, length us, event | category | flops | bytes accessed | tf_op | source)
XLA Modules:
  0.0 137.6 jit_solution(15808465502121646991)
XLA Ops:
  0.6 0.7 xor_multiply_fusion
  1.3 0.1 iota_add_fusion
  1.4 0.1 add.72.refs_3_.source_row_ref.refs_6_
  1.5 0.1 add.71
  1.6 0.7 and_select_fusion.refs_4_.chip_ref
  2.2 5.0 %collective-permute-start.2 = (bf16[2,8192]{1,0:T(2,128)(2,1)}, bf16[2,8192]{1,0:T(2,128)(2,1)S(1)}, u32[]{:S(2)}, u32[]{:S(2)}) collective-permute-start(bf16[2,8192]{1,0:T(2,128)(2,1)} %refs_0_.3), channel_id=1, source_target_pairs={{0,12},{1,13},{2,14},{3,15},{4,8},{5,9},{6,10},{7,11},{8,4},{9,5},... | collective-permute-start | bytes 98312 | tf_op jit(solution)/shard_map/ppermute | solution.py:439
  7.3 0.6 collective-permute-start
  7.9 0.1 copy.15.refs_2_.source_ref.refs_5_
  8.0 0.7 copy-done.20
  8.7 5.3 %fetch.2 = (bf16[2048,1792]{1,0:T(8,128)(2,1)S(1)}, bf16[2048,1792]{1,0:T(8,128)(2,1)S(1)}) custom-call(bf16[8192,1792]{1,0:T(8,128)(2,1)} %refs_5_.1, bf16[8192,1792]{1,0:T(8,128)(2,1)} %refs_4_.3, s32[32,1]{1,0:T(8,128)S(1)} %copy.15.refs_2_.source_ref.refs_5_, s32[1,32]{1,0:T(1,128)S(1)} %add.72.refs_3_.source_row_ref.refs_6_, ...), custom_call_target="tpu_custom_call" | custom-call | bytes 14680064 | tf_op jit(solution)/shard_map/fetch/pallas_call | solution.py:101
  14.0 0.1 stacked.1.refs_2_.refs_0_
  14.1 2.9 %copy-done = bf16[2048,1792]{1,0:T(8,128)(2,1)} copy-done((bf16[2048,1792]{1,0:T(8,128)(2,1)}, bf16[2048,1792]{1,0:T(8,128)(2,1)S(1)}, u32[]{:S(2)}) %copy-start) | copy-done | bytes 7340056
  17.0 2.3 %copy-done.3 = bf16[2048,1792]{1,0:T(8,128)(2,1)} copy-done((bf16[2048,1792]{1,0:T(8,128)(2,1)}, bf16[2048,1792]{1,0:T(8,128)(2,1)S(1)}, u32[]{:S(2)}) %copy-start.3) | copy-done | bytes 7340056
  19.3 1.7 %collective-permute-start.3 = (bf16[8,8192]{1,0:T(8,128)(2,1)S(1)}, bf16[8,8192]{1,0:T(8,128)(2,1)S(1)}, u32[]{:S(2)}, u32[]{:S(2)}) collective-permute-start(bf16[8,8192]{1,0:T(8,128)(2,1)S(1)} %stacked.1.refs_2_.refs_0_), channel_id=1, source_target_pairs={{0,2},{1,3},{2,0},{3,1},{4,6},{5,7},{6,4},{7,5},{8,10},{9,11},{10,... | collective-permute-start | bytes 393224 | tf_op jit(solution)/shard_map/ppermute | solution.py:439
  21.0 0.1 constant_dynamic-slice_fusion.3
  21.1 3.1 %copy-done.1 = bf16[2048,1792]{1,0:T(8,128)(2,1)S(1)} copy-done((bf16[2048,1792]{1,0:T(8,128)(2,1)S(1)}, bf16[2048,1792]{1,0:T(8,128)(2,1)}, u32[]{:S(2)}) %copy-start.1) | copy-done | bytes 7340056
  24.1 3.1 %copy-done.4 = bf16[2048,1792]{1,0:T(8,128)(2,1)S(1)} copy-done((bf16[2048,1792]{1,0:T(8,128)(2,1)S(1)}, bf16[2048,1792]{1,0:T(8,128)(2,1)}, u32[]{:S(2)}) %copy-start.4) | copy-done | bytes 7340056
  27.2 5.5 %fetch.3 = (bf16[2048,1792]{1,0:T(8,128)(2,1)S(1)}, bf16[2048,1792]{1,0:T(8,128)(2,1)S(1)}) custom-call(bf16[8192,1792]{1,0:T(8,128)(2,1)} %refs_5_.1, bf16[8192,1792]{1,0:T(8,128)(2,1)} %refs_4_.3, bf16[8,8192]{1,0:T(8,128)(2,1)S(1)} %stacked.1.refs_2_.refs_0_, bf16[2048,1792]{1,0:T(8,128)(2,1)S(1)} %copy-done.1, bf16[2048,1792]{1,0:T(8,128)(2,1)S(1)} %copy-done.4), custom_call_target="tpu_custom_call" | custom-call | bytes 14680064 | tf_op jit(solution)/shard_map/fetch/pallas_call | solution.py:101
  32.7 3.7 %copy-done.10 = bf16[2048,1792]{1,0:T(8,128)(2,1)} copy-done((bf16[2048,1792]{1,0:T(8,128)(2,1)}, bf16[2048,1792]{1,0:T(8,128)(2,1)S(1)}, u32[]{:S(2)}) %copy-start.10) | copy-done | bytes 7340056
  36.4 3.7 %copy-done.11 = bf16[2048,1792]{1,0:T(8,128)(2,1)} copy-done((bf16[2048,1792]{1,0:T(8,128)(2,1)}, bf16[2048,1792]{1,0:T(8,128)(2,1)S(1)}, u32[]{:S(2)}) %copy-start.11) | copy-done | bytes 7340056
  40.2 0.5 collective-permute-start.5
  40.7 0.1 constant_dynamic-slice_fusion.2
  40.8 0.1 constant_dynamic-slice_fusion.1
  40.8 0.8 collective-permute-done.5.refs_3_
  41.7 0.1 constant_dynamic-slice_fusion
  41.8 0.7 low_part.1.refs_8_
  42.5 0.4 collective-permute-start.6
  42.9 6.4 %forward.4 = (f32[32,1792]{1,0:T(8,128)S(1)}, f32[32,1792]{1,0:T(8,128)S(1)}, bf16[2048,1792]{1,0:T(8,128)(2,1)S(1)}, bf16[2048,1792]{1,0:T(8,128)(2,1)S(1)}) custom-call(bf16[8,8192]{1,0:T(8,128)(2,1)S(1)} %stacked.1.refs_2_.refs_0_, bf16[8,8192]{1,0:T(8,128)(2,1)S(1)} %collective-permute-done.3.refs_1_, ...), custom_call_target="tpu_custom_call" | custom-call | flops 469762048 | bytes 14680064 | tf_op jit(solution)/shard_map/forward/pallas_call | solution.py:101
  49.3 3.5 %copy-done.6 = bf16[2048,1792]{1,0:T(8,128)(2,1)} copy-done((bf16[2048,1792]{1,0:T(8,128)(2,1)}, bf16[2048,1792]{1,0:T(8,128)(2,1)S(1)}, u32[]{:S(2)}) %copy-start.6) | copy-done | bytes 7340056
  52.8 0.4 collective-permute-start.7
  53.3 0.3 slice-done.3
  53.5 7.4 %forward.5 = (f32[32,1792]{1,0:T(8,128)S(1)}, f32[32,1792]{1,0:T(8,128)S(1)}, bf16[2048,1792]{1,0:T(8,128)(2,1)S(1)}, bf16[2048,1792]{1,0:T(8,128)(2,1)S(1)}) custom-call(bf16[8,8192]{1,0:T(8,128)(2,1)S(1)} %stacked.1.refs_2_.refs_0_, bf16[8,8192]{1,0:T(8,128)(2,1)S(1)} %collective-permute-done.3.refs_1_, ...), custom_call_target="tpu_custom_call" | custom-call | flops 469762048 | bytes 14680064 | tf_op jit(solution)/shard_map/forward/pallas_call | solution.py:101
  60.9 1.3 collective-permute-start.8
  62.2 3.8 %forward.6 = (f32[32,1792]{1,0:T(8,128)S(1)}, f32[32,1792]{1,0:T(8,128)S(1)}, bf16[2048,1792]{1,0:T(8,128)(2,1)S(1)}) custom-call(bf16[8,8192]{1,0:T(8,128)(2,1)S(1)} %stacked.1.refs_2_.refs_0_, bf16[8,8192]{1,0:T(8,128)(2,1)S(1)} %collective-permute-done.3.refs_1_, bf16[8,8192]{1,0:T(8,128)(2,1)S(1)} %collective-permute-done.4.refs_2_, ...), custom_call_target="tpu_custom_call" | custom-call | flops 469762048 | bytes 7340032 | tf_op jit(solution)/shard_map/forward/pallas_call | solution.py:101
  66.1 3.0 %collective-permute-start.9 = (f32[32,64]{1,0:T(8,128)S(1)}, f32[32,64]{1,0:T(8,128)S(1)}, u32[]{:S(2)}, u32[]{:S(2)}) collective-permute-start(f32[32,64]{1,0:T(8,128)S(1)} %add.77.refs_8_), channel_id=1, source_target_pairs={{0,8},{1,9},{2,10},{3,11},{4,12},{5,13},{6,14},{7,15},{8,0},{9,1},... | collective-permute-start | bytes 24584 | tf_op jit(solution)/shard_map/ppermute | solution.py:439
  69.1 2.6 %forward.7 = (f32[32,1792]{1,0:T(8,128)S(1)}, f32[32,1792]{1,0:T(8,128)S(1)}) custom-call(bf16[8,8192]{1,0:T(8,128)(2,1)S(1)} %stacked.1.refs_2_.refs_0_, bf16[8,8192]{1,0:T(8,128)(2,1)S(1)} %collective-permute-done.3.refs_1_, bf16[8,8192]{1,0:T(8,128)(2,1)S(1)} %collective-permute-done.4.refs_2_, bf16[8,8192]{1,0:T(8,128)(2,1)S(1)} %collective-permute-done.5.refs_3_, ...), custom_call_target="tpu_custom_call" | custom-call | flops 469762048 | tf_op jit(solution)/shard_map/forward/pallas_call | solution.py:101
  71.7 0.0 copy-done.12
  71.7 3.1 %copy-done.13 = bf16[2048,1792]{1,0:T(8,128)(2,1)S(1)} copy-done((bf16[2048,1792]{1,0:T(8,128)(2,1)S(1)}, bf16[2048,1792]{1,0:T(8,128)(2,1)}, u32[]{:S(2)}) %copy-start.13) | copy-done | bytes 7340056
  74.8 5.2 %activation.1 = (bf16[32,1792]{1,0:T(8,128)(2,1)S(1)}, bf16[32,1792]{1,0:T(8,128)(2,1)S(1)}, f32[32,64]{1,0:T(8,128)S(1)}, bf16[32,2048]{1,0:T(8,128)(2,1)S(1)}, bf16[2048,1792]{1,0:T(8,128)(2,1)S(1)}) custom-call(f32[32,1792]{1,0:T(8,128)S(1)} %get-tuple-element.67.refs_0_, f32[32,1792]{1,0:T(8,128)S(1)} %get-tuple-element.68.refs_1_, ...), custom_call_target="tpu_custom_call" | custom-call | flops 469762048 | bytes 7340032 | tf_op jit(solution)/shard_map/activation/pallas_call | solution.py:101
  80.1 3.0 %copy-done.14 = bf16[2048,1792]{1,0:T(8,128)(2,1)} copy-done((bf16[2048,1792]{1,0:T(8,128)(2,1)}, bf16[2048,1792]{1,0:T(8,128)(2,1)S(1)}, u32[]{:S(2)}) %copy-start.14) | copy-done | bytes 7340056
  83.1 0.2 collective-permute-start.10
  83.2 1.0 collective-permute-done.10
  84.3 1.4 %collective-permute-start.11 = (f32[32,64]{1,0:T(8,128)S(1)}, f32[32,64]{1,0:T(8,128)S(1)}, u32[]{:S(2)}, u32[]{:S(2)}) collective-permute-start(f32[32,64]{1,0:T(8,128)S(1)} %add.79.refs_6_), channel_id=1, source_target_pairs={{0,2},{1,3},{2,0},{3,1},{4,6},{5,7},{6,4},{7,5},{8,10},{9,11},{10,... | collective-permute-start | bytes 24584 | tf_op jit(solution)/shard_map/ppermute | solution.py:439
  85.7 9.1 %backward.4 = (f32[16,2048]{1,0:T(8,128)S(1)}, bf16[16,2048]{1,0:T(8,128)(2,1)S(1)}, bf16[2048,1792]{1,0:T(8,128)(2,1)S(1)}, bf16[2048,1792]{1,0:T(8,128)(2,1)S(1)}) custom-call(bf16[32,1792]{1,0:T(8,128)(2,1)S(1)} %get-tuple-element.70.refs_0_.right_ref, bf16[32,1792]{1,0:T(8,128)(2,1)S(1)} %get-tuple-element.71.refs_1_, ...), custom_call_target="tpu_custom_call" | custom-call | flops 469762048 | bytes 14680064 | tf_op jit(solution)/shard_map/backward/pallas_call | solution.py:101
  94.8 2.9 %copy-done.16 = bf16[2048,1792]{1,0:T(8,128)(2,1)} copy-done((bf16[2048,1792]{1,0:T(8,128)(2,1)}, bf16[2048,1792]{1,0:T(8,128)(2,1)S(1)}, u32[]{:S(2)}) %copy-start.16) | copy-done | bytes 7340056
  97.7 0.1 collective-permute-start.12
  97.8 3.1 %copy-done.8 = bf16[2048,1792]{1,0:T(8,128)(2,1)S(1)} copy-done((bf16[2048,1792]{1,0:T(8,128)(2,1)S(1)}, bf16[2048,1792]{1,0:T(8,128)(2,1)}, u32[]{:S(2)}) %copy-start.8) | copy-done | bytes 7340056
  100.9 6.8 %backward.5 = (f32[16,2048]{1,0:T(8,128)S(1)}, bf16[16,2048]{1,0:T(8,128)(2,1)S(1)}, bf16[2048,1792]{1,0:T(8,128)(2,1)S(1)}) custom-call(bf16[32,1792]{1,0:T(8,128)(2,1)S(1)} %get-tuple-element.70.refs_0_.right_ref, bf16[32,1792]{1,0:T(8,128)(2,1)S(1)} %get-tuple-element.71.refs_1_, bf16[2048,1792]{1,0:T(8,128)(2,1)S(1)} %get-tuple-element.61.refs_4_.refs_2_, ...), custom_call_target="tpu_custom_call" | custom-call | flops 469762048 | bytes 7340032 | tf_op jit(solution)/shard_map/backward/pallas_call | solution.py:101
  107.7 0.6 collective-permute-start.16
  108.3 2.1 %collective-permute-start.13 = (f32[32,64]{1,0:T(8,128)S(1)}, f32[32,64]{1,0:T(8,128)S(1)}, u32[]{:S(2)}, u32[]{:S(2)}) collective-permute-start(f32[32,64]{1,0:T(8,128)S(1)} %add.81.refs_4_), channel_id=1, source_target_pairs={{0,8},{1,9},{2,10},{3,11},{4,12},{5,13},{6,14},{7,15},{8,0},{9,1},... | collective-permute-start | bytes 24584 | tf_op jit(solution)/shard_map/ppermute | solution.py:439
  110.3 4.3 %backward.7 = (f32[16,2048]{1,0:T(8,128)S(1)}, bf16[16,2048]{1,0:T(8,128)(2,1)S(1)}) custom-call(bf16[32,1792]{1,0:T(8,128)(2,1)S(1)} %get-tuple-element.70.refs_0_.right_ref, bf16[32,1792]{1,0:T(8,128)(2,1)S(1)} %get-tuple-element.71.refs_1_, bf16[2048,1792]{1,0:T(8,128)(2,1)S(1)} %copy-done.15, bf16[2048,1792]{1,0:T(8,128)(2,1)S(1)} %get-tuple-element.78.refs_3_, ...), custom_call_target="tpu_custom_call" | custom-call | flops 469762048 | tf_op jit(solution)/shard_map/backward/pallas_call | solution.py:101
  114.7 0.0 collective-permute-start.15
  114.7 0.9 adapter_part.1
  115.6 0.0 copy-done.17
  115.7 4.3 %backward.6 = (f32[16,2048]{1,0:T(8,128)S(1)}, bf16[16,2048]{1,0:T(8,128)(2,1)S(1)}) custom-call(bf16[32,1792]{1,0:T(8,128)(2,1)S(1)} %get-tuple-element.70.refs_0_.right_ref, bf16[32,1792]{1,0:T(8,128)(2,1)S(1)} %get-tuple-element.71.refs_1_, bf16[2048,1792]{1,0:T(8,128)(2,1)S(1)} %copy-done.17, bf16[2048,1792]{1,0:T(8,128)(2,1)S(1)} %get-tuple-element.74.refs_3_, ...), custom_call_target="tpu_custom_call" | custom-call | flops 469762048 | tf_op jit(solution)/shard_map/backward/pallas_call | solution.py:101
  120.0 0.5 collective-permute-start.14
  120.5 0.1 collective-permute-start.18
  120.6 1.1 collective-permute-done.18.refs_9_
  121.7 1.6 %merge.1 = bf16[8,16,1152]{2,1,0:T(8,128)(2,1)} custom-call(s32[8]{0:T(128)S(1)} %and_select_fusion.refs_4_.chip_ref, s32[1]{0:T(128)} %bitcast.refs_5_.core_ref, f32[16,2048]{1,0:T(8,128)S(1)} %get-tuple-element.76.refs_0_, f32[16,2048]{1,0:T(8,128)S(1)} %get-tuple-element.79.refs_1_, f32[16,2048]{1,0:T(8,128)S(1)} %get-tuple-element.80.refs_2_, ...), custom_call_target="tpu_custom_call" | custom-call | tf_op jit(solution)/shard_map/merge/pallas_call | solution.py:342
  123.4 3.4 %all-to-all-start = ((bf16[8,16,1152]{2,1,0:T(8,128)(2,1)}), bf16[8,16,1152]{2,1,0:T(8,128)(2,1)S(1)}, u32[]{:S(2)}, u32[]{:S(2)}) async-start(bf16[8,16,1152]{2,1,0:T(8,128)(2,1)} %merge.1), calls=%async_computation | async-start | bytes 589824 | tf_op jit(solution)/shard_map/all_to_all | solution.py:433
  126.8 5.9 %up_maps.1 = bf16[2048,1792]{1,0:T(8,128)(2,1)} custom-call(bf16[32,2048]{1,0:T(8,128)(2,1)S(1)} %get-tuple-element.88.left_ref, bf16[32,1792]{1,0:T(8,128)(2,1)S(1)} %get-tuple-element.70.refs_0_.right_ref), custom_call_target="tpu_custom_call" | custom-call | flops 234881024 | bytes 7340032 | tf_op jit(solution)/shard_map/up_maps/pallas_call | solution.py:410
  132.7 1.9 %down_maps.1 = bf16[512,2048]{1,0:T(8,128)(2,1)} custom-call(bf16[32,512]{1,0:T(8,128)(2,1)S(1)} %pad_maximum_fusion.span_ref.left_ref, bf16[32,2048]{1,0:T(8,128)(2,1)S(1)} %get-tuple-element.87.right_ref), custom_call_target="tpu_custom_call" | custom-call | flops 67108864 | bytes 2097152 | tf_op jit(solution)/shard_map/down_maps/pallas_call | solution.py:410
  134.6 2.3 %all-to-all-done.refs_0_ = bf16[8,16,1152]{2,1,0:T(8,128)(2,1)S(1)} async-done(((bf16[8,16,1152]{2,1,0:T(8,128)(2,1)}), bf16[8,16,1152]{2,1,0:T(8,128)(2,1)S(1)}, u32[]{:S(2)}, u32[]{:S(2)}) %all-to-all-start) | async-done | bytes 294944 | tf_op jit(solution)/shard_map/all_to_all | solution.py:433
  136.9 0.7 final.1
  (67 shorter events, 0.2 us)
Async XLA Ops:
  2.2 11.8 %collective-permute-start.2 = (bf16[2,8192]{1,0:T(2,128)(2,1)}, bf16[2,8192]{1,0:T(2,128)(2,1)S(1)}, u32[]{:S(2)}, u32[]{:S(2)}) collective-permute-start(bf16[2,8192]{1,0:T(2,128)(2,1)} %refs_0_.3), channel_id=1, source_target_pairs={{0,12},{1,13},{2,14},{3,15},{4,8},{5,9},{6,10},{7,11},{8,4},{9,5},... | collective-permute-start | bytes 98312 | tf_op jit(solution)/shard_map/ppermute | solution.py:439
  7.3 6.7 %collective-permute-start.1 = (bf16[2,8192]{1,0:T(2,128)(2,1)}, bf16[2,8192]{1,0:T(2,128)(2,1)S(1)}, u32[]{:S(2)}, u32[]{:S(2)}) collective-permute-start(bf16[2,8192]{1,0:T(2,128)(2,1)} %refs_0_.3), channel_id=1, source_target_pairs={{0,8},{1,9},{2,10},{3,11},{4,12},{5,13},{6,14},{7,15},{8,0},{9,1},... | collective-permute-start | bytes 98312 | tf_op jit(solution)/shard_map/ppermute | solution.py:439
  7.3 6.7 %collective-permute-start = (bf16[2,8192]{1,0:T(2,128)(2,1)}, bf16[2,8192]{1,0:T(2,128)(2,1)S(1)}, u32[]{:S(2)}, u32[]{:S(2)}) collective-permute-start(bf16[2,8192]{1,0:T(2,128)(2,1)} %refs_0_.3), channel_id=1, source_target_pairs={{0,4},{1,5},{2,6},{3,7},{4,0},{5,1},{6,2},{7,3},{8,12},{9,13},{10,... | collective-permute-start | bytes 98312 | tf_op jit(solution)/shard_map/ppermute | solution.py:439
  8.0 0.7 copy-start.20
  8.7 5.4 %copy-start.19 = (bf16[2,8192]{1,0:T(2,128)(2,1)S(1)}, bf16[2,8192]{1,0:T(2,128)(2,1)}, u32[]{:S(2)}) copy-start(bf16[2,8192]{1,0:T(2,128)(2,1)} %refs_0_.3) | copy-start | bytes 98308
  14.0 3.1 %copy-start = (bf16[2048,1792]{1,0:T(8,128)(2,1)}, bf16[2048,1792]{1,0:T(8,128)(2,1)S(1)}, u32[]{:S(2)}) copy-start(bf16[2048,1792]{1,0:T(8,128)(2,1)S(1)} %get-tuple-element.52.refs_4_.refs_3_) | copy-start | bytes 22020100
  14.0 5.3 %copy-start.3 = (bf16[2048,1792]{1,0:T(8,128)(2,1)}, bf16[2048,1792]{1,0:T(8,128)(2,1)S(1)}, u32[]{:S(2)}) copy-start(bf16[2048,1792]{1,0:T(8,128)(2,1)S(1)} %get-tuple-element.53.refs_5_.refs_4_) | copy-start | bytes 22020100
  19.3 20.8 %collective-permute-start.3 = (bf16[8,8192]{1,0:T(8,128)(2,1)S(1)}, bf16[8,8192]{1,0:T(8,128)(2,1)S(1)}, u32[]{:S(2)}, u32[]{:S(2)}) collective-permute-start(bf16[8,8192]{1,0:T(8,128)(2,1)S(1)} %stacked.1.refs_2_.refs_0_), channel_id=1, source_target_pairs={{0,2},{1,3},{2,0},{3,1},{4,6},{5,7},{6,4},{7,5},{8,10},{9,11},{10,... | collective-permute-start | bytes 393224 | tf_op jit(solution)/shard_map/ppermute | solution.py:439
  21.0 19.8 %collective-permute-start.4 = (bf16[8,8192]{1,0:T(8,128)(2,1)S(1)}, bf16[8,8192]{1,0:T(8,128)(2,1)S(1)}, u32[]{:S(2)}, u32[]{:S(2)}) collective-permute-start(bf16[8,8192]{1,0:T(8,128)(2,1)S(1)} %stacked.1.refs_2_.refs_0_), channel_id=1, source_target_pairs={{0,1},{1,0},{2,3},{3,2},{4,5},{5,4},{6,7},{7,6},{8,9},{9,8},{10,11... | collective-permute-start | bytes 393224 | tf_op jit(solution)/shard_map/ppermute | solution.py:439
  21.1 3.1 %copy-start.1 = (bf16[2048,1792]{1,0:T(8,128)(2,1)S(1)}, bf16[2048,1792]{1,0:T(8,128)(2,1)}, u32[]{:S(2)}) copy-start(bf16[2048,1792]{1,0:T(8,128)(2,1)} %copy-done) | copy-start | bytes 22020100
  24.1 3.1 %copy-start.4 = (bf16[2048,1792]{1,0:T(8,128)(2,1)S(1)}, bf16[2048,1792]{1,0:T(8,128)(2,1)}, u32[]{:S(2)}) copy-start(bf16[2048,1792]{1,0:T(8,128)(2,1)} %copy-done.3) | copy-start | bytes 22020100
  27.2 14.5 %copy-start.9 = (bf16[512,2048]{1,0:T(8,128)(2,1)S(1)}, bf16[512,2048]{1,0:T(8,128)(2,1)}, u32[]{:S(2)}) copy-start(bf16[512,2048]{1,0:T(8,128)(2,1)} %down_ref.3) | copy-start | bytes 6291460
  27.2 14.5 %copy-start.21 = (s32[32]{0:T(128)S(1)}, s32[32]{0:T(128)}, u32[]{:S(2)}) copy-start(s32[32]{0:T(128)} %param.14) | copy-start | bytes 388
  27.2 15.6 %copy-start.2 = (bf16[2048,1792]{1,0:T(8,128)(2,1)S(1)}, bf16[2048,1792]{1,0:T(8,128)(2,1)}, u32[]{:S(2)}) copy-start(bf16[2048,1792]{1,0:T(8,128)(2,1)} %copy-done) | copy-start | bytes 22020100
  27.2 15.6 %copy-start.5 = (bf16[2048,1792]{1,0:T(8,128)(2,1)S(1)}, bf16[2048,1792]{1,0:T(8,128)(2,1)}, u32[]{:S(2)}) copy-start(bf16[2048,1792]{1,0:T(8,128)(2,1)} %copy-done.3) | copy-start | bytes 22020100
  32.7 3.7 %copy-start.10 = (bf16[2048,1792]{1,0:T(8,128)(2,1)}, bf16[2048,1792]{1,0:T(8,128)(2,1)S(1)}, u32[]{:S(2)}) copy-start(bf16[2048,1792]{1,0:T(8,128)(2,1)S(1)} %get-tuple-element.54.refs_4_) | copy-start | bytes 22020100
  36.4 3.7 %copy-start.11 = (bf16[2048,1792]{1,0:T(8,128)(2,1)}, bf16[2048,1792]{1,0:T(8,128)(2,1)S(1)}, u32[]{:S(2)}) copy-start(bf16[2048,1792]{1,0:T(8,128)(2,1)S(1)} %get-tuple-element.55.refs_5_) | copy-start | bytes 22020100
  40.2 1.5 %collective-permute-start.5 = (bf16[8,8192]{1,0:T(8,128)(2,1)S(1)}, bf16[8,8192]{1,0:T(8,128)(2,1)S(1)}, u32[]{:S(2)}, u32[]{:S(2)}) collective-permute-start(bf16[8,8192]{1,0:T(8,128)(2,1)S(1)} %collective-permute-done.3.refs_1_), channel_id=1, source_target_pairs={{0,1},{1,0},{2,3},{3,2},{4,5},{5,4},{6,7},{7,6},{8,9},{9,8},{10,11... | collective-permute-start | bytes 393224 | tf_op jit(solution)/shard_map/ppermute | solution.py:439
  41.8 11.5 %slice-start = ((s8[7340032]{0:T(1024)(128)(4,1)}), s8[4194304]{0:T(1024)(128)(4,1)S(1)}, s32[]{:S(2)}) async-start(s8[7340032]{0:T(1024)(128)(4,1)} %bitcast.2), calls=%async_computation.1 | async-start | bytes 8388608
  41.8 11.5 %slice-start.2 = ((s8[7340032]{0:T(1024)(128)(4,1)}), s8[4194304]{0:T(1024)(128)(4,1)S(1)}, s32[]{:S(2)}) async-start(s8[7340032]{0:T(1024)(128)(4,1)} %bitcast.4), calls=%async_computation.3 | async-start | bytes 8388608
  42.4 10.8 %slice-start.1 = ((s8[7340032]{0:T(1024)(128)(4,1)}), s8[3145728]{0:T(1024)(128)(4,1)S(1)}, s32[]{:S(2)}) async-start(s8[7340032]{0:T(1024)(128)(4,1)} %bitcast.2), calls=%async_computation.2 | async-start | bytes 6291456
  42.4 11.1 %slice-start.3 = ((s8[7340032]{0:T(1024)(128)(4,1)}), s8[3145728]{0:T(1024)(128)(4,1)S(1)}, s32[]{:S(2)}) async-start(s8[7340032]{0:T(1024)(128)(4,1)} %bitcast.4), calls=%async_computation.4 | async-start | bytes 6291456
  42.5 10.3 %collective-permute-start.6 = (f32[32,64]{1,0:T(8,128)S(1)}, f32[32,64]{1,0:T(8,128)S(1)}, u32[]{:S(2)}, u32[]{:S(2)}) collective-permute-start(f32[32,64]{1,0:T(8,128)S(1)} %low_part.1.refs_8_), channel_id=1, source_target_pairs={{0,1},{1,0},{2,3},{3,2},{4,5},{5,4},{6,7},{7,6},{8,9},{9,8},{10,11... | collective-permute-start | bytes 24584 | tf_op jit(solution)/shard_map/ppermute | solution.py:439
  49.3 3.5 %copy-start.6 = (bf16[2048,1792]{1,0:T(8,128)(2,1)}, bf16[2048,1792]{1,0:T(8,128)(2,1)S(1)}, u32[]{:S(2)}) copy-start(bf16[2048,1792]{1,0:T(8,128)(2,1)S(1)} %get-tuple-element.62.refs_5_.refs_3_) | copy-start | bytes 22020100
  52.8 8.1 %collective-permute-start.7 = (f32[32,64]{1,0:T(8,128)S(1)}, f32[32,64]{1,0:T(8,128)S(1)}, u32[]{:S(2)}, u32[]{:S(2)}) collective-permute-start(f32[32,64]{1,0:T(8,128)S(1)} %add.75.refs_10_), channel_id=1, source_target_pairs={{0,2},{1,3},{2,0},{3,1},{4,6},{5,7},{6,4},{7,5},{8,10},{9,11},{10,... | collective-permute-start | bytes 24584 | tf_op jit(solution)/shard_map/ppermute | solution.py:439
  53.5 8.7 %copy-start.7 = (bf16[2048,1792]{1,0:T(8,128)(2,1)S(1)}, bf16[2048,1792]{1,0:T(8,128)(2,1)}, u32[]{:S(2)}) copy-start(bf16[2048,1792]{1,0:T(8,128)(2,1)} %copy-done.6) | copy-start | bytes 22020100
  60.9 5.1 %collective-permute-start.8 = (f32[32,64]{1,0:T(8,128)S(1)}, f32[32,64]{1,0:T(8,128)S(1)}, u32[]{:S(2)}, u32[]{:S(2)}) collective-permute-start(f32[32,64]{1,0:T(8,128)S(1)} %add.76.refs_9_), channel_id=1, source_target_pairs={{0,4},{1,5},{2,6},{3,7},{4,0},{5,1},{6,2},{7,3},{8,12},{9,13},{10,... | collective-permute-start | bytes 24584 | tf_op jit(solution)/shard_map/ppermute | solution.py:439
  66.1 5.6 %copy-start.12 = (bf16[2048,1792]{1,0:T(8,128)(2,1)}, bf16[2048,1792]{1,0:T(8,128)(2,1)S(1)}, u32[]{:S(2)}) copy-start(bf16[2048,1792]{1,0:T(8,128)(2,1)S(1)} %get-tuple-element.69.refs_7_) | copy-start | bytes 22020100
  66.1 5.6 %collective-permute-start.9 = (f32[32,64]{1,0:T(8,128)S(1)}, f32[32,64]{1,0:T(8,128)S(1)}, u32[]{:S(2)}, u32[]{:S(2)}) collective-permute-start(f32[32,64]{1,0:T(8,128)S(1)} %add.77.refs_8_), channel_id=1, source_target_pairs={{0,8},{1,9},{2,10},{3,11},{4,12},{5,13},{6,14},{7,15},{8,0},{9,1},... | collective-permute-start | bytes 24584 | tf_op jit(solution)/shard_map/ppermute | solution.py:439
  69.1 2.6 %copy-start.18 = (bf16[32,1792]{1,0:T(8,128)(2,1)S(1)}, bf16[32,1792]{1,0:T(8,128)(2,1)}, u32[]{:S(2)}) copy-start(bf16[32,1792]{1,0:T(8,128)(2,1)} %refs_2_.1) | copy-start | bytes 344068
  71.7 3.1 %copy-start.13 = (bf16[2048,1792]{1,0:T(8,128)(2,1)S(1)}, bf16[2048,1792]{1,0:T(8,128)(2,1)}, u32[]{:S(2)}) copy-start(bf16[2048,1792]{1,0:T(8,128)(2,1)} %copy-done.12) | copy-start | bytes 22020100
  80.1 3.0 %copy-start.14 = (bf16[2048,1792]{1,0:T(8,128)(2,1)}, bf16[2048,1792]{1,0:T(8,128)(2,1)S(1)}, u32[]{:S(2)}) copy-start(bf16[2048,1792]{1,0:T(8,128)(2,1)S(1)} %get-tuple-element.77.refs_2_) | copy-start | bytes 22020100
  83.1 1.2 collective-permute-start.10
  84.3 13.5 %collective-permute-start.11 = (f32[32,64]{1,0:T(8,128)S(1)}, f32[32,64]{1,0:T(8,128)S(1)}, u32[]{:S(2)}, u32[]{:S(2)}) collective-permute-start(f32[32,64]{1,0:T(8,128)S(1)} %add.79.refs_6_), channel_id=1, source_target_pairs={{0,2},{1,3},{2,0},{3,1},{4,6},{5,7},{6,4},{7,5},{8,10},{9,11},{10,... | collective-permute-start | bytes 24584 | tf_op jit(solution)/shard_map/ppermute | solution.py:439
  94.8 2.9 %copy-start.16 = (bf16[2048,1792]{1,0:T(8,128)(2,1)}, bf16[2048,1792]{1,0:T(8,128)(2,1)S(1)}, u32[]{:S(2)}) copy-start(bf16[2048,1792]{1,0:T(8,128)(2,1)S(1)} %get-tuple-element.73.refs_2_) | copy-start | bytes 22020100
  97.7 24.0 %collective-permute-start.17 = (bf16[16,2048]{1,0:T(8,128)(2,1)S(1)}, bf16[16,2048]{1,0:T(8,128)(2,1)S(1)}, u32[]{:S(2)}, u32[]{:S(2)}) collective-permute-start(bf16[16,2048]{1,0:T(8,128)(2,1)S(1)} %get-tuple-element.85), channel_id=1, source_target_pairs={{0,1},{1,0},{2,3},{3,2},{4,5},{5,4},{6,7},{7,6},{8,9},{9,8},{10,11... | collective-permute-start | bytes 196616 | tf_op jit(solution)/shard_map/ppermute | solution.py:439
  97.7 10.5 %collective-permute-start.12 = (f32[32,64]{1,0:T(8,128)S(1)}, f32[32,64]{1,0:T(8,128)S(1)}, u32[]{:S(2)}, u32[]{:S(2)}) collective-permute-start(f32[32,64]{1,0:T(8,128)S(1)} %add.80.refs_5_), channel_id=1, source_target_pairs={{0,4},{1,5},{2,6},{3,7},{4,0},{5,1},{6,2},{7,3},{8,12},{9,13},{10,... | collective-permute-start | bytes 24584 | tf_op jit(solution)/shard_map/ppermute | solution.py:439
  97.8 3.1 %copy-start.8 = (bf16[2048,1792]{1,0:T(8,128)(2,1)S(1)}, bf16[2048,1792]{1,0:T(8,128)(2,1)}, u32[]{:S(2)}) copy-start(bf16[2048,1792]{1,0:T(8,128)(2,1)} %copy-done.6) | copy-start | bytes 22020100
  100.9 9.4 %copy-start.15 = (bf16[2048,1792]{1,0:T(8,128)(2,1)S(1)}, bf16[2048,1792]{1,0:T(8,128)(2,1)}, u32[]{:S(2)}) copy-start(bf16[2048,1792]{1,0:T(8,128)(2,1)} %copy-done.14) | copy-start | bytes 22020100
  107.7 14.0 %collective-permute-start.16 = (bf16[16,2048]{1,0:T(8,128)(2,1)S(1)}, bf16[16,2048]{1,0:T(8,128)(2,1)S(1)}, u32[]{:S(2)}, u32[]{:S(2)}) collective-permute-start(bf16[16,2048]{1,0:T(8,128)(2,1)S(1)} %get-tuple-element.84), channel_id=1, source_target_pairs={{0,1},{1,0},{2,3},{3,2},{4,5},{5,4},{6,7},{7,6},{8,9},{9,8},{10,11... | collective-permute-start | bytes 196616 | tf_op jit(solution)/shard_map/ppermute | solution.py:439
  108.3 6.4 %collective-permute-start.13 = (f32[32,64]{1,0:T(8,128)S(1)}, f32[32,64]{1,0:T(8,128)S(1)}, u32[]{:S(2)}, u32[]{:S(2)}) collective-permute-start(f32[32,64]{1,0:T(8,128)S(1)} %add.81.refs_4_), channel_id=1, source_target_pairs={{0,8},{1,9},{2,10},{3,11},{4,12},{5,13},{6,14},{7,15},{8,0},{9,1},... | collective-permute-start | bytes 24584 | tf_op jit(solution)/shard_map/ppermute | solution.py:439
  110.3 5.3 %copy-start.17 = (bf16[2048,1792]{1,0:T(8,128)(2,1)S(1)}, bf16[2048,1792]{1,0:T(8,128)(2,1)}, u32[]{:S(2)}) copy-start(bf16[2048,1792]{1,0:T(8,128)(2,1)} %copy-done.16) | copy-start | bytes 22020100
  114.7 7.0 %collective-permute-start.15 = (bf16[16,2048]{1,0:T(8,128)(2,1)S(1)}, bf16[16,2048]{1,0:T(8,128)(2,1)S(1)}, u32[]{:S(2)}, u32[]{:S(2)}) collective-permute-start(bf16[16,2048]{1,0:T(8,128)(2,1)S(1)} %get-tuple-element.83), channel_id=1, source_target_pairs={{0,1},{1,0},{2,3},{3,2},{4,5},{5,4},{6,7},{7,6},{8,9},{9,8},{10,11... | collective-permute-start | bytes 196616 | tf_op jit(solution)/shard_map/ppermute | solution.py:439
  120.0 1.7 %collective-permute-start.14 = (bf16[16,2048]{1,0:T(8,128)(2,1)S(1)}, bf16[16,2048]{1,0:T(8,128)(2,1)S(1)}, u32[]{:S(2)}, u32[]{:S(2)}) collective-permute-start(bf16[16,2048]{1,0:T(8,128)(2,1)S(1)} %get-tuple-element.82), channel_id=1, source_target_pairs={{0,1},{1,0},{2,3},{3,2},{4,5},{5,4},{6,7},{7,6},{8,9},{9,8},{10,11... | collective-permute-start | bytes 196616 | tf_op jit(solution)/shard_map/ppermute | solution.py:439
  120.5 1.2 collective-permute-start.18
  123.4 13.5 %all-to-all-start = ((bf16[8,16,1152]{2,1,0:T(8,128)(2,1)}), bf16[8,16,1152]{2,1,0:T(8,128)(2,1)S(1)}, u32[]{:S(2)}, u32[]{:S(2)}) async-start(bf16[8,16,1152]{2,1,0:T(8,128)(2,1)} %merge.1), calls=%async_computation | async-start | bytes 589824 | tf_op jit(solution)/shard_map/all_to_all | solution.py:433

commit v6 on v5

v6 whole, which is shorter than its diff:
```python
import jax
import jax.numpy as jnp
from jax import lax
from jax.experimental import pallas as pl
from jax.experimental.pallas import tpu as pltpu
from jax.sharding import PartitionSpec as P

ADAPTER_RANK = 64
TENANT_COUNT = 32
SPREAD = ADAPTER_RANK * TENANT_COUNT

adapter_scale = 2.0


def block_of(size, largest):
    block = largest
    while size % block:
        block //= 2
    return block


def contracted_rows(left, right):
    return lax.dot_general(
        left, right, (((0,), (0,)), ((), ())), preferred_element_type=jnp.float32
    )


def contracted_columns(left, right):
    return lax.dot_general(
        left, right, (((1,), (1,)), ((), ())), preferred_element_type=jnp.float32
    )


def tenant_mask(tenants, rows):
    columns = lax.broadcasted_iota(jnp.int32, (rows, SPREAD), 1) // ADAPTER_RANK
    return tenants == columns


def select_block(wide_rows, mask):
    kept = jnp.where(mask, wide_rows, 0.0)
    pair = 2 * ADAPTER_RANK
    total = kept[:, :pair]
    for start in range(pair, SPREAD, pair):
        total = total + kept[:, start : start + pair]
    return total[:, :ADAPTER_RANK] + total[:, ADAPTER_RANK:]


def spread_rows(low_rows, mask):
    pair = jnp.concatenate([low_rows, low_rows], axis=1)
    wide = jnp.concatenate([pair] * (TENANT_COUNT // 2), axis=1)
    return jnp.where(mask, wide, 0.0).astype(jnp.bfloat16)


VMEM = pl.BlockSpec(memory_space=pltpu.VMEM)
SMEM = pl.BlockSpec(memory_space=pltpu.SMEM)
ANY = pl.BlockSpec(memory_space=pl.ANY)
CUTS = 4
COPIES = 4
SLOTS = 6


def store_call(kernel, store, fetches, operands, out_shapes, flops, name, smem=0, after=()):
    new = isinstance(store, jax.ShapeDtypeStruct)
    depth = store.shape[0] // SLOTS
    part = depth // COPIES
    sources = []
    for array, _, _ in fetches:
        if not any(array is known for known in sources):
            sources.append(array)
    places = [next(i for i, known in enumerate(sources) if known is f[0]) for f in fetches]
    n_in, n_out, n_hbm = len(operands), len(out_shapes), len(sources)

    def body(*refs):
        if not new:
            refs = refs[1:]
        ins, hbm = refs[:n_in], refs[n_in : n_in + n_hbm]
        rest = refs[n_in + n_hbm + len(after) :]
        store_ref, outs, scratch = rest[0], rest[1 : 1 + n_out], rest[1 + n_out :]
        copies = []
        for n, (place, (_, piece, slot)) in enumerate(zip(places, fetches)):
            for k in range(COPIES):
                copies.append(
                    pltpu.make_async_copy(
                        hbm[place].at[pl.ds(piece * depth + k * part, part)],
                        store_ref.at[pl.ds(slot * depth + k * part, part)],
                        scratch[0].at[n * COPIES + k],
                    )
                )
        for copy in copies:
            copy.start()
        kernel(lambda slot: store_ref[slot * depth : (slot + 1) * depth, :], *ins, *outs)
        for copy in copies:
            copy.wait()

    moved = 2 * depth * store.shape[1] * len(fetches)
    return pl.pallas_call(
        body,
        in_specs=([] if new else [VMEM])
        + [SMEM] * smem
        + [VMEM] * (n_in - smem)
        + [ANY] * (n_hbm + len(after)),
        out_specs=[VMEM] * (1 + n_out),
        out_shape=[pltpu.VMEM(store.shape, store.dtype), *out_shapes],
        input_output_aliases={} if new else {0: 0},
        scratch_shapes=[pltpu.SemaphoreType.DMA((COPIES * len(fetches),))] if fetches else [],
        compiler_params=pltpu.CompilerParams(vmem_limit_bytes=13 << 20),
        cost_estimate=pl.CostEstimate(flops=flops, bytes_accessed=moved, transcendentals=0),
        name=name,
    )(
        *([] if new else [store]),
        *operands,
        *[pltpu.with_memory_space_constraint(array, pltpu.HBM) for array in sources],
        *after,
    )


def stacked(blocks, after=()):
    rows = sum(block.shape[0] for block in blocks)

    def stack_kernel(*refs):
        refs[-1][...] = jnp.concatenate([ref[...] for ref in refs[: len(blocks)]], axis=0)

    return pl.pallas_call(
        stack_kernel,
        in_specs=[VMEM] * len(blocks) + [ANY] * len(after),
        out_shape=jax.ShapeDtypeStruct((rows, blocks[0].shape[1]), blocks[0].dtype),
        compiler_params=pltpu.CompilerParams(vmem_limit_bytes=6 << 20),
        name="stacked",
    )(*blocks, *after)


def block_owner(own, block, count):
    bits = count.bit_length() - 1
    hops = [1 << (bits - 2), 1 << (bits - 1)] + [1 << bit for bit in reversed(range(bits - 2))]
    for n, hop in enumerate(hops):
        own = own ^ (((block >> n) & 1) * hop)
    return own


def source_of(own, row, rows, count):
    tokens = rows // count
    return block_owner(own, row // tokens, count) * tokens + row % tokens


def pick_held(own, rows, count):
    held = source_of(own, lax.broadcasted_iota(jnp.int32, (rows, rows), 0), rows, count)
    return held == lax.broadcasted_iota(jnp.int32, (rows, rows), 1)


def pick_given(own, rows, count):
    held = source_of(own, lax.broadcasted_iota(jnp.int32, (rows, rows), 1), rows, count)
    return held == lax.broadcasted_iota(jnp.int32, (rows, rows), 0)


def picked(pick, block):
    if block.dtype == jnp.bfloat16:
        return jnp.dot(pick.astype(jnp.bfloat16), block, preferred_element_type=jnp.float32)
    return jnp.dot(pick.astype(jnp.float32), block, precision=lax.Precision.HIGHEST)


def held_mask(pick, tenants_row):
    tenants = jnp.sum(jnp.where(pick, tenants_row, 0).astype(jnp.float32), axis=1, keepdims=True)
    return tenant_mask(tenants.astype(jnp.int32), pick.shape[0])


def low_kernel(count, aligned, own_ref, down_ref, tenants_ref, *refs):
    x, (span_out, low_ref) = refs[:-2], refs[-2:]
    own = own_ref[0]
    if aligned:
        width = down_ref.shape[0]
        at = pl.ds(pl.multiple_of(own * width, width), width)
        span = jnp.concatenate([ref[:, at] for ref in x], axis=0)
    else:
        span = jnp.concatenate([ref[...] for ref in x], axis=0)
    span_out[...] = span
    rows = span.shape[0]
    wide = jnp.dot(span, down_ref[...], preferred_element_type=jnp.float32)
    low = select_block(wide, held_mask(pick_held(own, rows, count), tenants_ref[...]))
    low_ref[...] = picked(pick_given(own, rows, count), low)


def low_part(own, down, tenants, x, count):
    rows, span = sum(block.shape[0] for block in x), down.shape[0]
    aligned = span % 128 == 0
    if not aligned:
        x = [
            lax.dynamic_slice(
                block, (0, own[0] * span), (block.shape[0], span), allow_negative_indices=False
            )
            for block in x
        ]
    return pl.pallas_call(
        lambda *refs: low_kernel(count, aligned, *refs),
        in_specs=[SMEM] + [VMEM] * (2 + len(x)),
        out_shape=[
            jax.ShapeDtypeStruct((rows, span), x[0].dtype),
            jax.ShapeDtypeStruct((rows, ADAPTER_RANK), jnp.float32),
        ],
        compiler_params=pltpu.CompilerParams(vmem_limit_bytes=6 << 20),
        cost_estimate=pl.CostEstimate(
            flops=2 * rows * down.size, bytes_accessed=2 * down.size, transcendentals=0
        ),
        name="low_part",
    )(own, down, tenants, *x)


def forward_kernel(cut, slots, blocks, first, slot, *refs):
    x = refs[:blocks]
    gate_out, up_out = refs[-2:]
    gate_weight, up_weight = slot(slots[0]), slot(slots[1])
    depth = gate_weight.shape[0]
    at = slice(cut * depth, (cut + 1) * depth)
    rows = jnp.concatenate([ref[:, at] for ref in x], axis=0)
    gate = jnp.dot(rows, gate_weight, preferred_element_type=jnp.float32)
    up = jnp.dot(rows, up_weight, preferred_element_type=jnp.float32)
    if not first:
        gate = gate + refs[blocks][...]
        up = up + refs[blocks + 1][...]
    gate_out[...] = gate
    up_out[...] = up


def forward(cut, slots, x, store, sums, fetches, after):
    rows = sum(block.shape[0] for block in x)
    depth, hidden = store.shape[0] // SLOTS, store.shape[1]
    result = jax.ShapeDtypeStruct((rows, hidden), jnp.float32)
    store, gate, up = store_call(
        lambda *refs: forward_kernel(cut, slots, len(x), not sums, *refs),
        store,
        fetches,
        [*x, *sums],
        [result, result],
        4 * rows * depth * hidden,
        "forward",
        after=after,
    )
    return store, [gate, up]


def activation_kernel(
    count, maps_slot, slot, own_ref, gate_ref, up_ref, hidden_ref, low_ref, tenants_ref,
    dgate_ref, dup_ref, part_ref, spread_ref,
):
    rows = gate_ref.shape[0]
    maps = slot(maps_slot)
    pick = pick_held(own_ref[0], rows, count)
    mask = held_mask(pick, tenants_ref[...])
    spread = spread_rows(picked(pick, low_ref[...]), mask)
    spread_ref[...] = spread
    gate = gate_ref[...] + adapter_scale * jnp.dot(
        spread, maps, preferred_element_type=jnp.float32
    )
    s = jax.nn.sigmoid(gate)
    hidden = picked(pick, hidden_ref[...])
    dgate = (hidden * up_ref[...] * s * (1.0 + gate * (1.0 - s))).astype(jnp.bfloat16)
    dgate_ref[...] = dgate
    dup_ref[...] = (hidden * gate * s).astype(jnp.bfloat16)
    part = select_block(contracted_columns(dgate, maps), mask)
    part_ref[...] = picked(pick_given(own_ref[0], rows, count), part)


def activation(own, maps_slot, store, sums, hidden, low, tenants, count, fetches):
    rows, width = sums[0].shape
    value = jax.ShapeDtypeStruct((rows, width), jnp.bfloat16)
    return store_call(
        lambda *refs: activation_kernel(count, maps_slot, *refs),
        store,
        fetches,
        [own, *sums, hidden, low, tenants],
        [
            value,
            value,
            jax.ShapeDtypeStruct((rows, ADAPTER_RANK), jnp.float32),
            jax.ShapeDtypeStruct((rows, SPREAD), jnp.bfloat16),
        ],
        4 * rows * SPREAD * width,
        "activation",
        smem=1,
    )


def adapter_kernel(count, own_ref, low_ref, tenants_ref, down_ref, own_out, other_out, spread_ref):
    half = own_out.shape[0]
    pick = pick_held(own_ref[0], 2 * half, count)
    spread = spread_rows(picked(pick, low_ref[...]), held_mask(pick, tenants_ref[...]))
    spread_ref[...] = spread
    part = (adapter_scale * contracted_columns(spread, down_ref[...])).astype(jnp.bfloat16)
    own_out[...] = part[:half]
    other_out[...] = part[half:]


def adapter_part(own, low, tenants, down, count):
    rows, span = low.shape[0], down.shape[0]
    half = jax.ShapeDtypeStruct((rows // 2, span), jnp.bfloat16)
    return pl.pallas_call(
        lambda *refs: adapter_kernel(count, *refs),
        in_specs=[SMEM] + [VMEM] * 3,
        out_shape=[half, half, jax.ShapeDtypeStruct((rows, SPREAD), jnp.bfloat16)],
        compiler_params=pltpu.CompilerParams(vmem_limit_bytes=6 << 20),
        cost_estimate=pl.CostEstimate(
            flops=2 * rows * down.size, bytes_accessed=2 * down.size, transcendentals=0
        ),
        name="adapter_part",
    )(own, low, tenants, down)


def backward_kernel(slots, slot, dgate_ref, dup_ref, own_out, other_out):
    half = own_out.shape[0]
    part = contracted_columns(dgate_ref[...], slot(slots[0]))
    part = part + contracted_columns(dup_ref[...], slot(slots[1]))
    own_out[...] = part[:half]
    other_out[...] = part[half:].astype(jnp.bfloat16)


def backward(slots, dgate, dup, store, fetches, after):
    rows, hidden = dgate.shape
    depth = store.shape[0] // SLOTS
    return store_call(
        lambda *refs: backward_kernel(slots, *refs),
        store,
        fetches,
        [dgate, dup],
        [
            jax.ShapeDtypeStruct((rows // 2, depth), jnp.float32),
            jax.ShapeDtypeStruct((rows // 2, depth), jnp.bfloat16),
        ],
        4 * rows * hidden * depth,
        "backward",
        after=after,
    )


PARTS = 8


def merge_kernel(count, own_ref, *refs):
    own, came = refs[:CUTS], refs[CUTS : 2 * CUTS]
    adapter_own, adapter_came, out_ref, sums, tiles = refs[2 * CUTS :]
    chips, tile, lanes = out_ref.shape
    tokens = tile // PARTS
    per_part = (lanes - 128) // 128
    blocks = PARTS * per_part

    def put(first, value):
        for k in range(value.shape[1] // 128):
            sums[first + k] = value[:, k * 128 : (k + 1) * 128]

    for cut in range(CUTS):
        put(cut * blocks // CUTS, own[cut][...] + came[cut][...].astype(jnp.float32))
    mine = adapter_own[...].astype(jnp.float32)
    other = adapter_came[...].astype(jnp.float32)
    put(
        blocks,
        jnp.where(
            own_ref[0] % 2 == 0,
            jnp.concatenate([mine, other], axis=1),
            jnp.concatenate([other, mine], axis=1),
        ),
    )
    if sums.shape[0] < blocks + PARTS:
        tiles[per_part] = jnp.zeros(tiles.shape[1:], jnp.float32)
    for token in range(tokens):
        of_token = pl.ds(token, chips, stride=tokens)
        for part in range(PARTS):
            to = pl.ds(token * PARTS + part, chips, stride=tile)
            for k in range(per_part):
                tiles[k, to, :] = sums[part * per_part + k, of_token, :]
            if blocks + part < sums.shape[0]:
                tiles[per_part, to, :] = sums[blocks + part, of_token, :]
    for position in range(chips):
        chip = block_owner(own_ref[0], position, count) // 2
        for k in range(lanes // 128):
            out_ref[chip, :, k * 128 : (k + 1) * 128] = tiles[
                k, position * tile : (position + 1) * tile, :
            ].astype(jnp.bfloat16)


def merge(device, own, came, adapter_own, adapter_came, own_rows):
    half, depth = own[0].shape
    width = CUTS * depth
    pair = 2 * adapter_own.shape[1]
    lanes = width // PARTS + 128
    chips, tile = half // own_rows, own_rows * PARTS
    return pl.pallas_call(
        lambda *refs: merge_kernel(2 * chips, *refs),
        in_specs=[SMEM] + [VMEM] * (2 * CUTS + 2),
        out_shape=jax.ShapeDtypeStruct((chips, tile, lanes), jnp.bfloat16),
        scratch_shapes=[
            pltpu.VMEM(((width + pair) // 128, half, 128), jnp.float32),
            pltpu.VMEM((lanes // 128, chips * tile, 128), jnp.float32),
        ],
        compiler_params=pltpu.CompilerParams(vmem_limit_bytes=40 << 20),
        name="merge",
    )(device, *own, *came, adapter_own, adapter_came)


def final_kernel(pair, came_ref, out_ref, total, adapter):
    chips, tile, lanes = came_ref.shape
    tokens = tile // PARTS
    blocks = (lanes - 128) // 128
    for k in range(blocks):
        at = slice(k * 128, (k + 1) * 128)
        value = came_ref[0, :, at].astype(jnp.float32)
        for chip in range(1, chips):
            value = value + came_ref[chip, :, at].astype(jnp.float32)
        total[k] = value
    adapter[...] = came_ref[:, :, lanes - 128 :].astype(jnp.float32).reshape(adapter.shape)
    of_pair = pair // 128
    for token in range(tokens):
        rows = slice(token * PARTS, (token + 1) * PARTS)
        for k in range(blocks):
            chip, part = divmod(k, of_pair)
            source = pl.ds(
                chip * tile + token * PARTS + part, PARTS, stride=blocks // of_pair * tile
            )
            total[k, rows, :] += adapter[source, :]
    for part in range(PARTS):
        for k in range(blocks):
            at = (part * blocks + k) * 128
            out_ref[:, at : at + 128] = total[k, pl.ds(part, tokens, stride=PARTS), :].astype(
                jnp.bfloat16
            )


def final(came, pair):
    chips, tile, lanes = came.shape
    piece = lanes - 128
    return pl.pallas_call(
        lambda *refs: final_kernel(pair, *refs),
        out_shape=jax.ShapeDtypeStruct((tile // PARTS, piece * PARTS), jnp.bfloat16),
        scratch_shapes=[
            pltpu.VMEM((piece // 128, tile, 128), jnp.float32),
            pltpu.VMEM((chips * tile, 128), jnp.float32),
        ],
        compiler_params=pltpu.CompilerParams(vmem_limit_bytes=40 << 20),
        name="final",
    )(came)


def outer_kernel(left_ref, right_ref, out_ref):
    out_ref[...] = contracted_rows(
        left_ref[...] * jnp.bfloat16(adapter_scale), right_ref[...]
    ).astype(jnp.bfloat16)


def outer(left, right, name):
    rows, height = left.shape
    width = right.shape[1]
    block = block_of(height, 256)
    if block % 128:
        block = height
    return pl.pallas_call(
        outer_kernel,
        grid=(height // block,),
        in_specs=[
            pl.BlockSpec((rows, block), lambda k: (0, k)),
            pl.BlockSpec((rows, width), lambda k: (0, 0)),
        ],
        out_specs=pl.BlockSpec((block, width), lambda k: (k, 0)),
        out_shape=jax.ShapeDtypeStruct((height, width), jnp.bfloat16),
        compiler_params=pltpu.CompilerParams(vmem_limit_bytes=24 << 20),
        cost_estimate=pl.CostEstimate(
            flops=2 * rows * height * width, bytes_accessed=2 * height * width, transcendentals=0
        ),
        name=name,
    )(left, right)


def same_core_groups():
    count = lax.axis_size("tp")
    return [list(range(core, count, 2)) for core in range(2)]


def between_same_cores(blocks):
    return lax.all_to_all(
        blocks, "tp", split_axis=0, concat_axis=0, tiled=True, axis_index_groups=same_core_groups()
    )


def swapped(block, hop):
    return lax.ppermute(block, "tp", [(i, i ^ hop) for i in range(lax.axis_size("tp"))])


def local(
    normed_layer_input,
    hidden_unit_gradient,
    gate_weight,
    up_weight,
    adapter_down_maps,
    adapter_up_maps,
    token_tenant_index,
):
    count = lax.axis_size("tp")
    own = lax.axis_index("tp").astype(jnp.int32).reshape(1)
    own_rows, width = normed_layer_input.shape
    rows = own_rows * count
    hops = [1 << bit for bit in range(count.bit_length() - 1)]
    tenants = token_tenant_index.reshape(1, rows)

    def pair(cut, first, second):
        return [(gate_weight, cut, first), (up_weight, cut, second)]

    def mark(slot, token_ref):
        token_ref[...] = jnp.zeros_like(token_ref)

    token = jax.ShapeDtypeStruct((8, 128), jnp.float32)
    store = jax.ShapeDtypeStruct(
        (SLOTS * width // CUTS, gate_weight.shape[1]), gate_weight.dtype
    )
    far, near = hops[-1], hops[-2]
    came = [swapped(normed_layer_input, hop) for hop in (near, far, near | far)]
    store, token = store_call(mark, store, pair(0, 0, 1), [], [token], 0, "fetch", after=[own])
    block = stacked([normed_layer_input, *came], [token])
    for hop in reversed(hops[2:-2]):
        block = stacked([block, swapped(block, hop)])
    other = swapped(block, hops[1])
    x = [block, other, swapped(block, 1), swapped(other, 1)]
    store, token = store_call(mark, store, pair(1, 2, 3), [], [token], 0, "fetch", after=[block])

    input_span, low = low_part(own, adapter_down_maps, tenants, x, count)
    sums = []
    slots = {0: (0, 1), 1: (2, 3), 2: (4, 5), 3: (0, 1)}
    fetches = {
        0: pair(2, 4, 5), 1: pair(3, 0, 1), 2: [(adapter_up_maps, 0, 2)], 3: [(gate_weight, 1, 3)]
    }
    step = 0
    for cut in range(CUTS):
        after = [low]
        if step < len(hops):
            low = low + swapped(low, hops[step])
            step += 1
        store, sums = forward(cut, slots[cut], x, store, sums, fetches[cut], after)
    for hop in hops[step:]:
        low = low + swapped(low, hop)
    store, dgate, dup, low_grad, input_spread = activation(
        own, 2, store, sums, hidden_unit_gradient, low, tenants, count, []
    )

    low_grad = low_grad + swapped(low_grad, hops[0])
    step = 1
    parts, arrived = {}, {}
    slots = {3: (0, 1), 2: (4, 5), 1: (3, 2), 0: (0, 1)}
    fetches = {3: [(up_weight, 1, 2)], 2: pair(0, 0, 1), 1: [], 0: []}
    for cut in reversed(range(CUTS)):
        if cut > 0:
            after = [low_grad]
            if step < len(hops):
                low_grad = low_grad + swapped(low_grad, hops[step])
                step += 1
        store, own_part, other_part = backward(slots[cut], dgate, dup, store, fetches[cut], after)
        if cut == 1:
            for hop in hops[step:]:
                low_grad = low_grad + swapped(low_grad, hop)
            adapter_own, adapter_other, grad_spread = adapter_part(
                own, low_grad, tenants, adapter_down_maps, count
            )
            adapter_came = swapped(adapter_other, 1)
            after = [adapter_other]
        parts[cut] = own_part
        arrived[cut] = swapped(other_part, 1)
    merged = merge(
        own,
        [parts[cut] for cut in range(CUTS)],
        [arrived[cut] for cut in range(CUTS)],
        adapter_own,
        adapter_came,
        own_rows,
    )
    exchanged = between_same_cores(merged)
    down_map_gradient = outer(input_span, grad_spread, "down_maps")
    up_map_gradient = outer(input_spread, dgate, "up_maps")
    return (final(exchanged, 2 * input_span.shape[1]), down_map_gradient, up_map_gradient)


def solution(mesh):
    placed = (
        P(("groups", "tp"), None),
        P("groups", "tp"),
        P(None, "tp"),
        P(None, "tp"),
        P("tp", None),
        P(None, "tp"),
        P("groups"),
    )
    return jax.shard_map(
        local,
        mesh=mesh,
        in_specs=placed,
        out_specs=(P(("groups", "tp"), None), P("tp", "groups"), P("groups", "tp")),
        check_vma=False,
    )
```

time: 138 us -> 120 us (0.87)
  local copies, waits for them, and re-layouts: 35.9 us -> 3.34 us
  Pallas kernels: 72.6 us -> 78.8 us
  other arithmetic: 1.45 us -> 6.39 us
  waiting for transfers between devices: 5.32 us -> 7.89 us
    unnamed x52 -> x50, local copies, waits for them, and re-layouts: 35.3 us -> 3.34 us
    pallas_call x14, Pallas kernels: 64 us -> 70.3 us  [the longest x11 67.7 us: store_call(): pl.pallas_call(body, in_specs=([] if new else [VMEM]) + [SMEM] * smem + [...]
    add x4, other arithmetic: 0.02 us -> 3.5 us  [local(): low = low + swapped(low, hops[step])]
    ppermute x19, waiting for transfers between devices: 3 us -> 5.69 us  [swapped(): lax.ppermute(block, 'tp', [(i, i ^ hop) for i in range(lax.axis_size('tp'...]
    add x3, other arithmetic: 0.01 us -> 2.16 us  [local(): low_grad = low_grad + swapped(low_grad, hops[step])]
    all_to_all x1, starting transfers between devices: 3.42 us -> 5.04 us  [between_same_cores(): lax.all_to_all(blocks, 'tp', split_axis=0, concat_axis=0, tiled=True, axi...]
  transfers between devices with their start and end apart: 20 -> 20, of which waited for: 4 -> 4; matrix products, arithmetic and copies ran while one was open for 0% -> 2% of each run, Pallas kernels for 47% -> 59%
where the time goes in v6:
time: 120 us
  Pallas kernels  78.8 us (66%)
  starting transfers between devices  22.1 us (18%)
  waiting for transfers between devices  7.89 us (7%)
  other arithmetic  6.39 us (5%)
  local copies, waits for them, and re-layouts  3.34 us (3%)
    pallas_call x11, Pallas kernels, store_call(): pl.pallas_call(body, in_specs=([] if new else [VMEM]) + [SMEM] * smem + [...  67.7 us
    ppermute x19, starting transfers between devices, swapped(): lax.ppermute(block, 'tp', [(i, i ^ hop) for i in range(lax.axis_size('tp'...  17 us
    pallas_call x2, Pallas kernels, outer(): pl.pallas_call(outer_kernel, grid=(height // block,), in_specs=[pl.BlockS...  7.76 us
    ppermute x19, waiting for transfers between devices, swapped(): lax.ppermute(block, 'tp', [(i, i ^ hop) for i in range(lax.axis_size('tp'...  5.69 us
    all_to_all x1, starting transfers between devices, between_same_cores(): lax.all_to_all(blocks, 'tp', split_axis=0, concat_axis=0, tiled=True, axi...  5.04 us
    add x4, other arithmetic, local(): low = low + swapped(low, hops[step])  3.5 us
    unnamed x50, local copies, waits for them, and re-layouts  3.34 us
  transfers between devices with their start and end apart: 20, of which 4 were waited for; matrix products, arithmetic and copies ran while one was open for 2% of the time, Pallas kernels for 59%

profile of v6, /device:TPU:0, one launch (start us, length us, event | category | flops | bytes accessed | tf_op | source)
XLA Modules:
  0.0 119.5 jit_solution(5957012027037764592)
XLA Ops:
  0.6 3.1 %collective-permute-start = (bf16[2,8192]{1,0:T(2,128)(2,1)}, bf16[2,8192]{1,0:T(2,128)(2,1)S(1)}, u32[]{:S(2)}, u32[]{:S(2)}) collective-permute-start(bf16[2,8192]{1,0:T(2,128)(2,1)} %refs_0_.3), channel_id=1, source_target_pairs={{0,4},{1,5},{2,6},{3,7},{4,0},{5,1},{6,2},{7,3},{8,12},{9,13},{10,... | collective-permute-start | bytes 98312 | tf_op jit(solution)/shard_map/ppermute | solution.py:481
  3.7 2.6 %collective-permute-start.1 = (bf16[2,8192]{1,0:T(2,128)(2,1)}, bf16[2,8192]{1,0:T(2,128)(2,1)S(1)}, u32[]{:S(2)}, u32[]{:S(2)}) collective-permute-start(bf16[2,8192]{1,0:T(2,128)(2,1)} %refs_0_.3), channel_id=1, source_target_pairs={{0,8},{1,9},{2,10},{3,11},{4,12},{5,13},{6,14},{7,15},{8,0},{9,1},... | collective-permute-start | bytes 98312 | tf_op jit(solution)/shard_map/ppermute | solution.py:481
  6.3 5.9 %fetch.2 = (bf16[12288,1792]{1,0:T(8,128)(2,1)S(1)}, f32[8,128]{1,0:T(8,128)}) custom-call(bf16[8192,1792]{1,0:T(8,128)(2,1)} %refs_3_.4, bf16[8192,1792]{1,0:T(8,128)(2,1)} %refs_4_.3, s32[1]{0:T(128)} %bitcast.refs_2_.refs_0_.refs_1_), custom_call_target="tpu_custom_call" | custom-call | bytes 14680064 | tf_op jit(solution)/shard_map/fetch/pallas_call | solution.py:96
  12.2 0.0 collective-permute-done.refs_1_
  12.3 0.0 copy-start.18
  12.3 0.7 copy-done.18
  13.0 0.1 stacked.1.refs_3_.refs_1_
  13.1 1.8 %collective-permute-start.3 = (bf16[8,8192]{1,0:T(8,128)(2,1)S(1)}, bf16[8,8192]{1,0:T(8,128)(2,1)S(1)}, u32[]{:S(2)}, u32[]{:S(2)}) collective-permute-start(bf16[8,8192]{1,0:T(8,128)(2,1)S(1)} %stacked.1.refs_3_.refs_1_), channel_id=1, source_target_pairs={{0,2},{1,3},{2,0},{3,1},{4,6},{5,7},{6,4},{7,5},{8,10},{9,11},{10,... | collective-permute-start | bytes 393224 | tf_op jit(solution)/shard_map/ppermute | solution.py:481
  14.9 3.2 %collective-permute-done.3.refs_4_.refs_2_ = bf16[8,8192]{1,0:T(8,128)(2,1)S(1)} collective-permute-done((bf16[8,8192]{1,0:T(8,128)(2,1)S(1)}, bf16[8,8192]{1,0:T(8,128)(2,1)S(1)}, u32[]{:S(2)}, u32[]{:S(2)}) %collective-permute-start.3) | collective-permute-done | bytes 131104 | tf_op jit(solution)/shard_map/ppermute | solution.py:481
  18.1 0.0 collective-permute-start.5
  18.1 0.0 copy-start
  18.1 0.0 copy-start.16
  18.1 6.0 %fetch.3 = (bf16[12288,1792]{1,0:T(8,128)(2,1)S(1)}, f32[8,128]{1,0:T(8,128)}) custom-call(bf16[12288,1792]{1,0:T(8,128)(2,1)S(1)} %get-tuple-element.39.refs_0_, bf16[8192,1792]{1,0:T(8,128)(2,1)} %refs_3_.4, bf16[8192,1792]{1,0:T(8,128)(2,1)} %refs_4_.3, bf16[8,8192]{1,0:T(8,128)(2,1)} %copy-done.1), custom_call_target="tpu_custom_call", output_to_operand_aliasing={{0}: (0, {})} | custom-call | bytes 14680064 | tf_op jit(solution)/shard_map/fetch/pallas_call | solution.py:96
  24.2 0.0 collective-permute-done.4.refs_5_.refs_3_
  24.3 0.9 copy-done.2
  25.2 0.7 low_part.1
  25.9 0.5 collective-permute-start.6
  26.4 0.1 copy-done.12
  26.5 7.2 %forward.4 = (bf16[12288,1792]{1,0:T(8,128)(2,1)S(1)}, f32[32,1792]{1,0:T(8,128)}, f32[32,1792]{1,0:T(8,128)}) custom-call(bf16[12288,1792]{1,0:T(8,128)(2,1)S(1)} %get-tuple-element.41.refs_0_, bf16[8,8192]{1,0:T(8,128)(2,1)} %copy-done.1, bf16[8,8192]{1,0:T(8,128)(2,1)} %copy-done.3, bf16[8,8192]{1,0:T(8,128)(2,1)} %copy-done.4, ...), custom_call_target="tpu_custom_call", output_to_operand_aliasing={{0}: (0, {})} | custom-call | flops 469762048 | bytes 14680064 | tf_op jit(solution)/shard_map/forward/pallas_call | solution.py:96
  33.7 0.0 collective-permute-done.6
  33.7 0.7 add.24.refs_9_
  34.4 1.7 %collective-permute-start.7 = (f32[32,64]{1,0:T(8,128)S(1)}, f32[32,64]{1,0:T(8,128)S(1)}, u32[]{:S(2)}, u32[]{:S(2)}) collective-permute-start(f32[32,64]{1,0:T(8,128)S(1)} %add.24.refs_9_), channel_id=1, source_target_pairs={{0,2},{1,3},{2,0},{3,1},{4,6},{5,7},{6,4},{7,5},{8,10},{9,11},{10,... | collective-permute-start | bytes 24584 | tf_op jit(solution)/shard_map/ppermute | solution.py:481
  36.2 7.4 %forward.5 = (bf16[12288,1792]{1,0:T(8,128)(2,1)S(1)}, f32[32,1792]{1,0:T(8,128)}, f32[32,1792]{1,0:T(8,128)}) custom-call(bf16[12288,1792]{1,0:T(8,128)(2,1)S(1)} %get-tuple-element.43.refs_0_, bf16[8,8192]{1,0:T(8,128)(2,1)} %copy-done.1, bf16[8,8192]{1,0:T(8,128)(2,1)} %copy-done.3, bf16[8,8192]{1,0:T(8,128)(2,1)} %copy-done.4, ...), custom_call_target="tpu_custom_call", output_to_operand_aliasing={{0}: (0, {})} | custom-call | flops 469762048 | bytes 14680064 | tf_op jit(solution)/shard_map/forward/pallas_call | solution.py:96
  43.6 0.0 collective-permute-done.7
  43.6 0.7 add.25.refs_8_
  44.3 0.7 collective-permute-start.8
  45.0 5.2 %forward.6 = (bf16[12288,1792]{1,0:T(8,128)(2,1)S(1)}, f32[32,1792]{1,0:T(8,128)}, f32[32,1792]{1,0:T(8,128)}) custom-call(bf16[12288,1792]{1,0:T(8,128)(2,1)S(1)} %get-tuple-element.46.refs_0_, bf16[8,8192]{1,0:T(8,128)(2,1)} %copy-done.1, bf16[8,8192]{1,0:T(8,128)(2,1)} %copy-done.3, bf16[8,8192]{1,0:T(8,128)(2,1)} %copy-done.4, ...), custom_call_target="tpu_custom_call", output_to_operand_aliasing={{0}: (0, {})} | custom-call | flops 469762048 | bytes 7340032 | tf_op jit(solution)/shard_map/forward/pallas_call | solution.py:96
  50.2 0.0 collective-permute-done.8
  50.2 0.7 add.26.refs_8_
  50.9 3.5 %collective-permute-start.9 = (f32[32,64]{1,0:T(8,128)S(1)}, f32[32,64]{1,0:T(8,128)S(1)}, u32[]{:S(2)}, u32[]{:S(2)}) collective-permute-start(f32[32,64]{1,0:T(8,128)S(1)} %add.26.refs_8_), channel_id=1, source_target_pairs={{0,8},{1,9},{2,10},{3,11},{4,12},{5,13},{6,14},{7,15},{8,0},{9,1},... | collective-permute-start | bytes 24584 | tf_op jit(solution)/shard_map/ppermute | solution.py:481
  54.4 5.2 %forward.7 = (bf16[12288,1792]{1,0:T(8,128)(2,1)S(1)}, f32[32,1792]{1,0:T(8,128)}, f32[32,1792]{1,0:T(8,128)}) custom-call(bf16[12288,1792]{1,0:T(8,128)(2,1)S(1)} %get-tuple-element.49.refs_0_, bf16[8,8192]{1,0:T(8,128)(2,1)} %copy-done.1, bf16[8,8192]{1,0:T(8,128)(2,1)} %copy-done.3, bf16[8,8192]{1,0:T(8,128)(2,1)} %copy-done.4, ...), custom_call_target="tpu_custom_call", output_to_operand_aliasing={{0}: (0, {})} | custom-call | flops 469762048 | bytes 7340032 | tf_op jit(solution)/shard_map/forward/pallas_call | solution.py:96
  59.7 0.0 collective-permute-done.9
  59.7 1.3 %add.27.refs_5_ = f32[32,64]{1,0:T(8,128)} add(f32[32,64]{1,0:T(8,128)} %copy-done.19, f32[32,64]{1,0:T(8,128)S(1)} %collective-permute-done.9) | non-fusion elementwise | flops 2048 | bytes 24576 | tf_op jit(solution)/shard_map/add | solution.py:530
  61.0 5.6 %activation.1 = (bf16[12288,1792]{1,0:T(8,128)(2,1)S(1)}, bf16[32,1792]{1,0:T(8,128)(2,1)}, bf16[32,1792]{1,0:T(8,128)(2,1)}, f32[32,64]{1,0:T(8,128)}, bf16[32,2048]{1,0:T(8,128)(2,1)}) custom-call(bf16[12288,1792]{1,0:T(8,128)(2,1)S(1)} %get-tuple-element.52.refs_0_, s32[1]{0:T(128)} %bitcast.refs_2_.refs_0_.refs_1_, ...), custom_call_target="tpu_custom_call", output_to_operand_aliasing={{0}: (0, {})} | custom-call | flops 469762048 | tf_op jit(solution)/shard_map/activation/pallas_call | solution.py:96
  66.6 1.4 %collective-permute-done.10 = f32[32,64]{1,0:T(8,128)S(1)} collective-permute-done((f32[32,64]{1,0:T(8,128)}, f32[32,64]{1,0:T(8,128)S(1)}, u32[]{:S(2)}, u32[]{:S(2)}) %collective-permute-start.10) | collective-permute-done | bytes 8224 | tf_op jit(solution)/shard_map/ppermute | solution.py:481
  68.0 0.7 add.28.refs_4_
  68.7 0.6 collective-permute-start.11
  69.3 6.2 %backward.4 = (bf16[12288,1792]{1,0:T(8,128)(2,1)S(1)}, f32[16,2048]{1,0:T(8,128)}, bf16[16,2048]{1,0:T(8,128)(2,1)}) custom-call(bf16[12288,1792]{1,0:T(8,128)(2,1)S(1)} %get-tuple-element.55.refs_0_, bf16[32,1792]{1,0:T(8,128)(2,1)} %get-tuple-element.56.refs_1_.right_ref, ...), custom_call_target="tpu_custom_call", output_to_operand_aliasing={{0}: (0, {})} | custom-call | flops 469762048 | bytes 7340032 | tf_op jit(solution)/shard_map/backward/pallas_call | solution.py:96
  75.5 0.2 collective-permute-start.17
  75.7 0.7 add.29.refs_5_
  76.5 0.6 collective-permute-start.12
  77.1 6.9 %backward.5 = (bf16[12288,1792]{1,0:T(8,128)(2,1)S(1)}, f32[16,2048]{1,0:T(8,128)}, bf16[16,2048]{1,0:T(8,128)(2,1)}) custom-call(bf16[12288,1792]{1,0:T(8,128)(2,1)S(1)} %get-tuple-element.59.refs_0_, bf16[32,1792]{1,0:T(8,128)(2,1)} %get-tuple-element.56.refs_1_.right_ref, ...), custom_call_target="tpu_custom_call", output_to_operand_aliasing={{0}: (0, {})} | custom-call | flops 469762048 | bytes 14680064 | tf_op jit(solution)/shard_map/backward/pallas_call | solution.py:96
  84.0 0.0 copy-start.17
  84.0 0.4 collective-permute-start.16
  84.4 0.7 add.30.refs_3_
  85.2 0.6 collective-permute-start.13
  85.8 0.0 copy-start.11
  85.8 6.0 %backward.6 = (bf16[12288,1792]{1,0:T(8,128)(2,1)S(1)}, f32[16,2048]{1,0:T(8,128)}, bf16[16,2048]{1,0:T(8,128)(2,1)}) custom-call(bf16[12288,1792]{1,0:T(8,128)(2,1)S(1)} %get-tuple-element.60.refs_0_, bf16[32,1792]{1,0:T(8,128)(2,1)} %get-tuple-element.56.refs_1_.right_ref, ...), custom_call_target="tpu_custom_call", output_to_operand_aliasing={{0}: (0, {})} | custom-call | flops 469762048 | tf_op jit(solution)/shard_map/backward/pallas_call | solution.py:96
  91.8 0.2 collective-permute-start.15
  92.0 0.7 add.31.refs_1_
  92.7 0.9 adapter_part.1
  93.6 0.0 copy-start.14
  93.6 0.6 copy-done.14
  94.2 6.0 %backward.7 = (bf16[12288,1792]{1,0:T(8,128)(2,1)S(1)}, f32[16,2048]{1,0:T(8,128)}, bf16[16,2048]{1,0:T(8,128)(2,1)}) custom-call(bf16[12288,1792]{1,0:T(8,128)(2,1)S(1)} %get-tuple-element.61.refs_0_, bf16[32,1792]{1,0:T(8,128)(2,1)} %get-tuple-element.56.refs_1_.right_ref, ...), custom_call_target="tpu_custom_call", output_to_operand_aliasing={{0}: (0, {})} | custom-call | flops 469762048 | tf_op jit(solution)/shard_map/backward/pallas_call | solution.py:96
  100.2 0.4 collective-permute-start.14
  100.6 0.2 collective-permute-start.18
  100.7 1.0 collective-permute-done.18.refs_10_
  101.8 0.9 copy-done.10
  102.7 1.1 merge.1
  103.8 5.0 %all-to-all-start = ((bf16[8,16,1152]{2,1,0:T(8,128)(2,1)}), bf16[8,16,1152]{2,1,0:T(8,128)(2,1)S(1)}, u32[]{:S(2)}, u32[]{:S(2)}) async-start(bf16[8,16,1152]{2,1,0:T(8,128)(2,1)} %merge.1), calls=%async_computation | async-start | bytes 589824 | tf_op jit(solution)/shard_map/all_to_all | solution.py:475
  108.9 5.9 %up_maps.1 = bf16[2048,1792]{1,0:T(8,128)(2,1)} custom-call(bf16[32,2048]{1,0:T(8,128)(2,1)S(1)} %copy-done.11, bf16[32,1792]{1,0:T(8,128)(2,1)S(1)} %copy-done.6), custom_call_target="tpu_custom_call" | custom-call | flops 234881024 | bytes 7340032 | tf_op jit(solution)/shard_map/up_maps/pallas_call | solution.py:452
  114.7 1.9 %down_maps.1 = bf16[512,2048]{1,0:T(8,128)(2,1)} custom-call(bf16[32,512]{1,0:T(8,128)(2,1)S(1)} %get-tuple-element.72.left_ref, bf16[32,2048]{1,0:T(8,128)(2,1)S(1)} %get-tuple-element.73.right_ref), custom_call_target="tpu_custom_call" | custom-call | flops 67108864 | bytes 2097152 | tf_op jit(solution)/shard_map/down_maps/pallas_call | solution.py:452
  116.6 2.2 %all-to-all-done.refs_0_ = bf16[8,16,1152]{2,1,0:T(8,128)(2,1)S(1)} async-done(((bf16[8,16,1152]{2,1,0:T(8,128)(2,1)}), bf16[8,16,1152]{2,1,0:T(8,128)(2,1)S(1)}, u32[]{:S(2)}, u32[]{:S(2)}) %all-to-all-start) | async-done | bytes 294944 | tf_op jit(solution)/shard_map/all_to_all | solution.py:475
  118.8 0.7 final.1
  (52 shorter events, 0.1 us)
Async XLA Ops:
  0.6 11.6 %copy-start.13 = (bf16[2,8192]{1,0:T(2,128)(2,1)S(1)}, bf16[2,8192]{1,0:T(2,128)(2,1)}, u32[]{:S(2)}) copy-start(bf16[2,8192]{1,0:T(2,128)(2,1)} %refs_0_.3) | copy-start | bytes 98308
  0.6 11.6 %collective-permute-start = (bf16[2,8192]{1,0:T(2,128)(2,1)}, bf16[2,8192]{1,0:T(2,128)(2,1)S(1)}, u32[]{:S(2)}, u32[]{:S(2)}) collective-permute-start(bf16[2,8192]{1,0:T(2,128)(2,1)} %refs_0_.3), channel_id=1, source_target_pairs={{0,4},{1,5},{2,6},{3,7},{4,0},{5,1},{6,2},{7,3},{8,12},{9,13},{10,... | collective-permute-start | bytes 98312 | tf_op jit(solution)/shard_map/ppermute | solution.py:481
  3.7 8.5 %collective-permute-start.1 = (bf16[2,8192]{1,0:T(2,128)(2,1)}, bf16[2,8192]{1,0:T(2,128)(2,1)S(1)}, u32[]{:S(2)}, u32[]{:S(2)}) collective-permute-start(bf16[2,8192]{1,0:T(2,128)(2,1)} %refs_0_.3), channel_id=1, source_target_pairs={{0,8},{1,9},{2,10},{3,11},{4,12},{5,13},{6,14},{7,15},{8,0},{9,1},... | collective-permute-start | bytes 98312 | tf_op jit(solution)/shard_map/ppermute | solution.py:481
  6.3 5.9 %collective-permute-start.2 = (bf16[2,8192]{1,0:T(2,128)(2,1)}, bf16[2,8192]{1,0:T(2,128)(2,1)S(1)}, u32[]{:S(2)}, u32[]{:S(2)}) collective-permute-start(bf16[2,8192]{1,0:T(2,128)(2,1)} %refs_0_.3), channel_id=1, source_target_pairs={{0,12},{1,13},{2,14},{3,15},{4,8},{5,9},{6,10},{7,11},{8,4},{9,5},... | collective-permute-start | bytes 98312 | tf_op jit(solution)/shard_map/ppermute | solution.py:481
  12.3 0.7 copy-start.18
  13.1 5.1 %copy-start.1 = (bf16[8,8192]{1,0:T(8,128)(2,1)}, bf16[8,8192]{1,0:T(8,128)(2,1)S(1)}, u32[]{:S(2)}) copy-start(bf16[8,8192]{1,0:T(8,128)(2,1)S(1)} %stacked.1.refs_3_.refs_1_) | copy-start | bytes 393220
  13.1 5.0 %collective-permute-start.3 = (bf16[8,8192]{1,0:T(8,128)(2,1)S(1)}, bf16[8,8192]{1,0:T(8,128)(2,1)S(1)}, u32[]{:S(2)}, u32[]{:S(2)}) collective-permute-start(bf16[8,8192]{1,0:T(8,128)(2,1)S(1)} %stacked.1.refs_3_.refs_1_), channel_id=1, source_target_pairs={{0,2},{1,3},{2,0},{3,1},{4,6},{5,7},{6,4},{7,5},{8,10},{9,11},{10,... | collective-permute-start | bytes 393224 | tf_op jit(solution)/shard_map/ppermute | solution.py:481
  14.9 9.3 %collective-permute-start.4 = (bf16[8,8192]{1,0:T(8,128)(2,1)S(1)}, bf16[8,8192]{1,0:T(8,128)(2,1)S(1)}, u32[]{:S(2)}, u32[]{:S(2)}) collective-permute-start(bf16[8,8192]{1,0:T(8,128)(2,1)S(1)} %stacked.1.refs_3_.refs_1_), channel_id=1, source_target_pairs={{0,1},{1,0},{2,3},{3,2},{4,5},{5,4},{6,7},{7,6},{8,9},{9,8},{10,11... | collective-permute-start | bytes 393224 | tf_op jit(solution)/shard_map/ppermute | solution.py:481
  18.1 6.1 %copy-start.3 = (bf16[8,8192]{1,0:T(8,128)(2,1)}, bf16[8,8192]{1,0:T(8,128)(2,1)S(1)}, u32[]{:S(2)}) copy-start(bf16[8,8192]{1,0:T(8,128)(2,1)S(1)} %collective-permute-done.3.refs_4_.refs_2_) | copy-start | bytes 393220
  18.1 6.1 %collective-permute-start.5 = (bf16[8,8192]{1,0:T(8,128)(2,1)S(1)}, bf16[8,8192]{1,0:T(8,128)(2,1)S(1)}, u32[]{:S(2)}, u32[]{:S(2)}) collective-permute-start(bf16[8,8192]{1,0:T(8,128)(2,1)S(1)} %collective-permute-done.3.refs_4_.refs_2_), channel_id=1, source_target_pairs={{0,1},{1,0},{2,3},{3,2},{4,5},{5,4},{6,7},{7,6},{8,9},{9,8},{10,11... | collective-permute-start | bytes 393224 | tf_op jit(solution)/shard_map/ppermute | solution.py:481
  18.1 6.1 %copy-start = (bf16[512,2048]{1,0:T(8,128)(2,1)S(1)}, bf16[512,2048]{1,0:T(8,128)(2,1)}, u32[]{:S(2)}) copy-start(bf16[512,2048]{1,0:T(8,128)(2,1)} %refs_3_.5) | copy-start | bytes 6291460
  18.1 6.1 %copy-start.16 = (s32[32]{0:T(128)S(1)}, s32[32]{0:T(128)}, u32[]{:S(2)}) copy-start(s32[32]{0:T(128)} %param.13) | copy-start | bytes 388
  24.2 2.2 %copy-start.4 = (bf16[8,8192]{1,0:T(8,128)(2,1)}, bf16[8,8192]{1,0:T(8,128)(2,1)S(1)}, u32[]{:S(2)}) copy-start(bf16[8,8192]{1,0:T(8,128)(2,1)S(1)} %collective-permute-done.4.refs_5_.refs_3_) | copy-start | bytes 393220
  24.2 2.2 %copy-start.5 = (bf16[8,8192]{1,0:T(8,128)(2,1)}, bf16[8,8192]{1,0:T(8,128)(2,1)S(1)}, u32[]{:S(2)}) copy-start(bf16[8,8192]{1,0:T(8,128)(2,1)S(1)} %collective-permute-done.5.refs_6_.refs_4_) | copy-start | bytes 393220
  24.3 1.0 copy-start.2
  25.9 0.6 copy-start.12
  25.9 7.8 %collective-permute-start.6 = (f32[32,64]{1,0:T(8,128)S(1)}, f32[32,64]{1,0:T(8,128)S(1)}, u32[]{:S(2)}, u32[]{:S(2)}) collective-permute-start(f32[32,64]{1,0:T(8,128)S(1)} %get-tuple-element.42.refs_7_), channel_id=1, source_target_pairs={{0,1},{1,0},{2,3},{3,2},{4,5},{5,4},{6,7},{7,6},{8,9},{9,8},{10,11... | collective-permute-start | bytes 24584 | tf_op jit(solution)/shard_map/ppermute | solution.py:481
  34.4 1.7 %copy-start.22 = (f32[32,64]{1,0:T(8,128)}, f32[32,64]{1,0:T(8,128)S(1)}, u32[]{:S(2)}) copy-start(f32[32,64]{1,0:T(8,128)S(1)} %add.24.refs_9_) | copy-start | bytes 24580
  34.4 9.1 %collective-permute-start.7 = (f32[32,64]{1,0:T(8,128)S(1)}, f32[32,64]{1,0:T(8,128)S(1)}, u32[]{:S(2)}, u32[]{:S(2)}) collective-permute-start(f32[32,64]{1,0:T(8,128)S(1)} %add.24.refs_9_), channel_id=1, source_target_pairs={{0,2},{1,3},{2,0},{3,1},{4,6},{5,7},{6,4},{7,5},{8,10},{9,11},{10,... | collective-permute-start | bytes 24584 | tf_op jit(solution)/shard_map/ppermute | solution.py:481
  44.3 0.7 copy-start.23
  44.3 5.9 %collective-permute-start.8 = (f32[32,64]{1,0:T(8,128)S(1)}, f32[32,64]{1,0:T(8,128)S(1)}, u32[]{:S(2)}, u32[]{:S(2)}) collective-permute-start(f32[32,64]{1,0:T(8,128)S(1)} %add.25.refs_8_), channel_id=1, source_target_pairs={{0,4},{1,5},{2,6},{3,7},{4,0},{5,1},{6,2},{7,3},{8,12},{9,13},{10,... | collective-permute-start | bytes 24584 | tf_op jit(solution)/shard_map/ppermute | solution.py:481
  50.9 3.5 %copy-start.19 = (f32[32,64]{1,0:T(8,128)}, f32[32,64]{1,0:T(8,128)S(1)}, u32[]{:S(2)}) copy-start(f32[32,64]{1,0:T(8,128)S(1)} %add.26.refs_8_) | copy-start | bytes 24580
  50.9 8.7 %collective-permute-start.9 = (f32[32,64]{1,0:T(8,128)S(1)}, f32[32,64]{1,0:T(8,128)S(1)}, u32[]{:S(2)}, u32[]{:S(2)}) collective-permute-start(f32[32,64]{1,0:T(8,128)S(1)} %add.26.refs_8_), channel_id=1, source_target_pairs={{0,8},{1,9},{2,10},{3,11},{4,12},{5,13},{6,14},{7,15},{8,0},{9,1},... | collective-permute-start | bytes 24584 | tf_op jit(solution)/shard_map/ppermute | solution.py:481
  66.6 1.4 %collective-permute-start.10 = (f32[32,64]{1,0:T(8,128)}, f32[32,64]{1,0:T(8,128)S(1)}, u32[]{:S(2)}, u32[]{:S(2)}) collective-permute-start(f32[32,64]{1,0:T(8,128)} %get-tuple-element.58), channel_id=1, source_target_pairs={{0,1},{1,0},{2,3},{3,2},{4,5},{5,4},{6,7},{7,6},{8,9},{9,8},{10,11... | collective-permute-start | bytes 24584 | tf_op jit(solution)/shard_map/ppermute | solution.py:481
  68.7 0.6 copy-start.24
  68.7 7.0 %collective-permute-start.11 = (f32[32,64]{1,0:T(8,128)S(1)}, f32[32,64]{1,0:T(8,128)S(1)}, u32[]{:S(2)}, u32[]{:S(2)}) collective-permute-start(f32[32,64]{1,0:T(8,128)S(1)} %add.28.refs_4_), channel_id=1, source_target_pairs={{0,2},{1,3},{2,0},{3,1},{4,6},{5,7},{6,4},{7,5},{8,10},{9,11},{10,... | collective-permute-start | bytes 24584 | tf_op jit(solution)/shard_map/ppermute | solution.py:481
  75.5 26.2 %collective-permute-start.17 = (bf16[16,2048]{1,0:T(8,128)(2,1)}, bf16[16,2048]{1,0:T(8,128)(2,1)S(1)}, u32[]{:S(2)}, u32[]{:S(2)}) collective-permute-start(bf16[16,2048]{1,0:T(8,128)(2,1)} %get-tuple-element.70), channel_id=1, source_target_pairs={{0,1},{1,0},{2,3},{3,2},{4,5},{5,4},{6,7},{7,6},{8,9},{9,8},{10,11... | collective-permute-start | bytes 196616 | tf_op jit(solution)/shard_map/ppermute | solution.py:481
  76.5 0.6 copy-start.20
  76.5 8.0 %collective-permute-start.12 = (f32[32,64]{1,0:T(8,128)S(1)}, f32[32,64]{1,0:T(8,128)S(1)}, u32[]{:S(2)}, u32[]{:S(2)}) collective-permute-start(f32[32,64]{1,0:T(8,128)S(1)} %add.29.refs_5_), channel_id=1, source_target_pairs={{0,4},{1,5},{2,6},{3,7},{4,0},{5,1},{6,2},{7,3},{8,12},{9,13},{10,... | collective-permute-start | bytes 24584 | tf_op jit(solution)/shard_map/ppermute | solution.py:481
  84.0 8.7 %copy-start.17 = (s32[32]{0:T(128)S(1)}, s32[32]{0:T(128)}, u32[]{:S(2)}) copy-start(s32[32]{0:T(128)} %param.13) | copy-start | bytes 388
  84.0 17.7 %collective-permute-start.16 = (bf16[16,2048]{1,0:T(8,128)(2,1)}, bf16[16,2048]{1,0:T(8,128)(2,1)S(1)}, u32[]{:S(2)}, u32[]{:S(2)}) collective-permute-start(bf16[16,2048]{1,0:T(8,128)(2,1)} %get-tuple-element.69), channel_id=1, source_target_pairs={{0,1},{1,0},{2,3},{3,2},{4,5},{5,4},{6,7},{7,6},{8,9},{9,8},{10,11... | collective-permute-start | bytes 196616 | tf_op jit(solution)/shard_map/ppermute | solution.py:481
  85.2 0.6 copy-start.21
  85.2 6.8 %collective-permute-start.13 = (f32[32,64]{1,0:T(8,128)S(1)}, f32[32,64]{1,0:T(8,128)S(1)}, u32[]{:S(2)}, u32[]{:S(2)}) collective-permute-start(f32[32,64]{1,0:T(8,128)S(1)} %add.30.refs_3_), channel_id=1, source_target_pairs={{0,8},{1,9},{2,10},{3,11},{4,12},{5,13},{6,14},{7,15},{8,0},{9,1},... | collective-permute-start | bytes 24584 | tf_op jit(solution)/shard_map/ppermute | solution.py:481
  85.8 16.0 %copy-start.7 = (f32[16,2048]{1,0:T(8,128)S(1)}, f32[16,2048]{1,0:T(8,128)}, u32[]{:S(2)}) copy-start(f32[16,2048]{1,0:T(8,128)} %get-tuple-element.66.refs_4_) | copy-start | bytes 393220
  85.8 16.0 %copy-start.8 = (f32[16,2048]{1,0:T(8,128)S(1)}, f32[16,2048]{1,0:T(8,128)}, u32[]{:S(2)}) copy-start(f32[16,2048]{1,0:T(8,128)} %get-tuple-element.65.refs_3_) | copy-start | bytes 393220
  85.8 23.1 %copy-start.6 = (bf16[32,1792]{1,0:T(8,128)(2,1)S(1)}, bf16[32,1792]{1,0:T(8,128)(2,1)}, u32[]{:S(2)}) copy-start(bf16[32,1792]{1,0:T(8,128)(2,1)} %get-tuple-element.56.refs_1_.right_ref) | copy-start | bytes 344068
  85.8 23.1 %copy-start.11 = (bf16[32,2048]{1,0:T(8,128)(2,1)S(1)}, bf16[32,2048]{1,0:T(8,128)(2,1)}, u32[]{:S(2)}) copy-start(bf16[32,2048]{1,0:T(8,128)(2,1)} %get-tuple-element.74.left_ref) | copy-start | bytes 393220
  91.8 9.9 %copy-start.9 = (f32[16,2048]{1,0:T(8,128)S(1)}, f32[16,2048]{1,0:T(8,128)}, u32[]{:S(2)}) copy-start(f32[16,2048]{1,0:T(8,128)} %get-tuple-element.64.refs_2_) | copy-start | bytes 393220
  91.8 9.9 %collective-permute-start.15 = (bf16[16,2048]{1,0:T(8,128)(2,1)}, bf16[16,2048]{1,0:T(8,128)(2,1)S(1)}, u32[]{:S(2)}, u32[]{:S(2)}) collective-permute-start(bf16[16,2048]{1,0:T(8,128)(2,1)} %get-tuple-element.68), channel_id=1, source_target_pairs={{0,1},{1,0},{2,3},{3,2},{4,5},{5,4},{6,7},{7,6},{8,9},{9,8},{10,11... | collective-permute-start | bytes 196616 | tf_op jit(solution)/shard_map/ppermute | solution.py:481
  93.6 0.6 copy-start.14
  94.2 6.4 %copy-start.15 = (bf16[16,512]{1,0:T(8,128)(2,1)S(1)}, bf16[16,512]{1,0:T(8,128)(2,1)}, u32[]{:S(2)}) copy-start(bf16[16,512]{1,0:T(8,128)(2,1)} %copy-done.14) | copy-start | bytes 49156
  100.2 1.6 %collective-permute-start.14 = (bf16[16,2048]{1,0:T(8,128)(2,1)}, bf16[16,2048]{1,0:T(8,128)(2,1)S(1)}, u32[]{:S(2)}, u32[]{:S(2)}) collective-permute-start(bf16[16,2048]{1,0:T(8,128)(2,1)} %get-tuple-element.67), channel_id=1, source_target_pairs={{0,1},{1,0},{2,3},{3,2},{4,5},{5,4},{6,7},{7,6},{8,9},{9,8},{10,11... | collective-permute-start | bytes 196616 | tf_op jit(solution)/shard_map/ppermute | solution.py:481
  100.6 1.2 collective-permute-start.18
  101.8 0.9 copy-start.10
  103.8 15.0 %all-to-all-start = ((bf16[8,16,1152]{2,1,0:T(8,128)(2,1)}), bf16[8,16,1152]{2,1,0:T(8,128)(2,1)S(1)}, u32[]{:S(2)}, u32[]{:S(2)}) async-start(bf16[8,16,1152]{2,1,0:T(8,128)(2,1)} %merge.1), calls=%async_computation | async-start | bytes 589824 | tf_op jit(solution)/shard_map/all_to_all | solution.py:475

commit v7 on v6

--- a/solution.py
+++ b/solution.py
@@ -52,14 +52,14 @@
 
 
 VMEM = pl.BlockSpec(memory_space=pltpu.VMEM)
-SMEM = pl.BlockSpec(memory_space=pltpu.SMEM)
 ANY = pl.BlockSpec(memory_space=pl.ANY)
 CUTS = 4
 COPIES = 4
 SLOTS = 6
-
-
-def store_call(kernel, store, fetches, operands, out_shapes, flops, name, smem=0, after=()):
+STORE_GRANT = 10 << 20
+
+
+def store_call(kernel, store, fetches, operands, out_shapes, flops, name, after=()):
     new = isinstance(store, jax.ShapeDtypeStruct)
     depth = store.shape[0] // SLOTS
     part = depth // COPIES
@@ -95,15 +95,12 @@
     moved = 2 * depth * store.shape[1] * len(fetches)
     return pl.pallas_call(
         body,
-        in_specs=([] if new else [VMEM])
-        + [SMEM] * smem
-        + [VMEM] * (n_in - smem)
-        + [ANY] * (n_hbm + len(after)),
+        in_specs=[VMEM] * (n_in + (not new)) + [ANY] * (n_hbm + len(after)),
         out_specs=[VMEM] * (1 + n_out),
         out_shape=[pltpu.VMEM(store.shape, store.dtype), *out_shapes],
         input_output_aliases={} if new else {0: 0},
         scratch_shapes=[pltpu.SemaphoreType.DMA((COPIES * len(fetches),))] if fetches else [],
-        compiler_params=pltpu.CompilerParams(vmem_limit_bytes=13 << 20),
+        compiler_params=pltpu.CompilerParams(vmem_limit_bytes=STORE_GRANT),
         cost_estimate=pl.CostEstimate(flops=flops, bytes_accessed=moved, transcendentals=0),
         name=name,
     )(
@@ -124,7 +121,7 @@
         stack_kernel,
         in_specs=[VMEM] * len(blocks) + [ANY] * len(after),
         out_shape=jax.ShapeDtypeStruct((rows, blocks[0].shape[1]), blocks[0].dtype),
-        compiler_params=pltpu.CompilerParams(vmem_limit_bytes=6 << 20),
+        compiler_params=pltpu.CompilerParams(vmem_limit_bytes=4 << 20),
         name="stacked",
     )(*blocks, *after)
 
@@ -163,9 +160,9 @@
     return tenant_mask(tenants.astype(jnp.int32), pick.shape[0])
 
 
-def low_kernel(count, aligned, own_ref, down_ref, tenants_ref, *refs):
+def low_kernel(count, aligned, down_ref, tenants_ref, *refs):
     x, (span_out, low_ref) = refs[:-2], refs[-2:]
-    own = own_ref[0]
+    own = lax.axis_index("tp")
     if aligned:
         width = down_ref.shape[0]
         at = pl.ds(pl.multiple_of(own * width, width), width)
@@ -179,29 +176,31 @@
     low_ref[...] = picked(pick_given(own, rows, count), low)
 
 
-def low_part(own, down, tenants, x, count):
+def low_part(down, tenants, x, count):
     rows, span = sum(block.shape[0] for block in x), down.shape[0]
     aligned = span % 128 == 0
     if not aligned:
         x = [
             lax.dynamic_slice(
-                block, (0, own[0] * span), (block.shape[0], span), allow_negative_indices=False
+                block,
+                (0, lax.axis_index("tp") * span),
+                (block.shape[0], span),
+                allow_negative_indices=False,
             )
             for block in x
         ]
     return pl.pallas_call(
         lambda *refs: low_kernel(count, aligned, *refs),
-        in_specs=[SMEM] + [VMEM] * (2 + len(x)),
         out_shape=[
             jax.ShapeDtypeStruct((rows, span), x[0].dtype),
             jax.ShapeDtypeStruct((rows, ADAPTER_RANK), jnp.float32),
         ],
-        compiler_params=pltpu.CompilerParams(vmem_limit_bytes=6 << 20),
+        compiler_params=pltpu.CompilerParams(vmem_limit_bytes=4 << 20),
         cost_estimate=pl.CostEstimate(
             flops=2 * rows * down.size, bytes_accessed=2 * down.size, transcendentals=0
         ),
         name="low_part",
-    )(own, down, tenants, *x)
+    )(down, tenants, *x)
 
 
 def forward_kernel(cut, slots, blocks, first, slot, *refs):
@@ -238,12 +237,13 @@
 
 
 def activation_kernel(
-    count, maps_slot, slot, own_ref, gate_ref, up_ref, hidden_ref, low_ref, tenants_ref,
+    count, maps_slot, slot, gate_ref, up_ref, hidden_ref, low_ref, tenants_ref,
     dgate_ref, dup_ref, part_ref, spread_ref,
 ):
     rows = gate_ref.shape[0]
     maps = slot(maps_slot)
-    pick = pick_held(own_ref[0], rows, count)
+    own = lax.axis_index("tp")
+    pick = pick_held(own, rows, count)
     mask = held_mask(pick, tenants_ref[...])
     spread = spread_rows(picked(pick, low_ref[...]), mask)
     spread_ref[...] = spread
@@ -256,17 +256,17 @@
     dgate_ref[...] = dgate
     dup_ref[...] = (hidden * gate * s).astype(jnp.bfloat16)
     part = select_block(contracted_columns(dgate, maps), mask)
-    part_ref[...] = picked(pick_given(own_ref[0], rows, count), part)
-
-
-def activation(own, maps_slot, store, sums, hidden, low, tenants, count, fetches):
+    part_ref[...] = picked(pick_given(own, rows, count), part)
+
+
+def activation(maps_slot, store, sums, hidden, low, tenants, count, fetches):
     rows, width = sums[0].shape
     value = jax.ShapeDtypeStruct((rows, width), jnp.bfloat16)
     return store_call(
         lambda *refs: activation_kernel(count, maps_slot, *refs),
         store,
         fetches,
-        [own, *sums, hidden, low, tenants],
+        [*sums, hidden, low, tenants],
         [
             value,
             value,
@@ -275,13 +275,12 @@
         ],
         4 * rows * SPREAD * width,
         "activation",
-        smem=1,
-    )
-
-
-def adapter_kernel(count, own_ref, low_ref, tenants_ref, down_ref, own_out, other_out, spread_ref):
+    )
+
+
+def adapter_kernel(count, low_ref, tenants_ref, down_ref, own_out, other_out, spread_ref):
     half = own_out.shape[0]
-    pick = pick_held(own_ref[0], 2 * half, count)
+    pick = pick_held(lax.axis_index("tp"), 2 * half, count)
     spread = spread_rows(picked(pick, low_ref[...]), held_mask(pick, tenants_ref[...]))
     spread_ref[...] = spread
     part = (adapter_scale * contracted_columns(spread, down_ref[...])).astype(jnp.bfloat16)
@@ -289,19 +288,18 @@
     other_out[...] = part[half:]
 
 
-def adapter_part(own, low, tenants, down, count):
+def adapter_part(low, tenants, down, count):
     rows, span = low.shape[0], down.shape[0]
     half = jax.ShapeDtypeStruct((rows // 2, span), jnp.bfloat16)
     return pl.pallas_call(
         lambda *refs: adapter_kernel(count, *refs),
-        in_specs=[SMEM] + [VMEM] * 3,
         out_shape=[half, half, jax.ShapeDtypeStruct((rows, SPREAD), jnp.bfloat16)],
-        compiler_params=pltpu.CompilerParams(vmem_limit_bytes=6 << 20),
+        compiler_params=pltpu.CompilerParams(vmem_limit_bytes=4 << 20),
         cost_estimate=pl.CostEstimate(
             flops=2 * rows * down.size, bytes_accessed=2 * down.size, transcendentals=0
         ),
         name="adapter_part",
-    )(own, low, tenants, down)
+    )(low, tenants, down)
 
 
 def backward_kernel(slots, slot, dgate_ref, dup_ref, own_out, other_out):
@@ -333,7 +331,8 @@
 PARTS = 8
 
 
-def merge_kernel(count, own_ref, *refs):
+def merge_kernel(count, *refs):
+    device = lax.axis_index("tp")
     own, came = refs[:CUTS], refs[CUTS : 2 * CUTS]
     adapter_own, adapter_came, out_ref, sums, tiles = refs[2 * CUTS :]
     chips, tile, lanes = out_ref.shape
@@ -352,7 +351,7 @@
     put(
         blocks,
         jnp.where(
-            own_ref[0] % 2 == 0,
+            device % 2 == 0,
             jnp.concatenate([mine, other], axis=1),
             jnp.concatenate([other, mine], axis=1),
         ),
@@ -368,14 +367,14 @@
             if blocks + part < sums.shape[0]:
                 tiles[per_part, to, :] = sums[blocks + part, of_token, :]
     for position in range(chips):
-        chip = block_owner(own_ref[0], position, count) // 2
+        chip = block_owner(device, position, count) // 2
         for k in range(lanes // 128):
             out_ref[chip, :, k * 128 : (k + 1) * 128] = tiles[
                 k, position * tile : (position + 1) * tile, :
             ].astype(jnp.bfloat16)
 
 
-def merge(device, own, came, adapter_own, adapter_came, own_rows):
+def merge(own, came, adapter_own, adapter_came, own_rows):
     half, depth = own[0].shape
     width = CUTS * depth
     pair = 2 * adapter_own.shape[1]
@@ -383,7 +382,6 @@
     chips, tile = half // own_rows, own_rows * PARTS
     return pl.pallas_call(
         lambda *refs: merge_kernel(2 * chips, *refs),
-        in_specs=[SMEM] + [VMEM] * (2 * CUTS + 2),
         out_shape=jax.ShapeDtypeStruct((chips, tile, lanes), jnp.bfloat16),
         scratch_shapes=[
             pltpu.VMEM(((width + pair) // 128, half, 128), jnp.float32),
@@ -391,7 +389,7 @@
         ],
         compiler_params=pltpu.CompilerParams(vmem_limit_bytes=40 << 20),
         name="merge",
-    )(device, *own, *came, adapter_own, adapter_came)
+    )(*own, *came, adapter_own, adapter_came)
 
 
 def final_kernel(pair, came_ref, out_ref, total, adapter):
@@ -446,7 +444,7 @@
 def outer(left, right, name):
     rows, height = left.shape
     width = right.shape[1]
-    block = block_of(height, 256)
+    block = block_of(height, 512)
     if block % 128:
         block = height
     return pl.pallas_call(
@@ -477,6 +475,19 @@
     )
 
 
+def add_kernel(left_ref, right_ref, out_ref):
+    out_ref[...] = left_ref[...] + right_ref[...]
+
+
+def plus(left, right):
+    return pl.pallas_call(
+        add_kernel,
+        out_shape=jax.ShapeDtypeStruct(left.shape, left.dtype),
+        compiler_params=pltpu.CompilerParams(vmem_limit_bytes=2 << 20),
+        name="plus",
+    )(left, right)
+
+
 def swapped(block, hop):
     return lax.ppermute(block, "tp", [(i, i ^ hop) for i in range(lax.axis_size("tp"))])
 
@@ -491,7 +502,6 @@
     token_tenant_index,
 ):
     count = lax.axis_size("tp")
-    own = lax.axis_index("tp").astype(jnp.int32).reshape(1)
     own_rows, width = normed_layer_input.shape
     rows = own_rows * count
     hops = [1 << bit for bit in range(count.bit_length() - 1)]
@@ -503,21 +513,26 @@
     def mark(slot, token_ref):
         token_ref[...] = jnp.zeros_like(token_ref)
 
-    token = jax.ShapeDtypeStruct((8, 128), jnp.float32)
+    mark_shape = jax.ShapeDtypeStruct((8, 128), jnp.float32)
     store = jax.ShapeDtypeStruct(
         (SLOTS * width // CUTS, gate_weight.shape[1]), gate_weight.dtype
     )
     far, near = hops[-1], hops[-2]
     came = [swapped(normed_layer_input, hop) for hop in (near, far, near | far)]
-    store, token = store_call(mark, store, pair(0, 0, 1), [], [token], 0, "fetch", after=[own])
+    store, token = store_call(mark, store, pair(0, 0, 1), [], [mark_shape], 0, "fetch")
     block = stacked([normed_layer_input, *came], [token])
     for hop in reversed(hops[2:-2]):
         block = stacked([block, swapped(block, hop)])
     other = swapped(block, hops[1])
     x = [block, other, swapped(block, 1), swapped(other, 1)]
-    store, token = store_call(mark, store, pair(1, 2, 3), [], [token], 0, "fetch", after=[block])
-
-    input_span, low = low_part(own, adapter_down_maps, tenants, x, count)
+    store, token = store_call(
+        mark, store, [(gate_weight, 1, 2)], [], [mark_shape], 0, "fetch", after=[block]
+    )
+    store, token = store_call(
+        mark, store, [(up_weight, 1, 3)], [], [mark_shape], 0, "fetch", after=[other]
+    )
+
+    input_span, low = low_part(adapter_down_maps, tenants, x, count)
     sums = []
     slots = {0: (0, 1), 1: (2, 3), 2: (4, 5), 3: (0, 1)}
     fetches = {
@@ -527,16 +542,16 @@
     for cut in range(CUTS):
         after = [low]
         if step < len(hops):
-            low = low + swapped(low, hops[step])
+            low = plus(low, swapped(low, hops[step]))
             step += 1
         store, sums = forward(cut, slots[cut], x, store, sums, fetches[cut], after)
     for hop in hops[step:]:
-        low = low + swapped(low, hop)
+        low = plus(low, swapped(low, hop))
     store, dgate, dup, low_grad, input_spread = activation(
-        own, 2, store, sums, hidden_unit_gradient, low, tenants, count, []
-    )
-
-    low_grad = low_grad + swapped(low_grad, hops[0])
+        2, store, sums, hidden_unit_gradient, low, tenants, count, []
+    )
+
+    low_grad = plus(low_grad, swapped(low_grad, hops[0]))
     step = 1
     parts, arrived = {}, {}
     slots = {3: (0, 1), 2: (4, 5), 1: (3, 2), 0: (0, 1)}
@@ -545,21 +560,20 @@
         if cut > 0:
             after = [low_grad]
             if step < len(hops):
-                low_grad = low_grad + swapped(low_grad, hops[step])
+                low_grad = plus(low_grad, swapped(low_grad, hops[step]))
                 step += 1
         store, own_part, other_part = backward(slots[cut], dgate, dup, store, fetches[cut], after)
         if cut == 1:
             for hop in hops[step:]:
-                low_grad = low_grad + swapped(low_grad, hop)
+                low_grad = plus(low_grad, swapped(low_grad, hop))
             adapter_own, adapter_other, grad_spread = adapter_part(
-                own, low_grad, tenants, adapter_down_maps, count
+                low_grad, tenants, adapter_down_maps, count
             )
             adapter_came = swapped(adapter_other, 1)
             after = [adapter_other]
         parts[cut] = own_part
         arrived[cut] = swapped(other_part, 1)
     merged = merge(
-        own,
         [parts[cut] for cut in range(CUTS)],
         [arrived[cut] for cut in range(CUTS)],
         adapter_own,

time: 120 us -> 94.7 us (0.79)
  Pallas kernels: 78.8 us -> 62.4 us
  other arithmetic: 6.39 us -> 0 us
  local copies, waits for them, and re-layouts: 3.34 us -> 0.03 us
  waiting for transfers between devices: 7.89 us -> 9.82 us
    pallas_call x14 -> x23, Pallas kernels: 70.3 us -> 55.1 us  [the longest x12 52.2 us: store_call(): pl.pallas_call(body, in_specs=[VMEM] * (n_in + (not new)) + [ANY] * (n_hb...]
    add x8 -> x0, other arithmetic: 6.39 us -> none  [the longest x4 3.5 us: local(): low = low + swapped(low, hops[step])]
    unnamed x50 -> x10, local copies, waits for them, and re-layouts: 3.34 us -> 0.03 us
    pallas_call x2, Pallas kernels: 7.76 us -> 6.56 us  [outer(): pl.pallas_call(outer_kernel, grid=(height // block,), in_specs=[pl.BlockS...]
  transfers between devices with their start and end apart: 20 -> 20, of which waited for: 4 -> 6; matrix products, arithmetic and copies ran while one was open for 2% -> 0% of each run, Pallas kernels for 59% -> 59%
where the time goes in v7:
time: 94.7 us; the launch traced here: 94.5 us
  Pallas kernels  62.4 us (66%)
  starting transfers between devices  21.3 us (22%)
  waiting for transfers between devices  9.82 us (10%)
    pallas_call x12, Pallas kernels, store_call(): pl.pallas_call(body, in_specs=[VMEM] * (n_in + (not new)) + [ANY] * (n_hb...  52.2 us
    ppermute x19, starting transfers between devices, swapped(): lax.ppermute(block, 'tp', [(i, i ^ hop) for i in range(lax.axis_size('tp'...  16.6 us
    pallas_call x2, Pallas kernels, outer(): pl.pallas_call(outer_kernel, grid=(height // block,), in_specs=[pl.BlockS...  6.56 us
    ppermute x19, waiting for transfers between devices, swapped(): lax.ppermute(block, 'tp', [(i, i ^ hop) for i in range(lax.axis_size('tp'...  6.44 us
    all_to_all x1, starting transfers between devices, between_same_cores(): lax.all_to_all(blocks, 'tp', split_axis=0, concat_axis=0, tiled=True, axi...  4.76 us
    all_to_all x1, waiting for transfers between devices, between_same_cores(): lax.all_to_all(blocks, 'tp', split_axis=0, concat_axis=0, tiled=True, axi...  3.38 us
  transfers between devices with their start and end apart: 20, of which 6 were waited for; matrix products, arithmetic and copies ran while one was open for 0% of the time, Pallas kernels for 59%

profile of v7, /device:TPU:0, one launch (start us, length us, event | category | flops | bytes accessed | tf_op | source)
XLA Modules:
  0.0 94.5 jit_solution(1199910517148433703)
XLA Ops:
  0.6 3.1 %collective-permute-start = (bf16[2,8192]{1,0:T(2,128)(2,1)}, bf16[2,8192]{1,0:T(2,128)(2,1)S(1)}, u32[]{:S(2)}, u32[]{:S(2)}) collective-permute-start(bf16[2,8192]{1,0:T(2,128)(2,1)} %refs_0_.4), channel_id=1, source_target_pairs={{0,4},{1,5},{2,6},{3,7},{4,0},{5,1},{6,2},{7,3},{8,12},{9,13},{10,... | collective-permute-start | bytes 98312 | tf_op jit(solution)/shard_map/ppermute | solution.py:492
  3.7 2.6 %collective-permute-start.1 = (bf16[2,8192]{1,0:T(2,128)(2,1)}, bf16[2,8192]{1,0:T(2,128)(2,1)S(1)}, u32[]{:S(2)}, u32[]{:S(2)}) collective-permute-start(bf16[2,8192]{1,0:T(2,128)(2,1)} %refs_0_.4), channel_id=1, source_target_pairs={{0,8},{1,9},{2,10},{3,11},{4,12},{5,13},{6,14},{7,15},{8,0},{9,1},... | collective-permute-start | bytes 98312 | tf_op jit(solution)/shard_map/ppermute | solution.py:492
  6.3 0.0 collective-permute-start.2
  6.3 5.3 %fetch.3 = (bf16[12288,1792]{1,0:T(8,128)(2,1)S(1)}, f32[8,128]{1,0:T(8,128)S(1)}) custom-call(bf16[8192,1792]{1,0:T(8,128)(2,1)} %refs_3_.5, bf16[8192,1792]{1,0:T(8,128)(2,1)} %refs_4_.1), custom_call_target="tpu_custom_call" | custom-call | bytes 14680064 | tf_op jit(solution)/shard_map/fetch/pallas_call | solution.py:96
  11.6 0.0 collective-permute-done.refs_1_
  11.6 0.0 collective-permute-done.1.refs_2_
  11.7 0.6 collective-permute-done.2.refs_3_
  12.2 0.1 stacked.1.refs_2_.refs_1_
  12.3 1.6 %collective-permute-start.3 = (bf16[8,8192]{1,0:T(8,128)(2,1)S(1)}, bf16[8,8192]{1,0:T(8,128)(2,1)S(1)}, u32[]{:S(2)}, u32[]{:S(2)}) collective-permute-start(bf16[8,8192]{1,0:T(8,128)(2,1)S(1)} %stacked.1.refs_2_.refs_1_), channel_id=1, source_target_pairs={{0,2},{1,3},{2,0},{3,1},{4,6},{5,7},{6,4},{7,5},{8,10},{9,11},{10,... | collective-permute-start | bytes 393224 | tf_op jit(solution)/shard_map/ppermute | solution.py:492
  13.9 0.0 collective-permute-start.4
  13.9 3.4 %collective-permute-done.3.refs_2_.refs_3_ = bf16[8,8192]{1,0:T(8,128)(2,1)S(1)} collective-permute-done((bf16[8,8192]{1,0:T(8,128)(2,1)S(1)}, bf16[8,8192]{1,0:T(8,128)(2,1)S(1)}, u32[]{:S(2)}, u32[]{:S(2)}) %collective-permute-start.3) | collective-permute-done | bytes 131104 | tf_op jit(solution)/shard_map/ppermute | solution.py:492
  17.4 0.0 collective-permute-start.5
  17.4 3.8 %fetch.4 = (bf16[12288,1792]{1,0:T(8,128)(2,1)S(1)}, f32[8,128]{1,0:T(8,128)}) custom-call(bf16[12288,1792]{1,0:T(8,128)(2,1)S(1)} %get-tuple-element.40.refs_0_, bf16[8192,1792]{1,0:T(8,128)(2,1)} %refs_3_.5, bf16[8,8192]{1,0:T(8,128)(2,1)S(1)} %stacked.1.refs_2_.refs_1_), custom_call_target="tpu_custom_call", output_to_operand_aliasing={{0}: (0, {})} | custom-call | bytes 7340032 | tf_op jit(solution)/shard_map/fetch/pallas_call | solution.py:96
  21.2 0.0 copy-start
  21.2 0.0 copy-start.4
  21.2 3.9 %fetch.5 = (bf16[12288,1792]{1,0:T(8,128)(2,1)S(1)}, f32[8,128]{1,0:T(8,128)}) custom-call(bf16[12288,1792]{1,0:T(8,128)(2,1)S(1)} %get-tuple-element.42.refs_0_, bf16[8192,1792]{1,0:T(8,128)(2,1)} %refs_4_.1, bf16[8,8192]{1,0:T(8,128)(2,1)S(1)} %collective-permute-done.3.refs_2_.refs_3_), custom_call_target="tpu_custom_call", output_to_operand_aliasing={{0}: (0, {})} | custom-call | bytes 7340032 | tf_op jit(solution)/shard_map/fetch/pallas_call | solution.py:96
  25.1 0.0 collective-permute-done.4.refs_4_.refs_3_
  25.1 0.0 collective-permute-done.5.refs_5_.refs_4_
  25.2 0.7 low_part.1
  25.8 0.5 collective-permute-start.6
  26.4 5.3 %forward.4 = (bf16[12288,1792]{1,0:T(8,128)(2,1)S(1)}, f32[32,1792]{1,0:T(8,128)S(1)}, f32[32,1792]{1,0:T(8,128)S(1)}) custom-call(bf16[12288,1792]{1,0:T(8,128)(2,1)S(1)} %get-tuple-element.43.refs_0_, bf16[8,8192]{1,0:T(8,128)(2,1)S(1)} %stacked.1.refs_2_.refs_1_, ...), custom_call_target="tpu_custom_call", output_to_operand_aliasing={{0}: (0, {})} | custom-call | flops 469762048 | bytes 14680064 | tf_op jit(solution)/shard_map/forward/pallas_call | solution.py:96
  31.7 0.0 collective-permute-done.6.right_ref
  31.7 1.6 %collective-permute-start.7 = (f32[32,64]{1,0:T(8,128)S(1)}, f32[32,64]{1,0:T(8,128)S(1)}, u32[]{:S(2)}, u32[]{:S(2)}) collective-permute-start(f32[32,64]{1,0:T(8,128)S(1)} %plus.8.refs_9_.left_ref), channel_id=1, source_target_pairs={{0,2},{1,3},{2,0},{3,1},{4,6},{5,7},{6,4},{7,5},{8,10},{9,11},{10,... | collective-permute-start | bytes 24584 | tf_op jit(solution)/shard_map/ppermute | solution.py:492
  33.3 5.3 %forward.5 = (bf16[12288,1792]{1,0:T(8,128)(2,1)S(1)}, f32[32,1792]{1,0:T(8,128)S(1)}, f32[32,1792]{1,0:T(8,128)S(1)}) custom-call(bf16[12288,1792]{1,0:T(8,128)(2,1)S(1)} %get-tuple-element.45.refs_0_, bf16[8,8192]{1,0:T(8,128)(2,1)S(1)} %stacked.1.refs_2_.refs_1_, ...), custom_call_target="tpu_custom_call", output_to_operand_aliasing={{0}: (0, {})} | custom-call | flops 469762048 | bytes 14680064 | tf_op jit(solution)/shard_map/forward/pallas_call | solution.py:96
  38.6 0.0 collective-permute-done.7.right_ref
  38.7 0.4 collective-permute-start.8
  39.1 3.2 %forward.6 = (bf16[12288,1792]{1,0:T(8,128)(2,1)S(1)}, f32[32,1792]{1,0:T(8,128)S(1)}, f32[32,1792]{1,0:T(8,128)S(1)}) custom-call(bf16[12288,1792]{1,0:T(8,128)(2,1)S(1)} %get-tuple-element.48.refs_0_, bf16[8,8192]{1,0:T(8,128)(2,1)S(1)} %stacked.1.refs_2_.refs_1_, ...), custom_call_target="tpu_custom_call", output_to_operand_aliasing={{0}: (0, {})} | custom-call | flops 469762048 | bytes 7340032 | tf_op jit(solution)/shard_map/forward/pallas_call | solution.py:96
  42.3 0.0 copy-start.2
  42.3 0.2 collective-permute-done.8.right_ref
  42.5 3.4 %collective-permute-start.9 = (f32[32,64]{1,0:T(8,128)S(1)}, f32[32,64]{1,0:T(8,128)S(1)}, u32[]{:S(2)}, u32[]{:S(2)}) collective-permute-start(f32[32,64]{1,0:T(8,128)S(1)} %plus.10.refs_8_.left_ref), channel_id=1, source_target_pairs={{0,8},{1,9},{2,10},{3,11},{4,12},{5,13},{6,14},{7,15},{8,0},{9,1},... | collective-permute-start | bytes 24584 | tf_op jit(solution)/shard_map/ppermute | solution.py:492
  45.8 3.2 %forward.7 = (bf16[12288,1792]{1,0:T(8,128)(2,1)S(1)}, f32[32,1792]{1,0:T(8,128)S(1)}, f32[32,1792]{1,0:T(8,128)S(1)}) custom-call(bf16[12288,1792]{1,0:T(8,128)(2,1)S(1)} %get-tuple-element.51.refs_0_, bf16[8,8192]{1,0:T(8,128)(2,1)S(1)} %stacked.1.refs_2_.refs_1_, ...), custom_call_target="tpu_custom_call", output_to_operand_aliasing={{0}: (0, {})} | custom-call | flops 469762048 | bytes 7340032 | tf_op jit(solution)/shard_map/forward/pallas_call | solution.py:96
  49.0 0.0 collective-permute-done.9.right_ref
  49.1 3.8 %activation.1 = (bf16[12288,1792]{1,0:T(8,128)(2,1)S(1)}, bf16[32,1792]{1,0:T(8,128)(2,1)S(1)}, bf16[32,1792]{1,0:T(8,128)(2,1)S(1)}, f32[32,64]{1,0:T(8,128)S(1)}, bf16[32,2048]{1,0:T(8,128)(2,1)S(1)}) custom-call(bf16[12288,1792]{1,0:T(8,128)(2,1)S(1)} %get-tuple-element.54.refs_0_, ...), custom_call_target="tpu_custom_call", output_to_operand_aliasing={{0}: (0, {})} | custom-call | flops 469762048 | tf_op jit(solution)/shard_map/activation/pallas_call | solution.py:96
  52.9 0.0 collective-permute-start.10
  52.9 1.2 %collective-permute-done.10.right_ref = f32[32,64]{1,0:T(8,128)S(1)} collective-permute-done((f32[32,64]{1,0:T(8,128)S(1)}, f32[32,64]{1,0:T(8,128)S(1)}, u32[]{:S(2)}, u32[]{:S(2)}) %collective-permute-start.10) | collective-permute-done | bytes 8224 | tf_op jit(solution)/shard_map/ppermute | solution.py:492
  54.1 0.5 collective-permute-start.11
  54.6 4.4 %backward.4 = (bf16[12288,1792]{1,0:T(8,128)(2,1)S(1)}, f32[16,2048]{1,0:T(8,128)S(1)}, bf16[16,2048]{1,0:T(8,128)(2,1)S(1)}) custom-call(bf16[12288,1792]{1,0:T(8,128)(2,1)S(1)} %get-tuple-element.57.refs_0_, bf16[32,1792]{1,0:T(8,128)(2,1)S(1)} %get-tuple-element.58.refs_1_.right_ref, ...), custom_call_target="tpu_custom_call", output_to_operand_aliasing={{0}: (0, {})} | custom-call | flops 469762048 | bytes 7340032 | tf_op jit(solution)/shard_map/backward/pallas_call | solution.py:96
  59.0 0.1 collective-permute-start.17
  59.1 0.0 collective-permute-done.11.right_ref
  59.1 0.2 plus.13.refs_5_.left_ref
  59.3 0.5 collective-permute-start.12
  59.8 5.3 %backward.5 = (bf16[12288,1792]{1,0:T(8,128)(2,1)S(1)}, f32[16,2048]{1,0:T(8,128)S(1)}, bf16[16,2048]{1,0:T(8,128)(2,1)S(1)}) custom-call(bf16[12288,1792]{1,0:T(8,128)(2,1)S(1)} %get-tuple-element.61.refs_0_, bf16[32,1792]{1,0:T(8,128)(2,1)S(1)} %get-tuple-element.58.refs_1_.right_ref, ...), custom_call_target="tpu_custom_call", output_to_operand_aliasing={{0}: (0, {})} | custom-call | flops 469762048 | bytes 14680064 | tf_op jit(solution)/shard_map/backward/pallas_call | solution.py:96
  65.1 0.0 copy-start.1
  65.1 0.1 collective-permute-start.16
  65.2 0.0 collective-permute-done.12.right_ref
  65.2 1.5 %collective-permute-start.13 = (f32[32,64]{1,0:T(8,128)S(1)}, f32[32,64]{1,0:T(8,128)S(1)}, u32[]{:S(2)}, u32[]{:S(2)}) collective-permute-start(f32[32,64]{1,0:T(8,128)S(1)} %plus.14.refs_3_.left_ref), channel_id=1, source_target_pairs={{0,8},{1,9},{2,10},{3,11},{4,12},{5,13},{6,14},{7,15},{8,0},{9,1},... | collective-permute-start | bytes 24584 | tf_op jit(solution)/shard_map/ppermute | solution.py:492
  66.7 4.3 %backward.6 = (bf16[12288,1792]{1,0:T(8,128)(2,1)S(1)}, f32[16,2048]{1,0:T(8,128)S(1)}, bf16[16,2048]{1,0:T(8,128)(2,1)S(1)}) custom-call(bf16[12288,1792]{1,0:T(8,128)(2,1)S(1)} %get-tuple-element.62.refs_0_, bf16[32,1792]{1,0:T(8,128)(2,1)S(1)} %get-tuple-element.58.refs_1_.right_ref, ...), custom_call_target="tpu_custom_call", output_to_operand_aliasing={{0}: (0, {})} | custom-call | flops 469762048 | tf_op jit(solution)/shard_map/backward/pallas_call | solution.py:96
  71.0 0.2 collective-permute-start.15
  71.3 0.0 collective-permute-done.13.right_ref
  71.3 0.9 adapter_part.1
  72.2 4.3 %backward.7 = (bf16[12288,1792]{1,0:T(8,128)(2,1)S(1)}, f32[16,2048]{1,0:T(8,128)S(1)}, bf16[16,2048]{1,0:T(8,128)(2,1)S(1)}) custom-call(bf16[12288,1792]{1,0:T(8,128)(2,1)S(1)} %get-tuple-element.63.refs_0_, bf16[32,1792]{1,0:T(8,128)(2,1)S(1)} %get-tuple-element.58.refs_1_.right_ref, ...), custom_call_target="tpu_custom_call", output_to_operand_aliasing={{0}: (0, {})} | custom-call | flops 469762048 | tf_op jit(solution)/shard_map/backward/pallas_call | solution.py:96
  76.5 0.3 collective-permute-start.14
  76.8 0.2 collective-permute-start.18
  77.0 1.0 %collective-permute-done.18.refs_9_ = bf16[16,512]{1,0:T(8,128)(2,1)S(1)} collective-permute-done((bf16[16,512]{1,0:T(8,128)(2,1)S(1)}, bf16[16,512]{1,0:T(8,128)(2,1)S(1)}, u32[]{:S(2)}, u32[]{:S(2)}) %collective-permute-start.18) | collective-permute-done | bytes 16416 | tf_op jit(solution)/shard_map/ppermute | solution.py:492
  78.0 0.0 collective-permute-done.17.refs_7_
  78.0 0.0 collective-permute-done.16.refs_6_
  78.0 0.0 collective-permute-done.15.refs_5_
  78.0 0.0 collective-permute-done.14.refs_4_
  78.0 1.1 %merge.1 = bf16[8,16,1152]{2,1,0:T(8,128)(2,1)} custom-call(f32[16,2048]{1,0:T(8,128)S(1)} %get-tuple-element.65.refs_0_, f32[16,2048]{1,0:T(8,128)S(1)} %get-tuple-element.66.refs_1_, f32[16,2048]{1,0:T(8,128)S(1)} %get-tuple-element.67.refs_2_, f32[16,2048]{1,0:T(8,128)S(1)} %get-tuple-element.68.refs_3_, ...), custom_call_target="tpu_custom_call" | custom-call | tf_op jit(solution)/shard_map/merge/pallas_call | solution.py:383
  79.1 4.8 %all-to-all-start = ((bf16[8,16,1152]{2,1,0:T(8,128)(2,1)}), bf16[8,16,1152]{2,1,0:T(8,128)(2,1)S(1)}, u32[]{:S(2)}, u32[]{:S(2)}) async-start(bf16[8,16,1152]{2,1,0:T(8,128)(2,1)} %merge.1), calls=%async_computation | async-start | bytes 589824 | tf_op jit(solution)/shard_map/all_to_all | solution.py:473
  83.9 4.5 %up_maps.1 = bf16[2048,1792]{1,0:T(8,128)(2,1)} custom-call(bf16[32,2048]{1,0:T(8,128)(2,1)S(1)} %get-tuple-element.76.left_ref, bf16[32,1792]{1,0:T(8,128)(2,1)S(1)} %get-tuple-element.58.refs_1_.right_ref), custom_call_target="tpu_custom_call" | custom-call | flops 234881024 | bytes 7340032 | tf_op jit(solution)/shard_map/up_maps/pallas_call | solution.py:450
  88.4 2.1 %down_maps.1 = bf16[512,2048]{1,0:T(8,128)(2,1)} custom-call(bf16[32,512]{1,0:T(8,128)(2,1)S(1)} %get-tuple-element.74.left_ref, bf16[32,2048]{1,0:T(8,128)(2,1)S(1)} %get-tuple-element.75.right_ref), custom_call_target="tpu_custom_call" | custom-call | flops 67108864 | bytes 2097152 | tf_op jit(solution)/shard_map/down_maps/pallas_call | solution.py:450
  90.4 3.4 %all-to-all-done.refs_0_ = bf16[8,16,1152]{2,1,0:T(8,128)(2,1)S(1)} async-done(((bf16[8,16,1152]{2,1,0:T(8,128)(2,1)}), bf16[8,16,1152]{2,1,0:T(8,128)(2,1)S(1)}, u32[]{:S(2)}, u32[]{:S(2)}) %all-to-all-start) | async-done | bytes 294944 | tf_op jit(solution)/shard_map/all_to_all | solution.py:473
  93.8 0.7 final.1
  (13 shorter events, 0.0 us)
Async XLA Ops:
  0.6 11.6 %copy-start.3 = (bf16[2,8192]{1,0:T(2,128)(2,1)S(1)}, bf16[2,8192]{1,0:T(2,128)(2,1)}, u32[]{:S(2)}) copy-start(bf16[2,8192]{1,0:T(2,128)(2,1)} %refs_0_.4) | copy-start | bytes 98308
  0.6 11.0 %collective-permute-start = (bf16[2,8192]{1,0:T(2,128)(2,1)}, bf16[2,8192]{1,0:T(2,128)(2,1)S(1)}, u32[]{:S(2)}, u32[]{:S(2)}) collective-permute-start(bf16[2,8192]{1,0:T(2,128)(2,1)} %refs_0_.4), channel_id=1, source_target_pairs={{0,4},{1,5},{2,6},{3,7},{4,0},{5,1},{6,2},{7,3},{8,12},{9,13},{10,... | collective-permute-start | bytes 98312 | tf_op jit(solution)/shard_map/ppermute | solution.py:492
  3.7 7.9 %collective-permute-start.1 = (bf16[2,8192]{1,0:T(2,128)(2,1)}, bf16[2,8192]{1,0:T(2,128)(2,1)S(1)}, u32[]{:S(2)}, u32[]{:S(2)}) collective-permute-start(bf16[2,8192]{1,0:T(2,128)(2,1)} %refs_0_.4), channel_id=1, source_target_pairs={{0,8},{1,9},{2,10},{3,11},{4,12},{5,13},{6,14},{7,15},{8,0},{9,1},... | collective-permute-start | bytes 98312 | tf_op jit(solution)/shard_map/ppermute | solution.py:492
  6.3 5.9 %collective-permute-start.2 = (bf16[2,8192]{1,0:T(2,128)(2,1)}, bf16[2,8192]{1,0:T(2,128)(2,1)S(1)}, u32[]{:S(2)}, u32[]{:S(2)}) collective-permute-start(bf16[2,8192]{1,0:T(2,128)(2,1)} %refs_0_.4), channel_id=1, source_target_pairs={{0,12},{1,13},{2,14},{3,15},{4,8},{5,9},{6,10},{7,11},{8,4},{9,5},... | collective-permute-start | bytes 98312 | tf_op jit(solution)/shard_map/ppermute | solution.py:492
  12.3 5.0 %collective-permute-start.3 = (bf16[8,8192]{1,0:T(8,128)(2,1)S(1)}, bf16[8,8192]{1,0:T(8,128)(2,1)S(1)}, u32[]{:S(2)}, u32[]{:S(2)}) collective-permute-start(bf16[8,8192]{1,0:T(8,128)(2,1)S(1)} %stacked.1.refs_2_.refs_1_), channel_id=1, source_target_pairs={{0,2},{1,3},{2,0},{3,1},{4,6},{5,7},{6,4},{7,5},{8,10},{9,11},{10,... | collective-permute-start | bytes 393224 | tf_op jit(solution)/shard_map/ppermute | solution.py:492
  13.9 11.2 %collective-permute-start.4 = (bf16[8,8192]{1,0:T(8,128)(2,1)S(1)}, bf16[8,8192]{1,0:T(8,128)(2,1)S(1)}, u32[]{:S(2)}, u32[]{:S(2)}) collective-permute-start(bf16[8,8192]{1,0:T(8,128)(2,1)S(1)} %stacked.1.refs_2_.refs_1_), channel_id=1, source_target_pairs={{0,1},{1,0},{2,3},{3,2},{4,5},{5,4},{6,7},{7,6},{8,9},{9,8},{10,11... | collective-permute-start | bytes 393224 | tf_op jit(solution)/shard_map/ppermute | solution.py:492
  17.4 7.8 %collective-permute-start.5 = (bf16[8,8192]{1,0:T(8,128)(2,1)S(1)}, bf16[8,8192]{1,0:T(8,128)(2,1)S(1)}, u32[]{:S(2)}, u32[]{:S(2)}) collective-permute-start(bf16[8,8192]{1,0:T(8,128)(2,1)S(1)} %collective-permute-done.3.refs_2_.refs_3_), channel_id=1, source_target_pairs={{0,1},{1,0},{2,3},{3,2},{4,5},{5,4},{6,7},{7,6},{8,9},{9,8},{10,11... | collective-permute-start | bytes 393224 | tf_op jit(solution)/shard_map/ppermute | solution.py:492
  21.2 4.0 %copy-start = (bf16[512,2048]{1,0:T(8,128)(2,1)S(1)}, bf16[512,2048]{1,0:T(8,128)(2,1)}, u32[]{:S(2)}) copy-start(bf16[512,2048]{1,0:T(8,128)(2,1)} %refs_2_.1) | copy-start | bytes 6291460
  21.2 4.0 %copy-start.4 = (s32[32]{0:T(128)S(1)}, s32[32]{0:T(128)}, u32[]{:S(2)}) copy-start(s32[32]{0:T(128)} %param.13) | copy-start | bytes 388
  25.8 5.8 %collective-permute-start.6 = (f32[32,64]{1,0:T(8,128)S(1)}, f32[32,64]{1,0:T(8,128)S(1)}, u32[]{:S(2)}, u32[]{:S(2)}) collective-permute-start(f32[32,64]{1,0:T(8,128)S(1)} %get-tuple-element.44.refs_7_.left_ref), channel_id=1, source_target_pairs={{0,1},{1,0},{2,3},{3,2},{4,5},{5,4},{6,7},{7,6},{8,9},{9,8},{10,11... | collective-permute-start | bytes 24584 | tf_op jit(solution)/shard_map/ppermute | solution.py:492
  31.7 6.9 %collective-permute-start.7 = (f32[32,64]{1,0:T(8,128)S(1)}, f32[32,64]{1,0:T(8,128)S(1)}, u32[]{:S(2)}, u32[]{:S(2)}) collective-permute-start(f32[32,64]{1,0:T(8,128)S(1)} %plus.8.refs_9_.left_ref), channel_id=1, source_target_pairs={{0,2},{1,3},{2,0},{3,1},{4,6},{5,7},{6,4},{7,5},{8,10},{9,11},{10,... | collective-permute-start | bytes 24584 | tf_op jit(solution)/shard_map/ppermute | solution.py:492
  38.7 3.8 %collective-permute-start.8 = (f32[32,64]{1,0:T(8,128)S(1)}, f32[32,64]{1,0:T(8,128)S(1)}, u32[]{:S(2)}, u32[]{:S(2)}) collective-permute-start(f32[32,64]{1,0:T(8,128)S(1)} %plus.9.refs_8_.left_ref), channel_id=1, source_target_pairs={{0,4},{1,5},{2,6},{3,7},{4,0},{5,1},{6,2},{7,3},{8,12},{9,13},{10,... | collective-permute-start | bytes 24584 | tf_op jit(solution)/shard_map/ppermute | solution.py:492
  42.3 6.8 %copy-start.2 = (bf16[32,1792]{1,0:T(8,128)(2,1)S(1)}, bf16[32,1792]{1,0:T(8,128)(2,1)}, u32[]{:S(2)}) copy-start(bf16[32,1792]{1,0:T(8,128)(2,1)} %refs_3_.3) | copy-start | bytes 344068
  42.5 6.6 %collective-permute-start.9 = (f32[32,64]{1,0:T(8,128)S(1)}, f32[32,64]{1,0:T(8,128)S(1)}, u32[]{:S(2)}, u32[]{:S(2)}) collective-permute-start(f32[32,64]{1,0:T(8,128)S(1)} %plus.10.refs_8_.left_ref), channel_id=1, source_target_pairs={{0,8},{1,9},{2,10},{3,11},{4,12},{5,13},{6,14},{7,15},{8,0},{9,1},... | collective-permute-start | bytes 24584 | tf_op jit(solution)/shard_map/ppermute | solution.py:492
  52.9 1.2 %collective-permute-start.10 = (f32[32,64]{1,0:T(8,128)S(1)}, f32[32,64]{1,0:T(8,128)S(1)}, u32[]{:S(2)}, u32[]{:S(2)}) collective-permute-start(f32[32,64]{1,0:T(8,128)S(1)} %get-tuple-element.60.left_ref), channel_id=1, source_target_pairs={{0,1},{1,0},{2,3},{3,2},{4,5},{5,4},{6,7},{7,6},{8,9},{9,8},{10,11... | collective-permute-start | bytes 24584 | tf_op jit(solution)/shard_map/ppermute | solution.py:492
  54.1 5.0 %collective-permute-start.11 = (f32[32,64]{1,0:T(8,128)S(1)}, f32[32,64]{1,0:T(8,128)S(1)}, u32[]{:S(2)}, u32[]{:S(2)}) collective-permute-start(f32[32,64]{1,0:T(8,128)S(1)} %plus.12.refs_4_.left_ref), channel_id=1, source_target_pairs={{0,2},{1,3},{2,0},{3,1},{4,6},{5,7},{6,4},{7,5},{8,10},{9,11},{10,... | collective-permute-start | bytes 24584 | tf_op jit(solution)/shard_map/ppermute | solution.py:492
  59.0 19.0 %collective-permute-start.17 = (bf16[16,2048]{1,0:T(8,128)(2,1)S(1)}, bf16[16,2048]{1,0:T(8,128)(2,1)S(1)}, u32[]{:S(2)}, u32[]{:S(2)}) collective-permute-start(bf16[16,2048]{1,0:T(8,128)(2,1)S(1)} %get-tuple-element.72), channel_id=1, source_target_pairs={{0,1},{1,0},{2,3},{3,2},{4,5},{5,4},{6,7},{7,6},{8,9},{9,8},{10,11... | collective-permute-start | bytes 196616 | tf_op jit(solution)/shard_map/ppermute | solution.py:492
  59.3 5.9 %collective-permute-start.12 = (f32[32,64]{1,0:T(8,128)S(1)}, f32[32,64]{1,0:T(8,128)S(1)}, u32[]{:S(2)}, u32[]{:S(2)}) collective-permute-start(f32[32,64]{1,0:T(8,128)S(1)} %plus.13.refs_5_.left_ref), channel_id=1, source_target_pairs={{0,4},{1,5},{2,6},{3,7},{4,0},{5,1},{6,2},{7,3},{8,12},{9,13},{10,... | collective-permute-start | bytes 24584 | tf_op jit(solution)/shard_map/ppermute | solution.py:492
  65.1 6.2 %copy-start.1 = (bf16[512,2048]{1,0:T(8,128)(2,1)S(1)}, bf16[512,2048]{1,0:T(8,128)(2,1)}, u32[]{:S(2)}) copy-start(bf16[512,2048]{1,0:T(8,128)(2,1)} %refs_2_.1) | copy-start | bytes 6291460
  65.1 12.9 %collective-permute-start.16 = (bf16[16,2048]{1,0:T(8,128)(2,1)S(1)}, bf16[16,2048]{1,0:T(8,128)(2,1)S(1)}, u32[]{:S(2)}, u32[]{:S(2)}) collective-permute-start(bf16[16,2048]{1,0:T(8,128)(2,1)S(1)} %get-tuple-element.71), channel_id=1, source_target_pairs={{0,1},{1,0},{2,3},{3,2},{4,5},{5,4},{6,7},{7,6},{8,9},{9,8},{10,11... | collective-permute-start | bytes 196616 | tf_op jit(solution)/shard_map/ppermute | solution.py:492
  65.2 6.0 %collective-permute-start.13 = (f32[32,64]{1,0:T(8,128)S(1)}, f32[32,64]{1,0:T(8,128)S(1)}, u32[]{:S(2)}, u32[]{:S(2)}) collective-permute-start(f32[32,64]{1,0:T(8,128)S(1)} %plus.14.refs_3_.left_ref), channel_id=1, source_target_pairs={{0,8},{1,9},{2,10},{3,11},{4,12},{5,13},{6,14},{7,15},{8,0},{9,1},... | collective-permute-start | bytes 24584 | tf_op jit(solution)/shard_map/ppermute | solution.py:492
  71.0 7.0 %collective-permute-start.15 = (bf16[16,2048]{1,0:T(8,128)(2,1)S(1)}, bf16[16,2048]{1,0:T(8,128)(2,1)S(1)}, u32[]{:S(2)}, u32[]{:S(2)}) collective-permute-start(bf16[16,2048]{1,0:T(8,128)(2,1)S(1)} %get-tuple-element.70), channel_id=1, source_target_pairs={{0,1},{1,0},{2,3},{3,2},{4,5},{5,4},{6,7},{7,6},{8,9},{9,8},{10,11... | collective-permute-start | bytes 196616 | tf_op jit(solution)/shard_map/ppermute | solution.py:492
  76.5 1.5 %collective-permute-start.14 = (bf16[16,2048]{1,0:T(8,128)(2,1)S(1)}, bf16[16,2048]{1,0:T(8,128)(2,1)S(1)}, u32[]{:S(2)}, u32[]{:S(2)}) collective-permute-start(bf16[16,2048]{1,0:T(8,128)(2,1)S(1)} %get-tuple-element.69), channel_id=1, source_target_pairs={{0,1},{1,0},{2,3},{3,2},{4,5},{5,4},{6,7},{7,6},{8,9},{9,8},{10,11... | collective-permute-start | bytes 196616 | tf_op jit(solution)/shard_map/ppermute | solution.py:492
  76.8 1.2 %collective-permute-start.18 = (bf16[16,512]{1,0:T(8,128)(2,1)S(1)}, bf16[16,512]{1,0:T(8,128)(2,1)S(1)}, u32[]{:S(2)}, u32[]{:S(2)}) collective-permute-start(bf16[16,512]{1,0:T(8,128)(2,1)S(1)} %get-tuple-element.64.refs_3_), channel_id=1, source_target_pairs={{0,1},{1,0},{2,3},{3,2},{4,5},{5,4},{6,7},{7,6},{8,9},{9,8},{10,11... | collective-permute-start | bytes 49160 | tf_op jit(solution)/shard_map/ppermute | solution.py:492
  79.1 14.7 %all-to-all-start = ((bf16[8,16,1152]{2,1,0:T(8,128)(2,1)}), bf16[8,16,1152]{2,1,0:T(8,128)(2,1)S(1)}, u32[]{:S(2)}, u32[]{:S(2)}) async-start(bf16[8,16,1152]{2,1,0:T(8,128)(2,1)} %merge.1), calls=%async_computation | async-start | bytes 589824 | tf_op jit(solution)/shard_map/all_to_all | solution.py:473

commit v8 on v7

--- a/solution.py
+++ b/solution.py
@@ -54,7 +54,7 @@
 VMEM = pl.BlockSpec(memory_space=pltpu.VMEM)
 ANY = pl.BlockSpec(memory_space=pl.ANY)
 CUTS = 4
-COPIES = 4
+COPIES = 8
 SLOTS = 6
 STORE_GRANT = 10 << 20
 
@@ -524,19 +524,20 @@
     for hop in reversed(hops[2:-2]):
         block = stacked([block, swapped(block, hop)])
     other = swapped(block, hops[1])
-    x = [block, other, swapped(block, 1), swapped(other, 1)]
     store, token = store_call(
         mark, store, [(gate_weight, 1, 2)], [], [mark_shape], 0, "fetch", after=[block]
     )
+    block = stacked([block, other], [token])
+    x = [block, swapped(block, 1)]
     store, token = store_call(
-        mark, store, [(up_weight, 1, 3)], [], [mark_shape], 0, "fetch", after=[other]
+        mark, store, [(up_weight, 1, 3)], [], [mark_shape], 0, "fetch", after=[block]
     )
 
     input_span, low = low_part(adapter_down_maps, tenants, x, count)
     sums = []
     slots = {0: (0, 1), 1: (2, 3), 2: (4, 5), 3: (0, 1)}
     fetches = {
-        0: pair(2, 4, 5), 1: pair(3, 0, 1), 2: [(adapter_up_maps, 0, 2)], 3: [(gate_weight, 1, 3)]
+        0: pair(2, 4, 5), 1: pair(3, 0, 1), 2: [(adapter_up_maps, 0, 2)], 3: []
     }
     step = 0
     for cut in range(CUTS):
@@ -554,8 +555,10 @@
     low_grad = plus(low_grad, swapped(low_grad, hops[0]))
     step = 1
     parts, arrived = {}, {}
-    slots = {3: (0, 1), 2: (4, 5), 1: (3, 2), 0: (0, 1)}
-    fetches = {3: [(up_weight, 1, 2)], 2: pair(0, 0, 1), 1: [], 0: []}
+    slots = {3: (0, 1), 2: (4, 5), 1: (2, 3), 0: (0, 1)}
+    fetches = {
+        3: [(gate_weight, 1, 2)], 2: [(gate_weight, 0, 0)], 1: [(up_weight, 0, 1)], 0: []
+    }
     for cut in reversed(range(CUTS)):
         if cut > 0:
             after = [low_grad]

time: 94.7 us -> 89.8 us (0.948)
  waiting for transfers between devices: 9.82 us -> 6.7 us
  Pallas kernels: 62.4 us -> 60.6 us
    ppermute x19 -> x18, waiting for transfers between devices: 6.44 us -> 3.35 us  [swapped(): lax.ppermute(block, 'tp', [(i, i ^ hop) for i in range(lax.axis_size('tp'...]
    pallas_call x12, Pallas kernels: 52.2 us -> 50.6 us  [store_call(): pl.pallas_call(body, in_specs=[VMEM] * (n_in + (not new)) + [ANY] * (n_hb...]
    ppermute x19 -> x18, starting transfers between devices: 16.6 us -> 17.2 us  [swapped(): lax.ppermute(block, 'tp', [(i, i ^ hop) for i in range(lax.axis_size('tp'...]
  transfers between devices with their start and end apart: 20 -> 19, of which waited for: 6 -> 6; matrix products, arithmetic and copies ran while one was open for 0% -> 0% of each run, Pallas kernels for 59% -> 61%
where the time goes in v8:
time: 89.8 us; the launch traced here: 89.6 us
  Pallas kernels  60.6 us (67%)
  starting transfers between devices  21.3 us (24%)
  waiting for transfers between devices  6.7 us (7%)
  between operations  0.92 us (1%)
    pallas_call x12, Pallas kernels, store_call(): pl.pallas_call(body, in_specs=[VMEM] * (n_in + (not new)) + [ANY] * (n_hb...  50.6 us
    ppermute x18, starting transfers between devices, swapped(): lax.ppermute(block, 'tp', [(i, i ^ hop) for i in range(lax.axis_size('tp'...  17.2 us
    pallas_call x2, Pallas kernels, outer(): pl.pallas_call(outer_kernel, grid=(height // block,), in_specs=[pl.BlockS...  6.55 us
    all_to_all x1, starting transfers between devices, between_same_cores(): lax.all_to_all(blocks, 'tp', split_axis=0, concat_axis=0, tiled=True, axi...  4.16 us
    ppermute x18, waiting for transfers between devices, swapped(): lax.ppermute(block, 'tp', [(i, i ^ hop) for i in range(lax.axis_size('tp'...  3.35 us
    all_to_all x1, waiting for transfers between devices, between_same_cores(): lax.all_to_all(blocks, 'tp', split_axis=0, concat_axis=0, tiled=True, axi...  3.35 us
  transfers between devices with their start and end apart: 19, of which 6 were waited for; matrix products, arithmetic and copies ran while one was open for 0% of the time, Pallas kernels for 61%

profile of v8, /device:TPU:0, one launch (start us, length us, event | category | flops | bytes accessed | tf_op | source)
XLA Modules:
  0.0 89.6 jit_solution(10519983083659981357)
XLA Ops:
  0.6 0.0 copy-start.2
  0.6 3.1 %collective-permute-start = (bf16[2,8192]{1,0:T(2,128)(2,1)}, bf16[2,8192]{1,0:T(2,128)(2,1)S(1)}, u32[]{:S(2)}, u32[]{:S(2)}) collective-permute-start(bf16[2,8192]{1,0:T(2,128)(2,1)} %refs_0_.4), channel_id=1, source_target_pairs={{0,4},{1,5},{2,6},{3,7},{4,0},{5,1},{6,2},{7,3},{8,12},{9,13},{10,... | collective-permute-start | bytes 98312 | tf_op jit(solution)/shard_map/ppermute | solution.py:492
  3.7 2.6 %collective-permute-start.1 = (bf16[2,8192]{1,0:T(2,128)(2,1)}, bf16[2,8192]{1,0:T(2,128)(2,1)S(1)}, u32[]{:S(2)}, u32[]{:S(2)}) collective-permute-start(bf16[2,8192]{1,0:T(2,128)(2,1)} %refs_0_.4), channel_id=1, source_target_pairs={{0,8},{1,9},{2,10},{3,11},{4,12},{5,13},{6,14},{7,15},{8,0},{9,1},... | collective-permute-start | bytes 98312 | tf_op jit(solution)/shard_map/ppermute | solution.py:492
  6.3 0.0 collective-permute-start.2
  6.3 5.3 %fetch.3 = (bf16[12288,1792]{1,0:T(8,128)(2,1)S(1)}, f32[8,128]{1,0:T(8,128)S(1)}) custom-call(bf16[8192,1792]{1,0:T(8,128)(2,1)} %refs_3_.8, bf16[8192,1792]{1,0:T(8,128)(2,1)} %refs_3_.9), custom_call_target="tpu_custom_call" | custom-call | bytes 14680064 | tf_op jit(solution)/shard_map/fetch/pallas_call | solution.py:96
  11.7 0.0 collective-permute-done.refs_1_
  11.7 0.0 collective-permute-done.1.refs_2_
  11.7 0.6 collective-permute-done.2.refs_3_
  12.2 0.0 copy-done.2
  12.2 0.1 stacked.2.refs_2_.refs_0_
  12.3 1.6 %collective-permute-start.3 = (bf16[8,8192]{1,0:T(8,128)(2,1)S(1)}, bf16[8,8192]{1,0:T(8,128)(2,1)S(1)}, u32[]{:S(2)}, u32[]{:S(2)}) collective-permute-start(bf16[8,8192]{1,0:T(8,128)(2,1)S(1)} %stacked.2.refs_2_.refs_0_), channel_id=1, source_target_pairs={{0,2},{1,3},{2,0},{3,1},{4,6},{5,7},{6,4},{7,5},{8,10},{9,11},{10,... | collective-permute-start | bytes 393224 | tf_op jit(solution)/shard_map/ppermute | solution.py:492
  13.9 3.2 %fetch.4 = (bf16[12288,1792]{1,0:T(8,128)(2,1)S(1)}, f32[8,128]{1,0:T(8,128)S(1)}) custom-call(bf16[12288,1792]{1,0:T(8,128)(2,1)S(1)} %get-tuple-element.41.refs_0_, bf16[8192,1792]{1,0:T(8,128)(2,1)} %refs_3_.8, bf16[8,8192]{1,0:T(8,128)(2,1)S(1)} %stacked.2.refs_2_.refs_0_), custom_call_target="tpu_custom_call", output_to_operand_aliasing={{0}: (0, {})} | custom-call | bytes 7340032 | tf_op jit(solution)/shard_map/fetch/pallas_call | solution.py:96
  17.1 0.0 copy-start
  17.1 0.0 copy-start.3
  17.1 0.2 collective-permute-done.3.refs_1_
  17.4 0.1 collective-permute-start.4
  17.5 4.0 %fetch.5 = (bf16[12288,1792]{1,0:T(8,128)(2,1)S(1)}, f32[8,128]{1,0:T(8,128)}) custom-call(bf16[12288,1792]{1,0:T(8,128)(2,1)S(1)} %get-tuple-element.43.refs_0_, bf16[8192,1792]{1,0:T(8,128)(2,1)} %refs_3_.9, bf16[16,8192]{1,0:T(8,128)(2,1)S(1)} %stacked.3.refs_2_.refs_1_), custom_call_target="tpu_custom_call", output_to_operand_aliasing={{0}: (0, {})} | custom-call | bytes 7340032 | tf_op jit(solution)/shard_map/fetch/pallas_call | solution.py:96
  21.5 0.0 collective-permute-done.4.refs_3_.refs_2_
  21.5 0.0 copy-done
  21.5 0.0 copy-done.3
  21.5 0.7 low_part.1
  22.2 0.3 collective-permute-start.5
  22.5 5.3 %forward.4 = (bf16[12288,1792]{1,0:T(8,128)(2,1)S(1)}, f32[32,1792]{1,0:T(8,128)S(1)}, f32[32,1792]{1,0:T(8,128)S(1)}) custom-call(bf16[12288,1792]{1,0:T(8,128)(2,1)S(1)} %get-tuple-element.45.refs_0_, bf16[16,8192]{1,0:T(8,128)(2,1)S(1)} %stacked.3.refs_2_.refs_1_, ...), custom_call_target="tpu_custom_call", output_to_operand_aliasing={{0}: (0, {})} | custom-call | flops 469762048 | bytes 14680064 | tf_op jit(solution)/shard_map/forward/pallas_call | solution.py:96
  27.8 0.0 collective-permute-done.5.right_ref
  27.8 1.6 %collective-permute-start.6 = (f32[32,64]{1,0:T(8,128)S(1)}, f32[32,64]{1,0:T(8,128)S(1)}, u32[]{:S(2)}, u32[]{:S(2)}) collective-permute-start(f32[32,64]{1,0:T(8,128)S(1)} %plus.8.refs_7_.left_ref), channel_id=1, source_target_pairs={{0,2},{1,3},{2,0},{3,1},{4,6},{5,7},{6,4},{7,5},{8,10},{9,11},{10,... | collective-permute-start | bytes 24584 | tf_op jit(solution)/shard_map/ppermute | solution.py:492
  29.4 5.4 %forward.5 = (bf16[12288,1792]{1,0:T(8,128)(2,1)S(1)}, f32[32,1792]{1,0:T(8,128)S(1)}, f32[32,1792]{1,0:T(8,128)S(1)}) custom-call(bf16[12288,1792]{1,0:T(8,128)(2,1)S(1)} %get-tuple-element.47.refs_0_, bf16[16,8192]{1,0:T(8,128)(2,1)S(1)} %stacked.3.refs_2_.refs_1_, ...), custom_call_target="tpu_custom_call", output_to_operand_aliasing={{0}: (0, {})} | custom-call | flops 469762048 | bytes 14680064 | tf_op jit(solution)/shard_map/forward/pallas_call | solution.py:96
  34.8 0.0 collective-permute-done.6.right_ref
  34.9 0.4 collective-permute-start.7
  35.3 3.2 %forward.6 = (bf16[12288,1792]{1,0:T(8,128)(2,1)S(1)}, f32[32,1792]{1,0:T(8,128)S(1)}, f32[32,1792]{1,0:T(8,128)S(1)}) custom-call(bf16[12288,1792]{1,0:T(8,128)(2,1)S(1)} %get-tuple-element.50.refs_0_, bf16[16,8192]{1,0:T(8,128)(2,1)S(1)} %stacked.3.refs_2_.refs_1_, ...), custom_call_target="tpu_custom_call", output_to_operand_aliasing={{0}: (0, {})} | custom-call | flops 469762048 | bytes 7340032 | tf_op jit(solution)/shard_map/forward/pallas_call | solution.py:96
  38.5 0.2 collective-permute-done.7.right_ref
  38.7 3.4 %collective-permute-start.8 = (f32[32,64]{1,0:T(8,128)S(1)}, f32[32,64]{1,0:T(8,128)S(1)}, u32[]{:S(2)}, u32[]{:S(2)}) collective-permute-start(f32[32,64]{1,0:T(8,128)S(1)} %plus.10.refs_5_.left_ref), channel_id=1, source_target_pairs={{0,8},{1,9},{2,10},{3,11},{4,12},{5,13},{6,14},{7,15},{8,0},{9,1},... | collective-permute-start | bytes 24584 | tf_op jit(solution)/shard_map/ppermute | solution.py:492
  42.1 2.6 %forward.7 = (bf16[12288,1792]{1,0:T(8,128)(2,1)S(1)}, f32[32,1792]{1,0:T(8,128)S(1)}, f32[32,1792]{1,0:T(8,128)S(1)}) custom-call(bf16[12288,1792]{1,0:T(8,128)(2,1)S(1)} %get-tuple-element.53.refs_0_, bf16[16,8192]{1,0:T(8,128)(2,1)S(1)} %stacked.3.refs_2_.refs_1_, ...), custom_call_target="tpu_custom_call", output_to_operand_aliasing={{0}: (0, {})} | custom-call | flops 469762048 | tf_op jit(solution)/shard_map/forward/pallas_call | solution.py:96
  44.7 0.0 collective-permute-done.8.right_ref
  44.7 0.0 copy-done.1
  44.7 3.8 %activation.1 = (bf16[12288,1792]{1,0:T(8,128)(2,1)S(1)}, bf16[32,1792]{1,0:T(8,128)(2,1)S(1)}, bf16[32,1792]{1,0:T(8,128)(2,1)S(1)}, f32[32,64]{1,0:T(8,128)S(1)}, bf16[32,2048]{1,0:T(8,128)(2,1)S(1)}) custom-call(bf16[12288,1792]{1,0:T(8,128)(2,1)S(1)} %get-tuple-element.56.refs_0_, ...), custom_call_target="tpu_custom_call", output_to_operand_aliasing={{0}: (0, {})} | custom-call | flops 469762048 | tf_op jit(solution)/shard_map/activation/pallas_call | solution.py:96
  48.5 0.0 collective-permute-start.9
  48.5 1.2 %collective-permute-done.9.right_ref = f32[32,64]{1,0:T(8,128)S(1)} collective-permute-done((f32[32,64]{1,0:T(8,128)S(1)}, f32[32,64]{1,0:T(8,128)S(1)}, u32[]{:S(2)}, u32[]{:S(2)}) %collective-permute-start.9) | collective-permute-done | bytes 8224 | tf_op jit(solution)/shard_map/ppermute | solution.py:492
  49.7 0.5 collective-permute-start.10
  50.2 4.6 %backward.4 = (bf16[12288,1792]{1,0:T(8,128)(2,1)S(1)}, f32[16,2048]{1,0:T(8,128)S(1)}, bf16[16,2048]{1,0:T(8,128)(2,1)S(1)}) custom-call(bf16[12288,1792]{1,0:T(8,128)(2,1)S(1)} %get-tuple-element.59.refs_0_, bf16[32,1792]{1,0:T(8,128)(2,1)S(1)} %get-tuple-element.60.refs_1_.right_ref, ...), custom_call_target="tpu_custom_call", output_to_operand_aliasing={{0}: (0, {})} | custom-call | flops 469762048 | bytes 7340032 | tf_op jit(solution)/shard_map/backward/pallas_call | solution.py:96
  54.8 0.1 collective-permute-start.16
  54.9 0.0 collective-permute-done.10.right_ref
  54.9 0.5 collective-permute-start.11
  55.5 4.4 %backward.5 = (bf16[12288,1792]{1,0:T(8,128)(2,1)S(1)}, f32[16,2048]{1,0:T(8,128)S(1)}, bf16[16,2048]{1,0:T(8,128)(2,1)S(1)}) custom-call(bf16[12288,1792]{1,0:T(8,128)(2,1)S(1)} %get-tuple-element.63.refs_0_, bf16[32,1792]{1,0:T(8,128)(2,1)S(1)} %get-tuple-element.60.refs_1_.right_ref, ...), custom_call_target="tpu_custom_call", output_to_operand_aliasing={{0}: (0, {})} | custom-call | flops 469762048 | bytes 7340032 | tf_op jit(solution)/shard_map/backward/pallas_call | solution.py:96
  59.9 0.3 collective-permute-start.15
  60.2 0.0 collective-permute-done.11.right_ref
  60.2 2.1 %collective-permute-start.12 = (f32[32,64]{1,0:T(8,128)S(1)}, f32[32,64]{1,0:T(8,128)S(1)}, u32[]{:S(2)}, u32[]{:S(2)}) collective-permute-start(f32[32,64]{1,0:T(8,128)S(1)} %plus.14.refs_4_.left_ref), channel_id=1, source_target_pairs={{0,8},{1,9},{2,10},{3,11},{4,12},{5,13},{6,14},{7,15},{8,0},{9,1},... | collective-permute-start | bytes 24584 | tf_op jit(solution)/shard_map/ppermute | solution.py:492
  62.3 4.4 %backward.6 = (bf16[12288,1792]{1,0:T(8,128)(2,1)S(1)}, f32[16,2048]{1,0:T(8,128)S(1)}, bf16[16,2048]{1,0:T(8,128)(2,1)S(1)}) custom-call(bf16[12288,1792]{1,0:T(8,128)(2,1)S(1)} %get-tuple-element.64.refs_0_, bf16[32,1792]{1,0:T(8,128)(2,1)S(1)} %get-tuple-element.60.refs_1_.right_ref, ...), custom_call_target="tpu_custom_call", output_to_operand_aliasing={{0}: (0, {})} | custom-call | flops 469762048 | bytes 7340032 | tf_op jit(solution)/shard_map/backward/pallas_call | solution.py:96
  66.7 0.1 collective-permute-start.14
  66.8 0.0 collective-permute-done.12.right_ref
  66.8 0.9 adapter_part.1
  67.7 4.3 %backward.7 = (bf16[12288,1792]{1,0:T(8,128)(2,1)S(1)}, f32[16,2048]{1,0:T(8,128)S(1)}, bf16[16,2048]{1,0:T(8,128)(2,1)S(1)}) custom-call(bf16[12288,1792]{1,0:T(8,128)(2,1)S(1)} %get-tuple-element.65.refs_0_, bf16[32,1792]{1,0:T(8,128)(2,1)S(1)} %get-tuple-element.60.refs_1_.right_ref, ...), custom_call_target="tpu_custom_call", output_to_operand_aliasing={{0}: (0, {})} | custom-call | flops 469762048 | tf_op jit(solution)/shard_map/backward/pallas_call | solution.py:96
  72.0 0.5 collective-permute-start.13
  72.5 0.1 collective-permute-start.17
  72.6 1.1 %collective-permute-done.17.refs_9_ = bf16[16,512]{1,0:T(8,128)(2,1)S(1)} collective-permute-done((bf16[16,512]{1,0:T(8,128)(2,1)S(1)}, bf16[16,512]{1,0:T(8,128)(2,1)S(1)}, u32[]{:S(2)}, u32[]{:S(2)}) %collective-permute-start.17) | collective-permute-done | bytes 16416 | tf_op jit(solution)/shard_map/ppermute | solution.py:492
  73.7 0.0 collective-permute-done.16.refs_7_
  73.7 0.0 collective-permute-done.15.refs_6_
  73.7 0.0 collective-permute-done.14.refs_5_
  73.7 0.0 collective-permute-done.13.refs_4_
  73.7 1.1 %merge.1 = bf16[8,16,1152]{2,1,0:T(8,128)(2,1)} custom-call(f32[16,2048]{1,0:T(8,128)S(1)} %get-tuple-element.67.refs_0_, f32[16,2048]{1,0:T(8,128)S(1)} %get-tuple-element.68.refs_1_, f32[16,2048]{1,0:T(8,128)S(1)} %get-tuple-element.69.refs_2_, f32[16,2048]{1,0:T(8,128)S(1)} %get-tuple-element.70.refs_3_, ...), custom_call_target="tpu_custom_call" | custom-call | tf_op jit(solution)/shard_map/merge/pallas_call | solution.py:383
  74.8 4.2 %all-to-all-start = ((bf16[8,16,1152]{2,1,0:T(8,128)(2,1)}), bf16[8,16,1152]{2,1,0:T(8,128)(2,1)S(1)}, u32[]{:S(2)}, u32[]{:S(2)}) async-start(bf16[8,16,1152]{2,1,0:T(8,128)(2,1)} %merge.1), calls=%async_computation | async-start | bytes 589824 | tf_op jit(solution)/shard_map/all_to_all | solution.py:473
  79.0 4.5 %up_maps.1 = bf16[2048,1792]{1,0:T(8,128)(2,1)} custom-call(bf16[32,2048]{1,0:T(8,128)(2,1)S(1)} %get-tuple-element.78.left_ref, bf16[32,1792]{1,0:T(8,128)(2,1)S(1)} %get-tuple-element.60.refs_1_.right_ref), custom_call_target="tpu_custom_call" | custom-call | flops 234881024 | bytes 7340032 | tf_op jit(solution)/shard_map/up_maps/pallas_call | solution.py:450
  83.5 2.1 %down_maps.1 = bf16[512,2048]{1,0:T(8,128)(2,1)} custom-call(bf16[32,512]{1,0:T(8,128)(2,1)S(1)} %get-tuple-element.76.left_ref, bf16[32,2048]{1,0:T(8,128)(2,1)S(1)} %get-tuple-element.77.right_ref), custom_call_target="tpu_custom_call" | custom-call | flops 67108864 | bytes 2097152 | tf_op jit(solution)/shard_map/down_maps/pallas_call | solution.py:450
  85.5 3.3 %all-to-all-done.refs_0_ = bf16[8,16,1152]{2,1,0:T(8,128)(2,1)S(1)} async-done(((bf16[8,16,1152]{2,1,0:T(8,128)(2,1)}), bf16[8,16,1152]{2,1,0:T(8,128)(2,1)S(1)}, u32[]{:S(2)}, u32[]{:S(2)}) %all-to-all-start) | async-done | bytes 294944 | tf_op jit(solution)/shard_map/all_to_all | solution.py:473
  88.9 0.7 final.1
  (10 shorter events, 0.1 us)
Async XLA Ops:
  0.6 11.6 %copy-start.2 = (bf16[2,8192]{1,0:T(2,128)(2,1)S(1)}, bf16[2,8192]{1,0:T(2,128)(2,1)}, u32[]{:S(2)}) copy-start(bf16[2,8192]{1,0:T(2,128)(2,1)} %refs_0_.4) | copy-start | bytes 98308
  0.6 11.0 %collective-permute-start = (bf16[2,8192]{1,0:T(2,128)(2,1)}, bf16[2,8192]{1,0:T(2,128)(2,1)S(1)}, u32[]{:S(2)}, u32[]{:S(2)}) collective-permute-start(bf16[2,8192]{1,0:T(2,128)(2,1)} %refs_0_.4), channel_id=1, source_target_pairs={{0,4},{1,5},{2,6},{3,7},{4,0},{5,1},{6,2},{7,3},{8,12},{9,13},{10,... | collective-permute-start | bytes 98312 | tf_op jit(solution)/shard_map/ppermute | solution.py:492
  3.7 7.9 %collective-permute-start.1 = (bf16[2,8192]{1,0:T(2,128)(2,1)}, bf16[2,8192]{1,0:T(2,128)(2,1)S(1)}, u32[]{:S(2)}, u32[]{:S(2)}) collective-permute-start(bf16[2,8192]{1,0:T(2,128)(2,1)} %refs_0_.4), channel_id=1, source_target_pairs={{0,8},{1,9},{2,10},{3,11},{4,12},{5,13},{6,14},{7,15},{8,0},{9,1},... | collective-permute-start | bytes 98312 | tf_op jit(solution)/shard_map/ppermute | solution.py:492
  6.3 5.9 %collective-permute-start.2 = (bf16[2,8192]{1,0:T(2,128)(2,1)}, bf16[2,8192]{1,0:T(2,128)(2,1)S(1)}, u32[]{:S(2)}, u32[]{:S(2)}) collective-permute-start(bf16[2,8192]{1,0:T(2,128)(2,1)} %refs_0_.4), channel_id=1, source_target_pairs={{0,12},{1,13},{2,14},{3,15},{4,8},{5,9},{6,10},{7,11},{8,4},{9,5},... | collective-permute-start | bytes 98312 | tf_op jit(solution)/shard_map/ppermute | solution.py:492
  12.3 5.0 %collective-permute-start.3 = (bf16[8,8192]{1,0:T(8,128)(2,1)S(1)}, bf16[8,8192]{1,0:T(8,128)(2,1)S(1)}, u32[]{:S(2)}, u32[]{:S(2)}) collective-permute-start(bf16[8,8192]{1,0:T(8,128)(2,1)S(1)} %stacked.2.refs_2_.refs_0_), channel_id=1, source_target_pairs={{0,2},{1,3},{2,0},{3,1},{4,6},{5,7},{6,4},{7,5},{8,10},{9,11},{10,... | collective-permute-start | bytes 393224 | tf_op jit(solution)/shard_map/ppermute | solution.py:492
  17.1 4.4 %copy-start = (bf16[512,2048]{1,0:T(8,128)(2,1)S(1)}, bf16[512,2048]{1,0:T(8,128)(2,1)}, u32[]{:S(2)}) copy-start(bf16[512,2048]{1,0:T(8,128)(2,1)} %refs_2_.1) | copy-start | bytes 6291460
  17.1 4.4 %copy-start.3 = (s32[32]{0:T(128)S(1)}, s32[32]{0:T(128)}, u32[]{:S(2)}) copy-start(s32[32]{0:T(128)} %param.13) | copy-start | bytes 388
  17.4 4.0 %collective-permute-start.4 = (bf16[16,8192]{1,0:T(8,128)(2,1)S(1)}, bf16[16,8192]{1,0:T(8,128)(2,1)S(1)}, u32[]{:S(2)}, u32[]{:S(2)}) collective-permute-start(bf16[16,8192]{1,0:T(8,128)(2,1)S(1)} %stacked.3.refs_2_.refs_1_), channel_id=1, source_target_pairs={{0,1},{1,0},{2,3},{3,2},{4,5},{5,4},{6,7},{7,6},{8,9},{9,8},{10,11... | collective-permute-start | bytes 786440 | tf_op jit(solution)/shard_map/ppermute | solution.py:492
  22.2 5.7 %collective-permute-start.5 = (f32[32,64]{1,0:T(8,128)S(1)}, f32[32,64]{1,0:T(8,128)S(1)}, u32[]{:S(2)}, u32[]{:S(2)}) collective-permute-start(f32[32,64]{1,0:T(8,128)S(1)} %get-tuple-element.46.refs_5_.left_ref), channel_id=1, source_target_pairs={{0,1},{1,0},{2,3},{3,2},{4,5},{5,4},{6,7},{7,6},{8,9},{9,8},{10,11... | collective-permute-start | bytes 24584 | tf_op jit(solution)/shard_map/ppermute | solution.py:492
  27.8 7.0 %collective-permute-start.6 = (f32[32,64]{1,0:T(8,128)S(1)}, f32[32,64]{1,0:T(8,128)S(1)}, u32[]{:S(2)}, u32[]{:S(2)}) collective-permute-start(f32[32,64]{1,0:T(8,128)S(1)} %plus.8.refs_7_.left_ref), channel_id=1, source_target_pairs={{0,2},{1,3},{2,0},{3,1},{4,6},{5,7},{6,4},{7,5},{8,10},{9,11},{10,... | collective-permute-start | bytes 24584 | tf_op jit(solution)/shard_map/ppermute | solution.py:492
  34.9 3.8 %collective-permute-start.7 = (f32[32,64]{1,0:T(8,128)S(1)}, f32[32,64]{1,0:T(8,128)S(1)}, u32[]{:S(2)}, u32[]{:S(2)}) collective-permute-start(f32[32,64]{1,0:T(8,128)S(1)} %plus.9.refs_6_.left_ref), channel_id=1, source_target_pairs={{0,4},{1,5},{2,6},{3,7},{4,0},{5,1},{6,2},{7,3},{8,12},{9,13},{10,... | collective-permute-start | bytes 24584 | tf_op jit(solution)/shard_map/ppermute | solution.py:492
  35.3 9.4 %copy-start.1 = (bf16[32,1792]{1,0:T(8,128)(2,1)S(1)}, bf16[32,1792]{1,0:T(8,128)(2,1)}, u32[]{:S(2)}) copy-start(bf16[32,1792]{1,0:T(8,128)(2,1)} %refs_3_.6) | copy-start | bytes 344068
  38.7 6.0 %collective-permute-start.8 = (f32[32,64]{1,0:T(8,128)S(1)}, f32[32,64]{1,0:T(8,128)S(1)}, u32[]{:S(2)}, u32[]{:S(2)}) collective-permute-start(f32[32,64]{1,0:T(8,128)S(1)} %plus.10.refs_5_.left_ref), channel_id=1, source_target_pairs={{0,8},{1,9},{2,10},{3,11},{4,12},{5,13},{6,14},{7,15},{8,0},{9,1},... | collective-permute-start | bytes 24584 | tf_op jit(solution)/shard_map/ppermute | solution.py:492
  48.5 1.2 %collective-permute-start.9 = (f32[32,64]{1,0:T(8,128)S(1)}, f32[32,64]{1,0:T(8,128)S(1)}, u32[]{:S(2)}, u32[]{:S(2)}) collective-permute-start(f32[32,64]{1,0:T(8,128)S(1)} %get-tuple-element.62.left_ref), channel_id=1, source_target_pairs={{0,1},{1,0},{2,3},{3,2},{4,5},{5,4},{6,7},{7,6},{8,9},{9,8},{10,11... | collective-permute-start | bytes 24584 | tf_op jit(solution)/shard_map/ppermute | solution.py:492
  49.7 5.2 %collective-permute-start.10 = (f32[32,64]{1,0:T(8,128)S(1)}, f32[32,64]{1,0:T(8,128)S(1)}, u32[]{:S(2)}, u32[]{:S(2)}) collective-permute-start(f32[32,64]{1,0:T(8,128)S(1)} %plus.12.refs_4_.left_ref), channel_id=1, source_target_pairs={{0,2},{1,3},{2,0},{3,1},{4,6},{5,7},{6,4},{7,5},{8,10},{9,11},{10,... | collective-permute-start | bytes 24584 | tf_op jit(solution)/shard_map/ppermute | solution.py:492
  54.8 18.9 %collective-permute-start.16 = (bf16[16,2048]{1,0:T(8,128)(2,1)S(1)}, bf16[16,2048]{1,0:T(8,128)(2,1)S(1)}, u32[]{:S(2)}, u32[]{:S(2)}) collective-permute-start(bf16[16,2048]{1,0:T(8,128)(2,1)S(1)} %get-tuple-element.74), channel_id=1, source_target_pairs={{0,1},{1,0},{2,3},{3,2},{4,5},{5,4},{6,7},{7,6},{8,9},{9,8},{10,11... | collective-permute-start | bytes 196616 | tf_op jit(solution)/shard_map/ppermute | solution.py:492
  54.9 5.2 %collective-permute-start.11 = (f32[32,64]{1,0:T(8,128)S(1)}, f32[32,64]{1,0:T(8,128)S(1)}, u32[]{:S(2)}, u32[]{:S(2)}) collective-permute-start(f32[32,64]{1,0:T(8,128)S(1)} %plus.13.refs_4_.left_ref), channel_id=1, source_target_pairs={{0,4},{1,5},{2,6},{3,7},{4,0},{5,1},{6,2},{7,3},{8,12},{9,13},{10,... | collective-permute-start | bytes 24584 | tf_op jit(solution)/shard_map/ppermute | solution.py:492
  59.9 13.8 %collective-permute-start.15 = (bf16[16,2048]{1,0:T(8,128)(2,1)S(1)}, bf16[16,2048]{1,0:T(8,128)(2,1)S(1)}, u32[]{:S(2)}, u32[]{:S(2)}) collective-permute-start(bf16[16,2048]{1,0:T(8,128)(2,1)S(1)} %get-tuple-element.73), channel_id=1, source_target_pairs={{0,1},{1,0},{2,3},{3,2},{4,5},{5,4},{6,7},{7,6},{8,9},{9,8},{10,11... | collective-permute-start | bytes 196616 | tf_op jit(solution)/shard_map/ppermute | solution.py:492
  60.2 6.6 %collective-permute-start.12 = (f32[32,64]{1,0:T(8,128)S(1)}, f32[32,64]{1,0:T(8,128)S(1)}, u32[]{:S(2)}, u32[]{:S(2)}) collective-permute-start(f32[32,64]{1,0:T(8,128)S(1)} %plus.14.refs_4_.left_ref), channel_id=1, source_target_pairs={{0,8},{1,9},{2,10},{3,11},{4,12},{5,13},{6,14},{7,15},{8,0},{9,1},... | collective-permute-start | bytes 24584 | tf_op jit(solution)/shard_map/ppermute | solution.py:492
  66.7 7.0 %collective-permute-start.14 = (bf16[16,2048]{1,0:T(8,128)(2,1)S(1)}, bf16[16,2048]{1,0:T(8,128)(2,1)S(1)}, u32[]{:S(2)}, u32[]{:S(2)}) collective-permute-start(bf16[16,2048]{1,0:T(8,128)(2,1)S(1)} %get-tuple-element.72), channel_id=1, source_target_pairs={{0,1},{1,0},{2,3},{3,2},{4,5},{5,4},{6,7},{7,6},{8,9},{9,8},{10,11... | collective-permute-start | bytes 196616 | tf_op jit(solution)/shard_map/ppermute | solution.py:492
  72.0 1.7 %collective-permute-start.13 = (bf16[16,2048]{1,0:T(8,128)(2,1)S(1)}, bf16[16,2048]{1,0:T(8,128)(2,1)S(1)}, u32[]{:S(2)}, u32[]{:S(2)}) collective-permute-start(bf16[16,2048]{1,0:T(8,128)(2,1)S(1)} %get-tuple-element.71), channel_id=1, source_target_pairs={{0,1},{1,0},{2,3},{3,2},{4,5},{5,4},{6,7},{7,6},{8,9},{9,8},{10,11... | collective-permute-start | bytes 196616 | tf_op jit(solution)/shard_map/ppermute | solution.py:492
  72.5 1.2 %collective-permute-start.17 = (bf16[16,512]{1,0:T(8,128)(2,1)S(1)}, bf16[16,512]{1,0:T(8,128)(2,1)S(1)}, u32[]{:S(2)}, u32[]{:S(2)}) collective-permute-start(bf16[16,512]{1,0:T(8,128)(2,1)S(1)} %get-tuple-element.66.refs_3_), channel_id=1, source_target_pairs={{0,1},{1,0},{2,3},{3,2},{4,5},{5,4},{6,7},{7,6},{8,9},{9,8},{10,11... | collective-permute-start | bytes 49160 | tf_op jit(solution)/shard_map/ppermute | solution.py:492
  74.8 14.1 %all-to-all-start = ((bf16[8,16,1152]{2,1,0:T(8,128)(2,1)}), bf16[8,16,1152]{2,1,0:T(8,128)(2,1)S(1)}, u32[]{:S(2)}, u32[]{:S(2)}) async-start(bf16[8,16,1152]{2,1,0:T(8,128)(2,1)} %merge.1), calls=%async_computation | async-start | bytes 589824 | tf_op jit(solution)/shard_map/all_to_all | solution.py:473

commit v9 on v8

--- a/solution.py
+++ b/solution.py
@@ -203,33 +203,32 @@
     )(down, tenants, *x)
 
 
-def forward_kernel(cut, slots, blocks, first, slot, *refs):
+def forward_kernel(cuts, slots, blocks, first, slot, *refs):
     x = refs[:blocks]
     gate_out, up_out = refs[-2:]
-    gate_weight, up_weight = slot(slots[0]), slot(slots[1])
-    depth = gate_weight.shape[0]
-    at = slice(cut * depth, (cut + 1) * depth)
-    rows = jnp.concatenate([ref[:, at] for ref in x], axis=0)
-    gate = jnp.dot(rows, gate_weight, preferred_element_type=jnp.float32)
-    up = jnp.dot(rows, up_weight, preferred_element_type=jnp.float32)
-    if not first:
-        gate = gate + refs[blocks][...]
-        up = up + refs[blocks + 1][...]
+    gate, up = (0.0, 0.0) if first else (refs[blocks][...], refs[blocks + 1][...])
+    for cut in cuts:
+        gate_weight, up_weight = slot(slots[cut][0]), slot(slots[cut][1])
+        depth = gate_weight.shape[0]
+        at = slice(cut * depth, (cut + 1) * depth)
+        rows = jnp.concatenate([ref[:, at] for ref in x], axis=0)
+        gate = gate + jnp.dot(rows, gate_weight, preferred_element_type=jnp.float32)
+        up = up + jnp.dot(rows, up_weight, preferred_element_type=jnp.float32)
     gate_out[...] = gate
     up_out[...] = up
 
 
-def forward(cut, slots, x, store, sums, fetches, after):
+def forward(cuts, slots, x, store, sums, fetches, after):
     rows = sum(block.shape[0] for block in x)
     depth, hidden = store.shape[0] // SLOTS, store.shape[1]
     result = jax.ShapeDtypeStruct((rows, hidden), jnp.float32)
     store, gate, up = store_call(
-        lambda *refs: forward_kernel(cut, slots, len(x), not sums, *refs),
+        lambda *refs: forward_kernel(cuts, slots, len(x), not sums, *refs),
         store,
         fetches,
         [*x, *sums],
         [result, result],
-        4 * rows * depth * hidden,
+        4 * rows * depth * hidden * len(cuts),
         "forward",
         after=after,
     )
@@ -337,38 +336,31 @@
     adapter_own, adapter_came, out_ref, sums, tiles = refs[2 * CUTS :]
     chips, tile, lanes = out_ref.shape
     tokens = tile // PARTS
-    per_part = (lanes - 128) // 128
+    per_part = lanes // 128
     blocks = PARTS * per_part
-
-    def put(first, value):
-        for k in range(value.shape[1] // 128):
-            sums[first + k] = value[:, k * 128 : (k + 1) * 128]
-
     for cut in range(CUTS):
-        put(cut * blocks // CUTS, own[cut][...] + came[cut][...].astype(jnp.float32))
+        value = own[cut][...] + came[cut][...].astype(jnp.float32)
+        for k in range(blocks // CUTS):
+            sums[cut * blocks // CUTS + k] = value[:, k * 128 : (k + 1) * 128]
     mine = adapter_own[...].astype(jnp.float32)
     other = adapter_came[...].astype(jnp.float32)
-    put(
-        blocks,
-        jnp.where(
-            device % 2 == 0,
-            jnp.concatenate([mine, other], axis=1),
-            jnp.concatenate([other, mine], axis=1),
-        ),
-    )
-    if sums.shape[0] < blocks + PARTS:
-        tiles[per_part] = jnp.zeros(tiles.shape[1:], jnp.float32)
+    pair = jnp.where(
+        device % 2 == 0,
+        jnp.concatenate([mine, other], axis=1),
+        jnp.concatenate([other, mine], axis=1),
+    )
+    of_chip = blocks // chips
+    for k in range(of_chip):
+        sums[device // 2 * of_chip + k] += pair[:, k * 128 : (k + 1) * 128]
     for token in range(tokens):
         of_token = pl.ds(token, chips, stride=tokens)
         for part in range(PARTS):
             to = pl.ds(token * PARTS + part, chips, stride=tile)
             for k in range(per_part):
                 tiles[k, to, :] = sums[part * per_part + k, of_token, :]
-            if blocks + part < sums.shape[0]:
-                tiles[per_part, to, :] = sums[blocks + part, of_token, :]
     for position in range(chips):
         chip = block_owner(device, position, count) // 2
-        for k in range(lanes // 128):
+        for k in range(per_part):
             out_ref[chip, :, k * 128 : (k + 1) * 128] = tiles[
                 k, position * tile : (position + 1) * tile, :
             ].astype(jnp.bfloat16)
@@ -376,15 +368,13 @@
 
 def merge(own, came, adapter_own, adapter_came, own_rows):
     half, depth = own[0].shape
-    width = CUTS * depth
-    pair = 2 * adapter_own.shape[1]
-    lanes = width // PARTS + 128
+    lanes = CUTS * depth // PARTS
     chips, tile = half // own_rows, own_rows * PARTS
     return pl.pallas_call(
         lambda *refs: merge_kernel(2 * chips, *refs),
         out_shape=jax.ShapeDtypeStruct((chips, tile, lanes), jnp.bfloat16),
         scratch_shapes=[
-            pltpu.VMEM(((width + pair) // 128, half, 128), jnp.float32),
+            pltpu.VMEM((CUTS * depth // 128, half, 128), jnp.float32),
             pltpu.VMEM((lanes // 128, chips * tile, 128), jnp.float32),
         ],
         compiler_params=pltpu.CompilerParams(vmem_limit_bytes=40 << 20),
@@ -392,26 +382,16 @@
     )(*own, *came, adapter_own, adapter_came)
 
 
-def final_kernel(pair, came_ref, out_ref, total, adapter):
+def final_kernel(came_ref, out_ref, total):
     chips, tile, lanes = came_ref.shape
     tokens = tile // PARTS
-    blocks = (lanes - 128) // 128
+    blocks = lanes // 128
     for k in range(blocks):
         at = slice(k * 128, (k + 1) * 128)
         value = came_ref[0, :, at].astype(jnp.float32)
         for chip in range(1, chips):
             value = value + came_ref[chip, :, at].astype(jnp.float32)
         total[k] = value
-    adapter[...] = came_ref[:, :, lanes - 128 :].astype(jnp.float32).reshape(adapter.shape)
-    of_pair = pair // 128
-    for token in range(tokens):
-        rows = slice(token * PARTS, (token + 1) * PARTS)
-        for k in range(blocks):
-            chip, part = divmod(k, of_pair)
-            source = pl.ds(
-                chip * tile + token * PARTS + part, PARTS, stride=blocks // of_pair * tile
-            )
-            total[k, rows, :] += adapter[source, :]
     for part in range(PARTS):
         for k in range(blocks):
             at = (part * blocks + k) * 128
@@ -420,16 +400,12 @@
             )
 
 
-def final(came, pair):
+def final(came):
     chips, tile, lanes = came.shape
-    piece = lanes - 128
-    return pl.pallas_call(
-        lambda *refs: final_kernel(pair, *refs),
-        out_shape=jax.ShapeDtypeStruct((tile // PARTS, piece * PARTS), jnp.bfloat16),
-        scratch_shapes=[
-            pltpu.VMEM((piece // 128, tile, 128), jnp.float32),
-            pltpu.VMEM((chips * tile, 128), jnp.float32),
-        ],
+    return pl.pallas_call(
+        final_kernel,
+        out_shape=jax.ShapeDtypeStruct((tile // PARTS, lanes * PARTS), jnp.bfloat16),
+        scratch_shapes=[pltpu.VMEM((lanes // 128, tile, 128), jnp.float32)],
         compiler_params=pltpu.CompilerParams(vmem_limit_bytes=40 << 20),
         name="final",
     )(came)
@@ -536,46 +512,40 @@
     input_span, low = low_part(adapter_down_maps, tenants, x, count)
     sums = []
     slots = {0: (0, 1), 1: (2, 3), 2: (4, 5), 3: (0, 1)}
-    fetches = {
-        0: pair(2, 4, 5), 1: pair(3, 0, 1), 2: [(adapter_up_maps, 0, 2)], 3: []
-    }
     step = 0
-    for cut in range(CUTS):
+    for cuts, fetches in (
+        ((0, 1), pair(2, 4, 5)), ((2,), pair(3, 0, 1)), ((3,), [(adapter_up_maps, 0, 2)])
+    ):
         after = [low]
         if step < len(hops):
             low = plus(low, swapped(low, hops[step]))
             step += 1
-        store, sums = forward(cut, slots[cut], x, store, sums, fetches[cut], after)
+        store, sums = forward(cuts, slots, x, store, sums, fetches, after)
     for hop in hops[step:]:
         low = plus(low, swapped(low, hop))
     store, dgate, dup, low_grad, input_spread = activation(
         2, store, sums, hidden_unit_gradient, low, tenants, count, []
     )
 
-    low_grad = plus(low_grad, swapped(low_grad, hops[0]))
-    step = 1
+    later_hops = hops[1:] + hops[:1]
     parts, arrived = {}, {}
     slots = {3: (0, 1), 2: (4, 5), 1: (2, 3), 0: (0, 1)}
     fetches = {
         3: [(gate_weight, 1, 2)], 2: [(gate_weight, 0, 0)], 1: [(up_weight, 0, 1)], 0: []
     }
     for cut in reversed(range(CUTS)):
-        if cut > 0:
-            after = [low_grad]
-            if step < len(hops):
-                low_grad = plus(low_grad, swapped(low_grad, hops[step]))
-                step += 1
+        after = [low_grad]
+        turns = later_hops[:1] if cut > 0 else later_hops
+        later_hops = later_hops[len(turns) :]
+        for hop in turns:
+            low_grad = plus(low_grad, swapped(low_grad, hop))
         store, own_part, other_part = backward(slots[cut], dgate, dup, store, fetches[cut], after)
-        if cut == 1:
-            for hop in hops[step:]:
-                low_grad = plus(low_grad, swapped(low_grad, hop))
-            adapter_own, adapter_other, grad_spread = adapter_part(
-                low_grad, tenants, adapter_down_maps, count
-            )
-            adapter_came = swapped(adapter_other, 1)
-            after = [adapter_other]
         parts[cut] = own_part
         arrived[cut] = swapped(other_part, 1)
+    adapter_own, adapter_other, grad_spread = adapter_part(
+        low_grad, tenants, adapter_down_maps, count
+    )
+    adapter_came = swapped(adapter_other, 1)
     merged = merge(
         [parts[cut] for cut in range(CUTS)],
         [arrived[cut] for cut in range(CUTS)],
@@ -586,7 +556,7 @@
     exchanged = between_same_cores(merged)
     down_map_gradient = outer(input_span, grad_spread, "down_maps")
     up_map_gradient = outer(input_spread, dgate, "up_maps")
-    return (final(exchanged, 2 * input_span.shape[1]), down_map_gradient, up_map_gradient)
+    return (final(exchanged), down_map_gradient, up_map_gradient)
 
 
 def solution(mesh):

time: 89.8 us -> 87.6 us (0.976)
  Pallas kernels: 60.6 us -> 57.8 us
    pallas_call x12 -> x11, Pallas kernels: 50.6 us -> 47.6 us  [store_call(): pl.pallas_call(body, in_specs=[VMEM] * (n_in + (not new)) + [ANY] * (n_hb...]
    ppermute x18, waiting for transfers between devices: 3.35 us -> 4.51 us  [swapped(): lax.ppermute(block, 'tp', [(i, i ^ hop) for i in range(lax.axis_size('tp'...]
  transfers between devices with their start and end apart: 19 -> 19, of which waited for: 6 -> 6; matrix products, arithmetic and copies ran while one was open for 0% -> 0% of each run, Pallas kernels for 61% -> 59%
where the time goes in v9:
time: 87.6 us; the launch traced here: 87.4 us
  Pallas kernels  57.8 us (66%)
  starting transfers between devices  21.4 us (24%)
  waiting for transfers between devices  7.23 us (8%)
  between operations  0.93 us (1%)
    pallas_call x11, Pallas kernels, store_call(): pl.pallas_call(body, in_specs=[VMEM] * (n_in + (not new)) + [ANY] * (n_hb...  47.6 us
    ppermute x18, starting transfers between devices, swapped(): lax.ppermute(block, 'tp', [(i, i ^ hop) for i in range(lax.axis_size('tp'...  16.5 us
    pallas_call x2, Pallas kernels, outer(): pl.pallas_call(outer_kernel, grid=(height // block,), in_specs=[pl.BlockS...  6.55 us
    all_to_all x1, starting transfers between devices, between_same_cores(): lax.all_to_all(blocks, 'tp', split_axis=0, concat_axis=0, tiled=True, axi...  4.88 us
    ppermute x18, waiting for transfers between devices, swapped(): lax.ppermute(block, 'tp', [(i, i ^ hop) for i in range(lax.axis_size('tp'...  4.51 us
    all_to_all x1, waiting for transfers between devices, between_same_cores(): lax.all_to_all(blocks, 'tp', split_axis=0, concat_axis=0, tiled=True, axi...  2.72 us
  transfers between devices with their start and end apart: 19, of which 6 were waited for; matrix products, arithmetic and copies ran while one was open for 0% of the time, Pallas kernels for 59%

profile of v9, /device:TPU:0, one launch (start us, length us, event | category | flops | bytes accessed | tf_op | source)
XLA Modules:
  0.0 87.4 jit_solution(13867933404353750163)
XLA Ops:
  0.6 0.0 copy-start.2
  0.6 3.1 %collective-permute-start = (bf16[2,8192]{1,0:T(2,128)(2,1)}, bf16[2,8192]{1,0:T(2,128)(2,1)S(1)}, u32[]{:S(2)}, u32[]{:S(2)}) collective-permute-start(bf16[2,8192]{1,0:T(2,128)(2,1)} %refs_0_.4), channel_id=1, source_target_pairs={{0,4},{1,5},{2,6},{3,7},{4,0},{5,1},{6,2},{7,3},{8,12},{9,13},{10,... | collective-permute-start | bytes 98312 | tf_op jit(solution)/shard_map/ppermute | solution.py:468
  3.7 2.6 %collective-permute-start.1 = (bf16[2,8192]{1,0:T(2,128)(2,1)}, bf16[2,8192]{1,0:T(2,128)(2,1)S(1)}, u32[]{:S(2)}, u32[]{:S(2)}) collective-permute-start(bf16[2,8192]{1,0:T(2,128)(2,1)} %refs_0_.4), channel_id=1, source_target_pairs={{0,8},{1,9},{2,10},{3,11},{4,12},{5,13},{6,14},{7,15},{8,0},{9,1},... | collective-permute-start | bytes 98312 | tf_op jit(solution)/shard_map/ppermute | solution.py:468
  6.3 0.0 collective-permute-start.2
  6.3 5.3 %fetch.3 = (bf16[12288,1792]{1,0:T(8,128)(2,1)S(1)}, f32[8,128]{1,0:T(8,128)S(1)}) custom-call(bf16[8192,1792]{1,0:T(8,128)(2,1)} %refs_3_.8, bf16[8192,1792]{1,0:T(8,128)(2,1)} %refs_3_.9), custom_call_target="tpu_custom_call" | custom-call | bytes 14680064 | tf_op jit(solution)/shard_map/fetch/pallas_call | solution.py:96
  11.7 0.0 copy-start
  11.7 0.0 copy-start.3
  11.7 0.0 collective-permute-done.refs_1_
  11.7 0.0 collective-permute-done.1.refs_2_
  11.7 0.5 collective-permute-done.2.refs_3_
  12.2 0.0 copy-done.2
  12.2 0.1 stacked.2.refs_2_.refs_0_
  12.3 1.6 %collective-permute-start.3 = (bf16[8,8192]{1,0:T(8,128)(2,1)S(1)}, bf16[8,8192]{1,0:T(8,128)(2,1)S(1)}, u32[]{:S(2)}, u32[]{:S(2)}) collective-permute-start(bf16[8,8192]{1,0:T(8,128)(2,1)S(1)} %stacked.2.refs_2_.refs_0_), channel_id=1, source_target_pairs={{0,2},{1,3},{2,0},{3,1},{4,6},{5,7},{6,4},{7,5},{8,10},{9,11},{10,... | collective-permute-start | bytes 393224 | tf_op jit(solution)/shard_map/ppermute | solution.py:468
  13.9 3.2 %fetch.4 = (bf16[12288,1792]{1,0:T(8,128)(2,1)S(1)}, f32[8,128]{1,0:T(8,128)S(1)}) custom-call(bf16[12288,1792]{1,0:T(8,128)(2,1)S(1)} %get-tuple-element.38.refs_0_, bf16[8192,1792]{1,0:T(8,128)(2,1)} %refs_3_.8, bf16[8,8192]{1,0:T(8,128)(2,1)S(1)} %stacked.2.refs_2_.refs_0_), custom_call_target="tpu_custom_call", output_to_operand_aliasing={{0}: (0, {})} | custom-call | bytes 7340032 | tf_op jit(solution)/shard_map/fetch/pallas_call | solution.py:96
  17.1 0.3 collective-permute-done.3.refs_1_
  17.4 0.1 collective-permute-start.4
  17.5 1.5 %collective-permute-done.4.refs_3_.refs_2_ = bf16[16,8192]{1,0:T(8,128)(2,1)S(1)} collective-permute-done((bf16[16,8192]{1,0:T(8,128)(2,1)S(1)}, bf16[16,8192]{1,0:T(8,128)(2,1)S(1)}, u32[]{:S(2)}, u32[]{:S(2)}) %collective-permute-start.4) | collective-permute-done | bytes 262176 | tf_op jit(solution)/shard_map/ppermute | solution.py:468
  19.0 0.0 copy-done
  19.0 0.0 copy-done.3
  19.0 0.7 low_part.1
  19.7 0.2 collective-permute-start.5
  19.9 3.8 %fetch.5 = (bf16[12288,1792]{1,0:T(8,128)(2,1)S(1)}, f32[8,128]{1,0:T(8,128)}) custom-call(bf16[12288,1792]{1,0:T(8,128)(2,1)S(1)} %get-tuple-element.40.refs_0_, bf16[8192,1792]{1,0:T(8,128)(2,1)} %refs_3_.9, bf16[16,8192]{1,0:T(8,128)(2,1)S(1)} %stacked.3.refs_2_.refs_1_), custom_call_target="tpu_custom_call", output_to_operand_aliasing={{0}: (0, {})} | custom-call | bytes 7340032 | tf_op jit(solution)/shard_map/fetch/pallas_call | solution.py:96
  23.6 0.0 collective-permute-done.5.right_ref
  23.6 1.6 %collective-permute-start.6 = (f32[32,64]{1,0:T(8,128)S(1)}, f32[32,64]{1,0:T(8,128)S(1)}, u32[]{:S(2)}, u32[]{:S(2)}) collective-permute-start(f32[32,64]{1,0:T(8,128)S(1)} %plus.8.refs_7_.left_ref), channel_id=1, source_target_pairs={{0,2},{1,3},{2,0},{3,1},{4,6},{5,7},{6,4},{7,5},{8,10},{9,11},{10,... | collective-permute-start | bytes 24584 | tf_op jit(solution)/shard_map/ppermute | solution.py:468
  25.2 5.3 %forward.3 = (bf16[12288,1792]{1,0:T(8,128)(2,1)S(1)}, f32[32,1792]{1,0:T(8,128)S(1)}, f32[32,1792]{1,0:T(8,128)S(1)}) custom-call(bf16[12288,1792]{1,0:T(8,128)(2,1)S(1)} %get-tuple-element.42.refs_0_, bf16[16,8192]{1,0:T(8,128)(2,1)S(1)} %stacked.3.refs_2_.refs_1_, ...), custom_call_target="tpu_custom_call", output_to_operand_aliasing={{0}: (0, {})} | custom-call | flops 939524096 | bytes 14680064 | tf_op jit(solution)/shard_map/forward/pallas_call | solution.py:96
  30.6 0.0 collective-permute-done.6.right_ref
  30.6 0.4 collective-permute-start.7
  31.0 5.4 %forward.4 = (bf16[12288,1792]{1,0:T(8,128)(2,1)S(1)}, f32[32,1792]{1,0:T(8,128)S(1)}, f32[32,1792]{1,0:T(8,128)S(1)}) custom-call(bf16[12288,1792]{1,0:T(8,128)(2,1)S(1)} %get-tuple-element.44.refs_0_, bf16[16,8192]{1,0:T(8,128)(2,1)S(1)} %stacked.3.refs_2_.refs_1_, ...), custom_call_target="tpu_custom_call", output_to_operand_aliasing={{0}: (0, {})} | custom-call | flops 469762048 | bytes 14680064 | tf_op jit(solution)/shard_map/forward/pallas_call | solution.py:96
  36.5 0.0 copy-start.1
  36.5 0.0 collective-permute-done.7.right_ref
  36.5 3.6 %collective-permute-start.8 = (f32[32,64]{1,0:T(8,128)S(1)}, f32[32,64]{1,0:T(8,128)S(1)}, u32[]{:S(2)}, u32[]{:S(2)}) collective-permute-start(f32[32,64]{1,0:T(8,128)S(1)} %plus.10.left_ref), channel_id=1, source_target_pairs={{0,8},{1,9},{2,10},{3,11},{4,12},{5,13},{6,14},{7,15},{8,0},{9,1},... | collective-permute-start | bytes 24584 | tf_op jit(solution)/shard_map/ppermute | solution.py:468
  40.1 3.2 %forward.5 = (bf16[12288,1792]{1,0:T(8,128)(2,1)S(1)}, f32[32,1792]{1,0:T(8,128)S(1)}, f32[32,1792]{1,0:T(8,128)S(1)}) custom-call(bf16[12288,1792]{1,0:T(8,128)(2,1)S(1)} %get-tuple-element.47.refs_0_, bf16[16,8192]{1,0:T(8,128)(2,1)S(1)} %stacked.3.refs_2_.refs_1_, ...), custom_call_target="tpu_custom_call", output_to_operand_aliasing={{0}: (0, {})} | custom-call | flops 469762048 | bytes 7340032 | tf_op jit(solution)/shard_map/forward/pallas_call | solution.py:96
  43.2 0.0 collective-permute-done.8.right_ref
  43.3 3.8 %activation.1 = (bf16[12288,1792]{1,0:T(8,128)(2,1)S(1)}, bf16[32,1792]{1,0:T(8,128)(2,1)S(1)}, bf16[32,1792]{1,0:T(8,128)(2,1)S(1)}, f32[32,64]{1,0:T(8,128)S(1)}, bf16[32,2048]{1,0:T(8,128)(2,1)S(1)}) custom-call(bf16[12288,1792]{1,0:T(8,128)(2,1)S(1)} %get-tuple-element.50.refs_0_, ...), custom_call_target="tpu_custom_call", output_to_operand_aliasing={{0}: (0, {})} | custom-call | flops 469762048 | tf_op jit(solution)/shard_map/activation/pallas_call | solution.py:96
  47.1 0.5 collective-permute-start.9
  47.6 4.4 %backward.4 = (bf16[12288,1792]{1,0:T(8,128)(2,1)S(1)}, f32[16,2048]{1,0:T(8,128)S(1)}, bf16[16,2048]{1,0:T(8,128)(2,1)S(1)}) custom-call(bf16[12288,1792]{1,0:T(8,128)(2,1)S(1)} %get-tuple-element.53.refs_0_, bf16[32,1792]{1,0:T(8,128)(2,1)S(1)} %get-tuple-element.54.refs_1_.right_ref, ...), custom_call_target="tpu_custom_call", output_to_operand_aliasing={{0}: (0, {})} | custom-call | flops 469762048 | bytes 7340032 | tf_op jit(solution)/shard_map/backward/pallas_call | solution.py:96
  52.0 0.1 collective-permute-start.15
  52.1 0.0 collective-permute-done.9.right_ref
  52.1 0.2 plus.12.refs_4_.left_ref
  52.3 0.1 collective-permute-start.10
  52.4 4.4 %backward.5 = (bf16[12288,1792]{1,0:T(8,128)(2,1)S(1)}, f32[16,2048]{1,0:T(8,128)S(1)}, bf16[16,2048]{1,0:T(8,128)(2,1)S(1)}) custom-call(bf16[12288,1792]{1,0:T(8,128)(2,1)S(1)} %get-tuple-element.57.refs_0_, bf16[32,1792]{1,0:T(8,128)(2,1)S(1)} %get-tuple-element.54.refs_1_.right_ref, ...), custom_call_target="tpu_custom_call", output_to_operand_aliasing={{0}: (0, {})} | custom-call | flops 469762048 | bytes 7340032 | tf_op jit(solution)/shard_map/backward/pallas_call | solution.py:96
  56.9 0.4 collective-permute-start.14
  57.2 0.0 collective-permute-done.10.right_ref
  57.2 1.5 %collective-permute-start.11 = (f32[32,64]{1,0:T(8,128)S(1)}, f32[32,64]{1,0:T(8,128)S(1)}, u32[]{:S(2)}, u32[]{:S(2)}) collective-permute-start(f32[32,64]{1,0:T(8,128)S(1)} %plus.13.refs_4_.left_ref), channel_id=1, source_target_pairs={{0,8},{1,9},{2,10},{3,11},{4,12},{5,13},{6,14},{7,15},{8,0},{9,1},... | collective-permute-start | bytes 24584 | tf_op jit(solution)/shard_map/ppermute | solution.py:468
  58.7 4.4 %backward.6 = (bf16[12288,1792]{1,0:T(8,128)(2,1)S(1)}, f32[16,2048]{1,0:T(8,128)S(1)}, bf16[16,2048]{1,0:T(8,128)(2,1)S(1)}) custom-call(bf16[12288,1792]{1,0:T(8,128)(2,1)S(1)} %get-tuple-element.58.refs_0_, bf16[32,1792]{1,0:T(8,128)(2,1)S(1)} %get-tuple-element.54.refs_1_.right_ref, ...), custom_call_target="tpu_custom_call", output_to_operand_aliasing={{0}: (0, {})} | custom-call | flops 469762048 | bytes 7340032 | tf_op jit(solution)/shard_map/backward/pallas_call | solution.py:96
  63.2 0.1 collective-permute-start.13
  63.3 0.0 collective-permute-done.11.right_ref
  63.3 4.3 %backward.7 = (bf16[12288,1792]{1,0:T(8,128)(2,1)S(1)}, f32[16,2048]{1,0:T(8,128)S(1)}, bf16[16,2048]{1,0:T(8,128)(2,1)S(1)}) custom-call(bf16[12288,1792]{1,0:T(8,128)(2,1)S(1)} %get-tuple-element.59.refs_0_, bf16[32,1792]{1,0:T(8,128)(2,1)S(1)} %get-tuple-element.54.refs_1_.right_ref, ...), custom_call_target="tpu_custom_call", output_to_operand_aliasing={{0}: (0, {})} | custom-call | flops 469762048 | tf_op jit(solution)/shard_map/backward/pallas_call | solution.py:96
  67.6 0.5 collective-permute-start.12
  68.1 0.1 collective-permute-start.16
  68.2 1.1 %collective-permute-done.16.right_ref = f32[32,64]{1,0:T(8,128)S(1)} collective-permute-done((f32[32,64]{1,0:T(8,128)S(1)}, f32[32,64]{1,0:T(8,128)S(1)}, u32[]{:S(2)}, u32[]{:S(2)}) %collective-permute-start.16) | collective-permute-done | bytes 8224 | tf_op jit(solution)/shard_map/ppermute | solution.py:468
  69.3 0.9 adapter_part.1
  70.2 0.2 collective-permute-start.17
  70.4 1.0 %collective-permute-done.17.refs_9_ = bf16[16,512]{1,0:T(8,128)(2,1)S(1)} collective-permute-done((bf16[16,512]{1,0:T(8,128)(2,1)S(1)}, bf16[16,512]{1,0:T(8,128)(2,1)S(1)}, u32[]{:S(2)}, u32[]{:S(2)}) %collective-permute-start.17) | collective-permute-done | bytes 16416 | tf_op jit(solution)/shard_map/ppermute | solution.py:468
  71.5 0.0 collective-permute-done.15.refs_7_
  71.5 0.0 collective-permute-done.14.refs_6_
  71.5 0.0 collective-permute-done.13.refs_5_
  71.5 0.0 collective-permute-done.12.refs_4_
  71.5 1.1 %merge.1 = bf16[8,16,1024]{2,1,0:T(8,128)(2,1)} custom-call(f32[16,2048]{1,0:T(8,128)S(1)} %get-tuple-element.60.refs_0_, f32[16,2048]{1,0:T(8,128)S(1)} %get-tuple-element.61.refs_1_, f32[16,2048]{1,0:T(8,128)S(1)} %get-tuple-element.62.refs_2_, f32[16,2048]{1,0:T(8,128)S(1)} %get-tuple-element.63.refs_3_, ...), custom_call_target="tpu_custom_call" | custom-call | tf_op jit(solution)/shard_map/merge/pallas_call | solution.py:373
  72.5 4.9 %all-to-all-start = ((bf16[8,16,1024]{2,1,0:T(8,128)(2,1)}), bf16[8,16,1024]{2,1,0:T(8,128)(2,1)S(1)}, u32[]{:S(2)}, u32[]{:S(2)}) async-start(bf16[8,16,1024]{2,1,0:T(8,128)(2,1)} %merge.1), calls=%async_computation | async-start | bytes 524288 | tf_op jit(solution)/shard_map/all_to_all | solution.py:449
  77.4 4.5 %up_maps.1 = bf16[2048,1792]{1,0:T(8,128)(2,1)} custom-call(bf16[32,2048]{1,0:T(8,128)(2,1)S(1)} %get-tuple-element.72.left_ref, bf16[32,1792]{1,0:T(8,128)(2,1)S(1)} %get-tuple-element.54.refs_1_.right_ref), custom_call_target="tpu_custom_call" | custom-call | flops 234881024 | bytes 7340032 | tf_op jit(solution)/shard_map/up_maps/pallas_call | solution.py:426
  81.9 2.1 %down_maps.1 = bf16[512,2048]{1,0:T(8,128)(2,1)} custom-call(bf16[32,512]{1,0:T(8,128)(2,1)S(1)} %get-tuple-element.70.left_ref, bf16[32,2048]{1,0:T(8,128)(2,1)S(1)} %get-tuple-element.71.right_ref), custom_call_target="tpu_custom_call" | custom-call | flops 67108864 | bytes 2097152 | tf_op jit(solution)/shard_map/down_maps/pallas_call | solution.py:426
  84.0 2.7 %all-to-all-done.came_ref = bf16[8,16,1024]{2,1,0:T(8,128)(2,1)S(1)} async-done(((bf16[8,16,1024]{2,1,0:T(8,128)(2,1)}), bf16[8,16,1024]{2,1,0:T(8,128)(2,1)S(1)}, u32[]{:S(2)}, u32[]{:S(2)}) %all-to-all-start) | async-done | bytes 262176 | tf_op jit(solution)/shard_map/all_to_all | solution.py:449
  86.7 0.7 final.1
  (9 shorter events, 0.1 us)
Async XLA Ops:
  0.6 11.6 %copy-start.2 = (bf16[2,8192]{1,0:T(2,128)(2,1)S(1)}, bf16[2,8192]{1,0:T(2,128)(2,1)}, u32[]{:S(2)}) copy-start(bf16[2,8192]{1,0:T(2,128)(2,1)} %refs_0_.4) | copy-start | bytes 98308
  0.6 11.0 %collective-permute-start = (bf16[2,8192]{1,0:T(2,128)(2,1)}, bf16[2,8192]{1,0:T(2,128)(2,1)S(1)}, u32[]{:S(2)}, u32[]{:S(2)}) collective-permute-start(bf16[2,8192]{1,0:T(2,128)(2,1)} %refs_0_.4), channel_id=1, source_target_pairs={{0,4},{1,5},{2,6},{3,7},{4,0},{5,1},{6,2},{7,3},{8,12},{9,13},{10,... | collective-permute-start | bytes 98312 | tf_op jit(solution)/shard_map/ppermute | solution.py:468
  3.7 8.0 %collective-permute-start.1 = (bf16[2,8192]{1,0:T(2,128)(2,1)}, bf16[2,8192]{1,0:T(2,128)(2,1)S(1)}, u32[]{:S(2)}, u32[]{:S(2)}) collective-permute-start(bf16[2,8192]{1,0:T(2,128)(2,1)} %refs_0_.4), channel_id=1, source_target_pairs={{0,8},{1,9},{2,10},{3,11},{4,12},{5,13},{6,14},{7,15},{8,0},{9,1},... | collective-permute-start | bytes 98312 | tf_op jit(solution)/shard_map/ppermute | solution.py:468
  6.3 5.9 %collective-permute-start.2 = (bf16[2,8192]{1,0:T(2,128)(2,1)}, bf16[2,8192]{1,0:T(2,128)(2,1)S(1)}, u32[]{:S(2)}, u32[]{:S(2)}) collective-permute-start(bf16[2,8192]{1,0:T(2,128)(2,1)} %refs_0_.4), channel_id=1, source_target_pairs={{0,12},{1,13},{2,14},{3,15},{4,8},{5,9},{6,10},{7,11},{8,4},{9,5},... | collective-permute-start | bytes 98312 | tf_op jit(solution)/shard_map/ppermute | solution.py:468
  11.7 7.4 %copy-start = (bf16[512,2048]{1,0:T(8,128)(2,1)S(1)}, bf16[512,2048]{1,0:T(8,128)(2,1)}, u32[]{:S(2)}) copy-start(bf16[512,2048]{1,0:T(8,128)(2,1)} %refs_2_.1) | copy-start | bytes 6291460
  11.7 7.4 %copy-start.3 = (s32[32]{0:T(128)S(1)}, s32[32]{0:T(128)}, u32[]{:S(2)}) copy-start(s32[32]{0:T(128)} %param.13) | copy-start | bytes 388
  12.3 5.0 %collective-permute-start.3 = (bf16[8,8192]{1,0:T(8,128)(2,1)S(1)}, bf16[8,8192]{1,0:T(8,128)(2,1)S(1)}, u32[]{:S(2)}, u32[]{:S(2)}) collective-permute-start(bf16[8,8192]{1,0:T(8,128)(2,1)S(1)} %stacked.2.refs_2_.refs_0_), channel_id=1, source_target_pairs={{0,2},{1,3},{2,0},{3,1},{4,6},{5,7},{6,4},{7,5},{8,10},{9,11},{10,... | collective-permute-start | bytes 393224 | tf_op jit(solution)/shard_map/ppermute | solution.py:468
  17.4 1.6 %collective-permute-start.4 = (bf16[16,8192]{1,0:T(8,128)(2,1)S(1)}, bf16[16,8192]{1,0:T(8,128)(2,1)S(1)}, u32[]{:S(2)}, u32[]{:S(2)}) collective-permute-start(bf16[16,8192]{1,0:T(8,128)(2,1)S(1)} %stacked.3.refs_2_.refs_1_), channel_id=1, source_target_pairs={{0,1},{1,0},{2,3},{3,2},{4,5},{5,4},{6,7},{7,6},{8,9},{9,8},{10,11... | collective-permute-start | bytes 786440 | tf_op jit(solution)/shard_map/ppermute | solution.py:468
  19.7 3.9 %collective-permute-start.5 = (f32[32,64]{1,0:T(8,128)S(1)}, f32[32,64]{1,0:T(8,128)S(1)}, u32[]{:S(2)}, u32[]{:S(2)}) collective-permute-start(f32[32,64]{1,0:T(8,128)S(1)} %get-tuple-element.43.refs_5_.left_ref), channel_id=1, source_target_pairs={{0,1},{1,0},{2,3},{3,2},{4,5},{5,4},{6,7},{7,6},{8,9},{9,8},{10,11... | collective-permute-start | bytes 24584 | tf_op jit(solution)/shard_map/ppermute | solution.py:468
  23.6 6.9 %collective-permute-start.6 = (f32[32,64]{1,0:T(8,128)S(1)}, f32[32,64]{1,0:T(8,128)S(1)}, u32[]{:S(2)}, u32[]{:S(2)}) collective-permute-start(f32[32,64]{1,0:T(8,128)S(1)} %plus.8.refs_7_.left_ref), channel_id=1, source_target_pairs={{0,2},{1,3},{2,0},{3,1},{4,6},{5,7},{6,4},{7,5},{8,10},{9,11},{10,... | collective-permute-start | bytes 24584 | tf_op jit(solution)/shard_map/ppermute | solution.py:468
  30.6 5.9 %collective-permute-start.7 = (f32[32,64]{1,0:T(8,128)S(1)}, f32[32,64]{1,0:T(8,128)S(1)}, u32[]{:S(2)}, u32[]{:S(2)}) collective-permute-start(f32[32,64]{1,0:T(8,128)S(1)} %plus.9.refs_6_.left_ref), channel_id=1, source_target_pairs={{0,4},{1,5},{2,6},{3,7},{4,0},{5,1},{6,2},{7,3},{8,12},{9,13},{10,... | collective-permute-start | bytes 24584 | tf_op jit(solution)/shard_map/ppermute | solution.py:468
  36.5 6.8 %copy-start.1 = (bf16[32,1792]{1,0:T(8,128)(2,1)S(1)}, bf16[32,1792]{1,0:T(8,128)(2,1)}, u32[]{:S(2)}) copy-start(bf16[32,1792]{1,0:T(8,128)(2,1)} %refs_3_.6) | copy-start | bytes 344068
  36.5 6.7 %collective-permute-start.8 = (f32[32,64]{1,0:T(8,128)S(1)}, f32[32,64]{1,0:T(8,128)S(1)}, u32[]{:S(2)}, u32[]{:S(2)}) collective-permute-start(f32[32,64]{1,0:T(8,128)S(1)} %plus.10.left_ref), channel_id=1, source_target_pairs={{0,8},{1,9},{2,10},{3,11},{4,12},{5,13},{6,14},{7,15},{8,0},{9,1},... | collective-permute-start | bytes 24584 | tf_op jit(solution)/shard_map/ppermute | solution.py:468
  47.1 5.1 %collective-permute-start.9 = (f32[32,64]{1,0:T(8,128)S(1)}, f32[32,64]{1,0:T(8,128)S(1)}, u32[]{:S(2)}, u32[]{:S(2)}) collective-permute-start(f32[32,64]{1,0:T(8,128)S(1)} %get-tuple-element.56.refs_4_.left_ref), channel_id=1, source_target_pairs={{0,2},{1,3},{2,0},{3,1},{4,6},{5,7},{6,4},{7,5},{8,10},{9,11},{10,... | collective-permute-start | bytes 24584 | tf_op jit(solution)/shard_map/ppermute | solution.py:468
  52.0 19.4 %collective-permute-start.15 = (bf16[16,2048]{1,0:T(8,128)(2,1)S(1)}, bf16[16,2048]{1,0:T(8,128)(2,1)S(1)}, u32[]{:S(2)}, u32[]{:S(2)}) collective-permute-start(bf16[16,2048]{1,0:T(8,128)(2,1)S(1)} %get-tuple-element.67), channel_id=1, source_target_pairs={{0,1},{1,0},{2,3},{3,2},{4,5},{5,4},{6,7},{7,6},{8,9},{9,8},{10,11... | collective-permute-start | bytes 196616 | tf_op jit(solution)/shard_map/ppermute | solution.py:468
  52.3 4.9 %collective-permute-start.10 = (f32[32,64]{1,0:T(8,128)S(1)}, f32[32,64]{1,0:T(8,128)S(1)}, u32[]{:S(2)}, u32[]{:S(2)}) collective-permute-start(f32[32,64]{1,0:T(8,128)S(1)} %plus.12.refs_4_.left_ref), channel_id=1, source_target_pairs={{0,4},{1,5},{2,6},{3,7},{4,0},{5,1},{6,2},{7,3},{8,12},{9,13},{10,... | collective-permute-start | bytes 24584 | tf_op jit(solution)/shard_map/ppermute | solution.py:468
  56.9 14.6 %collective-permute-start.14 = (bf16[16,2048]{1,0:T(8,128)(2,1)S(1)}, bf16[16,2048]{1,0:T(8,128)(2,1)S(1)}, u32[]{:S(2)}, u32[]{:S(2)}) collective-permute-start(bf16[16,2048]{1,0:T(8,128)(2,1)S(1)} %get-tuple-element.66), channel_id=1, source_target_pairs={{0,1},{1,0},{2,3},{3,2},{4,5},{5,4},{6,7},{7,6},{8,9},{9,8},{10,11... | collective-permute-start | bytes 196616 | tf_op jit(solution)/shard_map/ppermute | solution.py:468
  57.2 6.0 %collective-permute-start.11 = (f32[32,64]{1,0:T(8,128)S(1)}, f32[32,64]{1,0:T(8,128)S(1)}, u32[]{:S(2)}, u32[]{:S(2)}) collective-permute-start(f32[32,64]{1,0:T(8,128)S(1)} %plus.13.refs_4_.left_ref), channel_id=1, source_target_pairs={{0,8},{1,9},{2,10},{3,11},{4,12},{5,13},{6,14},{7,15},{8,0},{9,1},... | collective-permute-start | bytes 24584 | tf_op jit(solution)/shard_map/ppermute | solution.py:468
  63.2 8.3 %collective-permute-start.13 = (bf16[16,2048]{1,0:T(8,128)(2,1)S(1)}, bf16[16,2048]{1,0:T(8,128)(2,1)S(1)}, u32[]{:S(2)}, u32[]{:S(2)}) collective-permute-start(bf16[16,2048]{1,0:T(8,128)(2,1)S(1)} %get-tuple-element.65), channel_id=1, source_target_pairs={{0,1},{1,0},{2,3},{3,2},{4,5},{5,4},{6,7},{7,6},{8,9},{9,8},{10,11... | collective-permute-start | bytes 196616 | tf_op jit(solution)/shard_map/ppermute | solution.py:468
  67.6 3.8 %collective-permute-start.12 = (bf16[16,2048]{1,0:T(8,128)(2,1)S(1)}, bf16[16,2048]{1,0:T(8,128)(2,1)S(1)}, u32[]{:S(2)}, u32[]{:S(2)}) collective-permute-start(bf16[16,2048]{1,0:T(8,128)(2,1)S(1)} %get-tuple-element.64), channel_id=1, source_target_pairs={{0,1},{1,0},{2,3},{3,2},{4,5},{5,4},{6,7},{7,6},{8,9},{9,8},{10,11... | collective-permute-start | bytes 196616 | tf_op jit(solution)/shard_map/ppermute | solution.py:468
  68.1 1.2 %collective-permute-start.16 = (f32[32,64]{1,0:T(8,128)S(1)}, f32[32,64]{1,0:T(8,128)S(1)}, u32[]{:S(2)}, u32[]{:S(2)}) collective-permute-start(f32[32,64]{1,0:T(8,128)S(1)} %plus.14.refs_3_.left_ref), channel_id=1, source_target_pairs={{0,1},{1,0},{2,3},{3,2},{4,5},{5,4},{6,7},{7,6},{8,9},{9,8},{10,11... | collective-permute-start | bytes 24584 | tf_op jit(solution)/shard_map/ppermute | solution.py:468
  70.2 1.2 %collective-permute-start.17 = (bf16[16,512]{1,0:T(8,128)(2,1)S(1)}, bf16[16,512]{1,0:T(8,128)(2,1)S(1)}, u32[]{:S(2)}, u32[]{:S(2)}) collective-permute-start(bf16[16,512]{1,0:T(8,128)(2,1)S(1)} %get-tuple-element.69), channel_id=1, source_target_pairs={{0,1},{1,0},{2,3},{3,2},{4,5},{5,4},{6,7},{7,6},{8,9},{9,8},{10,11... | collective-permute-start | bytes 49160 | tf_op jit(solution)/shard_map/ppermute | solution.py:468
  72.5 14.2 %all-to-all-start = ((bf16[8,16,1024]{2,1,0:T(8,128)(2,1)}), bf16[8,16,1024]{2,1,0:T(8,128)(2,1)S(1)}, u32[]{:S(2)}, u32[]{:S(2)}) async-start(bf16[8,16,1024]{2,1,0:T(8,128)(2,1)} %merge.1), calls=%async_computation | async-start | bytes 524288 | tf_op jit(solution)/shard_map/all_to_all | solution.py:449

commit v10 on v9

--- a/solution.py
+++ b/solution.py
@@ -59,7 +59,9 @@
 STORE_GRANT = 10 << 20
 
 
-def store_call(kernel, store, fetches, operands, out_shapes, flops, name, after=()):
+def store_call(
+    kernel, store, fetches, operands, out_shapes, flops, name, after=(), kept=None, scratch_shapes=()
+):
     new = isinstance(store, jax.ShapeDtypeStruct)
     depth = store.shape[0] // SLOTS
     part = depth // COPIES
@@ -70,12 +72,17 @@
     places = [next(i for i, known in enumerate(sources) if known is f[0]) for f in fetches]
     n_in, n_out, n_hbm = len(operands), len(out_shapes), len(sources)
 
+    first_kept = isinstance(kept, jax.ShapeDtypeStruct)
+    kept_in = [] if kept is None or first_kept else [kept]
+    kept_out = [] if kept is None else [pltpu.HBM(kept.shape, kept.dtype)]
+
     def body(*refs):
         if not new:
             refs = refs[1:]
         ins, hbm = refs[:n_in], refs[n_in : n_in + n_hbm]
-        rest = refs[n_in + n_hbm + len(after) :]
-        store_ref, outs, scratch = rest[0], rest[1 : 1 + n_out], rest[1 + n_out :]
+        rest = refs[n_in + n_hbm + len(after) + len(kept_in) :]
+        n_results = n_out + len(kept_out)
+        store_ref, outs, scratch = rest[0], rest[1 : 1 + n_results], rest[1 + n_results :]
         copies = []
         for n, (place, (_, piece, slot)) in enumerate(zip(places, fetches)):
             for k in range(COPIES):
@@ -88,18 +95,26 @@
                 )
         for copy in copies:
             copy.start()
-        kernel(lambda slot: store_ref[slot * depth : (slot + 1) * depth, :], *ins, *outs)
+        own_scratch = scratch[1:] if fetches else scratch
+        kernel(
+            lambda slot: store_ref[slot * depth : (slot + 1) * depth, :], *ins, *outs, *own_scratch
+        )
         for copy in copies:
             copy.wait()
 
     moved = 2 * depth * store.shape[1] * len(fetches)
+    n_before = (not new) + n_in + n_hbm + len(after)
+    aliases = {} if new else {0: 0}
+    if kept_in:
+        aliases[n_before] = 1 + n_out
+    semaphores = [pltpu.SemaphoreType.DMA((COPIES * len(fetches),))] if fetches else []
     return pl.pallas_call(
         body,
-        in_specs=[VMEM] * (n_in + (not new)) + [ANY] * (n_hbm + len(after)),
-        out_specs=[VMEM] * (1 + n_out),
-        out_shape=[pltpu.VMEM(store.shape, store.dtype), *out_shapes],
-        input_output_aliases={} if new else {0: 0},
-        scratch_shapes=[pltpu.SemaphoreType.DMA((COPIES * len(fetches),))] if fetches else [],
+        in_specs=[VMEM] * (n_in + (not new)) + [ANY] * (n_hbm + len(after) + len(kept_in)),
+        out_specs=[VMEM] * (1 + n_out) + [ANY] * len(kept_out),
+        out_shape=[pltpu.VMEM(store.shape, store.dtype), *out_shapes, *kept_out],
+        input_output_aliases=aliases,
+        scratch_shapes=[*semaphores, *scratch_shapes],
         compiler_params=pltpu.CompilerParams(vmem_limit_bytes=STORE_GRANT),
         cost_estimate=pl.CostEstimate(flops=flops, bytes_accessed=moved, transcendentals=0),
         name=name,
@@ -108,6 +123,7 @@
         *operands,
         *[pltpu.with_memory_space_constraint(array, pltpu.HBM) for array in sources],
         *after,
+        *kept_in,
     )
 
 
@@ -277,7 +293,10 @@
     )
 
 
-def adapter_kernel(count, low_ref, tenants_ref, down_ref, own_out, other_out, spread_ref):
+def adapter_kernel(
+    count, low_ref, tenants_ref, down_ref, after_ref, own_out, other_out, spread_ref
+):
+    del after_ref
     half = own_out.shape[0]
     pick = pick_held(lax.axis_index("tp"), 2 * half, count)
     spread = spread_rows(picked(pick, low_ref[...]), held_mask(pick, tenants_ref[...]))
@@ -287,36 +306,47 @@
     other_out[...] = part[half:]
 
 
-def adapter_part(low, tenants, down, count):
+def adapter_part(low, tenants, down, count, after):
     rows, span = low.shape[0], down.shape[0]
     half = jax.ShapeDtypeStruct((rows // 2, span), jnp.bfloat16)
     return pl.pallas_call(
         lambda *refs: adapter_kernel(count, *refs),
+        in_specs=[VMEM] * 3 + [ANY],
         out_shape=[half, half, jax.ShapeDtypeStruct((rows, SPREAD), jnp.bfloat16)],
         compiler_params=pltpu.CompilerParams(vmem_limit_bytes=4 << 20),
         cost_estimate=pl.CostEstimate(
             flops=2 * rows * down.size, bytes_accessed=2 * down.size, transcendentals=0
         ),
         name="adapter_part",
-    )(low, tenants, down)
-
-
-def backward_kernel(slots, slot, dgate_ref, dup_ref, own_out, other_out):
+    )(low, tenants, down, after)
+
+
+def backward_kernel(
+    cut, slots, slot, dgate_ref, dup_ref, spread_ref, own_out, other_out, maps_out, maps, sem
+):
     half = own_out.shape[0]
+    height = maps.shape[0]
+    at = slice(cut * height, (cut + 1) * height)
+    maps[...] = contracted_rows(
+        spread_ref[:, at] * jnp.bfloat16(adapter_scale), dgate_ref[...]
+    ).astype(jnp.bfloat16)
+    copy = pltpu.make_async_copy(maps, maps_out.at[pl.ds(cut * height, height)], sem)
+    copy.start()
     part = contracted_columns(dgate_ref[...], slot(slots[0]))
     part = part + contracted_columns(dup_ref[...], slot(slots[1]))
     own_out[...] = part[:half]
     other_out[...] = part[half:].astype(jnp.bfloat16)
-
-
-def backward(slots, dgate, dup, store, fetches, after):
+    copy.wait()
+
+
+def backward(cut, slots, dgate, dup, spread, maps, store, fetches, after):
     rows, hidden = dgate.shape
     depth = store.shape[0] // SLOTS
     return store_call(
-        lambda *refs: backward_kernel(slots, *refs),
+        lambda *refs: backward_kernel(cut, slots, *refs),
         store,
         fetches,
-        [dgate, dup],
+        [dgate, dup, spread],
         [
             jax.ShapeDtypeStruct((rows // 2, depth), jnp.float32),
             jax.ShapeDtypeStruct((rows // 2, depth), jnp.bfloat16),
@@ -324,17 +354,24 @@
         4 * rows * hidden * depth,
         "backward",
         after=after,
+        kept=maps,
+        scratch_shapes=[
+            pltpu.VMEM((SPREAD // CUTS, hidden), jnp.bfloat16),
+            pltpu.SemaphoreType.DMA,
+        ],
     )
 
 
 PARTS = 8
+DIRECT_CHIPS = 8
 
 
 def merge_kernel(count, *refs):
     device = lax.axis_index("tp")
     own, came = refs[:CUTS], refs[CUTS : 2 * CUTS]
-    adapter_own, adapter_came, out_ref, sums, tiles = refs[2 * CUTS :]
-    chips, tile, lanes = out_ref.shape
+    adapter_own, adapter_came, *outs, sums, tiles = refs[2 * CUTS :]
+    tile, lanes = outs[0].shape[-2:]
+    chips = tiles.shape[1] // tile
     tokens = tile // PARTS
     per_part = lanes // 128
     blocks = PARTS * per_part
@@ -359,9 +396,12 @@
             for k in range(per_part):
                 tiles[k, to, :] = sums[part * per_part + k, of_token, :]
     for position in range(chips):
-        chip = block_owner(device, position, count) // 2
+        if len(outs) == chips:
+            out_ref = outs[position]
+        else:
+            out_ref = outs[0].at[block_owner(device, position, count) // 2]
         for k in range(per_part):
-            out_ref[chip, :, k * 128 : (k + 1) * 128] = tiles[
+            out_ref[:, k * 128 : (k + 1) * 128] = tiles[
                 k, position * tile : (position + 1) * tile, :
             ].astype(jnp.bfloat16)
 
@@ -370,9 +410,13 @@
     half, depth = own[0].shape
     lanes = CUTS * depth // PARTS
     chips, tile = half // own_rows, own_rows * PARTS
+    if chips <= DIRECT_CHIPS:
+        out_shape = [jax.ShapeDtypeStruct((tile, lanes), jnp.bfloat16)] * chips
+    else:
+        out_shape = [jax.ShapeDtypeStruct((chips, tile, lanes), jnp.bfloat16)]
     return pl.pallas_call(
         lambda *refs: merge_kernel(2 * chips, *refs),
-        out_shape=jax.ShapeDtypeStruct((chips, tile, lanes), jnp.bfloat16),
+        out_shape=out_shape,
         scratch_shapes=[
             pltpu.VMEM((CUTS * depth // 128, half, 128), jnp.float32),
             pltpu.VMEM((lanes // 128, chips * tile, 128), jnp.float32),
@@ -382,15 +426,18 @@
     )(*own, *came, adapter_own, adapter_came)
 
 
-def final_kernel(came_ref, out_ref, total):
-    chips, tile, lanes = came_ref.shape
+def final_kernel(*refs):
+    came, (out_ref, total) = refs[:-2], refs[-2:]
+    if len(came) == 1:
+        came = [came[0].at[chip] for chip in range(came[0].shape[0])]
+    tile, lanes = came[0].shape
     tokens = tile // PARTS
     blocks = lanes // 128
     for k in range(blocks):
         at = slice(k * 128, (k + 1) * 128)
-        value = came_ref[0, :, at].astype(jnp.float32)
-        for chip in range(1, chips):
-            value = value + came_ref[chip, :, at].astype(jnp.float32)
+        value = came[0][:, at].astype(jnp.float32)
+        for ref in came[1:]:
+            value = value + ref[:, at].astype(jnp.float32)
         total[k] = value
     for part in range(PARTS):
         for k in range(blocks):
@@ -401,14 +448,14 @@
 
 
 def final(came):
-    chips, tile, lanes = came.shape
+    tile, lanes = came[0].shape[-2:]
     return pl.pallas_call(
         final_kernel,
         out_shape=jax.ShapeDtypeStruct((tile // PARTS, lanes * PARTS), jnp.bfloat16),
         scratch_shapes=[pltpu.VMEM((lanes // 128, tile, 128), jnp.float32)],
         compiler_params=pltpu.CompilerParams(vmem_limit_bytes=40 << 20),
         name="final",
-    )(came)
+    )(*came)
 
 
 def outer_kernel(left_ref, right_ref, out_ref):
@@ -529,6 +576,7 @@
 
     later_hops = hops[1:] + hops[:1]
     parts, arrived = {}, {}
+    up_map_gradient = jax.ShapeDtypeStruct(adapter_up_maps.shape, jnp.bfloat16)
     slots = {3: (0, 1), 2: (4, 5), 1: (2, 3), 0: (0, 1)}
     fetches = {
         3: [(gate_weight, 1, 2)], 2: [(gate_weight, 0, 0)], 1: [(up_weight, 0, 1)], 0: []
@@ -539,11 +587,13 @@
         later_hops = later_hops[len(turns) :]
         for hop in turns:
             low_grad = plus(low_grad, swapped(low_grad, hop))
-        store, own_part, other_part = backward(slots[cut], dgate, dup, store, fetches[cut], after)
+        store, own_part, other_part, up_map_gradient = backward(
+            cut, slots[cut], dgate, dup, input_spread, up_map_gradient, store, fetches[cut], after
+        )
         parts[cut] = own_part
         arrived[cut] = swapped(other_part, 1)
     adapter_own, adapter_other, grad_spread = adapter_part(
-        low_grad, tenants, adapter_down_maps, count
+        low_grad, tenants, adapter_down_maps, count, other_part
     )
     adapter_came = swapped(adapter_other, 1)
     merged = merge(
@@ -553,9 +603,13 @@
         adapter_came,
         own_rows,
     )
-    exchanged = between_same_cores(merged)
+    if count // 2 <= DIRECT_CHIPS:
+        hop_of = [block_owner(0, position, count) for position in range(count // 2)]
+        farthest = sorted(range(1, count // 2), key=lambda position: -hop_of[position])
+        exchanged = [merged[0]] + [swapped(merged[n], hop_of[n]) for n in farthest]
+    else:
+        exchanged = [between_same_cores(merged[0])]
     down_map_gradient = outer(input_span, grad_spread, "down_maps")
-    up_map_gradient = outer(input_spread, dgate, "up_maps")
     return (final(exchanged), down_map_gradient, up_map_gradient)
 
 

time: 87.6 us -> 93.3 us (1.065)
  starting transfers between devices: 21.4 us -> 28 us
  waiting for transfers between devices: 7.23 us -> 5.85 us
    ppermute x18 -> x25, starting transfers between devices: 16.5 us -> 28 us  [swapped(): lax.ppermute(block, 'tp', [(i, i ^ hop) for i in range(lax.axis_size('tp'...]
    pallas_call x11, Pallas kernels: 47.6 us -> 53.6 us  [store_call(): pl.pallas_call(body, in_specs=[VMEM] * (n_in + (not new)) + [ANY] * (n_hb...]
    all_to_all x1 -> x0, starting transfers between devices: 4.88 us -> none  [between_same_cores(): lax.all_to_all(blocks, 'tp', split_axis=0, concat_axis=0, tiled=True, axi...]
    pallas_call x2 -> x1, Pallas kernels: 6.55 us -> 2.05 us  [outer(): pl.pallas_call(outer_kernel, grid=(height // block,), in_specs=[pl.BlockS...]
    all_to_all x1 -> x0, waiting for transfers between devices: 2.72 us -> none  [between_same_cores(): lax.all_to_all(blocks, 'tp', split_axis=0, concat_axis=0, tiled=True, axi...]
    ppermute x18 -> x25, waiting for transfers between devices: 4.51 us -> 5.85 us  [swapped(): lax.ppermute(block, 'tp', [(i, i ^ hop) for i in range(lax.axis_size('tp'...]
  transfers between devices with their start and end apart: 19 -> 25, of which waited for: 6 -> 6; matrix products, arithmetic and copies ran while one was open for 0% -> 0% of each run, Pallas kernels for 59% -> 57%
where the time goes in v10:
time: 93.3 us; the launch traced here: 93.2 us
  Pallas kernels  58.4 us (63%)
  starting transfers between devices  28 us (30%)
  waiting for transfers between devices  5.85 us (6%)
  between operations  0.96 us (1%)
    pallas_call x11, Pallas kernels, store_call(): pl.pallas_call(body, in_specs=[VMEM] * (n_in + (not new)) + [ANY] * (n_hb...  53.6 us
    ppermute x25, starting transfers between devices, swapped(): lax.ppermute(block, 'tp', [(i, i ^ hop) for i in range(lax.axis_size('tp'...  28 us
    ppermute x25, waiting for transfers between devices, swapped(): lax.ppermute(block, 'tp', [(i, i ^ hop) for i in range(lax.axis_size('tp'...  5.85 us
    pallas_call x1, Pallas kernels, outer(): pl.pallas_call(outer_kernel, grid=(height // block,), in_specs=[pl.BlockS...  2.05 us
  transfers between devices with their start and end apart: 25, of which 6 were waited for; matrix products, arithmetic and copies ran while one was open for 0% of the time, Pallas kernels for 57%

profile of v10, /device:TPU:0, one launch (start us, length us, event | category | flops | bytes accessed | tf_op | source)
XLA Modules:
  0.0 93.2 jit_solution(10851623498324552193)
XLA Ops:
  0.6 3.1 %collective-permute-start = (bf16[2,8192]{1,0:T(2,128)(2,1)}, bf16[2,8192]{1,0:T(2,128)(2,1)S(1)}, u32[]{:S(2)}, u32[]{:S(2)}) collective-permute-start(bf16[2,8192]{1,0:T(2,128)(2,1)} %refs_0_.4), channel_id=1, source_target_pairs={{0,4},{1,5},{2,6},{3,7},{4,0},{5,1},{6,2},{7,3},{8,12},{9,13},{10,... | collective-permute-start | bytes 98312 | tf_op jit(solution)/shard_map/ppermute | solution.py:515
  3.7 2.6 %collective-permute-start.1 = (bf16[2,8192]{1,0:T(2,128)(2,1)}, bf16[2,8192]{1,0:T(2,128)(2,1)S(1)}, u32[]{:S(2)}, u32[]{:S(2)}) collective-permute-start(bf16[2,8192]{1,0:T(2,128)(2,1)} %refs_0_.4), channel_id=1, source_target_pairs={{0,8},{1,9},{2,10},{3,11},{4,12},{5,13},{6,14},{7,15},{8,0},{9,1},... | collective-permute-start | bytes 98312 | tf_op jit(solution)/shard_map/ppermute | solution.py:515
  6.3 0.0 collective-permute-start.2
  6.3 5.3 %fetch.3 = (bf16[12288,1792]{1,0:T(8,128)(2,1)S(1)}, f32[8,128]{1,0:T(8,128)S(1)}) custom-call(bf16[8192,1792]{1,0:T(8,128)(2,1)} %refs_4_.6, bf16[8192,1792]{1,0:T(8,128)(2,1)} %refs_4_.7), custom_call_target="tpu_custom_call" | custom-call | bytes 14680064 | tf_op jit(solution)/shard_map/fetch/pallas_call | solution.py:111
  11.7 0.0 copy-start
  11.7 0.0 copy-start.3
  11.7 0.0 collective-permute-done.refs_1_
  11.7 0.0 collective-permute-done.1.refs_2_
  11.7 0.5 collective-permute-done.2.refs_3_
  12.2 0.1 stacked.2.refs_2_.refs_0_
  12.3 1.6 %collective-permute-start.3 = (bf16[8,8192]{1,0:T(8,128)(2,1)S(1)}, bf16[8,8192]{1,0:T(8,128)(2,1)S(1)}, u32[]{:S(2)}, u32[]{:S(2)}) collective-permute-start(bf16[8,8192]{1,0:T(8,128)(2,1)S(1)} %stacked.2.refs_2_.refs_0_), channel_id=1, source_target_pairs={{0,2},{1,3},{2,0},{3,1},{4,6},{5,7},{6,4},{7,5},{8,10},{9,11},{10,... | collective-permute-start | bytes 393224 | tf_op jit(solution)/shard_map/ppermute | solution.py:515
  13.9 3.2 %fetch.4 = (bf16[12288,1792]{1,0:T(8,128)(2,1)S(1)}, f32[8,128]{1,0:T(8,128)S(1)}) custom-call(bf16[12288,1792]{1,0:T(8,128)(2,1)S(1)} %get-tuple-element.50.refs_0_, bf16[8192,1792]{1,0:T(8,128)(2,1)} %refs_4_.6, bf16[8,8192]{1,0:T(8,128)(2,1)S(1)} %stacked.2.refs_2_.refs_0_), custom_call_target="tpu_custom_call", output_to_operand_aliasing={{0}: (0, {})} | custom-call | bytes 7340032 | tf_op jit(solution)/shard_map/fetch/pallas_call | solution.py:111
  17.1 0.3 collective-permute-done.3.refs_1_
  17.4 0.1 collective-permute-start.4
  17.5 1.5 %collective-permute-done.4.refs_3_.refs_2_ = bf16[16,8192]{1,0:T(8,128)(2,1)S(1)} collective-permute-done((bf16[16,8192]{1,0:T(8,128)(2,1)S(1)}, bf16[16,8192]{1,0:T(8,128)(2,1)S(1)}, u32[]{:S(2)}, u32[]{:S(2)}) %collective-permute-start.4) | collective-permute-done | bytes 262176 | tf_op jit(solution)/shard_map/ppermute | solution.py:515
  19.0 0.7 low_part.1
  19.7 0.2 collective-permute-start.5
  19.9 3.8 %fetch.5 = (bf16[12288,1792]{1,0:T(8,128)(2,1)S(1)}, f32[8,128]{1,0:T(8,128)}) custom-call(bf16[12288,1792]{1,0:T(8,128)(2,1)S(1)} %get-tuple-element.52.refs_0_, bf16[8192,1792]{1,0:T(8,128)(2,1)} %refs_4_.7, bf16[16,8192]{1,0:T(8,128)(2,1)S(1)} %stacked.3.refs_2_.refs_1_), custom_call_target="tpu_custom_call", output_to_operand_aliasing={{0}: (0, {})} | custom-call | bytes 7340032 | tf_op jit(solution)/shard_map/fetch/pallas_call | solution.py:111
  23.6 0.0 collective-permute-done.5.right_ref
  23.6 1.6 %collective-permute-start.6 = (f32[32,64]{1,0:T(8,128)S(1)}, f32[32,64]{1,0:T(8,128)S(1)}, u32[]{:S(2)}, u32[]{:S(2)}) collective-permute-start(f32[32,64]{1,0:T(8,128)S(1)} %plus.8.refs_7_.left_ref), channel_id=1, source_target_pairs={{0,2},{1,3},{2,0},{3,1},{4,6},{5,7},{6,4},{7,5},{8,10},{9,11},{10,... | collective-permute-start | bytes 24584 | tf_op jit(solution)/shard_map/ppermute | solution.py:515
  25.2 5.3 %forward.3 = (bf16[12288,1792]{1,0:T(8,128)(2,1)S(1)}, f32[32,1792]{1,0:T(8,128)S(1)}, f32[32,1792]{1,0:T(8,128)S(1)}) custom-call(bf16[12288,1792]{1,0:T(8,128)(2,1)S(1)} %get-tuple-element.54.refs_0_, bf16[16,8192]{1,0:T(8,128)(2,1)S(1)} %stacked.3.refs_2_.refs_1_, ...), custom_call_target="tpu_custom_call", output_to_operand_aliasing={{0}: (0, {})} | custom-call | flops 939524096 | bytes 14680064 | tf_op jit(solution)/shard_map/forward/pallas_call | solution.py:111
  30.6 0.0 collective-permute-done.6.right_ref
  30.6 0.4 collective-permute-start.7
  31.0 5.4 %forward.4 = (bf16[12288,1792]{1,0:T(8,128)(2,1)S(1)}, f32[32,1792]{1,0:T(8,128)S(1)}, f32[32,1792]{1,0:T(8,128)S(1)}) custom-call(bf16[12288,1792]{1,0:T(8,128)(2,1)S(1)} %get-tuple-element.56.refs_0_, bf16[16,8192]{1,0:T(8,128)(2,1)S(1)} %stacked.3.refs_2_.refs_1_, ...), custom_call_target="tpu_custom_call", output_to_operand_aliasing={{0}: (0, {})} | custom-call | flops 469762048 | bytes 14680064 | tf_op jit(solution)/shard_map/forward/pallas_call | solution.py:111
  36.5 0.0 copy-start.1
  36.5 0.0 collective-permute-done.7.right_ref
  36.5 3.6 %collective-permute-start.8 = (f32[32,64]{1,0:T(8,128)S(1)}, f32[32,64]{1,0:T(8,128)S(1)}, u32[]{:S(2)}, u32[]{:S(2)}) collective-permute-start(f32[32,64]{1,0:T(8,128)S(1)} %plus.10.left_ref), channel_id=1, source_target_pairs={{0,8},{1,9},{2,10},{3,11},{4,12},{5,13},{6,14},{7,15},{8,0},{9,1},... | collective-permute-start | bytes 24584 | tf_op jit(solution)/shard_map/ppermute | solution.py:515
  40.1 3.2 %forward.5 = (bf16[12288,1792]{1,0:T(8,128)(2,1)S(1)}, f32[32,1792]{1,0:T(8,128)S(1)}, f32[32,1792]{1,0:T(8,128)S(1)}) custom-call(bf16[12288,1792]{1,0:T(8,128)(2,1)S(1)} %get-tuple-element.59.refs_0_, bf16[16,8192]{1,0:T(8,128)(2,1)S(1)} %stacked.3.refs_2_.refs_1_, ...), custom_call_target="tpu_custom_call", output_to_operand_aliasing={{0}: (0, {})} | custom-call | flops 469762048 | bytes 7340032 | tf_op jit(solution)/shard_map/forward/pallas_call | solution.py:111
  43.2 0.0 collective-permute-done.8.right_ref
  43.3 3.8 %activation.1 = (bf16[12288,1792]{1,0:T(8,128)(2,1)S(1)}, bf16[32,1792]{1,0:T(8,128)(2,1)S(1)}, bf16[32,1792]{1,0:T(8,128)(2,1)S(1)}, f32[32,64]{1,0:T(8,128)S(1)}, bf16[32,2048]{1,0:T(8,128)(2,1)S(1)}) custom-call(bf16[12288,1792]{1,0:T(8,128)(2,1)S(1)} %get-tuple-element.62.refs_0_, ...), custom_call_target="tpu_custom_call", output_to_operand_aliasing={{0}: (0, {})} | custom-call | flops 469762048 | tf_op jit(solution)/shard_map/activation/pallas_call | solution.py:111
  47.1 0.5 collective-permute-start.9
  47.6 6.1 %backward.4 = (bf16[12288,1792]{1,0:T(8,128)(2,1)S(1)}, f32[16,2048]{1,0:T(8,128)S(1)}, bf16[16,2048]{1,0:T(8,128)(2,1)S(1)}, bf16[2048,1792]{1,0:T(8,128)(2,1)}) custom-call(bf16[12288,1792]{1,0:T(8,128)(2,1)S(1)} %get-tuple-element.65.refs_0_, bf16[32,1792]{1,0:T(8,128)(2,1)S(1)} %get-tuple-element.66.refs_1_, ...), custom_call_target="tpu_custom_call", output_to_operand_aliasing={{0}: (0, {})} | custom-call | flops 469762048 | bytes 7340032 | tf_op jit(solution)/shard_map/backward/pallas_call | solution.py:111
  53.7 0.1 collective-permute-start.15
  53.7 0.0 collective-permute-done.9.right_ref
  53.8 0.1 collective-permute-start.10
  53.8 5.9 %backward.5 = (bf16[12288,1792]{1,0:T(8,128)(2,1)S(1)}, f32[16,2048]{1,0:T(8,128)S(1)}, bf16[16,2048]{1,0:T(8,128)(2,1)S(1)}, bf16[2048,1792]{1,0:T(8,128)(2,1)}) custom-call(bf16[12288,1792]{1,0:T(8,128)(2,1)S(1)} %get-tuple-element.70.refs_0_, bf16[32,1792]{1,0:T(8,128)(2,1)S(1)} %get-tuple-element.66.refs_1_, ...), custom_call_target="tpu_custom_call", output_to_operand_aliasing={{0}: (0, {}), {3}: (6, {})} | custom-call | flops 469762048 | bytes 7340032 | tf_op jit(solution)/shard_map/backward/pallas_call | solution.py:111
  59.7 0.6 collective-permute-start.14
  60.3 0.0 collective-permute-done.10.right_ref
  60.3 1.5 %collective-permute-start.11 = (f32[32,64]{1,0:T(8,128)S(1)}, f32[32,64]{1,0:T(8,128)S(1)}, u32[]{:S(2)}, u32[]{:S(2)}) collective-permute-start(f32[32,64]{1,0:T(8,128)S(1)} %plus.13.refs_5_.left_ref), channel_id=1, source_target_pairs={{0,8},{1,9},{2,10},{3,11},{4,12},{5,13},{6,14},{7,15},{8,0},{9,1},... | collective-permute-start | bytes 24584 | tf_op jit(solution)/shard_map/ppermute | solution.py:515
  61.8 5.9 %backward.6 = (bf16[12288,1792]{1,0:T(8,128)(2,1)S(1)}, f32[16,2048]{1,0:T(8,128)S(1)}, bf16[16,2048]{1,0:T(8,128)(2,1)S(1)}, bf16[2048,1792]{1,0:T(8,128)(2,1)}) custom-call(bf16[12288,1792]{1,0:T(8,128)(2,1)S(1)} %get-tuple-element.72.refs_0_, bf16[32,1792]{1,0:T(8,128)(2,1)S(1)} %get-tuple-element.66.refs_1_, ...), custom_call_target="tpu_custom_call", output_to_operand_aliasing={{0}: (0, {}), {3}: (6, {})} | custom-call | flops 469762048 | bytes 7340032 | tf_op jit(solution)/shard_map/backward/pallas_call | solution.py:111
  67.7 0.1 collective-permute-start.13
  67.8 5.8 %backward.7 = (bf16[12288,1792]{1,0:T(8,128)(2,1)S(1)}, f32[16,2048]{1,0:T(8,128)S(1)}, bf16[16,2048]{1,0:T(8,128)(2,1)S(1)}, bf16[2048,1792]{1,0:T(8,128)(2,1)}) custom-call(bf16[12288,1792]{1,0:T(8,128)(2,1)S(1)} %get-tuple-element.74.refs_0_, bf16[32,1792]{1,0:T(8,128)(2,1)S(1)} %get-tuple-element.66.refs_1_, ...), custom_call_target="tpu_custom_call", output_to_operand_aliasing={{0}: (0, {}), {3}: (5, {})} | custom-call | flops 469762048 | tf_op jit(solution)/shard_map/backward/pallas_call | solution.py:111
  73.7 0.5 collective-permute-start.12
  74.2 0.1 collective-permute-start.16
  74.3 1.1 %collective-permute-done.16.right_ref = f32[32,64]{1,0:T(8,128)S(1)} collective-permute-done((f32[32,64]{1,0:T(8,128)S(1)}, f32[32,64]{1,0:T(8,128)S(1)}, u32[]{:S(2)}, u32[]{:S(2)}) %collective-permute-start.16) | collective-permute-done | bytes 8224 | tf_op jit(solution)/shard_map/ppermute | solution.py:515
  75.4 0.9 adapter_part.1
  76.3 0.2 collective-permute-start.17
  76.5 1.0 %collective-permute-done.17.refs_9_ = bf16[16,512]{1,0:T(8,128)(2,1)S(1)} collective-permute-done((bf16[16,512]{1,0:T(8,128)(2,1)S(1)}, bf16[16,512]{1,0:T(8,128)(2,1)S(1)}, u32[]{:S(2)}, u32[]{:S(2)}) %collective-permute-start.17) | collective-permute-done | bytes 16416 | tf_op jit(solution)/shard_map/ppermute | solution.py:515
  77.5 0.0 collective-permute-done.14.refs_6_
  77.5 0.0 collective-permute-done.13.refs_5_
  77.5 0.0 collective-permute-done.12.refs_4_
  77.5 0.4 merge.1
  77.9 3.7 %collective-permute-start.18 = (bf16[16,1024]{1,0:T(8,128)(2,1)S(1)}, bf16[16,1024]{1,0:T(8,128)(2,1)S(1)}, u32[]{:S(2)}, u32[]{:S(2)}) collective-permute-start(bf16[16,1024]{1,0:T(8,128)(2,1)S(1)} %get-tuple-element.87), channel_id=1, source_target_pairs={{0,14},{1,15},{2,12},{3,13},{4,10},{5,11},{6,8},{7,9},{8,6},{9,7},... | collective-permute-start | bytes 98312 | tf_op jit(solution)/shard_map/ppermute | solution.py:515
  81.6 1.2 %collective-permute-start.19 = (bf16[16,1024]{1,0:T(8,128)(2,1)S(1)}, bf16[16,1024]{1,0:T(8,128)(2,1)S(1)}, u32[]{:S(2)}, u32[]{:S(2)}) collective-permute-start(bf16[16,1024]{1,0:T(8,128)(2,1)S(1)} %get-tuple-element.88), channel_id=1, source_target_pairs={{0,12},{1,13},{2,14},{3,15},{4,8},{5,9},{6,10},{7,11},{8,4},{9,5},... | collective-permute-start | bytes 98312 | tf_op jit(solution)/shard_map/ppermute | solution.py:515
  82.7 2.9 %collective-permute-start.21 = (bf16[16,1024]{1,0:T(8,128)(2,1)S(1)}, bf16[16,1024]{1,0:T(8,128)(2,1)S(1)}, u32[]{:S(2)}, u32[]{:S(2)}) collective-permute-start(bf16[16,1024]{1,0:T(8,128)(2,1)S(1)} %get-tuple-element.90), channel_id=1, source_target_pairs={{0,8},{1,9},{2,10},{3,11},{4,12},{5,13},{6,14},{7,15},{8,0},{9,1},... | collective-permute-start | bytes 98312 | tf_op jit(solution)/shard_map/ppermute | solution.py:515
  85.6 1.3 %collective-permute-start.22 = (bf16[16,1024]{1,0:T(8,128)(2,1)S(1)}, bf16[16,1024]{1,0:T(8,128)(2,1)S(1)}, u32[]{:S(2)}, u32[]{:S(2)}) collective-permute-start(bf16[16,1024]{1,0:T(8,128)(2,1)S(1)} %get-tuple-element.91), channel_id=1, source_target_pairs={{0,6},{1,7},{2,4},{3,5},{4,2},{5,3},{6,0},{7,1},{8,14},{9,15},{10,... | collective-permute-start | bytes 98312 | tf_op jit(solution)/shard_map/ppermute | solution.py:515
  86.9 1.7 %collective-permute-start.23 = (bf16[16,1024]{1,0:T(8,128)(2,1)S(1)}, bf16[16,1024]{1,0:T(8,128)(2,1)S(1)}, u32[]{:S(2)}, u32[]{:S(2)}) collective-permute-start(bf16[16,1024]{1,0:T(8,128)(2,1)S(1)} %get-tuple-element.92), channel_id=1, source_target_pairs={{0,4},{1,5},{2,6},{3,7},{4,0},{5,1},{6,2},{7,3},{8,12},{9,13},{10,... | collective-permute-start | bytes 98312 | tf_op jit(solution)/shard_map/ppermute | solution.py:515
  88.6 0.0 collective-permute-done.19.refs_2_
  88.6 0.5 collective-permute-start.24
  89.1 2.0 %down_maps.1 = bf16[512,2048]{1,0:T(8,128)(2,1)} custom-call(bf16[32,512]{1,0:T(8,128)(2,1)S(1)} %get-tuple-element.94.left_ref, bf16[32,2048]{1,0:T(8,128)(2,1)S(1)} %get-tuple-element.95.right_ref), custom_call_target="tpu_custom_call" | custom-call | flops 67108864 | bytes 2097152 | tf_op jit(solution)/shard_map/down_maps/pallas_call | solution.py:473
  91.2 0.0 collective-permute-done.22.refs_5_
  91.2 0.0 collective-permute-done.23.refs_6_
  91.2 1.3 %collective-permute-done.24.refs_7_ = bf16[16,1024]{1,0:T(8,128)(2,1)S(1)} collective-permute-done((bf16[16,1024]{1,0:T(8,128)(2,1)S(1)}, bf16[16,1024]{1,0:T(8,128)(2,1)S(1)}, u32[]{:S(2)}, u32[]{:S(2)}) %collective-permute-start.24) | collective-permute-done | bytes 32800 | tf_op jit(solution)/shard_map/ppermute | solution.py:515
  92.5 0.7 final.1
  (20 shorter events, 0.1 us)
Async XLA Ops:
  0.6 11.6 %copy-start.2 = (bf16[2,8192]{1,0:T(2,128)(2,1)S(1)}, bf16[2,8192]{1,0:T(2,128)(2,1)}, u32[]{:S(2)}) copy-start(bf16[2,8192]{1,0:T(2,128)(2,1)} %refs_0_.4) | copy-start | bytes 98308
  0.6 11.0 %collective-permute-start = (bf16[2,8192]{1,0:T(2,128)(2,1)}, bf16[2,8192]{1,0:T(2,128)(2,1)S(1)}, u32[]{:S(2)}, u32[]{:S(2)}) collective-permute-start(bf16[2,8192]{1,0:T(2,128)(2,1)} %refs_0_.4), channel_id=1, source_target_pairs={{0,4},{1,5},{2,6},{3,7},{4,0},{5,1},{6,2},{7,3},{8,12},{9,13},{10,... | collective-permute-start | bytes 98312 | tf_op jit(solution)/shard_map/ppermute | solution.py:515
  3.7 8.0 %collective-permute-start.1 = (bf16[2,8192]{1,0:T(2,128)(2,1)}, bf16[2,8192]{1,0:T(2,128)(2,1)S(1)}, u32[]{:S(2)}, u32[]{:S(2)}) collective-permute-start(bf16[2,8192]{1,0:T(2,128)(2,1)} %refs_0_.4), channel_id=1, source_target_pairs={{0,8},{1,9},{2,10},{3,11},{4,12},{5,13},{6,14},{7,15},{8,0},{9,1},... | collective-permute-start | bytes 98312 | tf_op jit(solution)/shard_map/ppermute | solution.py:515
  6.3 5.9 %collective-permute-start.2 = (bf16[2,8192]{1,0:T(2,128)(2,1)}, bf16[2,8192]{1,0:T(2,128)(2,1)S(1)}, u32[]{:S(2)}, u32[]{:S(2)}) collective-permute-start(bf16[2,8192]{1,0:T(2,128)(2,1)} %refs_0_.4), channel_id=1, source_target_pairs={{0,12},{1,13},{2,14},{3,15},{4,8},{5,9},{6,10},{7,11},{8,4},{9,5},... | collective-permute-start | bytes 98312 | tf_op jit(solution)/shard_map/ppermute | solution.py:515
  11.7 7.4 %copy-start = (bf16[512,2048]{1,0:T(8,128)(2,1)S(1)}, bf16[512,2048]{1,0:T(8,128)(2,1)}, u32[]{:S(2)}) copy-start(bf16[512,2048]{1,0:T(8,128)(2,1)} %refs_2_.1) | copy-start | bytes 6291460
  11.7 7.4 %copy-start.3 = (s32[32]{0:T(128)S(1)}, s32[32]{0:T(128)}, u32[]{:S(2)}) copy-start(s32[32]{0:T(128)} %param.13) | copy-start | bytes 388
  12.3 5.0 %collective-permute-start.3 = (bf16[8,8192]{1,0:T(8,128)(2,1)S(1)}, bf16[8,8192]{1,0:T(8,128)(2,1)S(1)}, u32[]{:S(2)}, u32[]{:S(2)}) collective-permute-start(bf16[8,8192]{1,0:T(8,128)(2,1)S(1)} %stacked.2.refs_2_.refs_0_), channel_id=1, source_target_pairs={{0,2},{1,3},{2,0},{3,1},{4,6},{5,7},{6,4},{7,5},{8,10},{9,11},{10,... | collective-permute-start | bytes 393224 | tf_op jit(solution)/shard_map/ppermute | solution.py:515
  17.4 1.6 %collective-permute-start.4 = (bf16[16,8192]{1,0:T(8,128)(2,1)S(1)}, bf16[16,8192]{1,0:T(8,128)(2,1)S(1)}, u32[]{:S(2)}, u32[]{:S(2)}) collective-permute-start(bf16[16,8192]{1,0:T(8,128)(2,1)S(1)} %stacked.3.refs_2_.refs_1_), channel_id=1, source_target_pairs={{0,1},{1,0},{2,3},{3,2},{4,5},{5,4},{6,7},{7,6},{8,9},{9,8},{10,11... | collective-permute-start | bytes 786440 | tf_op jit(solution)/shard_map/ppermute | solution.py:515
  19.7 3.9 %collective-permute-start.5 = (f32[32,64]{1,0:T(8,128)S(1)}, f32[32,64]{1,0:T(8,128)S(1)}, u32[]{:S(2)}, u32[]{:S(2)}) collective-permute-start(f32[32,64]{1,0:T(8,128)S(1)} %get-tuple-element.55.refs_5_.left_ref), channel_id=1, source_target_pairs={{0,1},{1,0},{2,3},{3,2},{4,5},{5,4},{6,7},{7,6},{8,9},{9,8},{10,11... | collective-permute-start | bytes 24584 | tf_op jit(solution)/shard_map/ppermute | solution.py:515
  23.6 6.9 %collective-permute-start.6 = (f32[32,64]{1,0:T(8,128)S(1)}, f32[32,64]{1,0:T(8,128)S(1)}, u32[]{:S(2)}, u32[]{:S(2)}) collective-permute-start(f32[32,64]{1,0:T(8,128)S(1)} %plus.8.refs_7_.left_ref), channel_id=1, source_target_pairs={{0,2},{1,3},{2,0},{3,1},{4,6},{5,7},{6,4},{7,5},{8,10},{9,11},{10,... | collective-permute-start | bytes 24584 | tf_op jit(solution)/shard_map/ppermute | solution.py:515
  30.6 5.9 %collective-permute-start.7 = (f32[32,64]{1,0:T(8,128)S(1)}, f32[32,64]{1,0:T(8,128)S(1)}, u32[]{:S(2)}, u32[]{:S(2)}) collective-permute-start(f32[32,64]{1,0:T(8,128)S(1)} %plus.9.refs_6_.left_ref), channel_id=1, source_target_pairs={{0,4},{1,5},{2,6},{3,7},{4,0},{5,1},{6,2},{7,3},{8,12},{9,13},{10,... | collective-permute-start | bytes 24584 | tf_op jit(solution)/shard_map/ppermute | solution.py:515
  36.5 6.8 %copy-start.1 = (bf16[32,1792]{1,0:T(8,128)(2,1)S(1)}, bf16[32,1792]{1,0:T(8,128)(2,1)}, u32[]{:S(2)}) copy-start(bf16[32,1792]{1,0:T(8,128)(2,1)} %refs_3_.3) | copy-start | bytes 344068
  36.5 6.7 %collective-permute-start.8 = (f32[32,64]{1,0:T(8,128)S(1)}, f32[32,64]{1,0:T(8,128)S(1)}, u32[]{:S(2)}, u32[]{:S(2)}) collective-permute-start(f32[32,64]{1,0:T(8,128)S(1)} %plus.10.left_ref), channel_id=1, source_target_pairs={{0,8},{1,9},{2,10},{3,11},{4,12},{5,13},{6,14},{7,15},{8,0},{9,1},... | collective-permute-start | bytes 24584 | tf_op jit(solution)/shard_map/ppermute | solution.py:515
  47.1 6.7 %collective-permute-start.9 = (f32[32,64]{1,0:T(8,128)S(1)}, f32[32,64]{1,0:T(8,128)S(1)}, u32[]{:S(2)}, u32[]{:S(2)}) collective-permute-start(f32[32,64]{1,0:T(8,128)S(1)} %get-tuple-element.69.refs_5_.left_ref), channel_id=1, source_target_pairs={{0,2},{1,3},{2,0},{3,1},{4,6},{5,7},{6,4},{7,5},{8,10},{9,11},{10,... | collective-permute-start | bytes 24584 | tf_op jit(solution)/shard_map/ppermute | solution.py:515
  53.7 23.9 %collective-permute-start.15 = (bf16[16,2048]{1,0:T(8,128)(2,1)S(1)}, bf16[16,2048]{1,0:T(8,128)(2,1)S(1)}, u32[]{:S(2)}, u32[]{:S(2)}) collective-permute-start(bf16[16,2048]{1,0:T(8,128)(2,1)S(1)} %get-tuple-element.83), channel_id=1, source_target_pairs={{0,1},{1,0},{2,3},{3,2},{4,5},{5,4},{6,7},{7,6},{8,9},{9,8},{10,11... | collective-permute-start | bytes 196616 | tf_op jit(solution)/shard_map/ppermute | solution.py:515
  53.8 6.5 %collective-permute-start.10 = (f32[32,64]{1,0:T(8,128)S(1)}, f32[32,64]{1,0:T(8,128)S(1)}, u32[]{:S(2)}, u32[]{:S(2)}) collective-permute-start(f32[32,64]{1,0:T(8,128)S(1)} %plus.12.refs_5_.left_ref), channel_id=1, source_target_pairs={{0,4},{1,5},{2,6},{3,7},{4,0},{5,1},{6,2},{7,3},{8,12},{9,13},{10,... | collective-permute-start | bytes 24584 | tf_op jit(solution)/shard_map/ppermute | solution.py:515
  59.7 17.8 %collective-permute-start.14 = (bf16[16,2048]{1,0:T(8,128)(2,1)S(1)}, bf16[16,2048]{1,0:T(8,128)(2,1)S(1)}, u32[]{:S(2)}, u32[]{:S(2)}) collective-permute-start(bf16[16,2048]{1,0:T(8,128)(2,1)S(1)} %get-tuple-element.82), channel_id=1, source_target_pairs={{0,1},{1,0},{2,3},{3,2},{4,5},{5,4},{6,7},{7,6},{8,9},{9,8},{10,11... | collective-permute-start | bytes 196616 | tf_op jit(solution)/shard_map/ppermute | solution.py:515
  60.3 7.5 %collective-permute-start.11 = (f32[32,64]{1,0:T(8,128)S(1)}, f32[32,64]{1,0:T(8,128)S(1)}, u32[]{:S(2)}, u32[]{:S(2)}) collective-permute-start(f32[32,64]{1,0:T(8,128)S(1)} %plus.13.refs_5_.left_ref), channel_id=1, source_target_pairs={{0,8},{1,9},{2,10},{3,11},{4,12},{5,13},{6,14},{7,15},{8,0},{9,1},... | collective-permute-start | bytes 24584 | tf_op jit(solution)/shard_map/ppermute | solution.py:515
  67.7 9.8 %collective-permute-start.13 = (bf16[16,2048]{1,0:T(8,128)(2,1)S(1)}, bf16[16,2048]{1,0:T(8,128)(2,1)S(1)}, u32[]{:S(2)}, u32[]{:S(2)}) collective-permute-start(bf16[16,2048]{1,0:T(8,128)(2,1)S(1)} %get-tuple-element.81), channel_id=1, source_target_pairs={{0,1},{1,0},{2,3},{3,2},{4,5},{5,4},{6,7},{7,6},{8,9},{9,8},{10,11... | collective-permute-start | bytes 196616 | tf_op jit(solution)/shard_map/ppermute | solution.py:515
  73.7 3.9 %collective-permute-start.12 = (bf16[16,2048]{1,0:T(8,128)(2,1)S(1)}, bf16[16,2048]{1,0:T(8,128)(2,1)S(1)}, u32[]{:S(2)}, u32[]{:S(2)}) collective-permute-start(bf16[16,2048]{1,0:T(8,128)(2,1)S(1)} %get-tuple-element.80.refs_3_), channel_id=1, source_target_pairs={{0,1},{1,0},{2,3},{3,2},{4,5},{5,4},{6,7},{7,6},{8,9},{9,8},{10,11... | collective-permute-start | bytes 196616 | tf_op jit(solution)/shard_map/ppermute | solution.py:515
  74.2 1.2 %collective-permute-start.16 = (f32[32,64]{1,0:T(8,128)S(1)}, f32[32,64]{1,0:T(8,128)S(1)}, u32[]{:S(2)}, u32[]{:S(2)}) collective-permute-start(f32[32,64]{1,0:T(8,128)S(1)} %plus.14.refs_4_.left_ref), channel_id=1, source_target_pairs={{0,1},{1,0},{2,3},{3,2},{4,5},{5,4},{6,7},{7,6},{8,9},{9,8},{10,11... | collective-permute-start | bytes 24584 | tf_op jit(solution)/shard_map/ppermute | solution.py:515
  76.3 1.2 %collective-permute-start.17 = (bf16[16,512]{1,0:T(8,128)(2,1)S(1)}, bf16[16,512]{1,0:T(8,128)(2,1)S(1)}, u32[]{:S(2)}, u32[]{:S(2)}) collective-permute-start(bf16[16,512]{1,0:T(8,128)(2,1)S(1)} %get-tuple-element.85), channel_id=1, source_target_pairs={{0,1},{1,0},{2,3},{3,2},{4,5},{5,4},{6,7},{7,6},{8,9},{9,8},{10,11... | collective-permute-start | bytes 49160 | tf_op jit(solution)/shard_map/ppermute | solution.py:515
  77.9 9.0 %collective-permute-start.18 = (bf16[16,1024]{1,0:T(8,128)(2,1)S(1)}, bf16[16,1024]{1,0:T(8,128)(2,1)S(1)}, u32[]{:S(2)}, u32[]{:S(2)}) collective-permute-start(bf16[16,1024]{1,0:T(8,128)(2,1)S(1)} %get-tuple-element.87), channel_id=1, source_target_pairs={{0,14},{1,15},{2,12},{3,13},{4,10},{5,11},{6,8},{7,9},{8,6},{9,7},... | collective-permute-start | bytes 98312 | tf_op jit(solution)/shard_map/ppermute | solution.py:515
  81.6 7.0 %collective-permute-start.19 = (bf16[16,1024]{1,0:T(8,128)(2,1)S(1)}, bf16[16,1024]{1,0:T(8,128)(2,1)S(1)}, u32[]{:S(2)}, u32[]{:S(2)}) collective-permute-start(bf16[16,1024]{1,0:T(8,128)(2,1)S(1)} %get-tuple-element.88), channel_id=1, source_target_pairs={{0,12},{1,13},{2,14},{3,15},{4,8},{5,9},{6,10},{7,11},{8,4},{9,5},... | collective-permute-start | bytes 98312 | tf_op jit(solution)/shard_map/ppermute | solution.py:515
  82.7 8.4 %collective-permute-start.20 = (bf16[16,1024]{1,0:T(8,128)(2,1)S(1)}, bf16[16,1024]{1,0:T(8,128)(2,1)S(1)}, u32[]{:S(2)}, u32[]{:S(2)}) collective-permute-start(bf16[16,1024]{1,0:T(8,128)(2,1)S(1)} %get-tuple-element.89), channel_id=1, source_target_pairs={{0,10},{1,11},{2,8},{3,9},{4,14},{5,15},{6,12},{7,13},{8,2},{9,3},... | collective-permute-start | bytes 98312 | tf_op jit(solution)/shard_map/ppermute | solution.py:515
  82.7 8.4 %collective-permute-start.21 = (bf16[16,1024]{1,0:T(8,128)(2,1)S(1)}, bf16[16,1024]{1,0:T(8,128)(2,1)S(1)}, u32[]{:S(2)}, u32[]{:S(2)}) collective-permute-start(bf16[16,1024]{1,0:T(8,128)(2,1)S(1)} %get-tuple-element.90), channel_id=1, source_target_pairs={{0,8},{1,9},{2,10},{3,11},{4,12},{5,13},{6,14},{7,15},{8,0},{9,1},... | collective-permute-start | bytes 98312 | tf_op jit(solution)/shard_map/ppermute | solution.py:515
  85.6 5.6 %collective-permute-start.22 = (bf16[16,1024]{1,0:T(8,128)(2,1)S(1)}, bf16[16,1024]{1,0:T(8,128)(2,1)S(1)}, u32[]{:S(2)}, u32[]{:S(2)}) collective-permute-start(bf16[16,1024]{1,0:T(8,128)(2,1)S(1)} %get-tuple-element.91), channel_id=1, source_target_pairs={{0,6},{1,7},{2,4},{3,5},{4,2},{5,3},{6,0},{7,1},{8,14},{9,15},{10,... | collective-permute-start | bytes 98312 | tf_op jit(solution)/shard_map/ppermute | solution.py:515
  86.9 4.3 %collective-permute-start.23 = (bf16[16,1024]{1,0:T(8,128)(2,1)S(1)}, bf16[16,1024]{1,0:T(8,128)(2,1)S(1)}, u32[]{:S(2)}, u32[]{:S(2)}) collective-permute-start(bf16[16,1024]{1,0:T(8,128)(2,1)S(1)} %get-tuple-element.92), channel_id=1, source_target_pairs={{0,4},{1,5},{2,6},{3,7},{4,0},{5,1},{6,2},{7,3},{8,12},{9,13},{10,... | collective-permute-start | bytes 98312 | tf_op jit(solution)/shard_map/ppermute | solution.py:515
  88.6 3.9 %collective-permute-start.24 = (bf16[16,1024]{1,0:T(8,128)(2,1)S(1)}, bf16[16,1024]{1,0:T(8,128)(2,1)S(1)}, u32[]{:S(2)}, u32[]{:S(2)}) collective-permute-start(bf16[16,1024]{1,0:T(8,128)(2,1)S(1)} %get-tuple-element.93), channel_id=1, source_target_pairs={{0,2},{1,3},{2,0},{3,1},{4,6},{5,7},{6,4},{7,5},{8,10},{9,11},{10,... | collective-permute-start | bytes 98312 | tf_op jit(solution)/shard_map/ppermute | solution.py:515

commit v11 on v9

--- a/solution.py
+++ b/solution.py
@@ -301,47 +301,42 @@
     )(low, tenants, down)
 
 
-def backward_kernel(slots, slot, dgate_ref, dup_ref, own_out, other_out):
+def backward_kernel(slots, start, height, slot, dgate_ref, dup_ref, own_out, other_out):
     half = own_out.shape[0]
-    part = contracted_columns(dgate_ref[...], slot(slots[0]))
-    part = part + contracted_columns(dup_ref[...], slot(slots[1]))
+    at = slice(start, start + height)
+    part = contracted_columns(dgate_ref[...], slot(slots[0])[at, :])
+    part = part + contracted_columns(dup_ref[...], slot(slots[1])[at, :])
     own_out[...] = part[:half]
     other_out[...] = part[half:].astype(jnp.bfloat16)
 
 
-def backward(slots, dgate, dup, store, fetches, after):
+def backward(slots, start, height, dgate, dup, store, fetches, after):
     rows, hidden = dgate.shape
-    depth = store.shape[0] // SLOTS
     return store_call(
-        lambda *refs: backward_kernel(slots, *refs),
+        lambda *refs: backward_kernel(slots, start, height, *refs),
         store,
         fetches,
         [dgate, dup],
         [
-            jax.ShapeDtypeStruct((rows // 2, depth), jnp.float32),
-            jax.ShapeDtypeStruct((rows // 2, depth), jnp.bfloat16),
-        ],
-        4 * rows * hidden * depth,
+            jax.ShapeDtypeStruct((rows // 2, height), jnp.float32),
+            jax.ShapeDtypeStruct((rows // 2, height), jnp.bfloat16),
+        ],
+        4 * rows * hidden * height,
         "backward",
         after=after,
     )
 
 
-PARTS = 8
-
-
-def merge_kernel(count, *refs):
+def first_halves_kernel(count, adapter_own, adapter_came, *refs):
+    keep_ref, send_ref, sums = refs[-3:]
+    pieces = refs[:-3]
+    half = keep_ref.shape[0]
     device = lax.axis_index("tp")
-    own, came = refs[:CUTS], refs[CUTS : 2 * CUTS]
-    adapter_own, adapter_came, out_ref, sums, tiles = refs[2 * CUTS :]
-    chips, tile, lanes = out_ref.shape
-    tokens = tile // PARTS
-    per_part = lanes // 128
-    blocks = PARTS * per_part
-    for cut in range(CUTS):
-        value = own[cut][...] + came[cut][...].astype(jnp.float32)
-        for k in range(blocks // CUTS):
-            sums[cut * blocks // CUTS + k] = value[:, k * 128 : (k + 1) * 128]
+    at = 0
+    for own, came in zip(pieces[::2], pieces[1::2]):
+        width = own.shape[1]
+        sums[:, at : at + width] = own[...] + came[...].astype(jnp.float32)
+        at += width
     mine = adapter_own[...].astype(jnp.float32)
     other = adapter_came[...].astype(jnp.float32)
     pair = jnp.where(
@@ -349,106 +344,105 @@
         jnp.concatenate([mine, other], axis=1),
         jnp.concatenate([other, mine], axis=1),
     )
-    of_chip = blocks // chips
-    for k in range(of_chip):
-        sums[device // 2 * of_chip + k] += pair[:, k * 128 : (k + 1) * 128]
-    for token in range(tokens):
-        of_token = pl.ds(token, chips, stride=tokens)
-        for part in range(PARTS):
-            to = pl.ds(token * PARTS + part, chips, stride=tile)
-            for k in range(per_part):
-                tiles[k, to, :] = sums[part * per_part + k, of_token, :]
-    for position in range(chips):
-        chip = block_owner(device, position, count) // 2
-        for k in range(per_part):
-            out_ref[chip, :, k * 128 : (k + 1) * 128] = tiles[
-                k, position * tile : (position + 1) * tile, :
-            ].astype(jnp.bfloat16)
-
-
-def merge(own, came, adapter_own, adapter_came, own_rows):
-    half, depth = own[0].shape
-    lanes = CUTS * depth // PARTS
-    chips, tile = half // own_rows, own_rows * PARTS
-    return pl.pallas_call(
-        lambda *refs: merge_kernel(2 * chips, *refs),
-        out_shape=jax.ShapeDtypeStruct((chips, tile, lanes), jnp.bfloat16),
-        scratch_shapes=[
-            pltpu.VMEM((CUTS * depth // 128, half, 128), jnp.float32),
-            pltpu.VMEM((lanes // 128, chips * tile, 128), jnp.float32),
-        ],
+    width = pair.shape[1]
+    sums[:, pl.ds(pl.multiple_of(device // 2 * width, width), width)] += pair
+    keep_ref[...] = sums[:half, :]
+    send_ref[...] = sums[half:, :].astype(jnp.bfloat16)
+
+
+def first_halves(pieces, adapter_own, adapter_came, count):
+    rows = adapter_own.shape[0]
+    width = sum(own.shape[1] for own, _ in pieces)
+    return pl.pallas_call(
+        lambda *refs: first_halves_kernel(count, *refs),
+        out_shape=[
+            jax.ShapeDtypeStruct((rows // 2, width), jnp.float32),
+            jax.ShapeDtypeStruct((rows // 2, width), jnp.bfloat16),
+        ],
+        scratch_shapes=[pltpu.VMEM((rows, width), jnp.float32)],
         compiler_params=pltpu.CompilerParams(vmem_limit_bytes=40 << 20),
-        name="merge",
-    )(*own, *came, adapter_own, adapter_came)
-
-
-def final_kernel(came_ref, out_ref, total):
-    chips, tile, lanes = came_ref.shape
-    tokens = tile // PARTS
-    blocks = lanes // 128
-    for k in range(blocks):
-        at = slice(k * 128, (k + 1) * 128)
-        value = came_ref[0, :, at].astype(jnp.float32)
-        for chip in range(1, chips):
-            value = value + came_ref[chip, :, at].astype(jnp.float32)
-        total[k] = value
-    for part in range(PARTS):
-        for k in range(blocks):
-            at = (part * blocks + k) * 128
-            out_ref[:, at : at + 128] = total[k, pl.ds(part, tokens, stride=PARTS), :].astype(
-                jnp.bfloat16
-            )
-
-
-def final(came):
-    chips, tile, lanes = came.shape
+        name="first_halves",
+    )(adapter_own, adapter_came, *[array for pair in pieces for array in pair])
+
+
+def halves(keep, came, after):
+    rows, width = keep.shape
+
+    def halves_kernel(keep_ref, came_ref, after_ref, keep_out, send_out):
+        del after_ref
+        total = keep_ref[...] + came_ref[...].astype(jnp.float32)
+        keep_out[...] = total[: rows // 2]
+        send_out[...] = total[rows // 2 :].astype(jnp.bfloat16)
+
+    return pl.pallas_call(
+        halves_kernel,
+        in_specs=[VMEM, VMEM, ANY],
+        out_shape=[
+            jax.ShapeDtypeStruct((rows // 2, width), jnp.float32),
+            jax.ShapeDtypeStruct((rows // 2, width), jnp.bfloat16),
+        ],
+        compiler_params=pltpu.CompilerParams(vmem_limit_bytes=40 << 20),
+        name="halves",
+    )(keep, came, after)
+
+
+def final(keep, came, after):
+    def final_kernel(keep_ref, came_ref, after_ref, out_ref):
+        del after_ref
+        out_ref[...] = (keep_ref[...] + came_ref[...].astype(jnp.float32)).astype(jnp.bfloat16)
+
     return pl.pallas_call(
         final_kernel,
-        out_shape=jax.ShapeDtypeStruct((tile // PARTS, lanes * PARTS), jnp.bfloat16),
-        scratch_shapes=[pltpu.VMEM((lanes // 128, tile, 128), jnp.float32)],
+        in_specs=[VMEM, VMEM, ANY],
+        out_shape=jax.ShapeDtypeStruct(keep.shape, jnp.bfloat16),
         compiler_params=pltpu.CompilerParams(vmem_limit_bytes=40 << 20),
         name="final",
-    )(came)
-
-
-def outer_kernel(left_ref, right_ref, out_ref):
+    )(keep, came, after)
+
+
+def outer_kernel(left_ref, right_ref, *refs):
+    out_ref, token_ref = refs[-2:]
     out_ref[...] = contracted_rows(
         left_ref[...] * jnp.bfloat16(adapter_scale), right_ref[...]
     ).astype(jnp.bfloat16)
-
-
-def outer(left, right, name):
+    token_ref[...] = jnp.zeros_like(token_ref)
+
+
+def outer(left, right, name, after, parts=1, part=0, earlier=None):
     rows, height = left.shape
     width = right.shape[1]
-    block = block_of(height, 512)
+    block = block_of(height // parts, 512)
     if block % 128:
-        block = height
+        block = height // parts
+    steps = height // parts // block
+    first = part * steps
+    kept = [] if earlier is None else [earlier]
     return pl.pallas_call(
         outer_kernel,
-        grid=(height // block,),
+        grid=(steps,),
         in_specs=[
-            pl.BlockSpec((rows, block), lambda k: (0, k)),
+            pl.BlockSpec((rows, block), lambda k: (0, k + first)),
             pl.BlockSpec((rows, width), lambda k: (0, 0)),
-        ],
-        out_specs=pl.BlockSpec((block, width), lambda k: (k, 0)),
-        out_shape=jax.ShapeDtypeStruct((height, width), jnp.bfloat16),
+            ANY,
+        ]
+        + [ANY] * len(kept),
+        out_specs=[
+            pl.BlockSpec((block, width), lambda k: (k + first, 0)),
+            pl.BlockSpec((8, 128), lambda k: (0, 0)),
+        ],
+        out_shape=[
+            jax.ShapeDtypeStruct((height, width), jnp.bfloat16),
+            jax.ShapeDtypeStruct((8, 128), jnp.float32),
+        ],
+        input_output_aliases={3: 0} if kept else {},
         compiler_params=pltpu.CompilerParams(vmem_limit_bytes=24 << 20),
         cost_estimate=pl.CostEstimate(
-            flops=2 * rows * height * width, bytes_accessed=2 * height * width, transcendentals=0
+            flops=2 * rows * (height // parts) * width,
+            bytes_accessed=2 * (height // parts) * width,
+            transcendentals=0,
         ),
         name=name,
-    )(left, right)
-
-
-def same_core_groups():
-    count = lax.axis_size("tp")
-    return [list(range(core, count, 2)) for core in range(2)]
-
-
-def between_same_cores(blocks):
-    return lax.all_to_all(
-        blocks, "tp", split_axis=0, concat_axis=0, tiled=True, axis_index_groups=same_core_groups()
-    )
+    )(left, right, after, *kept)
 
 
 def add_kernel(left_ref, right_ref, out_ref):
@@ -528,35 +522,49 @@
     )
 
     later_hops = hops[1:] + hops[:1]
-    parts, arrived = {}, {}
-    slots = {3: (0, 1), 2: (4, 5), 1: (2, 3), 0: (0, 1)}
-    fetches = {
-        3: [(gate_weight, 1, 2)], 2: [(gate_weight, 0, 0)], 1: [(up_weight, 0, 1)], 0: []
-    }
-    for cut in reversed(range(CUTS)):
+    depth = width // CUTS
+    part_list = [
+        (3, (0, 1), 0, depth, [(gate_weight, 1, 2)]),
+        (2, (4, 5), 0, depth, [(gate_weight, 0, 0)]),
+        (1, (2, 3), 0, depth, [(up_weight, 0, 1)]),
+        (0, (0, 1), 0, depth // 2, []),
+        (0, (0, 1), depth // 2, depth // 2, []),
+    ]
+    columns = {}
+    for n, (piece, slots, first, height, fetches) in enumerate(part_list):
         after = [low_grad]
-        turns = later_hops[:1] if cut > 0 else later_hops
-        later_hops = later_hops[len(turns) :]
-        for hop in turns:
-            low_grad = plus(low_grad, swapped(low_grad, hop))
-        store, own_part, other_part = backward(slots[cut], dgate, dup, store, fetches[cut], after)
-        parts[cut] = own_part
-        arrived[cut] = swapped(other_part, 1)
-    adapter_own, adapter_other, grad_spread = adapter_part(
-        low_grad, tenants, adapter_down_maps, count
-    )
-    adapter_came = swapped(adapter_other, 1)
-    merged = merge(
-        [parts[cut] for cut in range(CUTS)],
-        [arrived[cut] for cut in range(CUTS)],
-        adapter_own,
-        adapter_came,
-        own_rows,
-    )
-    exchanged = between_same_cores(merged)
-    down_map_gradient = outer(input_span, grad_spread, "down_maps")
-    up_map_gradient = outer(input_spread, dgate, "up_maps")
-    return (final(exchanged), down_map_gradient, up_map_gradient)
+        if n == len(part_list) - 1:
+            adapter_own, adapter_other, grad_spread = adapter_part(
+                low_grad, tenants, adapter_down_maps, count
+            )
+            adapter_came = swapped(adapter_other, 1)
+            after = [adapter_other]
+        else:
+            turns = later_hops[:1] if n < len(part_list) - 2 else later_hops
+            later_hops = later_hops[len(turns) :]
+            for hop in turns:
+                low_grad = plus(low_grad, swapped(low_grad, hop))
+        store, own_part, other_part = backward(
+            slots, first, height, dgate, dup, store, fetches, after
+        )
+        columns[piece * depth + first] = (own_part, swapped(other_part, 1))
+
+    keep, send = first_halves(
+        [columns[start] for start in sorted(columns)], adapter_own, adapter_came, count
+    )
+    halvings = [block_owner(0, 1 << bit, count) for bit in reversed(range(len(hops) - 1))]
+    up_map_gradient = None
+    for n, hop in enumerate(halvings[:-1]):
+        came = swapped(send, hop)
+        beside = send
+        if n < 2:
+            up_map_gradient, beside = outer(
+                input_spread, dgate, "up_maps", send, 2, n, up_map_gradient
+            )
+        keep, send = halves(keep, came, beside)
+    came = swapped(send, halvings[-1])
+    down_map_gradient, beside = outer(input_span, grad_spread, "down_maps", send)
+    return (final(keep, came, beside), down_map_gradient, up_map_gradient)
 
 
 def solution(mesh):

time: 87.6 us -> 87.2 us (level)
    ppermute x18 -> x22, starting transfers between devices: 16.5 us -> 21.6 us  [swapped(): lax.ppermute(block, 'tp', [(i, i ^ hop) for i in range(lax.axis_size('tp'...]
    all_to_all x1 -> x0, starting transfers between devices: 4.88 us -> none  [between_same_cores(): lax.all_to_all(blocks, 'tp', split_axis=0, concat_axis=0, tiled=True, axi...]
    all_to_all x1 -> x0, waiting for transfers between devices: 2.72 us -> none  [between_same_cores(): lax.all_to_all(blocks, 'tp', split_axis=0, concat_axis=0, tiled=True, axi...]
    ppermute x18 -> x22, waiting for transfers between devices: 4.51 us -> 6.85 us  [swapped(): lax.ppermute(block, 'tp', [(i, i ^ hop) for i in range(lax.axis_size('tp'...]
    pallas_call x4 -> x7, Pallas kernels: 8.29 us -> 8.03 us  [the longest x3 7.21 us: outer(): pl.pallas_call(outer_kernel, grid=(steps,), in_specs=[pl.BlockSpec((rows,...]
    pallas_call x11 -> x12, Pallas kernels: 47.6 us -> 47.7 us  [store_call(): pl.pallas_call(body, in_specs=[VMEM] * (n_in + (not new)) + [ANY] * (n_hb...]
  transfers between devices with their start and end apart: 19 -> 22, of which waited for: 6 -> 7; matrix products, arithmetic and copies ran while one was open for 0% -> 0% of each run, Pallas kernels for 59% -> 60%
where the time goes in v11:
time: 87.2 us; the launch traced here: 87 us
  Pallas kernels  57.6 us (66%)
  starting transfers between devices  21.6 us (25%)
  waiting for transfers between devices  6.85 us (8%)
  between operations  0.95 us (1%)
    pallas_call x12, Pallas kernels, store_call(): pl.pallas_call(body, in_specs=[VMEM] * (n_in + (not new)) + [ANY] * (n_hb...  47.7 us
    ppermute x22, starting transfers between devices, swapped(): lax.ppermute(block, 'tp', [(i, i ^ hop) for i in range(lax.axis_size('tp'...  21.6 us
    pallas_call x3, Pallas kernels, outer(): pl.pallas_call(outer_kernel, grid=(steps,), in_specs=[pl.BlockSpec((rows,...  7.21 us
    ppermute x22, waiting for transfers between devices, swapped(): lax.ppermute(block, 'tp', [(i, i ^ hop) for i in range(lax.axis_size('tp'...  6.85 us
  transfers between devices with their start and end apart: 22, of which 7 were waited for; matrix products, arithmetic and copies ran while one was open for 0% of the time, Pallas kernels for 60%

profile of v11, /device:TPU:0, one launch (start us, length us, event | category | flops | bytes accessed | tf_op | source)
XLA Modules:
  0.0 87.0 jit_solution(7218210009960799694)
XLA Ops:
  0.6 3.1 %collective-permute-start = (bf16[2,8192]{1,0:T(2,128)(2,1)}, bf16[2,8192]{1,0:T(2,128)(2,1)S(1)}, u32[]{:S(2)}, u32[]{:S(2)}) collective-permute-start(bf16[2,8192]{1,0:T(2,128)(2,1)} %refs_0_.4), channel_id=1, source_target_pairs={{0,4},{1,5},{2,6},{3,7},{4,0},{5,1},{6,2},{7,3},{8,12},{9,13},{10,... | collective-permute-start | bytes 98312 | tf_op jit(solution)/shard_map/ppermute | solution.py:462
  3.7 2.6 %collective-permute-start.1 = (bf16[2,8192]{1,0:T(2,128)(2,1)}, bf16[2,8192]{1,0:T(2,128)(2,1)S(1)}, u32[]{:S(2)}, u32[]{:S(2)}) collective-permute-start(bf16[2,8192]{1,0:T(2,128)(2,1)} %refs_0_.4), channel_id=1, source_target_pairs={{0,8},{1,9},{2,10},{3,11},{4,12},{5,13},{6,14},{7,15},{8,0},{9,1},... | collective-permute-start | bytes 98312 | tf_op jit(solution)/shard_map/ppermute | solution.py:462
  6.3 0.0 collective-permute-start.2
  6.3 5.3 %fetch.3 = (bf16[12288,1792]{1,0:T(8,128)(2,1)S(1)}, f32[8,128]{1,0:T(8,128)S(1)}) custom-call(bf16[8192,1792]{1,0:T(8,128)(2,1)} %refs_3_.8, bf16[8192,1792]{1,0:T(8,128)(2,1)} %refs_3_.9), custom_call_target="tpu_custom_call" | custom-call | bytes 14680064 | tf_op jit(solution)/shard_map/fetch/pallas_call | solution.py:96
  11.7 0.0 copy-start
  11.7 0.0 copy-start.3
  11.7 0.0 collective-permute-done.refs_1_
  11.7 0.0 collective-permute-done.1.refs_2_
  11.7 0.5 collective-permute-done.2.refs_3_
  12.2 0.1 stacked.2.refs_2_.refs_0_
  12.3 1.6 %collective-permute-start.3 = (bf16[8,8192]{1,0:T(8,128)(2,1)S(1)}, bf16[8,8192]{1,0:T(8,128)(2,1)S(1)}, u32[]{:S(2)}, u32[]{:S(2)}) collective-permute-start(bf16[8,8192]{1,0:T(8,128)(2,1)S(1)} %stacked.2.refs_2_.refs_0_), channel_id=1, source_target_pairs={{0,2},{1,3},{2,0},{3,1},{4,6},{5,7},{6,4},{7,5},{8,10},{9,11},{10,... | collective-permute-start | bytes 393224 | tf_op jit(solution)/shard_map/ppermute | solution.py:462
  13.9 3.2 %fetch.4 = (bf16[12288,1792]{1,0:T(8,128)(2,1)S(1)}, f32[8,128]{1,0:T(8,128)S(1)}) custom-call(bf16[12288,1792]{1,0:T(8,128)(2,1)S(1)} %get-tuple-element.53.refs_0_, bf16[8192,1792]{1,0:T(8,128)(2,1)} %refs_3_.8, bf16[8,8192]{1,0:T(8,128)(2,1)S(1)} %stacked.2.refs_2_.refs_0_), custom_call_target="tpu_custom_call", output_to_operand_aliasing={{0}: (0, {})} | custom-call | bytes 7340032 | tf_op jit(solution)/shard_map/fetch/pallas_call | solution.py:96
  17.1 0.3 collective-permute-done.3.refs_1_
  17.4 0.1 collective-permute-start.4
  17.5 1.5 %collective-permute-done.4.refs_3_.refs_2_ = bf16[16,8192]{1,0:T(8,128)(2,1)S(1)} collective-permute-done((bf16[16,8192]{1,0:T(8,128)(2,1)S(1)}, bf16[16,8192]{1,0:T(8,128)(2,1)S(1)}, u32[]{:S(2)}, u32[]{:S(2)}) %collective-permute-start.4) | collective-permute-done | bytes 262176 | tf_op jit(solution)/shard_map/ppermute | solution.py:462
  19.0 0.7 low_part.1
  19.7 0.2 collective-permute-start.5
  19.9 3.8 %fetch.5 = (bf16[12288,1792]{1,0:T(8,128)(2,1)S(1)}, f32[8,128]{1,0:T(8,128)}) custom-call(bf16[12288,1792]{1,0:T(8,128)(2,1)S(1)} %get-tuple-element.55.refs_0_, bf16[8192,1792]{1,0:T(8,128)(2,1)} %refs_3_.9, bf16[16,8192]{1,0:T(8,128)(2,1)S(1)} %stacked.3.refs_2_.refs_1_), custom_call_target="tpu_custom_call", output_to_operand_aliasing={{0}: (0, {})} | custom-call | bytes 7340032 | tf_op jit(solution)/shard_map/fetch/pallas_call | solution.py:96
  23.6 0.0 collective-permute-done.5.right_ref
  23.6 1.6 %collective-permute-start.6 = (f32[32,64]{1,0:T(8,128)S(1)}, f32[32,64]{1,0:T(8,128)S(1)}, u32[]{:S(2)}, u32[]{:S(2)}) collective-permute-start(f32[32,64]{1,0:T(8,128)S(1)} %plus.8.refs_7_.left_ref), channel_id=1, source_target_pairs={{0,2},{1,3},{2,0},{3,1},{4,6},{5,7},{6,4},{7,5},{8,10},{9,11},{10,... | collective-permute-start | bytes 24584 | tf_op jit(solution)/shard_map/ppermute | solution.py:462
  25.2 5.3 %forward.3 = (bf16[12288,1792]{1,0:T(8,128)(2,1)S(1)}, f32[32,1792]{1,0:T(8,128)S(1)}, f32[32,1792]{1,0:T(8,128)S(1)}) custom-call(bf16[12288,1792]{1,0:T(8,128)(2,1)S(1)} %get-tuple-element.57.refs_0_, bf16[16,8192]{1,0:T(8,128)(2,1)S(1)} %stacked.3.refs_2_.refs_1_, ...), custom_call_target="tpu_custom_call", output_to_operand_aliasing={{0}: (0, {})} | custom-call | flops 939524096 | bytes 14680064 | tf_op jit(solution)/shard_map/forward/pallas_call | solution.py:96
  30.6 0.0 collective-permute-done.6.right_ref
  30.6 0.4 collective-permute-start.7
  31.0 5.4 %forward.4 = (bf16[12288,1792]{1,0:T(8,128)(2,1)S(1)}, f32[32,1792]{1,0:T(8,128)S(1)}, f32[32,1792]{1,0:T(8,128)S(1)}) custom-call(bf16[12288,1792]{1,0:T(8,128)(2,1)S(1)} %get-tuple-element.59.refs_0_, bf16[16,8192]{1,0:T(8,128)(2,1)S(1)} %stacked.3.refs_2_.refs_1_, ...), custom_call_target="tpu_custom_call", output_to_operand_aliasing={{0}: (0, {})} | custom-call | flops 469762048 | bytes 14680064 | tf_op jit(solution)/shard_map/forward/pallas_call | solution.py:96
  36.5 0.0 copy-start.1
  36.5 0.0 collective-permute-done.7.right_ref
  36.5 3.6 %collective-permute-start.8 = (f32[32,64]{1,0:T(8,128)S(1)}, f32[32,64]{1,0:T(8,128)S(1)}, u32[]{:S(2)}, u32[]{:S(2)}) collective-permute-start(f32[32,64]{1,0:T(8,128)S(1)} %plus.10.left_ref), channel_id=1, source_target_pairs={{0,8},{1,9},{2,10},{3,11},{4,12},{5,13},{6,14},{7,15},{8,0},{9,1},... | collective-permute-start | bytes 24584 | tf_op jit(solution)/shard_map/ppermute | solution.py:462
  40.1 3.2 %forward.5 = (bf16[12288,1792]{1,0:T(8,128)(2,1)S(1)}, f32[32,1792]{1,0:T(8,128)S(1)}, f32[32,1792]{1,0:T(8,128)S(1)}) custom-call(bf16[12288,1792]{1,0:T(8,128)(2,1)S(1)} %get-tuple-element.62.refs_0_, bf16[16,8192]{1,0:T(8,128)(2,1)S(1)} %stacked.3.refs_2_.refs_1_, ...), custom_call_target="tpu_custom_call", output_to_operand_aliasing={{0}: (0, {})} | custom-call | flops 469762048 | bytes 7340032 | tf_op jit(solution)/shard_map/forward/pallas_call | solution.py:96
  43.2 0.0 collective-permute-done.8.right_ref
  43.3 3.8 %activation.1 = (bf16[12288,1792]{1,0:T(8,128)(2,1)S(1)}, bf16[32,1792]{1,0:T(8,128)(2,1)S(1)}, bf16[32,1792]{1,0:T(8,128)(2,1)S(1)}, f32[32,64]{1,0:T(8,128)S(1)}, bf16[32,2048]{1,0:T(8,128)(2,1)S(1)}) custom-call(bf16[12288,1792]{1,0:T(8,128)(2,1)S(1)} %get-tuple-element.65.refs_0_, ...), custom_call_target="tpu_custom_call", output_to_operand_aliasing={{0}: (0, {})} | custom-call | flops 469762048 | tf_op jit(solution)/shard_map/activation/pallas_call | solution.py:96
  47.1 0.5 collective-permute-start.9
  47.6 4.4 %backward.5 = (bf16[12288,1792]{1,0:T(8,128)(2,1)S(1)}, f32[16,2048]{1,0:T(8,128)S(1)}, bf16[16,2048]{1,0:T(8,128)(2,1)S(1)}) custom-call(bf16[12288,1792]{1,0:T(8,128)(2,1)S(1)} %get-tuple-element.71.refs_0_, bf16[32,1792]{1,0:T(8,128)(2,1)S(1)} %get-tuple-element.72.refs_1_.right_ref, ...), custom_call_target="tpu_custom_call", output_to_operand_aliasing={{0}: (0, {})} | custom-call | flops 469762048 | bytes 7340032 | tf_op jit(solution)/shard_map/backward/pallas_call | solution.py:96
  52.0 0.1 collective-permute-start.18
  52.1 0.2 plus.12.left_ref.refs_4_
  52.3 0.1 collective-permute-start.10
  52.4 4.4 %backward.6 = (bf16[12288,1792]{1,0:T(8,128)(2,1)S(1)}, f32[16,2048]{1,0:T(8,128)S(1)}, bf16[16,2048]{1,0:T(8,128)(2,1)S(1)}) custom-call(bf16[12288,1792]{1,0:T(8,128)(2,1)S(1)} %get-tuple-element.74.refs_0_, bf16[32,1792]{1,0:T(8,128)(2,1)S(1)} %get-tuple-element.72.refs_1_.right_ref, ...), custom_call_target="tpu_custom_call", output_to_operand_aliasing={{0}: (0, {})} | custom-call | flops 469762048 | bytes 7340032 | tf_op jit(solution)/shard_map/backward/pallas_call | solution.py:96
  56.9 0.4 collective-permute-start.17
  57.2 1.5 %collective-permute-start.11 = (f32[32,64]{1,0:T(8,128)S(1)}, f32[32,64]{1,0:T(8,128)S(1)}, u32[]{:S(2)}, u32[]{:S(2)}) collective-permute-start(f32[32,64]{1,0:T(8,128)S(1)} %plus.13.left_ref.refs_4_), channel_id=1, source_target_pairs={{0,8},{1,9},{2,10},{3,11},{4,12},{5,13},{6,14},{7,15},{8,0},{9,1},... | collective-permute-start | bytes 24584 | tf_op jit(solution)/shard_map/ppermute | solution.py:462
  58.7 4.4 %backward.7 = (bf16[12288,1792]{1,0:T(8,128)(2,1)S(1)}, f32[16,2048]{1,0:T(8,128)S(1)}, bf16[16,2048]{1,0:T(8,128)(2,1)S(1)}) custom-call(bf16[12288,1792]{1,0:T(8,128)(2,1)S(1)} %get-tuple-element.75.refs_0_, bf16[32,1792]{1,0:T(8,128)(2,1)S(1)} %get-tuple-element.72.refs_1_.right_ref, ...), custom_call_target="tpu_custom_call", output_to_operand_aliasing={{0}: (0, {})} | custom-call | flops 469762048 | bytes 7340032 | tf_op jit(solution)/shard_map/backward/pallas_call | solution.py:96
  63.2 0.1 collective-permute-start.16
  63.3 0.5 collective-permute-start.12
  63.9 2.2 %backward.8 = (bf16[12288,1792]{1,0:T(8,128)(2,1)S(1)}, f32[16,1024]{1,0:T(8,128)S(1)}, bf16[16,1024]{1,0:T(8,128)(2,1)S(1)}) custom-call(bf16[12288,1792]{1,0:T(8,128)(2,1)S(1)} %get-tuple-element.76.refs_0_, bf16[32,1792]{1,0:T(8,128)(2,1)S(1)} %get-tuple-element.72.refs_1_.right_ref, ...), custom_call_target="tpu_custom_call", output_to_operand_aliasing={{0}: (0, {})} | custom-call | flops 234881024 | tf_op jit(solution)/shard_map/backward/pallas_call | solution.py:96
  66.1 0.0 collective-permute-start.14
  66.1 0.0 collective-permute-done.12.right_ref
  66.1 0.9 adapter_part.1
  67.0 0.6 collective-permute-start.13
  67.5 2.2 %backward.9 = (bf16[12288,1792]{1,0:T(8,128)(2,1)S(1)}, f32[16,1024]{1,0:T(8,128)S(1)}, bf16[16,1024]{1,0:T(8,128)(2,1)S(1)}) custom-call(bf16[12288,1792]{1,0:T(8,128)(2,1)S(1)} %get-tuple-element.79.refs_0_, bf16[32,1792]{1,0:T(8,128)(2,1)S(1)} %get-tuple-element.72.refs_1_.right_ref, ...), custom_call_target="tpu_custom_call", output_to_operand_aliasing={{0}: (0, {})} | custom-call | flops 234881024 | tf_op jit(solution)/shard_map/backward/pallas_call | solution.py:96
  69.8 0.0 collective-permute-done.13.refs_1_
  69.8 0.1 collective-permute-start.15
  69.9 0.0 collective-permute-done.18.refs_11_
  69.9 1.2 %collective-permute-done.15.refs_5_ = bf16[16,1024]{1,0:T(8,128)(2,1)S(1)} collective-permute-done((bf16[16,1024]{1,0:T(8,128)(2,1)S(1)}, bf16[16,1024]{1,0:T(8,128)(2,1)S(1)}, u32[]{:S(2)}, u32[]{:S(2)}) %collective-permute-start.15) | collective-permute-done | bytes 32800 | tf_op jit(solution)/shard_map/ppermute | solution.py:462
  71.1 0.0 collective-permute-done.17.refs_9_
  71.1 0.0 collective-permute-done.16.refs_7_
  71.1 0.1 first_halves.1
  71.2 1.6 %collective-permute-start.19 = (bf16[8,8192]{1,0:T(8,128)(2,1)S(1)}, bf16[8,8192]{1,0:T(8,128)(2,1)S(1)}, u32[]{:S(2)}, u32[]{:S(2)}) collective-permute-start(bf16[8,8192]{1,0:T(8,128)(2,1)S(1)} %get-tuple-element.89.refs_0_), channel_id=1, source_target_pairs={{0,2},{1,3},{2,0},{3,1},{4,6},{5,7},{6,4},{7,5},{8,10},{9,11},{10,... | collective-permute-start | bytes 393224 | tf_op jit(solution)/shard_map/ppermute | solution.py:462
  72.7 2.6 %up_maps.2 = (bf16[2048,1792]{1,0:T(8,128)(2,1)}, f32[8,128]{1,0:T(8,128)S(1)}) custom-call(bf16[32,2048]{1,0:T(8,128)(2,1)S(1)} %get-tuple-element.90.left_ref, bf16[32,1792]{1,0:T(8,128)(2,1)S(1)} %get-tuple-element.72.refs_1_.right_ref, bf16[8,8192]{1,0:T(8,128)(2,1)S(1)} %get-tuple-element.89.refs_0_), custom_call_target="tpu_custom_call" | custom-call | flops 117440512 | bytes 3670016 | tf_op jit(solution)/shard_map/up_maps/pallas_call | solution.py:420
  75.3 1.5 %collective-permute-done.19.came_ref = bf16[8,8192]{1,0:T(8,128)(2,1)S(1)} collective-permute-done((bf16[8,8192]{1,0:T(8,128)(2,1)S(1)}, bf16[8,8192]{1,0:T(8,128)(2,1)S(1)}, u32[]{:S(2)}, u32[]{:S(2)}) %collective-permute-start.19) | collective-permute-done | bytes 131104 | tf_op jit(solution)/shard_map/ppermute | solution.py:462
  76.8 1.6 %collective-permute-start.20 = (bf16[4,8192]{1,0:T(4,128)(2,1)S(1)}, bf16[4,8192]{1,0:T(4,128)(2,1)S(1)}, u32[]{:S(2)}, u32[]{:S(2)}) collective-permute-start(bf16[4,8192]{1,0:T(4,128)(2,1)S(1)} %get-tuple-element.93.refs_0_), channel_id=1, source_target_pairs={{0,8},{1,9},{2,10},{3,11},{4,12},{5,13},{6,14},{7,15},{8,0},{9,1},... | collective-permute-start | bytes 196616 | tf_op jit(solution)/shard_map/ppermute | solution.py:462
  78.4 2.6 %up_maps.3 = (bf16[2048,1792]{1,0:T(8,128)(2,1)}, f32[8,128]{1,0:T(8,128)S(1)}) custom-call(bf16[32,2048]{1,0:T(8,128)(2,1)S(1)} %get-tuple-element.90.left_ref, bf16[32,1792]{1,0:T(8,128)(2,1)S(1)} %get-tuple-element.72.refs_1_.right_ref, bf16[4,8192]{1,0:T(4,128)(2,1)S(1)} %get-tuple-element.93.refs_0_, ...), custom_call_target="tpu_custom_call", output_to_operand_aliasing={{0}: (3, {})} | custom-call | flops 117440512 | bytes 3670016 | tf_op jit(solution)/shard_map/up_maps/pallas_call | solution.py:420
  81.0 1.4 %collective-permute-done.20.came_ref = bf16[4,8192]{1,0:T(4,128)(2,1)S(1)} collective-permute-done((bf16[4,8192]{1,0:T(4,128)(2,1)S(1)}, bf16[4,8192]{1,0:T(4,128)(2,1)S(1)}, u32[]{:S(2)}, u32[]{:S(2)}) %collective-permute-start.20) | collective-permute-done | bytes 65568 | tf_op jit(solution)/shard_map/ppermute | solution.py:462
  82.4 1.5 %collective-permute-start.21 = (bf16[2,8192]{1,0:T(2,128)(2,1)S(1)}, bf16[2,8192]{1,0:T(2,128)(2,1)S(1)}, u32[]{:S(2)}, u32[]{:S(2)}) collective-permute-start(bf16[2,8192]{1,0:T(2,128)(2,1)S(1)} %get-tuple-element.97.refs_0_), channel_id=1, source_target_pairs={{0,4},{1,5},{2,6},{3,7},{4,0},{5,1},{6,2},{7,3},{8,12},{9,13},{10,... | collective-permute-start | bytes 98312 | tf_op jit(solution)/shard_map/ppermute | solution.py:462
  83.9 2.0 %down_maps.1 = (bf16[512,2048]{1,0:T(8,128)(2,1)}, f32[8,128]{1,0:T(8,128)S(1)}) custom-call(bf16[32,512]{1,0:T(8,128)(2,1)S(1)} %get-tuple-element.98.left_ref, bf16[32,2048]{1,0:T(8,128)(2,1)S(1)} %get-tuple-element.99.right_ref, bf16[2,8192]{1,0:T(2,128)(2,1)S(1)} %get-tuple-element.97.refs_0_), custom_call_target="tpu_custom_call" | custom-call | flops 67108864 | bytes 2097152 | tf_op jit(solution)/shard_map/down_maps/pallas_call | solution.py:420
  86.0 0.4 collective-permute-done.21.came_ref
  86.4 0.7 final.1
  (19 shorter events, 0.2 us)
Async XLA Ops:
  0.6 11.6 %copy-start.2 = (bf16[2,8192]{1,0:T(2,128)(2,1)S(1)}, bf16[2,8192]{1,0:T(2,128)(2,1)}, u32[]{:S(2)}) copy-start(bf16[2,8192]{1,0:T(2,128)(2,1)} %refs_0_.4) | copy-start | bytes 98308
  0.6 11.0 %collective-permute-start = (bf16[2,8192]{1,0:T(2,128)(2,1)}, bf16[2,8192]{1,0:T(2,128)(2,1)S(1)}, u32[]{:S(2)}, u32[]{:S(2)}) collective-permute-start(bf16[2,8192]{1,0:T(2,128)(2,1)} %refs_0_.4), channel_id=1, source_target_pairs={{0,4},{1,5},{2,6},{3,7},{4,0},{5,1},{6,2},{7,3},{8,12},{9,13},{10,... | collective-permute-start | bytes 98312 | tf_op jit(solution)/shard_map/ppermute | solution.py:462
  3.7 8.0 %collective-permute-start.1 = (bf16[2,8192]{1,0:T(2,128)(2,1)}, bf16[2,8192]{1,0:T(2,128)(2,1)S(1)}, u32[]{:S(2)}, u32[]{:S(2)}) collective-permute-start(bf16[2,8192]{1,0:T(2,128)(2,1)} %refs_0_.4), channel_id=1, source_target_pairs={{0,8},{1,9},{2,10},{3,11},{4,12},{5,13},{6,14},{7,15},{8,0},{9,1},... | collective-permute-start | bytes 98312 | tf_op jit(solution)/shard_map/ppermute | solution.py:462
  6.3 5.9 %collective-permute-start.2 = (bf16[2,8192]{1,0:T(2,128)(2,1)}, bf16[2,8192]{1,0:T(2,128)(2,1)S(1)}, u32[]{:S(2)}, u32[]{:S(2)}) collective-permute-start(bf16[2,8192]{1,0:T(2,128)(2,1)} %refs_0_.4), channel_id=1, source_target_pairs={{0,12},{1,13},{2,14},{3,15},{4,8},{5,9},{6,10},{7,11},{8,4},{9,5},... | collective-permute-start | bytes 98312 | tf_op jit(solution)/shard_map/ppermute | solution.py:462
  11.7 7.4 %copy-start = (bf16[512,2048]{1,0:T(8,128)(2,1)S(1)}, bf16[512,2048]{1,0:T(8,128)(2,1)}, u32[]{:S(2)}) copy-start(bf16[512,2048]{1,0:T(8,128)(2,1)} %refs_2_.1) | copy-start | bytes 6291460
  11.7 7.4 %copy-start.3 = (s32[32]{0:T(128)S(1)}, s32[32]{0:T(128)}, u32[]{:S(2)}) copy-start(s32[32]{0:T(128)} %param.13) | copy-start | bytes 388
  12.3 5.0 %collective-permute-start.3 = (bf16[8,8192]{1,0:T(8,128)(2,1)S(1)}, bf16[8,8192]{1,0:T(8,128)(2,1)S(1)}, u32[]{:S(2)}, u32[]{:S(2)}) collective-permute-start(bf16[8,8192]{1,0:T(8,128)(2,1)S(1)} %stacked.2.refs_2_.refs_0_), channel_id=1, source_target_pairs={{0,2},{1,3},{2,0},{3,1},{4,6},{5,7},{6,4},{7,5},{8,10},{9,11},{10,... | collective-permute-start | bytes 393224 | tf_op jit(solution)/shard_map/ppermute | solution.py:462
  17.4 1.6 %collective-permute-start.4 = (bf16[16,8192]{1,0:T(8,128)(2,1)S(1)}, bf16[16,8192]{1,0:T(8,128)(2,1)S(1)}, u32[]{:S(2)}, u32[]{:S(2)}) collective-permute-start(bf16[16,8192]{1,0:T(8,128)(2,1)S(1)} %stacked.3.refs_2_.refs_1_), channel_id=1, source_target_pairs={{0,1},{1,0},{2,3},{3,2},{4,5},{5,4},{6,7},{7,6},{8,9},{9,8},{10,11... | collective-permute-start | bytes 786440 | tf_op jit(solution)/shard_map/ppermute | solution.py:462
  19.7 3.9 %collective-permute-start.5 = (f32[32,64]{1,0:T(8,128)S(1)}, f32[32,64]{1,0:T(8,128)S(1)}, u32[]{:S(2)}, u32[]{:S(2)}) collective-permute-start(f32[32,64]{1,0:T(8,128)S(1)} %get-tuple-element.58.refs_5_.left_ref), channel_id=1, source_target_pairs={{0,1},{1,0},{2,3},{3,2},{4,5},{5,4},{6,7},{7,6},{8,9},{9,8},{10,11... | collective-permute-start | bytes 24584 | tf_op jit(solution)/shard_map/ppermute | solution.py:462
  23.6 6.9 %collective-permute-start.6 = (f32[32,64]{1,0:T(8,128)S(1)}, f32[32,64]{1,0:T(8,128)S(1)}, u32[]{:S(2)}, u32[]{:S(2)}) collective-permute-start(f32[32,64]{1,0:T(8,128)S(1)} %plus.8.refs_7_.left_ref), channel_id=1, source_target_pairs={{0,2},{1,3},{2,0},{3,1},{4,6},{5,7},{6,4},{7,5},{8,10},{9,11},{10,... | collective-permute-start | bytes 24584 | tf_op jit(solution)/shard_map/ppermute | solution.py:462
  30.6 5.9 %collective-permute-start.7 = (f32[32,64]{1,0:T(8,128)S(1)}, f32[32,64]{1,0:T(8,128)S(1)}, u32[]{:S(2)}, u32[]{:S(2)}) collective-permute-start(f32[32,64]{1,0:T(8,128)S(1)} %plus.9.refs_6_.left_ref), channel_id=1, source_target_pairs={{0,4},{1,5},{2,6},{3,7},{4,0},{5,1},{6,2},{7,3},{8,12},{9,13},{10,... | collective-permute-start | bytes 24584 | tf_op jit(solution)/shard_map/ppermute | solution.py:462
  36.5 6.8 %copy-start.1 = (bf16[32,1792]{1,0:T(8,128)(2,1)S(1)}, bf16[32,1792]{1,0:T(8,128)(2,1)}, u32[]{:S(2)}) copy-start(bf16[32,1792]{1,0:T(8,128)(2,1)} %refs_3_.6) | copy-start | bytes 344068
  36.5 6.7 %collective-permute-start.8 = (f32[32,64]{1,0:T(8,128)S(1)}, f32[32,64]{1,0:T(8,128)S(1)}, u32[]{:S(2)}, u32[]{:S(2)}) collective-permute-start(f32[32,64]{1,0:T(8,128)S(1)} %plus.10.left_ref), channel_id=1, source_target_pairs={{0,8},{1,9},{2,10},{3,11},{4,12},{5,13},{6,14},{7,15},{8,0},{9,1},... | collective-permute-start | bytes 24584 | tf_op jit(solution)/shard_map/ppermute | solution.py:462
  47.1 5.1 %collective-permute-start.9 = (f32[32,64]{1,0:T(8,128)S(1)}, f32[32,64]{1,0:T(8,128)S(1)}, u32[]{:S(2)}, u32[]{:S(2)}) collective-permute-start(f32[32,64]{1,0:T(8,128)S(1)} %get-tuple-element.68.left_ref.refs_4_), channel_id=1, source_target_pairs={{0,2},{1,3},{2,0},{3,1},{4,6},{5,7},{6,4},{7,5},{8,10},{9,11},{10,... | collective-permute-start | bytes 24584 | tf_op jit(solution)/shard_map/ppermute | solution.py:462
  52.0 17.8 %collective-permute-start.18 = (bf16[16,2048]{1,0:T(8,128)(2,1)S(1)}, bf16[16,2048]{1,0:T(8,128)(2,1)S(1)}, u32[]{:S(2)}, u32[]{:S(2)}) collective-permute-start(bf16[16,2048]{1,0:T(8,128)(2,1)S(1)} %get-tuple-element.87), channel_id=1, source_target_pairs={{0,1},{1,0},{2,3},{3,2},{4,5},{5,4},{6,7},{7,6},{8,9},{9,8},{10,11... | collective-permute-start | bytes 196616 | tf_op jit(solution)/shard_map/ppermute | solution.py:462
  52.3 4.9 %collective-permute-start.10 = (f32[32,64]{1,0:T(8,128)S(1)}, f32[32,64]{1,0:T(8,128)S(1)}, u32[]{:S(2)}, u32[]{:S(2)}) collective-permute-start(f32[32,64]{1,0:T(8,128)S(1)} %plus.12.left_ref.refs_4_), channel_id=1, source_target_pairs={{0,4},{1,5},{2,6},{3,7},{4,0},{5,1},{6,2},{7,3},{8,12},{9,13},{10,... | collective-permute-start | bytes 24584 | tf_op jit(solution)/shard_map/ppermute | solution.py:462
  56.9 14.2 %collective-permute-start.17 = (bf16[16,2048]{1,0:T(8,128)(2,1)S(1)}, bf16[16,2048]{1,0:T(8,128)(2,1)S(1)}, u32[]{:S(2)}, u32[]{:S(2)}) collective-permute-start(bf16[16,2048]{1,0:T(8,128)(2,1)S(1)} %get-tuple-element.85), channel_id=1, source_target_pairs={{0,1},{1,0},{2,3},{3,2},{4,5},{5,4},{6,7},{7,6},{8,9},{9,8},{10,11... | collective-permute-start | bytes 196616 | tf_op jit(solution)/shard_map/ppermute | solution.py:462
  57.2 6.0 %collective-permute-start.11 = (f32[32,64]{1,0:T(8,128)S(1)}, f32[32,64]{1,0:T(8,128)S(1)}, u32[]{:S(2)}, u32[]{:S(2)}) collective-permute-start(f32[32,64]{1,0:T(8,128)S(1)} %plus.13.left_ref.refs_4_), channel_id=1, source_target_pairs={{0,8},{1,9},{2,10},{3,11},{4,12},{5,13},{6,14},{7,15},{8,0},{9,1},... | collective-permute-start | bytes 24584 | tf_op jit(solution)/shard_map/ppermute | solution.py:462
  63.2 7.9 %collective-permute-start.16 = (bf16[16,2048]{1,0:T(8,128)(2,1)S(1)}, bf16[16,2048]{1,0:T(8,128)(2,1)S(1)}, u32[]{:S(2)}, u32[]{:S(2)}) collective-permute-start(bf16[16,2048]{1,0:T(8,128)(2,1)S(1)} %get-tuple-element.83), channel_id=1, source_target_pairs={{0,1},{1,0},{2,3},{3,2},{4,5},{5,4},{6,7},{7,6},{8,9},{9,8},{10,11... | collective-permute-start | bytes 196616 | tf_op jit(solution)/shard_map/ppermute | solution.py:462
  63.3 2.8 %collective-permute-start.12 = (f32[32,64]{1,0:T(8,128)S(1)}, f32[32,64]{1,0:T(8,128)S(1)}, u32[]{:S(2)}, u32[]{:S(2)}) collective-permute-start(f32[32,64]{1,0:T(8,128)S(1)} %plus.14.left_ref.refs_3_), channel_id=1, source_target_pairs={{0,1},{1,0},{2,3},{3,2},{4,5},{5,4},{6,7},{7,6},{8,9},{9,8},{10,11... | collective-permute-start | bytes 24584 | tf_op jit(solution)/shard_map/ppermute | solution.py:462
  66.1 3.8 %collective-permute-start.14 = (bf16[16,1024]{1,0:T(8,128)(2,1)S(1)}, bf16[16,1024]{1,0:T(8,128)(2,1)S(1)}, u32[]{:S(2)}, u32[]{:S(2)}) collective-permute-start(bf16[16,1024]{1,0:T(8,128)(2,1)S(1)} %get-tuple-element.78), channel_id=1, source_target_pairs={{0,1},{1,0},{2,3},{3,2},{4,5},{5,4},{6,7},{7,6},{8,9},{9,8},{10,11... | collective-permute-start | bytes 98312 | tf_op jit(solution)/shard_map/ppermute | solution.py:462
  67.0 2.8 %collective-permute-start.13 = (bf16[16,512]{1,0:T(8,128)(2,1)S(1)}, bf16[16,512]{1,0:T(8,128)(2,1)S(1)}, u32[]{:S(2)}, u32[]{:S(2)}) collective-permute-start(bf16[16,512]{1,0:T(8,128)(2,1)S(1)} %get-tuple-element.70.refs_3_), channel_id=1, source_target_pairs={{0,1},{1,0},{2,3},{3,2},{4,5},{5,4},{6,7},{7,6},{8,9},{9,8},{10,11... | collective-permute-start | bytes 49160 | tf_op jit(solution)/shard_map/ppermute | solution.py:462
  69.8 1.3 %collective-permute-start.15 = (bf16[16,1024]{1,0:T(8,128)(2,1)S(1)}, bf16[16,1024]{1,0:T(8,128)(2,1)S(1)}, u32[]{:S(2)}, u32[]{:S(2)}) collective-permute-start(bf16[16,1024]{1,0:T(8,128)(2,1)S(1)} %get-tuple-element.81), channel_id=1, source_target_pairs={{0,1},{1,0},{2,3},{3,2},{4,5},{5,4},{6,7},{7,6},{8,9},{9,8},{10,11... | collective-permute-start | bytes 98312 | tf_op jit(solution)/shard_map/ppermute | solution.py:462
  71.2 5.6 %collective-permute-start.19 = (bf16[8,8192]{1,0:T(8,128)(2,1)S(1)}, bf16[8,8192]{1,0:T(8,128)(2,1)S(1)}, u32[]{:S(2)}, u32[]{:S(2)}) collective-permute-start(bf16[8,8192]{1,0:T(8,128)(2,1)S(1)} %get-tuple-element.89.refs_0_), channel_id=1, source_target_pairs={{0,2},{1,3},{2,0},{3,1},{4,6},{5,7},{6,4},{7,5},{8,10},{9,11},{10,... | collective-permute-start | bytes 393224 | tf_op jit(solution)/shard_map/ppermute | solution.py:462
  76.8 5.5 %collective-permute-start.20 = (bf16[4,8192]{1,0:T(4,128)(2,1)S(1)}, bf16[4,8192]{1,0:T(4,128)(2,1)S(1)}, u32[]{:S(2)}, u32[]{:S(2)}) collective-permute-start(bf16[4,8192]{1,0:T(4,128)(2,1)S(1)} %get-tuple-element.93.refs_0_), channel_id=1, source_target_pairs={{0,8},{1,9},{2,10},{3,11},{4,12},{5,13},{6,14},{7,15},{8,0},{9,1},... | collective-permute-start | bytes 196616 | tf_op jit(solution)/shard_map/ppermute | solution.py:462
  82.4 4.0 %collective-permute-start.21 = (bf16[2,8192]{1,0:T(2,128)(2,1)S(1)}, bf16[2,8192]{1,0:T(2,128)(2,1)S(1)}, u32[]{:S(2)}, u32[]{:S(2)}) collective-permute-start(bf16[2,8192]{1,0:T(2,128)(2,1)S(1)} %get-tuple-element.97.refs_0_), channel_id=1, source_target_pairs={{0,4},{1,5},{2,6},{3,7},{4,0},{5,1},{6,2},{7,3},{8,12},{9,13},{10,... | collective-permute-start | bytes 98312 | tf_op jit(solution)/shard_map/ppermute | solution.py:462

commit v12 on v11

--- a/solution.py
+++ b/solution.py
@@ -55,6 +55,7 @@
 ANY = pl.BlockSpec(memory_space=pl.ANY)
 CUTS = 4
 COPIES = 8
+STRIP = 256
 SLOTS = 6
 STORE_GRANT = 10 << 20
 
@@ -64,7 +65,7 @@
     depth = store.shape[0] // SLOTS
     part = depth // COPIES
     sources = []
-    for array, _, _ in fetches:
+    for array, *_ in fetches:
         if not any(array is known for known in sources):
             sources.append(array)
     places = [next(i for i, known in enumerate(sources) if known is f[0]) for f in fetches]
@@ -77,8 +78,10 @@
         rest = refs[n_in + n_hbm + len(after) :]
         store_ref, outs, scratch = rest[0], rest[1 : 1 + n_out], rest[1 + n_out :]
         copies = []
-        for n, (place, (_, piece, slot)) in enumerate(zip(places, fetches)):
+        for n, (place, (_, piece, slot, *half)) in enumerate(zip(places, fetches)):
             for k in range(COPIES):
+                if half and k // (COPIES // 2) != half[0]:
+                    continue
                 copies.append(
                     pltpu.make_async_copy(
                         hbm[place].at[pl.ds(piece * depth + k * part, part)],
@@ -88,7 +91,10 @@
                 )
         for copy in copies:
             copy.start()
-        kernel(lambda slot: store_ref[slot * depth : (slot + 1) * depth, :], *ins, *outs)
+        def rows_of(slot, at=slice(0, depth)):
+            return store_ref[slot * depth + at.start : slot * depth + at.stop, :]
+
+        kernel(rows_of, *ins, *outs)
         for copy in copies:
             copy.wait()
 
@@ -161,7 +167,7 @@
 
 
 def low_kernel(count, aligned, down_ref, tenants_ref, *refs):
-    x, (span_out, low_ref) = refs[:-2], refs[-2:]
+    x, (span_out, low_ref) = refs[:-3], refs[-2:]
     own = lax.axis_index("tp")
     if aligned:
         width = down_ref.shape[0]
@@ -176,7 +182,7 @@
     low_ref[...] = picked(pick_given(own, rows, count), low)
 
 
-def low_part(down, tenants, x, count):
+def low_part(down, tenants, x, count, after):
     rows, span = sum(block.shape[0] for block in x), down.shape[0]
     aligned = span % 128 == 0
     if not aligned:
@@ -191,6 +197,7 @@
         ]
     return pl.pallas_call(
         lambda *refs: low_kernel(count, aligned, *refs),
+        in_specs=[VMEM] * (2 + len(x)) + [ANY],
         out_shape=[
             jax.ShapeDtypeStruct((rows, span), x[0].dtype),
             jax.ShapeDtypeStruct((rows, ADAPTER_RANK), jnp.float32),
@@ -200,7 +207,7 @@
             flops=2 * rows * down.size, bytes_accessed=2 * down.size, transcendentals=0
         ),
         name="low_part",
-    )(down, tenants, *x)
+    )(down, tenants, *x, after)
 
 
 def forward_kernel(cuts, slots, blocks, first, slot, *refs):
@@ -303,11 +310,13 @@
 
 def backward_kernel(slots, start, height, slot, dgate_ref, dup_ref, own_out, other_out):
     half = own_out.shape[0]
-    at = slice(start, start + height)
-    part = contracted_columns(dgate_ref[...], slot(slots[0])[at, :])
-    part = part + contracted_columns(dup_ref[...], slot(slots[1])[at, :])
-    own_out[...] = part[:half]
-    other_out[...] = part[half:].astype(jnp.bfloat16)
+    dgate, dup = dgate_ref[...], dup_ref[...]
+    for strip in range(0, height, STRIP):
+        at = slice(start + strip, start + strip + STRIP)
+        part = contracted_columns(dgate, slot(slots[0], at))
+        part = part + contracted_columns(dup, slot(slots[1], at))
+        own_out[:, strip : strip + STRIP] = part[:half]
+        other_out[:, strip : strip + STRIP] = part[half:].astype(jnp.bfloat16)
 
 
 def backward(slots, start, height, dgate, dup, store, fetches, after):
@@ -500,10 +509,13 @@
     block = stacked([block, other], [token])
     x = [block, swapped(block, 1)]
     store, token = store_call(
-        mark, store, [(up_weight, 1, 3)], [], [mark_shape], 0, "fetch", after=[block]
-    )
-
-    input_span, low = low_part(adapter_down_maps, tenants, x, count)
+        mark, store, [(up_weight, 1, 3, 0)], [], [mark_shape], 0, "fetch", after=[block]
+    )
+
+    input_span, low = low_part(adapter_down_maps, tenants, x, count, token)
+    store, token = store_call(
+        mark, store, [(up_weight, 1, 3, 1)], [], [mark_shape], 0, "fetch", after=[low]
+    )
     sums = []
     slots = {0: (0, 1), 1: (2, 3), 2: (4, 5), 3: (0, 1)}
     step = 0

time: 87.2 us -> 87.1 us (level)
  waiting for transfers between devices: 6.85 us -> 5.19 us
  Pallas kernels: 57.6 us -> 58.6 us
    ppermute x22, waiting for transfers between devices: 6.85 us -> 5.19 us  [swapped(): lax.ppermute(block, 'tp', [(i, i ^ hop) for i in range(lax.axis_size('tp'...]
    pallas_call x12 -> x13, Pallas kernels: 47.7 us -> 48.9 us  [store_call(): pl.pallas_call(body, in_specs=[VMEM] * (n_in + (not new)) + [ANY] * (n_hb...]
  transfers between devices with their start and end apart: 22 -> 22, of which waited for: 7 -> 6; matrix products, arithmetic and copies ran while one was open for 0% -> 0% of each run, Pallas kernels for 60% -> 61%
where the time goes in v12:
time: 87.1 us; the launch traced here: 87 us
  Pallas kernels  58.6 us (67%)
  starting transfers between devices  22.1 us (25%)
  waiting for transfers between devices  5.19 us (6%)
  between operations  0.98 us (1%)
    pallas_call x13, Pallas kernels, store_call(): pl.pallas_call(body, in_specs=[VMEM] * (n_in + (not new)) + [ANY] * (n_hb...  48.9 us
    ppermute x22, starting transfers between devices, swapped(): lax.ppermute(block, 'tp', [(i, i ^ hop) for i in range(lax.axis_size('tp'...  22.1 us
    pallas_call x3, Pallas kernels, outer(): pl.pallas_call(outer_kernel, grid=(steps,), in_specs=[pl.BlockSpec((rows,...  7.21 us
    ppermute x22, waiting for transfers between devices, swapped(): lax.ppermute(block, 'tp', [(i, i ^ hop) for i in range(lax.axis_size('tp'...  5.19 us
  transfers between devices with their start and end apart: 22, of which 6 were waited for; matrix products, arithmetic and copies ran while one was open for 0% of the time, Pallas kernels for 61%

profile of v12, /device:TPU:0, one launch (start us, length us, event | category | flops | bytes accessed | tf_op | source)
XLA Modules:
  0.0 87.0 jit_solution(2956535370707075004)
XLA Ops:
  0.6 3.1 %collective-permute-start = (bf16[2,8192]{1,0:T(2,128)(2,1)}, bf16[2,8192]{1,0:T(2,128)(2,1)S(1)}, u32[]{:S(2)}, u32[]{:S(2)}) collective-permute-start(bf16[2,8192]{1,0:T(2,128)(2,1)} %refs_0_.4), channel_id=1, source_target_pairs={{0,4},{1,5},{2,6},{3,7},{4,0},{5,1},{6,2},{7,3},{8,12},{9,13},{10,... | collective-permute-start | bytes 98312 | tf_op jit(solution)/shard_map/ppermute | solution.py:471
  3.7 2.6 %collective-permute-start.1 = (bf16[2,8192]{1,0:T(2,128)(2,1)}, bf16[2,8192]{1,0:T(2,128)(2,1)S(1)}, u32[]{:S(2)}, u32[]{:S(2)}) collective-permute-start(bf16[2,8192]{1,0:T(2,128)(2,1)} %refs_0_.4), channel_id=1, source_target_pairs={{0,8},{1,9},{2,10},{3,11},{4,12},{5,13},{6,14},{7,15},{8,0},{9,1},... | collective-permute-start | bytes 98312 | tf_op jit(solution)/shard_map/ppermute | solution.py:471
  6.3 0.0 collective-permute-start.2
  6.3 5.3 %fetch.4 = (bf16[12288,1792]{1,0:T(8,128)(2,1)S(1)}, f32[8,128]{1,0:T(8,128)S(1)}) custom-call(bf16[8192,1792]{1,0:T(8,128)(2,1)} %refs_3_.8, bf16[8192,1792]{1,0:T(8,128)(2,1)} %refs_3_.9), custom_call_target="tpu_custom_call" | custom-call | bytes 14680064 | tf_op jit(solution)/shard_map/fetch/pallas_call | solution.py:102
  11.7 0.0 collective-permute-done.refs_1_
  11.7 0.0 collective-permute-done.1.refs_2_
  11.7 0.6 collective-permute-done.2.refs_3_
  12.2 0.1 stacked.2.refs_2_.refs_0_
  12.3 1.6 %collective-permute-start.3 = (bf16[8,8192]{1,0:T(8,128)(2,1)S(1)}, bf16[8,8192]{1,0:T(8,128)(2,1)S(1)}, u32[]{:S(2)}, u32[]{:S(2)}) collective-permute-start(bf16[8,8192]{1,0:T(8,128)(2,1)S(1)} %stacked.2.refs_2_.refs_0_), channel_id=1, source_target_pairs={{0,2},{1,3},{2,0},{3,1},{4,6},{5,7},{6,4},{7,5},{8,10},{9,11},{10,... | collective-permute-start | bytes 393224 | tf_op jit(solution)/shard_map/ppermute | solution.py:471
  13.9 3.2 %fetch.5 = (bf16[12288,1792]{1,0:T(8,128)(2,1)S(1)}, f32[8,128]{1,0:T(8,128)S(1)}) custom-call(bf16[12288,1792]{1,0:T(8,128)(2,1)S(1)} %get-tuple-element.55.refs_0_, bf16[8192,1792]{1,0:T(8,128)(2,1)} %refs_3_.8, bf16[8,8192]{1,0:T(8,128)(2,1)S(1)} %stacked.2.refs_2_.refs_0_), custom_call_target="tpu_custom_call", output_to_operand_aliasing={{0}: (0, {})} | custom-call | bytes 7340032 | tf_op jit(solution)/shard_map/fetch/pallas_call | solution.py:102
  17.1 0.0 copy-start
  17.1 0.0 copy-start.3
  17.1 0.2 collective-permute-done.3.refs_1_
  17.4 0.1 collective-permute-start.4
  17.5 2.3 %fetch.6 = (bf16[12288,1792]{1,0:T(8,128)(2,1)S(1)}, f32[8,128]{1,0:T(8,128)S(1)}) custom-call(bf16[12288,1792]{1,0:T(8,128)(2,1)S(1)} %get-tuple-element.57.refs_0_, bf16[8192,1792]{1,0:T(8,128)(2,1)} %refs_3_.9, bf16[16,8192]{1,0:T(8,128)(2,1)S(1)} %stacked.3.refs_2_.refs_1_), custom_call_target="tpu_custom_call", output_to_operand_aliasing={{0}: (0, {})} | custom-call | bytes 7340032 | tf_op jit(solution)/shard_map/fetch/pallas_call | solution.py:102
  19.8 0.0 collective-permute-done.4.refs_3_.refs_2_
  19.8 0.0 copy-done
  19.8 0.7 low_part.1
  20.5 0.3 collective-permute-start.5
  20.8 2.7 %fetch.7 = (bf16[12288,1792]{1,0:T(8,128)(2,1)S(1)}, f32[8,128]{1,0:T(8,128)}) custom-call(bf16[12288,1792]{1,0:T(8,128)(2,1)S(1)} %get-tuple-element.59.refs_0_, bf16[8192,1792]{1,0:T(8,128)(2,1)} %refs_3_.9, f32[32,64]{1,0:T(8,128)S(1)} %get-tuple-element.61.refs_2_.refs_5_.left_ref), custom_call_target="tpu_custom_call", output_to_operand_aliasing={{0}: (0, {})} | custom-call | bytes 7340032 | tf_op jit(solution)/shard_map/fetch/pallas_call | solution.py:102
  23.5 0.0 collective-permute-done.5.right_ref
  23.5 1.6 %collective-permute-start.6 = (f32[32,64]{1,0:T(8,128)S(1)}, f32[32,64]{1,0:T(8,128)S(1)}, u32[]{:S(2)}, u32[]{:S(2)}) collective-permute-start(f32[32,64]{1,0:T(8,128)S(1)} %plus.8.refs_7_.left_ref), channel_id=1, source_target_pairs={{0,2},{1,3},{2,0},{3,1},{4,6},{5,7},{6,4},{7,5},{8,10},{9,11},{10,... | collective-permute-start | bytes 24584 | tf_op jit(solution)/shard_map/ppermute | solution.py:471
  25.1 5.3 %forward.3 = (bf16[12288,1792]{1,0:T(8,128)(2,1)S(1)}, f32[32,1792]{1,0:T(8,128)S(1)}, f32[32,1792]{1,0:T(8,128)S(1)}) custom-call(bf16[12288,1792]{1,0:T(8,128)(2,1)S(1)} %get-tuple-element.62.refs_0_, bf16[16,8192]{1,0:T(8,128)(2,1)S(1)} %stacked.3.refs_2_.refs_1_, ...), custom_call_target="tpu_custom_call", output_to_operand_aliasing={{0}: (0, {})} | custom-call | flops 939524096 | bytes 14680064 | tf_op jit(solution)/shard_map/forward/pallas_call | solution.py:102
  30.4 0.4 collective-permute-start.7
  30.9 5.4 %forward.4 = (bf16[12288,1792]{1,0:T(8,128)(2,1)S(1)}, f32[32,1792]{1,0:T(8,128)S(1)}, f32[32,1792]{1,0:T(8,128)S(1)}) custom-call(bf16[12288,1792]{1,0:T(8,128)(2,1)S(1)} %get-tuple-element.63.refs_0_, bf16[16,8192]{1,0:T(8,128)(2,1)S(1)} %stacked.3.refs_2_.refs_1_, ...), custom_call_target="tpu_custom_call", output_to_operand_aliasing={{0}: (0, {})} | custom-call | flops 469762048 | bytes 14680064 | tf_op jit(solution)/shard_map/forward/pallas_call | solution.py:102
  36.3 0.0 copy-start.1
  36.3 0.0 collective-permute-done.7.right_ref
  36.3 3.6 %collective-permute-start.8 = (f32[32,64]{1,0:T(8,128)S(1)}, f32[32,64]{1,0:T(8,128)S(1)}, u32[]{:S(2)}, u32[]{:S(2)}) collective-permute-start(f32[32,64]{1,0:T(8,128)S(1)} %plus.10.left_ref), channel_id=1, source_target_pairs={{0,8},{1,9},{2,10},{3,11},{4,12},{5,13},{6,14},{7,15},{8,0},{9,1},... | collective-permute-start | bytes 24584 | tf_op jit(solution)/shard_map/ppermute | solution.py:471
  39.9 3.2 %forward.5 = (bf16[12288,1792]{1,0:T(8,128)(2,1)S(1)}, f32[32,1792]{1,0:T(8,128)S(1)}, f32[32,1792]{1,0:T(8,128)S(1)}) custom-call(bf16[12288,1792]{1,0:T(8,128)(2,1)S(1)} %get-tuple-element.66.refs_0_, bf16[16,8192]{1,0:T(8,128)(2,1)S(1)} %stacked.3.refs_2_.refs_1_, ...), custom_call_target="tpu_custom_call", output_to_operand_aliasing={{0}: (0, {})} | custom-call | flops 469762048 | bytes 7340032 | tf_op jit(solution)/shard_map/forward/pallas_call | solution.py:102
  43.1 0.0 collective-permute-done.8.right_ref
  43.1 3.8 %activation.1 = (bf16[12288,1792]{1,0:T(8,128)(2,1)S(1)}, bf16[32,1792]{1,0:T(8,128)(2,1)S(1)}, bf16[32,1792]{1,0:T(8,128)(2,1)S(1)}, f32[32,64]{1,0:T(8,128)S(1)}, bf16[32,2048]{1,0:T(8,128)(2,1)S(1)}) custom-call(bf16[12288,1792]{1,0:T(8,128)(2,1)S(1)} %get-tuple-element.69.refs_0_, ...), custom_call_target="tpu_custom_call", output_to_operand_aliasing={{0}: (0, {})} | custom-call | flops 469762048 | tf_op jit(solution)/shard_map/activation/pallas_call | solution.py:102
  46.9 0.5 collective-permute-start.9
  47.4 4.4 %backward.5 = (bf16[12288,1792]{1,0:T(8,128)(2,1)S(1)}, f32[16,2048]{1,0:T(8,128)S(1)}, bf16[16,2048]{1,0:T(8,128)(2,1)S(1)}) custom-call(bf16[12288,1792]{1,0:T(8,128)(2,1)S(1)} %get-tuple-element.75.refs_0_, bf16[32,1792]{1,0:T(8,128)(2,1)S(1)} %get-tuple-element.76.refs_1_.right_ref, ...), custom_call_target="tpu_custom_call", output_to_operand_aliasing={{0}: (0, {})} | custom-call | flops 469762048 | bytes 7340032 | tf_op jit(solution)/shard_map/backward/pallas_call | solution.py:102
  51.9 0.3 collective-permute-start.18
  52.1 0.0 collective-permute-done.9.right_ref
  52.1 0.1 collective-permute-start.10
  52.2 4.4 %backward.6 = (bf16[12288,1792]{1,0:T(8,128)(2,1)S(1)}, f32[16,2048]{1,0:T(8,128)S(1)}, bf16[16,2048]{1,0:T(8,128)(2,1)S(1)}) custom-call(bf16[12288,1792]{1,0:T(8,128)(2,1)S(1)} %get-tuple-element.78.refs_0_, bf16[32,1792]{1,0:T(8,128)(2,1)S(1)} %get-tuple-element.76.refs_1_.right_ref, ...), custom_call_target="tpu_custom_call", output_to_operand_aliasing={{0}: (0, {})} | custom-call | flops 469762048 | bytes 7340032 | tf_op jit(solution)/shard_map/backward/pallas_call | solution.py:102
  56.7 0.6 collective-permute-start.17
  57.3 1.5 %collective-permute-start.11 = (f32[32,64]{1,0:T(8,128)S(1)}, f32[32,64]{1,0:T(8,128)S(1)}, u32[]{:S(2)}, u32[]{:S(2)}) collective-permute-start(f32[32,64]{1,0:T(8,128)S(1)} %plus.13.left_ref.refs_4_), channel_id=1, source_target_pairs={{0,8},{1,9},{2,10},{3,11},{4,12},{5,13},{6,14},{7,15},{8,0},{9,1},... | collective-permute-start | bytes 24584 | tf_op jit(solution)/shard_map/ppermute | solution.py:471
  58.8 4.4 %backward.7 = (bf16[12288,1792]{1,0:T(8,128)(2,1)S(1)}, f32[16,2048]{1,0:T(8,128)S(1)}, bf16[16,2048]{1,0:T(8,128)(2,1)S(1)}) custom-call(bf16[12288,1792]{1,0:T(8,128)(2,1)S(1)} %get-tuple-element.79.refs_0_, bf16[32,1792]{1,0:T(8,128)(2,1)S(1)} %get-tuple-element.76.refs_1_.right_ref, ...), custom_call_target="tpu_custom_call", output_to_operand_aliasing={{0}: (0, {})} | custom-call | flops 469762048 | bytes 7340032 | tf_op jit(solution)/shard_map/backward/pallas_call | solution.py:102
  63.2 0.1 collective-permute-start.16
  63.3 0.5 collective-permute-start.12
  63.9 2.2 %backward.8 = (bf16[12288,1792]{1,0:T(8,128)(2,1)S(1)}, f32[16,1024]{1,0:T(8,128)S(1)}, bf16[16,1024]{1,0:T(8,128)(2,1)S(1)}) custom-call(bf16[12288,1792]{1,0:T(8,128)(2,1)S(1)} %get-tuple-element.80.refs_0_, bf16[32,1792]{1,0:T(8,128)(2,1)S(1)} %get-tuple-element.76.refs_1_.right_ref, ...), custom_call_target="tpu_custom_call", output_to_operand_aliasing={{0}: (0, {})} | custom-call | flops 234881024 | tf_op jit(solution)/shard_map/backward/pallas_call | solution.py:102
  66.1 0.0 collective-permute-start.14
  66.1 0.0 collective-permute-done.12.right_ref
  66.1 0.9 adapter_part.1
  67.0 0.6 collective-permute-start.13
  67.6 2.2 %backward.9 = (bf16[12288,1792]{1,0:T(8,128)(2,1)S(1)}, f32[16,1024]{1,0:T(8,128)S(1)}, bf16[16,1024]{1,0:T(8,128)(2,1)S(1)}) custom-call(bf16[12288,1792]{1,0:T(8,128)(2,1)S(1)} %get-tuple-element.83.refs_0_, bf16[32,1792]{1,0:T(8,128)(2,1)S(1)} %get-tuple-element.76.refs_1_.right_ref, ...), custom_call_target="tpu_custom_call", output_to_operand_aliasing={{0}: (0, {})} | custom-call | flops 234881024 | tf_op jit(solution)/shard_map/backward/pallas_call | solution.py:102
  69.8 0.0 collective-permute-done.13.refs_1_
  69.8 0.1 collective-permute-start.15
  69.9 1.2 %collective-permute-done.15.refs_5_ = bf16[16,1024]{1,0:T(8,128)(2,1)S(1)} collective-permute-done((bf16[16,1024]{1,0:T(8,128)(2,1)S(1)}, bf16[16,1024]{1,0:T(8,128)(2,1)S(1)}, u32[]{:S(2)}, u32[]{:S(2)}) %collective-permute-start.15) | collective-permute-done | bytes 32800 | tf_op jit(solution)/shard_map/ppermute | solution.py:471
  71.1 0.0 collective-permute-done.17.refs_9_
  71.1 0.0 collective-permute-done.16.refs_7_
  71.1 0.1 first_halves.1
  71.2 1.6 %collective-permute-start.19 = (bf16[8,8192]{1,0:T(8,128)(2,1)S(1)}, bf16[8,8192]{1,0:T(8,128)(2,1)S(1)}, u32[]{:S(2)}, u32[]{:S(2)}) collective-permute-start(bf16[8,8192]{1,0:T(8,128)(2,1)S(1)} %get-tuple-element.93.refs_0_), channel_id=1, source_target_pairs={{0,2},{1,3},{2,0},{3,1},{4,6},{5,7},{6,4},{7,5},{8,10},{9,11},{10,... | collective-permute-start | bytes 393224 | tf_op jit(solution)/shard_map/ppermute | solution.py:471
  72.7 2.6 %up_maps.2 = (bf16[2048,1792]{1,0:T(8,128)(2,1)}, f32[8,128]{1,0:T(8,128)S(1)}) custom-call(bf16[32,2048]{1,0:T(8,128)(2,1)S(1)} %get-tuple-element.94.left_ref, bf16[32,1792]{1,0:T(8,128)(2,1)S(1)} %get-tuple-element.76.refs_1_.right_ref, bf16[8,8192]{1,0:T(8,128)(2,1)S(1)} %get-tuple-element.93.refs_0_), custom_call_target="tpu_custom_call" | custom-call | flops 117440512 | bytes 3670016 | tf_op jit(solution)/shard_map/up_maps/pallas_call | solution.py:429
  75.3 1.5 %collective-permute-done.19.came_ref = bf16[8,8192]{1,0:T(8,128)(2,1)S(1)} collective-permute-done((bf16[8,8192]{1,0:T(8,128)(2,1)S(1)}, bf16[8,8192]{1,0:T(8,128)(2,1)S(1)}, u32[]{:S(2)}, u32[]{:S(2)}) %collective-permute-start.19) | collective-permute-done | bytes 131104 | tf_op jit(solution)/shard_map/ppermute | solution.py:471
  76.8 1.6 %collective-permute-start.20 = (bf16[4,8192]{1,0:T(4,128)(2,1)S(1)}, bf16[4,8192]{1,0:T(4,128)(2,1)S(1)}, u32[]{:S(2)}, u32[]{:S(2)}) collective-permute-start(bf16[4,8192]{1,0:T(4,128)(2,1)S(1)} %get-tuple-element.97.refs_0_), channel_id=1, source_target_pairs={{0,8},{1,9},{2,10},{3,11},{4,12},{5,13},{6,14},{7,15},{8,0},{9,1},... | collective-permute-start | bytes 196616 | tf_op jit(solution)/shard_map/ppermute | solution.py:471
  78.4 2.6 %up_maps.3 = (bf16[2048,1792]{1,0:T(8,128)(2,1)}, f32[8,128]{1,0:T(8,128)S(1)}) custom-call(bf16[32,2048]{1,0:T(8,128)(2,1)S(1)} %get-tuple-element.94.left_ref, bf16[32,1792]{1,0:T(8,128)(2,1)S(1)} %get-tuple-element.76.refs_1_.right_ref, bf16[4,8192]{1,0:T(4,128)(2,1)S(1)} %get-tuple-element.97.refs_0_, ...), custom_call_target="tpu_custom_call", output_to_operand_aliasing={{0}: (3, {})} | custom-call | flops 117440512 | bytes 3670016 | tf_op jit(solution)/shard_map/up_maps/pallas_call | solution.py:429
  81.0 1.3 %collective-permute-done.20.came_ref = bf16[4,8192]{1,0:T(4,128)(2,1)S(1)} collective-permute-done((bf16[4,8192]{1,0:T(4,128)(2,1)S(1)}, bf16[4,8192]{1,0:T(4,128)(2,1)S(1)}, u32[]{:S(2)}, u32[]{:S(2)}) %collective-permute-start.20) | collective-permute-done | bytes 65568 | tf_op jit(solution)/shard_map/ppermute | solution.py:471
  82.3 1.6 %collective-permute-start.21 = (bf16[2,8192]{1,0:T(2,128)(2,1)S(1)}, bf16[2,8192]{1,0:T(2,128)(2,1)S(1)}, u32[]{:S(2)}, u32[]{:S(2)}) collective-permute-start(bf16[2,8192]{1,0:T(2,128)(2,1)S(1)} %get-tuple-element.101.refs_0_), channel_id=1, source_target_pairs={{0,4},{1,5},{2,6},{3,7},{4,0},{5,1},{6,2},{7,3},{8,12},{9,13},{10,... | collective-permute-start | bytes 98312 | tf_op jit(solution)/shard_map/ppermute | solution.py:471
  83.9 2.1 %down_maps.1 = (bf16[512,2048]{1,0:T(8,128)(2,1)}, f32[8,128]{1,0:T(8,128)S(1)}) custom-call(bf16[32,512]{1,0:T(8,128)(2,1)S(1)} %get-tuple-element.102.left_ref, bf16[32,2048]{1,0:T(8,128)(2,1)S(1)} %get-tuple-element.103.right_ref, bf16[2,8192]{1,0:T(2,128)(2,1)S(1)} %get-tuple-element.101.refs_0_), custom_call_target="tpu_custom_call" | custom-call | flops 67108864 | bytes 2097152 | tf_op jit(solution)/shard_map/down_maps/pallas_call | solution.py:429
  86.0 0.4 collective-permute-done.21.came_ref
  86.3 0.7 final.1
  (20 shorter events, 0.2 us)
Async XLA Ops:
  0.6 11.6 %copy-start.2 = (bf16[2,8192]{1,0:T(2,128)(2,1)S(1)}, bf16[2,8192]{1,0:T(2,128)(2,1)}, u32[]{:S(2)}) copy-start(bf16[2,8192]{1,0:T(2,128)(2,1)} %refs_0_.4) | copy-start | bytes 98308
  0.6 11.0 %collective-permute-start = (bf16[2,8192]{1,0:T(2,128)(2,1)}, bf16[2,8192]{1,0:T(2,128)(2,1)S(1)}, u32[]{:S(2)}, u32[]{:S(2)}) collective-permute-start(bf16[2,8192]{1,0:T(2,128)(2,1)} %refs_0_.4), channel_id=1, source_target_pairs={{0,4},{1,5},{2,6},{3,7},{4,0},{5,1},{6,2},{7,3},{8,12},{9,13},{10,... | collective-permute-start | bytes 98312 | tf_op jit(solution)/shard_map/ppermute | solution.py:471
  3.7 7.9 %collective-permute-start.1 = (bf16[2,8192]{1,0:T(2,128)(2,1)}, bf16[2,8192]{1,0:T(2,128)(2,1)S(1)}, u32[]{:S(2)}, u32[]{:S(2)}) collective-permute-start(bf16[2,8192]{1,0:T(2,128)(2,1)} %refs_0_.4), channel_id=1, source_target_pairs={{0,8},{1,9},{2,10},{3,11},{4,12},{5,13},{6,14},{7,15},{8,0},{9,1},... | collective-permute-start | bytes 98312 | tf_op jit(solution)/shard_map/ppermute | solution.py:471
  6.3 5.9 %collective-permute-start.2 = (bf16[2,8192]{1,0:T(2,128)(2,1)}, bf16[2,8192]{1,0:T(2,128)(2,1)S(1)}, u32[]{:S(2)}, u32[]{:S(2)}) collective-permute-start(bf16[2,8192]{1,0:T(2,128)(2,1)} %refs_0_.4), channel_id=1, source_target_pairs={{0,12},{1,13},{2,14},{3,15},{4,8},{5,9},{6,10},{7,11},{8,4},{9,5},... | collective-permute-start | bytes 98312 | tf_op jit(solution)/shard_map/ppermute | solution.py:471
  12.3 5.0 %collective-permute-start.3 = (bf16[8,8192]{1,0:T(8,128)(2,1)S(1)}, bf16[8,8192]{1,0:T(8,128)(2,1)S(1)}, u32[]{:S(2)}, u32[]{:S(2)}) collective-permute-start(bf16[8,8192]{1,0:T(8,128)(2,1)S(1)} %stacked.2.refs_2_.refs_0_), channel_id=1, source_target_pairs={{0,2},{1,3},{2,0},{3,1},{4,6},{5,7},{6,4},{7,5},{8,10},{9,11},{10,... | collective-permute-start | bytes 393224 | tf_op jit(solution)/shard_map/ppermute | solution.py:471
  17.1 2.7 %copy-start = (bf16[512,2048]{1,0:T(8,128)(2,1)S(1)}, bf16[512,2048]{1,0:T(8,128)(2,1)}, u32[]{:S(2)}) copy-start(bf16[512,2048]{1,0:T(8,128)(2,1)} %refs_2_.1) | copy-start | bytes 6291460
  17.1 2.7 %copy-start.3 = (s32[32]{0:T(128)S(1)}, s32[32]{0:T(128)}, u32[]{:S(2)}) copy-start(s32[32]{0:T(128)} %param.13) | copy-start | bytes 388
  17.4 2.4 %collective-permute-start.4 = (bf16[16,8192]{1,0:T(8,128)(2,1)S(1)}, bf16[16,8192]{1,0:T(8,128)(2,1)S(1)}, u32[]{:S(2)}, u32[]{:S(2)}) collective-permute-start(bf16[16,8192]{1,0:T(8,128)(2,1)S(1)} %stacked.3.refs_2_.refs_1_), channel_id=1, source_target_pairs={{0,1},{1,0},{2,3},{3,2},{4,5},{5,4},{6,7},{7,6},{8,9},{9,8},{10,11... | collective-permute-start | bytes 786440 | tf_op jit(solution)/shard_map/ppermute | solution.py:471
  20.5 3.0 %collective-permute-start.5 = (f32[32,64]{1,0:T(8,128)S(1)}, f32[32,64]{1,0:T(8,128)S(1)}, u32[]{:S(2)}, u32[]{:S(2)}) collective-permute-start(f32[32,64]{1,0:T(8,128)S(1)} %get-tuple-element.61.refs_2_.refs_5_.left_ref), channel_id=1, source_target_pairs={{0,1},{1,0},{2,3},{3,2},{4,5},{5,4},{6,7},{7,6},{8,9},{9,8},{10,11... | collective-permute-start | bytes 24584 | tf_op jit(solution)/shard_map/ppermute | solution.py:471
  23.5 6.9 %collective-permute-start.6 = (f32[32,64]{1,0:T(8,128)S(1)}, f32[32,64]{1,0:T(8,128)S(1)}, u32[]{:S(2)}, u32[]{:S(2)}) collective-permute-start(f32[32,64]{1,0:T(8,128)S(1)} %plus.8.refs_7_.left_ref), channel_id=1, source_target_pairs={{0,2},{1,3},{2,0},{3,1},{4,6},{5,7},{6,4},{7,5},{8,10},{9,11},{10,... | collective-permute-start | bytes 24584 | tf_op jit(solution)/shard_map/ppermute | solution.py:471
  30.4 5.9 %collective-permute-start.7 = (f32[32,64]{1,0:T(8,128)S(1)}, f32[32,64]{1,0:T(8,128)S(1)}, u32[]{:S(2)}, u32[]{:S(2)}) collective-permute-start(f32[32,64]{1,0:T(8,128)S(1)} %plus.9.refs_6_.left_ref), channel_id=1, source_target_pairs={{0,4},{1,5},{2,6},{3,7},{4,0},{5,1},{6,2},{7,3},{8,12},{9,13},{10,... | collective-permute-start | bytes 24584 | tf_op jit(solution)/shard_map/ppermute | solution.py:471
  36.3 6.8 %copy-start.1 = (bf16[32,1792]{1,0:T(8,128)(2,1)S(1)}, bf16[32,1792]{1,0:T(8,128)(2,1)}, u32[]{:S(2)}) copy-start(bf16[32,1792]{1,0:T(8,128)(2,1)} %refs_3_.6) | copy-start | bytes 344068
  36.3 6.7 %collective-permute-start.8 = (f32[32,64]{1,0:T(8,128)S(1)}, f32[32,64]{1,0:T(8,128)S(1)}, u32[]{:S(2)}, u32[]{:S(2)}) collective-permute-start(f32[32,64]{1,0:T(8,128)S(1)} %plus.10.left_ref), channel_id=1, source_target_pairs={{0,8},{1,9},{2,10},{3,11},{4,12},{5,13},{6,14},{7,15},{8,0},{9,1},... | collective-permute-start | bytes 24584 | tf_op jit(solution)/shard_map/ppermute | solution.py:471
  46.9 5.2 %collective-permute-start.9 = (f32[32,64]{1,0:T(8,128)S(1)}, f32[32,64]{1,0:T(8,128)S(1)}, u32[]{:S(2)}, u32[]{:S(2)}) collective-permute-start(f32[32,64]{1,0:T(8,128)S(1)} %get-tuple-element.72.left_ref.refs_4_), channel_id=1, source_target_pairs={{0,2},{1,3},{2,0},{3,1},{4,6},{5,7},{6,4},{7,5},{8,10},{9,11},{10,... | collective-permute-start | bytes 24584 | tf_op jit(solution)/shard_map/ppermute | solution.py:471
  51.9 18.0 %collective-permute-start.18 = (bf16[16,2048]{1,0:T(8,128)(2,1)S(1)}, bf16[16,2048]{1,0:T(8,128)(2,1)S(1)}, u32[]{:S(2)}, u32[]{:S(2)}) collective-permute-start(bf16[16,2048]{1,0:T(8,128)(2,1)S(1)} %get-tuple-element.91), channel_id=1, source_target_pairs={{0,1},{1,0},{2,3},{3,2},{4,5},{5,4},{6,7},{7,6},{8,9},{9,8},{10,11... | collective-permute-start | bytes 196616 | tf_op jit(solution)/shard_map/ppermute | solution.py:471
  52.1 5.1 %collective-permute-start.10 = (f32[32,64]{1,0:T(8,128)S(1)}, f32[32,64]{1,0:T(8,128)S(1)}, u32[]{:S(2)}, u32[]{:S(2)}) collective-permute-start(f32[32,64]{1,0:T(8,128)S(1)} %plus.12.left_ref.refs_4_), channel_id=1, source_target_pairs={{0,4},{1,5},{2,6},{3,7},{4,0},{5,1},{6,2},{7,3},{8,12},{9,13},{10,... | collective-permute-start | bytes 24584 | tf_op jit(solution)/shard_map/ppermute | solution.py:471
  56.7 14.4 %collective-permute-start.17 = (bf16[16,2048]{1,0:T(8,128)(2,1)S(1)}, bf16[16,2048]{1,0:T(8,128)(2,1)S(1)}, u32[]{:S(2)}, u32[]{:S(2)}) collective-permute-start(bf16[16,2048]{1,0:T(8,128)(2,1)S(1)} %get-tuple-element.89), channel_id=1, source_target_pairs={{0,1},{1,0},{2,3},{3,2},{4,5},{5,4},{6,7},{7,6},{8,9},{9,8},{10,11... | collective-permute-start | bytes 196616 | tf_op jit(solution)/shard_map/ppermute | solution.py:471
  57.3 6.0 %collective-permute-start.11 = (f32[32,64]{1,0:T(8,128)S(1)}, f32[32,64]{1,0:T(8,128)S(1)}, u32[]{:S(2)}, u32[]{:S(2)}) collective-permute-start(f32[32,64]{1,0:T(8,128)S(1)} %plus.13.left_ref.refs_4_), channel_id=1, source_target_pairs={{0,8},{1,9},{2,10},{3,11},{4,12},{5,13},{6,14},{7,15},{8,0},{9,1},... | collective-permute-start | bytes 24584 | tf_op jit(solution)/shard_map/ppermute | solution.py:471
  63.2 7.9 %collective-permute-start.16 = (bf16[16,2048]{1,0:T(8,128)(2,1)S(1)}, bf16[16,2048]{1,0:T(8,128)(2,1)S(1)}, u32[]{:S(2)}, u32[]{:S(2)}) collective-permute-start(bf16[16,2048]{1,0:T(8,128)(2,1)S(1)} %get-tuple-element.87), channel_id=1, source_target_pairs={{0,1},{1,0},{2,3},{3,2},{4,5},{5,4},{6,7},{7,6},{8,9},{9,8},{10,11... | collective-permute-start | bytes 196616 | tf_op jit(solution)/shard_map/ppermute | solution.py:471
  63.3 2.8 %collective-permute-start.12 = (f32[32,64]{1,0:T(8,128)S(1)}, f32[32,64]{1,0:T(8,128)S(1)}, u32[]{:S(2)}, u32[]{:S(2)}) collective-permute-start(f32[32,64]{1,0:T(8,128)S(1)} %plus.14.left_ref.refs_3_), channel_id=1, source_target_pairs={{0,1},{1,0},{2,3},{3,2},{4,5},{5,4},{6,7},{7,6},{8,9},{9,8},{10,11... | collective-permute-start | bytes 24584 | tf_op jit(solution)/shard_map/ppermute | solution.py:471
  66.1 3.8 %collective-permute-start.14 = (bf16[16,1024]{1,0:T(8,128)(2,1)S(1)}, bf16[16,1024]{1,0:T(8,128)(2,1)S(1)}, u32[]{:S(2)}, u32[]{:S(2)}) collective-permute-start(bf16[16,1024]{1,0:T(8,128)(2,1)S(1)} %get-tuple-element.82), channel_id=1, source_target_pairs={{0,1},{1,0},{2,3},{3,2},{4,5},{5,4},{6,7},{7,6},{8,9},{9,8},{10,11... | collective-permute-start | bytes 98312 | tf_op jit(solution)/shard_map/ppermute | solution.py:471
  67.0 2.8 %collective-permute-start.13 = (bf16[16,512]{1,0:T(8,128)(2,1)S(1)}, bf16[16,512]{1,0:T(8,128)(2,1)S(1)}, u32[]{:S(2)}, u32[]{:S(2)}) collective-permute-start(bf16[16,512]{1,0:T(8,128)(2,1)S(1)} %get-tuple-element.74.refs_3_), channel_id=1, source_target_pairs={{0,1},{1,0},{2,3},{3,2},{4,5},{5,4},{6,7},{7,6},{8,9},{9,8},{10,11... | collective-permute-start | bytes 49160 | tf_op jit(solution)/shard_map/ppermute | solution.py:471
  69.8 1.3 %collective-permute-start.15 = (bf16[16,1024]{1,0:T(8,128)(2,1)S(1)}, bf16[16,1024]{1,0:T(8,128)(2,1)S(1)}, u32[]{:S(2)}, u32[]{:S(2)}) collective-permute-start(bf16[16,1024]{1,0:T(8,128)(2,1)S(1)} %get-tuple-element.85), channel_id=1, source_target_pairs={{0,1},{1,0},{2,3},{3,2},{4,5},{5,4},{6,7},{7,6},{8,9},{9,8},{10,11... | collective-permute-start | bytes 98312 | tf_op jit(solution)/shard_map/ppermute | solution.py:471
  71.2 5.6 %collective-permute-start.19 = (bf16[8,8192]{1,0:T(8,128)(2,1)S(1)}, bf16[8,8192]{1,0:T(8,128)(2,1)S(1)}, u32[]{:S(2)}, u32[]{:S(2)}) collective-permute-start(bf16[8,8192]{1,0:T(8,128)(2,1)S(1)} %get-tuple-element.93.refs_0_), channel_id=1, source_target_pairs={{0,2},{1,3},{2,0},{3,1},{4,6},{5,7},{6,4},{7,5},{8,10},{9,11},{10,... | collective-permute-start | bytes 393224 | tf_op jit(solution)/shard_map/ppermute | solution.py:471
  76.8 5.4 %collective-permute-start.20 = (bf16[4,8192]{1,0:T(4,128)(2,1)S(1)}, bf16[4,8192]{1,0:T(4,128)(2,1)S(1)}, u32[]{:S(2)}, u32[]{:S(2)}) collective-permute-start(bf16[4,8192]{1,0:T(4,128)(2,1)S(1)} %get-tuple-element.97.refs_0_), channel_id=1, source_target_pairs={{0,8},{1,9},{2,10},{3,11},{4,12},{5,13},{6,14},{7,15},{8,0},{9,1},... | collective-permute-start | bytes 196616 | tf_op jit(solution)/shard_map/ppermute | solution.py:471
  82.3 4.0 %collective-permute-start.21 = (bf16[2,8192]{1,0:T(2,128)(2,1)S(1)}, bf16[2,8192]{1,0:T(2,128)(2,1)S(1)}, u32[]{:S(2)}, u32[]{:S(2)}) collective-permute-start(bf16[2,8192]{1,0:T(2,128)(2,1)S(1)} %get-tuple-element.101.refs_0_), channel_id=1, source_target_pairs={{0,4},{1,5},{2,6},{3,7},{4,0},{5,1},{6,2},{7,3},{8,12},{9,13},{10,... | collective-permute-start | bytes 98312 | tf_op jit(solution)/shard_map/ppermute | solution.py:471

commit v13 on v12

--- a/solution.py
+++ b/solution.py
@@ -284,51 +284,61 @@
     )
 
 
-def adapter_kernel(count, low_ref, tenants_ref, down_ref, own_out, other_out, spread_ref):
+def adapter_kernel(count, low_ref, tenants_ref, down_ref, earlier, own_out, other_out, spread_ref):
     half = own_out.shape[0]
+    before = earlier.shape[1]
     pick = pick_held(lax.axis_index("tp"), 2 * half, count)
     spread = spread_rows(picked(pick, low_ref[...]), held_mask(pick, tenants_ref[...]))
     spread_ref[...] = spread
     part = (adapter_scale * contracted_columns(spread, down_ref[...])).astype(jnp.bfloat16)
     own_out[...] = part[:half]
-    other_out[...] = part[half:]
-
-
-def adapter_part(low, tenants, down, count):
+    other_out[:, :before] = earlier[...]
+    other_out[:, before:] = part[half:]
+
+
+def adapter_part(low, tenants, down, count, earlier):
     rows, span = low.shape[0], down.shape[0]
-    half = jax.ShapeDtypeStruct((rows // 2, span), jnp.bfloat16)
     return pl.pallas_call(
         lambda *refs: adapter_kernel(count, *refs),
-        out_shape=[half, half, jax.ShapeDtypeStruct((rows, SPREAD), jnp.bfloat16)],
+        out_shape=[
+            jax.ShapeDtypeStruct((rows // 2, span), jnp.bfloat16),
+            jax.ShapeDtypeStruct((rows // 2, earlier.shape[1] + span), jnp.bfloat16),
+            jax.ShapeDtypeStruct((rows, SPREAD), jnp.bfloat16),
+        ],
         compiler_params=pltpu.CompilerParams(vmem_limit_bytes=4 << 20),
         cost_estimate=pl.CostEstimate(
             flops=2 * rows * down.size, bytes_accessed=2 * down.size, transcendentals=0
         ),
         name="adapter_part",
-    )(low, tenants, down)
-
-
-def backward_kernel(slots, start, height, slot, dgate_ref, dup_ref, own_out, other_out):
+    )(low, tenants, down, earlier)
+
+
+def backward_kernel(slots, start, height, slot, dgate_ref, dup_ref, *refs):
+    own_out, other_out = refs[-2:]
     half = own_out.shape[0]
+    before = other_out.shape[1] - height
+    if before:
+        other_out[:, :before] = refs[0][...]
     dgate, dup = dgate_ref[...], dup_ref[...]
     for strip in range(0, height, STRIP):
         at = slice(start + strip, start + strip + STRIP)
         part = contracted_columns(dgate, slot(slots[0], at))
         part = part + contracted_columns(dup, slot(slots[1], at))
         own_out[:, strip : strip + STRIP] = part[:half]
-        other_out[:, strip : strip + STRIP] = part[half:].astype(jnp.bfloat16)
-
-
-def backward(slots, start, height, dgate, dup, store, fetches, after):
+        other_out[:, before + strip : before + strip + STRIP] = part[half:].astype(jnp.bfloat16)
+
+
+def backward(slots, start, height, dgate, dup, store, fetches, after, earlier=()):
     rows, hidden = dgate.shape
+    other_width = height + sum(part.shape[1] for part in earlier)
     return store_call(
         lambda *refs: backward_kernel(slots, start, height, *refs),
         store,
         fetches,
-        [dgate, dup],
+        [dgate, dup, *earlier],
         [
             jax.ShapeDtypeStruct((rows // 2, height), jnp.float32),
-            jax.ShapeDtypeStruct((rows // 2, height), jnp.bfloat16),
+            jax.ShapeDtypeStruct((rows // 2, other_width), jnp.bfloat16),
         ],
         4 * rows * hidden * height,
         "backward",
@@ -336,18 +346,18 @@
     )
 
 
-def first_halves_kernel(count, adapter_own, adapter_came, *refs):
+def first_halves_kernel(places, span, adapter_own, *refs):
     keep_ref, send_ref, sums = refs[-3:]
-    pieces = refs[:-3]
+    own, came = refs[: len(places)], refs[len(places) : -3]
     half = keep_ref.shape[0]
     device = lax.axis_index("tp")
-    at = 0
-    for own, came in zip(pieces[::2], pieces[1::2]):
-        width = own.shape[1]
-        sums[:, at : at + width] = own[...] + came[...].astype(jnp.float32)
-        at += width
+    for part, (at, group, start) in zip(own, places):
+        width = part.shape[1]
+        other = came[group][:, start : start + width].astype(jnp.float32)
+        sums[:, at : at + width] = part[...] + other
     mine = adapter_own[...].astype(jnp.float32)
-    other = adapter_came[...].astype(jnp.float32)
+    group, start = span
+    other = came[group][:, start : start + mine.shape[1]].astype(jnp.float32)
     pair = jnp.where(
         device % 2 == 0,
         jnp.concatenate([mine, other], axis=1),
@@ -359,11 +369,11 @@
     send_ref[...] = sums[half:, :].astype(jnp.bfloat16)
 
 
-def first_halves(pieces, adapter_own, adapter_came, count):
+def first_halves(own, places, adapter_own, span, came):
     rows = adapter_own.shape[0]
-    width = sum(own.shape[1] for own, _ in pieces)
-    return pl.pallas_call(
-        lambda *refs: first_halves_kernel(count, *refs),
+    width = sum(part.shape[1] for part in own)
+    return pl.pallas_call(
+        lambda *refs: first_halves_kernel(places, span, *refs),
         out_shape=[
             jax.ShapeDtypeStruct((rows // 2, width), jnp.float32),
             jax.ShapeDtypeStruct((rows // 2, width), jnp.bfloat16),
@@ -371,7 +381,7 @@
         scratch_shapes=[pltpu.VMEM((rows, width), jnp.float32)],
         compiler_params=pltpu.CompilerParams(vmem_limit_bytes=40 << 20),
         name="first_halves",
-    )(adapter_own, adapter_came, *[array for pair in pieces for array in pair])
+    )(adapter_own, *own, *came)
 
 
 def halves(keep, came, after):
@@ -536,34 +546,39 @@
     later_hops = hops[1:] + hops[:1]
     depth = width // CUTS
     part_list = [
-        (3, (0, 1), 0, depth, [(gate_weight, 1, 2)]),
-        (2, (4, 5), 0, depth, [(gate_weight, 0, 0)]),
-        (1, (2, 3), 0, depth, [(up_weight, 0, 1)]),
-        (0, (0, 1), 0, depth // 2, []),
-        (0, (0, 1), depth // 2, depth // 2, []),
+        (3, (0, 1), 0, depth, [(gate_weight, 1, 2)], True),
+        (2, (4, 5), 0, depth, [(gate_weight, 0, 0)], False),
+        (1, (2, 3), 0, depth, [(up_weight, 0, 1)], True),
+        (0, (0, 1), depth // 2, depth // 2, [], True),
+        (0, (0, 1), 0, depth // 2, [], False),
     ]
-    columns = {}
-    for n, (piece, slots, first, height, fetches) in enumerate(part_list):
+    own_parts, places, came, waiting = [], [], [], []
+    for n, (piece, slots, first, height, fetches, waits) in enumerate(part_list):
         after = [low_grad]
         if n == len(part_list) - 1:
-            adapter_own, adapter_other, grad_spread = adapter_part(
-                low_grad, tenants, adapter_down_maps, count
+            span = (len(came), waiting[0].shape[1])
+            adapter_own, to_send, grad_spread = adapter_part(
+                low_grad, tenants, adapter_down_maps, count, waiting[0]
             )
-            adapter_came = swapped(adapter_other, 1)
-            after = [adapter_other]
+            came.append(swapped(to_send, 1))
+            after, waiting = [to_send], []
         else:
             turns = later_hops[:1] if n < len(part_list) - 2 else later_hops
             later_hops = later_hops[len(turns) :]
             for hop in turns:
                 low_grad = plus(low_grad, swapped(low_grad, hop))
+        begin = sum(part.shape[1] for part in waiting)
         store, own_part, other_part = backward(
-            slots, first, height, dgate, dup, store, fetches, after
+            slots, first, height, dgate, dup, store, fetches, after, waiting
         )
-        columns[piece * depth + first] = (own_part, swapped(other_part, 1))
-
-    keep, send = first_halves(
-        [columns[start] for start in sorted(columns)], adapter_own, adapter_came, count
-    )
+        own_parts.append(own_part)
+        places.append((piece * depth + first, len(came), begin))
+        waiting = [other_part]
+        if not waits:
+            came.append(swapped(other_part, 1))
+            waiting = []
+
+    keep, send = first_halves(own_parts, places, adapter_own, span, came)
     halvings = [block_owner(0, 1 << bit, count) for bit in reversed(range(len(hops) - 1))]
     up_map_gradient = None
     for n, hop in enumerate(halvings[:-1]):

time: 87.1 us -> 86.3 us (level)
  starting transfers between devices: 22.1 us -> 21.2 us
    ppermute x22 -> x19, starting transfers between devices: 22.1 us -> 21.2 us  [swapped(): lax.ppermute(block, 'tp', [(i, i ^ hop) for i in range(lax.axis_size('tp'...]
    ppermute x22 -> x19, waiting for transfers between devices: 5.19 us -> 5.33 us  [swapped(): lax.ppermute(block, 'tp', [(i, i ^ hop) for i in range(lax.axis_size('tp'...]
  transfers between devices with their start and end apart: 22 -> 19, of which waited for: 6 -> 6; matrix products, arithmetic and copies ran while one was open for 0% -> 0% of each run, Pallas kernels for 61% -> 62%
where the time goes in v13:
time: 86.3 us; the launch traced here: 86.2 us
  Pallas kernels  58.6 us (68%)
  starting transfers between devices  21.2 us (25%)
  waiting for transfers between devices  5.33 us (6%)
  between operations  0.98 us (1%)
    pallas_call x13, Pallas kernels, store_call(): pl.pallas_call(body, in_specs=[VMEM] * (n_in + (not new)) + [ANY] * (n_hb...  48.9 us
    ppermute x19, starting transfers between devices, swapped(): lax.ppermute(block, 'tp', [(i, i ^ hop) for i in range(lax.axis_size('tp'...  21.2 us
    pallas_call x3, Pallas kernels, outer(): pl.pallas_call(outer_kernel, grid=(steps,), in_specs=[pl.BlockSpec((rows,...  7.21 us
    ppermute x19, waiting for transfers between devices, swapped(): lax.ppermute(block, 'tp', [(i, i ^ hop) for i in range(lax.axis_size('tp'...  5.33 us
  transfers between devices with their start and end apart: 19, of which 6 were waited for; matrix products, arithmetic and copies ran while one was open for 0% of the time, Pallas kernels for 62%

profile of v13, /device:TPU:0, one launch (start us, length us, event | category | flops | bytes accessed | tf_op | source)
XLA Modules:
  0.0 86.2 jit_solution(13705987324803273419)
XLA Ops:
  0.6 0.0 copy-start.2
  0.6 3.1 %collective-permute-start = (bf16[2,8192]{1,0:T(2,128)(2,1)}, bf16[2,8192]{1,0:T(2,128)(2,1)S(1)}, u32[]{:S(2)}, u32[]{:S(2)}) collective-permute-start(bf16[2,8192]{1,0:T(2,128)(2,1)} %refs_0_.4), channel_id=1, source_target_pairs={{0,4},{1,5},{2,6},{3,7},{4,0},{5,1},{6,2},{7,3},{8,12},{9,13},{10,... | collective-permute-start | bytes 98312 | tf_op jit(solution)/shard_map/ppermute | solution.py:481
  3.7 2.6 %collective-permute-start.1 = (bf16[2,8192]{1,0:T(2,128)(2,1)}, bf16[2,8192]{1,0:T(2,128)(2,1)S(1)}, u32[]{:S(2)}, u32[]{:S(2)}) collective-permute-start(bf16[2,8192]{1,0:T(2,128)(2,1)} %refs_0_.4), channel_id=1, source_target_pairs={{0,8},{1,9},{2,10},{3,11},{4,12},{5,13},{6,14},{7,15},{8,0},{9,1},... | collective-permute-start | bytes 98312 | tf_op jit(solution)/shard_map/ppermute | solution.py:481
  6.3 0.0 collective-permute-start.2
  6.3 5.3 %fetch.4 = (bf16[12288,1792]{1,0:T(8,128)(2,1)S(1)}, f32[8,128]{1,0:T(8,128)S(1)}) custom-call(bf16[8192,1792]{1,0:T(8,128)(2,1)} %refs_4_.3, bf16[8192,1792]{1,0:T(8,128)(2,1)} %refs_3_.7), custom_call_target="tpu_custom_call" | custom-call | bytes 14680064 | tf_op jit(solution)/shard_map/fetch/pallas_call | solution.py:102
  11.7 0.0 collective-permute-done.refs_1_
  11.7 0.0 collective-permute-done.1.refs_2_
  11.7 0.6 collective-permute-done.2.refs_3_
  12.2 0.1 stacked.2.refs_2_.refs_0_
  12.3 1.6 %collective-permute-start.3 = (bf16[8,8192]{1,0:T(8,128)(2,1)S(1)}, bf16[8,8192]{1,0:T(8,128)(2,1)S(1)}, u32[]{:S(2)}, u32[]{:S(2)}) collective-permute-start(bf16[8,8192]{1,0:T(8,128)(2,1)S(1)} %stacked.2.refs_2_.refs_0_), channel_id=1, source_target_pairs={{0,2},{1,3},{2,0},{3,1},{4,6},{5,7},{6,4},{7,5},{8,10},{9,11},{10,... | collective-permute-start | bytes 393224 | tf_op jit(solution)/shard_map/ppermute | solution.py:481
  13.9 3.2 %fetch.5 = (bf16[12288,1792]{1,0:T(8,128)(2,1)S(1)}, f32[8,128]{1,0:T(8,128)S(1)}) custom-call(bf16[12288,1792]{1,0:T(8,128)(2,1)S(1)} %get-tuple-element.55.refs_0_, bf16[8192,1792]{1,0:T(8,128)(2,1)} %refs_4_.3, bf16[8,8192]{1,0:T(8,128)(2,1)S(1)} %stacked.2.refs_2_.refs_0_), custom_call_target="tpu_custom_call", output_to_operand_aliasing={{0}: (0, {})} | custom-call | bytes 7340032 | tf_op jit(solution)/shard_map/fetch/pallas_call | solution.py:102
  17.1 0.0 copy-start
  17.1 0.0 copy-start.3
  17.1 0.2 collective-permute-done.3.refs_1_
  17.4 0.1 collective-permute-start.4
  17.5 2.3 %fetch.6 = (bf16[12288,1792]{1,0:T(8,128)(2,1)S(1)}, f32[8,128]{1,0:T(8,128)S(1)}) custom-call(bf16[12288,1792]{1,0:T(8,128)(2,1)S(1)} %get-tuple-element.57.refs_0_, bf16[8192,1792]{1,0:T(8,128)(2,1)} %refs_3_.7, bf16[16,8192]{1,0:T(8,128)(2,1)S(1)} %stacked.3.refs_2_.refs_1_), custom_call_target="tpu_custom_call", output_to_operand_aliasing={{0}: (0, {})} | custom-call | bytes 7340032 | tf_op jit(solution)/shard_map/fetch/pallas_call | solution.py:102
  19.8 0.0 collective-permute-done.4.refs_3_.refs_2_
  19.8 0.0 copy-done
  19.8 0.7 low_part.1
  20.5 0.3 collective-permute-start.5
  20.8 2.7 %fetch.7 = (bf16[12288,1792]{1,0:T(8,128)(2,1)S(1)}, f32[8,128]{1,0:T(8,128)}) custom-call(bf16[12288,1792]{1,0:T(8,128)(2,1)S(1)} %get-tuple-element.59.refs_0_, bf16[8192,1792]{1,0:T(8,128)(2,1)} %refs_3_.7, f32[32,64]{1,0:T(8,128)S(1)} %get-tuple-element.61.refs_2_.refs_5_.left_ref), custom_call_target="tpu_custom_call", output_to_operand_aliasing={{0}: (0, {})} | custom-call | bytes 7340032 | tf_op jit(solution)/shard_map/fetch/pallas_call | solution.py:102
  23.5 0.0 collective-permute-done.5.right_ref
  23.5 1.6 %collective-permute-start.6 = (f32[32,64]{1,0:T(8,128)S(1)}, f32[32,64]{1,0:T(8,128)S(1)}, u32[]{:S(2)}, u32[]{:S(2)}) collective-permute-start(f32[32,64]{1,0:T(8,128)S(1)} %plus.8.refs_7_.left_ref), channel_id=1, source_target_pairs={{0,2},{1,3},{2,0},{3,1},{4,6},{5,7},{6,4},{7,5},{8,10},{9,11},{10,... | collective-permute-start | bytes 24584 | tf_op jit(solution)/shard_map/ppermute | solution.py:481
  25.1 5.3 %forward.3 = (bf16[12288,1792]{1,0:T(8,128)(2,1)S(1)}, f32[32,1792]{1,0:T(8,128)S(1)}, f32[32,1792]{1,0:T(8,128)S(1)}) custom-call(bf16[12288,1792]{1,0:T(8,128)(2,1)S(1)} %get-tuple-element.62.refs_0_, bf16[16,8192]{1,0:T(8,128)(2,1)S(1)} %stacked.3.refs_2_.refs_1_, ...), custom_call_target="tpu_custom_call", output_to_operand_aliasing={{0}: (0, {})} | custom-call | flops 939524096 | bytes 14680064 | tf_op jit(solution)/shard_map/forward/pallas_call | solution.py:102
  30.4 0.0 collective-permute-done.6.right_ref
  30.4 0.4 collective-permute-start.7
  30.9 5.4 %forward.4 = (bf16[12288,1792]{1,0:T(8,128)(2,1)S(1)}, f32[32,1792]{1,0:T(8,128)S(1)}, f32[32,1792]{1,0:T(8,128)S(1)}) custom-call(bf16[12288,1792]{1,0:T(8,128)(2,1)S(1)} %get-tuple-element.63.refs_0_, bf16[16,8192]{1,0:T(8,128)(2,1)S(1)} %stacked.3.refs_2_.refs_1_, ...), custom_call_target="tpu_custom_call", output_to_operand_aliasing={{0}: (0, {})} | custom-call | flops 469762048 | bytes 14680064 | tf_op jit(solution)/shard_map/forward/pallas_call | solution.py:102
  36.3 0.0 copy-start.1
  36.3 0.0 collective-permute-done.7.right_ref
  36.3 3.6 %collective-permute-start.8 = (f32[32,64]{1,0:T(8,128)S(1)}, f32[32,64]{1,0:T(8,128)S(1)}, u32[]{:S(2)}, u32[]{:S(2)}) collective-permute-start(f32[32,64]{1,0:T(8,128)S(1)} %plus.10.left_ref), channel_id=1, source_target_pairs={{0,8},{1,9},{2,10},{3,11},{4,12},{5,13},{6,14},{7,15},{8,0},{9,1},... | collective-permute-start | bytes 24584 | tf_op jit(solution)/shard_map/ppermute | solution.py:481
  39.9 3.2 %forward.5 = (bf16[12288,1792]{1,0:T(8,128)(2,1)S(1)}, f32[32,1792]{1,0:T(8,128)S(1)}, f32[32,1792]{1,0:T(8,128)S(1)}) custom-call(bf16[12288,1792]{1,0:T(8,128)(2,1)S(1)} %get-tuple-element.66.refs_0_, bf16[16,8192]{1,0:T(8,128)(2,1)S(1)} %stacked.3.refs_2_.refs_1_, ...), custom_call_target="tpu_custom_call", output_to_operand_aliasing={{0}: (0, {})} | custom-call | flops 469762048 | bytes 7340032 | tf_op jit(solution)/shard_map/forward/pallas_call | solution.py:102
  43.1 0.0 collective-permute-done.8.right_ref
  43.1 3.8 %activation.1 = (bf16[12288,1792]{1,0:T(8,128)(2,1)S(1)}, bf16[32,1792]{1,0:T(8,128)(2,1)S(1)}, bf16[32,1792]{1,0:T(8,128)(2,1)S(1)}, f32[32,64]{1,0:T(8,128)S(1)}, bf16[32,2048]{1,0:T(8,128)(2,1)S(1)}) custom-call(bf16[12288,1792]{1,0:T(8,128)(2,1)S(1)} %get-tuple-element.69.refs_0_, ...), custom_call_target="tpu_custom_call", output_to_operand_aliasing={{0}: (0, {})} | custom-call | flops 469762048 | tf_op jit(solution)/shard_map/activation/pallas_call | solution.py:102
  46.9 0.5 collective-permute-start.9
  47.4 4.4 %backward.5 = (bf16[12288,1792]{1,0:T(8,128)(2,1)S(1)}, f32[16,2048]{1,0:T(8,128)S(1)}, bf16[16,2048]{1,0:T(8,128)(2,1)S(1)}) custom-call(bf16[12288,1792]{1,0:T(8,128)(2,1)S(1)} %get-tuple-element.73.refs_0_, bf16[32,1792]{1,0:T(8,128)(2,1)S(1)} %get-tuple-element.74.refs_1_.right_ref, ...), custom_call_target="tpu_custom_call", output_to_operand_aliasing={{0}: (0, {})} | custom-call | flops 469762048 | bytes 7340032 | tf_op jit(solution)/shard_map/backward/pallas_call | solution.py:102
  51.9 0.0 collective-permute-done.9.right_ref
  51.9 0.3 collective-permute-start.10
  52.2 4.5 %backward.6 = (bf16[12288,1792]{1,0:T(8,128)(2,1)S(1)}, f32[16,2048]{1,0:T(8,128)S(1)}, bf16[16,4096]{1,0:T(8,128)(2,1)S(1)}) custom-call(bf16[12288,1792]{1,0:T(8,128)(2,1)S(1)} %get-tuple-element.76.refs_0_, bf16[32,1792]{1,0:T(8,128)(2,1)S(1)} %get-tuple-element.74.refs_1_.right_ref, ...), custom_call_target="tpu_custom_call", output_to_operand_aliasing={{0}: (0, {})} | custom-call | flops 469762048 | bytes 7340032 | tf_op jit(solution)/shard_map/backward/pallas_call | solution.py:102
  56.6 0.1 collective-permute-start.13
  56.7 0.0 collective-permute-done.10.right_ref
  56.7 1.5 %collective-permute-start.11 = (f32[32,64]{1,0:T(8,128)S(1)}, f32[32,64]{1,0:T(8,128)S(1)}, u32[]{:S(2)}, u32[]{:S(2)}) collective-permute-start(f32[32,64]{1,0:T(8,128)S(1)} %plus.13.left_ref.refs_4_), channel_id=1, source_target_pairs={{0,8},{1,9},{2,10},{3,11},{4,12},{5,13},{6,14},{7,15},{8,0},{9,1},... | collective-permute-start | bytes 24584 | tf_op jit(solution)/shard_map/ppermute | solution.py:481
  58.2 4.4 %backward.7 = (bf16[12288,1792]{1,0:T(8,128)(2,1)S(1)}, f32[16,2048]{1,0:T(8,128)S(1)}, bf16[16,2048]{1,0:T(8,128)(2,1)S(1)}) custom-call(bf16[12288,1792]{1,0:T(8,128)(2,1)S(1)} %get-tuple-element.78.refs_0_, bf16[32,1792]{1,0:T(8,128)(2,1)S(1)} %get-tuple-element.74.refs_1_.right_ref, ...), custom_call_target="tpu_custom_call", output_to_operand_aliasing={{0}: (0, {})} | custom-call | flops 469762048 | bytes 7340032 | tf_op jit(solution)/shard_map/backward/pallas_call | solution.py:102
  62.7 0.0 collective-permute-done.11.right_ref
  62.7 0.3 collective-permute-start.12
  63.0 2.2 %backward.8 = (bf16[12288,1792]{1,0:T(8,128)(2,1)S(1)}, f32[16,1024]{1,0:T(8,128)S(1)}, bf16[16,3072]{1,0:T(8,128)(2,1)S(1)}) custom-call(bf16[12288,1792]{1,0:T(8,128)(2,1)S(1)} %get-tuple-element.79.refs_0_, bf16[32,1792]{1,0:T(8,128)(2,1)S(1)} %get-tuple-element.74.refs_1_.right_ref, ...), custom_call_target="tpu_custom_call", output_to_operand_aliasing={{0}: (0, {})} | custom-call | flops 234881024 | tf_op jit(solution)/shard_map/backward/pallas_call | solution.py:102
  65.2 0.0 collective-permute-done.12.right_ref
  65.2 0.9 adapter_part.1
  66.1 0.4 collective-permute-start.14
  66.5 2.2 %backward.9 = (bf16[12288,1792]{1,0:T(8,128)(2,1)S(1)}, f32[16,1024]{1,0:T(8,128)S(1)}, bf16[16,1024]{1,0:T(8,128)(2,1)S(1)}) custom-call(bf16[12288,1792]{1,0:T(8,128)(2,1)S(1)} %get-tuple-element.87.refs_0_, bf16[32,1792]{1,0:T(8,128)(2,1)S(1)} %get-tuple-element.74.refs_1_.right_ref, ...), custom_call_target="tpu_custom_call", output_to_operand_aliasing={{0}: (0, {})} | custom-call | flops 234881024 | tf_op jit(solution)/shard_map/backward/pallas_call | solution.py:102
  68.7 0.2 collective-permute-start.15
  68.9 1.0 %collective-permute-done.15.refs_8_ = bf16[16,1024]{1,0:T(8,128)(2,1)S(1)} collective-permute-done((bf16[16,1024]{1,0:T(8,128)(2,1)S(1)}, bf16[16,1024]{1,0:T(8,128)(2,1)S(1)}, u32[]{:S(2)}, u32[]{:S(2)}) %collective-permute-start.15) | collective-permute-done | bytes 32800 | tf_op jit(solution)/shard_map/ppermute | solution.py:481
  69.9 0.0 collective-permute-done.13.refs_6_
  69.9 0.0 collective-permute-done.14.refs_7_
  69.9 0.1 first_halves.1
  70.0 1.7 %collective-permute-start.16 = (bf16[8,8192]{1,0:T(8,128)(2,1)S(1)}, bf16[8,8192]{1,0:T(8,128)(2,1)S(1)}, u32[]{:S(2)}, u32[]{:S(2)}) collective-permute-start(bf16[8,8192]{1,0:T(8,128)(2,1)S(1)} %get-tuple-element.93.refs_0_), channel_id=1, source_target_pairs={{0,2},{1,3},{2,0},{3,1},{4,6},{5,7},{6,4},{7,5},{8,10},{9,11},{10,... | collective-permute-start | bytes 393224 | tf_op jit(solution)/shard_map/ppermute | solution.py:481
  71.7 2.6 %up_maps.2 = (bf16[2048,1792]{1,0:T(8,128)(2,1)}, f32[8,128]{1,0:T(8,128)S(1)}) custom-call(bf16[32,2048]{1,0:T(8,128)(2,1)S(1)} %get-tuple-element.94.left_ref, bf16[32,1792]{1,0:T(8,128)(2,1)S(1)} %get-tuple-element.74.refs_1_.right_ref, bf16[8,8192]{1,0:T(8,128)(2,1)S(1)} %get-tuple-element.93.refs_0_), custom_call_target="tpu_custom_call" | custom-call | flops 117440512 | bytes 3670016 | tf_op jit(solution)/shard_map/up_maps/pallas_call | solution.py:439
  74.3 1.4 %collective-permute-done.16.came_ref = bf16[8,8192]{1,0:T(8,128)(2,1)S(1)} collective-permute-done((bf16[8,8192]{1,0:T(8,128)(2,1)S(1)}, bf16[8,8192]{1,0:T(8,128)(2,1)S(1)}, u32[]{:S(2)}, u32[]{:S(2)}) %collective-permute-start.16) | collective-permute-done | bytes 131104 | tf_op jit(solution)/shard_map/ppermute | solution.py:481
  75.7 1.5 %collective-permute-start.17 = (bf16[4,8192]{1,0:T(4,128)(2,1)S(1)}, bf16[4,8192]{1,0:T(4,128)(2,1)S(1)}, u32[]{:S(2)}, u32[]{:S(2)}) collective-permute-start(bf16[4,8192]{1,0:T(4,128)(2,1)S(1)} %get-tuple-element.97.refs_0_), channel_id=1, source_target_pairs={{0,8},{1,9},{2,10},{3,11},{4,12},{5,13},{6,14},{7,15},{8,0},{9,1},... | collective-permute-start | bytes 196616 | tf_op jit(solution)/shard_map/ppermute | solution.py:481
  77.3 2.6 %up_maps.3 = (bf16[2048,1792]{1,0:T(8,128)(2,1)}, f32[8,128]{1,0:T(8,128)S(1)}) custom-call(bf16[32,2048]{1,0:T(8,128)(2,1)S(1)} %get-tuple-element.94.left_ref, bf16[32,1792]{1,0:T(8,128)(2,1)S(1)} %get-tuple-element.74.refs_1_.right_ref, bf16[4,8192]{1,0:T(4,128)(2,1)S(1)} %get-tuple-element.97.refs_0_, ...), custom_call_target="tpu_custom_call", output_to_operand_aliasing={{0}: (3, {})} | custom-call | flops 117440512 | bytes 3670016 | tf_op jit(solution)/shard_map/up_maps/pallas_call | solution.py:439
  79.8 1.6 %collective-permute-done.17.came_ref = bf16[4,8192]{1,0:T(4,128)(2,1)S(1)} collective-permute-done((bf16[4,8192]{1,0:T(4,128)(2,1)S(1)}, bf16[4,8192]{1,0:T(4,128)(2,1)S(1)}, u32[]{:S(2)}, u32[]{:S(2)}) %collective-permute-start.17) | collective-permute-done | bytes 65568 | tf_op jit(solution)/shard_map/ppermute | solution.py:481
  81.5 1.5 %collective-permute-start.18 = (bf16[2,8192]{1,0:T(2,128)(2,1)S(1)}, bf16[2,8192]{1,0:T(2,128)(2,1)S(1)}, u32[]{:S(2)}, u32[]{:S(2)}) collective-permute-start(bf16[2,8192]{1,0:T(2,128)(2,1)S(1)} %get-tuple-element.101.refs_0_), channel_id=1, source_target_pairs={{0,4},{1,5},{2,6},{3,7},{4,0},{5,1},{6,2},{7,3},{8,12},{9,13},{10,... | collective-permute-start | bytes 98312 | tf_op jit(solution)/shard_map/ppermute | solution.py:481
  83.0 2.1 %down_maps.1 = (bf16[512,2048]{1,0:T(8,128)(2,1)}, f32[8,128]{1,0:T(8,128)S(1)}) custom-call(bf16[32,512]{1,0:T(8,128)(2,1)S(1)} %get-tuple-element.102.left_ref, bf16[32,2048]{1,0:T(8,128)(2,1)S(1)} %get-tuple-element.103.right_ref, bf16[2,8192]{1,0:T(2,128)(2,1)S(1)} %get-tuple-element.101.refs_0_), custom_call_target="tpu_custom_call" | custom-call | flops 67108864 | bytes 2097152 | tf_op jit(solution)/shard_map/down_maps/pallas_call | solution.py:439
  85.1 0.4 collective-permute-done.18.came_ref
  85.5 0.7 final.1
  (14 shorter events, 0.2 us)
Async XLA Ops:
  0.6 11.6 %copy-start.2 = (bf16[2,8192]{1,0:T(2,128)(2,1)S(1)}, bf16[2,8192]{1,0:T(2,128)(2,1)}, u32[]{:S(2)}) copy-start(bf16[2,8192]{1,0:T(2,128)(2,1)} %refs_0_.4) | copy-start | bytes 98308
  0.6 11.0 %collective-permute-start = (bf16[2,8192]{1,0:T(2,128)(2,1)}, bf16[2,8192]{1,0:T(2,128)(2,1)S(1)}, u32[]{:S(2)}, u32[]{:S(2)}) collective-permute-start(bf16[2,8192]{1,0:T(2,128)(2,1)} %refs_0_.4), channel_id=1, source_target_pairs={{0,4},{1,5},{2,6},{3,7},{4,0},{5,1},{6,2},{7,3},{8,12},{9,13},{10,... | collective-permute-start | bytes 98312 | tf_op jit(solution)/shard_map/ppermute | solution.py:481
  3.7 7.9 %collective-permute-start.1 = (bf16[2,8192]{1,0:T(2,128)(2,1)}, bf16[2,8192]{1,0:T(2,128)(2,1)S(1)}, u32[]{:S(2)}, u32[]{:S(2)}) collective-permute-start(bf16[2,8192]{1,0:T(2,128)(2,1)} %refs_0_.4), channel_id=1, source_target_pairs={{0,8},{1,9},{2,10},{3,11},{4,12},{5,13},{6,14},{7,15},{8,0},{9,1},... | collective-permute-start | bytes 98312 | tf_op jit(solution)/shard_map/ppermute | solution.py:481
  6.3 5.9 %collective-permute-start.2 = (bf16[2,8192]{1,0:T(2,128)(2,1)}, bf16[2,8192]{1,0:T(2,128)(2,1)S(1)}, u32[]{:S(2)}, u32[]{:S(2)}) collective-permute-start(bf16[2,8192]{1,0:T(2,128)(2,1)} %refs_0_.4), channel_id=1, source_target_pairs={{0,12},{1,13},{2,14},{3,15},{4,8},{5,9},{6,10},{7,11},{8,4},{9,5},... | collective-permute-start | bytes 98312 | tf_op jit(solution)/shard_map/ppermute | solution.py:481
  12.3 5.0 %collective-permute-start.3 = (bf16[8,8192]{1,0:T(8,128)(2,1)S(1)}, bf16[8,8192]{1,0:T(8,128)(2,1)S(1)}, u32[]{:S(2)}, u32[]{:S(2)}) collective-permute-start(bf16[8,8192]{1,0:T(8,128)(2,1)S(1)} %stacked.2.refs_2_.refs_0_), channel_id=1, source_target_pairs={{0,2},{1,3},{2,0},{3,1},{4,6},{5,7},{6,4},{7,5},{8,10},{9,11},{10,... | collective-permute-start | bytes 393224 | tf_op jit(solution)/shard_map/ppermute | solution.py:481
  17.1 2.7 %copy-start = (bf16[512,2048]{1,0:T(8,128)(2,1)S(1)}, bf16[512,2048]{1,0:T(8,128)(2,1)}, u32[]{:S(2)}) copy-start(bf16[512,2048]{1,0:T(8,128)(2,1)} %refs_2_.1) | copy-start | bytes 6291460
  17.1 2.7 %copy-start.3 = (s32[32]{0:T(128)S(1)}, s32[32]{0:T(128)}, u32[]{:S(2)}) copy-start(s32[32]{0:T(128)} %param.13) | copy-start | bytes 388
  17.4 2.4 %collective-permute-start.4 = (bf16[16,8192]{1,0:T(8,128)(2,1)S(1)}, bf16[16,8192]{1,0:T(8,128)(2,1)S(1)}, u32[]{:S(2)}, u32[]{:S(2)}) collective-permute-start(bf16[16,8192]{1,0:T(8,128)(2,1)S(1)} %stacked.3.refs_2_.refs_1_), channel_id=1, source_target_pairs={{0,1},{1,0},{2,3},{3,2},{4,5},{5,4},{6,7},{7,6},{8,9},{9,8},{10,11... | collective-permute-start | bytes 786440 | tf_op jit(solution)/shard_map/ppermute | solution.py:481
  20.5 3.0 %collective-permute-start.5 = (f32[32,64]{1,0:T(8,128)S(1)}, f32[32,64]{1,0:T(8,128)S(1)}, u32[]{:S(2)}, u32[]{:S(2)}) collective-permute-start(f32[32,64]{1,0:T(8,128)S(1)} %get-tuple-element.61.refs_2_.refs_5_.left_ref), channel_id=1, source_target_pairs={{0,1},{1,0},{2,3},{3,2},{4,5},{5,4},{6,7},{7,6},{8,9},{9,8},{10,11... | collective-permute-start | bytes 24584 | tf_op jit(solution)/shard_map/ppermute | solution.py:481
  23.5 6.9 %collective-permute-start.6 = (f32[32,64]{1,0:T(8,128)S(1)}, f32[32,64]{1,0:T(8,128)S(1)}, u32[]{:S(2)}, u32[]{:S(2)}) collective-permute-start(f32[32,64]{1,0:T(8,128)S(1)} %plus.8.refs_7_.left_ref), channel_id=1, source_target_pairs={{0,2},{1,3},{2,0},{3,1},{4,6},{5,7},{6,4},{7,5},{8,10},{9,11},{10,... | collective-permute-start | bytes 24584 | tf_op jit(solution)/shard_map/ppermute | solution.py:481
  30.4 5.9 %collective-permute-start.7 = (f32[32,64]{1,0:T(8,128)S(1)}, f32[32,64]{1,0:T(8,128)S(1)}, u32[]{:S(2)}, u32[]{:S(2)}) collective-permute-start(f32[32,64]{1,0:T(8,128)S(1)} %plus.9.refs_6_.left_ref), channel_id=1, source_target_pairs={{0,4},{1,5},{2,6},{3,7},{4,0},{5,1},{6,2},{7,3},{8,12},{9,13},{10,... | collective-permute-start | bytes 24584 | tf_op jit(solution)/shard_map/ppermute | solution.py:481
  36.3 6.8 %copy-start.1 = (bf16[32,1792]{1,0:T(8,128)(2,1)S(1)}, bf16[32,1792]{1,0:T(8,128)(2,1)}, u32[]{:S(2)}) copy-start(bf16[32,1792]{1,0:T(8,128)(2,1)} %refs_3_.5) | copy-start | bytes 344068
  36.3 6.7 %collective-permute-start.8 = (f32[32,64]{1,0:T(8,128)S(1)}, f32[32,64]{1,0:T(8,128)S(1)}, u32[]{:S(2)}, u32[]{:S(2)}) collective-permute-start(f32[32,64]{1,0:T(8,128)S(1)} %plus.10.left_ref), channel_id=1, source_target_pairs={{0,8},{1,9},{2,10},{3,11},{4,12},{5,13},{6,14},{7,15},{8,0},{9,1},... | collective-permute-start | bytes 24584 | tf_op jit(solution)/shard_map/ppermute | solution.py:481
  46.9 5.0 %collective-permute-start.9 = (f32[32,64]{1,0:T(8,128)S(1)}, f32[32,64]{1,0:T(8,128)S(1)}, u32[]{:S(2)}, u32[]{:S(2)}) collective-permute-start(f32[32,64]{1,0:T(8,128)S(1)} %get-tuple-element.72.left_ref.refs_4_), channel_id=1, source_target_pairs={{0,2},{1,3},{2,0},{3,1},{4,6},{5,7},{6,4},{7,5},{8,10},{9,11},{10,... | collective-permute-start | bytes 24584 | tf_op jit(solution)/shard_map/ppermute | solution.py:481
  51.9 4.8 %collective-permute-start.10 = (f32[32,64]{1,0:T(8,128)S(1)}, f32[32,64]{1,0:T(8,128)S(1)}, u32[]{:S(2)}, u32[]{:S(2)}) collective-permute-start(f32[32,64]{1,0:T(8,128)S(1)} %plus.12.left_ref.refs_5_), channel_id=1, source_target_pairs={{0,4},{1,5},{2,6},{3,7},{4,0},{5,1},{6,2},{7,3},{8,12},{9,13},{10,... | collective-permute-start | bytes 24584 | tf_op jit(solution)/shard_map/ppermute | solution.py:481
  56.6 13.3 %collective-permute-start.13 = (bf16[16,4096]{1,0:T(8,128)(2,1)S(1)}, bf16[16,4096]{1,0:T(8,128)(2,1)S(1)}, u32[]{:S(2)}, u32[]{:S(2)}) collective-permute-start(bf16[16,4096]{1,0:T(8,128)(2,1)S(1)} %get-tuple-element.90), channel_id=1, source_target_pairs={{0,1},{1,0},{2,3},{3,2},{4,5},{5,4},{6,7},{7,6},{8,9},{9,8},{10,11... | collective-permute-start | bytes 393224 | tf_op jit(solution)/shard_map/ppermute | solution.py:481
  56.7 6.0 %collective-permute-start.11 = (f32[32,64]{1,0:T(8,128)S(1)}, f32[32,64]{1,0:T(8,128)S(1)}, u32[]{:S(2)}, u32[]{:S(2)}) collective-permute-start(f32[32,64]{1,0:T(8,128)S(1)} %plus.13.left_ref.refs_4_), channel_id=1, source_target_pairs={{0,8},{1,9},{2,10},{3,11},{4,12},{5,13},{6,14},{7,15},{8,0},{9,1},... | collective-permute-start | bytes 24584 | tf_op jit(solution)/shard_map/ppermute | solution.py:481
  62.7 2.5 %collective-permute-start.12 = (f32[32,64]{1,0:T(8,128)S(1)}, f32[32,64]{1,0:T(8,128)S(1)}, u32[]{:S(2)}, u32[]{:S(2)}) collective-permute-start(f32[32,64]{1,0:T(8,128)S(1)} %plus.14.left_ref.refs_4_), channel_id=1, source_target_pairs={{0,1},{1,0},{2,3},{3,2},{4,5},{5,4},{6,7},{7,6},{8,9},{9,8},{10,11... | collective-permute-start | bytes 24584 | tf_op jit(solution)/shard_map/ppermute | solution.py:481
  66.1 3.8 %collective-permute-start.14 = (bf16[16,3584]{1,0:T(8,128)(2,1)S(1)}, bf16[16,3584]{1,0:T(8,128)(2,1)S(1)}, u32[]{:S(2)}, u32[]{:S(2)}) collective-permute-start(bf16[16,3584]{1,0:T(8,128)(2,1)S(1)} %get-tuple-element.88.refs_3_), channel_id=1, source_target_pairs={{0,1},{1,0},{2,3},{3,2},{4,5},{5,4},{6,7},{7,6},{8,9},{9,8},{10,11... | collective-permute-start | bytes 344072 | tf_op jit(solution)/shard_map/ppermute | solution.py:481
  68.7 1.2 %collective-permute-start.15 = (bf16[16,1024]{1,0:T(8,128)(2,1)S(1)}, bf16[16,1024]{1,0:T(8,128)(2,1)S(1)}, u32[]{:S(2)}, u32[]{:S(2)}) collective-permute-start(bf16[16,1024]{1,0:T(8,128)(2,1)S(1)} %get-tuple-element.91), channel_id=1, source_target_pairs={{0,1},{1,0},{2,3},{3,2},{4,5},{5,4},{6,7},{7,6},{8,9},{9,8},{10,11... | collective-permute-start | bytes 98312 | tf_op jit(solution)/shard_map/ppermute | solution.py:481
  70.0 5.7 %collective-permute-start.16 = (bf16[8,8192]{1,0:T(8,128)(2,1)S(1)}, bf16[8,8192]{1,0:T(8,128)(2,1)S(1)}, u32[]{:S(2)}, u32[]{:S(2)}) collective-permute-start(bf16[8,8192]{1,0:T(8,128)(2,1)S(1)} %get-tuple-element.93.refs_0_), channel_id=1, source_target_pairs={{0,2},{1,3},{2,0},{3,1},{4,6},{5,7},{6,4},{7,5},{8,10},{9,11},{10,... | collective-permute-start | bytes 393224 | tf_op jit(solution)/shard_map/ppermute | solution.py:481
  75.7 5.8 %collective-permute-start.17 = (bf16[4,8192]{1,0:T(4,128)(2,1)S(1)}, bf16[4,8192]{1,0:T(4,128)(2,1)S(1)}, u32[]{:S(2)}, u32[]{:S(2)}) collective-permute-start(bf16[4,8192]{1,0:T(4,128)(2,1)S(1)} %get-tuple-element.97.refs_0_), channel_id=1, source_target_pairs={{0,8},{1,9},{2,10},{3,11},{4,12},{5,13},{6,14},{7,15},{8,0},{9,1},... | collective-permute-start | bytes 196616 | tf_op jit(solution)/shard_map/ppermute | solution.py:481
  81.5 4.0 %collective-permute-start.18 = (bf16[2,8192]{1,0:T(2,128)(2,1)S(1)}, bf16[2,8192]{1,0:T(2,128)(2,1)S(1)}, u32[]{:S(2)}, u32[]{:S(2)}) collective-permute-start(bf16[2,8192]{1,0:T(2,128)(2,1)S(1)} %get-tuple-element.101.refs_0_), channel_id=1, source_target_pairs={{0,4},{1,5},{2,6},{3,7},{4,0},{5,1},{6,2},{7,3},{8,12},{9,13},{10,... | collective-permute-start | bytes 98312 | tf_op jit(solution)/shard_map/ppermute | solution.py:481

commit v14 on v13

--- a/solution.py
+++ b/solution.py
@@ -387,36 +387,34 @@
 def halves(keep, came, after):
     rows, width = keep.shape
 
-    def halves_kernel(keep_ref, came_ref, after_ref, keep_out, send_out):
-        del after_ref
+    def halves_kernel(keep_ref, came_ref, *refs):
+        keep_out, send_out = refs[-2:]
         total = keep_ref[...] + came_ref[...].astype(jnp.float32)
         keep_out[...] = total[: rows // 2]
         send_out[...] = total[rows // 2 :].astype(jnp.bfloat16)
 
     return pl.pallas_call(
         halves_kernel,
-        in_specs=[VMEM, VMEM, ANY],
+        in_specs=[VMEM, VMEM] + [ANY] * len(after),
         out_shape=[
             jax.ShapeDtypeStruct((rows // 2, width), jnp.float32),
             jax.ShapeDtypeStruct((rows // 2, width), jnp.bfloat16),
         ],
         compiler_params=pltpu.CompilerParams(vmem_limit_bytes=40 << 20),
         name="halves",
-    )(keep, came, after)
-
-
-def final(keep, came, after):
-    def final_kernel(keep_ref, came_ref, after_ref, out_ref):
-        del after_ref
+    )(keep, came, *after)
+
+
+def final(keep, came):
+    def final_kernel(keep_ref, came_ref, out_ref):
         out_ref[...] = (keep_ref[...] + came_ref[...].astype(jnp.float32)).astype(jnp.bfloat16)
 
     return pl.pallas_call(
         final_kernel,
-        in_specs=[VMEM, VMEM, ANY],
         out_shape=jax.ShapeDtypeStruct(keep.shape, jnp.bfloat16),
         compiler_params=pltpu.CompilerParams(vmem_limit_bytes=40 << 20),
         name="final",
-    )(keep, came, after)
+    )(keep, came)
 
 
 def outer_kernel(left_ref, right_ref, *refs):
@@ -427,14 +425,14 @@
     token_ref[...] = jnp.zeros_like(token_ref)
 
 
-def outer(left, right, name, after, parts=1, part=0, earlier=None):
+def outer(left, right, name, after, parts=1, span=(0, 1), earlier=None):
     rows, height = left.shape
     width = right.shape[1]
     block = block_of(height // parts, 512)
     if block % 128:
         block = height // parts
-    steps = height // parts // block
-    first = part * steps
+    per_part = height // parts // block
+    first, steps = span[0] * per_part, (span[1] - span[0]) * per_part
     kept = [] if earlier is None else [earlier]
     return pl.pallas_call(
         outer_kernel,
@@ -456,8 +454,8 @@
         input_output_aliases={3: 0} if kept else {},
         compiler_params=pltpu.CompilerParams(vmem_limit_bytes=24 << 20),
         cost_estimate=pl.CostEstimate(
-            flops=2 * rows * (height // parts) * width,
-            bytes_accessed=2 * (height // parts) * width,
+            flops=2 * rows * steps * block * width,
+            bytes_accessed=2 * steps * block * width,
             transcendentals=0,
         ),
         name=name,
@@ -580,18 +578,21 @@
 
     keep, send = first_halves(own_parts, places, adapter_own, span, came)
     halvings = [block_owner(0, 1 << bit, count) for bit in reversed(range(len(hops) - 1))]
-    up_map_gradient = None
     for n, hop in enumerate(halvings[:-1]):
         came = swapped(send, hop)
-        beside = send
-        if n < 2:
-            up_map_gradient, beside = outer(
-                input_spread, dgate, "up_maps", send, 2, n, up_map_gradient
+        beside = [send]
+        if n == 0:
+            up_map_gradient, token = outer(input_spread, dgate, "up_maps", send, 4, (0, 3))
+            beside = [token]
+        elif n == 1:
+            up_map_gradient, token = outer(
+                input_spread, dgate, "up_maps", send, 4, (3, 4), up_map_gradient
             )
+            down_map_gradient, other_token = outer(input_span, grad_spread, "down_maps", send)
+            beside = [token, other_token]
         keep, send = halves(keep, came, beside)
     came = swapped(send, halvings[-1])
-    down_map_gradient, beside = outer(input_span, grad_spread, "down_maps", send)
-    return (final(keep, came, beside), down_map_gradient, up_map_gradient)
+    return (final(keep, came), down_map_gradient, up_map_gradient)
 
 
 def solution(mesh):

time: 86.3 us -> 86.5 us (level)
  no operation moved by 1% of the time
where the time goes in v14:
time: 86.5 us; the launch traced here: 86.3 us
  Pallas kernels  59.2 us (68%)
  starting transfers between devices  21.3 us (25%)
  waiting for transfers between devices  4.86 us (6%)
  between operations  0.98 us (1%)
    pallas_call x13, Pallas kernels, store_call(): pl.pallas_call(body, in_specs=[VMEM] * (n_in + (not new)) + [ANY] * (n_hb...  48.9 us
    ppermute x19, starting transfers between devices, swapped(): lax.ppermute(block, 'tp', [(i, i ^ hop) for i in range(lax.axis_size('tp'...  21.3 us
    pallas_call x3, Pallas kernels, outer(): pl.pallas_call(outer_kernel, grid=(steps,), in_specs=[pl.BlockSpec((rows,...  7.74 us
    ppermute x19, waiting for transfers between devices, swapped(): lax.ppermute(block, 'tp', [(i, i ^ hop) for i in range(lax.axis_size('tp'...  4.86 us
  transfers between devices with their start and end apart: 19, of which 6 were waited for; matrix products, arithmetic and copies ran while one was open for 0% of the time, Pallas kernels for 62%

profile of v14, /device:TPU:0, one launch (start us, length us, event | category | flops | bytes accessed | tf_op | source)
XLA Modules:
  0.0 86.3 jit_solution(16348332314322626141)
XLA Ops:
  0.6 0.0 copy-start.2
  0.6 3.1 %collective-permute-start = (bf16[2,8192]{1,0:T(2,128)(2,1)}, bf16[2,8192]{1,0:T(2,128)(2,1)S(1)}, u32[]{:S(2)}, u32[]{:S(2)}) collective-permute-start(bf16[2,8192]{1,0:T(2,128)(2,1)} %refs_0_.4), channel_id=1, source_target_pairs={{0,4},{1,5},{2,6},{3,7},{4,0},{5,1},{6,2},{7,3},{8,12},{9,13},{10,... | collective-permute-start | bytes 98312 | tf_op jit(solution)/shard_map/ppermute | solution.py:479
  3.7 2.6 %collective-permute-start.1 = (bf16[2,8192]{1,0:T(2,128)(2,1)}, bf16[2,8192]{1,0:T(2,128)(2,1)S(1)}, u32[]{:S(2)}, u32[]{:S(2)}) collective-permute-start(bf16[2,8192]{1,0:T(2,128)(2,1)} %refs_0_.4), channel_id=1, source_target_pairs={{0,8},{1,9},{2,10},{3,11},{4,12},{5,13},{6,14},{7,15},{8,0},{9,1},... | collective-permute-start | bytes 98312 | tf_op jit(solution)/shard_map/ppermute | solution.py:479
  6.3 0.0 collective-permute-start.2
  6.3 5.3 %fetch.4 = (bf16[12288,1792]{1,0:T(8,128)(2,1)S(1)}, f32[8,128]{1,0:T(8,128)S(1)}) custom-call(bf16[8192,1792]{1,0:T(8,128)(2,1)} %refs_4_.3, bf16[8192,1792]{1,0:T(8,128)(2,1)} %refs_3_.7), custom_call_target="tpu_custom_call" | custom-call | bytes 14680064 | tf_op jit(solution)/shard_map/fetch/pallas_call | solution.py:102
  11.7 0.0 collective-permute-done.refs_1_
  11.7 0.0 collective-permute-done.1.refs_2_
  11.7 0.6 collective-permute-done.2.refs_3_
  12.2 0.1 stacked.2.refs_2_.refs_0_
  12.3 1.6 %collective-permute-start.3 = (bf16[8,8192]{1,0:T(8,128)(2,1)S(1)}, bf16[8,8192]{1,0:T(8,128)(2,1)S(1)}, u32[]{:S(2)}, u32[]{:S(2)}) collective-permute-start(bf16[8,8192]{1,0:T(8,128)(2,1)S(1)} %stacked.2.refs_2_.refs_0_), channel_id=1, source_target_pairs={{0,2},{1,3},{2,0},{3,1},{4,6},{5,7},{6,4},{7,5},{8,10},{9,11},{10,... | collective-permute-start | bytes 393224 | tf_op jit(solution)/shard_map/ppermute | solution.py:479
  13.9 3.2 %fetch.5 = (bf16[12288,1792]{1,0:T(8,128)(2,1)S(1)}, f32[8,128]{1,0:T(8,128)S(1)}) custom-call(bf16[12288,1792]{1,0:T(8,128)(2,1)S(1)} %get-tuple-element.55.refs_0_, bf16[8192,1792]{1,0:T(8,128)(2,1)} %refs_4_.3, bf16[8,8192]{1,0:T(8,128)(2,1)S(1)} %stacked.2.refs_2_.refs_0_), custom_call_target="tpu_custom_call", output_to_operand_aliasing={{0}: (0, {})} | custom-call | bytes 7340032 | tf_op jit(solution)/shard_map/fetch/pallas_call | solution.py:102
  17.1 0.0 copy-start
  17.1 0.0 copy-start.3
  17.1 0.2 collective-permute-done.3.refs_1_
  17.4 0.1 collective-permute-start.4
  17.5 2.3 %fetch.6 = (bf16[12288,1792]{1,0:T(8,128)(2,1)S(1)}, f32[8,128]{1,0:T(8,128)S(1)}) custom-call(bf16[12288,1792]{1,0:T(8,128)(2,1)S(1)} %get-tuple-element.57.refs_0_, bf16[8192,1792]{1,0:T(8,128)(2,1)} %refs_3_.7, bf16[16,8192]{1,0:T(8,128)(2,1)S(1)} %stacked.3.refs_2_.refs_1_), custom_call_target="tpu_custom_call", output_to_operand_aliasing={{0}: (0, {})} | custom-call | bytes 7340032 | tf_op jit(solution)/shard_map/fetch/pallas_call | solution.py:102
  19.8 0.0 collective-permute-done.4.refs_3_.refs_2_
  19.8 0.0 copy-done
  19.8 0.7 low_part.1
  20.5 0.3 collective-permute-start.5
  20.8 2.7 %fetch.7 = (bf16[12288,1792]{1,0:T(8,128)(2,1)S(1)}, f32[8,128]{1,0:T(8,128)}) custom-call(bf16[12288,1792]{1,0:T(8,128)(2,1)S(1)} %get-tuple-element.59.refs_0_, bf16[8192,1792]{1,0:T(8,128)(2,1)} %refs_3_.7, f32[32,64]{1,0:T(8,128)S(1)} %get-tuple-element.61.refs_2_.refs_5_.left_ref), custom_call_target="tpu_custom_call", output_to_operand_aliasing={{0}: (0, {})} | custom-call | bytes 7340032 | tf_op jit(solution)/shard_map/fetch/pallas_call | solution.py:102
  23.5 0.0 collective-permute-done.5.right_ref
  23.5 1.6 %collective-permute-start.6 = (f32[32,64]{1,0:T(8,128)S(1)}, f32[32,64]{1,0:T(8,128)S(1)}, u32[]{:S(2)}, u32[]{:S(2)}) collective-permute-start(f32[32,64]{1,0:T(8,128)S(1)} %plus.8.refs_7_.left_ref), channel_id=1, source_target_pairs={{0,2},{1,3},{2,0},{3,1},{4,6},{5,7},{6,4},{7,5},{8,10},{9,11},{10,... | collective-permute-start | bytes 24584 | tf_op jit(solution)/shard_map/ppermute | solution.py:479
  25.1 5.3 %forward.3 = (bf16[12288,1792]{1,0:T(8,128)(2,1)S(1)}, f32[32,1792]{1,0:T(8,128)S(1)}, f32[32,1792]{1,0:T(8,128)S(1)}) custom-call(bf16[12288,1792]{1,0:T(8,128)(2,1)S(1)} %get-tuple-element.62.refs_0_, bf16[16,8192]{1,0:T(8,128)(2,1)S(1)} %stacked.3.refs_2_.refs_1_, ...), custom_call_target="tpu_custom_call", output_to_operand_aliasing={{0}: (0, {})} | custom-call | flops 939524096 | bytes 14680064 | tf_op jit(solution)/shard_map/forward/pallas_call | solution.py:102
  30.4 0.0 collective-permute-done.6.right_ref
  30.4 0.4 collective-permute-start.7
  30.9 5.4 %forward.4 = (bf16[12288,1792]{1,0:T(8,128)(2,1)S(1)}, f32[32,1792]{1,0:T(8,128)S(1)}, f32[32,1792]{1,0:T(8,128)S(1)}) custom-call(bf16[12288,1792]{1,0:T(8,128)(2,1)S(1)} %get-tuple-element.63.refs_0_, bf16[16,8192]{1,0:T(8,128)(2,1)S(1)} %stacked.3.refs_2_.refs_1_, ...), custom_call_target="tpu_custom_call", output_to_operand_aliasing={{0}: (0, {})} | custom-call | flops 469762048 | bytes 14680064 | tf_op jit(solution)/shard_map/forward/pallas_call | solution.py:102
  36.3 0.0 copy-start.1
  36.3 0.0 collective-permute-done.7.right_ref
  36.3 3.6 %collective-permute-start.8 = (f32[32,64]{1,0:T(8,128)S(1)}, f32[32,64]{1,0:T(8,128)S(1)}, u32[]{:S(2)}, u32[]{:S(2)}) collective-permute-start(f32[32,64]{1,0:T(8,128)S(1)} %plus.10.left_ref), channel_id=1, source_target_pairs={{0,8},{1,9},{2,10},{3,11},{4,12},{5,13},{6,14},{7,15},{8,0},{9,1},... | collective-permute-start | bytes 24584 | tf_op jit(solution)/shard_map/ppermute | solution.py:479
  39.9 3.2 %forward.5 = (bf16[12288,1792]{1,0:T(8,128)(2,1)S(1)}, f32[32,1792]{1,0:T(8,128)S(1)}, f32[32,1792]{1,0:T(8,128)S(1)}) custom-call(bf16[12288,1792]{1,0:T(8,128)(2,1)S(1)} %get-tuple-element.66.refs_0_, bf16[16,8192]{1,0:T(8,128)(2,1)S(1)} %stacked.3.refs_2_.refs_1_, ...), custom_call_target="tpu_custom_call", output_to_operand_aliasing={{0}: (0, {})} | custom-call | flops 469762048 | bytes 7340032 | tf_op jit(solution)/shard_map/forward/pallas_call | solution.py:102
  43.1 0.0 collective-permute-done.8.right_ref
  43.1 3.8 %activation.1 = (bf16[12288,1792]{1,0:T(8,128)(2,1)S(1)}, bf16[32,1792]{1,0:T(8,128)(2,1)S(1)}, bf16[32,1792]{1,0:T(8,128)(2,1)S(1)}, f32[32,64]{1,0:T(8,128)S(1)}, bf16[32,2048]{1,0:T(8,128)(2,1)S(1)}) custom-call(bf16[12288,1792]{1,0:T(8,128)(2,1)S(1)} %get-tuple-element.69.refs_0_, ...), custom_call_target="tpu_custom_call", output_to_operand_aliasing={{0}: (0, {})} | custom-call | flops 469762048 | tf_op jit(solution)/shard_map/activation/pallas_call | solution.py:102
  46.9 0.5 collective-permute-start.9
  47.4 4.4 %backward.5 = (bf16[12288,1792]{1,0:T(8,128)(2,1)S(1)}, f32[16,2048]{1,0:T(8,128)S(1)}, bf16[16,2048]{1,0:T(8,128)(2,1)S(1)}) custom-call(bf16[12288,1792]{1,0:T(8,128)(2,1)S(1)} %get-tuple-element.73.refs_0_, bf16[32,1792]{1,0:T(8,128)(2,1)S(1)} %get-tuple-element.74.refs_1_.right_ref, ...), custom_call_target="tpu_custom_call", output_to_operand_aliasing={{0}: (0, {})} | custom-call | flops 469762048 | bytes 7340032 | tf_op jit(solution)/shard_map/backward/pallas_call | solution.py:102
  51.9 0.0 collective-permute-done.9.right_ref
  51.9 0.3 collective-permute-start.10
  52.2 4.5 %backward.6 = (bf16[12288,1792]{1,0:T(8,128)(2,1)S(1)}, f32[16,2048]{1,0:T(8,128)S(1)}, bf16[16,4096]{1,0:T(8,128)(2,1)S(1)}) custom-call(bf16[12288,1792]{1,0:T(8,128)(2,1)S(1)} %get-tuple-element.76.refs_0_, bf16[32,1792]{1,0:T(8,128)(2,1)S(1)} %get-tuple-element.74.refs_1_.right_ref, ...), custom_call_target="tpu_custom_call", output_to_operand_aliasing={{0}: (0, {})} | custom-call | flops 469762048 | bytes 7340032 | tf_op jit(solution)/shard_map/backward/pallas_call | solution.py:102
  56.6 0.1 collective-permute-start.13
  56.7 0.0 collective-permute-done.10.right_ref
  56.7 1.5 %collective-permute-start.11 = (f32[32,64]{1,0:T(8,128)S(1)}, f32[32,64]{1,0:T(8,128)S(1)}, u32[]{:S(2)}, u32[]{:S(2)}) collective-permute-start(f32[32,64]{1,0:T(8,128)S(1)} %plus.13.left_ref.refs_4_), channel_id=1, source_target_pairs={{0,8},{1,9},{2,10},{3,11},{4,12},{5,13},{6,14},{7,15},{8,0},{9,1},... | collective-permute-start | bytes 24584 | tf_op jit(solution)/shard_map/ppermute | solution.py:479
  58.2 4.4 %backward.7 = (bf16[12288,1792]{1,0:T(8,128)(2,1)S(1)}, f32[16,2048]{1,0:T(8,128)S(1)}, bf16[16,2048]{1,0:T(8,128)(2,1)S(1)}) custom-call(bf16[12288,1792]{1,0:T(8,128)(2,1)S(1)} %get-tuple-element.78.refs_0_, bf16[32,1792]{1,0:T(8,128)(2,1)S(1)} %get-tuple-element.74.refs_1_.right_ref, ...), custom_call_target="tpu_custom_call", output_to_operand_aliasing={{0}: (0, {})} | custom-call | flops 469762048 | bytes 7340032 | tf_op jit(solution)/shard_map/backward/pallas_call | solution.py:102
  62.7 0.0 collective-permute-done.11.right_ref
  62.7 0.3 collective-permute-start.12
  63.0 2.2 %backward.8 = (bf16[12288,1792]{1,0:T(8,128)(2,1)S(1)}, f32[16,1024]{1,0:T(8,128)S(1)}, bf16[16,3072]{1,0:T(8,128)(2,1)S(1)}) custom-call(bf16[12288,1792]{1,0:T(8,128)(2,1)S(1)} %get-tuple-element.79.refs_0_, bf16[32,1792]{1,0:T(8,128)(2,1)S(1)} %get-tuple-element.74.refs_1_.right_ref, ...), custom_call_target="tpu_custom_call", output_to_operand_aliasing={{0}: (0, {})} | custom-call | flops 234881024 | tf_op jit(solution)/shard_map/backward/pallas_call | solution.py:102
  65.2 0.0 collective-permute-done.12.right_ref
  65.2 0.9 adapter_part.1
  66.1 0.4 collective-permute-start.14
  66.5 2.2 %backward.9 = (bf16[12288,1792]{1,0:T(8,128)(2,1)S(1)}, f32[16,1024]{1,0:T(8,128)S(1)}, bf16[16,1024]{1,0:T(8,128)(2,1)S(1)}) custom-call(bf16[12288,1792]{1,0:T(8,128)(2,1)S(1)} %get-tuple-element.87.refs_0_, bf16[32,1792]{1,0:T(8,128)(2,1)S(1)} %get-tuple-element.74.refs_1_.right_ref, ...), custom_call_target="tpu_custom_call", output_to_operand_aliasing={{0}: (0, {})} | custom-call | flops 234881024 | tf_op jit(solution)/shard_map/backward/pallas_call | solution.py:102
  68.7 0.2 collective-permute-start.15
  68.9 1.0 %collective-permute-done.15.refs_8_ = bf16[16,1024]{1,0:T(8,128)(2,1)S(1)} collective-permute-done((bf16[16,1024]{1,0:T(8,128)(2,1)S(1)}, bf16[16,1024]{1,0:T(8,128)(2,1)S(1)}, u32[]{:S(2)}, u32[]{:S(2)}) %collective-permute-start.15) | collective-permute-done | bytes 32800 | tf_op jit(solution)/shard_map/ppermute | solution.py:479
  69.9 0.0 collective-permute-done.13.refs_6_
  69.9 0.0 collective-permute-done.14.refs_7_
  69.9 0.1 first_halves.1
  70.0 1.7 %collective-permute-start.16 = (bf16[8,8192]{1,0:T(8,128)(2,1)S(1)}, bf16[8,8192]{1,0:T(8,128)(2,1)S(1)}, u32[]{:S(2)}, u32[]{:S(2)}) collective-permute-start(bf16[8,8192]{1,0:T(8,128)(2,1)S(1)} %get-tuple-element.93.refs_0_), channel_id=1, source_target_pairs={{0,2},{1,3},{2,0},{3,1},{4,6},{5,7},{6,4},{7,5},{8,10},{9,11},{10,... | collective-permute-start | bytes 393224 | tf_op jit(solution)/shard_map/ppermute | solution.py:479
  71.7 3.8 %up_maps.2 = (bf16[2048,1792]{1,0:T(8,128)(2,1)}, f32[8,128]{1,0:T(8,128)S(1)}) custom-call(bf16[32,2048]{1,0:T(8,128)(2,1)S(1)} %get-tuple-element.94.left_ref, bf16[32,1792]{1,0:T(8,128)(2,1)S(1)} %get-tuple-element.74.refs_1_.right_ref, bf16[8,8192]{1,0:T(8,128)(2,1)S(1)} %get-tuple-element.93.refs_0_), custom_call_target="tpu_custom_call" | custom-call | flops 176160768 | bytes 5505024 | tf_op jit(solution)/shard_map/up_maps/pallas_call | solution.py:437
  75.5 0.2 collective-permute-done.16.came_ref
  75.7 1.5 %collective-permute-start.17 = (bf16[4,8192]{1,0:T(4,128)(2,1)S(1)}, bf16[4,8192]{1,0:T(4,128)(2,1)S(1)}, u32[]{:S(2)}, u32[]{:S(2)}) collective-permute-start(bf16[4,8192]{1,0:T(4,128)(2,1)S(1)} %get-tuple-element.97.refs_0_), channel_id=1, source_target_pairs={{0,8},{1,9},{2,10},{3,11},{4,12},{5,13},{6,14},{7,15},{8,0},{9,1},... | collective-permute-start | bytes 196616 | tf_op jit(solution)/shard_map/ppermute | solution.py:479
  77.3 1.9 %up_maps.3 = (bf16[2048,1792]{1,0:T(8,128)(2,1)}, f32[8,128]{1,0:T(8,128)S(1)}) custom-call(bf16[32,2048]{1,0:T(8,128)(2,1)S(1)} %get-tuple-element.94.left_ref, bf16[32,1792]{1,0:T(8,128)(2,1)S(1)} %get-tuple-element.74.refs_1_.right_ref, bf16[4,8192]{1,0:T(4,128)(2,1)S(1)} %get-tuple-element.97.refs_0_, ...), custom_call_target="tpu_custom_call", output_to_operand_aliasing={{0}: (3, {})} | custom-call | flops 58720256 | bytes 1835008 | tf_op jit(solution)/shard_map/up_maps/pallas_call | solution.py:437
  79.2 2.1 %down_maps.1 = (bf16[512,2048]{1,0:T(8,128)(2,1)}, f32[8,128]{1,0:T(8,128)S(1)}) custom-call(bf16[32,512]{1,0:T(8,128)(2,1)S(1)} %get-tuple-element.100.left_ref, bf16[32,2048]{1,0:T(8,128)(2,1)S(1)} %get-tuple-element.101.right_ref, bf16[4,8192]{1,0:T(4,128)(2,1)S(1)} %get-tuple-element.97.refs_0_), custom_call_target="tpu_custom_call" | custom-call | flops 67108864 | bytes 2097152 | tf_op jit(solution)/shard_map/down_maps/pallas_call | solution.py:437
  81.2 0.4 collective-permute-done.17.came_ref
  81.7 1.6 %collective-permute-start.18 = (bf16[2,8192]{1,0:T(2,128)(2,1)S(1)}, bf16[2,8192]{1,0:T(2,128)(2,1)S(1)}, u32[]{:S(2)}, u32[]{:S(2)}) collective-permute-start(bf16[2,8192]{1,0:T(2,128)(2,1)S(1)} %get-tuple-element.104), channel_id=1, source_target_pairs={{0,4},{1,5},{2,6},{3,7},{4,0},{5,1},{6,2},{7,3},{8,12},{9,13},{10,... | collective-permute-start | bytes 98312 | tf_op jit(solution)/shard_map/ppermute | solution.py:479
  83.3 2.4 %collective-permute-done.18.came_ref = bf16[2,8192]{1,0:T(2,128)(2,1)S(1)} collective-permute-done((bf16[2,8192]{1,0:T(2,128)(2,1)S(1)}, bf16[2,8192]{1,0:T(2,128)(2,1)S(1)}, u32[]{:S(2)}, u32[]{:S(2)}) %collective-permute-start.18) | collective-permute-done | bytes 32800 | tf_op jit(solution)/shard_map/ppermute | solution.py:479
  85.7 0.7 final.1
  (14 shorter events, 0.2 us)
Async XLA Ops:
  0.6 11.6 %copy-start.2 = (bf16[2,8192]{1,0:T(2,128)(2,1)S(1)}, bf16[2,8192]{1,0:T(2,128)(2,1)}, u32[]{:S(2)}) copy-start(bf16[2,8192]{1,0:T(2,128)(2,1)} %refs_0_.4) | copy-start | bytes 98308
  0.6 11.0 %collective-permute-start = (bf16[2,8192]{1,0:T(2,128)(2,1)}, bf16[2,8192]{1,0:T(2,128)(2,1)S(1)}, u32[]{:S(2)}, u32[]{:S(2)}) collective-permute-start(bf16[2,8192]{1,0:T(2,128)(2,1)} %refs_0_.4), channel_id=1, source_target_pairs={{0,4},{1,5},{2,6},{3,7},{4,0},{5,1},{6,2},{7,3},{8,12},{9,13},{10,... | collective-permute-start | bytes 98312 | tf_op jit(solution)/shard_map/ppermute | solution.py:479
  3.7 7.9 %collective-permute-start.1 = (bf16[2,8192]{1,0:T(2,128)(2,1)}, bf16[2,8192]{1,0:T(2,128)(2,1)S(1)}, u32[]{:S(2)}, u32[]{:S(2)}) collective-permute-start(bf16[2,8192]{1,0:T(2,128)(2,1)} %refs_0_.4), channel_id=1, source_target_pairs={{0,8},{1,9},{2,10},{3,11},{4,12},{5,13},{6,14},{7,15},{8,0},{9,1},... | collective-permute-start | bytes 98312 | tf_op jit(solution)/shard_map/ppermute | solution.py:479
  6.3 5.9 %collective-permute-start.2 = (bf16[2,8192]{1,0:T(2,128)(2,1)}, bf16[2,8192]{1,0:T(2,128)(2,1)S(1)}, u32[]{:S(2)}, u32[]{:S(2)}) collective-permute-start(bf16[2,8192]{1,0:T(2,128)(2,1)} %refs_0_.4), channel_id=1, source_target_pairs={{0,12},{1,13},{2,14},{3,15},{4,8},{5,9},{6,10},{7,11},{8,4},{9,5},... | collective-permute-start | bytes 98312 | tf_op jit(solution)/shard_map/ppermute | solution.py:479
  12.3 5.0 %collective-permute-start.3 = (bf16[8,8192]{1,0:T(8,128)(2,1)S(1)}, bf16[8,8192]{1,0:T(8,128)(2,1)S(1)}, u32[]{:S(2)}, u32[]{:S(2)}) collective-permute-start(bf16[8,8192]{1,0:T(8,128)(2,1)S(1)} %stacked.2.refs_2_.refs_0_), channel_id=1, source_target_pairs={{0,2},{1,3},{2,0},{3,1},{4,6},{5,7},{6,4},{7,5},{8,10},{9,11},{10,... | collective-permute-start | bytes 393224 | tf_op jit(solution)/shard_map/ppermute | solution.py:479
  17.1 2.7 %copy-start = (bf16[512,2048]{1,0:T(8,128)(2,1)S(1)}, bf16[512,2048]{1,0:T(8,128)(2,1)}, u32[]{:S(2)}) copy-start(bf16[512,2048]{1,0:T(8,128)(2,1)} %refs_2_.1) | copy-start | bytes 6291460
  17.1 2.7 %copy-start.3 = (s32[32]{0:T(128)S(1)}, s32[32]{0:T(128)}, u32[]{:S(2)}) copy-start(s32[32]{0:T(128)} %param.13) | copy-start | bytes 388
  17.4 2.4 %collective-permute-start.4 = (bf16[16,8192]{1,0:T(8,128)(2,1)S(1)}, bf16[16,8192]{1,0:T(8,128)(2,1)S(1)}, u32[]{:S(2)}, u32[]{:S(2)}) collective-permute-start(bf16[16,8192]{1,0:T(8,128)(2,1)S(1)} %stacked.3.refs_2_.refs_1_), channel_id=1, source_target_pairs={{0,1},{1,0},{2,3},{3,2},{4,5},{5,4},{6,7},{7,6},{8,9},{9,8},{10,11... | collective-permute-start | bytes 786440 | tf_op jit(solution)/shard_map/ppermute | solution.py:479
  20.5 3.0 %collective-permute-start.5 = (f32[32,64]{1,0:T(8,128)S(1)}, f32[32,64]{1,0:T(8,128)S(1)}, u32[]{:S(2)}, u32[]{:S(2)}) collective-permute-start(f32[32,64]{1,0:T(8,128)S(1)} %get-tuple-element.61.refs_2_.refs_5_.left_ref), channel_id=1, source_target_pairs={{0,1},{1,0},{2,3},{3,2},{4,5},{5,4},{6,7},{7,6},{8,9},{9,8},{10,11... | collective-permute-start | bytes 24584 | tf_op jit(solution)/shard_map/ppermute | solution.py:479
  23.5 6.9 %collective-permute-start.6 = (f32[32,64]{1,0:T(8,128)S(1)}, f32[32,64]{1,0:T(8,128)S(1)}, u32[]{:S(2)}, u32[]{:S(2)}) collective-permute-start(f32[32,64]{1,0:T(8,128)S(1)} %plus.8.refs_7_.left_ref), channel_id=1, source_target_pairs={{0,2},{1,3},{2,0},{3,1},{4,6},{5,7},{6,4},{7,5},{8,10},{9,11},{10,... | collective-permute-start | bytes 24584 | tf_op jit(solution)/shard_map/ppermute | solution.py:479
  30.4 5.9 %collective-permute-start.7 = (f32[32,64]{1,0:T(8,128)S(1)}, f32[32,64]{1,0:T(8,128)S(1)}, u32[]{:S(2)}, u32[]{:S(2)}) collective-permute-start(f32[32,64]{1,0:T(8,128)S(1)} %plus.9.refs_6_.left_ref), channel_id=1, source_target_pairs={{0,4},{1,5},{2,6},{3,7},{4,0},{5,1},{6,2},{7,3},{8,12},{9,13},{10,... | collective-permute-start | bytes 24584 | tf_op jit(solution)/shard_map/ppermute | solution.py:479
  36.3 6.8 %copy-start.1 = (bf16[32,1792]{1,0:T(8,128)(2,1)S(1)}, bf16[32,1792]{1,0:T(8,128)(2,1)}, u32[]{:S(2)}) copy-start(bf16[32,1792]{1,0:T(8,128)(2,1)} %refs_3_.5) | copy-start | bytes 344068
  36.3 6.7 %collective-permute-start.8 = (f32[32,64]{1,0:T(8,128)S(1)}, f32[32,64]{1,0:T(8,128)S(1)}, u32[]{:S(2)}, u32[]{:S(2)}) collective-permute-start(f32[32,64]{1,0:T(8,128)S(1)} %plus.10.left_ref), channel_id=1, source_target_pairs={{0,8},{1,9},{2,10},{3,11},{4,12},{5,13},{6,14},{7,15},{8,0},{9,1},... | collective-permute-start | bytes 24584 | tf_op jit(solution)/shard_map/ppermute | solution.py:479
  46.9 5.0 %collective-permute-start.9 = (f32[32,64]{1,0:T(8,128)S(1)}, f32[32,64]{1,0:T(8,128)S(1)}, u32[]{:S(2)}, u32[]{:S(2)}) collective-permute-start(f32[32,64]{1,0:T(8,128)S(1)} %get-tuple-element.72.left_ref.refs_4_), channel_id=1, source_target_pairs={{0,2},{1,3},{2,0},{3,1},{4,6},{5,7},{6,4},{7,5},{8,10},{9,11},{10,... | collective-permute-start | bytes 24584 | tf_op jit(solution)/shard_map/ppermute | solution.py:479
  51.9 4.8 %collective-permute-start.10 = (f32[32,64]{1,0:T(8,128)S(1)}, f32[32,64]{1,0:T(8,128)S(1)}, u32[]{:S(2)}, u32[]{:S(2)}) collective-permute-start(f32[32,64]{1,0:T(8,128)S(1)} %plus.12.left_ref.refs_5_), channel_id=1, source_target_pairs={{0,4},{1,5},{2,6},{3,7},{4,0},{5,1},{6,2},{7,3},{8,12},{9,13},{10,... | collective-permute-start | bytes 24584 | tf_op jit(solution)/shard_map/ppermute | solution.py:479
  56.6 13.3 %collective-permute-start.13 = (bf16[16,4096]{1,0:T(8,128)(2,1)S(1)}, bf16[16,4096]{1,0:T(8,128)(2,1)S(1)}, u32[]{:S(2)}, u32[]{:S(2)}) collective-permute-start(bf16[16,4096]{1,0:T(8,128)(2,1)S(1)} %get-tuple-element.90), channel_id=1, source_target_pairs={{0,1},{1,0},{2,3},{3,2},{4,5},{5,4},{6,7},{7,6},{8,9},{9,8},{10,11... | collective-permute-start | bytes 393224 | tf_op jit(solution)/shard_map/ppermute | solution.py:479
  56.7 6.0 %collective-permute-start.11 = (f32[32,64]{1,0:T(8,128)S(1)}, f32[32,64]{1,0:T(8,128)S(1)}, u32[]{:S(2)}, u32[]{:S(2)}) collective-permute-start(f32[32,64]{1,0:T(8,128)S(1)} %plus.13.left_ref.refs_4_), channel_id=1, source_target_pairs={{0,8},{1,9},{2,10},{3,11},{4,12},{5,13},{6,14},{7,15},{8,0},{9,1},... | collective-permute-start | bytes 24584 | tf_op jit(solution)/shard_map/ppermute | solution.py:479
  62.7 2.5 %collective-permute-start.12 = (f32[32,64]{1,0:T(8,128)S(1)}, f32[32,64]{1,0:T(8,128)S(1)}, u32[]{:S(2)}, u32[]{:S(2)}) collective-permute-start(f32[32,64]{1,0:T(8,128)S(1)} %plus.14.left_ref.refs_4_), channel_id=1, source_target_pairs={{0,1},{1,0},{2,3},{3,2},{4,5},{5,4},{6,7},{7,6},{8,9},{9,8},{10,11... | collective-permute-start | bytes 24584 | tf_op jit(solution)/shard_map/ppermute | solution.py:479
  66.1 3.8 %collective-permute-start.14 = (bf16[16,3584]{1,0:T(8,128)(2,1)S(1)}, bf16[16,3584]{1,0:T(8,128)(2,1)S(1)}, u32[]{:S(2)}, u32[]{:S(2)}) collective-permute-start(bf16[16,3584]{1,0:T(8,128)(2,1)S(1)} %get-tuple-element.88.refs_3_), channel_id=1, source_target_pairs={{0,1},{1,0},{2,3},{3,2},{4,5},{5,4},{6,7},{7,6},{8,9},{9,8},{10,11... | collective-permute-start | bytes 344072 | tf_op jit(solution)/shard_map/ppermute | solution.py:479
  68.7 1.2 %collective-permute-start.15 = (bf16[16,1024]{1,0:T(8,128)(2,1)S(1)}, bf16[16,1024]{1,0:T(8,128)(2,1)S(1)}, u32[]{:S(2)}, u32[]{:S(2)}) collective-permute-start(bf16[16,1024]{1,0:T(8,128)(2,1)S(1)} %get-tuple-element.91), channel_id=1, source_target_pairs={{0,1},{1,0},{2,3},{3,2},{4,5},{5,4},{6,7},{7,6},{8,9},{9,8},{10,11... | collective-permute-start | bytes 98312 | tf_op jit(solution)/shard_map/ppermute | solution.py:479
  70.0 5.7 %collective-permute-start.16 = (bf16[8,8192]{1,0:T(8,128)(2,1)S(1)}, bf16[8,8192]{1,0:T(8,128)(2,1)S(1)}, u32[]{:S(2)}, u32[]{:S(2)}) collective-permute-start(bf16[8,8192]{1,0:T(8,128)(2,1)S(1)} %get-tuple-element.93.refs_0_), channel_id=1, source_target_pairs={{0,2},{1,3},{2,0},{3,1},{4,6},{5,7},{6,4},{7,5},{8,10},{9,11},{10,... | collective-permute-start | bytes 393224 | tf_op jit(solution)/shard_map/ppermute | solution.py:479
  75.7 5.9 %collective-permute-start.17 = (bf16[4,8192]{1,0:T(4,128)(2,1)S(1)}, bf16[4,8192]{1,0:T(4,128)(2,1)S(1)}, u32[]{:S(2)}, u32[]{:S(2)}) collective-permute-start(bf16[4,8192]{1,0:T(4,128)(2,1)S(1)} %get-tuple-element.97.refs_0_), channel_id=1, source_target_pairs={{0,8},{1,9},{2,10},{3,11},{4,12},{5,13},{6,14},{7,15},{8,0},{9,1},... | collective-permute-start | bytes 196616 | tf_op jit(solution)/shard_map/ppermute | solution.py:479
  81.7 4.0 %collective-permute-start.18 = (bf16[2,8192]{1,0:T(2,128)(2,1)S(1)}, bf16[2,8192]{1,0:T(2,128)(2,1)S(1)}, u32[]{:S(2)}, u32[]{:S(2)}) collective-permute-start(bf16[2,8192]{1,0:T(2,128)(2,1)S(1)} %get-tuple-element.104), channel_id=1, source_target_pairs={{0,4},{1,5},{2,6},{3,7},{4,0},{5,1},{6,2},{7,3},{8,12},{9,13},{10,... | collective-permute-start | bytes 98312 | tf_op jit(solution)/shard_map/ppermute | solution.py:479

commit v15 on v14

--- a/solution.py
+++ b/solution.py
@@ -405,16 +405,41 @@
     )(keep, came, *after)
 
 
-def final(keep, came):
-    def final_kernel(keep_ref, came_ref, out_ref):
-        out_ref[...] = (keep_ref[...] + came_ref[...].astype(jnp.float32)).astype(jnp.bfloat16)
+def quarters(keep, came, after):
+    rows, width = keep.shape
+    quarter = rows // 4
+
+    def quarters_kernel(keep_ref, came_ref, *refs):
+        keep_out, *sends = refs[-4:]
+        total = keep_ref[...] + came_ref[...].astype(jnp.float32)
+        keep_out[...] = total[:quarter]
+        for n, send_out in enumerate(sends, 1):
+            send_out[...] = total[n * quarter : (n + 1) * quarter].astype(jnp.bfloat16)
+
+    return pl.pallas_call(
+        quarters_kernel,
+        in_specs=[VMEM, VMEM] + [ANY] * len(after),
+        out_shape=[jax.ShapeDtypeStruct((quarter, width), jnp.float32)]
+        + [jax.ShapeDtypeStruct((quarter, width), jnp.bfloat16)] * 3,
+        compiler_params=pltpu.CompilerParams(vmem_limit_bytes=40 << 20),
+        name="quarters",
+    )(keep, came, *after)
+
+
+def final(keep, came, after):
+    def final_kernel(keep_ref, *refs):
+        total = keep_ref[...]
+        for ref in refs[: len(came)]:
+            total = total + ref[...].astype(jnp.float32)
+        refs[-1][...] = total.astype(jnp.bfloat16)
 
     return pl.pallas_call(
         final_kernel,
+        in_specs=[VMEM] * (1 + len(came)) + [ANY] * len(after),
         out_shape=jax.ShapeDtypeStruct(keep.shape, jnp.bfloat16),
         compiler_params=pltpu.CompilerParams(vmem_limit_bytes=40 << 20),
         name="final",
-    )(keep, came)
+    )(keep, *came, *after)
 
 
 def outer_kernel(left_ref, right_ref, *refs):
@@ -577,22 +602,21 @@
             waiting = []
 
     keep, send = first_halves(own_parts, places, adapter_own, span, came)
-    halvings = [block_owner(0, 1 << bit, count) for bit in reversed(range(len(hops) - 1))]
-    for n, hop in enumerate(halvings[:-1]):
+    halvings = [block_owner(0, 1 << bit, count) for bit in reversed(range(2, len(hops) - 1))]
+    for n, hop in enumerate(halvings):
         came = swapped(send, hop)
         beside = [send]
-        if n == 0:
+        if n == len(halvings) - 1:
             up_map_gradient, token = outer(input_spread, dgate, "up_maps", send, 4, (0, 3))
-            beside = [token]
-        elif n == 1:
-            up_map_gradient, token = outer(
-                input_spread, dgate, "up_maps", send, 4, (3, 4), up_map_gradient
-            )
-            down_map_gradient, other_token = outer(input_span, grad_spread, "down_maps", send)
-            beside = [token, other_token]
-        keep, send = halves(keep, came, beside)
-    came = swapped(send, halvings[-1])
-    return (final(keep, came), down_map_gradient, up_map_gradient)
+            keep, *sends = quarters(keep, came, [token])
+        else:
+            keep, send = halves(keep, came, beside)
+    came = [swapped(sends[n - 1], block_owner(0, n, count)) for n in (3, 2, 1)]
+    up_map_gradient, token = outer(
+        input_spread, dgate, "up_maps", sends[0], 4, (3, 4), up_map_gradient
+    )
+    down_map_gradient, other_token = outer(input_span, grad_spread, "down_maps", sends[0])
+    return (final(keep, came, [token, other_token]), down_map_gradient, up_map_gradient)
 
 
 def solution(mesh):

time: 86.5 us -> 84.9 us (0.982)
  waiting for transfers between devices: 4.86 us -> 2.08 us
  starting transfers between devices: 21.3 us -> 22.6 us
    ppermute x19 -> x20, waiting for transfers between devices: 4.86 us -> 2.08 us  [swapped(): lax.ppermute(block, 'tp', [(i, i ^ hop) for i in range(lax.axis_size('tp'...]
    ppermute x19 -> x20, starting transfers between devices: 21.3 us -> 22.6 us  [swapped(): lax.ppermute(block, 'tp', [(i, i ^ hop) for i in range(lax.axis_size('tp'...]
  transfers between devices with their start and end apart: 19 -> 20, of which waited for: 6 -> 4; matrix products, arithmetic and copies ran while one was open for 0% -> 0% of each run, Pallas kernels for 62% -> 63%
where the time goes in v15:
time: 84.9 us; the launch traced here: 84.8 us
  Pallas kernels  59.1 us (70%)
  starting transfers between devices  22.6 us (27%)
  waiting for transfers between devices  2.08 us (2%)
  between operations  0.98 us (1%)
    pallas_call x13, Pallas kernels, store_call(): pl.pallas_call(body, in_specs=[VMEM] * (n_in + (not new)) + [ANY] * (n_hb...  48.9 us
    ppermute x20, starting transfers between devices, swapped(): lax.ppermute(block, 'tp', [(i, i ^ hop) for i in range(lax.axis_size('tp'...  22.6 us
    pallas_call x3, Pallas kernels, outer(): pl.pallas_call(outer_kernel, grid=(steps,), in_specs=[pl.BlockSpec((rows,...  7.73 us
    ppermute x20, waiting for transfers between devices, swapped(): lax.ppermute(block, 'tp', [(i, i ^ hop) for i in range(lax.axis_size('tp'...  2.08 us
  transfers between devices with their start and end apart: 20, of which 4 were waited for; matrix products, arithmetic and copies ran while one was open for 0% of the time, Pallas kernels for 63%

profile of v15, /device:TPU:0, one launch (start us, length us, event | category | flops | bytes accessed | tf_op | source)
XLA Modules:
  0.0 84.8 jit_solution(15991253260200113950)
XLA Ops:
  0.6 3.1 %collective-permute-start = (bf16[2,8192]{1,0:T(2,128)(2,1)}, bf16[2,8192]{1,0:T(2,128)(2,1)S(1)}, u32[]{:S(2)}, u32[]{:S(2)}) collective-permute-start(bf16[2,8192]{1,0:T(2,128)(2,1)} %refs_0_.4), channel_id=1, source_target_pairs={{0,4},{1,5},{2,6},{3,7},{4,0},{5,1},{6,2},{7,3},{8,12},{9,13},{10,... | collective-permute-start | bytes 98312 | tf_op jit(solution)/shard_map/ppermute | solution.py:504
  3.7 2.6 %collective-permute-start.1 = (bf16[2,8192]{1,0:T(2,128)(2,1)}, bf16[2,8192]{1,0:T(2,128)(2,1)S(1)}, u32[]{:S(2)}, u32[]{:S(2)}) collective-permute-start(bf16[2,8192]{1,0:T(2,128)(2,1)} %refs_0_.4), channel_id=1, source_target_pairs={{0,8},{1,9},{2,10},{3,11},{4,12},{5,13},{6,14},{7,15},{8,0},{9,1},... | collective-permute-start | bytes 98312 | tf_op jit(solution)/shard_map/ppermute | solution.py:504
  6.3 0.0 collective-permute-start.2
  6.3 5.3 %fetch.4 = (bf16[12288,1792]{1,0:T(8,128)(2,1)S(1)}, f32[8,128]{1,0:T(8,128)S(1)}) custom-call(bf16[8192,1792]{1,0:T(8,128)(2,1)} %refs_4_.3, bf16[8192,1792]{1,0:T(8,128)(2,1)} %refs_3_.7), custom_call_target="tpu_custom_call" | custom-call | bytes 14680064 | tf_op jit(solution)/shard_map/fetch/pallas_call | solution.py:102
  11.7 0.0 collective-permute-done.refs_1_
  11.7 0.0 collective-permute-done.1.refs_2_
  11.7 0.6 collective-permute-done.2.refs_3_
  12.2 0.1 stacked.2.refs_2_.refs_0_
  12.3 1.6 %collective-permute-start.3 = (bf16[8,8192]{1,0:T(8,128)(2,1)S(1)}, bf16[8,8192]{1,0:T(8,128)(2,1)S(1)}, u32[]{:S(2)}, u32[]{:S(2)}) collective-permute-start(bf16[8,8192]{1,0:T(8,128)(2,1)S(1)} %stacked.2.refs_2_.refs_0_), channel_id=1, source_target_pairs={{0,2},{1,3},{2,0},{3,1},{4,6},{5,7},{6,4},{7,5},{8,10},{9,11},{10,... | collective-permute-start | bytes 393224 | tf_op jit(solution)/shard_map/ppermute | solution.py:504
  13.9 3.2 %fetch.5 = (bf16[12288,1792]{1,0:T(8,128)(2,1)S(1)}, f32[8,128]{1,0:T(8,128)S(1)}) custom-call(bf16[12288,1792]{1,0:T(8,128)(2,1)S(1)} %get-tuple-element.55.refs_0_, bf16[8192,1792]{1,0:T(8,128)(2,1)} %refs_4_.3, bf16[8,8192]{1,0:T(8,128)(2,1)S(1)} %stacked.2.refs_2_.refs_0_), custom_call_target="tpu_custom_call", output_to_operand_aliasing={{0}: (0, {})} | custom-call | bytes 7340032 | tf_op jit(solution)/shard_map/fetch/pallas_call | solution.py:102
  17.1 0.0 copy-start
  17.1 0.0 copy-start.3
  17.1 0.2 collective-permute-done.3.refs_1_
  17.4 0.1 collective-permute-start.4
  17.5 2.3 %fetch.6 = (bf16[12288,1792]{1,0:T(8,128)(2,1)S(1)}, f32[8,128]{1,0:T(8,128)S(1)}) custom-call(bf16[12288,1792]{1,0:T(8,128)(2,1)S(1)} %get-tuple-element.57.refs_0_, bf16[8192,1792]{1,0:T(8,128)(2,1)} %refs_3_.7, bf16[16,8192]{1,0:T(8,128)(2,1)S(1)} %stacked.3.refs_2_.refs_1_), custom_call_target="tpu_custom_call", output_to_operand_aliasing={{0}: (0, {})} | custom-call | bytes 7340032 | tf_op jit(solution)/shard_map/fetch/pallas_call | solution.py:102
  19.8 0.0 collective-permute-done.4.refs_3_.refs_2_
  19.8 0.0 copy-done
  19.8 0.7 low_part.1
  20.5 0.3 collective-permute-start.5
  20.8 2.7 %fetch.7 = (bf16[12288,1792]{1,0:T(8,128)(2,1)S(1)}, f32[8,128]{1,0:T(8,128)}) custom-call(bf16[12288,1792]{1,0:T(8,128)(2,1)S(1)} %get-tuple-element.59.refs_0_, bf16[8192,1792]{1,0:T(8,128)(2,1)} %refs_3_.7, f32[32,64]{1,0:T(8,128)S(1)} %get-tuple-element.61.refs_2_.refs_5_.left_ref), custom_call_target="tpu_custom_call", output_to_operand_aliasing={{0}: (0, {})} | custom-call | bytes 7340032 | tf_op jit(solution)/shard_map/fetch/pallas_call | solution.py:102
  23.5 0.0 collective-permute-done.5.right_ref
  23.5 1.6 %collective-permute-start.6 = (f32[32,64]{1,0:T(8,128)S(1)}, f32[32,64]{1,0:T(8,128)S(1)}, u32[]{:S(2)}, u32[]{:S(2)}) collective-permute-start(f32[32,64]{1,0:T(8,128)S(1)} %plus.8.refs_7_.left_ref), channel_id=1, source_target_pairs={{0,2},{1,3},{2,0},{3,1},{4,6},{5,7},{6,4},{7,5},{8,10},{9,11},{10,... | collective-permute-start | bytes 24584 | tf_op jit(solution)/shard_map/ppermute | solution.py:504
  25.1 5.3 %forward.3 = (bf16[12288,1792]{1,0:T(8,128)(2,1)S(1)}, f32[32,1792]{1,0:T(8,128)S(1)}, f32[32,1792]{1,0:T(8,128)S(1)}) custom-call(bf16[12288,1792]{1,0:T(8,128)(2,1)S(1)} %get-tuple-element.62.refs_0_, bf16[16,8192]{1,0:T(8,128)(2,1)S(1)} %stacked.3.refs_2_.refs_1_, ...), custom_call_target="tpu_custom_call", output_to_operand_aliasing={{0}: (0, {})} | custom-call | flops 939524096 | bytes 14680064 | tf_op jit(solution)/shard_map/forward/pallas_call | solution.py:102
  30.4 0.4 collective-permute-start.7
  30.9 5.4 %forward.4 = (bf16[12288,1792]{1,0:T(8,128)(2,1)S(1)}, f32[32,1792]{1,0:T(8,128)S(1)}, f32[32,1792]{1,0:T(8,128)S(1)}) custom-call(bf16[12288,1792]{1,0:T(8,128)(2,1)S(1)} %get-tuple-element.63.refs_0_, bf16[16,8192]{1,0:T(8,128)(2,1)S(1)} %stacked.3.refs_2_.refs_1_, ...), custom_call_target="tpu_custom_call", output_to_operand_aliasing={{0}: (0, {})} | custom-call | flops 469762048 | bytes 14680064 | tf_op jit(solution)/shard_map/forward/pallas_call | solution.py:102
  36.3 0.0 copy-start.1
  36.3 0.0 collective-permute-done.7.right_ref
  36.3 3.6 %collective-permute-start.8 = (f32[32,64]{1,0:T(8,128)S(1)}, f32[32,64]{1,0:T(8,128)S(1)}, u32[]{:S(2)}, u32[]{:S(2)}) collective-permute-start(f32[32,64]{1,0:T(8,128)S(1)} %plus.10.left_ref), channel_id=1, source_target_pairs={{0,8},{1,9},{2,10},{3,11},{4,12},{5,13},{6,14},{7,15},{8,0},{9,1},... | collective-permute-start | bytes 24584 | tf_op jit(solution)/shard_map/ppermute | solution.py:504
  39.9 3.2 %forward.5 = (bf16[12288,1792]{1,0:T(8,128)(2,1)S(1)}, f32[32,1792]{1,0:T(8,128)S(1)}, f32[32,1792]{1,0:T(8,128)S(1)}) custom-call(bf16[12288,1792]{1,0:T(8,128)(2,1)S(1)} %get-tuple-element.66.refs_0_, bf16[16,8192]{1,0:T(8,128)(2,1)S(1)} %stacked.3.refs_2_.refs_1_, ...), custom_call_target="tpu_custom_call", output_to_operand_aliasing={{0}: (0, {})} | custom-call | flops 469762048 | bytes 7340032 | tf_op jit(solution)/shard_map/forward/pallas_call | solution.py:102
  43.1 0.0 collective-permute-done.8.right_ref
  43.1 3.8 %activation.1 = (bf16[12288,1792]{1,0:T(8,128)(2,1)S(1)}, bf16[32,1792]{1,0:T(8,128)(2,1)S(1)}, bf16[32,1792]{1,0:T(8,128)(2,1)S(1)}, f32[32,64]{1,0:T(8,128)S(1)}, bf16[32,2048]{1,0:T(8,128)(2,1)S(1)}) custom-call(bf16[12288,1792]{1,0:T(8,128)(2,1)S(1)} %get-tuple-element.69.refs_0_, ...), custom_call_target="tpu_custom_call", output_to_operand_aliasing={{0}: (0, {})} | custom-call | flops 469762048 | tf_op jit(solution)/shard_map/activation/pallas_call | solution.py:102
  46.9 0.5 collective-permute-start.9
  47.4 4.4 %backward.5 = (bf16[12288,1792]{1,0:T(8,128)(2,1)S(1)}, f32[16,2048]{1,0:T(8,128)S(1)}, bf16[16,2048]{1,0:T(8,128)(2,1)S(1)}) custom-call(bf16[12288,1792]{1,0:T(8,128)(2,1)S(1)} %get-tuple-element.73.refs_0_, bf16[32,1792]{1,0:T(8,128)(2,1)S(1)} %get-tuple-element.74.refs_1_.right_ref, ...), custom_call_target="tpu_custom_call", output_to_operand_aliasing={{0}: (0, {})} | custom-call | flops 469762048 | bytes 7340032 | tf_op jit(solution)/shard_map/backward/pallas_call | solution.py:102
  51.9 0.0 collective-permute-done.9.right_ref
  51.9 0.3 collective-permute-start.10
  52.2 4.5 %backward.6 = (bf16[12288,1792]{1,0:T(8,128)(2,1)S(1)}, f32[16,2048]{1,0:T(8,128)S(1)}, bf16[16,4096]{1,0:T(8,128)(2,1)S(1)}) custom-call(bf16[12288,1792]{1,0:T(8,128)(2,1)S(1)} %get-tuple-element.76.refs_0_, bf16[32,1792]{1,0:T(8,128)(2,1)S(1)} %get-tuple-element.74.refs_1_.right_ref, ...), custom_call_target="tpu_custom_call", output_to_operand_aliasing={{0}: (0, {})} | custom-call | flops 469762048 | bytes 7340032 | tf_op jit(solution)/shard_map/backward/pallas_call | solution.py:102
  56.6 0.1 collective-permute-start.13
  56.7 0.0 collective-permute-done.10.right_ref
  56.7 1.5 %collective-permute-start.11 = (f32[32,64]{1,0:T(8,128)S(1)}, f32[32,64]{1,0:T(8,128)S(1)}, u32[]{:S(2)}, u32[]{:S(2)}) collective-permute-start(f32[32,64]{1,0:T(8,128)S(1)} %plus.13.left_ref.refs_4_), channel_id=1, source_target_pairs={{0,8},{1,9},{2,10},{3,11},{4,12},{5,13},{6,14},{7,15},{8,0},{9,1},... | collective-permute-start | bytes 24584 | tf_op jit(solution)/shard_map/ppermute | solution.py:504
  58.2 4.4 %backward.7 = (bf16[12288,1792]{1,0:T(8,128)(2,1)S(1)}, f32[16,2048]{1,0:T(8,128)S(1)}, bf16[16,2048]{1,0:T(8,128)(2,1)S(1)}) custom-call(bf16[12288,1792]{1,0:T(8,128)(2,1)S(1)} %get-tuple-element.78.refs_0_, bf16[32,1792]{1,0:T(8,128)(2,1)S(1)} %get-tuple-element.74.refs_1_.right_ref, ...), custom_call_target="tpu_custom_call", output_to_operand_aliasing={{0}: (0, {})} | custom-call | flops 469762048 | bytes 7340032 | tf_op jit(solution)/shard_map/backward/pallas_call | solution.py:102
  62.7 0.3 collective-permute-start.12
  63.0 2.2 %backward.8 = (bf16[12288,1792]{1,0:T(8,128)(2,1)S(1)}, f32[16,1024]{1,0:T(8,128)S(1)}, bf16[16,3072]{1,0:T(8,128)(2,1)S(1)}) custom-call(bf16[12288,1792]{1,0:T(8,128)(2,1)S(1)} %get-tuple-element.79.refs_0_, bf16[32,1792]{1,0:T(8,128)(2,1)S(1)} %get-tuple-element.74.refs_1_.right_ref, ...), custom_call_target="tpu_custom_call", output_to_operand_aliasing={{0}: (0, {})} | custom-call | flops 234881024 | tf_op jit(solution)/shard_map/backward/pallas_call | solution.py:102
  65.2 0.0 collective-permute-done.12.right_ref
  65.2 0.9 %adapter_part.1 = (bf16[16,512]{1,0:T(8,128)(2,1)S(1)}, bf16[16,3584]{1,0:T(8,128)(2,1)S(1)}, bf16[32,2048]{1,0:T(8,128)(2,1)S(1)}) custom-call(f32[32,64]{1,0:T(8,128)S(1)} %plus.15.refs_0_, s32[1,32]{1,0:T(1,128)S(1)} %bitcast.3, bf16[512,2048]{1,0:T(8,128)(2,1)S(1)} %copy-done, bf16[16,3072]{1,0:T(8,128)(2,1)S(1)} %get-tuple-element.81.refs_3_), custom_call_target="tpu_custom_call" | custom-call | flops 67108864 | bytes 2097152 | tf_op jit(solution)/shard_map/adapter_part/pallas_call | solution.py:301
  66.1 0.4 collective-permute-start.14
  66.5 2.2 %backward.9 = (bf16[12288,1792]{1,0:T(8,128)(2,1)S(1)}, f32[16,1024]{1,0:T(8,128)S(1)}, bf16[16,1024]{1,0:T(8,128)(2,1)S(1)}) custom-call(bf16[12288,1792]{1,0:T(8,128)(2,1)S(1)} %get-tuple-element.87.refs_0_, bf16[32,1792]{1,0:T(8,128)(2,1)S(1)} %get-tuple-element.74.refs_1_.right_ref, ...), custom_call_target="tpu_custom_call", output_to_operand_aliasing={{0}: (0, {})} | custom-call | flops 234881024 | tf_op jit(solution)/shard_map/backward/pallas_call | solution.py:102
  68.7 0.2 collective-permute-start.15
  68.9 1.0 %collective-permute-done.15.refs_8_ = bf16[16,1024]{1,0:T(8,128)(2,1)S(1)} collective-permute-done((bf16[16,1024]{1,0:T(8,128)(2,1)S(1)}, bf16[16,1024]{1,0:T(8,128)(2,1)S(1)}, u32[]{:S(2)}, u32[]{:S(2)}) %collective-permute-start.15) | collective-permute-done | bytes 32800 | tf_op jit(solution)/shard_map/ppermute | solution.py:504
  69.9 0.0 collective-permute-done.13.refs_6_
  69.9 0.0 collective-permute-done.14.refs_7_
  69.9 0.1 first_halves.1
  70.0 1.7 %collective-permute-start.16 = (bf16[8,8192]{1,0:T(8,128)(2,1)S(1)}, bf16[8,8192]{1,0:T(8,128)(2,1)S(1)}, u32[]{:S(2)}, u32[]{:S(2)}) collective-permute-start(bf16[8,8192]{1,0:T(8,128)(2,1)S(1)} %get-tuple-element.93.refs_0_), channel_id=1, source_target_pairs={{0,2},{1,3},{2,0},{3,1},{4,6},{5,7},{6,4},{7,5},{8,10},{9,11},{10,... | collective-permute-start | bytes 393224 | tf_op jit(solution)/shard_map/ppermute | solution.py:504
  71.7 3.8 %up_maps.2 = (bf16[2048,1792]{1,0:T(8,128)(2,1)}, f32[8,128]{1,0:T(8,128)S(1)}) custom-call(bf16[32,2048]{1,0:T(8,128)(2,1)S(1)} %get-tuple-element.94.left_ref, bf16[32,1792]{1,0:T(8,128)(2,1)S(1)} %get-tuple-element.74.refs_1_.right_ref, bf16[8,8192]{1,0:T(8,128)(2,1)S(1)} %get-tuple-element.93.refs_0_), custom_call_target="tpu_custom_call" | custom-call | flops 176160768 | bytes 5505024 | tf_op jit(solution)/shard_map/up_maps/pallas_call | solution.py:462
  75.5 0.2 collective-permute-done.16.came_ref
  75.7 0.1 quarters.1
  75.7 3.0 %collective-permute-start.17 = (bf16[2,8192]{1,0:T(2,128)(2,1)S(1)}, bf16[2,8192]{1,0:T(2,128)(2,1)S(1)}, u32[]{:S(2)}, u32[]{:S(2)}) collective-permute-start(bf16[2,8192]{1,0:T(2,128)(2,1)S(1)} %get-tuple-element.97), channel_id=1, source_target_pairs={{0,12},{1,13},{2,14},{3,15},{4,8},{5,9},{6,10},{7,11},{8,4},{9,5},... | collective-permute-start | bytes 98312 | tf_op jit(solution)/shard_map/ppermute | solution.py:504
  78.7 0.5 collective-permute-start.18
  79.3 0.9 %collective-permute-start.19 = (bf16[2,8192]{1,0:T(2,128)(2,1)S(1)}, bf16[2,8192]{1,0:T(2,128)(2,1)S(1)}, u32[]{:S(2)}, u32[]{:S(2)}) collective-permute-start(bf16[2,8192]{1,0:T(2,128)(2,1)S(1)} %get-tuple-element.99.refs_0_), channel_id=1, source_target_pairs={{0,4},{1,5},{2,6},{3,7},{4,0},{5,1},{6,2},{7,3},{8,12},{9,13},{10,... | collective-permute-start | bytes 98312 | tf_op jit(solution)/shard_map/ppermute | solution.py:504
  80.2 1.9 %up_maps.3 = (bf16[2048,1792]{1,0:T(8,128)(2,1)}, f32[8,128]{1,0:T(8,128)S(1)}) custom-call(bf16[32,2048]{1,0:T(8,128)(2,1)S(1)} %get-tuple-element.94.left_ref, bf16[32,1792]{1,0:T(8,128)(2,1)S(1)} %get-tuple-element.74.refs_1_.right_ref, bf16[2,8192]{1,0:T(2,128)(2,1)S(1)} %get-tuple-element.99.refs_0_, ...), custom_call_target="tpu_custom_call", output_to_operand_aliasing={{0}: (3, {})} | custom-call | flops 58720256 | bytes 1835008 | tf_op jit(solution)/shard_map/up_maps/pallas_call | solution.py:462
  82.1 2.0 %down_maps.1 = (bf16[512,2048]{1,0:T(8,128)(2,1)}, f32[8,128]{1,0:T(8,128)S(1)}) custom-call(bf16[32,512]{1,0:T(8,128)(2,1)S(1)} %get-tuple-element.102.left_ref, bf16[32,2048]{1,0:T(8,128)(2,1)S(1)} %get-tuple-element.103.right_ref, bf16[2,8192]{1,0:T(2,128)(2,1)S(1)} %get-tuple-element.99.refs_0_), custom_call_target="tpu_custom_call" | custom-call | flops 67108864 | bytes 2097152 | tf_op jit(solution)/shard_map/down_maps/pallas_call | solution.py:462
  84.1 0.0 collective-permute-done.17.refs_0_
  84.1 0.0 collective-permute-done.18.refs_1_
  84.1 0.0 collective-permute-done.19.refs_2_
  84.1 0.7 final.1
  (15 shorter events, 0.1 us)
Async XLA Ops:
  0.6 11.6 %copy-start.2 = (bf16[2,8192]{1,0:T(2,128)(2,1)S(1)}, bf16[2,8192]{1,0:T(2,128)(2,1)}, u32[]{:S(2)}) copy-start(bf16[2,8192]{1,0:T(2,128)(2,1)} %refs_0_.4) | copy-start | bytes 98308
  0.6 11.0 %collective-permute-start = (bf16[2,8192]{1,0:T(2,128)(2,1)}, bf16[2,8192]{1,0:T(2,128)(2,1)S(1)}, u32[]{:S(2)}, u32[]{:S(2)}) collective-permute-start(bf16[2,8192]{1,0:T(2,128)(2,1)} %refs_0_.4), channel_id=1, source_target_pairs={{0,4},{1,5},{2,6},{3,7},{4,0},{5,1},{6,2},{7,3},{8,12},{9,13},{10,... | collective-permute-start | bytes 98312 | tf_op jit(solution)/shard_map/ppermute | solution.py:504
  3.7 7.9 %collective-permute-start.1 = (bf16[2,8192]{1,0:T(2,128)(2,1)}, bf16[2,8192]{1,0:T(2,128)(2,1)S(1)}, u32[]{:S(2)}, u32[]{:S(2)}) collective-permute-start(bf16[2,8192]{1,0:T(2,128)(2,1)} %refs_0_.4), channel_id=1, source_target_pairs={{0,8},{1,9},{2,10},{3,11},{4,12},{5,13},{6,14},{7,15},{8,0},{9,1},... | collective-permute-start | bytes 98312 | tf_op jit(solution)/shard_map/ppermute | solution.py:504
  6.3 5.9 %collective-permute-start.2 = (bf16[2,8192]{1,0:T(2,128)(2,1)}, bf16[2,8192]{1,0:T(2,128)(2,1)S(1)}, u32[]{:S(2)}, u32[]{:S(2)}) collective-permute-start(bf16[2,8192]{1,0:T(2,128)(2,1)} %refs_0_.4), channel_id=1, source_target_pairs={{0,12},{1,13},{2,14},{3,15},{4,8},{5,9},{6,10},{7,11},{8,4},{9,5},... | collective-permute-start | bytes 98312 | tf_op jit(solution)/shard_map/ppermute | solution.py:504
  12.3 5.0 %collective-permute-start.3 = (bf16[8,8192]{1,0:T(8,128)(2,1)S(1)}, bf16[8,8192]{1,0:T(8,128)(2,1)S(1)}, u32[]{:S(2)}, u32[]{:S(2)}) collective-permute-start(bf16[8,8192]{1,0:T(8,128)(2,1)S(1)} %stacked.2.refs_2_.refs_0_), channel_id=1, source_target_pairs={{0,2},{1,3},{2,0},{3,1},{4,6},{5,7},{6,4},{7,5},{8,10},{9,11},{10,... | collective-permute-start | bytes 393224 | tf_op jit(solution)/shard_map/ppermute | solution.py:504
  17.1 2.7 %copy-start = (bf16[512,2048]{1,0:T(8,128)(2,1)S(1)}, bf16[512,2048]{1,0:T(8,128)(2,1)}, u32[]{:S(2)}) copy-start(bf16[512,2048]{1,0:T(8,128)(2,1)} %refs_2_.1) | copy-start | bytes 6291460
  17.1 2.7 %copy-start.3 = (s32[32]{0:T(128)S(1)}, s32[32]{0:T(128)}, u32[]{:S(2)}) copy-start(s32[32]{0:T(128)} %param.13) | copy-start | bytes 388
  17.4 2.4 %collective-permute-start.4 = (bf16[16,8192]{1,0:T(8,128)(2,1)S(1)}, bf16[16,8192]{1,0:T(8,128)(2,1)S(1)}, u32[]{:S(2)}, u32[]{:S(2)}) collective-permute-start(bf16[16,8192]{1,0:T(8,128)(2,1)S(1)} %stacked.3.refs_2_.refs_1_), channel_id=1, source_target_pairs={{0,1},{1,0},{2,3},{3,2},{4,5},{5,4},{6,7},{7,6},{8,9},{9,8},{10,11... | collective-permute-start | bytes 786440 | tf_op jit(solution)/shard_map/ppermute | solution.py:504
  20.5 3.0 %collective-permute-start.5 = (f32[32,64]{1,0:T(8,128)S(1)}, f32[32,64]{1,0:T(8,128)S(1)}, u32[]{:S(2)}, u32[]{:S(2)}) collective-permute-start(f32[32,64]{1,0:T(8,128)S(1)} %get-tuple-element.61.refs_2_.refs_5_.left_ref), channel_id=1, source_target_pairs={{0,1},{1,0},{2,3},{3,2},{4,5},{5,4},{6,7},{7,6},{8,9},{9,8},{10,11... | collective-permute-start | bytes 24584 | tf_op jit(solution)/shard_map/ppermute | solution.py:504
  23.5 6.9 %collective-permute-start.6 = (f32[32,64]{1,0:T(8,128)S(1)}, f32[32,64]{1,0:T(8,128)S(1)}, u32[]{:S(2)}, u32[]{:S(2)}) collective-permute-start(f32[32,64]{1,0:T(8,128)S(1)} %plus.8.refs_7_.left_ref), channel_id=1, source_target_pairs={{0,2},{1,3},{2,0},{3,1},{4,6},{5,7},{6,4},{7,5},{8,10},{9,11},{10,... | collective-permute-start | bytes 24584 | tf_op jit(solution)/shard_map/ppermute | solution.py:504
  30.4 5.9 %collective-permute-start.7 = (f32[32,64]{1,0:T(8,128)S(1)}, f32[32,64]{1,0:T(8,128)S(1)}, u32[]{:S(2)}, u32[]{:S(2)}) collective-permute-start(f32[32,64]{1,0:T(8,128)S(1)} %plus.9.refs_6_.left_ref), channel_id=1, source_target_pairs={{0,4},{1,5},{2,6},{3,7},{4,0},{5,1},{6,2},{7,3},{8,12},{9,13},{10,... | collective-permute-start | bytes 24584 | tf_op jit(solution)/shard_map/ppermute | solution.py:504
  36.3 6.8 %copy-start.1 = (bf16[32,1792]{1,0:T(8,128)(2,1)S(1)}, bf16[32,1792]{1,0:T(8,128)(2,1)}, u32[]{:S(2)}) copy-start(bf16[32,1792]{1,0:T(8,128)(2,1)} %refs_3_.5) | copy-start | bytes 344068
  36.3 6.7 %collective-permute-start.8 = (f32[32,64]{1,0:T(8,128)S(1)}, f32[32,64]{1,0:T(8,128)S(1)}, u32[]{:S(2)}, u32[]{:S(2)}) collective-permute-start(f32[32,64]{1,0:T(8,128)S(1)} %plus.10.left_ref), channel_id=1, source_target_pairs={{0,8},{1,9},{2,10},{3,11},{4,12},{5,13},{6,14},{7,15},{8,0},{9,1},... | collective-permute-start | bytes 24584 | tf_op jit(solution)/shard_map/ppermute | solution.py:504
  46.9 5.0 %collective-permute-start.9 = (f32[32,64]{1,0:T(8,128)S(1)}, f32[32,64]{1,0:T(8,128)S(1)}, u32[]{:S(2)}, u32[]{:S(2)}) collective-permute-start(f32[32,64]{1,0:T(8,128)S(1)} %get-tuple-element.72.left_ref.refs_4_), channel_id=1, source_target_pairs={{0,2},{1,3},{2,0},{3,1},{4,6},{5,7},{6,4},{7,5},{8,10},{9,11},{10,... | collective-permute-start | bytes 24584 | tf_op jit(solution)/shard_map/ppermute | solution.py:504
  51.9 4.8 %collective-permute-start.10 = (f32[32,64]{1,0:T(8,128)S(1)}, f32[32,64]{1,0:T(8,128)S(1)}, u32[]{:S(2)}, u32[]{:S(2)}) collective-permute-start(f32[32,64]{1,0:T(8,128)S(1)} %plus.12.left_ref.refs_5_), channel_id=1, source_target_pairs={{0,4},{1,5},{2,6},{3,7},{4,0},{5,1},{6,2},{7,3},{8,12},{9,13},{10,... | collective-permute-start | bytes 24584 | tf_op jit(solution)/shard_map/ppermute | solution.py:504
  56.6 13.3 %collective-permute-start.13 = (bf16[16,4096]{1,0:T(8,128)(2,1)S(1)}, bf16[16,4096]{1,0:T(8,128)(2,1)S(1)}, u32[]{:S(2)}, u32[]{:S(2)}) collective-permute-start(bf16[16,4096]{1,0:T(8,128)(2,1)S(1)} %get-tuple-element.90), channel_id=1, source_target_pairs={{0,1},{1,0},{2,3},{3,2},{4,5},{5,4},{6,7},{7,6},{8,9},{9,8},{10,11... | collective-permute-start | bytes 393224 | tf_op jit(solution)/shard_map/ppermute | solution.py:504
  56.7 6.0 %collective-permute-start.11 = (f32[32,64]{1,0:T(8,128)S(1)}, f32[32,64]{1,0:T(8,128)S(1)}, u32[]{:S(2)}, u32[]{:S(2)}) collective-permute-start(f32[32,64]{1,0:T(8,128)S(1)} %plus.13.left_ref.refs_4_), channel_id=1, source_target_pairs={{0,8},{1,9},{2,10},{3,11},{4,12},{5,13},{6,14},{7,15},{8,0},{9,1},... | collective-permute-start | bytes 24584 | tf_op jit(solution)/shard_map/ppermute | solution.py:504
  62.7 2.5 %collective-permute-start.12 = (f32[32,64]{1,0:T(8,128)S(1)}, f32[32,64]{1,0:T(8,128)S(1)}, u32[]{:S(2)}, u32[]{:S(2)}) collective-permute-start(f32[32,64]{1,0:T(8,128)S(1)} %plus.14.left_ref.refs_4_), channel_id=1, source_target_pairs={{0,1},{1,0},{2,3},{3,2},{4,5},{5,4},{6,7},{7,6},{8,9},{9,8},{10,11... | collective-permute-start | bytes 24584 | tf_op jit(solution)/shard_map/ppermute | solution.py:504
  66.1 3.8 %collective-permute-start.14 = (bf16[16,3584]{1,0:T(8,128)(2,1)S(1)}, bf16[16,3584]{1,0:T(8,128)(2,1)S(1)}, u32[]{:S(2)}, u32[]{:S(2)}) collective-permute-start(bf16[16,3584]{1,0:T(8,128)(2,1)S(1)} %get-tuple-element.88.refs_3_), channel_id=1, source_target_pairs={{0,1},{1,0},{2,3},{3,2},{4,5},{5,4},{6,7},{7,6},{8,9},{9,8},{10,11... | collective-permute-start | bytes 344072 | tf_op jit(solution)/shard_map/ppermute | solution.py:504
  68.7 1.2 %collective-permute-start.15 = (bf16[16,1024]{1,0:T(8,128)(2,1)S(1)}, bf16[16,1024]{1,0:T(8,128)(2,1)S(1)}, u32[]{:S(2)}, u32[]{:S(2)}) collective-permute-start(bf16[16,1024]{1,0:T(8,128)(2,1)S(1)} %get-tuple-element.91), channel_id=1, source_target_pairs={{0,1},{1,0},{2,3},{3,2},{4,5},{5,4},{6,7},{7,6},{8,9},{9,8},{10,11... | collective-permute-start | bytes 98312 | tf_op jit(solution)/shard_map/ppermute | solution.py:504
  70.0 5.7 %collective-permute-start.16 = (bf16[8,8192]{1,0:T(8,128)(2,1)S(1)}, bf16[8,8192]{1,0:T(8,128)(2,1)S(1)}, u32[]{:S(2)}, u32[]{:S(2)}) collective-permute-start(bf16[8,8192]{1,0:T(8,128)(2,1)S(1)} %get-tuple-element.93.refs_0_), channel_id=1, source_target_pairs={{0,2},{1,3},{2,0},{3,1},{4,6},{5,7},{6,4},{7,5},{8,10},{9,11},{10,... | collective-permute-start | bytes 393224 | tf_op jit(solution)/shard_map/ppermute | solution.py:504
  75.7 8.4 %collective-permute-start.17 = (bf16[2,8192]{1,0:T(2,128)(2,1)S(1)}, bf16[2,8192]{1,0:T(2,128)(2,1)S(1)}, u32[]{:S(2)}, u32[]{:S(2)}) collective-permute-start(bf16[2,8192]{1,0:T(2,128)(2,1)S(1)} %get-tuple-element.97), channel_id=1, source_target_pairs={{0,12},{1,13},{2,14},{3,15},{4,8},{5,9},{6,10},{7,11},{8,4},{9,5},... | collective-permute-start | bytes 98312 | tf_op jit(solution)/shard_map/ppermute | solution.py:504
  78.7 5.4 %collective-permute-start.18 = (bf16[2,8192]{1,0:T(2,128)(2,1)S(1)}, bf16[2,8192]{1,0:T(2,128)(2,1)S(1)}, u32[]{:S(2)}, u32[]{:S(2)}) collective-permute-start(bf16[2,8192]{1,0:T(2,128)(2,1)S(1)} %get-tuple-element.98), channel_id=1, source_target_pairs={{0,8},{1,9},{2,10},{3,11},{4,12},{5,13},{6,14},{7,15},{8,0},{9,1},... | collective-permute-start | bytes 98312 | tf_op jit(solution)/shard_map/ppermute | solution.py:504
  79.3 4.9 %collective-permute-start.19 = (bf16[2,8192]{1,0:T(2,128)(2,1)S(1)}, bf16[2,8192]{1,0:T(2,128)(2,1)S(1)}, u32[]{:S(2)}, u32[]{:S(2)}) collective-permute-start(bf16[2,8192]{1,0:T(2,128)(2,1)S(1)} %get-tuple-element.99.refs_0_), channel_id=1, source_target_pairs={{0,4},{1,5},{2,6},{3,7},{4,0},{5,1},{6,2},{7,3},{8,12},{9,13},{10,... | collective-permute-start | bytes 98312 | tf_op jit(solution)/shard_map/ppermute | solution.py:504

commit v16 on v15

--- a/solution.py
+++ b/solution.py
@@ -450,41 +450,34 @@
     token_ref[...] = jnp.zeros_like(token_ref)
 
 
-def outer(left, right, name, after, parts=1, span=(0, 1), earlier=None):
+def outer(left, right, name, after, largest):
     rows, height = left.shape
     width = right.shape[1]
-    block = block_of(height // parts, 512)
+    block = block_of(height, largest)
     if block % 128:
-        block = height // parts
-    per_part = height // parts // block
-    first, steps = span[0] * per_part, (span[1] - span[0]) * per_part
-    kept = [] if earlier is None else [earlier]
+        block = height
     return pl.pallas_call(
         outer_kernel,
-        grid=(steps,),
+        grid=(height // block,),
         in_specs=[
-            pl.BlockSpec((rows, block), lambda k: (0, k + first)),
+            pl.BlockSpec((rows, block), lambda k: (0, k)),
             pl.BlockSpec((rows, width), lambda k: (0, 0)),
             ANY,
-        ]
-        + [ANY] * len(kept),
+        ],
         out_specs=[
-            pl.BlockSpec((block, width), lambda k: (k + first, 0)),
+            pl.BlockSpec((block, width), lambda k: (k, 0)),
             pl.BlockSpec((8, 128), lambda k: (0, 0)),
         ],
         out_shape=[
             jax.ShapeDtypeStruct((height, width), jnp.bfloat16),
             jax.ShapeDtypeStruct((8, 128), jnp.float32),
         ],
-        input_output_aliases={3: 0} if kept else {},
         compiler_params=pltpu.CompilerParams(vmem_limit_bytes=24 << 20),
         cost_estimate=pl.CostEstimate(
-            flops=2 * rows * steps * block * width,
-            bytes_accessed=2 * steps * block * width,
-            transcendentals=0,
+            flops=2 * rows * height * width, bytes_accessed=2 * height * width, transcendentals=0
         ),
         name=name,
-    )(left, right, after, *kept)
+    )(left, right, after)
 
 
 def add_kernel(left_ref, right_ref, out_ref):
@@ -537,18 +530,22 @@
         block = stacked([block, swapped(block, hop)])
     other = swapped(block, hops[1])
     store, token = store_call(
-        mark, store, [(gate_weight, 1, 2)], [], [mark_shape], 0, "fetch", after=[block]
+        mark,
+        store,
+        [(gate_weight, 1, 2), (up_weight, 1, 3, 0)],
+        [],
+        [mark_shape],
+        0,
+        "fetch",
+        after=[block],
     )
     block = stacked([block, other], [token])
     x = [block, swapped(block, 1)]
     store, token = store_call(
-        mark, store, [(up_weight, 1, 3, 0)], [], [mark_shape], 0, "fetch", after=[block]
+        mark, store, [(up_weight, 1, 3, 1)], [], [mark_shape], 0, "fetch", after=[block]
     )
 
     input_span, low = low_part(adapter_down_maps, tenants, x, count, token)
-    store, token = store_call(
-        mark, store, [(up_weight, 1, 3, 1)], [], [mark_shape], 0, "fetch", after=[low]
-    )
     sums = []
     slots = {0: (0, 1), 1: (2, 3), 2: (4, 5), 3: (0, 1)}
     step = 0
@@ -607,16 +604,13 @@
         came = swapped(send, hop)
         beside = [send]
         if n == len(halvings) - 1:
-            up_map_gradient, token = outer(input_spread, dgate, "up_maps", send, 4, (0, 3))
+            up_map_gradient, token = outer(input_spread, dgate, "up_maps", send, 512)
             keep, *sends = quarters(keep, came, [token])
         else:
             keep, send = halves(keep, came, beside)
     came = [swapped(sends[n - 1], block_owner(0, n, count)) for n in (3, 2, 1)]
-    up_map_gradient, token = outer(
-        input_spread, dgate, "up_maps", sends[0], 4, (3, 4), up_map_gradient
-    )
-    down_map_gradient, other_token = outer(input_span, grad_spread, "down_maps", sends[0])
-    return (final(keep, came, [token, other_token]), down_map_gradient, up_map_gradient)
+    down_map_gradient, token = outer(input_span, grad_spread, "down_maps", sends[0], 256)
+    return (final(keep, came, [token]), down_map_gradient, up_map_gradient)
 
 
 def solution(mesh):

time: 84.9 us -> 83.6 us (0.985)
  Pallas kernels: 59.1 us -> 56.2 us
  waiting for transfers between devices: 2.08 us -> 4.8 us
  starting transfers between devices: 22.6 us -> 21.2 us
    ppermute x20, waiting for transfers between devices: 2.08 us -> 4.8 us  [swapped(): lax.ppermute(block, 'tp', [(i, i ^ hop) for i in range(lax.axis_size('tp'...]
    pallas_call x13 -> x12, Pallas kernels: 48.9 us -> 47.3 us  [store_call(): pl.pallas_call(body, in_specs=[VMEM] * (n_in + (not new)) + [ANY] * (n_hb...]
    ppermute x20, starting transfers between devices: 22.6 us -> 21.2 us  [swapped(): lax.ppermute(block, 'tp', [(i, i ^ hop) for i in range(lax.axis_size('tp'...]
    pallas_call x3 -> x2, Pallas kernels: 7.73 us -> 6.38 us  [outer(): pl.pallas_call(outer_kernel, grid=(height // block,), in_specs=[pl.BlockS...]
  transfers between devices with their start and end apart: 20 -> 20, of which waited for: 4 -> 5; matrix products, arithmetic and copies ran while one was open for 0% -> 0% of each run, Pallas kernels for 63% -> 61%
where the time goes in v16:
time: 83.6 us; the launch traced here: 83.4 us
  Pallas kernels  56.2 us (67%)
  starting transfers between devices  21.2 us (25%)
  waiting for transfers between devices  4.8 us (6%)
  between operations  0.95 us (1%)
    pallas_call x12, Pallas kernels, store_call(): pl.pallas_call(body, in_specs=[VMEM] * (n_in + (not new)) + [ANY] * (n_hb...  47.3 us
    ppermute x20, starting transfers between devices, swapped(): lax.ppermute(block, 'tp', [(i, i ^ hop) for i in range(lax.axis_size('tp'...  21.2 us
    pallas_call x2, Pallas kernels, outer(): pl.pallas_call(outer_kernel, grid=(height // block,), in_specs=[pl.BlockS...  6.38 us
    ppermute x20, waiting for transfers between devices, swapped(): lax.ppermute(block, 'tp', [(i, i ^ hop) for i in range(lax.axis_size('tp'...  4.8 us
  transfers between devices with their start and end apart: 20, of which 5 were waited for; matrix products, arithmetic and copies ran while one was open for 0% of the time, Pallas kernels for 61%

profile of v16, /device:TPU:0, one launch (start us, length us, event | category | flops | bytes accessed | tf_op | source)
XLA Modules:
  0.0 83.4 jit_solution(9781988714225335600)
XLA Ops:
  0.6 3.1 %collective-permute-start = (bf16[2,8192]{1,0:T(2,128)(2,1)}, bf16[2,8192]{1,0:T(2,128)(2,1)S(1)}, u32[]{:S(2)}, u32[]{:S(2)}) collective-permute-start(bf16[2,8192]{1,0:T(2,128)(2,1)} %refs_0_.4), channel_id=1, source_target_pairs={{0,4},{1,5},{2,6},{3,7},{4,0},{5,1},{6,2},{7,3},{8,12},{9,13},{10,... | collective-permute-start | bytes 98312 | tf_op jit(solution)/shard_map/ppermute | solution.py:497
  3.7 2.6 %collective-permute-start.1 = (bf16[2,8192]{1,0:T(2,128)(2,1)}, bf16[2,8192]{1,0:T(2,128)(2,1)S(1)}, u32[]{:S(2)}, u32[]{:S(2)}) collective-permute-start(bf16[2,8192]{1,0:T(2,128)(2,1)} %refs_0_.4), channel_id=1, source_target_pairs={{0,8},{1,9},{2,10},{3,11},{4,12},{5,13},{6,14},{7,15},{8,0},{9,1},... | collective-permute-start | bytes 98312 | tf_op jit(solution)/shard_map/ppermute | solution.py:497
  6.3 0.0 collective-permute-start.2
  6.3 5.3 %fetch.3 = (bf16[12288,1792]{1,0:T(8,128)(2,1)S(1)}, f32[8,128]{1,0:T(8,128)S(1)}) custom-call(bf16[8192,1792]{1,0:T(8,128)(2,1)} %refs_4_.3, bf16[8192,1792]{1,0:T(8,128)(2,1)} %refs_3_.7), custom_call_target="tpu_custom_call" | custom-call | bytes 14680064 | tf_op jit(solution)/shard_map/fetch/pallas_call | solution.py:102
  11.7 0.0 collective-permute-done.refs_1_
  11.7 0.0 collective-permute-done.1.refs_2_
  11.7 0.6 collective-permute-done.2.refs_3_
  12.2 0.1 stacked.2.refs_3_.refs_0_
  12.3 1.6 %collective-permute-start.3 = (bf16[8,8192]{1,0:T(8,128)(2,1)S(1)}, bf16[8,8192]{1,0:T(8,128)(2,1)S(1)}, u32[]{:S(2)}, u32[]{:S(2)}) collective-permute-start(bf16[8,8192]{1,0:T(8,128)(2,1)S(1)} %stacked.2.refs_3_.refs_0_), channel_id=1, source_target_pairs={{0,2},{1,3},{2,0},{3,1},{4,6},{5,7},{6,4},{7,5},{8,10},{9,11},{10,... | collective-permute-start | bytes 393224 | tf_op jit(solution)/shard_map/ppermute | solution.py:497
  13.9 4.3 %fetch.4 = (bf16[12288,1792]{1,0:T(8,128)(2,1)S(1)}, f32[8,128]{1,0:T(8,128)S(1)}) custom-call(bf16[12288,1792]{1,0:T(8,128)(2,1)S(1)} %get-tuple-element.52.refs_0_, bf16[8192,1792]{1,0:T(8,128)(2,1)} %refs_4_.3, bf16[8192,1792]{1,0:T(8,128)(2,1)} %refs_3_.7, bf16[8,8192]{1,0:T(8,128)(2,1)S(1)} %stacked.2.refs_3_.refs_0_), custom_call_target="tpu_custom_call", output_to_operand_aliasing={{0}: (0, {})} | custom-call | bytes 14680064 | tf_op jit(solution)/shard_map/fetch/pallas_call | solution.py:102
  18.2 0.0 copy-start
  18.2 0.0 copy-start.3
  18.2 0.0 collective-permute-done.3.refs_1_
  18.3 0.1 collective-permute-start.4
  18.4 2.2 %fetch.5 = (bf16[12288,1792]{1,0:T(8,128)(2,1)S(1)}, f32[8,128]{1,0:T(8,128)S(1)}) custom-call(bf16[12288,1792]{1,0:T(8,128)(2,1)S(1)} %get-tuple-element.54.refs_0_, bf16[8192,1792]{1,0:T(8,128)(2,1)} %refs_3_.7, bf16[16,8192]{1,0:T(8,128)(2,1)S(1)} %stacked.3.refs_2_.refs_1_), custom_call_target="tpu_custom_call", output_to_operand_aliasing={{0}: (0, {})} | custom-call | bytes 7340032 | tf_op jit(solution)/shard_map/fetch/pallas_call | solution.py:102
  20.6 0.0 collective-permute-done.4.refs_3_.refs_2_
  20.6 0.3 copy-done
  20.9 0.7 low_part.1
  21.6 0.1 collective-permute-start.5
  21.7 1.1 %collective-permute-done.5.right_ref = f32[32,64]{1,0:T(8,128)S(1)} collective-permute-done((f32[32,64]{1,0:T(8,128)S(1)}, f32[32,64]{1,0:T(8,128)S(1)}, u32[]{:S(2)}, u32[]{:S(2)}) %collective-permute-start.5) | collective-permute-done | bytes 8224 | tf_op jit(solution)/shard_map/ppermute | solution.py:497
  22.8 0.5 collective-permute-start.6
  23.3 5.3 %forward.3 = (bf16[12288,1792]{1,0:T(8,128)(2,1)S(1)}, f32[32,1792]{1,0:T(8,128)S(1)}, f32[32,1792]{1,0:T(8,128)S(1)}) custom-call(bf16[12288,1792]{1,0:T(8,128)(2,1)S(1)} %get-tuple-element.56.refs_0_, bf16[16,8192]{1,0:T(8,128)(2,1)S(1)} %stacked.3.refs_2_.refs_1_, ...), custom_call_target="tpu_custom_call", output_to_operand_aliasing={{0}: (0, {})} | custom-call | flops 939524096 | bytes 14680064 | tf_op jit(solution)/shard_map/forward/pallas_call | solution.py:102
  28.6 0.0 collective-permute-done.6.right_ref
  28.7 0.4 collective-permute-start.7
  29.1 5.4 %forward.4 = (bf16[12288,1792]{1,0:T(8,128)(2,1)S(1)}, f32[32,1792]{1,0:T(8,128)S(1)}, f32[32,1792]{1,0:T(8,128)S(1)}) custom-call(bf16[12288,1792]{1,0:T(8,128)(2,1)S(1)} %get-tuple-element.59.refs_0_, bf16[16,8192]{1,0:T(8,128)(2,1)S(1)} %stacked.3.refs_2_.refs_1_, ...), custom_call_target="tpu_custom_call", output_to_operand_aliasing={{0}: (0, {})} | custom-call | flops 469762048 | bytes 14680064 | tf_op jit(solution)/shard_map/forward/pallas_call | solution.py:102
  34.5 0.0 copy-start.1
  34.5 0.0 collective-permute-done.7.right_ref
  34.5 3.5 %collective-permute-start.8 = (f32[32,64]{1,0:T(8,128)S(1)}, f32[32,64]{1,0:T(8,128)S(1)}, u32[]{:S(2)}, u32[]{:S(2)}) collective-permute-start(f32[32,64]{1,0:T(8,128)S(1)} %plus.10.left_ref), channel_id=1, source_target_pairs={{0,8},{1,9},{2,10},{3,11},{4,12},{5,13},{6,14},{7,15},{8,0},{9,1},... | collective-permute-start | bytes 24584 | tf_op jit(solution)/shard_map/ppermute | solution.py:497
  38.1 3.2 %forward.5 = (bf16[12288,1792]{1,0:T(8,128)(2,1)S(1)}, f32[32,1792]{1,0:T(8,128)S(1)}, f32[32,1792]{1,0:T(8,128)S(1)}) custom-call(bf16[12288,1792]{1,0:T(8,128)(2,1)S(1)} %get-tuple-element.62.refs_0_, bf16[16,8192]{1,0:T(8,128)(2,1)S(1)} %stacked.3.refs_2_.refs_1_, ...), custom_call_target="tpu_custom_call", output_to_operand_aliasing={{0}: (0, {})} | custom-call | flops 469762048 | bytes 7340032 | tf_op jit(solution)/shard_map/forward/pallas_call | solution.py:102
  41.3 0.0 collective-permute-done.8.right_ref
  41.3 3.8 %activation.1 = (bf16[12288,1792]{1,0:T(8,128)(2,1)S(1)}, bf16[32,1792]{1,0:T(8,128)(2,1)S(1)}, bf16[32,1792]{1,0:T(8,128)(2,1)S(1)}, f32[32,64]{1,0:T(8,128)S(1)}, bf16[32,2048]{1,0:T(8,128)(2,1)S(1)}) custom-call(bf16[12288,1792]{1,0:T(8,128)(2,1)S(1)} %get-tuple-element.65.refs_0_, ...), custom_call_target="tpu_custom_call", output_to_operand_aliasing={{0}: (0, {})} | custom-call | flops 469762048 | tf_op jit(solution)/shard_map/activation/pallas_call | solution.py:102
  45.1 1.6 %collective-permute-start.9 = (f32[32,64]{1,0:T(8,128)S(1)}, f32[32,64]{1,0:T(8,128)S(1)}, u32[]{:S(2)}, u32[]{:S(2)}) collective-permute-start(f32[32,64]{1,0:T(8,128)S(1)} %get-tuple-element.68.left_ref.refs_4_), channel_id=1, source_target_pairs={{0,2},{1,3},{2,0},{3,1},{4,6},{5,7},{6,4},{7,5},{8,10},{9,11},{10,... | collective-permute-start | bytes 24584 | tf_op jit(solution)/shard_map/ppermute | solution.py:497
  46.6 4.4 %backward.5 = (bf16[12288,1792]{1,0:T(8,128)(2,1)S(1)}, f32[16,2048]{1,0:T(8,128)S(1)}, bf16[16,2048]{1,0:T(8,128)(2,1)S(1)}) custom-call(bf16[12288,1792]{1,0:T(8,128)(2,1)S(1)} %get-tuple-element.69.refs_0_, bf16[32,1792]{1,0:T(8,128)(2,1)S(1)} %get-tuple-element.70.refs_1_.right_ref, ...), custom_call_target="tpu_custom_call", output_to_operand_aliasing={{0}: (0, {})} | custom-call | flops 469762048 | bytes 7340032 | tf_op jit(solution)/shard_map/backward/pallas_call | solution.py:102
  51.1 0.0 collective-permute-done.9.right_ref
  51.1 0.3 collective-permute-start.10
  51.4 4.5 %backward.6 = (bf16[12288,1792]{1,0:T(8,128)(2,1)S(1)}, f32[16,2048]{1,0:T(8,128)S(1)}, bf16[16,4096]{1,0:T(8,128)(2,1)S(1)}) custom-call(bf16[12288,1792]{1,0:T(8,128)(2,1)S(1)} %get-tuple-element.72.refs_0_, bf16[32,1792]{1,0:T(8,128)(2,1)S(1)} %get-tuple-element.70.refs_1_.right_ref, ...), custom_call_target="tpu_custom_call", output_to_operand_aliasing={{0}: (0, {})} | custom-call | flops 469762048 | bytes 7340032 | tf_op jit(solution)/shard_map/backward/pallas_call | solution.py:102
  55.8 0.1 collective-permute-start.13
  55.9 0.0 collective-permute-done.10.right_ref
  55.9 1.5 %collective-permute-start.11 = (f32[32,64]{1,0:T(8,128)S(1)}, f32[32,64]{1,0:T(8,128)S(1)}, u32[]{:S(2)}, u32[]{:S(2)}) collective-permute-start(f32[32,64]{1,0:T(8,128)S(1)} %plus.13.left_ref.refs_4_), channel_id=1, source_target_pairs={{0,8},{1,9},{2,10},{3,11},{4,12},{5,13},{6,14},{7,15},{8,0},{9,1},... | collective-permute-start | bytes 24584 | tf_op jit(solution)/shard_map/ppermute | solution.py:497
  57.5 4.4 %backward.7 = (bf16[12288,1792]{1,0:T(8,128)(2,1)S(1)}, f32[16,2048]{1,0:T(8,128)S(1)}, bf16[16,2048]{1,0:T(8,128)(2,1)S(1)}) custom-call(bf16[12288,1792]{1,0:T(8,128)(2,1)S(1)} %get-tuple-element.74.refs_0_, bf16[32,1792]{1,0:T(8,128)(2,1)S(1)} %get-tuple-element.70.refs_1_.right_ref, ...), custom_call_target="tpu_custom_call", output_to_operand_aliasing={{0}: (0, {})} | custom-call | flops 469762048 | bytes 7340032 | tf_op jit(solution)/shard_map/backward/pallas_call | solution.py:102
  61.9 0.0 collective-permute-done.11.right_ref
  61.9 0.3 collective-permute-start.12
  62.2 2.2 %backward.8 = (bf16[12288,1792]{1,0:T(8,128)(2,1)S(1)}, f32[16,1024]{1,0:T(8,128)S(1)}, bf16[16,3072]{1,0:T(8,128)(2,1)S(1)}) custom-call(bf16[12288,1792]{1,0:T(8,128)(2,1)S(1)} %get-tuple-element.75.refs_0_, bf16[32,1792]{1,0:T(8,128)(2,1)S(1)} %get-tuple-element.70.refs_1_.right_ref, ...), custom_call_target="tpu_custom_call", output_to_operand_aliasing={{0}: (0, {})} | custom-call | flops 234881024 | tf_op jit(solution)/shard_map/backward/pallas_call | solution.py:102
  64.4 0.0 collective-permute-done.12.right_ref
  64.4 0.9 %adapter_part.1 = (bf16[16,512]{1,0:T(8,128)(2,1)S(1)}, bf16[16,3584]{1,0:T(8,128)(2,1)S(1)}, bf16[32,2048]{1,0:T(8,128)(2,1)S(1)}) custom-call(f32[32,64]{1,0:T(8,128)S(1)} %plus.15.refs_0_, s32[1,32]{1,0:T(1,128)S(1)} %bitcast.3, bf16[512,2048]{1,0:T(8,128)(2,1)S(1)} %copy-done, bf16[16,3072]{1,0:T(8,128)(2,1)S(1)} %get-tuple-element.77.refs_3_), custom_call_target="tpu_custom_call" | custom-call | flops 67108864 | bytes 2097152 | tf_op jit(solution)/shard_map/adapter_part/pallas_call | solution.py:301
  65.3 0.4 collective-permute-start.14
  65.7 2.2 %backward.9 = (bf16[12288,1792]{1,0:T(8,128)(2,1)S(1)}, f32[16,1024]{1,0:T(8,128)S(1)}, bf16[16,1024]{1,0:T(8,128)(2,1)S(1)}) custom-call(bf16[12288,1792]{1,0:T(8,128)(2,1)S(1)} %get-tuple-element.83.refs_0_, bf16[32,1792]{1,0:T(8,128)(2,1)S(1)} %get-tuple-element.70.refs_1_.right_ref, ...), custom_call_target="tpu_custom_call", output_to_operand_aliasing={{0}: (0, {})} | custom-call | flops 234881024 | tf_op jit(solution)/shard_map/backward/pallas_call | solution.py:102
  67.9 0.2 collective-permute-start.15
  68.1 1.0 %collective-permute-done.15.refs_8_ = bf16[16,1024]{1,0:T(8,128)(2,1)S(1)} collective-permute-done((bf16[16,1024]{1,0:T(8,128)(2,1)S(1)}, bf16[16,1024]{1,0:T(8,128)(2,1)S(1)}, u32[]{:S(2)}, u32[]{:S(2)}) %collective-permute-start.15) | collective-permute-done | bytes 32800 | tf_op jit(solution)/shard_map/ppermute | solution.py:497
  69.1 0.0 collective-permute-done.13.refs_6_
  69.1 0.0 collective-permute-done.14.refs_7_
  69.1 0.1 first_halves.1
  69.2 0.6 collective-permute-start.16
  69.8 4.5 %up_maps.1 = (bf16[2048,1792]{1,0:T(8,128)(2,1)}, f32[8,128]{1,0:T(8,128)S(1)}) custom-call(bf16[32,2048]{1,0:T(8,128)(2,1)S(1)} %get-tuple-element.90.left_ref, bf16[32,1792]{1,0:T(8,128)(2,1)S(1)} %get-tuple-element.70.refs_1_.right_ref, bf16[8,8192]{1,0:T(8,128)(2,1)S(1)} %get-tuple-element.89.refs_0_), custom_call_target="tpu_custom_call" | custom-call | flops 234881024 | bytes 7340032 | tf_op jit(solution)/shard_map/up_maps/pallas_call | solution.py:459
  74.3 0.6 collective-permute-done.16.came_ref
  74.9 0.1 quarters.1
  75.0 3.0 %collective-permute-start.17 = (bf16[2,8192]{1,0:T(2,128)(2,1)S(1)}, bf16[2,8192]{1,0:T(2,128)(2,1)S(1)}, u32[]{:S(2)}, u32[]{:S(2)}) collective-permute-start(bf16[2,8192]{1,0:T(2,128)(2,1)S(1)} %get-tuple-element.93), channel_id=1, source_target_pairs={{0,12},{1,13},{2,14},{3,15},{4,8},{5,9},{6,10},{7,11},{8,4},{9,5},... | collective-permute-start | bytes 98312 | tf_op jit(solution)/shard_map/ppermute | solution.py:497
  77.9 0.5 collective-permute-start.18
  78.5 0.9 %collective-permute-start.19 = (bf16[2,8192]{1,0:T(2,128)(2,1)S(1)}, bf16[2,8192]{1,0:T(2,128)(2,1)S(1)}, u32[]{:S(2)}, u32[]{:S(2)}) collective-permute-start(bf16[2,8192]{1,0:T(2,128)(2,1)S(1)} %get-tuple-element.95.refs_0_), channel_id=1, source_target_pairs={{0,4},{1,5},{2,6},{3,7},{4,0},{5,1},{6,2},{7,3},{8,12},{9,13},{10,... | collective-permute-start | bytes 98312 | tf_op jit(solution)/shard_map/ppermute | solution.py:497
  79.4 1.9 %down_maps.1 = (bf16[512,2048]{1,0:T(8,128)(2,1)}, f32[8,128]{1,0:T(8,128)S(1)}) custom-call(bf16[32,512]{1,0:T(8,128)(2,1)S(1)} %get-tuple-element.96.left_ref, bf16[32,2048]{1,0:T(8,128)(2,1)S(1)} %get-tuple-element.97.right_ref, bf16[2,8192]{1,0:T(2,128)(2,1)S(1)} %get-tuple-element.95.refs_0_), custom_call_target="tpu_custom_call" | custom-call | flops 67108864 | bytes 2097152 | tf_op jit(solution)/shard_map/down_maps/pallas_call | solution.py:459
  81.3 0.0 collective-permute-done.17.refs_0_
  81.3 1.4 %collective-permute-done.18.refs_1_ = bf16[2,8192]{1,0:T(2,128)(2,1)S(1)} collective-permute-done((bf16[2,8192]{1,0:T(2,128)(2,1)S(1)}, bf16[2,8192]{1,0:T(2,128)(2,1)S(1)}, u32[]{:S(2)}, u32[]{:S(2)}) %collective-permute-start.18) | collective-permute-done | bytes 32800 | tf_op jit(solution)/shard_map/ppermute | solution.py:497
  82.8 0.0 collective-permute-done.19.refs_2_
  82.8 0.7 final.1
  (13 shorter events, 0.1 us)
Async XLA Ops:
  0.6 11.6 %copy-start.2 = (bf16[2,8192]{1,0:T(2,128)(2,1)S(1)}, bf16[2,8192]{1,0:T(2,128)(2,1)}, u32[]{:S(2)}) copy-start(bf16[2,8192]{1,0:T(2,128)(2,1)} %refs_0_.4) | copy-start | bytes 98308
  0.6 11.0 %collective-permute-start = (bf16[2,8192]{1,0:T(2,128)(2,1)}, bf16[2,8192]{1,0:T(2,128)(2,1)S(1)}, u32[]{:S(2)}, u32[]{:S(2)}) collective-permute-start(bf16[2,8192]{1,0:T(2,128)(2,1)} %refs_0_.4), channel_id=1, source_target_pairs={{0,4},{1,5},{2,6},{3,7},{4,0},{5,1},{6,2},{7,3},{8,12},{9,13},{10,... | collective-permute-start | bytes 98312 | tf_op jit(solution)/shard_map/ppermute | solution.py:497
  3.7 7.9 %collective-permute-start.1 = (bf16[2,8192]{1,0:T(2,128)(2,1)}, bf16[2,8192]{1,0:T(2,128)(2,1)S(1)}, u32[]{:S(2)}, u32[]{:S(2)}) collective-permute-start(bf16[2,8192]{1,0:T(2,128)(2,1)} %refs_0_.4), channel_id=1, source_target_pairs={{0,8},{1,9},{2,10},{3,11},{4,12},{5,13},{6,14},{7,15},{8,0},{9,1},... | collective-permute-start | bytes 98312 | tf_op jit(solution)/shard_map/ppermute | solution.py:497
  6.3 5.9 %collective-permute-start.2 = (bf16[2,8192]{1,0:T(2,128)(2,1)}, bf16[2,8192]{1,0:T(2,128)(2,1)S(1)}, u32[]{:S(2)}, u32[]{:S(2)}) collective-permute-start(bf16[2,8192]{1,0:T(2,128)(2,1)} %refs_0_.4), channel_id=1, source_target_pairs={{0,12},{1,13},{2,14},{3,15},{4,8},{5,9},{6,10},{7,11},{8,4},{9,5},... | collective-permute-start | bytes 98312 | tf_op jit(solution)/shard_map/ppermute | solution.py:497
  12.3 5.9 %collective-permute-start.3 = (bf16[8,8192]{1,0:T(8,128)(2,1)S(1)}, bf16[8,8192]{1,0:T(8,128)(2,1)S(1)}, u32[]{:S(2)}, u32[]{:S(2)}) collective-permute-start(bf16[8,8192]{1,0:T(8,128)(2,1)S(1)} %stacked.2.refs_3_.refs_0_), channel_id=1, source_target_pairs={{0,2},{1,3},{2,0},{3,1},{4,6},{5,7},{6,4},{7,5},{8,10},{9,11},{10,... | collective-permute-start | bytes 393224 | tf_op jit(solution)/shard_map/ppermute | solution.py:497
  18.2 2.7 %copy-start = (bf16[512,2048]{1,0:T(8,128)(2,1)S(1)}, bf16[512,2048]{1,0:T(8,128)(2,1)}, u32[]{:S(2)}) copy-start(bf16[512,2048]{1,0:T(8,128)(2,1)} %refs_2_.3) | copy-start | bytes 6291460
  18.2 2.7 %copy-start.3 = (s32[32]{0:T(128)S(1)}, s32[32]{0:T(128)}, u32[]{:S(2)}) copy-start(s32[32]{0:T(128)} %param.13) | copy-start | bytes 388
  18.3 2.3 %collective-permute-start.4 = (bf16[16,8192]{1,0:T(8,128)(2,1)S(1)}, bf16[16,8192]{1,0:T(8,128)(2,1)S(1)}, u32[]{:S(2)}, u32[]{:S(2)}) collective-permute-start(bf16[16,8192]{1,0:T(8,128)(2,1)S(1)} %stacked.3.refs_2_.refs_1_), channel_id=1, source_target_pairs={{0,1},{1,0},{2,3},{3,2},{4,5},{5,4},{6,7},{7,6},{8,9},{9,8},{10,11... | collective-permute-start | bytes 786440 | tf_op jit(solution)/shard_map/ppermute | solution.py:497
  21.6 1.2 %collective-permute-start.5 = (f32[32,64]{1,0:T(8,128)S(1)}, f32[32,64]{1,0:T(8,128)S(1)}, u32[]{:S(2)}, u32[]{:S(2)}) collective-permute-start(f32[32,64]{1,0:T(8,128)S(1)} %get-tuple-element.58.refs_5_.left_ref), channel_id=1, source_target_pairs={{0,1},{1,0},{2,3},{3,2},{4,5},{5,4},{6,7},{7,6},{8,9},{9,8},{10,11... | collective-permute-start | bytes 24584 | tf_op jit(solution)/shard_map/ppermute | solution.py:497
  22.8 5.8 %collective-permute-start.6 = (f32[32,64]{1,0:T(8,128)S(1)}, f32[32,64]{1,0:T(8,128)S(1)}, u32[]{:S(2)}, u32[]{:S(2)}) collective-permute-start(f32[32,64]{1,0:T(8,128)S(1)} %plus.8.refs_7_.left_ref), channel_id=1, source_target_pairs={{0,2},{1,3},{2,0},{3,1},{4,6},{5,7},{6,4},{7,5},{8,10},{9,11},{10,... | collective-permute-start | bytes 24584 | tf_op jit(solution)/shard_map/ppermute | solution.py:497
  28.7 5.9 %collective-permute-start.7 = (f32[32,64]{1,0:T(8,128)S(1)}, f32[32,64]{1,0:T(8,128)S(1)}, u32[]{:S(2)}, u32[]{:S(2)}) collective-permute-start(f32[32,64]{1,0:T(8,128)S(1)} %plus.9.refs_6_.left_ref), channel_id=1, source_target_pairs={{0,4},{1,5},{2,6},{3,7},{4,0},{5,1},{6,2},{7,3},{8,12},{9,13},{10,... | collective-permute-start | bytes 24584 | tf_op jit(solution)/shard_map/ppermute | solution.py:497
  34.5 6.8 %copy-start.1 = (bf16[32,1792]{1,0:T(8,128)(2,1)S(1)}, bf16[32,1792]{1,0:T(8,128)(2,1)}, u32[]{:S(2)}) copy-start(bf16[32,1792]{1,0:T(8,128)(2,1)} %refs_3_.5) | copy-start | bytes 344068
  34.5 6.7 %collective-permute-start.8 = (f32[32,64]{1,0:T(8,128)S(1)}, f32[32,64]{1,0:T(8,128)S(1)}, u32[]{:S(2)}, u32[]{:S(2)}) collective-permute-start(f32[32,64]{1,0:T(8,128)S(1)} %plus.10.left_ref), channel_id=1, source_target_pairs={{0,8},{1,9},{2,10},{3,11},{4,12},{5,13},{6,14},{7,15},{8,0},{9,1},... | collective-permute-start | bytes 24584 | tf_op jit(solution)/shard_map/ppermute | solution.py:497
  45.1 6.0 %collective-permute-start.9 = (f32[32,64]{1,0:T(8,128)S(1)}, f32[32,64]{1,0:T(8,128)S(1)}, u32[]{:S(2)}, u32[]{:S(2)}) collective-permute-start(f32[32,64]{1,0:T(8,128)S(1)} %get-tuple-element.68.left_ref.refs_4_), channel_id=1, source_target_pairs={{0,2},{1,3},{2,0},{3,1},{4,6},{5,7},{6,4},{7,5},{8,10},{9,11},{10,... | collective-permute-start | bytes 24584 | tf_op jit(solution)/shard_map/ppermute | solution.py:497
  51.1 4.8 %collective-permute-start.10 = (f32[32,64]{1,0:T(8,128)S(1)}, f32[32,64]{1,0:T(8,128)S(1)}, u32[]{:S(2)}, u32[]{:S(2)}) collective-permute-start(f32[32,64]{1,0:T(8,128)S(1)} %plus.12.left_ref.refs_5_), channel_id=1, source_target_pairs={{0,4},{1,5},{2,6},{3,7},{4,0},{5,1},{6,2},{7,3},{8,12},{9,13},{10,... | collective-permute-start | bytes 24584 | tf_op jit(solution)/shard_map/ppermute | solution.py:497
  55.8 13.3 %collective-permute-start.13 = (bf16[16,4096]{1,0:T(8,128)(2,1)S(1)}, bf16[16,4096]{1,0:T(8,128)(2,1)S(1)}, u32[]{:S(2)}, u32[]{:S(2)}) collective-permute-start(bf16[16,4096]{1,0:T(8,128)(2,1)S(1)} %get-tuple-element.86), channel_id=1, source_target_pairs={{0,1},{1,0},{2,3},{3,2},{4,5},{5,4},{6,7},{7,6},{8,9},{9,8},{10,11... | collective-permute-start | bytes 393224 | tf_op jit(solution)/shard_map/ppermute | solution.py:497
  55.9 6.0 %collective-permute-start.11 = (f32[32,64]{1,0:T(8,128)S(1)}, f32[32,64]{1,0:T(8,128)S(1)}, u32[]{:S(2)}, u32[]{:S(2)}) collective-permute-start(f32[32,64]{1,0:T(8,128)S(1)} %plus.13.left_ref.refs_4_), channel_id=1, source_target_pairs={{0,8},{1,9},{2,10},{3,11},{4,12},{5,13},{6,14},{7,15},{8,0},{9,1},... | collective-permute-start | bytes 24584 | tf_op jit(solution)/shard_map/ppermute | solution.py:497
  61.9 2.5 %collective-permute-start.12 = (f32[32,64]{1,0:T(8,128)S(1)}, f32[32,64]{1,0:T(8,128)S(1)}, u32[]{:S(2)}, u32[]{:S(2)}) collective-permute-start(f32[32,64]{1,0:T(8,128)S(1)} %plus.14.left_ref.refs_4_), channel_id=1, source_target_pairs={{0,1},{1,0},{2,3},{3,2},{4,5},{5,4},{6,7},{7,6},{8,9},{9,8},{10,11... | collective-permute-start | bytes 24584 | tf_op jit(solution)/shard_map/ppermute | solution.py:497
  65.3 3.8 %collective-permute-start.14 = (bf16[16,3584]{1,0:T(8,128)(2,1)S(1)}, bf16[16,3584]{1,0:T(8,128)(2,1)S(1)}, u32[]{:S(2)}, u32[]{:S(2)}) collective-permute-start(bf16[16,3584]{1,0:T(8,128)(2,1)S(1)} %get-tuple-element.84.refs_3_), channel_id=1, source_target_pairs={{0,1},{1,0},{2,3},{3,2},{4,5},{5,4},{6,7},{7,6},{8,9},{9,8},{10,11... | collective-permute-start | bytes 344072 | tf_op jit(solution)/shard_map/ppermute | solution.py:497
  67.9 1.2 %collective-permute-start.15 = (bf16[16,1024]{1,0:T(8,128)(2,1)S(1)}, bf16[16,1024]{1,0:T(8,128)(2,1)S(1)}, u32[]{:S(2)}, u32[]{:S(2)}) collective-permute-start(bf16[16,1024]{1,0:T(8,128)(2,1)S(1)} %get-tuple-element.87), channel_id=1, source_target_pairs={{0,1},{1,0},{2,3},{3,2},{4,5},{5,4},{6,7},{7,6},{8,9},{9,8},{10,11... | collective-permute-start | bytes 98312 | tf_op jit(solution)/shard_map/ppermute | solution.py:497
  69.2 5.7 %collective-permute-start.16 = (bf16[8,8192]{1,0:T(8,128)(2,1)S(1)}, bf16[8,8192]{1,0:T(8,128)(2,1)S(1)}, u32[]{:S(2)}, u32[]{:S(2)}) collective-permute-start(bf16[8,8192]{1,0:T(8,128)(2,1)S(1)} %get-tuple-element.89.refs_0_), channel_id=1, source_target_pairs={{0,2},{1,3},{2,0},{3,1},{4,6},{5,7},{6,4},{7,5},{8,10},{9,11},{10,... | collective-permute-start | bytes 393224 | tf_op jit(solution)/shard_map/ppermute | solution.py:497
  75.0 6.4 %collective-permute-start.17 = (bf16[2,8192]{1,0:T(2,128)(2,1)S(1)}, bf16[2,8192]{1,0:T(2,128)(2,1)S(1)}, u32[]{:S(2)}, u32[]{:S(2)}) collective-permute-start(bf16[2,8192]{1,0:T(2,128)(2,1)S(1)} %get-tuple-element.93), channel_id=1, source_target_pairs={{0,12},{1,13},{2,14},{3,15},{4,8},{5,9},{6,10},{7,11},{8,4},{9,5},... | collective-permute-start | bytes 98312 | tf_op jit(solution)/shard_map/ppermute | solution.py:497
  77.9 4.8 %collective-permute-start.18 = (bf16[2,8192]{1,0:T(2,128)(2,1)S(1)}, bf16[2,8192]{1,0:T(2,128)(2,1)S(1)}, u32[]{:S(2)}, u32[]{:S(2)}) collective-permute-start(bf16[2,8192]{1,0:T(2,128)(2,1)S(1)} %get-tuple-element.94), channel_id=1, source_target_pairs={{0,8},{1,9},{2,10},{3,11},{4,12},{5,13},{6,14},{7,15},{8,0},{9,1},... | collective-permute-start | bytes 98312 | tf_op jit(solution)/shard_map/ppermute | solution.py:497
  78.5 4.3 %collective-permute-start.19 = (bf16[2,8192]{1,0:T(2,128)(2,1)S(1)}, bf16[2,8192]{1,0:T(2,128)(2,1)S(1)}, u32[]{:S(2)}, u32[]{:S(2)}) collective-permute-start(bf16[2,8192]{1,0:T(2,128)(2,1)S(1)} %get-tuple-element.95.refs_0_), channel_id=1, source_target_pairs={{0,4},{1,5},{2,6},{3,7},{4,0},{5,1},{6,2},{7,3},{8,12},{9,13},{10,... | collective-permute-start | bytes 98312 | tf_op jit(solution)/shard_map/ppermute | solution.py:497

commit v17 on v16

--- a/solution.py
+++ b/solution.py
@@ -54,7 +54,7 @@
 VMEM = pl.BlockSpec(memory_space=pltpu.VMEM)
 ANY = pl.BlockSpec(memory_space=pl.ANY)
 CUTS = 4
-COPIES = 8
+COPIES = 16
 STRIP = 256
 SLOTS = 6
 STORE_GRANT = 10 << 20
@@ -528,21 +528,9 @@
     block = stacked([normed_layer_input, *came], [token])
     for hop in reversed(hops[2:-2]):
         block = stacked([block, swapped(block, hop)])
-    other = swapped(block, hops[1])
+    x = [block] + [swapped(block, hop) for hop in (hops[1], 1, hops[1] | 1)]
     store, token = store_call(
-        mark,
-        store,
-        [(gate_weight, 1, 2), (up_weight, 1, 3, 0)],
-        [],
-        [mark_shape],
-        0,
-        "fetch",
-        after=[block],
-    )
-    block = stacked([block, other], [token])
-    x = [block, swapped(block, 1)]
-    store, token = store_call(
-        mark, store, [(up_weight, 1, 3, 1)], [], [mark_shape], 0, "fetch", after=[block]
+        mark, store, pair(1, 2, 3), [], [mark_shape], 0, "fetch", after=[block]
     )
 
     input_span, low = low_part(adapter_down_maps, tenants, x, count, token)

time: 83.6 us -> 84.1 us (level)
  starting transfers between devices: 21.2 us -> 22.6 us
    ppermute x20 -> x21, starting transfers between devices: 21.2 us -> 22.6 us  [swapped(): lax.ppermute(block, 'tp', [(i, i ^ hop) for i in range(lax.axis_size('tp'...]
    ppermute x20 -> x21, waiting for transfers between devices: 4.8 us -> 4.19 us  [swapped(): lax.ppermute(block, 'tp', [(i, i ^ hop) for i in range(lax.axis_size('tp'...]
    pallas_call x12 -> x11, Pallas kernels: 47.3 us -> 47.2 us  [store_call(): pl.pallas_call(body, in_specs=[VMEM] * (n_in + (not new)) + [ANY] * (n_hb...]
  transfers between devices with their start and end apart: 20 -> 21, of which waited for: 5 -> 4; matrix products, arithmetic and copies ran while one was open for 0% -> 0% of each run, Pallas kernels for 61% -> 60%
where the time goes in v17:
time: 84.1 us; the launch traced here: 84 us
  Pallas kernels  56.1 us (67%)
  starting transfers between devices  22.6 us (27%)
  waiting for transfers between devices  4.19 us (5%)
  between operations  0.93 us (1%)
    pallas_call x11, Pallas kernels, store_call(): pl.pallas_call(body, in_specs=[VMEM] * (n_in + (not new)) + [ANY] * (n_hb...  47.2 us
    ppermute x21, starting transfers between devices, swapped(): lax.ppermute(block, 'tp', [(i, i ^ hop) for i in range(lax.axis_size('tp'...  22.6 us
    pallas_call x2, Pallas kernels, outer(): pl.pallas_call(outer_kernel, grid=(height // block,), in_specs=[pl.BlockS...  6.38 us
    ppermute x21, waiting for transfers between devices, swapped(): lax.ppermute(block, 'tp', [(i, i ^ hop) for i in range(lax.axis_size('tp'...  4.19 us
  transfers between devices with their start and end apart: 21, of which 4 were waited for; matrix products, arithmetic and copies ran while one was open for 0% of the time, Pallas kernels for 60%

profile of v17, /device:TPU:0, one launch (start us, length us, event | category | flops | bytes accessed | tf_op | source)
XLA Modules:
  0.0 84.0 jit_solution(9800741596404396672)
XLA Ops:
  0.6 0.0 copy-start.3
  0.6 3.1 %collective-permute-start = (bf16[2,8192]{1,0:T(2,128)(2,1)}, bf16[2,8192]{1,0:T(2,128)(2,1)S(1)}, u32[]{:S(2)}, u32[]{:S(2)}) collective-permute-start(bf16[2,8192]{1,0:T(2,128)(2,1)} %refs_0_.4), channel_id=1, source_target_pairs={{0,4},{1,5},{2,6},{3,7},{4,0},{5,1},{6,2},{7,3},{8,12},{9,13},{10,... | collective-permute-start | bytes 98312 | tf_op jit(solution)/shard_map/ppermute | solution.py:497
  3.7 2.6 %collective-permute-start.1 = (bf16[2,8192]{1,0:T(2,128)(2,1)}, bf16[2,8192]{1,0:T(2,128)(2,1)S(1)}, u32[]{:S(2)}, u32[]{:S(2)}) collective-permute-start(bf16[2,8192]{1,0:T(2,128)(2,1)} %refs_0_.4), channel_id=1, source_target_pairs={{0,8},{1,9},{2,10},{3,11},{4,12},{5,13},{6,14},{7,15},{8,0},{9,1},... | collective-permute-start | bytes 98312 | tf_op jit(solution)/shard_map/ppermute | solution.py:497
  6.3 0.0 collective-permute-start.2
  6.3 5.4 %fetch.2 = (bf16[12288,1792]{1,0:T(8,128)(2,1)S(1)}, f32[8,128]{1,0:T(8,128)S(1)}) custom-call(bf16[8192,1792]{1,0:T(8,128)(2,1)} %refs_4_.1, bf16[8192,1792]{1,0:T(8,128)(2,1)} %refs_3_.5), custom_call_target="tpu_custom_call" | custom-call | bytes 14680064 | tf_op jit(solution)/shard_map/fetch/pallas_call | solution.py:102
  11.8 0.0 collective-permute-done.refs_1_
  11.8 0.0 collective-permute-done.1.refs_2_
  11.8 0.5 collective-permute-done.2.refs_3_
  12.2 0.1 stacked.1.refs_3_.refs_2_.refs_1_
  12.3 1.6 %collective-permute-start.3 = (bf16[8,8192]{1,0:T(8,128)(2,1)S(1)}, bf16[8,8192]{1,0:T(8,128)(2,1)S(1)}, u32[]{:S(2)}, u32[]{:S(2)}) collective-permute-start(bf16[8,8192]{1,0:T(8,128)(2,1)S(1)} %stacked.1.refs_3_.refs_2_.refs_1_), channel_id=1, source_target_pairs={{0,2},{1,3},{2,0},{3,1},{4,6},{5,7},{6,4},{7,5},{8,10},{9,11},{10,... | collective-permute-start | bytes 393224 | tf_op jit(solution)/shard_map/ppermute | solution.py:497
  13.9 0.0 collective-permute-start.4
  13.9 0.6 collective-permute-start.5
  14.5 5.6 %fetch.3 = (bf16[12288,1792]{1,0:T(8,128)(2,1)S(1)}, f32[8,128]{1,0:T(8,128)S(1)}) custom-call(bf16[12288,1792]{1,0:T(8,128)(2,1)S(1)} %get-tuple-element.50.refs_0_, bf16[8192,1792]{1,0:T(8,128)(2,1)} %refs_4_.1, bf16[8192,1792]{1,0:T(8,128)(2,1)} %refs_3_.5, bf16[8,8192]{1,0:T(8,128)(2,1)S(1)} %stacked.1.refs_3_.refs_2_.refs_1_), custom_call_target="tpu_custom_call", output_to_operand_aliasing={{0}: (0, {})} | custom-call | bytes 14680064 | tf_op jit(solution)/shard_map/fetch/pallas_call | solution.py:102
  20.1 0.0 collective-permute-done.3.refs_3_.refs_2_
  20.1 0.0 collective-permute-done.4.refs_4_.refs_3_
  20.2 0.0 collective-permute-done.5.refs_5_.refs_4_
  20.2 0.2 copy-done
  20.4 0.7 low_part.1
  21.1 0.0 collective-permute-start.6
  21.1 1.2 %collective-permute-done.6.right_ref = f32[32,64]{1,0:T(8,128)S(1)} collective-permute-done((f32[32,64]{1,0:T(8,128)S(1)}, f32[32,64]{1,0:T(8,128)S(1)}, u32[]{:S(2)}, u32[]{:S(2)}) %collective-permute-start.6) | collective-permute-done | bytes 8224 | tf_op jit(solution)/shard_map/ppermute | solution.py:497
  22.3 1.5 %collective-permute-start.7 = (f32[32,64]{1,0:T(8,128)S(1)}, f32[32,64]{1,0:T(8,128)S(1)}, u32[]{:S(2)}, u32[]{:S(2)}) collective-permute-start(f32[32,64]{1,0:T(8,128)S(1)} %plus.8.refs_9_.left_ref), channel_id=1, source_target_pairs={{0,2},{1,3},{2,0},{3,1},{4,6},{5,7},{6,4},{7,5},{8,10},{9,11},{10,... | collective-permute-start | bytes 24584 | tf_op jit(solution)/shard_map/ppermute | solution.py:497
  23.8 5.5 %forward.3 = (bf16[12288,1792]{1,0:T(8,128)(2,1)S(1)}, f32[32,1792]{1,0:T(8,128)S(1)}, f32[32,1792]{1,0:T(8,128)S(1)}) custom-call(bf16[12288,1792]{1,0:T(8,128)(2,1)S(1)} %get-tuple-element.52.refs_0_, bf16[8,8192]{1,0:T(8,128)(2,1)S(1)} %stacked.1.refs_3_.refs_2_.refs_1_, ...), custom_call_target="tpu_custom_call", output_to_operand_aliasing={{0}: (0, {})} | custom-call | flops 939524096 | bytes 14680064 | tf_op jit(solution)/shard_map/forward/pallas_call | solution.py:102
  29.3 0.0 collective-permute-done.7.right_ref
  29.3 0.5 collective-permute-start.8
  29.8 5.6 %forward.4 = (bf16[12288,1792]{1,0:T(8,128)(2,1)S(1)}, f32[32,1792]{1,0:T(8,128)S(1)}, f32[32,1792]{1,0:T(8,128)S(1)}) custom-call(bf16[12288,1792]{1,0:T(8,128)(2,1)S(1)} %get-tuple-element.55.refs_0_, bf16[8,8192]{1,0:T(8,128)(2,1)S(1)} %stacked.1.refs_3_.refs_2_.refs_1_, ...), custom_call_target="tpu_custom_call", output_to_operand_aliasing={{0}: (0, {})} | custom-call | flops 469762048 | bytes 14680064 | tf_op jit(solution)/shard_map/forward/pallas_call | solution.py:102
  35.4 0.0 copy-start.2
  35.4 0.0 collective-permute-done.8.right_ref
  35.4 3.6 %collective-permute-start.9 = (f32[32,64]{1,0:T(8,128)S(1)}, f32[32,64]{1,0:T(8,128)S(1)}, u32[]{:S(2)}, u32[]{:S(2)}) collective-permute-start(f32[32,64]{1,0:T(8,128)S(1)} %plus.10.left_ref), channel_id=1, source_target_pairs={{0,8},{1,9},{2,10},{3,11},{4,12},{5,13},{6,14},{7,15},{8,0},{9,1},... | collective-permute-start | bytes 24584 | tf_op jit(solution)/shard_map/ppermute | solution.py:497
  39.0 3.2 %forward.5 = (bf16[12288,1792]{1,0:T(8,128)(2,1)S(1)}, f32[32,1792]{1,0:T(8,128)S(1)}, f32[32,1792]{1,0:T(8,128)S(1)}) custom-call(bf16[12288,1792]{1,0:T(8,128)(2,1)S(1)} %get-tuple-element.58.refs_0_, bf16[8,8192]{1,0:T(8,128)(2,1)S(1)} %stacked.1.refs_3_.refs_2_.refs_1_, ...), custom_call_target="tpu_custom_call", output_to_operand_aliasing={{0}: (0, {})} | custom-call | flops 469762048 | bytes 7340032 | tf_op jit(solution)/shard_map/forward/pallas_call | solution.py:102
  42.2 0.0 collective-permute-done.9.right_ref
  42.2 3.8 %activation.1 = (bf16[12288,1792]{1,0:T(8,128)(2,1)S(1)}, bf16[32,1792]{1,0:T(8,128)(2,1)S(1)}, bf16[32,1792]{1,0:T(8,128)(2,1)S(1)}, f32[32,64]{1,0:T(8,128)S(1)}, bf16[32,2048]{1,0:T(8,128)(2,1)S(1)}) custom-call(bf16[12288,1792]{1,0:T(8,128)(2,1)S(1)} %get-tuple-element.61.refs_0_, ...), custom_call_target="tpu_custom_call", output_to_operand_aliasing={{0}: (0, {})} | custom-call | flops 469762048 | tf_op jit(solution)/shard_map/activation/pallas_call | solution.py:102
  46.0 0.5 collective-permute-start.10
  46.6 4.7 %backward.5 = (bf16[12288,1792]{1,0:T(8,128)(2,1)S(1)}, f32[16,2048]{1,0:T(8,128)S(1)}, bf16[16,2048]{1,0:T(8,128)(2,1)S(1)}) custom-call(bf16[12288,1792]{1,0:T(8,128)(2,1)S(1)} %get-tuple-element.65.refs_0_, bf16[32,1792]{1,0:T(8,128)(2,1)S(1)} %get-tuple-element.66.refs_1_.right_ref, ...), custom_call_target="tpu_custom_call", output_to_operand_aliasing={{0}: (0, {})} | custom-call | flops 469762048 | bytes 7340032 | tf_op jit(solution)/shard_map/backward/pallas_call | solution.py:102
  51.2 0.0 collective-permute-done.10.right_ref
  51.3 0.1 collective-permute-start.11
  51.4 4.5 %backward.6 = (bf16[12288,1792]{1,0:T(8,128)(2,1)S(1)}, f32[16,2048]{1,0:T(8,128)S(1)}, bf16[16,4096]{1,0:T(8,128)(2,1)S(1)}) custom-call(bf16[12288,1792]{1,0:T(8,128)(2,1)S(1)} %get-tuple-element.68.refs_0_, bf16[32,1792]{1,0:T(8,128)(2,1)S(1)} %get-tuple-element.66.refs_1_.right_ref, ...), custom_call_target="tpu_custom_call", output_to_operand_aliasing={{0}: (0, {})} | custom-call | flops 469762048 | bytes 7340032 | tf_op jit(solution)/shard_map/backward/pallas_call | solution.py:102
  55.9 0.1 collective-permute-start.14
  56.0 0.0 collective-permute-done.11.right_ref
  56.0 1.5 %collective-permute-start.12 = (f32[32,64]{1,0:T(8,128)S(1)}, f32[32,64]{1,0:T(8,128)S(1)}, u32[]{:S(2)}, u32[]{:S(2)}) collective-permute-start(f32[32,64]{1,0:T(8,128)S(1)} %plus.13.left_ref.refs_4_), channel_id=1, source_target_pairs={{0,8},{1,9},{2,10},{3,11},{4,12},{5,13},{6,14},{7,15},{8,0},{9,1},... | collective-permute-start | bytes 24584 | tf_op jit(solution)/shard_map/ppermute | solution.py:497
  57.5 4.5 %backward.7 = (bf16[12288,1792]{1,0:T(8,128)(2,1)S(1)}, f32[16,2048]{1,0:T(8,128)S(1)}, bf16[16,2048]{1,0:T(8,128)(2,1)S(1)}) custom-call(bf16[12288,1792]{1,0:T(8,128)(2,1)S(1)} %get-tuple-element.70.refs_0_, bf16[32,1792]{1,0:T(8,128)(2,1)S(1)} %get-tuple-element.66.refs_1_.right_ref, ...), custom_call_target="tpu_custom_call", output_to_operand_aliasing={{0}: (0, {})} | custom-call | flops 469762048 | bytes 7340032 | tf_op jit(solution)/shard_map/backward/pallas_call | solution.py:102
  62.0 0.0 collective-permute-done.12.right_ref
  62.0 0.3 collective-permute-start.13
  62.3 2.2 %backward.8 = (bf16[12288,1792]{1,0:T(8,128)(2,1)S(1)}, f32[16,1024]{1,0:T(8,128)S(1)}, bf16[16,3072]{1,0:T(8,128)(2,1)S(1)}) custom-call(bf16[12288,1792]{1,0:T(8,128)(2,1)S(1)} %get-tuple-element.71.refs_0_, bf16[32,1792]{1,0:T(8,128)(2,1)S(1)} %get-tuple-element.66.refs_1_.right_ref, ...), custom_call_target="tpu_custom_call", output_to_operand_aliasing={{0}: (0, {})} | custom-call | flops 234881024 | tf_op jit(solution)/shard_map/backward/pallas_call | solution.py:102
  64.5 0.0 collective-permute-done.13.right_ref
  64.6 0.9 %adapter_part.1 = (bf16[16,512]{1,0:T(8,128)(2,1)S(1)}, bf16[16,3584]{1,0:T(8,128)(2,1)S(1)}, bf16[32,2048]{1,0:T(8,128)(2,1)S(1)}) custom-call(f32[32,64]{1,0:T(8,128)S(1)} %plus.15.refs_0_, s32[1,32]{1,0:T(1,128)S(1)} %bitcast.3, bf16[512,2048]{1,0:T(8,128)(2,1)S(1)} %copy-done.1, bf16[16,3072]{1,0:T(8,128)(2,1)S(1)} %get-tuple-element.73.refs_3_), custom_call_target="tpu_custom_call" | custom-call | flops 67108864 | bytes 2097152 | tf_op jit(solution)/shard_map/adapter_part/pallas_call | solution.py:301
  65.4 0.4 collective-permute-start.15
  65.8 2.2 %backward.9 = (bf16[12288,1792]{1,0:T(8,128)(2,1)S(1)}, f32[16,1024]{1,0:T(8,128)S(1)}, bf16[16,1024]{1,0:T(8,128)(2,1)S(1)}) custom-call(bf16[12288,1792]{1,0:T(8,128)(2,1)S(1)} %get-tuple-element.79.refs_0_, bf16[32,1792]{1,0:T(8,128)(2,1)S(1)} %get-tuple-element.66.refs_1_.right_ref, ...), custom_call_target="tpu_custom_call", output_to_operand_aliasing={{0}: (0, {})} | custom-call | flops 234881024 | tf_op jit(solution)/shard_map/backward/pallas_call | solution.py:102
  68.0 0.2 collective-permute-start.16
  68.2 1.0 %collective-permute-done.16.refs_8_ = bf16[16,1024]{1,0:T(8,128)(2,1)S(1)} collective-permute-done((bf16[16,1024]{1,0:T(8,128)(2,1)S(1)}, bf16[16,1024]{1,0:T(8,128)(2,1)S(1)}, u32[]{:S(2)}, u32[]{:S(2)}) %collective-permute-start.16) | collective-permute-done | bytes 32800 | tf_op jit(solution)/shard_map/ppermute | solution.py:497
  69.3 0.0 collective-permute-done.14.refs_6_
  69.3 0.0 collective-permute-done.15.refs_7_
  69.3 0.1 first_halves.1
  69.3 1.6 %collective-permute-start.17 = (bf16[8,8192]{1,0:T(8,128)(2,1)S(1)}, bf16[8,8192]{1,0:T(8,128)(2,1)S(1)}, u32[]{:S(2)}, u32[]{:S(2)}) collective-permute-start(bf16[8,8192]{1,0:T(8,128)(2,1)S(1)} %get-tuple-element.85.refs_0_), channel_id=1, source_target_pairs={{0,2},{1,3},{2,0},{3,1},{4,6},{5,7},{6,4},{7,5},{8,10},{9,11},{10,... | collective-permute-start | bytes 393224 | tf_op jit(solution)/shard_map/ppermute | solution.py:497
  70.9 4.5 %up_maps.1 = (bf16[2048,1792]{1,0:T(8,128)(2,1)}, f32[8,128]{1,0:T(8,128)S(1)}) custom-call(bf16[32,2048]{1,0:T(8,128)(2,1)S(1)} %get-tuple-element.86.left_ref, bf16[32,1792]{1,0:T(8,128)(2,1)S(1)} %get-tuple-element.66.refs_1_.right_ref, bf16[8,8192]{1,0:T(8,128)(2,1)S(1)} %get-tuple-element.85.refs_0_), custom_call_target="tpu_custom_call" | custom-call | flops 234881024 | bytes 7340032 | tf_op jit(solution)/shard_map/up_maps/pallas_call | solution.py:459
  75.4 0.0 collective-permute-done.17.came_ref
  75.4 0.1 quarters.1
  75.5 3.0 %collective-permute-start.18 = (bf16[2,8192]{1,0:T(2,128)(2,1)S(1)}, bf16[2,8192]{1,0:T(2,128)(2,1)S(1)}, u32[]{:S(2)}, u32[]{:S(2)}) collective-permute-start(bf16[2,8192]{1,0:T(2,128)(2,1)S(1)} %get-tuple-element.89), channel_id=1, source_target_pairs={{0,12},{1,13},{2,14},{3,15},{4,8},{5,9},{6,10},{7,11},{8,4},{9,5},... | collective-permute-start | bytes 98312 | tf_op jit(solution)/shard_map/ppermute | solution.py:497
  78.5 0.5 collective-permute-start.19
  79.0 0.9 %collective-permute-start.20 = (bf16[2,8192]{1,0:T(2,128)(2,1)S(1)}, bf16[2,8192]{1,0:T(2,128)(2,1)S(1)}, u32[]{:S(2)}, u32[]{:S(2)}) collective-permute-start(bf16[2,8192]{1,0:T(2,128)(2,1)S(1)} %get-tuple-element.91.refs_0_), channel_id=1, source_target_pairs={{0,4},{1,5},{2,6},{3,7},{4,0},{5,1},{6,2},{7,3},{8,12},{9,13},{10,... | collective-permute-start | bytes 98312 | tf_op jit(solution)/shard_map/ppermute | solution.py:497
  79.9 1.9 %down_maps.1 = (bf16[512,2048]{1,0:T(8,128)(2,1)}, f32[8,128]{1,0:T(8,128)S(1)}) custom-call(bf16[32,512]{1,0:T(8,128)(2,1)S(1)} %get-tuple-element.92.left_ref, bf16[32,2048]{1,0:T(8,128)(2,1)S(1)} %get-tuple-element.93.right_ref, bf16[2,8192]{1,0:T(2,128)(2,1)S(1)} %get-tuple-element.91.refs_0_), custom_call_target="tpu_custom_call" | custom-call | flops 67108864 | bytes 2097152 | tf_op jit(solution)/shard_map/down_maps/pallas_call | solution.py:459
  81.8 0.0 collective-permute-done.18.refs_0_
  81.8 1.5 %collective-permute-done.19.refs_1_ = bf16[2,8192]{1,0:T(2,128)(2,1)S(1)} collective-permute-done((bf16[2,8192]{1,0:T(2,128)(2,1)S(1)}, bf16[2,8192]{1,0:T(2,128)(2,1)S(1)}, u32[]{:S(2)}, u32[]{:S(2)}) %collective-permute-start.19) | collective-permute-done | bytes 32800 | tf_op jit(solution)/shard_map/ppermute | solution.py:497
  83.3 0.0 collective-permute-done.20.refs_2_
  83.3 0.7 final.1
  (15 shorter events, 0.1 us)
Async XLA Ops:
  0.6 11.6 %copy-start.3 = (bf16[2,8192]{1,0:T(2,128)(2,1)S(1)}, bf16[2,8192]{1,0:T(2,128)(2,1)}, u32[]{:S(2)}) copy-start(bf16[2,8192]{1,0:T(2,128)(2,1)} %refs_0_.4) | copy-start | bytes 98308
  0.6 11.1 %collective-permute-start = (bf16[2,8192]{1,0:T(2,128)(2,1)}, bf16[2,8192]{1,0:T(2,128)(2,1)S(1)}, u32[]{:S(2)}, u32[]{:S(2)}) collective-permute-start(bf16[2,8192]{1,0:T(2,128)(2,1)} %refs_0_.4), channel_id=1, source_target_pairs={{0,4},{1,5},{2,6},{3,7},{4,0},{5,1},{6,2},{7,3},{8,12},{9,13},{10,... | collective-permute-start | bytes 98312 | tf_op jit(solution)/shard_map/ppermute | solution.py:497
  3.7 8.1 %collective-permute-start.1 = (bf16[2,8192]{1,0:T(2,128)(2,1)}, bf16[2,8192]{1,0:T(2,128)(2,1)S(1)}, u32[]{:S(2)}, u32[]{:S(2)}) collective-permute-start(bf16[2,8192]{1,0:T(2,128)(2,1)} %refs_0_.4), channel_id=1, source_target_pairs={{0,8},{1,9},{2,10},{3,11},{4,12},{5,13},{6,14},{7,15},{8,0},{9,1},... | collective-permute-start | bytes 98312 | tf_op jit(solution)/shard_map/ppermute | solution.py:497
  6.3 5.9 %collective-permute-start.2 = (bf16[2,8192]{1,0:T(2,128)(2,1)}, bf16[2,8192]{1,0:T(2,128)(2,1)S(1)}, u32[]{:S(2)}, u32[]{:S(2)}) collective-permute-start(bf16[2,8192]{1,0:T(2,128)(2,1)} %refs_0_.4), channel_id=1, source_target_pairs={{0,12},{1,13},{2,14},{3,15},{4,8},{5,9},{6,10},{7,11},{8,4},{9,5},... | collective-permute-start | bytes 98312 | tf_op jit(solution)/shard_map/ppermute | solution.py:497
  12.3 7.8 %collective-permute-start.3 = (bf16[8,8192]{1,0:T(8,128)(2,1)S(1)}, bf16[8,8192]{1,0:T(8,128)(2,1)S(1)}, u32[]{:S(2)}, u32[]{:S(2)}) collective-permute-start(bf16[8,8192]{1,0:T(8,128)(2,1)S(1)} %stacked.1.refs_3_.refs_2_.refs_1_), channel_id=1, source_target_pairs={{0,2},{1,3},{2,0},{3,1},{4,6},{5,7},{6,4},{7,5},{8,10},{9,11},{10,... | collective-permute-start | bytes 393224 | tf_op jit(solution)/shard_map/ppermute | solution.py:497
  13.9 6.2 %collective-permute-start.4 = (bf16[8,8192]{1,0:T(8,128)(2,1)S(1)}, bf16[8,8192]{1,0:T(8,128)(2,1)S(1)}, u32[]{:S(2)}, u32[]{:S(2)}) collective-permute-start(bf16[8,8192]{1,0:T(8,128)(2,1)S(1)} %stacked.1.refs_3_.refs_2_.refs_1_), channel_id=1, source_target_pairs={{0,1},{1,0},{2,3},{3,2},{4,5},{5,4},{6,7},{7,6},{8,9},{9,8},{10,11... | collective-permute-start | bytes 393224 | tf_op jit(solution)/shard_map/ppermute | solution.py:497
  13.9 6.2 %collective-permute-start.5 = (bf16[8,8192]{1,0:T(8,128)(2,1)S(1)}, bf16[8,8192]{1,0:T(8,128)(2,1)S(1)}, u32[]{:S(2)}, u32[]{:S(2)}) collective-permute-start(bf16[8,8192]{1,0:T(8,128)(2,1)S(1)} %stacked.1.refs_3_.refs_2_.refs_1_), channel_id=1, source_target_pairs={{0,3},{1,2},{2,1},{3,0},{4,7},{5,6},{6,5},{7,4},{8,11},{9,10},{10,... | collective-permute-start | bytes 393224 | tf_op jit(solution)/shard_map/ppermute | solution.py:497
  14.5 5.8 %copy-start = (bf16[512,2048]{1,0:T(8,128)(2,1)S(1)}, bf16[512,2048]{1,0:T(8,128)(2,1)}, u32[]{:S(2)}) copy-start(bf16[512,2048]{1,0:T(8,128)(2,1)} %refs_2_.3) | copy-start | bytes 6291460
  14.5 5.8 %copy-start.4 = (s32[32]{0:T(128)S(1)}, s32[32]{0:T(128)}, u32[]{:S(2)}) copy-start(s32[32]{0:T(128)} %param.13) | copy-start | bytes 388
  21.1 1.2 %collective-permute-start.6 = (f32[32,64]{1,0:T(8,128)S(1)}, f32[32,64]{1,0:T(8,128)S(1)}, u32[]{:S(2)}, u32[]{:S(2)}) collective-permute-start(f32[32,64]{1,0:T(8,128)S(1)} %get-tuple-element.54.refs_7_.left_ref), channel_id=1, source_target_pairs={{0,1},{1,0},{2,3},{3,2},{4,5},{5,4},{6,7},{7,6},{8,9},{9,8},{10,11... | collective-permute-start | bytes 24584 | tf_op jit(solution)/shard_map/ppermute | solution.py:497
  22.3 7.0 %collective-permute-start.7 = (f32[32,64]{1,0:T(8,128)S(1)}, f32[32,64]{1,0:T(8,128)S(1)}, u32[]{:S(2)}, u32[]{:S(2)}) collective-permute-start(f32[32,64]{1,0:T(8,128)S(1)} %plus.8.refs_9_.left_ref), channel_id=1, source_target_pairs={{0,2},{1,3},{2,0},{3,1},{4,6},{5,7},{6,4},{7,5},{8,10},{9,11},{10,... | collective-permute-start | bytes 24584 | tf_op jit(solution)/shard_map/ppermute | solution.py:497
  29.3 6.1 %collective-permute-start.8 = (f32[32,64]{1,0:T(8,128)S(1)}, f32[32,64]{1,0:T(8,128)S(1)}, u32[]{:S(2)}, u32[]{:S(2)}) collective-permute-start(f32[32,64]{1,0:T(8,128)S(1)} %plus.9.refs_8_.left_ref), channel_id=1, source_target_pairs={{0,4},{1,5},{2,6},{3,7},{4,0},{5,1},{6,2},{7,3},{8,12},{9,13},{10,... | collective-permute-start | bytes 24584 | tf_op jit(solution)/shard_map/ppermute | solution.py:497
  35.4 6.8 %copy-start.2 = (bf16[32,1792]{1,0:T(8,128)(2,1)S(1)}, bf16[32,1792]{1,0:T(8,128)(2,1)}, u32[]{:S(2)}) copy-start(bf16[32,1792]{1,0:T(8,128)(2,1)} %refs_3_.3) | copy-start | bytes 344068
  35.4 6.8 %collective-permute-start.9 = (f32[32,64]{1,0:T(8,128)S(1)}, f32[32,64]{1,0:T(8,128)S(1)}, u32[]{:S(2)}, u32[]{:S(2)}) collective-permute-start(f32[32,64]{1,0:T(8,128)S(1)} %plus.10.left_ref), channel_id=1, source_target_pairs={{0,8},{1,9},{2,10},{3,11},{4,12},{5,13},{6,14},{7,15},{8,0},{9,1},... | collective-permute-start | bytes 24584 | tf_op jit(solution)/shard_map/ppermute | solution.py:497
  46.0 5.2 %collective-permute-start.10 = (f32[32,64]{1,0:T(8,128)S(1)}, f32[32,64]{1,0:T(8,128)S(1)}, u32[]{:S(2)}, u32[]{:S(2)}) collective-permute-start(f32[32,64]{1,0:T(8,128)S(1)} %get-tuple-element.64.left_ref.refs_4_), channel_id=1, source_target_pairs={{0,2},{1,3},{2,0},{3,1},{4,6},{5,7},{6,4},{7,5},{8,10},{9,11},{10,... | collective-permute-start | bytes 24584 | tf_op jit(solution)/shard_map/ppermute | solution.py:497
  51.3 4.7 %collective-permute-start.11 = (f32[32,64]{1,0:T(8,128)S(1)}, f32[32,64]{1,0:T(8,128)S(1)}, u32[]{:S(2)}, u32[]{:S(2)}) collective-permute-start(f32[32,64]{1,0:T(8,128)S(1)} %plus.12.left_ref.refs_5_), channel_id=1, source_target_pairs={{0,4},{1,5},{2,6},{3,7},{4,0},{5,1},{6,2},{7,3},{8,12},{9,13},{10,... | collective-permute-start | bytes 24584 | tf_op jit(solution)/shard_map/ppermute | solution.py:497
  55.9 13.3 %collective-permute-start.14 = (bf16[16,4096]{1,0:T(8,128)(2,1)S(1)}, bf16[16,4096]{1,0:T(8,128)(2,1)S(1)}, u32[]{:S(2)}, u32[]{:S(2)}) collective-permute-start(bf16[16,4096]{1,0:T(8,128)(2,1)S(1)} %get-tuple-element.82), channel_id=1, source_target_pairs={{0,1},{1,0},{2,3},{3,2},{4,5},{5,4},{6,7},{7,6},{8,9},{9,8},{10,11... | collective-permute-start | bytes 393224 | tf_op jit(solution)/shard_map/ppermute | solution.py:497
  56.0 6.0 %collective-permute-start.12 = (f32[32,64]{1,0:T(8,128)S(1)}, f32[32,64]{1,0:T(8,128)S(1)}, u32[]{:S(2)}, u32[]{:S(2)}) collective-permute-start(f32[32,64]{1,0:T(8,128)S(1)} %plus.13.left_ref.refs_4_), channel_id=1, source_target_pairs={{0,8},{1,9},{2,10},{3,11},{4,12},{5,13},{6,14},{7,15},{8,0},{9,1},... | collective-permute-start | bytes 24584 | tf_op jit(solution)/shard_map/ppermute | solution.py:497
  57.5 7.1 %copy-start.1 = (bf16[512,2048]{1,0:T(8,128)(2,1)S(1)}, bf16[512,2048]{1,0:T(8,128)(2,1)}, u32[]{:S(2)}) copy-start(bf16[512,2048]{1,0:T(8,128)(2,1)} %refs_2_.3) | copy-start | bytes 6291460
  62.0 2.5 %collective-permute-start.13 = (f32[32,64]{1,0:T(8,128)S(1)}, f32[32,64]{1,0:T(8,128)S(1)}, u32[]{:S(2)}, u32[]{:S(2)}) collective-permute-start(f32[32,64]{1,0:T(8,128)S(1)} %plus.14.left_ref.refs_4_), channel_id=1, source_target_pairs={{0,1},{1,0},{2,3},{3,2},{4,5},{5,4},{6,7},{7,6},{8,9},{9,8},{10,11... | collective-permute-start | bytes 24584 | tf_op jit(solution)/shard_map/ppermute | solution.py:497
  65.4 3.8 %collective-permute-start.15 = (bf16[16,3584]{1,0:T(8,128)(2,1)S(1)}, bf16[16,3584]{1,0:T(8,128)(2,1)S(1)}, u32[]{:S(2)}, u32[]{:S(2)}) collective-permute-start(bf16[16,3584]{1,0:T(8,128)(2,1)S(1)} %get-tuple-element.80.refs_3_), channel_id=1, source_target_pairs={{0,1},{1,0},{2,3},{3,2},{4,5},{5,4},{6,7},{7,6},{8,9},{9,8},{10,11... | collective-permute-start | bytes 344072 | tf_op jit(solution)/shard_map/ppermute | solution.py:497
  68.0 1.2 %collective-permute-start.16 = (bf16[16,1024]{1,0:T(8,128)(2,1)S(1)}, bf16[16,1024]{1,0:T(8,128)(2,1)S(1)}, u32[]{:S(2)}, u32[]{:S(2)}) collective-permute-start(bf16[16,1024]{1,0:T(8,128)(2,1)S(1)} %get-tuple-element.83), channel_id=1, source_target_pairs={{0,1},{1,0},{2,3},{3,2},{4,5},{5,4},{6,7},{7,6},{8,9},{9,8},{10,11... | collective-permute-start | bytes 98312 | tf_op jit(solution)/shard_map/ppermute | solution.py:497
  69.3 6.1 %collective-permute-start.17 = (bf16[8,8192]{1,0:T(8,128)(2,1)S(1)}, bf16[8,8192]{1,0:T(8,128)(2,1)S(1)}, u32[]{:S(2)}, u32[]{:S(2)}) collective-permute-start(bf16[8,8192]{1,0:T(8,128)(2,1)S(1)} %get-tuple-element.85.refs_0_), channel_id=1, source_target_pairs={{0,2},{1,3},{2,0},{3,1},{4,6},{5,7},{6,4},{7,5},{8,10},{9,11},{10,... | collective-permute-start | bytes 393224 | tf_op jit(solution)/shard_map/ppermute | solution.py:497
  75.5 6.4 %collective-permute-start.18 = (bf16[2,8192]{1,0:T(2,128)(2,1)S(1)}, bf16[2,8192]{1,0:T(2,128)(2,1)S(1)}, u32[]{:S(2)}, u32[]{:S(2)}) collective-permute-start(bf16[2,8192]{1,0:T(2,128)(2,1)S(1)} %get-tuple-element.89), channel_id=1, source_target_pairs={{0,12},{1,13},{2,14},{3,15},{4,8},{5,9},{6,10},{7,11},{8,4},{9,5},... | collective-permute-start | bytes 98312 | tf_op jit(solution)/shard_map/ppermute | solution.py:497
  78.5 4.8 %collective-permute-start.19 = (bf16[2,8192]{1,0:T(2,128)(2,1)S(1)}, bf16[2,8192]{1,0:T(2,128)(2,1)S(1)}, u32[]{:S(2)}, u32[]{:S(2)}) collective-permute-start(bf16[2,8192]{1,0:T(2,128)(2,1)S(1)} %get-tuple-element.90), channel_id=1, source_target_pairs={{0,8},{1,9},{2,10},{3,11},{4,12},{5,13},{6,14},{7,15},{8,0},{9,1},... | collective-permute-start | bytes 98312 | tf_op jit(solution)/shard_map/ppermute | solution.py:497
  79.0 4.3 %collective-permute-start.20 = (bf16[2,8192]{1,0:T(2,128)(2,1)S(1)}, bf16[2,8192]{1,0:T(2,128)(2,1)S(1)}, u32[]{:S(2)}, u32[]{:S(2)}) collective-permute-start(bf16[2,8192]{1,0:T(2,128)(2,1)S(1)} %get-tuple-element.91.refs_0_), channel_id=1, source_target_pairs={{0,4},{1,5},{2,6},{3,7},{4,0},{5,1},{6,2},{7,3},{8,12},{9,13},{10,... | collective-permute-start | bytes 98312 | tf_op jit(solution)/shard_map/ppermute | solution.py:497

commit v18 on v17

--- a/solution.py
+++ b/solution.py
@@ -54,7 +54,7 @@
 VMEM = pl.BlockSpec(memory_space=pltpu.VMEM)
 ANY = pl.BlockSpec(memory_space=pl.ANY)
 CUTS = 4
-COPIES = 16
+COPIES = 8
 STRIP = 256
 SLOTS = 6
 STORE_GRANT = 10 << 20

time: 84.1 us -> 83.5 us (level)
  Pallas kernels: 56.1 us -> 55.1 us
    pallas_call x11, Pallas kernels: 47.2 us -> 46.3 us  [store_call(): pl.pallas_call(body, in_specs=[VMEM] * (n_in + (not new)) + [ANY] * (n_hb...]
where the time goes in v18:
time: 83.5 us; the launch traced here: 83.3 us
  Pallas kernels  55.1 us (66%)
  starting transfers between devices  22.7 us (27%)
  waiting for transfers between devices  4.26 us (5%)
  between operations  0.93 us (1%)
    pallas_call x11, Pallas kernels, store_call(): pl.pallas_call(body, in_specs=[VMEM] * (n_in + (not new)) + [ANY] * (n_hb...  46.3 us
    ppermute x21, starting transfers between devices, swapped(): lax.ppermute(block, 'tp', [(i, i ^ hop) for i in range(lax.axis_size('tp'...  22.7 us
    pallas_call x2, Pallas kernels, outer(): pl.pallas_call(outer_kernel, grid=(height // block,), in_specs=[pl.BlockS...  6.38 us
    ppermute x21, waiting for transfers between devices, swapped(): lax.ppermute(block, 'tp', [(i, i ^ hop) for i in range(lax.axis_size('tp'...  4.26 us
  transfers between devices with their start and end apart: 21, of which 4 were waited for; matrix products, arithmetic and copies ran while one was open for 0% of the time, Pallas kernels for 60%

profile of v18, /device:TPU:0, one launch (start us, length us, event | category | flops | bytes accessed | tf_op | source)
XLA Modules:
  0.0 83.3 jit_solution(15958375583182940664)
XLA Ops:
  0.6 0.0 copy-start.3
  0.6 3.1 %collective-permute-start = (bf16[2,8192]{1,0:T(2,128)(2,1)}, bf16[2,8192]{1,0:T(2,128)(2,1)S(1)}, u32[]{:S(2)}, u32[]{:S(2)}) collective-permute-start(bf16[2,8192]{1,0:T(2,128)(2,1)} %refs_0_.4), channel_id=1, source_target_pairs={{0,4},{1,5},{2,6},{3,7},{4,0},{5,1},{6,2},{7,3},{8,12},{9,13},{10,... | collective-permute-start | bytes 98312 | tf_op jit(solution)/shard_map/ppermute | solution.py:497
  3.7 2.6 %collective-permute-start.1 = (bf16[2,8192]{1,0:T(2,128)(2,1)}, bf16[2,8192]{1,0:T(2,128)(2,1)S(1)}, u32[]{:S(2)}, u32[]{:S(2)}) collective-permute-start(bf16[2,8192]{1,0:T(2,128)(2,1)} %refs_0_.4), channel_id=1, source_target_pairs={{0,8},{1,9},{2,10},{3,11},{4,12},{5,13},{6,14},{7,15},{8,0},{9,1},... | collective-permute-start | bytes 98312 | tf_op jit(solution)/shard_map/ppermute | solution.py:497
  6.3 0.0 collective-permute-start.2
  6.3 5.3 %fetch.2 = (bf16[12288,1792]{1,0:T(8,128)(2,1)S(1)}, f32[8,128]{1,0:T(8,128)S(1)}) custom-call(bf16[8192,1792]{1,0:T(8,128)(2,1)} %refs_4_.1, bf16[8192,1792]{1,0:T(8,128)(2,1)} %refs_3_.5), custom_call_target="tpu_custom_call" | custom-call | bytes 14680064 | tf_op jit(solution)/shard_map/fetch/pallas_call | solution.py:102
  11.7 0.0 collective-permute-done.refs_1_
  11.7 0.0 collective-permute-done.1.refs_2_
  11.7 0.6 collective-permute-done.2.refs_3_
  12.2 0.1 stacked.1.refs_3_.refs_2_.refs_1_
  12.3 1.6 %collective-permute-start.3 = (bf16[8,8192]{1,0:T(8,128)(2,1)S(1)}, bf16[8,8192]{1,0:T(8,128)(2,1)S(1)}, u32[]{:S(2)}, u32[]{:S(2)}) collective-permute-start(bf16[8,8192]{1,0:T(8,128)(2,1)S(1)} %stacked.1.refs_3_.refs_2_.refs_1_), channel_id=1, source_target_pairs={{0,2},{1,3},{2,0},{3,1},{4,6},{5,7},{6,4},{7,5},{8,10},{9,11},{10,... | collective-permute-start | bytes 393224 | tf_op jit(solution)/shard_map/ppermute | solution.py:497
  13.9 0.0 collective-permute-start.4
  13.9 0.6 collective-permute-start.5
  14.5 5.5 %fetch.3 = (bf16[12288,1792]{1,0:T(8,128)(2,1)S(1)}, f32[8,128]{1,0:T(8,128)S(1)}) custom-call(bf16[12288,1792]{1,0:T(8,128)(2,1)S(1)} %get-tuple-element.50.refs_0_, bf16[8192,1792]{1,0:T(8,128)(2,1)} %refs_4_.1, bf16[8192,1792]{1,0:T(8,128)(2,1)} %refs_3_.5, bf16[8,8192]{1,0:T(8,128)(2,1)S(1)} %stacked.1.refs_3_.refs_2_.refs_1_), custom_call_target="tpu_custom_call", output_to_operand_aliasing={{0}: (0, {})} | custom-call | bytes 14680064 | tf_op jit(solution)/shard_map/fetch/pallas_call | solution.py:102
  20.0 0.0 collective-permute-done.3.refs_3_.refs_2_
  20.0 0.0 collective-permute-done.4.refs_4_.refs_3_
  20.0 0.0 collective-permute-done.5.refs_5_.refs_4_
  20.1 0.3 copy-done
  20.4 0.7 low_part.1
  21.1 0.0 collective-permute-start.6
  21.1 1.2 %collective-permute-done.6.right_ref = f32[32,64]{1,0:T(8,128)S(1)} collective-permute-done((f32[32,64]{1,0:T(8,128)S(1)}, f32[32,64]{1,0:T(8,128)S(1)}, u32[]{:S(2)}, u32[]{:S(2)}) %collective-permute-start.6) | collective-permute-done | bytes 8224 | tf_op jit(solution)/shard_map/ppermute | solution.py:497
  22.3 1.5 %collective-permute-start.7 = (f32[32,64]{1,0:T(8,128)S(1)}, f32[32,64]{1,0:T(8,128)S(1)}, u32[]{:S(2)}, u32[]{:S(2)}) collective-permute-start(f32[32,64]{1,0:T(8,128)S(1)} %plus.8.refs_9_.left_ref), channel_id=1, source_target_pairs={{0,2},{1,3},{2,0},{3,1},{4,6},{5,7},{6,4},{7,5},{8,10},{9,11},{10,... | collective-permute-start | bytes 24584 | tf_op jit(solution)/shard_map/ppermute | solution.py:497
  23.8 5.3 %forward.3 = (bf16[12288,1792]{1,0:T(8,128)(2,1)S(1)}, f32[32,1792]{1,0:T(8,128)S(1)}, f32[32,1792]{1,0:T(8,128)S(1)}) custom-call(bf16[12288,1792]{1,0:T(8,128)(2,1)S(1)} %get-tuple-element.52.refs_0_, bf16[8,8192]{1,0:T(8,128)(2,1)S(1)} %stacked.1.refs_3_.refs_2_.refs_1_, ...), custom_call_target="tpu_custom_call", output_to_operand_aliasing={{0}: (0, {})} | custom-call | flops 939524096 | bytes 14680064 | tf_op jit(solution)/shard_map/forward/pallas_call | solution.py:102
  29.1 0.0 collective-permute-done.7.right_ref
  29.1 0.4 collective-permute-start.8
  29.6 5.4 %forward.4 = (bf16[12288,1792]{1,0:T(8,128)(2,1)S(1)}, f32[32,1792]{1,0:T(8,128)S(1)}, f32[32,1792]{1,0:T(8,128)S(1)}) custom-call(bf16[12288,1792]{1,0:T(8,128)(2,1)S(1)} %get-tuple-element.55.refs_0_, bf16[8,8192]{1,0:T(8,128)(2,1)S(1)} %stacked.1.refs_3_.refs_2_.refs_1_, ...), custom_call_target="tpu_custom_call", output_to_operand_aliasing={{0}: (0, {})} | custom-call | flops 469762048 | bytes 14680064 | tf_op jit(solution)/shard_map/forward/pallas_call | solution.py:102
  35.0 0.0 copy-start.2
  35.0 0.0 collective-permute-done.8.right_ref
  35.0 3.5 %collective-permute-start.9 = (f32[32,64]{1,0:T(8,128)S(1)}, f32[32,64]{1,0:T(8,128)S(1)}, u32[]{:S(2)}, u32[]{:S(2)}) collective-permute-start(f32[32,64]{1,0:T(8,128)S(1)} %plus.10.left_ref), channel_id=1, source_target_pairs={{0,8},{1,9},{2,10},{3,11},{4,12},{5,13},{6,14},{7,15},{8,0},{9,1},... | collective-permute-start | bytes 24584 | tf_op jit(solution)/shard_map/ppermute | solution.py:497
  38.6 3.2 %forward.5 = (bf16[12288,1792]{1,0:T(8,128)(2,1)S(1)}, f32[32,1792]{1,0:T(8,128)S(1)}, f32[32,1792]{1,0:T(8,128)S(1)}) custom-call(bf16[12288,1792]{1,0:T(8,128)(2,1)S(1)} %get-tuple-element.58.refs_0_, bf16[8,8192]{1,0:T(8,128)(2,1)S(1)} %stacked.1.refs_3_.refs_2_.refs_1_, ...), custom_call_target="tpu_custom_call", output_to_operand_aliasing={{0}: (0, {})} | custom-call | flops 469762048 | bytes 7340032 | tf_op jit(solution)/shard_map/forward/pallas_call | solution.py:102
  41.8 0.0 collective-permute-done.9.right_ref
  41.8 3.8 %activation.1 = (bf16[12288,1792]{1,0:T(8,128)(2,1)S(1)}, bf16[32,1792]{1,0:T(8,128)(2,1)S(1)}, bf16[32,1792]{1,0:T(8,128)(2,1)S(1)}, f32[32,64]{1,0:T(8,128)S(1)}, bf16[32,2048]{1,0:T(8,128)(2,1)S(1)}) custom-call(bf16[12288,1792]{1,0:T(8,128)(2,1)S(1)} %get-tuple-element.61.refs_0_, ...), custom_call_target="tpu_custom_call", output_to_operand_aliasing={{0}: (0, {})} | custom-call | flops 469762048 | tf_op jit(solution)/shard_map/activation/pallas_call | solution.py:102
  45.6 0.5 collective-permute-start.10
  46.1 4.4 %backward.5 = (bf16[12288,1792]{1,0:T(8,128)(2,1)S(1)}, f32[16,2048]{1,0:T(8,128)S(1)}, bf16[16,2048]{1,0:T(8,128)(2,1)S(1)}) custom-call(bf16[12288,1792]{1,0:T(8,128)(2,1)S(1)} %get-tuple-element.65.refs_0_, bf16[32,1792]{1,0:T(8,128)(2,1)S(1)} %get-tuple-element.66.refs_1_.right_ref, ...), custom_call_target="tpu_custom_call", output_to_operand_aliasing={{0}: (0, {})} | custom-call | flops 469762048 | bytes 7340032 | tf_op jit(solution)/shard_map/backward/pallas_call | solution.py:102
  50.6 0.0 collective-permute-done.10.right_ref
  50.6 0.3 collective-permute-start.11
  50.9 4.4 %backward.6 = (bf16[12288,1792]{1,0:T(8,128)(2,1)S(1)}, f32[16,2048]{1,0:T(8,128)S(1)}, bf16[16,4096]{1,0:T(8,128)(2,1)S(1)}) custom-call(bf16[12288,1792]{1,0:T(8,128)(2,1)S(1)} %get-tuple-element.68.refs_0_, bf16[32,1792]{1,0:T(8,128)(2,1)S(1)} %get-tuple-element.66.refs_1_.right_ref, ...), custom_call_target="tpu_custom_call", output_to_operand_aliasing={{0}: (0, {})} | custom-call | flops 469762048 | bytes 7340032 | tf_op jit(solution)/shard_map/backward/pallas_call | solution.py:102
  55.3 0.1 collective-permute-start.14
  55.4 0.0 collective-permute-done.11.right_ref
  55.4 1.5 %collective-permute-start.12 = (f32[32,64]{1,0:T(8,128)S(1)}, f32[32,64]{1,0:T(8,128)S(1)}, u32[]{:S(2)}, u32[]{:S(2)}) collective-permute-start(f32[32,64]{1,0:T(8,128)S(1)} %plus.13.left_ref.refs_4_), channel_id=1, source_target_pairs={{0,8},{1,9},{2,10},{3,11},{4,12},{5,13},{6,14},{7,15},{8,0},{9,1},... | collective-permute-start | bytes 24584 | tf_op jit(solution)/shard_map/ppermute | solution.py:497
  56.9 4.4 %backward.7 = (bf16[12288,1792]{1,0:T(8,128)(2,1)S(1)}, f32[16,2048]{1,0:T(8,128)S(1)}, bf16[16,2048]{1,0:T(8,128)(2,1)S(1)}) custom-call(bf16[12288,1792]{1,0:T(8,128)(2,1)S(1)} %get-tuple-element.70.refs_0_, bf16[32,1792]{1,0:T(8,128)(2,1)S(1)} %get-tuple-element.66.refs_1_.right_ref, ...), custom_call_target="tpu_custom_call", output_to_operand_aliasing={{0}: (0, {})} | custom-call | flops 469762048 | bytes 7340032 | tf_op jit(solution)/shard_map/backward/pallas_call | solution.py:102
  61.4 0.0 collective-permute-done.12.right_ref
  61.4 0.3 collective-permute-start.13
  61.7 2.2 %backward.8 = (bf16[12288,1792]{1,0:T(8,128)(2,1)S(1)}, f32[16,1024]{1,0:T(8,128)S(1)}, bf16[16,3072]{1,0:T(8,128)(2,1)S(1)}) custom-call(bf16[12288,1792]{1,0:T(8,128)(2,1)S(1)} %get-tuple-element.71.refs_0_, bf16[32,1792]{1,0:T(8,128)(2,1)S(1)} %get-tuple-element.66.refs_1_.right_ref, ...), custom_call_target="tpu_custom_call", output_to_operand_aliasing={{0}: (0, {})} | custom-call | flops 234881024 | tf_op jit(solution)/shard_map/backward/pallas_call | solution.py:102
  63.9 0.0 collective-permute-done.13.right_ref
  63.9 0.9 %adapter_part.1 = (bf16[16,512]{1,0:T(8,128)(2,1)S(1)}, bf16[16,3584]{1,0:T(8,128)(2,1)S(1)}, bf16[32,2048]{1,0:T(8,128)(2,1)S(1)}) custom-call(f32[32,64]{1,0:T(8,128)S(1)} %plus.15.refs_0_, s32[1,32]{1,0:T(1,128)S(1)} %bitcast.3, bf16[512,2048]{1,0:T(8,128)(2,1)S(1)} %copy-done.1, bf16[16,3072]{1,0:T(8,128)(2,1)S(1)} %get-tuple-element.73.refs_3_), custom_call_target="tpu_custom_call" | custom-call | flops 67108864 | bytes 2097152 | tf_op jit(solution)/shard_map/adapter_part/pallas_call | solution.py:301
  64.8 0.4 collective-permute-start.15
  65.2 2.2 %backward.9 = (bf16[12288,1792]{1,0:T(8,128)(2,1)S(1)}, f32[16,1024]{1,0:T(8,128)S(1)}, bf16[16,1024]{1,0:T(8,128)(2,1)S(1)}) custom-call(bf16[12288,1792]{1,0:T(8,128)(2,1)S(1)} %get-tuple-element.79.refs_0_, bf16[32,1792]{1,0:T(8,128)(2,1)S(1)} %get-tuple-element.66.refs_1_.right_ref, ...), custom_call_target="tpu_custom_call", output_to_operand_aliasing={{0}: (0, {})} | custom-call | flops 234881024 | tf_op jit(solution)/shard_map/backward/pallas_call | solution.py:102
  67.4 0.2 collective-permute-start.16
  67.6 1.0 %collective-permute-done.16.refs_8_ = bf16[16,1024]{1,0:T(8,128)(2,1)S(1)} collective-permute-done((bf16[16,1024]{1,0:T(8,128)(2,1)S(1)}, bf16[16,1024]{1,0:T(8,128)(2,1)S(1)}, u32[]{:S(2)}, u32[]{:S(2)}) %collective-permute-start.16) | collective-permute-done | bytes 32800 | tf_op jit(solution)/shard_map/ppermute | solution.py:497
  68.6 0.0 collective-permute-done.14.refs_6_
  68.6 0.0 collective-permute-done.15.refs_7_
  68.6 0.1 first_halves.1
  68.7 1.6 %collective-permute-start.17 = (bf16[8,8192]{1,0:T(8,128)(2,1)S(1)}, bf16[8,8192]{1,0:T(8,128)(2,1)S(1)}, u32[]{:S(2)}, u32[]{:S(2)}) collective-permute-start(bf16[8,8192]{1,0:T(8,128)(2,1)S(1)} %get-tuple-element.85.refs_0_), channel_id=1, source_target_pairs={{0,2},{1,3},{2,0},{3,1},{4,6},{5,7},{6,4},{7,5},{8,10},{9,11},{10,... | collective-permute-start | bytes 393224 | tf_op jit(solution)/shard_map/ppermute | solution.py:497
  70.3 4.5 %up_maps.1 = (bf16[2048,1792]{1,0:T(8,128)(2,1)}, f32[8,128]{1,0:T(8,128)S(1)}) custom-call(bf16[32,2048]{1,0:T(8,128)(2,1)S(1)} %get-tuple-element.86.left_ref, bf16[32,1792]{1,0:T(8,128)(2,1)S(1)} %get-tuple-element.66.refs_1_.right_ref, bf16[8,8192]{1,0:T(8,128)(2,1)S(1)} %get-tuple-element.85.refs_0_), custom_call_target="tpu_custom_call" | custom-call | flops 234881024 | bytes 7340032 | tf_op jit(solution)/shard_map/up_maps/pallas_call | solution.py:459
  74.8 0.0 collective-permute-done.17.came_ref
  74.8 0.1 quarters.1
  74.9 3.0 %collective-permute-start.18 = (bf16[2,8192]{1,0:T(2,128)(2,1)S(1)}, bf16[2,8192]{1,0:T(2,128)(2,1)S(1)}, u32[]{:S(2)}, u32[]{:S(2)}) collective-permute-start(bf16[2,8192]{1,0:T(2,128)(2,1)S(1)} %get-tuple-element.89), channel_id=1, source_target_pairs={{0,12},{1,13},{2,14},{3,15},{4,8},{5,9},{6,10},{7,11},{8,4},{9,5},... | collective-permute-start | bytes 98312 | tf_op jit(solution)/shard_map/ppermute | solution.py:497
  77.8 0.5 collective-permute-start.19
  78.4 0.9 %collective-permute-start.20 = (bf16[2,8192]{1,0:T(2,128)(2,1)S(1)}, bf16[2,8192]{1,0:T(2,128)(2,1)S(1)}, u32[]{:S(2)}, u32[]{:S(2)}) collective-permute-start(bf16[2,8192]{1,0:T(2,128)(2,1)S(1)} %get-tuple-element.91.refs_0_), channel_id=1, source_target_pairs={{0,4},{1,5},{2,6},{3,7},{4,0},{5,1},{6,2},{7,3},{8,12},{9,13},{10,... | collective-permute-start | bytes 98312 | tf_op jit(solution)/shard_map/ppermute | solution.py:497
  79.3 1.9 %down_maps.1 = (bf16[512,2048]{1,0:T(8,128)(2,1)}, f32[8,128]{1,0:T(8,128)S(1)}) custom-call(bf16[32,512]{1,0:T(8,128)(2,1)S(1)} %get-tuple-element.92.left_ref, bf16[32,2048]{1,0:T(8,128)(2,1)S(1)} %get-tuple-element.93.right_ref, bf16[2,8192]{1,0:T(2,128)(2,1)S(1)} %get-tuple-element.91.refs_0_), custom_call_target="tpu_custom_call" | custom-call | flops 67108864 | bytes 2097152 | tf_op jit(solution)/shard_map/down_maps/pallas_call | solution.py:459
  81.2 0.0 collective-permute-done.18.refs_0_
  81.2 1.4 %collective-permute-done.19.refs_1_ = bf16[2,8192]{1,0:T(2,128)(2,1)S(1)} collective-permute-done((bf16[2,8192]{1,0:T(2,128)(2,1)S(1)}, bf16[2,8192]{1,0:T(2,128)(2,1)S(1)}, u32[]{:S(2)}, u32[]{:S(2)}) %collective-permute-start.19) | collective-permute-done | bytes 32800 | tf_op jit(solution)/shard_map/ppermute | solution.py:497
  82.6 0.0 collective-permute-done.20.refs_2_
  82.7 0.7 final.1
  (15 shorter events, 0.1 us)
Async XLA Ops:
  0.6 11.6 %copy-start.3 = (bf16[2,8192]{1,0:T(2,128)(2,1)S(1)}, bf16[2,8192]{1,0:T(2,128)(2,1)}, u32[]{:S(2)}) copy-start(bf16[2,8192]{1,0:T(2,128)(2,1)} %refs_0_.4) | copy-start | bytes 98308
  0.6 11.0 %collective-permute-start = (bf16[2,8192]{1,0:T(2,128)(2,1)}, bf16[2,8192]{1,0:T(2,128)(2,1)S(1)}, u32[]{:S(2)}, u32[]{:S(2)}) collective-permute-start(bf16[2,8192]{1,0:T(2,128)(2,1)} %refs_0_.4), channel_id=1, source_target_pairs={{0,4},{1,5},{2,6},{3,7},{4,0},{5,1},{6,2},{7,3},{8,12},{9,13},{10,... | collective-permute-start | bytes 98312 | tf_op jit(solution)/shard_map/ppermute | solution.py:497
  3.7 7.9 %collective-permute-start.1 = (bf16[2,8192]{1,0:T(2,128)(2,1)}, bf16[2,8192]{1,0:T(2,128)(2,1)S(1)}, u32[]{:S(2)}, u32[]{:S(2)}) collective-permute-start(bf16[2,8192]{1,0:T(2,128)(2,1)} %refs_0_.4), channel_id=1, source_target_pairs={{0,8},{1,9},{2,10},{3,11},{4,12},{5,13},{6,14},{7,15},{8,0},{9,1},... | collective-permute-start | bytes 98312 | tf_op jit(solution)/shard_map/ppermute | solution.py:497
  6.3 5.9 %collective-permute-start.2 = (bf16[2,8192]{1,0:T(2,128)(2,1)}, bf16[2,8192]{1,0:T(2,128)(2,1)S(1)}, u32[]{:S(2)}, u32[]{:S(2)}) collective-permute-start(bf16[2,8192]{1,0:T(2,128)(2,1)} %refs_0_.4), channel_id=1, source_target_pairs={{0,12},{1,13},{2,14},{3,15},{4,8},{5,9},{6,10},{7,11},{8,4},{9,5},... | collective-permute-start | bytes 98312 | tf_op jit(solution)/shard_map/ppermute | solution.py:497
  12.3 7.7 %collective-permute-start.3 = (bf16[8,8192]{1,0:T(8,128)(2,1)S(1)}, bf16[8,8192]{1,0:T(8,128)(2,1)S(1)}, u32[]{:S(2)}, u32[]{:S(2)}) collective-permute-start(bf16[8,8192]{1,0:T(8,128)(2,1)S(1)} %stacked.1.refs_3_.refs_2_.refs_1_), channel_id=1, source_target_pairs={{0,2},{1,3},{2,0},{3,1},{4,6},{5,7},{6,4},{7,5},{8,10},{9,11},{10,... | collective-permute-start | bytes 393224 | tf_op jit(solution)/shard_map/ppermute | solution.py:497
  13.9 6.1 %collective-permute-start.4 = (bf16[8,8192]{1,0:T(8,128)(2,1)S(1)}, bf16[8,8192]{1,0:T(8,128)(2,1)S(1)}, u32[]{:S(2)}, u32[]{:S(2)}) collective-permute-start(bf16[8,8192]{1,0:T(8,128)(2,1)S(1)} %stacked.1.refs_3_.refs_2_.refs_1_), channel_id=1, source_target_pairs={{0,1},{1,0},{2,3},{3,2},{4,5},{5,4},{6,7},{7,6},{8,9},{9,8},{10,11... | collective-permute-start | bytes 393224 | tf_op jit(solution)/shard_map/ppermute | solution.py:497
  13.9 6.1 %collective-permute-start.5 = (bf16[8,8192]{1,0:T(8,128)(2,1)S(1)}, bf16[8,8192]{1,0:T(8,128)(2,1)S(1)}, u32[]{:S(2)}, u32[]{:S(2)}) collective-permute-start(bf16[8,8192]{1,0:T(8,128)(2,1)S(1)} %stacked.1.refs_3_.refs_2_.refs_1_), channel_id=1, source_target_pairs={{0,3},{1,2},{2,1},{3,0},{4,7},{5,6},{6,5},{7,4},{8,11},{9,10},{10,... | collective-permute-start | bytes 393224 | tf_op jit(solution)/shard_map/ppermute | solution.py:497
  14.5 5.8 %copy-start = (bf16[512,2048]{1,0:T(8,128)(2,1)S(1)}, bf16[512,2048]{1,0:T(8,128)(2,1)}, u32[]{:S(2)}) copy-start(bf16[512,2048]{1,0:T(8,128)(2,1)} %refs_2_.3) | copy-start | bytes 6291460
  14.5 5.8 %copy-start.4 = (s32[32]{0:T(128)S(1)}, s32[32]{0:T(128)}, u32[]{:S(2)}) copy-start(s32[32]{0:T(128)} %param.13) | copy-start | bytes 388
  21.1 1.2 %collective-permute-start.6 = (f32[32,64]{1,0:T(8,128)S(1)}, f32[32,64]{1,0:T(8,128)S(1)}, u32[]{:S(2)}, u32[]{:S(2)}) collective-permute-start(f32[32,64]{1,0:T(8,128)S(1)} %get-tuple-element.54.refs_7_.left_ref), channel_id=1, source_target_pairs={{0,1},{1,0},{2,3},{3,2},{4,5},{5,4},{6,7},{7,6},{8,9},{9,8},{10,11... | collective-permute-start | bytes 24584 | tf_op jit(solution)/shard_map/ppermute | solution.py:497
  22.3 6.9 %collective-permute-start.7 = (f32[32,64]{1,0:T(8,128)S(1)}, f32[32,64]{1,0:T(8,128)S(1)}, u32[]{:S(2)}, u32[]{:S(2)}) collective-permute-start(f32[32,64]{1,0:T(8,128)S(1)} %plus.8.refs_9_.left_ref), channel_id=1, source_target_pairs={{0,2},{1,3},{2,0},{3,1},{4,6},{5,7},{6,4},{7,5},{8,10},{9,11},{10,... | collective-permute-start | bytes 24584 | tf_op jit(solution)/shard_map/ppermute | solution.py:497
  29.1 5.9 %collective-permute-start.8 = (f32[32,64]{1,0:T(8,128)S(1)}, f32[32,64]{1,0:T(8,128)S(1)}, u32[]{:S(2)}, u32[]{:S(2)}) collective-permute-start(f32[32,64]{1,0:T(8,128)S(1)} %plus.9.refs_8_.left_ref), channel_id=1, source_target_pairs={{0,4},{1,5},{2,6},{3,7},{4,0},{5,1},{6,2},{7,3},{8,12},{9,13},{10,... | collective-permute-start | bytes 24584 | tf_op jit(solution)/shard_map/ppermute | solution.py:497
  35.0 6.8 %copy-start.2 = (bf16[32,1792]{1,0:T(8,128)(2,1)S(1)}, bf16[32,1792]{1,0:T(8,128)(2,1)}, u32[]{:S(2)}) copy-start(bf16[32,1792]{1,0:T(8,128)(2,1)} %refs_3_.3) | copy-start | bytes 344068
  35.0 6.7 %collective-permute-start.9 = (f32[32,64]{1,0:T(8,128)S(1)}, f32[32,64]{1,0:T(8,128)S(1)}, u32[]{:S(2)}, u32[]{:S(2)}) collective-permute-start(f32[32,64]{1,0:T(8,128)S(1)} %plus.10.left_ref), channel_id=1, source_target_pairs={{0,8},{1,9},{2,10},{3,11},{4,12},{5,13},{6,14},{7,15},{8,0},{9,1},... | collective-permute-start | bytes 24584 | tf_op jit(solution)/shard_map/ppermute | solution.py:497
  45.6 5.0 %collective-permute-start.10 = (f32[32,64]{1,0:T(8,128)S(1)}, f32[32,64]{1,0:T(8,128)S(1)}, u32[]{:S(2)}, u32[]{:S(2)}) collective-permute-start(f32[32,64]{1,0:T(8,128)S(1)} %get-tuple-element.64.left_ref.refs_4_), channel_id=1, source_target_pairs={{0,2},{1,3},{2,0},{3,1},{4,6},{5,7},{6,4},{7,5},{8,10},{9,11},{10,... | collective-permute-start | bytes 24584 | tf_op jit(solution)/shard_map/ppermute | solution.py:497
  50.6 4.8 %collective-permute-start.11 = (f32[32,64]{1,0:T(8,128)S(1)}, f32[32,64]{1,0:T(8,128)S(1)}, u32[]{:S(2)}, u32[]{:S(2)}) collective-permute-start(f32[32,64]{1,0:T(8,128)S(1)} %plus.12.left_ref.refs_5_), channel_id=1, source_target_pairs={{0,4},{1,5},{2,6},{3,7},{4,0},{5,1},{6,2},{7,3},{8,12},{9,13},{10,... | collective-permute-start | bytes 24584 | tf_op jit(solution)/shard_map/ppermute | solution.py:497
  55.3 13.3 %collective-permute-start.14 = (bf16[16,4096]{1,0:T(8,128)(2,1)S(1)}, bf16[16,4096]{1,0:T(8,128)(2,1)S(1)}, u32[]{:S(2)}, u32[]{:S(2)}) collective-permute-start(bf16[16,4096]{1,0:T(8,128)(2,1)S(1)} %get-tuple-element.82), channel_id=1, source_target_pairs={{0,1},{1,0},{2,3},{3,2},{4,5},{5,4},{6,7},{7,6},{8,9},{9,8},{10,11... | collective-permute-start | bytes 393224 | tf_op jit(solution)/shard_map/ppermute | solution.py:497
  55.4 6.0 %collective-permute-start.12 = (f32[32,64]{1,0:T(8,128)S(1)}, f32[32,64]{1,0:T(8,128)S(1)}, u32[]{:S(2)}, u32[]{:S(2)}) collective-permute-start(f32[32,64]{1,0:T(8,128)S(1)} %plus.13.left_ref.refs_4_), channel_id=1, source_target_pairs={{0,8},{1,9},{2,10},{3,11},{4,12},{5,13},{6,14},{7,15},{8,0},{9,1},... | collective-permute-start | bytes 24584 | tf_op jit(solution)/shard_map/ppermute | solution.py:497
  56.9 7.0 %copy-start.1 = (bf16[512,2048]{1,0:T(8,128)(2,1)S(1)}, bf16[512,2048]{1,0:T(8,128)(2,1)}, u32[]{:S(2)}) copy-start(bf16[512,2048]{1,0:T(8,128)(2,1)} %refs_2_.3) | copy-start | bytes 6291460
  61.4 2.5 %collective-permute-start.13 = (f32[32,64]{1,0:T(8,128)S(1)}, f32[32,64]{1,0:T(8,128)S(1)}, u32[]{:S(2)}, u32[]{:S(2)}) collective-permute-start(f32[32,64]{1,0:T(8,128)S(1)} %plus.14.left_ref.refs_4_), channel_id=1, source_target_pairs={{0,1},{1,0},{2,3},{3,2},{4,5},{5,4},{6,7},{7,6},{8,9},{9,8},{10,11... | collective-permute-start | bytes 24584 | tf_op jit(solution)/shard_map/ppermute | solution.py:497
  64.8 3.8 %collective-permute-start.15 = (bf16[16,3584]{1,0:T(8,128)(2,1)S(1)}, bf16[16,3584]{1,0:T(8,128)(2,1)S(1)}, u32[]{:S(2)}, u32[]{:S(2)}) collective-permute-start(bf16[16,3584]{1,0:T(8,128)(2,1)S(1)} %get-tuple-element.80.refs_3_), channel_id=1, source_target_pairs={{0,1},{1,0},{2,3},{3,2},{4,5},{5,4},{6,7},{7,6},{8,9},{9,8},{10,11... | collective-permute-start | bytes 344072 | tf_op jit(solution)/shard_map/ppermute | solution.py:497
  67.4 1.2 %collective-permute-start.16 = (bf16[16,1024]{1,0:T(8,128)(2,1)S(1)}, bf16[16,1024]{1,0:T(8,128)(2,1)S(1)}, u32[]{:S(2)}, u32[]{:S(2)}) collective-permute-start(bf16[16,1024]{1,0:T(8,128)(2,1)S(1)} %get-tuple-element.83), channel_id=1, source_target_pairs={{0,1},{1,0},{2,3},{3,2},{4,5},{5,4},{6,7},{7,6},{8,9},{9,8},{10,11... | collective-permute-start | bytes 98312 | tf_op jit(solution)/shard_map/ppermute | solution.py:497
  68.7 6.1 %collective-permute-start.17 = (bf16[8,8192]{1,0:T(8,128)(2,1)S(1)}, bf16[8,8192]{1,0:T(8,128)(2,1)S(1)}, u32[]{:S(2)}, u32[]{:S(2)}) collective-permute-start(bf16[8,8192]{1,0:T(8,128)(2,1)S(1)} %get-tuple-element.85.refs_0_), channel_id=1, source_target_pairs={{0,2},{1,3},{2,0},{3,1},{4,6},{5,7},{6,4},{7,5},{8,10},{9,11},{10,... | collective-permute-start | bytes 393224 | tf_op jit(solution)/shard_map/ppermute | solution.py:497
  74.9 6.4 %collective-permute-start.18 = (bf16[2,8192]{1,0:T(2,128)(2,1)S(1)}, bf16[2,8192]{1,0:T(2,128)(2,1)S(1)}, u32[]{:S(2)}, u32[]{:S(2)}) collective-permute-start(bf16[2,8192]{1,0:T(2,128)(2,1)S(1)} %get-tuple-element.89), channel_id=1, source_target_pairs={{0,12},{1,13},{2,14},{3,15},{4,8},{5,9},{6,10},{7,11},{8,4},{9,5},... | collective-permute-start | bytes 98312 | tf_op jit(solution)/shard_map/ppermute | solution.py:497
  77.8 4.8 %collective-permute-start.19 = (bf16[2,8192]{1,0:T(2,128)(2,1)S(1)}, bf16[2,8192]{1,0:T(2,128)(2,1)S(1)}, u32[]{:S(2)}, u32[]{:S(2)}) collective-permute-start(bf16[2,8192]{1,0:T(2,128)(2,1)S(1)} %get-tuple-element.90), channel_id=1, source_target_pairs={{0,8},{1,9},{2,10},{3,11},{4,12},{5,13},{6,14},{7,15},{8,0},{9,1},... | collective-permute-start | bytes 98312 | tf_op jit(solution)/shard_map/ppermute | solution.py:497
  78.4 4.3 %collective-permute-start.20 = (bf16[2,8192]{1,0:T(2,128)(2,1)S(1)}, bf16[2,8192]{1,0:T(2,128)(2,1)S(1)}, u32[]{:S(2)}, u32[]{:S(2)}) collective-permute-start(bf16[2,8192]{1,0:T(2,128)(2,1)S(1)} %get-tuple-element.91.refs_0_), channel_id=1, source_target_pairs={{0,4},{1,5},{2,6},{3,7},{4,0},{5,1},{6,2},{7,3},{8,12},{9,13},{10,... | collective-permute-start | bytes 98312 | tf_op jit(solution)/shard_map/ppermute | solution.py:497

commit v19 on v18

--- a/solution.py
+++ b/solution.py
@@ -166,48 +166,50 @@
     return tenant_mask(tenants.astype(jnp.int32), pick.shape[0])
 
 
-def low_kernel(count, aligned, down_ref, tenants_ref, *refs):
+def low_kernel(count, aligned, down_ref, other_down_ref, tenants_ref, *refs):
     x, (span_out, low_ref) = refs[:-3], refs[-2:]
     own = lax.axis_index("tp")
-    if aligned:
-        width = down_ref.shape[0]
-        at = pl.ds(pl.multiple_of(own * width, width), width)
-        span = jnp.concatenate([ref[:, at] for ref in x], axis=0)
-    else:
-        span = jnp.concatenate([ref[...] for ref in x], axis=0)
-    span_out[...] = span
-    rows = span.shape[0]
-    wide = jnp.dot(span, down_ref[...], preferred_element_type=jnp.float32)
+    width = down_ref.shape[0]
+    spans = []
+    for n, device in enumerate((own, own ^ 1)):
+        if aligned:
+            at = pl.ds(pl.multiple_of(device * width, width), width)
+            spans.append(jnp.concatenate([ref[:, at] for ref in x], axis=0))
+        else:
+            spans.append(jnp.concatenate([ref[...] for ref in x[n::2]], axis=0))
+    span_out[...] = spans[0]
+    rows = spans[0].shape[0]
+    wide = jnp.dot(spans[0], down_ref[...], preferred_element_type=jnp.float32)
+    wide = wide + jnp.dot(spans[1], other_down_ref[...], preferred_element_type=jnp.float32)
     low = select_block(wide, held_mask(pick_held(own, rows, count), tenants_ref[...]))
     low_ref[...] = picked(pick_given(own, rows, count), low)
 
 
-def low_part(down, tenants, x, count, after):
+def low_part(down, other_down, tenants, x, count, after):
     rows, span = sum(block.shape[0] for block in x), down.shape[0]
     aligned = span % 128 == 0
     if not aligned:
+        own = lax.axis_index("tp")
         x = [
             lax.dynamic_slice(
-                block,
-                (0, lax.axis_index("tp") * span),
-                (block.shape[0], span),
-                allow_negative_indices=False,
+                block, (0, device * span), (block.shape[0], span), allow_negative_indices=False
             )
             for block in x
+            for device in (own, own ^ 1)
         ]
     return pl.pallas_call(
         lambda *refs: low_kernel(count, aligned, *refs),
-        in_specs=[VMEM] * (2 + len(x)) + [ANY],
+        in_specs=[VMEM] * (3 + len(x)) + [ANY],
         out_shape=[
             jax.ShapeDtypeStruct((rows, span), x[0].dtype),
             jax.ShapeDtypeStruct((rows, ADAPTER_RANK), jnp.float32),
         ],
-        compiler_params=pltpu.CompilerParams(vmem_limit_bytes=4 << 20),
+        compiler_params=pltpu.CompilerParams(vmem_limit_bytes=5 << 20),
         cost_estimate=pl.CostEstimate(
-            flops=2 * rows * down.size, bytes_accessed=2 * down.size, transcendentals=0
+            flops=4 * rows * down.size, bytes_accessed=4 * down.size, transcendentals=0
         ),
         name="low_part",
-    )(down, tenants, *x, after)
+    )(down, other_down, tenants, *x, after)
 
 
 def forward_kernel(cuts, slots, blocks, first, slot, *refs):
@@ -524,6 +526,7 @@
     )
     far, near = hops[-1], hops[-2]
     came = [swapped(normed_layer_input, hop) for hop in (near, far, near | far)]
+    other_down_maps = swapped(adapter_down_maps, 1)
     store, token = store_call(mark, store, pair(0, 0, 1), [], [mark_shape], 0, "fetch")
     block = stacked([normed_layer_input, *came], [token])
     for hop in reversed(hops[2:-2]):
@@ -533,10 +536,10 @@
         mark, store, pair(1, 2, 3), [], [mark_shape], 0, "fetch", after=[block]
     )
 
-    input_span, low = low_part(adapter_down_maps, tenants, x, count, token)
+    input_span, low = low_part(adapter_down_maps, other_down_maps, tenants, x, count, token)
     sums = []
     slots = {0: (0, 1), 1: (2, 3), 2: (4, 5), 3: (0, 1)}
-    step = 0
+    step = 1
     for cuts, fetches in (
         ((0, 1), pair(2, 4, 5)), ((2,), pair(3, 0, 1)), ((3,), [(adapter_up_maps, 0, 2)])
     ):

time: 83.5 us -> 82.7 us (level)
  waiting for transfers between devices: 4.26 us -> 3.02 us
    ppermute x21, waiting for transfers between devices: 4.26 us -> 3.02 us  [swapped(): lax.ppermute(block, 'tp', [(i, i ^ hop) for i in range(lax.axis_size('tp'...]
  transfers between devices with their start and end apart: 21 -> 21, of which waited for: 4 -> 3; matrix products, arithmetic and copies ran while one was open for 0% -> 0% of each run, Pallas kernels for 60% -> 61%
where the time goes in v19:
time: 82.7 us; the launch traced here: 82.5 us
  Pallas kernels  55.6 us (67%)
  starting transfers between devices  22.6 us (27%)
  waiting for transfers between devices  3.02 us (4%)
  between operations  0.94 us (1%)
    pallas_call x11, Pallas kernels, store_call(): pl.pallas_call(body, in_specs=[VMEM] * (n_in + (not new)) + [ANY] * (n_hb...  46.4 us
    ppermute x21, starting transfers between devices, swapped(): lax.ppermute(block, 'tp', [(i, i ^ hop) for i in range(lax.axis_size('tp'...  22.6 us
    pallas_call x2, Pallas kernels, outer(): pl.pallas_call(outer_kernel, grid=(height // block,), in_specs=[pl.BlockS...  6.37 us
    ppermute x21, waiting for transfers between devices, swapped(): lax.ppermute(block, 'tp', [(i, i ^ hop) for i in range(lax.axis_size('tp'...  3.02 us
  transfers between devices with their start and end apart: 21, of which 3 were waited for; matrix products, arithmetic and copies ran while one was open for 0% of the time, Pallas kernels for 61%

profile of v19, /device:TPU:0, one launch (start us, length us, event | category | flops | bytes accessed | tf_op | source)
XLA Modules:
  0.0 82.5 jit_solution(3133243175648024554)
XLA Ops:
  0.6 0.0 copy-start.3
  0.6 0.5 collective-permute-start.6
  1.2 2.7 %collective-permute-start = (bf16[2,8192]{1,0:T(2,128)(2,1)}, bf16[2,8192]{1,0:T(2,128)(2,1)S(1)}, u32[]{:S(2)}, u32[]{:S(2)}) collective-permute-start(bf16[2,8192]{1,0:T(2,128)(2,1)} %refs_0_.4), channel_id=1, source_target_pairs={{0,4},{1,5},{2,6},{3,7},{4,0},{5,1},{6,2},{7,3},{8,12},{9,13},{10,... | collective-permute-start | bytes 98312 | tf_op jit(solution)/shard_map/ppermute | solution.py:499
  3.8 2.6 %collective-permute-start.1 = (bf16[2,8192]{1,0:T(2,128)(2,1)}, bf16[2,8192]{1,0:T(2,128)(2,1)S(1)}, u32[]{:S(2)}, u32[]{:S(2)}) collective-permute-start(bf16[2,8192]{1,0:T(2,128)(2,1)} %refs_0_.4), channel_id=1, source_target_pairs={{0,8},{1,9},{2,10},{3,11},{4,12},{5,13},{6,14},{7,15},{8,0},{9,1},... | collective-permute-start | bytes 98312 | tf_op jit(solution)/shard_map/ppermute | solution.py:499
  6.4 0.0 collective-permute-start.2
  6.4 5.3 %fetch.2 = (bf16[12288,1792]{1,0:T(8,128)(2,1)S(1)}, f32[8,128]{1,0:T(8,128)S(1)}) custom-call(bf16[8192,1792]{1,0:T(8,128)(2,1)} %refs_4_.1, bf16[8192,1792]{1,0:T(8,128)(2,1)} %refs_3_.5), custom_call_target="tpu_custom_call" | custom-call | bytes 14680064 | tf_op jit(solution)/shard_map/fetch/pallas_call | solution.py:102
  11.7 0.0 collective-permute-done.refs_1_
  11.7 0.0 collective-permute-done.1.refs_2_
  11.8 0.6 collective-permute-done.2.refs_3_
  12.3 0.1 stacked.1.refs_3_.refs_1_
  12.4 1.6 %collective-permute-start.3 = (bf16[8,8192]{1,0:T(8,128)(2,1)S(1)}, bf16[8,8192]{1,0:T(8,128)(2,1)S(1)}, u32[]{:S(2)}, u32[]{:S(2)}) collective-permute-start(bf16[8,8192]{1,0:T(8,128)(2,1)S(1)} %stacked.1.refs_3_.refs_1_), channel_id=1, source_target_pairs={{0,2},{1,3},{2,0},{3,1},{4,6},{5,7},{6,4},{7,5},{8,10},{9,11},{10,... | collective-permute-start | bytes 393224 | tf_op jit(solution)/shard_map/ppermute | solution.py:499
  14.0 0.0 collective-permute-start.4
  14.0 0.6 collective-permute-start.5
  14.6 5.5 %fetch.3 = (bf16[12288,1792]{1,0:T(8,128)(2,1)S(1)}, f32[8,128]{1,0:T(8,128)S(1)}) custom-call(bf16[12288,1792]{1,0:T(8,128)(2,1)S(1)} %get-tuple-element.50.refs_0_, bf16[8192,1792]{1,0:T(8,128)(2,1)} %refs_4_.1, bf16[8192,1792]{1,0:T(8,128)(2,1)} %refs_3_.5, bf16[8,8192]{1,0:T(8,128)(2,1)S(1)} %stacked.1.refs_3_.refs_1_), custom_call_target="tpu_custom_call", output_to_operand_aliasing={{0}: (0, {})} | custom-call | bytes 14680064 | tf_op jit(solution)/shard_map/fetch/pallas_call | solution.py:102
  20.1 0.0 collective-permute-done.3.refs_4_.refs_2_
  20.1 0.0 collective-permute-done.4.refs_5_.refs_3_
  20.1 0.0 collective-permute-done.5.refs_6_.refs_4_
  20.1 0.0 collective-permute-done.6.refs_1_
  20.1 0.3 copy-done
  20.5 1.0 %low_part.1 = (bf16[32,512]{1,0:T(8,128)(2,1)S(1)}, f32[32,64]{1,0:T(8,128)S(1)}) custom-call(bf16[512,2048]{1,0:T(8,128)(2,1)S(1)} %copy-done, bf16[512,2048]{1,0:T(8,128)(2,1)S(1)} %collective-permute-done.6.refs_1_, s32[1,32]{1,0:T(1,128)S(1)} %bitcast.1, bf16[8,8192]{1,0:T(8,128)(2,1)S(1)} %stacked.1.refs_3_.refs_1_, ...), custom_call_target="tpu_custom_call" | custom-call | flops 134217728 | bytes 4194304 | tf_op jit(solution)/shard_map/low_part/pallas_call | solution.py:200
  21.5 1.5 %collective-permute-start.7 = (f32[32,64]{1,0:T(8,128)S(1)}, f32[32,64]{1,0:T(8,128)S(1)}, u32[]{:S(2)}, u32[]{:S(2)}) collective-permute-start(f32[32,64]{1,0:T(8,128)S(1)} %get-tuple-element.54.refs_7_.left_ref), channel_id=1, source_target_pairs={{0,2},{1,3},{2,0},{3,1},{4,6},{5,7},{6,4},{7,5},{8,10},{9,11},{10,... | collective-permute-start | bytes 24584 | tf_op jit(solution)/shard_map/ppermute | solution.py:499
  23.0 5.3 %forward.3 = (bf16[12288,1792]{1,0:T(8,128)(2,1)S(1)}, f32[32,1792]{1,0:T(8,128)S(1)}, f32[32,1792]{1,0:T(8,128)S(1)}) custom-call(bf16[12288,1792]{1,0:T(8,128)(2,1)S(1)} %get-tuple-element.52.refs_0_, bf16[8,8192]{1,0:T(8,128)(2,1)S(1)} %stacked.1.refs_3_.refs_1_, ...), custom_call_target="tpu_custom_call", output_to_operand_aliasing={{0}: (0, {})} | custom-call | flops 939524096 | bytes 14680064 | tf_op jit(solution)/shard_map/forward/pallas_call | solution.py:102
  28.4 0.0 collective-permute-done.7.right_ref
  28.4 0.4 collective-permute-start.8
  28.8 5.4 %forward.4 = (bf16[12288,1792]{1,0:T(8,128)(2,1)S(1)}, f32[32,1792]{1,0:T(8,128)S(1)}, f32[32,1792]{1,0:T(8,128)S(1)}) custom-call(bf16[12288,1792]{1,0:T(8,128)(2,1)S(1)} %get-tuple-element.55.refs_0_, bf16[8,8192]{1,0:T(8,128)(2,1)S(1)} %stacked.1.refs_3_.refs_1_, ...), custom_call_target="tpu_custom_call", output_to_operand_aliasing={{0}: (0, {})} | custom-call | flops 469762048 | bytes 14680064 | tf_op jit(solution)/shard_map/forward/pallas_call | solution.py:102
  34.2 0.0 copy-start.2
  34.3 0.0 collective-permute-done.8.right_ref
  34.3 3.6 %collective-permute-start.9 = (f32[32,64]{1,0:T(8,128)S(1)}, f32[32,64]{1,0:T(8,128)S(1)}, u32[]{:S(2)}, u32[]{:S(2)}) collective-permute-start(f32[32,64]{1,0:T(8,128)S(1)} %plus.8.refs_8_.left_ref), channel_id=1, source_target_pairs={{0,8},{1,9},{2,10},{3,11},{4,12},{5,13},{6,14},{7,15},{8,0},{9,1},... | collective-permute-start | bytes 24584 | tf_op jit(solution)/shard_map/ppermute | solution.py:499
  37.8 3.2 %forward.5 = (bf16[12288,1792]{1,0:T(8,128)(2,1)S(1)}, f32[32,1792]{1,0:T(8,128)S(1)}, f32[32,1792]{1,0:T(8,128)S(1)}) custom-call(bf16[12288,1792]{1,0:T(8,128)(2,1)S(1)} %get-tuple-element.58.refs_0_, bf16[8,8192]{1,0:T(8,128)(2,1)S(1)} %stacked.1.refs_3_.refs_1_, ...), custom_call_target="tpu_custom_call", output_to_operand_aliasing={{0}: (0, {})} | custom-call | flops 469762048 | bytes 7340032 | tf_op jit(solution)/shard_map/forward/pallas_call | solution.py:102
  41.0 0.0 collective-permute-done.9.right_ref
  41.0 3.8 %activation.1 = (bf16[12288,1792]{1,0:T(8,128)(2,1)S(1)}, bf16[32,1792]{1,0:T(8,128)(2,1)S(1)}, bf16[32,1792]{1,0:T(8,128)(2,1)S(1)}, f32[32,64]{1,0:T(8,128)S(1)}, bf16[32,2048]{1,0:T(8,128)(2,1)S(1)}) custom-call(bf16[12288,1792]{1,0:T(8,128)(2,1)S(1)} %get-tuple-element.61.refs_0_, ...), custom_call_target="tpu_custom_call", output_to_operand_aliasing={{0}: (0, {})} | custom-call | flops 469762048 | tf_op jit(solution)/shard_map/activation/pallas_call | solution.py:102
  44.8 0.5 collective-permute-start.10
  45.4 4.6 %backward.5 = (bf16[12288,1792]{1,0:T(8,128)(2,1)S(1)}, f32[16,2048]{1,0:T(8,128)S(1)}, bf16[16,2048]{1,0:T(8,128)(2,1)S(1)}) custom-call(bf16[12288,1792]{1,0:T(8,128)(2,1)S(1)} %get-tuple-element.65.refs_0_, bf16[32,1792]{1,0:T(8,128)(2,1)S(1)} %get-tuple-element.66.refs_1_.right_ref, ...), custom_call_target="tpu_custom_call", output_to_operand_aliasing={{0}: (0, {})} | custom-call | flops 469762048 | bytes 7340032 | tf_op jit(solution)/shard_map/backward/pallas_call | solution.py:102
  50.0 0.0 collective-permute-done.10.right_ref
  50.0 0.1 collective-permute-start.11
  50.1 4.4 %backward.6 = (bf16[12288,1792]{1,0:T(8,128)(2,1)S(1)}, f32[16,2048]{1,0:T(8,128)S(1)}, bf16[16,4096]{1,0:T(8,128)(2,1)S(1)}) custom-call(bf16[12288,1792]{1,0:T(8,128)(2,1)S(1)} %get-tuple-element.68.refs_0_, bf16[32,1792]{1,0:T(8,128)(2,1)S(1)} %get-tuple-element.66.refs_1_.right_ref, ...), custom_call_target="tpu_custom_call", output_to_operand_aliasing={{0}: (0, {})} | custom-call | flops 469762048 | bytes 7340032 | tf_op jit(solution)/shard_map/backward/pallas_call | solution.py:102
  54.5 0.1 collective-permute-start.14
  54.6 0.0 collective-permute-done.11.right_ref
  54.6 1.6 %collective-permute-start.12 = (f32[32,64]{1,0:T(8,128)S(1)}, f32[32,64]{1,0:T(8,128)S(1)}, u32[]{:S(2)}, u32[]{:S(2)}) collective-permute-start(f32[32,64]{1,0:T(8,128)S(1)} %plus.11.left_ref.refs_4_), channel_id=1, source_target_pairs={{0,8},{1,9},{2,10},{3,11},{4,12},{5,13},{6,14},{7,15},{8,0},{9,1},... | collective-permute-start | bytes 24584 | tf_op jit(solution)/shard_map/ppermute | solution.py:499
  56.2 4.4 %backward.7 = (bf16[12288,1792]{1,0:T(8,128)(2,1)S(1)}, f32[16,2048]{1,0:T(8,128)S(1)}, bf16[16,2048]{1,0:T(8,128)(2,1)S(1)}) custom-call(bf16[12288,1792]{1,0:T(8,128)(2,1)S(1)} %get-tuple-element.70.refs_0_, bf16[32,1792]{1,0:T(8,128)(2,1)S(1)} %get-tuple-element.66.refs_1_.right_ref, ...), custom_call_target="tpu_custom_call", output_to_operand_aliasing={{0}: (0, {})} | custom-call | flops 469762048 | bytes 7340032 | tf_op jit(solution)/shard_map/backward/pallas_call | solution.py:102
  60.7 0.0 collective-permute-done.12.right_ref
  60.7 0.3 collective-permute-start.13
  61.0 2.2 %backward.8 = (bf16[12288,1792]{1,0:T(8,128)(2,1)S(1)}, f32[16,1024]{1,0:T(8,128)S(1)}, bf16[16,3072]{1,0:T(8,128)(2,1)S(1)}) custom-call(bf16[12288,1792]{1,0:T(8,128)(2,1)S(1)} %get-tuple-element.71.refs_0_, bf16[32,1792]{1,0:T(8,128)(2,1)S(1)} %get-tuple-element.66.refs_1_.right_ref, ...), custom_call_target="tpu_custom_call", output_to_operand_aliasing={{0}: (0, {})} | custom-call | flops 234881024 | tf_op jit(solution)/shard_map/backward/pallas_call | solution.py:102
  63.2 0.0 collective-permute-done.13.right_ref
  63.2 0.9 %adapter_part.1 = (bf16[16,512]{1,0:T(8,128)(2,1)S(1)}, bf16[16,3584]{1,0:T(8,128)(2,1)S(1)}, bf16[32,2048]{1,0:T(8,128)(2,1)S(1)}) custom-call(f32[32,64]{1,0:T(8,128)S(1)} %plus.13.refs_0_, s32[1,32]{1,0:T(1,128)S(1)} %bitcast.3, bf16[512,2048]{1,0:T(8,128)(2,1)S(1)} %copy-done.1, bf16[16,3072]{1,0:T(8,128)(2,1)S(1)} %get-tuple-element.73.refs_3_), custom_call_target="tpu_custom_call" | custom-call | flops 67108864 | bytes 2097152 | tf_op jit(solution)/shard_map/adapter_part/pallas_call | solution.py:303
  64.1 0.4 collective-permute-start.15
  64.5 2.2 %backward.9 = (bf16[12288,1792]{1,0:T(8,128)(2,1)S(1)}, f32[16,1024]{1,0:T(8,128)S(1)}, bf16[16,1024]{1,0:T(8,128)(2,1)S(1)}) custom-call(bf16[12288,1792]{1,0:T(8,128)(2,1)S(1)} %get-tuple-element.79.refs_0_, bf16[32,1792]{1,0:T(8,128)(2,1)S(1)} %get-tuple-element.66.refs_1_.right_ref, ...), custom_call_target="tpu_custom_call", output_to_operand_aliasing={{0}: (0, {})} | custom-call | flops 234881024 | tf_op jit(solution)/shard_map/backward/pallas_call | solution.py:102
  66.7 0.2 collective-permute-start.16
  66.9 1.0 %collective-permute-done.16.refs_8_ = bf16[16,1024]{1,0:T(8,128)(2,1)S(1)} collective-permute-done((bf16[16,1024]{1,0:T(8,128)(2,1)S(1)}, bf16[16,1024]{1,0:T(8,128)(2,1)S(1)}, u32[]{:S(2)}, u32[]{:S(2)}) %collective-permute-start.16) | collective-permute-done | bytes 32800 | tf_op jit(solution)/shard_map/ppermute | solution.py:499
  67.9 0.0 collective-permute-done.14.refs_6_
  67.9 0.0 collective-permute-done.15.refs_7_
  67.9 0.1 first_halves.1
  68.0 1.6 %collective-permute-start.17 = (bf16[8,8192]{1,0:T(8,128)(2,1)S(1)}, bf16[8,8192]{1,0:T(8,128)(2,1)S(1)}, u32[]{:S(2)}, u32[]{:S(2)}) collective-permute-start(bf16[8,8192]{1,0:T(8,128)(2,1)S(1)} %get-tuple-element.85.refs_0_), channel_id=1, source_target_pairs={{0,2},{1,3},{2,0},{3,1},{4,6},{5,7},{6,4},{7,5},{8,10},{9,11},{10,... | collective-permute-start | bytes 393224 | tf_op jit(solution)/shard_map/ppermute | solution.py:499
  69.6 4.5 %up_maps.1 = (bf16[2048,1792]{1,0:T(8,128)(2,1)}, f32[8,128]{1,0:T(8,128)S(1)}) custom-call(bf16[32,2048]{1,0:T(8,128)(2,1)S(1)} %get-tuple-element.86.left_ref, bf16[32,1792]{1,0:T(8,128)(2,1)S(1)} %get-tuple-element.66.refs_1_.right_ref, bf16[8,8192]{1,0:T(8,128)(2,1)S(1)} %get-tuple-element.85.refs_0_), custom_call_target="tpu_custom_call" | custom-call | flops 234881024 | bytes 7340032 | tf_op jit(solution)/shard_map/up_maps/pallas_call | solution.py:461
  74.1 0.0 collective-permute-done.17.came_ref
  74.1 0.1 quarters.1
  74.2 2.9 %collective-permute-start.18 = (bf16[2,8192]{1,0:T(2,128)(2,1)S(1)}, bf16[2,8192]{1,0:T(2,128)(2,1)S(1)}, u32[]{:S(2)}, u32[]{:S(2)}) collective-permute-start(bf16[2,8192]{1,0:T(2,128)(2,1)S(1)} %get-tuple-element.89), channel_id=1, source_target_pairs={{0,12},{1,13},{2,14},{3,15},{4,8},{5,9},{6,10},{7,11},{8,4},{9,5},... | collective-permute-start | bytes 98312 | tf_op jit(solution)/shard_map/ppermute | solution.py:499
  77.1 0.5 collective-permute-start.19
  77.6 1.0 %collective-permute-start.20 = (bf16[2,8192]{1,0:T(2,128)(2,1)S(1)}, bf16[2,8192]{1,0:T(2,128)(2,1)S(1)}, u32[]{:S(2)}, u32[]{:S(2)}) collective-permute-start(bf16[2,8192]{1,0:T(2,128)(2,1)S(1)} %get-tuple-element.91.refs_0_), channel_id=1, source_target_pairs={{0,4},{1,5},{2,6},{3,7},{4,0},{5,1},{6,2},{7,3},{8,12},{9,13},{10,... | collective-permute-start | bytes 98312 | tf_op jit(solution)/shard_map/ppermute | solution.py:499
  78.6 1.9 %down_maps.1 = (bf16[512,2048]{1,0:T(8,128)(2,1)}, f32[8,128]{1,0:T(8,128)S(1)}) custom-call(bf16[32,512]{1,0:T(8,128)(2,1)S(1)} %get-tuple-element.92.left_ref, bf16[32,2048]{1,0:T(8,128)(2,1)S(1)} %get-tuple-element.93.right_ref, bf16[2,8192]{1,0:T(2,128)(2,1)S(1)} %get-tuple-element.91.refs_0_), custom_call_target="tpu_custom_call" | custom-call | flops 67108864 | bytes 2097152 | tf_op jit(solution)/shard_map/down_maps/pallas_call | solution.py:461
  80.5 0.0 collective-permute-done.18.refs_0_
  80.5 1.4 %collective-permute-done.19.refs_1_ = bf16[2,8192]{1,0:T(2,128)(2,1)S(1)} collective-permute-done((bf16[2,8192]{1,0:T(2,128)(2,1)S(1)}, bf16[2,8192]{1,0:T(2,128)(2,1)S(1)}, u32[]{:S(2)}, u32[]{:S(2)}) %collective-permute-start.19) | collective-permute-done | bytes 32800 | tf_op jit(solution)/shard_map/ppermute | solution.py:499
  81.9 0.0 collective-permute-done.20.refs_2_
  81.9 0.7 final.1
  (14 shorter events, 0.1 us)
Async XLA Ops:
  0.6 11.7 %copy-start.3 = (bf16[2,8192]{1,0:T(2,128)(2,1)S(1)}, bf16[2,8192]{1,0:T(2,128)(2,1)}, u32[]{:S(2)}) copy-start(bf16[2,8192]{1,0:T(2,128)(2,1)} %refs_0_.4) | copy-start | bytes 98308
  0.6 19.5 %collective-permute-start.6 = (bf16[512,2048]{1,0:T(8,128)(2,1)}, bf16[512,2048]{1,0:T(8,128)(2,1)S(1)}, u32[]{:S(2)}, u32[]{:S(2)}) collective-permute-start(bf16[512,2048]{1,0:T(8,128)(2,1)} %refs_2_.3), channel_id=1, source_target_pairs={{0,1},{1,0},{2,3},{3,2},{4,5},{5,4},{6,7},{7,6},{8,9},{9,8},{10,11... | collective-permute-start | bytes 6291464 | tf_op jit(solution)/shard_map/ppermute | solution.py:499
  1.2 10.6 %collective-permute-start = (bf16[2,8192]{1,0:T(2,128)(2,1)}, bf16[2,8192]{1,0:T(2,128)(2,1)S(1)}, u32[]{:S(2)}, u32[]{:S(2)}) collective-permute-start(bf16[2,8192]{1,0:T(2,128)(2,1)} %refs_0_.4), channel_id=1, source_target_pairs={{0,4},{1,5},{2,6},{3,7},{4,0},{5,1},{6,2},{7,3},{8,12},{9,13},{10,... | collective-permute-start | bytes 98312 | tf_op jit(solution)/shard_map/ppermute | solution.py:499
  3.8 7.9 %collective-permute-start.1 = (bf16[2,8192]{1,0:T(2,128)(2,1)}, bf16[2,8192]{1,0:T(2,128)(2,1)S(1)}, u32[]{:S(2)}, u32[]{:S(2)}) collective-permute-start(bf16[2,8192]{1,0:T(2,128)(2,1)} %refs_0_.4), channel_id=1, source_target_pairs={{0,8},{1,9},{2,10},{3,11},{4,12},{5,13},{6,14},{7,15},{8,0},{9,1},... | collective-permute-start | bytes 98312 | tf_op jit(solution)/shard_map/ppermute | solution.py:499
  6.4 5.9 %collective-permute-start.2 = (bf16[2,8192]{1,0:T(2,128)(2,1)}, bf16[2,8192]{1,0:T(2,128)(2,1)S(1)}, u32[]{:S(2)}, u32[]{:S(2)}) collective-permute-start(bf16[2,8192]{1,0:T(2,128)(2,1)} %refs_0_.4), channel_id=1, source_target_pairs={{0,12},{1,13},{2,14},{3,15},{4,8},{5,9},{6,10},{7,11},{8,4},{9,5},... | collective-permute-start | bytes 98312 | tf_op jit(solution)/shard_map/ppermute | solution.py:499
  12.4 7.7 %collective-permute-start.3 = (bf16[8,8192]{1,0:T(8,128)(2,1)S(1)}, bf16[8,8192]{1,0:T(8,128)(2,1)S(1)}, u32[]{:S(2)}, u32[]{:S(2)}) collective-permute-start(bf16[8,8192]{1,0:T(8,128)(2,1)S(1)} %stacked.1.refs_3_.refs_1_), channel_id=1, source_target_pairs={{0,2},{1,3},{2,0},{3,1},{4,6},{5,7},{6,4},{7,5},{8,10},{9,11},{10,... | collective-permute-start | bytes 393224 | tf_op jit(solution)/shard_map/ppermute | solution.py:499
  14.0 6.1 %collective-permute-start.4 = (bf16[8,8192]{1,0:T(8,128)(2,1)S(1)}, bf16[8,8192]{1,0:T(8,128)(2,1)S(1)}, u32[]{:S(2)}, u32[]{:S(2)}) collective-permute-start(bf16[8,8192]{1,0:T(8,128)(2,1)S(1)} %stacked.1.refs_3_.refs_1_), channel_id=1, source_target_pairs={{0,1},{1,0},{2,3},{3,2},{4,5},{5,4},{6,7},{7,6},{8,9},{9,8},{10,11... | collective-permute-start | bytes 393224 | tf_op jit(solution)/shard_map/ppermute | solution.py:499
  14.0 6.1 %collective-permute-start.5 = (bf16[8,8192]{1,0:T(8,128)(2,1)S(1)}, bf16[8,8192]{1,0:T(8,128)(2,1)S(1)}, u32[]{:S(2)}, u32[]{:S(2)}) collective-permute-start(bf16[8,8192]{1,0:T(8,128)(2,1)S(1)} %stacked.1.refs_3_.refs_1_), channel_id=1, source_target_pairs={{0,3},{1,2},{2,1},{3,0},{4,7},{5,6},{6,5},{7,4},{8,11},{9,10},{10,... | collective-permute-start | bytes 393224 | tf_op jit(solution)/shard_map/ppermute | solution.py:499
  14.6 5.8 %copy-start = (bf16[512,2048]{1,0:T(8,128)(2,1)S(1)}, bf16[512,2048]{1,0:T(8,128)(2,1)}, u32[]{:S(2)}) copy-start(bf16[512,2048]{1,0:T(8,128)(2,1)} %refs_2_.3) | copy-start | bytes 6291460
  14.6 5.8 %copy-start.4 = (s32[32]{0:T(128)S(1)}, s32[32]{0:T(128)}, u32[]{:S(2)}) copy-start(s32[32]{0:T(128)} %param.13) | copy-start | bytes 388
  21.5 6.9 %collective-permute-start.7 = (f32[32,64]{1,0:T(8,128)S(1)}, f32[32,64]{1,0:T(8,128)S(1)}, u32[]{:S(2)}, u32[]{:S(2)}) collective-permute-start(f32[32,64]{1,0:T(8,128)S(1)} %get-tuple-element.54.refs_7_.left_ref), channel_id=1, source_target_pairs={{0,2},{1,3},{2,0},{3,1},{4,6},{5,7},{6,4},{7,5},{8,10},{9,11},{10,... | collective-permute-start | bytes 24584 | tf_op jit(solution)/shard_map/ppermute | solution.py:499
  28.4 5.9 %collective-permute-start.8 = (f32[32,64]{1,0:T(8,128)S(1)}, f32[32,64]{1,0:T(8,128)S(1)}, u32[]{:S(2)}, u32[]{:S(2)}) collective-permute-start(f32[32,64]{1,0:T(8,128)S(1)} %plus.7.refs_9_.left_ref), channel_id=1, source_target_pairs={{0,4},{1,5},{2,6},{3,7},{4,0},{5,1},{6,2},{7,3},{8,12},{9,13},{10,... | collective-permute-start | bytes 24584 | tf_op jit(solution)/shard_map/ppermute | solution.py:499
  34.2 6.8 %copy-start.2 = (bf16[32,1792]{1,0:T(8,128)(2,1)S(1)}, bf16[32,1792]{1,0:T(8,128)(2,1)}, u32[]{:S(2)}) copy-start(bf16[32,1792]{1,0:T(8,128)(2,1)} %refs_3_.3) | copy-start | bytes 344068
  34.3 6.7 %collective-permute-start.9 = (f32[32,64]{1,0:T(8,128)S(1)}, f32[32,64]{1,0:T(8,128)S(1)}, u32[]{:S(2)}, u32[]{:S(2)}) collective-permute-start(f32[32,64]{1,0:T(8,128)S(1)} %plus.8.refs_8_.left_ref), channel_id=1, source_target_pairs={{0,8},{1,9},{2,10},{3,11},{4,12},{5,13},{6,14},{7,15},{8,0},{9,1},... | collective-permute-start | bytes 24584 | tf_op jit(solution)/shard_map/ppermute | solution.py:499
  44.8 5.1 %collective-permute-start.10 = (f32[32,64]{1,0:T(8,128)S(1)}, f32[32,64]{1,0:T(8,128)S(1)}, u32[]{:S(2)}, u32[]{:S(2)}) collective-permute-start(f32[32,64]{1,0:T(8,128)S(1)} %get-tuple-element.64.left_ref.refs_4_), channel_id=1, source_target_pairs={{0,2},{1,3},{2,0},{3,1},{4,6},{5,7},{6,4},{7,5},{8,10},{9,11},{10,... | collective-permute-start | bytes 24584 | tf_op jit(solution)/shard_map/ppermute | solution.py:499
  50.0 4.6 %collective-permute-start.11 = (f32[32,64]{1,0:T(8,128)S(1)}, f32[32,64]{1,0:T(8,128)S(1)}, u32[]{:S(2)}, u32[]{:S(2)}) collective-permute-start(f32[32,64]{1,0:T(8,128)S(1)} %plus.10.left_ref.refs_5_), channel_id=1, source_target_pairs={{0,4},{1,5},{2,6},{3,7},{4,0},{5,1},{6,2},{7,3},{8,12},{9,13},{10,... | collective-permute-start | bytes 24584 | tf_op jit(solution)/shard_map/ppermute | solution.py:499
  54.5 13.4 %collective-permute-start.14 = (bf16[16,4096]{1,0:T(8,128)(2,1)S(1)}, bf16[16,4096]{1,0:T(8,128)(2,1)S(1)}, u32[]{:S(2)}, u32[]{:S(2)}) collective-permute-start(bf16[16,4096]{1,0:T(8,128)(2,1)S(1)} %get-tuple-element.82), channel_id=1, source_target_pairs={{0,1},{1,0},{2,3},{3,2},{4,5},{5,4},{6,7},{7,6},{8,9},{9,8},{10,11... | collective-permute-start | bytes 393224 | tf_op jit(solution)/shard_map/ppermute | solution.py:499
  54.6 6.1 %collective-permute-start.12 = (f32[32,64]{1,0:T(8,128)S(1)}, f32[32,64]{1,0:T(8,128)S(1)}, u32[]{:S(2)}, u32[]{:S(2)}) collective-permute-start(f32[32,64]{1,0:T(8,128)S(1)} %plus.11.left_ref.refs_4_), channel_id=1, source_target_pairs={{0,8},{1,9},{2,10},{3,11},{4,12},{5,13},{6,14},{7,15},{8,0},{9,1},... | collective-permute-start | bytes 24584 | tf_op jit(solution)/shard_map/ppermute | solution.py:499
  56.2 7.0 %copy-start.1 = (bf16[512,2048]{1,0:T(8,128)(2,1)S(1)}, bf16[512,2048]{1,0:T(8,128)(2,1)}, u32[]{:S(2)}) copy-start(bf16[512,2048]{1,0:T(8,128)(2,1)} %refs_2_.3) | copy-start | bytes 6291460
  60.7 2.5 %collective-permute-start.13 = (f32[32,64]{1,0:T(8,128)S(1)}, f32[32,64]{1,0:T(8,128)S(1)}, u32[]{:S(2)}, u32[]{:S(2)}) collective-permute-start(f32[32,64]{1,0:T(8,128)S(1)} %plus.12.left_ref.refs_4_), channel_id=1, source_target_pairs={{0,1},{1,0},{2,3},{3,2},{4,5},{5,4},{6,7},{7,6},{8,9},{9,8},{10,11... | collective-permute-start | bytes 24584 | tf_op jit(solution)/shard_map/ppermute | solution.py:499
  64.1 3.8 %collective-permute-start.15 = (bf16[16,3584]{1,0:T(8,128)(2,1)S(1)}, bf16[16,3584]{1,0:T(8,128)(2,1)S(1)}, u32[]{:S(2)}, u32[]{:S(2)}) collective-permute-start(bf16[16,3584]{1,0:T(8,128)(2,1)S(1)} %get-tuple-element.80.refs_3_), channel_id=1, source_target_pairs={{0,1},{1,0},{2,3},{3,2},{4,5},{5,4},{6,7},{7,6},{8,9},{9,8},{10,11... | collective-permute-start | bytes 344072 | tf_op jit(solution)/shard_map/ppermute | solution.py:499
  66.7 1.2 %collective-permute-start.16 = (bf16[16,1024]{1,0:T(8,128)(2,1)S(1)}, bf16[16,1024]{1,0:T(8,128)(2,1)S(1)}, u32[]{:S(2)}, u32[]{:S(2)}) collective-permute-start(bf16[16,1024]{1,0:T(8,128)(2,1)S(1)} %get-tuple-element.83), channel_id=1, source_target_pairs={{0,1},{1,0},{2,3},{3,2},{4,5},{5,4},{6,7},{7,6},{8,9},{9,8},{10,11... | collective-permute-start | bytes 98312 | tf_op jit(solution)/shard_map/ppermute | solution.py:499
  68.0 6.1 %collective-permute-start.17 = (bf16[8,8192]{1,0:T(8,128)(2,1)S(1)}, bf16[8,8192]{1,0:T(8,128)(2,1)S(1)}, u32[]{:S(2)}, u32[]{:S(2)}) collective-permute-start(bf16[8,8192]{1,0:T(8,128)(2,1)S(1)} %get-tuple-element.85.refs_0_), channel_id=1, source_target_pairs={{0,2},{1,3},{2,0},{3,1},{4,6},{5,7},{6,4},{7,5},{8,10},{9,11},{10,... | collective-permute-start | bytes 393224 | tf_op jit(solution)/shard_map/ppermute | solution.py:499
  74.2 6.4 %collective-permute-start.18 = (bf16[2,8192]{1,0:T(2,128)(2,1)S(1)}, bf16[2,8192]{1,0:T(2,128)(2,1)S(1)}, u32[]{:S(2)}, u32[]{:S(2)}) collective-permute-start(bf16[2,8192]{1,0:T(2,128)(2,1)S(1)} %get-tuple-element.89), channel_id=1, source_target_pairs={{0,12},{1,13},{2,14},{3,15},{4,8},{5,9},{6,10},{7,11},{8,4},{9,5},... | collective-permute-start | bytes 98312 | tf_op jit(solution)/shard_map/ppermute | solution.py:499
  77.1 4.8 %collective-permute-start.19 = (bf16[2,8192]{1,0:T(2,128)(2,1)S(1)}, bf16[2,8192]{1,0:T(2,128)(2,1)S(1)}, u32[]{:S(2)}, u32[]{:S(2)}) collective-permute-start(bf16[2,8192]{1,0:T(2,128)(2,1)S(1)} %get-tuple-element.90), channel_id=1, source_target_pairs={{0,8},{1,9},{2,10},{3,11},{4,12},{5,13},{6,14},{7,15},{8,0},{9,1},... | collective-permute-start | bytes 98312 | tf_op jit(solution)/shard_map/ppermute | solution.py:499
  77.6 4.3 %collective-permute-start.20 = (bf16[2,8192]{1,0:T(2,128)(2,1)S(1)}, bf16[2,8192]{1,0:T(2,128)(2,1)S(1)}, u32[]{:S(2)}, u32[]{:S(2)}) collective-permute-start(bf16[2,8192]{1,0:T(2,128)(2,1)S(1)} %get-tuple-element.91.refs_0_), channel_id=1, source_target_pairs={{0,4},{1,5},{2,6},{3,7},{4,0},{5,1},{6,2},{7,3},{8,12},{9,13},{10,... | collective-permute-start | bytes 98312 | tf_op jit(solution)/shard_map/ppermute | solution.py:499

commit v20 on v19

--- a/solution.py
+++ b/solution.py
@@ -245,7 +245,7 @@
 
 
 def activation_kernel(
-    count, maps_slot, slot, gate_ref, up_ref, hidden_ref, low_ref, tenants_ref,
+    count, maps_slot, slot, gate_ref, up_ref, hidden_ref, low_ref, came_ref, tenants_ref,
     dgate_ref, dup_ref, part_ref, spread_ref,
 ):
     rows = gate_ref.shape[0]
@@ -253,7 +253,7 @@
     own = lax.axis_index("tp")
     pick = pick_held(own, rows, count)
     mask = held_mask(pick, tenants_ref[...])
-    spread = spread_rows(picked(pick, low_ref[...]), mask)
+    spread = spread_rows(picked(pick, low_ref[...] + came_ref[...]), mask)
     spread_ref[...] = spread
     gate = gate_ref[...] + adapter_scale * jnp.dot(
         spread, maps, preferred_element_type=jnp.float32
@@ -267,14 +267,14 @@
     part_ref[...] = picked(pick_given(own, rows, count), part)
 
 
-def activation(maps_slot, store, sums, hidden, low, tenants, count, fetches):
+def activation(maps_slot, store, sums, hidden, low, came, tenants, count, fetches):
     rows, width = sums[0].shape
     value = jax.ShapeDtypeStruct((rows, width), jnp.bfloat16)
     return store_call(
         lambda *refs: activation_kernel(count, maps_slot, *refs),
         store,
         fetches,
-        [*sums, hidden, low, tenants],
+        [*sums, hidden, low, came, tenants],
         [
             value,
             value,
@@ -286,11 +286,14 @@
     )
 
 
-def adapter_kernel(count, low_ref, tenants_ref, down_ref, earlier, own_out, other_out, spread_ref):
+def adapter_kernel(
+    count, low_ref, came_ref, tenants_ref, down_ref, earlier, own_out, other_out, spread_ref
+):
     half = own_out.shape[0]
     before = earlier.shape[1]
     pick = pick_held(lax.axis_index("tp"), 2 * half, count)
-    spread = spread_rows(picked(pick, low_ref[...]), held_mask(pick, tenants_ref[...]))
+    low = low_ref[...] + came_ref[...]
+    spread = spread_rows(picked(pick, low), held_mask(pick, tenants_ref[...]))
     spread_ref[...] = spread
     part = (adapter_scale * contracted_columns(spread, down_ref[...])).astype(jnp.bfloat16)
     own_out[...] = part[:half]
@@ -298,7 +301,7 @@
     other_out[:, before:] = part[half:]
 
 
-def adapter_part(low, tenants, down, count, earlier):
+def adapter_part(low, came, tenants, down, count, earlier):
     rows, span = low.shape[0], down.shape[0]
     return pl.pallas_call(
         lambda *refs: adapter_kernel(count, *refs),
@@ -312,7 +315,7 @@
             flops=2 * rows * down.size, bytes_accessed=2 * down.size, transcendentals=0
         ),
         name="adapter_part",
-    )(low, tenants, down, earlier)
+    )(low, came, tenants, down, earlier)
 
 
 def backward_kernel(slots, start, height, slot, dgate_ref, dup_ref, *refs):
@@ -545,13 +548,17 @@
     ):
         after = [low]
         if step < len(hops):
-            low = plus(low, swapped(low, hops[step]))
+            came_low = swapped(low, hops[step])
+            if step < len(hops) - 1:
+                low = plus(low, came_low)
             step += 1
         store, sums = forward(cuts, slots, x, store, sums, fetches, after)
     for hop in hops[step:]:
-        low = plus(low, swapped(low, hop))
+        came_low = swapped(low, hop)
+        if hop != hops[-1]:
+            low = plus(low, came_low)
     store, dgate, dup, low_grad, input_spread = activation(
-        2, store, sums, hidden_unit_gradient, low, tenants, count, []
+        2, store, sums, hidden_unit_gradient, low, came_low, tenants, count, []
     )
 
     later_hops = hops[1:] + hops[:1]
@@ -569,7 +576,7 @@
         if n == len(part_list) - 1:
             span = (len(came), waiting[0].shape[1])
             adapter_own, to_send, grad_spread = adapter_part(
-                low_grad, tenants, adapter_down_maps, count, waiting[0]
+                low_grad, came_grad, tenants, adapter_down_maps, count, waiting[0]
             )
             came.append(swapped(to_send, 1))
             after, waiting = [to_send], []
@@ -577,7 +584,9 @@
             turns = later_hops[:1] if n < len(part_list) - 2 else later_hops
             later_hops = later_hops[len(turns) :]
             for hop in turns:
-                low_grad = plus(low_grad, swapped(low_grad, hop))
+                came_grad = swapped(low_grad, hop)
+                if hop != hops[0]:
+                    low_grad = plus(low_grad, came_grad)
         begin = sum(part.shape[1] for part in waiting)
         store, own_part, other_part = backward(
             slots, first, height, dgate, dup, store, fetches, after, waiting
@@ -600,7 +609,7 @@
         else:
             keep, send = halves(keep, came, beside)
     came = [swapped(sends[n - 1], block_owner(0, n, count)) for n in (3, 2, 1)]
-    down_map_gradient, token = outer(input_span, grad_spread, "down_maps", sends[0], 256)
+    down_map_gradient, token = outer(input_span, grad_spread, "down_maps", sends[0], 128)
     return (final(keep, came, [token]), down_map_gradient, up_map_gradient)
 
 

time: 82.7 us -> 82.7 us (level)
  no operation moved by 1% of the time
where the time goes in v20:
time: 82.7 us; the launch traced here: 82.5 us
  Pallas kernels  56.3 us (68%)
  starting transfers between devices  22.7 us (27%)
  waiting for transfers between devices  2.33 us (3%)
  between operations  0.92 us (1%)
    pallas_call x11, Pallas kernels, store_call(): pl.pallas_call(body, in_specs=[VMEM] * (n_in + (not new)) + [ANY] * (n_hb...  46.4 us
    ppermute x21, starting transfers between devices, swapped(): lax.ppermute(block, 'tp', [(i, i ^ hop) for i in range(lax.axis_size('tp'...  22.7 us
    pallas_call x2, Pallas kernels, outer(): pl.pallas_call(outer_kernel, grid=(height // block,), in_specs=[pl.BlockS...  7.05 us
    ppermute x21, waiting for transfers between devices, swapped(): lax.ppermute(block, 'tp', [(i, i ^ hop) for i in range(lax.axis_size('tp'...  2.33 us
  transfers between devices with their start and end apart: 21, of which 3 were waited for; matrix products, arithmetic and copies ran while one was open for 0% of the time, Pallas kernels for 61%

profile of v20, /device:TPU:0, one launch (start us, length us, event | category | flops | bytes accessed | tf_op | source)
XLA Modules:
  0.0 82.5 jit_solution(1538273249976346755)
XLA Ops:
  0.6 0.0 copy-start.3
  0.6 0.5 collective-permute-start.6
  1.2 2.7 %collective-permute-start = (bf16[2,8192]{1,0:T(2,128)(2,1)}, bf16[2,8192]{1,0:T(2,128)(2,1)S(1)}, u32[]{:S(2)}, u32[]{:S(2)}) collective-permute-start(bf16[2,8192]{1,0:T(2,128)(2,1)} %refs_0_.4), channel_id=1, source_target_pairs={{0,4},{1,5},{2,6},{3,7},{4,0},{5,1},{6,2},{7,3},{8,12},{9,13},{10,... | collective-permute-start | bytes 98312 | tf_op jit(solution)/shard_map/ppermute | solution.py:502
  3.8 2.6 %collective-permute-start.1 = (bf16[2,8192]{1,0:T(2,128)(2,1)}, bf16[2,8192]{1,0:T(2,128)(2,1)S(1)}, u32[]{:S(2)}, u32[]{:S(2)}) collective-permute-start(bf16[2,8192]{1,0:T(2,128)(2,1)} %refs_0_.4), channel_id=1, source_target_pairs={{0,8},{1,9},{2,10},{3,11},{4,12},{5,13},{6,14},{7,15},{8,0},{9,1},... | collective-permute-start | bytes 98312 | tf_op jit(solution)/shard_map/ppermute | solution.py:502
  6.4 0.0 collective-permute-start.2
  6.4 5.3 %fetch.2 = (bf16[12288,1792]{1,0:T(8,128)(2,1)S(1)}, f32[8,128]{1,0:T(8,128)S(1)}) custom-call(bf16[8192,1792]{1,0:T(8,128)(2,1)} %refs_4_.1, bf16[8192,1792]{1,0:T(8,128)(2,1)} %refs_3_.6), custom_call_target="tpu_custom_call" | custom-call | bytes 14680064 | tf_op jit(solution)/shard_map/fetch/pallas_call | solution.py:102
  11.7 0.0 collective-permute-done.refs_1_
  11.7 0.0 collective-permute-done.1.refs_2_
  11.8 0.6 collective-permute-done.2.refs_3_
  12.3 0.1 stacked.1.refs_3_.refs_1_
  12.4 1.6 %collective-permute-start.3 = (bf16[8,8192]{1,0:T(8,128)(2,1)S(1)}, bf16[8,8192]{1,0:T(8,128)(2,1)S(1)}, u32[]{:S(2)}, u32[]{:S(2)}) collective-permute-start(bf16[8,8192]{1,0:T(8,128)(2,1)S(1)} %stacked.1.refs_3_.refs_1_), channel_id=1, source_target_pairs={{0,2},{1,3},{2,0},{3,1},{4,6},{5,7},{6,4},{7,5},{8,10},{9,11},{10,... | collective-permute-start | bytes 393224 | tf_op jit(solution)/shard_map/ppermute | solution.py:502
  14.0 0.0 collective-permute-start.4
  14.0 0.6 collective-permute-start.5
  14.6 5.5 %fetch.3 = (bf16[12288,1792]{1,0:T(8,128)(2,1)S(1)}, f32[8,128]{1,0:T(8,128)S(1)}) custom-call(bf16[12288,1792]{1,0:T(8,128)(2,1)S(1)} %get-tuple-element.50.refs_0_, bf16[8192,1792]{1,0:T(8,128)(2,1)} %refs_4_.1, bf16[8192,1792]{1,0:T(8,128)(2,1)} %refs_3_.6, bf16[8,8192]{1,0:T(8,128)(2,1)S(1)} %stacked.1.refs_3_.refs_1_), custom_call_target="tpu_custom_call", output_to_operand_aliasing={{0}: (0, {})} | custom-call | bytes 14680064 | tf_op jit(solution)/shard_map/fetch/pallas_call | solution.py:102
  20.1 0.0 collective-permute-done.3.refs_4_.refs_2_
  20.1 0.0 collective-permute-done.4.refs_5_.refs_3_
  20.1 0.0 collective-permute-done.5.refs_6_.refs_4_
  20.1 0.0 collective-permute-done.6.refs_1_
  20.1 0.3 copy-done
  20.5 1.0 %low_part.1 = (bf16[32,512]{1,0:T(8,128)(2,1)S(1)}, f32[32,64]{1,0:T(8,128)S(1)}) custom-call(bf16[512,2048]{1,0:T(8,128)(2,1)S(1)} %copy-done, bf16[512,2048]{1,0:T(8,128)(2,1)S(1)} %collective-permute-done.6.refs_1_, s32[1,32]{1,0:T(1,128)S(1)} %bitcast.1, bf16[8,8192]{1,0:T(8,128)(2,1)S(1)} %stacked.1.refs_3_.refs_1_, ...), custom_call_target="tpu_custom_call" | custom-call | flops 134217728 | bytes 4194304 | tf_op jit(solution)/shard_map/low_part/pallas_call | solution.py:200
  21.5 1.5 %collective-permute-start.7 = (f32[32,64]{1,0:T(8,128)S(1)}, f32[32,64]{1,0:T(8,128)S(1)}, u32[]{:S(2)}, u32[]{:S(2)}) collective-permute-start(f32[32,64]{1,0:T(8,128)S(1)} %get-tuple-element.54.refs_7_.left_ref), channel_id=1, source_target_pairs={{0,2},{1,3},{2,0},{3,1},{4,6},{5,7},{6,4},{7,5},{8,10},{9,11},{10,... | collective-permute-start | bytes 24584 | tf_op jit(solution)/shard_map/ppermute | solution.py:502
  23.0 5.3 %forward.3 = (bf16[12288,1792]{1,0:T(8,128)(2,1)S(1)}, f32[32,1792]{1,0:T(8,128)S(1)}, f32[32,1792]{1,0:T(8,128)S(1)}) custom-call(bf16[12288,1792]{1,0:T(8,128)(2,1)S(1)} %get-tuple-element.52.refs_0_, bf16[8,8192]{1,0:T(8,128)(2,1)S(1)} %stacked.1.refs_3_.refs_1_, ...), custom_call_target="tpu_custom_call", output_to_operand_aliasing={{0}: (0, {})} | custom-call | flops 939524096 | bytes 14680064 | tf_op jit(solution)/shard_map/forward/pallas_call | solution.py:102
  28.4 0.0 collective-permute-done.7.right_ref
  28.4 0.4 collective-permute-start.8
  28.8 5.4 %forward.4 = (bf16[12288,1792]{1,0:T(8,128)(2,1)S(1)}, f32[32,1792]{1,0:T(8,128)S(1)}, f32[32,1792]{1,0:T(8,128)S(1)}) custom-call(bf16[12288,1792]{1,0:T(8,128)(2,1)S(1)} %get-tuple-element.55.refs_0_, bf16[8,8192]{1,0:T(8,128)(2,1)S(1)} %stacked.1.refs_3_.refs_1_, ...), custom_call_target="tpu_custom_call", output_to_operand_aliasing={{0}: (0, {})} | custom-call | flops 469762048 | bytes 14680064 | tf_op jit(solution)/shard_map/forward/pallas_call | solution.py:102
  34.2 0.0 copy-start.2
  34.3 0.0 collective-permute-done.8.right_ref
  34.3 3.6 %collective-permute-start.9 = (f32[32,64]{1,0:T(8,128)S(1)}, f32[32,64]{1,0:T(8,128)S(1)}, u32[]{:S(2)}, u32[]{:S(2)}) collective-permute-start(f32[32,64]{1,0:T(8,128)S(1)} %plus.6.refs_8_.refs_4_), channel_id=1, source_target_pairs={{0,8},{1,9},{2,10},{3,11},{4,12},{5,13},{6,14},{7,15},{8,0},{9,1},... | collective-permute-start | bytes 24584 | tf_op jit(solution)/shard_map/ppermute | solution.py:502
  37.8 3.2 %forward.5 = (bf16[12288,1792]{1,0:T(8,128)(2,1)S(1)}, f32[32,1792]{1,0:T(8,128)S(1)}, f32[32,1792]{1,0:T(8,128)S(1)}) custom-call(bf16[12288,1792]{1,0:T(8,128)(2,1)S(1)} %get-tuple-element.58.refs_0_, bf16[8,8192]{1,0:T(8,128)(2,1)S(1)} %stacked.1.refs_3_.refs_1_, ...), custom_call_target="tpu_custom_call", output_to_operand_aliasing={{0}: (0, {})} | custom-call | flops 469762048 | bytes 7340032 | tf_op jit(solution)/shard_map/forward/pallas_call | solution.py:102
  41.0 0.0 collective-permute-done.9.refs_5_
  41.0 3.8 %activation.1 = (bf16[12288,1792]{1,0:T(8,128)(2,1)S(1)}, bf16[32,1792]{1,0:T(8,128)(2,1)S(1)}, bf16[32,1792]{1,0:T(8,128)(2,1)S(1)}, f32[32,64]{1,0:T(8,128)S(1)}, bf16[32,2048]{1,0:T(8,128)(2,1)S(1)}) custom-call(bf16[12288,1792]{1,0:T(8,128)(2,1)S(1)} %get-tuple-element.61.refs_0_, ...), custom_call_target="tpu_custom_call", output_to_operand_aliasing={{0}: (0, {})} | custom-call | flops 469762048 | tf_op jit(solution)/shard_map/activation/pallas_call | solution.py:102
  44.8 0.5 collective-permute-start.10
  45.4 4.6 %backward.5 = (bf16[12288,1792]{1,0:T(8,128)(2,1)S(1)}, f32[16,2048]{1,0:T(8,128)S(1)}, bf16[16,2048]{1,0:T(8,128)(2,1)S(1)}) custom-call(bf16[12288,1792]{1,0:T(8,128)(2,1)S(1)} %get-tuple-element.65.refs_0_, bf16[32,1792]{1,0:T(8,128)(2,1)S(1)} %get-tuple-element.66.refs_1_.right_ref, ...), custom_call_target="tpu_custom_call", output_to_operand_aliasing={{0}: (0, {})} | custom-call | flops 469762048 | bytes 7340032 | tf_op jit(solution)/shard_map/backward/pallas_call | solution.py:102
  50.0 0.0 collective-permute-done.10.right_ref
  50.0 0.1 collective-permute-start.11
  50.1 4.4 %backward.6 = (bf16[12288,1792]{1,0:T(8,128)(2,1)S(1)}, f32[16,2048]{1,0:T(8,128)S(1)}, bf16[16,4096]{1,0:T(8,128)(2,1)S(1)}) custom-call(bf16[12288,1792]{1,0:T(8,128)(2,1)S(1)} %get-tuple-element.68.refs_0_, bf16[32,1792]{1,0:T(8,128)(2,1)S(1)} %get-tuple-element.66.refs_1_.right_ref, ...), custom_call_target="tpu_custom_call", output_to_operand_aliasing={{0}: (0, {})} | custom-call | flops 469762048 | bytes 7340032 | tf_op jit(solution)/shard_map/backward/pallas_call | solution.py:102
  54.5 0.1 collective-permute-start.14
  54.6 0.0 collective-permute-done.11.right_ref
  54.6 1.6 %collective-permute-start.12 = (f32[32,64]{1,0:T(8,128)S(1)}, f32[32,64]{1,0:T(8,128)S(1)}, u32[]{:S(2)}, u32[]{:S(2)}) collective-permute-start(f32[32,64]{1,0:T(8,128)S(1)} %plus.8.left_ref.refs_4_), channel_id=1, source_target_pairs={{0,8},{1,9},{2,10},{3,11},{4,12},{5,13},{6,14},{7,15},{8,0},{9,1},... | collective-permute-start | bytes 24584 | tf_op jit(solution)/shard_map/ppermute | solution.py:502
  56.2 4.4 %backward.7 = (bf16[12288,1792]{1,0:T(8,128)(2,1)S(1)}, f32[16,2048]{1,0:T(8,128)S(1)}, bf16[16,2048]{1,0:T(8,128)(2,1)S(1)}) custom-call(bf16[12288,1792]{1,0:T(8,128)(2,1)S(1)} %get-tuple-element.70.refs_0_, bf16[32,1792]{1,0:T(8,128)(2,1)S(1)} %get-tuple-element.66.refs_1_.right_ref, ...), custom_call_target="tpu_custom_call", output_to_operand_aliasing={{0}: (0, {})} | custom-call | flops 469762048 | bytes 7340032 | tf_op jit(solution)/shard_map/backward/pallas_call | solution.py:102
  60.7 0.0 collective-permute-done.12.right_ref
  60.7 0.3 collective-permute-start.13
  61.0 2.2 %backward.8 = (bf16[12288,1792]{1,0:T(8,128)(2,1)S(1)}, f32[16,1024]{1,0:T(8,128)S(1)}, bf16[16,3072]{1,0:T(8,128)(2,1)S(1)}) custom-call(bf16[12288,1792]{1,0:T(8,128)(2,1)S(1)} %get-tuple-element.71.refs_0_, bf16[32,1792]{1,0:T(8,128)(2,1)S(1)} %get-tuple-element.66.refs_1_.right_ref, ...), custom_call_target="tpu_custom_call", output_to_operand_aliasing={{0}: (0, {})} | custom-call | flops 234881024 | tf_op jit(solution)/shard_map/backward/pallas_call | solution.py:102
  63.2 0.0 collective-permute-done.13.refs_1_
  63.2 0.9 %adapter_part.1 = (bf16[16,512]{1,0:T(8,128)(2,1)S(1)}, bf16[16,3584]{1,0:T(8,128)(2,1)S(1)}, bf16[32,2048]{1,0:T(8,128)(2,1)S(1)}) custom-call(f32[32,64]{1,0:T(8,128)S(1)} %plus.9.refs_4_.refs_0_, f32[32,64]{1,0:T(8,128)S(1)} %collective-permute-done.13.refs_1_, s32[1,32]{1,0:T(1,128)S(1)} %bitcast.3, bf16[512,2048]{1,0:T(8,128)(2,1)S(1)} %copy-done.1, ...), custom_call_target="tpu_custom_call" | custom-call | flops 67108864 | bytes 2097152 | tf_op jit(solution)/shard_map/adapter_part/pallas_call | solution.py:306
  64.1 0.4 collective-permute-start.15
  64.5 2.2 %backward.9 = (bf16[12288,1792]{1,0:T(8,128)(2,1)S(1)}, f32[16,1024]{1,0:T(8,128)S(1)}, bf16[16,1024]{1,0:T(8,128)(2,1)S(1)}) custom-call(bf16[12288,1792]{1,0:T(8,128)(2,1)S(1)} %get-tuple-element.79.refs_0_, bf16[32,1792]{1,0:T(8,128)(2,1)S(1)} %get-tuple-element.66.refs_1_.right_ref, ...), custom_call_target="tpu_custom_call", output_to_operand_aliasing={{0}: (0, {})} | custom-call | flops 234881024 | tf_op jit(solution)/shard_map/backward/pallas_call | solution.py:102
  66.7 0.2 collective-permute-start.16
  66.9 1.0 %collective-permute-done.16.refs_8_ = bf16[16,1024]{1,0:T(8,128)(2,1)S(1)} collective-permute-done((bf16[16,1024]{1,0:T(8,128)(2,1)S(1)}, bf16[16,1024]{1,0:T(8,128)(2,1)S(1)}, u32[]{:S(2)}, u32[]{:S(2)}) %collective-permute-start.16) | collective-permute-done | bytes 32800 | tf_op jit(solution)/shard_map/ppermute | solution.py:502
  67.9 0.0 collective-permute-done.14.refs_6_
  67.9 0.0 collective-permute-done.15.refs_7_
  67.9 0.1 first_halves.1
  68.0 1.6 %collective-permute-start.17 = (bf16[8,8192]{1,0:T(8,128)(2,1)S(1)}, bf16[8,8192]{1,0:T(8,128)(2,1)S(1)}, u32[]{:S(2)}, u32[]{:S(2)}) collective-permute-start(bf16[8,8192]{1,0:T(8,128)(2,1)S(1)} %get-tuple-element.85.refs_0_), channel_id=1, source_target_pairs={{0,2},{1,3},{2,0},{3,1},{4,6},{5,7},{6,4},{7,5},{8,10},{9,11},{10,... | collective-permute-start | bytes 393224 | tf_op jit(solution)/shard_map/ppermute | solution.py:502
  69.6 4.5 %up_maps.1 = (bf16[2048,1792]{1,0:T(8,128)(2,1)}, f32[8,128]{1,0:T(8,128)S(1)}) custom-call(bf16[32,2048]{1,0:T(8,128)(2,1)S(1)} %get-tuple-element.86.left_ref, bf16[32,1792]{1,0:T(8,128)(2,1)S(1)} %get-tuple-element.66.refs_1_.right_ref, bf16[8,8192]{1,0:T(8,128)(2,1)S(1)} %get-tuple-element.85.refs_0_), custom_call_target="tpu_custom_call" | custom-call | flops 234881024 | bytes 7340032 | tf_op jit(solution)/shard_map/up_maps/pallas_call | solution.py:464
  74.1 0.0 collective-permute-done.17.came_ref
  74.1 0.1 quarters.1
  74.1 2.9 %collective-permute-start.18 = (bf16[2,8192]{1,0:T(2,128)(2,1)S(1)}, bf16[2,8192]{1,0:T(2,128)(2,1)S(1)}, u32[]{:S(2)}, u32[]{:S(2)}) collective-permute-start(bf16[2,8192]{1,0:T(2,128)(2,1)S(1)} %get-tuple-element.89), channel_id=1, source_target_pairs={{0,12},{1,13},{2,14},{3,15},{4,8},{5,9},{6,10},{7,11},{8,4},{9,5},... | collective-permute-start | bytes 98312 | tf_op jit(solution)/shard_map/ppermute | solution.py:502
  77.0 0.5 collective-permute-start.19
  77.6 1.0 %collective-permute-start.20 = (bf16[2,8192]{1,0:T(2,128)(2,1)S(1)}, bf16[2,8192]{1,0:T(2,128)(2,1)S(1)}, u32[]{:S(2)}, u32[]{:S(2)}) collective-permute-start(bf16[2,8192]{1,0:T(2,128)(2,1)S(1)} %get-tuple-element.91.refs_0_), channel_id=1, source_target_pairs={{0,4},{1,5},{2,6},{3,7},{4,0},{5,1},{6,2},{7,3},{8,12},{9,13},{10,... | collective-permute-start | bytes 98312 | tf_op jit(solution)/shard_map/ppermute | solution.py:502
  78.6 2.6 %down_maps.1 = (bf16[512,2048]{1,0:T(8,128)(2,1)}, f32[8,128]{1,0:T(8,128)S(1)}) custom-call(bf16[32,512]{1,0:T(8,128)(2,1)S(1)} %get-tuple-element.92.left_ref, bf16[32,2048]{1,0:T(8,128)(2,1)S(1)} %get-tuple-element.93.right_ref, bf16[2,8192]{1,0:T(2,128)(2,1)S(1)} %get-tuple-element.91.refs_0_), custom_call_target="tpu_custom_call" | custom-call | flops 67108864 | bytes 2097152 | tf_op jit(solution)/shard_map/down_maps/pallas_call | solution.py:464
  81.2 0.0 collective-permute-done.18.refs_0_
  81.2 0.7 collective-permute-done.19.refs_1_
  81.9 0.0 collective-permute-done.20.refs_2_
  81.9 0.7 final.1
  (12 shorter events, 0.0 us)
Async XLA Ops:
  0.6 11.7 %copy-start.3 = (bf16[2,8192]{1,0:T(2,128)(2,1)S(1)}, bf16[2,8192]{1,0:T(2,128)(2,1)}, u32[]{:S(2)}) copy-start(bf16[2,8192]{1,0:T(2,128)(2,1)} %refs_0_.4) | copy-start | bytes 98308
  0.6 19.5 %collective-permute-start.6 = (bf16[512,2048]{1,0:T(8,128)(2,1)}, bf16[512,2048]{1,0:T(8,128)(2,1)S(1)}, u32[]{:S(2)}, u32[]{:S(2)}) collective-permute-start(bf16[512,2048]{1,0:T(8,128)(2,1)} %refs_3_.7), channel_id=1, source_target_pairs={{0,1},{1,0},{2,3},{3,2},{4,5},{5,4},{6,7},{7,6},{8,9},{9,8},{10,11... | collective-permute-start | bytes 6291464 | tf_op jit(solution)/shard_map/ppermute | solution.py:502
  1.2 10.6 %collective-permute-start = (bf16[2,8192]{1,0:T(2,128)(2,1)}, bf16[2,8192]{1,0:T(2,128)(2,1)S(1)}, u32[]{:S(2)}, u32[]{:S(2)}) collective-permute-start(bf16[2,8192]{1,0:T(2,128)(2,1)} %refs_0_.4), channel_id=1, source_target_pairs={{0,4},{1,5},{2,6},{3,7},{4,0},{5,1},{6,2},{7,3},{8,12},{9,13},{10,... | collective-permute-start | bytes 98312 | tf_op jit(solution)/shard_map/ppermute | solution.py:502
  3.8 7.9 %collective-permute-start.1 = (bf16[2,8192]{1,0:T(2,128)(2,1)}, bf16[2,8192]{1,0:T(2,128)(2,1)S(1)}, u32[]{:S(2)}, u32[]{:S(2)}) collective-permute-start(bf16[2,8192]{1,0:T(2,128)(2,1)} %refs_0_.4), channel_id=1, source_target_pairs={{0,8},{1,9},{2,10},{3,11},{4,12},{5,13},{6,14},{7,15},{8,0},{9,1},... | collective-permute-start | bytes 98312 | tf_op jit(solution)/shard_map/ppermute | solution.py:502
  6.4 5.9 %collective-permute-start.2 = (bf16[2,8192]{1,0:T(2,128)(2,1)}, bf16[2,8192]{1,0:T(2,128)(2,1)S(1)}, u32[]{:S(2)}, u32[]{:S(2)}) collective-permute-start(bf16[2,8192]{1,0:T(2,128)(2,1)} %refs_0_.4), channel_id=1, source_target_pairs={{0,12},{1,13},{2,14},{3,15},{4,8},{5,9},{6,10},{7,11},{8,4},{9,5},... | collective-permute-start | bytes 98312 | tf_op jit(solution)/shard_map/ppermute | solution.py:502
  12.4 7.7 %collective-permute-start.3 = (bf16[8,8192]{1,0:T(8,128)(2,1)S(1)}, bf16[8,8192]{1,0:T(8,128)(2,1)S(1)}, u32[]{:S(2)}, u32[]{:S(2)}) collective-permute-start(bf16[8,8192]{1,0:T(8,128)(2,1)S(1)} %stacked.1.refs_3_.refs_1_), channel_id=1, source_target_pairs={{0,2},{1,3},{2,0},{3,1},{4,6},{5,7},{6,4},{7,5},{8,10},{9,11},{10,... | collective-permute-start | bytes 393224 | tf_op jit(solution)/shard_map/ppermute | solution.py:502
  14.0 6.1 %collective-permute-start.4 = (bf16[8,8192]{1,0:T(8,128)(2,1)S(1)}, bf16[8,8192]{1,0:T(8,128)(2,1)S(1)}, u32[]{:S(2)}, u32[]{:S(2)}) collective-permute-start(bf16[8,8192]{1,0:T(8,128)(2,1)S(1)} %stacked.1.refs_3_.refs_1_), channel_id=1, source_target_pairs={{0,1},{1,0},{2,3},{3,2},{4,5},{5,4},{6,7},{7,6},{8,9},{9,8},{10,11... | collective-permute-start | bytes 393224 | tf_op jit(solution)/shard_map/ppermute | solution.py:502
  14.0 6.1 %collective-permute-start.5 = (bf16[8,8192]{1,0:T(8,128)(2,1)S(1)}, bf16[8,8192]{1,0:T(8,128)(2,1)S(1)}, u32[]{:S(2)}, u32[]{:S(2)}) collective-permute-start(bf16[8,8192]{1,0:T(8,128)(2,1)S(1)} %stacked.1.refs_3_.refs_1_), channel_id=1, source_target_pairs={{0,3},{1,2},{2,1},{3,0},{4,7},{5,6},{6,5},{7,4},{8,11},{9,10},{10,... | collective-permute-start | bytes 393224 | tf_op jit(solution)/shard_map/ppermute | solution.py:502
  14.6 5.8 %copy-start = (bf16[512,2048]{1,0:T(8,128)(2,1)S(1)}, bf16[512,2048]{1,0:T(8,128)(2,1)}, u32[]{:S(2)}) copy-start(bf16[512,2048]{1,0:T(8,128)(2,1)} %refs_3_.7) | copy-start | bytes 6291460
  14.6 5.8 %copy-start.4 = (s32[32]{0:T(128)S(1)}, s32[32]{0:T(128)}, u32[]{:S(2)}) copy-start(s32[32]{0:T(128)} %param.13) | copy-start | bytes 388
  21.5 6.9 %collective-permute-start.7 = (f32[32,64]{1,0:T(8,128)S(1)}, f32[32,64]{1,0:T(8,128)S(1)}, u32[]{:S(2)}, u32[]{:S(2)}) collective-permute-start(f32[32,64]{1,0:T(8,128)S(1)} %get-tuple-element.54.refs_7_.left_ref), channel_id=1, source_target_pairs={{0,2},{1,3},{2,0},{3,1},{4,6},{5,7},{6,4},{7,5},{8,10},{9,11},{10,... | collective-permute-start | bytes 24584 | tf_op jit(solution)/shard_map/ppermute | solution.py:502
  28.4 5.9 %collective-permute-start.8 = (f32[32,64]{1,0:T(8,128)S(1)}, f32[32,64]{1,0:T(8,128)S(1)}, u32[]{:S(2)}, u32[]{:S(2)}) collective-permute-start(f32[32,64]{1,0:T(8,128)S(1)} %plus.5.refs_9_.left_ref), channel_id=1, source_target_pairs={{0,4},{1,5},{2,6},{3,7},{4,0},{5,1},{6,2},{7,3},{8,12},{9,13},{10,... | collective-permute-start | bytes 24584 | tf_op jit(solution)/shard_map/ppermute | solution.py:502
  34.2 6.8 %copy-start.2 = (bf16[32,1792]{1,0:T(8,128)(2,1)S(1)}, bf16[32,1792]{1,0:T(8,128)(2,1)}, u32[]{:S(2)}) copy-start(bf16[32,1792]{1,0:T(8,128)(2,1)} %refs_3_.4) | copy-start | bytes 344068
  34.3 6.7 %collective-permute-start.9 = (f32[32,64]{1,0:T(8,128)S(1)}, f32[32,64]{1,0:T(8,128)S(1)}, u32[]{:S(2)}, u32[]{:S(2)}) collective-permute-start(f32[32,64]{1,0:T(8,128)S(1)} %plus.6.refs_8_.refs_4_), channel_id=1, source_target_pairs={{0,8},{1,9},{2,10},{3,11},{4,12},{5,13},{6,14},{7,15},{8,0},{9,1},... | collective-permute-start | bytes 24584 | tf_op jit(solution)/shard_map/ppermute | solution.py:502
  44.8 5.1 %collective-permute-start.10 = (f32[32,64]{1,0:T(8,128)S(1)}, f32[32,64]{1,0:T(8,128)S(1)}, u32[]{:S(2)}, u32[]{:S(2)}) collective-permute-start(f32[32,64]{1,0:T(8,128)S(1)} %get-tuple-element.64.left_ref.refs_4_), channel_id=1, source_target_pairs={{0,2},{1,3},{2,0},{3,1},{4,6},{5,7},{6,4},{7,5},{8,10},{9,11},{10,... | collective-permute-start | bytes 24584 | tf_op jit(solution)/shard_map/ppermute | solution.py:502
  50.0 4.6 %collective-permute-start.11 = (f32[32,64]{1,0:T(8,128)S(1)}, f32[32,64]{1,0:T(8,128)S(1)}, u32[]{:S(2)}, u32[]{:S(2)}) collective-permute-start(f32[32,64]{1,0:T(8,128)S(1)} %plus.7.left_ref.refs_5_), channel_id=1, source_target_pairs={{0,4},{1,5},{2,6},{3,7},{4,0},{5,1},{6,2},{7,3},{8,12},{9,13},{10,... | collective-permute-start | bytes 24584 | tf_op jit(solution)/shard_map/ppermute | solution.py:502
  54.5 13.4 %collective-permute-start.14 = (bf16[16,4096]{1,0:T(8,128)(2,1)S(1)}, bf16[16,4096]{1,0:T(8,128)(2,1)S(1)}, u32[]{:S(2)}, u32[]{:S(2)}) collective-permute-start(bf16[16,4096]{1,0:T(8,128)(2,1)S(1)} %get-tuple-element.82), channel_id=1, source_target_pairs={{0,1},{1,0},{2,3},{3,2},{4,5},{5,4},{6,7},{7,6},{8,9},{9,8},{10,11... | collective-permute-start | bytes 393224 | tf_op jit(solution)/shard_map/ppermute | solution.py:502
  54.6 6.1 %collective-permute-start.12 = (f32[32,64]{1,0:T(8,128)S(1)}, f32[32,64]{1,0:T(8,128)S(1)}, u32[]{:S(2)}, u32[]{:S(2)}) collective-permute-start(f32[32,64]{1,0:T(8,128)S(1)} %plus.8.left_ref.refs_4_), channel_id=1, source_target_pairs={{0,8},{1,9},{2,10},{3,11},{4,12},{5,13},{6,14},{7,15},{8,0},{9,1},... | collective-permute-start | bytes 24584 | tf_op jit(solution)/shard_map/ppermute | solution.py:502
  56.2 7.0 %copy-start.1 = (bf16[512,2048]{1,0:T(8,128)(2,1)S(1)}, bf16[512,2048]{1,0:T(8,128)(2,1)}, u32[]{:S(2)}) copy-start(bf16[512,2048]{1,0:T(8,128)(2,1)} %refs_3_.7) | copy-start | bytes 6291460
  60.7 2.5 %collective-permute-start.13 = (f32[32,64]{1,0:T(8,128)S(1)}, f32[32,64]{1,0:T(8,128)S(1)}, u32[]{:S(2)}, u32[]{:S(2)}) collective-permute-start(f32[32,64]{1,0:T(8,128)S(1)} %plus.9.refs_4_.refs_0_), channel_id=1, source_target_pairs={{0,1},{1,0},{2,3},{3,2},{4,5},{5,4},{6,7},{7,6},{8,9},{9,8},{10,11... | collective-permute-start | bytes 24584 | tf_op jit(solution)/shard_map/ppermute | solution.py:502
  64.1 3.8 %collective-permute-start.15 = (bf16[16,3584]{1,0:T(8,128)(2,1)S(1)}, bf16[16,3584]{1,0:T(8,128)(2,1)S(1)}, u32[]{:S(2)}, u32[]{:S(2)}) collective-permute-start(bf16[16,3584]{1,0:T(8,128)(2,1)S(1)} %get-tuple-element.80.refs_3_), channel_id=1, source_target_pairs={{0,1},{1,0},{2,3},{3,2},{4,5},{5,4},{6,7},{7,6},{8,9},{9,8},{10,11... | collective-permute-start | bytes 344072 | tf_op jit(solution)/shard_map/ppermute | solution.py:502
  66.7 1.2 %collective-permute-start.16 = (bf16[16,1024]{1,0:T(8,128)(2,1)S(1)}, bf16[16,1024]{1,0:T(8,128)(2,1)S(1)}, u32[]{:S(2)}, u32[]{:S(2)}) collective-permute-start(bf16[16,1024]{1,0:T(8,128)(2,1)S(1)} %get-tuple-element.83), channel_id=1, source_target_pairs={{0,1},{1,0},{2,3},{3,2},{4,5},{5,4},{6,7},{7,6},{8,9},{9,8},{10,11... | collective-permute-start | bytes 98312 | tf_op jit(solution)/shard_map/ppermute | solution.py:502
  68.0 6.1 %collective-permute-start.17 = (bf16[8,8192]{1,0:T(8,128)(2,1)S(1)}, bf16[8,8192]{1,0:T(8,128)(2,1)S(1)}, u32[]{:S(2)}, u32[]{:S(2)}) collective-permute-start(bf16[8,8192]{1,0:T(8,128)(2,1)S(1)} %get-tuple-element.85.refs_0_), channel_id=1, source_target_pairs={{0,2},{1,3},{2,0},{3,1},{4,6},{5,7},{6,4},{7,5},{8,10},{9,11},{10,... | collective-permute-start | bytes 393224 | tf_op jit(solution)/shard_map/ppermute | solution.py:502
  74.1 7.0 %collective-permute-start.18 = (bf16[2,8192]{1,0:T(2,128)(2,1)S(1)}, bf16[2,8192]{1,0:T(2,128)(2,1)S(1)}, u32[]{:S(2)}, u32[]{:S(2)}) collective-permute-start(bf16[2,8192]{1,0:T(2,128)(2,1)S(1)} %get-tuple-element.89), channel_id=1, source_target_pairs={{0,12},{1,13},{2,14},{3,15},{4,8},{5,9},{6,10},{7,11},{8,4},{9,5},... | collective-permute-start | bytes 98312 | tf_op jit(solution)/shard_map/ppermute | solution.py:502
  77.0 4.8 %collective-permute-start.19 = (bf16[2,8192]{1,0:T(2,128)(2,1)S(1)}, bf16[2,8192]{1,0:T(2,128)(2,1)S(1)}, u32[]{:S(2)}, u32[]{:S(2)}) collective-permute-start(bf16[2,8192]{1,0:T(2,128)(2,1)S(1)} %get-tuple-element.90), channel_id=1, source_target_pairs={{0,8},{1,9},{2,10},{3,11},{4,12},{5,13},{6,14},{7,15},{8,0},{9,1},... | collective-permute-start | bytes 98312 | tf_op jit(solution)/shard_map/ppermute | solution.py:502
  77.6 4.3 %collective-permute-start.20 = (bf16[2,8192]{1,0:T(2,128)(2,1)S(1)}, bf16[2,8192]{1,0:T(2,128)(2,1)S(1)}, u32[]{:S(2)}, u32[]{:S(2)}) collective-permute-start(bf16[2,8192]{1,0:T(2,128)(2,1)S(1)} %get-tuple-element.91.refs_0_), channel_id=1, source_target_pairs={{0,4},{1,5},{2,6},{3,7},{4,0},{5,1},{6,2},{7,3},{8,12},{9,13},{10,... | collective-permute-start | bytes 98312 | tf_op jit(solution)/shard_map/ppermute | solution.py:502
